TPU v7x, 32 devices: a whole 2x2x4 slice. The times are simulated.
32 devices in a mesh: vox: 8 (over z, x), smp: 4 (over y, core).
Axes of the slice: x: 2, y: 2, z: 4, core: 2. Of those that a mesh axis runs over, the one named last changes fastest.
Arguments:
- ensemble: float32 [1024, 32, 128], P('vox', 'smp'), may hold values from -6 to 6
- voxel_factor: float32 [1024, 128], P('vox'), may hold values from -6 to 6
- sample_factor: float32 [32, 128], P('smp'), may hold values from -6 to 6
- time_factor: float32 [128, 128], replicated, may hold values from -6 to 6
- weights: float32 [128], replicated, may hold values from 0.005 to 0.02
Outputs:
- voxel_result: float32 [1024, 128], P('vox')
- sample_result: float32 [32, 128], P('smp')
- time_result: float32 [128, 128], replicated
- scale_result: float32 [128], replicated
All inputs are finite; a program needn't handle non-finite values. Where the computation divides by a largest or mean magnitude, that divisor is 1e-20 or more.
Results may differ from a plain program's by a relative error of at most 0.0001.
Values sent between devices are 32-bit elements; how exact they have to be, the bound alone decides.
No kernel may reach another device: no remote copies, remote signals or barrier semaphores. Data moves between devices by JAX's collectives and lax.ppermute only.
A program may use at most 64 MiB of HBM per device.

v0:
```python
import jax
import jax.numpy as jnp
from jax import lax
from jax.sharding import PartitionSpec as P

HIGH = lax.Precision.HIGHEST


def descend(factor, terms, hadamard, weights):
    coupled = weights[:, None] * weights[None, :] * hadamard
    step_size = 1.0 / jnp.max(jnp.sum(jnp.abs(coupled), axis=1))
    product = jnp.dot(factor, coupled, precision=HIGH, preferred_element_type=jnp.float32)
    return factor - step_size * (product - terms * weights[None, :])


def rescale(moved, gram, row_count):
    scales = jnp.sqrt(jnp.diagonal(gram) / row_count + 1e-06)
    return (moved / scales[None, :], gram / (scales[:, None] * scales[None, :]), scales)


def local_gram(moved):
    return jnp.dot(moved.T, moved, precision=HIGH, preferred_element_type=jnp.float32)


def per_device(ensemble, voxel_factor, sample_factor, time_factor, weights):
    vox_rows, smp_rows, time_count = ensemble.shape
    rank_count = voxel_factor.shape[1]
    voxel_total = vox_rows * lax.axis_size("vox")
    sample_total = smp_rows * lax.axis_size("smp")
    vox_count = lax.axis_size("vox")
    flat = ensemble.reshape(vox_rows * smp_rows, time_count)
    gram_b = lax.psum(local_gram(sample_factor), "smp")
    gram_c = local_gram(time_factor)
    contracted = jnp.dot(flat, time_factor, precision=HIGH, preferred_element_type=jnp.float32)
    contracted = contracted.reshape(vox_rows, smp_rows, rank_count)
    partial_value = jnp.einsum("ijr,jr->ir", contracted, sample_factor, precision=HIGH)
    terms_a = lax.psum(partial_value, "smp")
    moved = descend(voxel_factor, terms_a, gram_b * gram_c, weights)
    raw_b = jnp.einsum("ijr,ir->jr", contracted, moved, precision=HIGH)
    gram, summed_b = lax.psum((local_gram(moved), raw_b), "vox")
    voxel_factor, gram_a, scales = rescale(moved, gram, voxel_total)
    terms_b = summed_b / scales[None, :]
    weights = weights * scales
    moved = descend(sample_factor, terms_b, gram_a * gram_c, weights)
    paired = (voxel_factor[:, None, :] * moved[None, :, :]).reshape(vox_rows * smp_rows, rank_count)
    raw_c = jnp.einsum("nk,nr->kr", flat, paired, precision=HIGH)
    gram_sum, summed_c = lax.psum((local_gram(moved), raw_c), ("vox", "smp"))
    sample_factor, gram_b, scales = rescale(moved, gram_sum / vox_count, sample_total)
    terms_c = summed_c / scales[None, :]
    weights = weights * scales
    moved = descend(time_factor, terms_c, gram_a * gram_b, weights)
    time_factor, gram_c, scales = rescale(moved, local_gram(moved), time_count)
    weights = weights * scales
    return (voxel_factor, sample_factor, time_factor, weights)


def solution(mesh):
    return jax.shard_map(
        per_device,
        mesh=mesh,
        in_specs=(P("vox", "smp", None), P("vox", None), P("smp", None), P(), P()),
        out_specs=(P("vox", None), P("smp", None), P(), P()),
        check_vma=False,
    )
```

profile of v0, /device:TPU:0, one launch (start us, length us, event | category | flops | bytes accessed | tf_op | source)
XLA Modules:
  0.0 262.1 jit_solution(2450352190232389603)
XLA Ops:
  7.2 0.0 copy-start.2
  7.2 0.0 all-reduce.10.cloned.1.call-start
  7.2 0.0 copy-start.6
  7.2 1.7 fusion.19
  8.9 0.0 copy-done.2
  8.9 0.0 copy-done.6
  8.9 2.2 multiply_reduce_fusion.1
  11.2 0.0 all-reduce.10.cloned.1.call-update
  11.2 0.0 all-reduce.6.cloned.1.call-start
  11.3 0.0 copy-start.9
  11.3 34.3 %all-reduce.10.cloned.1.call-done = (f32[128,128]{1,0:T(8,128)}, f32[128,128]{1,0:T(8,128)}) async-done(((f32[128,128]{1,0:T(8,128)}, f32[128,128]{1,0:T(8,128)}), (f32[128,128]{1,0:T(8,128)}, f32[128,128]{1,0:T(8,128)})) %all-reduce.10.cloned.1.call-update) | async-done | bytes 131088 | tf_op jit(solution)/shard_map/psum | solution.py:37
  45.6 0.0 copy-done.9
  45.6 1.3 abs_reduce_fusion.2
  46.8 0.6 reduce_max.27
  48.1 0.0 copy-done.5
  48.1 0.0 copy-done.7
  48.2 0.0 copy-done.8
  48.2 0.3 fusion.5
  48.5 0.9 fusion.20
  49.4 0.0 all-reduce.6.cloned.1.call-update
  49.4 0.0 all-reduce.8.cloned.1.call-start
  49.5 21.4 %psum.45 = f32[8,128]{1,0:T(8,128)S(1)} all-reduce(f32[8,128]{1,0:T(8,128)S(1)} %bitcast.61), channel_id=1, replica_groups=mesh['vox'=8,'smp'=4] {'vox'}, use_global_device_ids=true, to_apply=%region_7.8 | all-reduce | flops 1024 | bytes 8192 | tf_op jit(solution)/shard_map/psum | solution.py:40
  70.9 47.5 %all-reduce.6.cloned.1.call-done = f32[128,128]{1,0:T(8,128)} async-done(((f32[128,128]{1,0:T(8,128)}), f32[128,128]{1,0:T(8,128)}) %all-reduce.6.cloned.1.call-update) | async-done | bytes 65552 | tf_op jit(solution)/shard_map/psum | solution.py:40
  118.4 2.0 gather_fusion
  120.5 0.0 copy-done
  120.5 0.2 abs_reduce_fusion.1
  120.7 0.0 copy-start.3
  120.7 0.6 reduce_max.28
  122.0 0.2 fusion.8
  122.1 0.9 fusion.21
  123.1 0.0 copy-done.3
  123.1 0.1 copy.22
  123.2 0.0 copy-done.1
  123.2 1.8 convolution_bitcast_fusion
  124.9 0.0 all-reduce.8.cloned.1.call-update
  125.0 123.5 %all-reduce.8.cloned.1.call-done = (f32[128,128]{1,0:T(8,128)}, f32[128,128]{1,0:T(8,128)}) async-done(((f32[128,128]{1,0:T(8,128)}, f32[128,128]{1,0:T(8,128)}), (f32[128,128]{1,0:T(8,128)}, f32[128,128]{1,0:T(8,128)})) %all-reduce.8.cloned.1.call-update) | async-done | bytes 131088 | tf_op jit(solution)/shard_map/psum | solution.py:47
  248.5 0.8 broadcast_multiply_fusion
  249.3 1.2 gather_fusion.1
  250.6 0.6 broadcast_divide_fusion.2
  251.2 0.0 copy-done.4
  251.2 0.2 abs_reduce_fusion
  251.4 0.6 reduce_max.29
  252.7 0.0 copy-done.10
  252.7 0.2 fusion.2
  252.9 0.3 fusion.22
  253.2 1.2 gather_fusion.2
  254.4 0.5 fusion.18
  255.0 0.6 broadcast_divide_fusion
  (11 shorter events, 0.1 us)
Async XLA Ops:
  7.2 1.8 copy-start.2
  7.2 38.4 %all-reduce.10.cloned.1.call-start = ((), (), s32[]{:S(2)}) async-start(), calls=%async_computation.2 | async-start | bytes 262144 | tf_op jit(solution)/shard_map/psum | solution.py:37
  7.2 1.7 copy-start.6
  11.2 107.2 %all-reduce.6.cloned.1.call-start = ((), (), s32[]{:S(2)}) async-start(), calls=%async_computation | async-start | bytes 131072 | tf_op jit(solution)/shard_map/psum | solution.py:40
  11.3 34.3 %copy-start.9 = (f32[128]{0:T(128)S(1)}, f32[128]{0:T(128)}, u32[]{:S(2)}) copy-start(f32[128]{0:T(128)} %param.9) | copy-start | bytes 1540
  45.6 2.6 copy-start.5
  45.6 2.6 copy-start.7
  45.6 2.6 copy-start.8
  49.4 199.1 %all-reduce.8.cloned.1.call-start = ((), (), s32[]{:S(2)}) async-start(), calls=%async_computation.1 | async-start | bytes 262144 | tf_op jit(solution)/shard_map/psum | solution.py:47
  70.9 52.3 %copy-start.1 = (f32[128,8,128]{2,1,0:T(8,128)S(1)}, f32[128,8,128]{2,1,0:T(8,128)}, u32[]{:S(2)}) copy-start(f32[128,8,128]{2,1,0:T(8,128)} %param.5) | copy-start | bytes 1572868
  118.4 2.0 copy-start
  120.7 2.4 copy-start.3
  249.3 1.9 copy-start.4
  251.2 1.5 copy-start.10
Sparse Core Ops, SparseCore 0:
  11.3 34.1 all-reduce.9
  49.9 68.4 all-reduce.5
  125.7 122.7 all-reduce.7
where the time goes:
time: 263 us; the launch traced here: 262 us
  waiting for transfers between devices  205 us (78%)
  blocking collectives  21.4 us (8%)
  between operations  16 us (6%)
  matrix products  9.78 us (4%)
  other arithmetic  4.89 us (2%)
  local copies, waits for them, and re-layouts  4.63 us (2%)
    psum x1, waiting for transfers between devices, per_device(): gram_sum, summed_c = lax.psum((local_gram(moved), raw_c), ('vox', 'smp'))  123 us
    psum x1, waiting for transfers between devices, per_device(): gram, summed_b = lax.psum((local_gram(moved), raw_b), 'vox')  47.5 us
    psum x1, waiting for transfers between devices, per_device(): terms_a = lax.psum(partial_value, 'smp')  34.3 us
    psum x1, blocking collectives, per_device(): gram, summed_b = lax.psum((local_gram(moved), raw_b), 'vox')  21.4 us
  transfers between devices with their start and end apart: 3, of which 3 were waited for; matrix products, arithmetic and copies ran while one was open for 0% of the time, Pallas kernels for 0%

commit v1 on v0

--- a/solution.py
+++ b/solution.py
@@ -4,6 +4,24 @@
 from jax.sharding import PartitionSpec as P
 
 HIGH = lax.Precision.HIGHEST
+
+
+def exchange_sum(values, axes, bits_per_round):
+    count = lax.axis_size(axes)
+    if count & (count - 1):
+        return lax.psum(values, axes)
+    low = 1
+    while low < count:
+        width = min(bits_per_round, (count // low).bit_length() - 1)
+        parts = [values]
+        for pattern in range(1, 1 << width):
+            pairs = [(i, i ^ (pattern * low)) for i in range(count)]
+            parts.append(lax.ppermute(values, axes, pairs))
+        while len(parts) > 1:
+            parts = [a + b for a, b in zip(parts[::2], parts[1::2])]
+        values = parts[0]
+        low <<= width
+    return values
 
 
 def descend(factor, terms, hadamard, weights):
@@ -13,8 +31,13 @@
     return factor - step_size * (product - terms * weights[None, :])
 
 
+def scales_of(moved_gram, row_count):
+    eye = jnp.eye(moved_gram.shape[0], dtype=jnp.float32)
+    return jnp.sqrt(jnp.sum(moved_gram * eye, axis=0) / row_count + 1e-06)
+
+
 def rescale(moved, gram, row_count):
-    scales = jnp.sqrt(jnp.diagonal(gram) / row_count + 1e-06)
+    scales = scales_of(gram, row_count)
     return (moved / scales[None, :], gram / (scales[:, None] * scales[None, :]), scales)
 
 
@@ -29,22 +52,24 @@
     sample_total = smp_rows * lax.axis_size("smp")
     vox_count = lax.axis_size("vox")
     flat = ensemble.reshape(vox_rows * smp_rows, time_count)
-    gram_b = lax.psum(local_gram(sample_factor), "smp")
     gram_c = local_gram(time_factor)
     contracted = jnp.dot(flat, time_factor, precision=HIGH, preferred_element_type=jnp.float32)
     contracted = contracted.reshape(vox_rows, smp_rows, rank_count)
     partial_value = jnp.einsum("ijr,jr->ir", contracted, sample_factor, precision=HIGH)
-    terms_a = lax.psum(partial_value, "smp")
+    both = exchange_sum(jnp.concatenate([partial_value, local_gram(sample_factor)], axis=0), "smp", 2)
+    terms_a, gram_b = both[:vox_rows], both[vox_rows:]
     moved = descend(voxel_factor, terms_a, gram_b * gram_c, weights)
     raw_b = jnp.einsum("ijr,ir->jr", contracted, moved, precision=HIGH)
-    gram, summed_b = lax.psum((local_gram(moved), raw_b), "vox")
+    both = exchange_sum(jnp.concatenate([local_gram(moved), raw_b], axis=0), "vox", 1)
+    gram, summed_b = both[:rank_count], both[rank_count:]
     voxel_factor, gram_a, scales = rescale(moved, gram, voxel_total)
     terms_b = summed_b / scales[None, :]
     weights = weights * scales
     moved = descend(sample_factor, terms_b, gram_a * gram_c, weights)
     paired = (voxel_factor[:, None, :] * moved[None, :, :]).reshape(vox_rows * smp_rows, rank_count)
     raw_c = jnp.einsum("nk,nr->kr", flat, paired, precision=HIGH)
-    gram_sum, summed_c = lax.psum((local_gram(moved), raw_c), ("vox", "smp"))
+    both = exchange_sum(jnp.concatenate([raw_c, local_gram(moved)], axis=0), ("vox", "smp"), 1)
+    summed_c, gram_sum = both[:time_count], both[time_count:]
     sample_factor, gram_b, scales = rescale(moved, gram_sum / vox_count, sample_total)
     terms_c = summed_c / scales[None, :]
     weights = weights * scales

time: 263 us -> 60.3 us (0.23)
  waiting for transfers between devices: 205 us -> 28 us
  blocking collectives: 21.4 us -> 0 us
  starting transfers between devices: 0.12 us -> 18 us
  between operations: 16 us -> 2.9 us
  matrix products: 9.78 us -> 4.69 us
  local copies, waits for them, and re-layouts: 4.63 us -> 1.92 us
    psum x3 -> x0, waiting for transfers between devices: 205 us -> none  [the longest x1 123 us: per_device(): gram_sum, summed_c = lax.psum((local_gram(moved), raw_c), ('vox', 'smp'))]
    ppermute x0 -> x11, waiting for transfers between devices: none -> 28 us  [exchange_sum(): parts.append(lax.ppermute(values, axes, pairs))]
    psum x1 -> x0, blocking collectives: 21.4 us -> none  [per_device(): gram, summed_b = lax.psum((local_gram(moved), raw_b), 'vox')]
    ppermute x0 -> x11, starting transfers between devices: none -> 18 us  [exchange_sum(): parts.append(lax.ppermute(values, axes, pairs))]
    gather x3 -> x0, local copies, waits for them, and re-layouts: 4.5 us -> none  [rescale(): scales = jnp.sqrt(jnp.diagonal(gram) / row_count + 1e-06)]
    dot_general x5, matrix products: 5.11 us -> 2.31 us  [local_gram(): jnp.dot(moved.T, moved, precision=HIGH, preferred_element_type=jnp.float32)]
  transfers between devices with their start and end apart: 3 -> 11, of which waited for: 3 -> 10; matrix products, arithmetic and copies ran while one was open for 0% -> 0% of each run, Pallas kernels for 0% -> 0%
where the time goes in v1:
time: 60.3 us; the launch traced here: 59.9 us
  waiting for transfers between devices  28 us (46%)
  starting transfers between devices  18 us (30%)
  matrix products  4.69 us (8%)
  other arithmetic  4.3 us (7%)
  between operations  2.9 us (5%)
  local copies, waits for them, and re-layouts  1.92 us (3%)
    ppermute x11, waiting for transfers between devices, exchange_sum(): parts.append(lax.ppermute(values, axes, pairs))  28 us
    ppermute x11, starting transfers between devices, exchange_sum(): parts.append(lax.ppermute(values, axes, pairs))  18 us
    dot_general x5, matrix products, local_gram(): jnp.dot(moved.T, moved, precision=HIGH, preferred_element_type=jnp.float32)  2.31 us
    unnamed x11, local copies, waits for them, and re-layouts  1.92 us
    reduce_max x3, other arithmetic, descend(): step_size = 1.0 / jnp.max(jnp.sum(jnp.abs(coupled), axis=1))  1.82 us
    div x2, other arithmetic, rescale(): moved / scales[None, :]  1.25 us
  transfers between devices with their start and end apart: 11, of which 10 were waited for; matrix products, arithmetic and copies ran while one was open for 0% of the time, Pallas kernels for 0%

profile of v1, /device:TPU:0, one launch (start us, length us, event | category | flops | bytes accessed | tf_op | source)
XLA Modules:
  0.0 59.9 jit_solution(11986637346114136531)
XLA Ops:
  0.6 1.0 %fusion.26 = f32[128,128]{1,0:T(8,128)S(1)} fusion(f32[8,128]{1,0:T(8,128)} %param.7), kind=kOutput, calls=%fused_computation.54 | convolution fusion | flops 1572864 | bytes 69632 | tf_op jit(solution)/shard_map/dot_general | solution.py:45
  1.7 0.0 copy-start
  1.7 0.0 copy-start.3
  1.7 1.3 %copy.13 = f32[128,8,128]{0,2,1:T(8,128)S(1)} copy(f32[128,8,128]{2,1,0:T(8,128)} %param.5) | data formatting | bytes 1048576 | tf_op args[0]
  3.0 0.0 copy-done
  3.0 0.0 copy-done.3
  3.0 1.0 %multiply_reduce_fusion.1 = (f32[128,128]{0,1:T(8,128)S(1)}, f32[128,8,128]{2,0,1:T(8,128)S(1)}) fusion(f32[128,8]{0,1:T(8,128)S(1)} %bitcast.50, f32[128,8,128]{0,2,1:T(8,128)S(1)} %copy.13, f32[128,128]{1,0:T(8,128)S(1)} %copy-done), kind=kOutput, calls=%fused_computation.7 | convolution fusion | flops 201572352 | bytes 1183744 | tf_op jit(solution)/shard_map/dot_general | solution.py:56
  4.0 3.0 %collective-permute-start.1 = (f32[256,128]{1,0:T(8,128)S(1)}, f32[256,128]{1,0:T(8,128)S(1)}, u32[]{:S(2)}, u32[]{:S(2)}) collective-permute-start(f32[256,128]{1,0:T(8,128)S(1)} %pad_maximum_fusion), channel_id=1, source_target_pairs={{0,2},{1,3},{2,0},{3,1},{4,6},{5,7},{6,4},{7,5},{8,10},{9,11},{10,... | collective-permute-start | bytes 393224 | tf_op jit(solution)/shard_map/ppermute | solution.py:19
  7.1 0.0 collective-permute-start.2
  7.1 0.2 collective-permute-start
  7.3 3.7 %collective-permute-done.1 = f32[256,128]{1,0:T(8,128)S(1)} collective-permute-done((f32[256,128]{1,0:T(8,128)S(1)}, f32[256,128]{1,0:T(8,128)S(1)}, u32[]{:S(2)}, u32[]{:S(2)}) %collective-permute-start.1) | collective-permute-done | bytes 131104 | tf_op jit(solution)/shard_map/ppermute | solution.py:19
  11.0 1.9 %collective-permute-done.2 = f32[256,128]{1,0:T(8,128)S(1)} collective-permute-done((f32[256,128]{1,0:T(8,128)S(1)}, f32[256,128]{1,0:T(8,128)S(1)}, u32[]{:S(2)}, u32[]{:S(2)}) %collective-permute-start.2) | collective-permute-done | bytes 131104 | tf_op jit(solution)/shard_map/ppermute | solution.py:19
  12.9 0.0 collective-permute-done
  13.0 0.6 %copy-done.4 = f32[128]{0:T(128)S(1)} copy-done((f32[128]{0:T(128)S(1)}, f32[128]{0:T(128)}, u32[]{:S(2)}) %copy-start.4) | copy-done | bytes 536
  13.6 0.4 abs_reduce_fusion.2
  13.9 0.6 %reduce_max.27 = f32[]{:T(128)} reduce(f32[128]{0:T(128)S(1)} %get-tuple-element.16, f32[]{:T(128)} %constant.17.clone.1), dimensions={0}, to_apply=%region_1.0 | reduce | flops 127 | bytes 520 | tf_op jit(solution)/shard_map/reduce_max | solution.py:29
  15.2 0.0 copy-done.2
  15.3 0.3 fusion.10
  15.5 0.3 fusion.27
  15.9 1.5 %collective-permute-start.3 = (f32[136,128]{1,0:T(8,128)S(1)}, f32[136,128]{1,0:T(8,128)S(1)}, u32[]{:S(2)}, u32[]{:S(2)}) collective-permute-start(f32[136,128]{1,0:T(8,128)S(1)} %pad_maximum_fusion.2), channel_id=1, source_target_pairs={{0,4},{4,0},{8,12},{12,8},{16,20},{20,16},{24,28},{28,24},{1,5},{5... | collective-permute-start | bytes 208904 | tf_op jit(solution)/shard_map/ppermute | solution.py:19
  17.4 2.9 %collective-permute-done.3 = f32[136,128]{1,0:T(8,128)S(1)} collective-permute-done((f32[136,128]{1,0:T(8,128)S(1)}, f32[136,128]{1,0:T(8,128)S(1)}, u32[]{:S(2)}, u32[]{:S(2)}) %collective-permute-start.3) | collective-permute-done | bytes 69664 | tf_op jit(solution)/shard_map/ppermute | solution.py:19
  20.3 1.9 %collective-permute-start.4 = (f32[136,128]{1,0:T(8,128)S(1)}, f32[136,128]{1,0:T(8,128)S(1)}, u32[]{:S(2)}, u32[]{:S(2)}) collective-permute-start(f32[136,128]{1,0:T(8,128)S(1)} %fusion.24), channel_id=1, source_target_pairs={{0,8},{4,12},{8,0},{12,4},{16,24},{20,28},{24,16},{28,20},{1,9},{5... | collective-permute-start | bytes 208904 | tf_op jit(solution)/shard_map/ppermute | solution.py:19
  22.2 2.5 %collective-permute-done.4 = f32[136,128]{1,0:T(8,128)S(1)} collective-permute-done((f32[136,128]{1,0:T(8,128)S(1)}, f32[136,128]{1,0:T(8,128)S(1)}, u32[]{:S(2)}, u32[]{:S(2)}) %collective-permute-start.4) | collective-permute-done | bytes 69664 | tf_op jit(solution)/shard_map/ppermute | solution.py:19
  24.7 2.9 %collective-permute-start.5 = (f32[136,128]{1,0:T(8,128)S(1)}, f32[136,128]{1,0:T(8,128)S(1)}, u32[]{:S(2)}, u32[]{:S(2)}) collective-permute-start(f32[136,128]{1,0:T(8,128)S(1)} %add.66), channel_id=1, source_target_pairs={{0,16},{4,20},{8,24},{12,28},{16,0},{20,4},{24,8},{28,12},{1,17},{... | collective-permute-start | bytes 208904 | tf_op jit(solution)/shard_map/ppermute | solution.py:19
  27.6 2.4 %collective-permute-done.5 = f32[136,128]{1,0:T(8,128)S(1)} collective-permute-done((f32[136,128]{1,0:T(8,128)S(1)}, f32[136,128]{1,0:T(8,128)S(1)}, u32[]{:S(2)}, u32[]{:S(2)}) %collective-permute-start.5) | collective-permute-done | bytes 69664 | tf_op jit(solution)/shard_map/ppermute | solution.py:19
  30.1 0.2 abs_reduce_fusion.1
  30.3 0.0 copy-start.1
  30.3 0.6 %reduce_max.28 = f32[]{:T(128)} reduce(f32[128]{0:T(128)S(1)} %get-tuple-element.10, f32[]{:T(128)} %constant.17.clone.1), dimensions={0}, to_apply=%region_4.0 | reduce | flops 127 | bytes 520 | tf_op jit(solution)/shard_map/reduce_max | solution.py:29
  31.6 0.2 fusion.16
  31.8 0.3 fusion.28
  32.1 0.7 %convolution_bitcast_fusion.1 = f32[128,128]{1,0:T(8,128)S(1)} fusion(f32[128,8,128]{0,2,1:T(8,128)S(1)} %copy.13, f32[8,128]{1,0:T(8,128)S(1)} %fusion.16, f32[128,128]{1,0:T(8,128)S(1)} %get-tuple-element.11), kind=kOutput, calls=%fused_computation.2 | convolution fusion | flops 201457664 | bytes 659456 | tf_op jit(solution)/shard_map/nk,nr->kr/dot_general | solution.py:70
  32.8 0.1 collective-permute-start.6
  32.9 1.3 %collective-permute-done.6 = f32[256,128]{1,0:T(8,128)S(1)} collective-permute-done((f32[256,128]{1,0:T(8,128)S(1)}, f32[256,128]{1,0:T(8,128)S(1)}, u32[]{:S(2)}, u32[]{:S(2)}) %collective-permute-start.6) | collective-permute-done | bytes 131104 | tf_op jit(solution)/shard_map/ppermute | solution.py:19
  34.2 1.8 %collective-permute-start.7 = (f32[256,128]{1,0:T(8,128)S(1)}, f32[256,128]{1,0:T(8,128)S(1)}, u32[]{:S(2)}, u32[]{:S(2)}) collective-permute-start(f32[256,128]{1,0:T(8,128)S(1)} %fusion.25), channel_id=1, source_target_pairs={{0,2},{1,3},{2,0},{3,1},{4,6},{5,7},{6,4},{7,5},{8,10},{9,11},{10,... | collective-permute-start | bytes 393224 | tf_op jit(solution)/shard_map/ppermute | solution.py:19
  36.0 3.8 %collective-permute-done.7 = f32[256,128]{1,0:T(8,128)S(1)} collective-permute-done((f32[256,128]{1,0:T(8,128)S(1)}, f32[256,128]{1,0:T(8,128)S(1)}, u32[]{:S(2)}, u32[]{:S(2)}) %collective-permute-start.7) | collective-permute-done | bytes 131104 | tf_op jit(solution)/shard_map/ppermute | solution.py:19
  39.9 1.8 %collective-permute-start.8 = (f32[256,128]{1,0:T(8,128)S(1)}, f32[256,128]{1,0:T(8,128)S(1)}, u32[]{:S(2)}, u32[]{:S(2)}) collective-permute-start(f32[256,128]{1,0:T(8,128)S(1)} %add.70), channel_id=1, source_target_pairs={{0,4},{1,5},{2,6},{3,7},{4,0},{5,1},{6,2},{7,3},{8,12},{9,13},{10,... | collective-permute-start | bytes 393224 | tf_op jit(solution)/shard_map/ppermute | solution.py:19
  41.7 3.3 %collective-permute-done.8 = f32[256,128]{1,0:T(8,128)S(1)} collective-permute-done((f32[256,128]{1,0:T(8,128)S(1)}, f32[256,128]{1,0:T(8,128)S(1)}, u32[]{:S(2)}, u32[]{:S(2)}) %collective-permute-start.8) | collective-permute-done | bytes 131104 | tf_op jit(solution)/shard_map/ppermute | solution.py:19
  44.9 1.9 %collective-permute-start.9 = (f32[256,128]{1,0:T(8,128)S(1)}, f32[256,128]{1,0:T(8,128)S(1)}, u32[]{:S(2)}, u32[]{:S(2)}) collective-permute-start(f32[256,128]{1,0:T(8,128)S(1)} %add.71), channel_id=1, source_target_pairs={{0,8},{1,9},{2,10},{3,11},{4,12},{5,13},{6,14},{7,15},{8,0},{9,1},... | collective-permute-start | bytes 393224 | tf_op jit(solution)/shard_map/ppermute | solution.py:19
  46.8 3.2 %collective-permute-done.9 = f32[256,128]{1,0:T(8,128)S(1)} collective-permute-done((f32[256,128]{1,0:T(8,128)S(1)}, f32[256,128]{1,0:T(8,128)S(1)}, u32[]{:S(2)}, u32[]{:S(2)}) %collective-permute-start.9) | collective-permute-done | bytes 131104 | tf_op jit(solution)/shard_map/ppermute | solution.py:19
  50.0 3.1 %collective-permute-start.10 = (f32[256,128]{1,0:T(8,128)S(1)}, f32[256,128]{1,0:T(8,128)S(1)}, u32[]{:S(2)}, u32[]{:S(2)}) collective-permute-start(f32[256,128]{1,0:T(8,128)S(1)} %add.72), channel_id=1, source_target_pairs={{0,16},{1,17},{2,18},{3,19},{4,20},{5,21},{6,22},{7,23},{8,24},{9,... | collective-permute-start | bytes 393224 | tf_op jit(solution)/shard_map/ppermute | solution.py:19
  53.0 2.9 %collective-permute-done.10 = f32[256,128]{1,0:T(8,128)S(1)} collective-permute-done((f32[256,128]{1,0:T(8,128)S(1)}, f32[256,128]{1,0:T(8,128)S(1)}, u32[]{:S(2)}, u32[]{:S(2)}) %collective-permute-start.10) | collective-permute-done | bytes 131104 | tf_op jit(solution)/shard_map/ppermute | solution.py:19
  56.1 0.6 %broadcast_divide_fusion.2 = f32[8,128]{1,0:T(8,128)} fusion(f32[8,128]{1,0:T(8,128)S(1)} %fusion.16, f32[128]{0:T(128)S(1)} %get-tuple-element.9), kind=kLoop, calls=%fused_computation.45 | loop fusion | flops 1024 | bytes 8704 | tf_op jit(solution)/shard_map/div | solution.py:41
  56.7 0.2 abs_reduce_fusion
  56.9 0.6 %reduce_max.29 = f32[]{:T(128)} reduce(f32[128]{0:T(128)S(1)} %get-tuple-element.4, f32[]{:T(128)} %constant.17.clone.1), dimensions={0}, to_apply=%region_7.0 | reduce | flops 127 | bytes 520 | tf_op jit(solution)/shard_map/reduce_max | solution.py:29
  58.2 0.2 fusion.7
  58.4 0.3 fusion
  58.7 0.5 fusion.23
  59.2 0.6 %broadcast_divide_fusion = f32[128,128]{1,0:T(8,128)} fusion(f32[128,128]{1,0:T(8,128)S(1)} %fusion.7, f32[128]{0:T(128)S(1)} %get-tuple-element.7), kind=kLoop, calls=%fused_computation.38 | loop fusion | flops 16384 | bytes 131584 | tf_op jit(solution)/shard_map/div | solution.py:41
  (20 shorter events, 0.3 us)
Async XLA Ops:
  1.7 1.3 %copy-start = (f32[128,128]{1,0:T(8,128)S(1)}, f32[128,128]{1,0:T(8,128)}, u32[]{:S(2)}) copy-start(f32[128,128]{1,0:T(8,128)} %param.8) | copy-start | bytes 196612
  1.7 1.3 %copy-start.3 = (f32[8,128]{1,0:T(8,128)S(1)}, f32[8,128]{1,0:T(8,128)}, u32[]{:S(2)}) copy-start(f32[8,128]{1,0:T(8,128)} %param.7) | copy-start | bytes 12292
  4.0 7.0 %collective-permute-start.1 = (f32[256,128]{1,0:T(8,128)S(1)}, f32[256,128]{1,0:T(8,128)S(1)}, u32[]{:S(2)}, u32[]{:S(2)}) collective-permute-start(f32[256,128]{1,0:T(8,128)S(1)} %pad_maximum_fusion), channel_id=1, source_target_pairs={{0,2},{1,3},{2,0},{3,1},{4,6},{5,7},{6,4},{7,5},{8,10},{9,11},{10,... | collective-permute-start | bytes 393224 | tf_op jit(solution)/shard_map/ppermute | solution.py:19
  7.1 5.9 %collective-permute-start.2 = (f32[256,128]{1,0:T(8,128)S(1)}, f32[256,128]{1,0:T(8,128)S(1)}, u32[]{:S(2)}, u32[]{:S(2)}) collective-permute-start(f32[256,128]{1,0:T(8,128)S(1)} %pad_maximum_fusion), channel_id=1, source_target_pairs={{0,3},{1,2},{2,1},{3,0},{4,7},{5,6},{6,5},{7,4},{8,11},{9,10},{10,... | collective-permute-start | bytes 393224 | tf_op jit(solution)/shard_map/ppermute | solution.py:19
  7.1 5.9 %collective-permute-start = (f32[256,128]{1,0:T(8,128)S(1)}, f32[256,128]{1,0:T(8,128)S(1)}, u32[]{:S(2)}, u32[]{:S(2)}) collective-permute-start(f32[256,128]{1,0:T(8,128)S(1)} %pad_maximum_fusion), channel_id=1, source_target_pairs={{0,1},{1,0},{2,3},{3,2},{4,5},{5,4},{6,7},{7,6},{8,9},{9,8},{10,11... | collective-permute-start | bytes 393224 | tf_op jit(solution)/shard_map/ppermute | solution.py:19
  12.9 0.7 %copy-start.4 = (f32[128]{0:T(128)S(1)}, f32[128]{0:T(128)}, u32[]{:S(2)}) copy-start(f32[128]{0:T(128)} %param.9) | copy-start | bytes 1540
  13.6 1.7 %copy-start.2 = (f32[128,128]{1,0:T(8,128)S(1)}, f32[128,128]{1,0:T(8,128)}, u32[]{:S(2)}) copy-start(f32[128,128]{1,0:T(8,128)} %param.6) | copy-start | bytes 196612
  15.9 4.4 %collective-permute-start.3 = (f32[136,128]{1,0:T(8,128)S(1)}, f32[136,128]{1,0:T(8,128)S(1)}, u32[]{:S(2)}, u32[]{:S(2)}) collective-permute-start(f32[136,128]{1,0:T(8,128)S(1)} %pad_maximum_fusion.2), channel_id=1, source_target_pairs={{0,4},{4,0},{8,12},{12,8},{16,20},{20,16},{24,28},{28,24},{1,5},{5... | collective-permute-start | bytes 208904 | tf_op jit(solution)/shard_map/ppermute | solution.py:19
  20.3 4.4 %collective-permute-start.4 = (f32[136,128]{1,0:T(8,128)S(1)}, f32[136,128]{1,0:T(8,128)S(1)}, u32[]{:S(2)}, u32[]{:S(2)}) collective-permute-start(f32[136,128]{1,0:T(8,128)S(1)} %fusion.24), channel_id=1, source_target_pairs={{0,8},{4,12},{8,0},{12,4},{16,24},{20,28},{24,16},{28,20},{1,9},{5... | collective-permute-start | bytes 208904 | tf_op jit(solution)/shard_map/ppermute | solution.py:19
  24.7 5.3 %collective-permute-start.5 = (f32[136,128]{1,0:T(8,128)S(1)}, f32[136,128]{1,0:T(8,128)S(1)}, u32[]{:S(2)}, u32[]{:S(2)}) collective-permute-start(f32[136,128]{1,0:T(8,128)S(1)} %add.66), channel_id=1, source_target_pairs={{0,16},{4,20},{8,24},{12,28},{16,0},{20,4},{24,8},{28,12},{1,17},{... | collective-permute-start | bytes 208904 | tf_op jit(solution)/shard_map/ppermute | solution.py:19
  30.3 1.9 %copy-start.1 = (f32[128,128]{1,0:T(8,128)}, f32[128,128]{1,0:T(8,128)S(1)}, u32[]{:S(2)}) copy-start(f32[128,128]{1,0:T(8,128)S(1)} %get-tuple-element.11) | copy-start | bytes 196612
  32.8 1.4 %collective-permute-start.6 = (f32[256,128]{1,0:T(8,128)S(1)}, f32[256,128]{1,0:T(8,128)S(1)}, u32[]{:S(2)}, u32[]{:S(2)}) collective-permute-start(f32[256,128]{1,0:T(8,128)S(1)} %pad_maximum_fusion.1), channel_id=1, source_target_pairs={{0,1},{1,0},{2,3},{3,2},{4,5},{5,4},{6,7},{7,6},{8,9},{9,8},{10,11... | collective-permute-start | bytes 393224 | tf_op jit(solution)/shard_map/ppermute | solution.py:19
  34.2 5.6 %collective-permute-start.7 = (f32[256,128]{1,0:T(8,128)S(1)}, f32[256,128]{1,0:T(8,128)S(1)}, u32[]{:S(2)}, u32[]{:S(2)}) collective-permute-start(f32[256,128]{1,0:T(8,128)S(1)} %fusion.25), channel_id=1, source_target_pairs={{0,2},{1,3},{2,0},{3,1},{4,6},{5,7},{6,4},{7,5},{8,10},{9,11},{10,... | collective-permute-start | bytes 393224 | tf_op jit(solution)/shard_map/ppermute | solution.py:19
  39.9 5.0 %collective-permute-start.8 = (f32[256,128]{1,0:T(8,128)S(1)}, f32[256,128]{1,0:T(8,128)S(1)}, u32[]{:S(2)}, u32[]{:S(2)}) collective-permute-start(f32[256,128]{1,0:T(8,128)S(1)} %add.70), channel_id=1, source_target_pairs={{0,4},{1,5},{2,6},{3,7},{4,0},{5,1},{6,2},{7,3},{8,12},{9,13},{10,... | collective-permute-start | bytes 393224 | tf_op jit(solution)/shard_map/ppermute | solution.py:19
  44.9 5.0 %collective-permute-start.9 = (f32[256,128]{1,0:T(8,128)S(1)}, f32[256,128]{1,0:T(8,128)S(1)}, u32[]{:S(2)}, u32[]{:S(2)}) collective-permute-start(f32[256,128]{1,0:T(8,128)S(1)} %add.71), channel_id=1, source_target_pairs={{0,8},{1,9},{2,10},{3,11},{4,12},{5,13},{6,14},{7,15},{8,0},{9,1},... | collective-permute-start | bytes 393224 | tf_op jit(solution)/shard_map/ppermute | solution.py:19
  50.0 6.0 %collective-permute-start.10 = (f32[256,128]{1,0:T(8,128)S(1)}, f32[256,128]{1,0:T(8,128)S(1)}, u32[]{:S(2)}, u32[]{:S(2)}) collective-permute-start(f32[256,128]{1,0:T(8,128)S(1)} %add.72), channel_id=1, source_target_pairs={{0,16},{1,17},{2,18},{3,19},{4,20},{5,21},{6,22},{7,23},{8,24},{9,... | collective-permute-start | bytes 393224 | tf_op jit(solution)/shard_map/ppermute | solution.py:19

commit v2 on v1

--- a/solution.py
+++ b/solution.py
@@ -22,6 +22,16 @@
         values = parts[0]
         low <<= width
     return values
+
+
+def scatter_sum(values, axes):
+    count = lax.axis_size(axes)
+    rows, columns = values.shape
+    if rows % count:
+        return exchange_sum(values, axes, 1)
+    pieces = values.reshape(count, rows // count, columns)
+    held = jnp.sum(lax.all_to_all(pieces, axes, 0, 0), axis=0)
+    return lax.all_to_all(jnp.broadcast_to(held, pieces.shape), axes, 0, 0).reshape(rows, columns)
 
 
 def descend(factor, terms, hadamard, weights):
@@ -56,11 +66,11 @@
     contracted = jnp.dot(flat, time_factor, precision=HIGH, preferred_element_type=jnp.float32)
     contracted = contracted.reshape(vox_rows, smp_rows, rank_count)
     partial_value = jnp.einsum("ijr,jr->ir", contracted, sample_factor, precision=HIGH)
-    both = exchange_sum(jnp.concatenate([partial_value, local_gram(sample_factor)], axis=0), "smp", 2)
+    both = exchange_sum(jnp.concatenate([partial_value, local_gram(sample_factor)], axis=0), "smp", 1)
     terms_a, gram_b = both[:vox_rows], both[vox_rows:]
     moved = descend(voxel_factor, terms_a, gram_b * gram_c, weights)
     raw_b = jnp.einsum("ijr,ir->jr", contracted, moved, precision=HIGH)
-    both = exchange_sum(jnp.concatenate([local_gram(moved), raw_b], axis=0), "vox", 1)
+    both = scatter_sum(jnp.concatenate([local_gram(moved), raw_b], axis=0), "vox")
     gram, summed_b = both[:rank_count], both[rank_count:]
     voxel_factor, gram_a, scales = rescale(moved, gram, voxel_total)
     terms_b = summed_b / scales[None, :]
@@ -68,7 +78,7 @@
     moved = descend(sample_factor, terms_b, gram_a * gram_c, weights)
     paired = (voxel_factor[:, None, :] * moved[None, :, :]).reshape(vox_rows * smp_rows, rank_count)
     raw_c = jnp.einsum("nk,nr->kr", flat, paired, precision=HIGH)
-    both = exchange_sum(jnp.concatenate([raw_c, local_gram(moved)], axis=0), ("vox", "smp"), 1)
+    both = scatter_sum(jnp.concatenate([raw_c, local_gram(moved)], axis=0), ("vox", "smp"))
     summed_c, gram_sum = both[:time_count], both[time_count:]
     sample_factor, gram_b, scales = rescale(moved, gram_sum / vox_count, sample_total)
     terms_c = summed_c / scales[None, :]

time: 60.3 us -> 66.4 us (1.10)
  blocking collectives: 0 us -> 32.8 us
  waiting for transfers between devices: 28 us -> 13 us
  starting transfers between devices: 18 us -> 6.03 us
  local copies, waits for them, and re-layouts: 1.92 us -> 3.11 us
  matrix products: 4.69 us -> 3.93 us
    all_to_all x0 -> x3, blocking collectives: none -> 32.8 us  [the longest x2 23.2 us: scatter_sum(): held = jnp.sum(lax.all_to_all(pieces, axes, 0, 0), axis=0)]
    ppermute x11 -> x2, waiting for transfers between devices: 28 us -> 4.8 us  [exchange_sum(): parts.append(lax.ppermute(values, axes, pairs))]
    ppermute x11 -> x2, starting transfers between devices: 18 us -> 3.46 us  [exchange_sum(): parts.append(lax.ppermute(values, axes, pairs))]
    all_to_all x0 -> x1, waiting for transfers between devices: none -> 8.22 us  [scatter_sum(): lax.all_to_all(jnp.broadcast_to(held, pieces.shape), axes, 0, 0)]
    all_to_all x0 -> x1, starting transfers between devices: none -> 2.57 us  [scatter_sum(): lax.all_to_all(jnp.broadcast_to(held, pieces.shape), axes, 0, 0)]
    dot_general x5, matrix products: 2.31 us -> 1.54 us  [local_gram(): jnp.dot(moved.T, moved, precision=HIGH, preferred_element_type=jnp.float32)]
  transfers between devices with their start and end apart: 11 -> 3, of which waited for: 10 -> 3; matrix products, arithmetic and copies ran while one was open for 0% -> 0% of each run, Pallas kernels for 0% -> 0%
where the time goes in v2:
time: 66.4 us; the launch traced here: 66 us
  blocking collectives  32.8 us (49%)
  waiting for transfers between devices  13 us (20%)
  starting transfers between devices  6.03 us (9%)
  other arithmetic  4.31 us (6%)
  matrix products  3.93 us (6%)
  local copies, waits for them, and re-layouts  3.11 us (5%)
  between operations  2.9 us (4%)
    all_to_all x2, blocking collectives, scatter_sum(): held = jnp.sum(lax.all_to_all(pieces, axes, 0, 0), axis=0)  23.2 us
    all_to_all x1, blocking collectives, scatter_sum(): lax.all_to_all(jnp.broadcast_to(held, pieces.shape), axes, 0, 0)  9.51 us
    all_to_all x1, waiting for transfers between devices, scatter_sum(): lax.all_to_all(jnp.broadcast_to(held, pieces.shape), axes, 0, 0)  8.22 us
    ppermute x2, waiting for transfers between devices, exchange_sum(): parts.append(lax.ppermute(values, axes, pairs))  4.8 us
    ppermute x2, starting transfers between devices, exchange_sum(): parts.append(lax.ppermute(values, axes, pairs))  3.46 us
    all_to_all x1, starting transfers between devices, scatter_sum(): lax.all_to_all(jnp.broadcast_to(held, pieces.shape), axes, 0, 0)  2.57 us
    unnamed x11, local copies, waits for them, and re-layouts  2.44 us
    reduce_max x3, other arithmetic, descend(): step_size = 1.0 / jnp.max(jnp.sum(jnp.abs(coupled), axis=1))  1.82 us
  transfers between devices with their start and end apart: 3, of which 3 were waited for; matrix products, arithmetic and copies ran while one was open for 0% of the time, Pallas kernels for 0%

profile of v2, /device:TPU:0, one launch (start us, length us, event | category | flops | bytes accessed | tf_op | source)
XLA Modules:
  0.0 66.0 jit_solution(7435787305003628430)
XLA Ops:
  0.6 0.0 copy-start.3
  0.6 1.2 %copy.19 = f32[128,8,128]{0,2,1:T(8,128)S(1)} copy(f32[128,8,128]{2,1,0:T(8,128)} %param.5) | data formatting | bytes 1048576 | tf_op args[0]
  1.9 0.0 copy-done.3
  1.9 0.0 copy-start
  1.9 0.3 fusion.27
  2.2 0.5 copy-done
  2.7 1.0 %multiply_reduce_fusion.1 = (f32[128,128]{0,1:T(8,128)S(1)}, f32[128,8,128]{2,0,1:T(8,128)S(1)}) fusion(f32[128,8]{0,1:T(8,128)S(1)} %bitcast.77, f32[128,8,128]{0,2,1:T(8,128)S(1)} %copy.19, f32[128,128]{1,0:T(8,128)S(1)} %copy-done), kind=kOutput, calls=%fused_computation.16 | convolution fusion | flops 201572352 | bytes 1183744 | tf_op jit(solution)/shard_map/dot_general | solution.py:66
  3.8 0.5 collective-permute-start
  4.3 1.0 %collective-permute-done = f32[256,128]{1,0:T(8,128)S(1)} collective-permute-done((f32[256,128]{1,0:T(8,128)S(1)}, f32[256,128]{1,0:T(8,128)S(1)}, u32[]{:S(2)}, u32[]{:S(2)}) %collective-permute-start) | collective-permute-done | bytes 131104 | tf_op jit(solution)/shard_map/ppermute | solution.py:19
  5.3 2.9 %collective-permute-start.1 = (f32[256,128]{1,0:T(8,128)S(1)}, f32[256,128]{1,0:T(8,128)S(1)}, u32[]{:S(2)}, u32[]{:S(2)}) collective-permute-start(f32[256,128]{1,0:T(8,128)S(1)} %fusion.25), channel_id=1, source_target_pairs={{0,2},{1,3},{2,0},{3,1},{4,6},{5,7},{6,4},{7,5},{8,10},{9,11},{10,... | collective-permute-start | bytes 393224 | tf_op jit(solution)/shard_map/ppermute | solution.py:19
  8.2 3.8 %collective-permute-done.1 = f32[256,128]{1,0:T(8,128)S(1)} collective-permute-done((f32[256,128]{1,0:T(8,128)S(1)}, f32[256,128]{1,0:T(8,128)S(1)}, u32[]{:S(2)}, u32[]{:S(2)}) %collective-permute-start.1) | collective-permute-done | bytes 131104 | tf_op jit(solution)/shard_map/ppermute | solution.py:19
  12.0 0.0 copy-start.4
  12.1 0.6 copy-done.4
  12.7 0.0 copy-start.2
  12.7 0.4 abs_reduce_fusion.2
  13.1 0.6 reduce_max.27
  14.4 0.0 copy-done.2
  14.4 0.3 fusion.5
  14.7 0.3 fusion.28
  15.0 12.9 %all_to_all.20 = f32[8,17,128]{2,1,0:T(8,128)S(1)} all-to-all(f32[8,17,128]{2,1,0:T(8,128)S(1)} %reshape.70), channel_id=1, replica_groups=mesh['vox'=8,'smp'=4] {'vox'}, dimensions={0} | all-to-all | bytes 139264 | tf_op jit(solution)/shard_map/all_to_all | solution.py:33
  28.0 9.5 %all_to_all.21 = f32[8,17,128]{2,1,0:T(8,128)S(1)} all-to-all(f32[8,17,128]{2,1,0:T(8,128)S(1)} %broadcast_in_dim.4), channel_id=1, replica_groups=mesh['vox'=8,'smp'=4] {'vox'}, dimensions={0} | all-to-all | bytes 139264 | tf_op jit(solution)/shard_map/all_to_all | solution.py:34
  37.6 0.2 abs_reduce_fusion.1
  37.8 0.0 copy-start.1
  37.8 0.6 reduce_max.28
  39.1 0.2 fusion.9
  39.3 0.3 fusion.29
  39.6 0.0 copy-done.1
  39.7 0.7 convolution_bitcast_fusion.1
  40.3 10.3 %all_to_all.22 = f32[32,8,128]{2,1,0:T(8,128)S(1)} all-to-all(f32[32,8,128]{2,1,0:T(8,128)S(1)} %maximum_bitcast_fusion), channel_id=1, replica_groups=mesh['vox'=8,'smp'=4] {'vox','smp'}, dimensions={0} | all-to-all | bytes 262144 | tf_op jit(solution)/shard_map/all_to_all | solution.py:33
  50.7 0.6 broadcast_in_dim.5
  51.3 2.6 %all-to-all-start.3 = ((f32[32,8,128]{2,1,0:T(8,128)}), f32[32,8,128]{2,1,0:T(8,128)S(1)}, u32[]{:S(2)}, u32[]{:S(2)}) async-start(f32[32,8,128]{2,1,0:T(8,128)} %broadcast_in_dim.5), calls=%async_computation.3 | async-start | bytes 262144 | tf_op jit(solution)/shard_map/all_to_all | solution.py:34
  53.9 8.2 %all-to-all-done.3 = f32[32,8,128]{2,1,0:T(8,128)S(1)} async-done(((f32[32,8,128]{2,1,0:T(8,128)}), f32[32,8,128]{2,1,0:T(8,128)S(1)}, u32[]{:S(2)}, u32[]{:S(2)}) %all-to-all-start.3) | async-done | bytes 131104 | tf_op jit(solution)/shard_map/all_to_all | solution.py:34
  62.1 0.1 select_reduce_fusion
  62.2 0.6 broadcast_divide_fusion.2
  62.8 0.2 abs_reduce_fusion
  63.0 0.6 reduce_max.29
  64.4 0.2 fusion.2
  64.6 0.3 fusion.6
  64.9 0.5 fusion.24
  65.4 0.6 broadcast_divide_fusion
  (15 shorter events, 0.2 us)
Async XLA Ops:
  0.6 1.3 %copy-start.3 = (f32[8,128]{1,0:T(8,128)S(1)}, f32[8,128]{1,0:T(8,128)}, u32[]{:S(2)}) copy-start(f32[8,128]{1,0:T(8,128)} %param.7) | copy-start | bytes 12292
  1.9 0.8 %copy-start = (f32[128,128]{1,0:T(8,128)S(1)}, f32[128,128]{1,0:T(8,128)}, u32[]{:S(2)}) copy-start(f32[128,128]{1,0:T(8,128)} %param.8) | copy-start | bytes 196612
  3.8 1.5 %collective-permute-start = (f32[256,128]{1,0:T(8,128)S(1)}, f32[256,128]{1,0:T(8,128)S(1)}, u32[]{:S(2)}, u32[]{:S(2)}) collective-permute-start(f32[256,128]{1,0:T(8,128)S(1)} %pad_maximum_fusion), channel_id=1, source_target_pairs={{0,1},{1,0},{2,3},{3,2},{4,5},{5,4},{6,7},{7,6},{8,9},{9,8},{10,11... | collective-permute-start | bytes 393224 | tf_op jit(solution)/shard_map/ppermute | solution.py:19
  5.3 6.8 %collective-permute-start.1 = (f32[256,128]{1,0:T(8,128)S(1)}, f32[256,128]{1,0:T(8,128)S(1)}, u32[]{:S(2)}, u32[]{:S(2)}) collective-permute-start(f32[256,128]{1,0:T(8,128)S(1)} %fusion.25), channel_id=1, source_target_pairs={{0,2},{1,3},{2,0},{3,1},{4,6},{5,7},{6,4},{7,5},{8,10},{9,11},{10,... | collective-permute-start | bytes 393224 | tf_op jit(solution)/shard_map/ppermute | solution.py:19
  12.0 0.7 copy-start.4
  12.7 1.7 %copy-start.2 = (f32[128,128]{1,0:T(8,128)S(1)}, f32[128,128]{1,0:T(8,128)}, u32[]{:S(2)}) copy-start(f32[128,128]{1,0:T(8,128)} %param.6) | copy-start | bytes 196612
  37.8 1.9 %copy-start.1 = (f32[128,128]{1,0:T(8,128)}, f32[128,128]{1,0:T(8,128)S(1)}, u32[]{:S(2)}) copy-start(f32[128,128]{1,0:T(8,128)S(1)} %get-tuple-element.11) | copy-start | bytes 196612
  51.3 10.8 %all-to-all-start.3 = ((f32[32,8,128]{2,1,0:T(8,128)}), f32[32,8,128]{2,1,0:T(8,128)S(1)}, u32[]{:S(2)}, u32[]{:S(2)}) async-start(f32[32,8,128]{2,1,0:T(8,128)} %broadcast_in_dim.5), calls=%async_computation.3 | async-start | bytes 262144 | tf_op jit(solution)/shard_map/all_to_all | solution.py:34

commit v3 on v0

v3 whole, which is shorter than its diff:
```python
import jax
import jax.numpy as jnp
from jax import lax
from jax.experimental import pallas as pl
from jax.experimental.pallas import tpu as pltpu
from jax.sharding import PartitionSpec as P

HIGH = lax.Precision.HIGHEST
F32 = jnp.float32
VMEM_LIMIT = 12 * 1024 * 1024


def dot(a, b):
    return jnp.dot(a, b, precision=HIGH, preferred_element_type=F32)


def dot_rows(a, b):
    return lax.dot_general(a, b, (((0,), (0,)), ((), ())), precision=HIGH, preferred_element_type=F32)


def step_of(coupled):
    sums = jnp.sum(jnp.abs(coupled), axis=0, keepdims=True)
    return 1.0 / jnp.max(sums, axis=1, keepdims=True)


def diagonal_row(gram):
    rows = lax.broadcasted_iota(jnp.int32, gram.shape, 0)
    columns = lax.broadcasted_iota(jnp.int32, gram.shape, 1)
    return jnp.sum(jnp.where(rows == columns, gram, 0.0), axis=0, keepdims=True)


def call(kernel, outs, operands, flops, scratch=(), in_hbm=0):
    spaces = [pltpu.HBM if i < in_hbm else pltpu.VMEM for i in range(len(operands))]
    placed = [pltpu.with_memory_space_constraint(x, space) for x, space in zip(operands, spaces)]
    specs = [pl.BlockSpec(memory_space=space) for space in spaces]
    return pl.pallas_call(
        kernel,
        out_shape=outs,
        in_specs=specs,
        out_specs=[pl.BlockSpec(memory_space=pltpu.VMEM)] * len(outs),
        scratch_shapes=list(scratch),
        compiler_params=pltpu.CompilerParams(vmem_limit_bytes=VMEM_LIMIT),
        cost_estimate=pl.CostEstimate(flops=flops, bytes_accessed=1 << 16, transcendentals=0),
    )(*placed)


def near(shape):
    return pltpu.VMEM(shape, F32)


def far(shape):
    return jax.ShapeDtypeStruct(shape, F32)


def in_order(position, own, received, scratch):
    size = scratch.shape[0]
    half = size // 2
    block = size // lax.axis_size("smp")
    for p in range(size // block):
        source = own if p * block < half else received
        start = p * block % half
        scratch[pl.ds(pl.multiple_of((position ^ p) * block, block), block), :] = source[start : start + block, :]
    return scratch[...]


def partner(values, axes, bit):
    count = lax.axis_size(axes)
    return lax.ppermute(values, axes, [(i, i ^ bit) for i in range(count)])


def bits_of(count):
    if count & (count - 1):
        raise ValueError("axis size")
    return [1 << b for b in range(count.bit_length() - 1)]


def per_device(ensemble, voxel_factor, sample_factor, time_factor, weights):
    vox_rows, smp_rows, times = ensemble.shape
    rank = voxel_factor.shape[1]
    flat_rows = vox_rows * smp_rows
    vox_count, smp_count = lax.axis_size("vox"), lax.axis_size("smp")
    vox_total, smp_total = vox_rows * vox_count, smp_rows * smp_count
    vox_bits, smp_bits = bits_of(vox_count), bits_of(smp_count)
    gram_half, time_half = rank // 2, times // 2
    chunks = 4 if vox_rows % 32 == 0 else 1
    chunk_vox = vox_rows // chunks
    chunk_rows = chunk_vox * smp_rows
    position = lambda: lax.axis_index("smp")
    wide = (rank, rank)

    def open_kernel(x_hbm, c_hbm, b_hbm, x, send, con, c, sems):
        copies = [pltpu.make_async_copy(c_hbm, c, sems.at[0])]
        copies += [pltpu.make_async_copy(b_hbm, send.at[pl.ds(vox_rows, smp_rows), :], sems.at[1])]
        for n in range(chunks):
            part = pl.ds(n * chunk_rows, chunk_rows)
            copies.append(pltpu.make_async_copy(x_hbm.at[part, :], x.at[part, :], sems.at[2 + n]))
        for copy in copies:
            copy.start()
        copies[0].wait()
        copies[1].wait()
        factor = c[...]
        b = send[pl.ds(vox_rows, smp_rows), :]
        for n in range(chunks):
            copies[2 + n].wait()
            total = None
            rows = pl.ds(n * chunk_vox, chunk_vox)
            for j in range(smp_rows):
                block = x[pl.ds(n * chunk_rows + j, chunk_vox, stride=smp_rows), :]
                made = dot(block, factor)
                con[j, rows, :] = made
                made = made * b[j : j + 1, :]
                total = made if total is None else total + made
            send[rows, :] = total

    flat = ensemble.reshape(flat_rows, times)
    x, sent, con = call(
        open_kernel,
        (near((flat_rows, times)), near((vox_rows + smp_rows, rank)), near((smp_rows, vox_rows, rank))),
        (flat, time_factor, sample_factor),
        2 * flat_rows * times * rank * 6,
        scratch=(near((times, rank)), pltpu.SemaphoreType.DMA((2 + chunks,))),
        in_hbm=3,
    )

    def weigh_kernel(c, w, outer, outer_c):
        row = w[...]
        squared = dot_rows(row, row)
        outer[...] = squared
        outer_c[...] = squared * dot_rows(c[...], c[...])

    w_row = weights.reshape(1, rank)
    outer, outer_c = call(weigh_kernel, (near(wide), near(wide)), (time_factor, w_row), 2 * rank * rank * times * 6)

    for bit in smp_bits[:-1]:
        got = partner(sent, "smp", bit)
        sent = jnp.concatenate([sent[:vox_rows] + got[:vox_rows], sent[vox_rows:], got[vox_rows:]], axis=0)
    got = partner(sent, "smp", smp_bits[-1])

    def voxel_kernel(own, other, a, w, outer_c, con, moved_out, keep, all_b, gram_all):
        b = in_order(position(), own.at[pl.ds(vox_rows, smp_total // 2), :], other.at[pl.ds(vox_rows, smp_total // 2), :], all_b)
        coupled = outer_c[...] * dot_rows(b, b)
        terms = own[:vox_rows, :] + other[:vox_rows, :]
        moved = a[...] - step_of(coupled) * (dot(a[...], coupled) - terms * w[...])
        moved_out[...] = moved
        gram_all[...] = dot_rows(moved, moved)
        mine = (position() & 1) * gram_half
        keep[:gram_half, :] = gram_all[pl.ds(pl.multiple_of(mine, gram_half), gram_half), :]
        for j in range(smp_rows):
            keep[gram_half + j : gram_half + j + 1, :] = jnp.sum(con[j] * moved, axis=0, keepdims=True)

    moved_a, sums = call(
        voxel_kernel,
        (near((vox_rows, rank)), near((gram_half + smp_rows, rank))),
        (sent, got, voxel_factor, w_row, outer_c, con),
        2 * rank * rank * vox_rows * 12,
        scratch=(near((smp_total, rank)), near(wide)),
    )

    def time_kernel(x, moved, each):
        for j in range(smp_rows):
            each[j] = dot_rows(x[pl.ds(j, vox_rows, stride=smp_rows), :], moved[...])

    (each,) = call(
        time_kernel, (near((smp_rows, times, rank)),), (x, moved_a), 2 * flat_rows * times * rank * 6
    )

    for bit in vox_bits:
        sums = sums + partner(sums, "vox", bit)
    other_half = partner(sums[:gram_half], "smp", 1)

    def sample_kernel(sums, half, b, w, outer_c, each, moved_out, gram_out, keep, give):
        mine = (position() & 1) * gram_half
        gram_out[pl.ds(pl.multiple_of(mine, gram_half), gram_half), :] = sums[:gram_half, :]
        gram_out[pl.ds(pl.multiple_of(gram_half - mine, gram_half), gram_half), :] = half[...]
        coupled = outer_c[...] * gram_out[...]
        moved = b[...] - step_of(coupled) * (dot(b[...], coupled) - sums[gram_half:, :] * w[...])
        moved_out[...] = moved
        first = (position() & 1) * time_half
        for start, out in ((time_half - first, give), (first, keep)):
            total = None
            for j in range(smp_rows):
                made = each[j, pl.ds(pl.multiple_of(start, time_half), time_half), :] * moved[j : j + 1, :]
                total = made if total is None else total + made
            out[:time_half, :] = total
        give[time_half:, :] = moved

    moved_b, gram_a, kept, given = call(
        sample_kernel,
        (near((smp_rows, rank)), near(wide), near((time_half, rank)), near((time_half + smp_rows, rank))),
        (sums, other_half, sample_factor, w_row, outer_c, each),
        2 * rank * rank * smp_rows * 6,
    )

    def scale_kernel(gram, moved, outer, result, scales_out, weighed):
        scales = jnp.sqrt(diagonal_row(gram[...]) / vox_total + 1e-06)
        scales_out[...] = scales
        result[...] = moved[...] / scales
        weighed[...] = outer[...] * gram[...]

    voxel_result, scales_a, weighed = call(
        scale_kernel,
        (far((vox_rows, rank)), near((1, rank)), near(wide)),
        (gram_a, moved_a, outer),
        vox_rows * rank * 8,
    )

    got = partner(given, "smp", 1)
    kept = kept + got[:time_half]
    rows_b = jnp.concatenate([moved_b, got[time_half:]], axis=0)
    for bit in smp_bits[1:]:
        got = partner(jnp.concatenate([kept, rows_b], axis=0), "smp", bit)
        kept = kept + got[:time_half]
        rows_b = jnp.concatenate([rows_b, got[time_half:]], axis=0)
    for bit in vox_bits:
        kept = kept + partner(kept, "vox", bit)
    other_half = partner(kept, "smp", 1)

    def last_kernel(kept, half, rows, moved_b, c, w, weighed, scales_a, b_out, c_out, w_out, all_b, terms):
        half_rows = smp_total // 2
        b = in_order(position(), rows.at[pl.ds(0, half_rows), :], rows.at[pl.ds(half_rows, half_rows), :], all_b)
        coupled = weighed[...] * dot_rows(b, b)
        scales_b = jnp.sqrt(jnp.sum(b * b, axis=0, keepdims=True) / smp_total + 1e-06)
        b_out[...] = moved_b[...] / scales_b
        mine = (position() & 1) * time_half
        terms[pl.ds(pl.multiple_of(mine, time_half), time_half), :] = kept[...]
        terms[pl.ds(pl.multiple_of(time_half - mine, time_half), time_half), :] = half[...]
        moved = c[...] - step_of(coupled) * (dot(c[...], coupled) - terms[...] * w[...])
        scales_c = jnp.sqrt(jnp.sum(moved * moved, axis=0, keepdims=True) / times + 1e-06)
        c_out[...] = moved / scales_c
        w_out[...] = w[...] * scales_a[...] * scales_b * scales_c

    sample_result, time_result, scale_result = call(
        last_kernel,
        (far((smp_rows, rank)), far((times, rank)), far((1, rank))),
        (kept, other_half, rows_b, moved_b, time_factor, w_row, weighed, scales_a),
        2 * rank * rank * times * 6,
        scratch=(near((smp_total, rank)), near((times, rank))),
    )
    return voxel_result, sample_result, time_result, scale_result.reshape(rank)


def solution(mesh):
    return jax.shard_map(
        per_device,
        mesh=mesh,
        in_specs=(P("vox", "smp", None), P("vox", None), P("smp", None), P(), P()),
        out_specs=(P("vox", None), P("smp", None), P(), P()),
        check_vma=False,
    )
```

time: 263 us -> 46.6 us (0.18)
  waiting for transfers between devices: 205 us -> 20 us
  blocking collectives: 21.4 us -> 0 us
  starting transfers between devices: 0.12 us -> 18.6 us
  between operations: 16 us -> 0.78 us
  matrix products: 9.78 us -> 0 us
  Pallas kernels: 0 us -> 6.97 us
  other arithmetic: 4.89 us -> 0.07 us
  local copies, waits for them, and re-layouts: 4.63 us -> 0.04 us
    psum x3 -> x0, waiting for transfers between devices: 205 us -> none  [the longest x1 123 us: per_device(): gram_sum, summed_c = lax.psum((local_gram(moved), raw_c), ('vox', 'smp'))]
    psum x1 -> x0, blocking collectives: 21.4 us -> none  [per_device(): gram, summed_b = lax.psum((local_gram(moved), raw_b), 'vox')]
    ppermute x0 -> x12, waiting for transfers between devices: none -> 20 us  [partner(): return lax.ppermute(values, axes, [(i, i ^ bit) for i in range(count)])]
    ppermute x0 -> x12, starting transfers between devices: none -> 18.6 us  [partner(): return lax.ppermute(values, axes, [(i, i ^ bit) for i in range(count)])]
    dot_general x10 -> x0, matrix products: 9.78 us -> none  [the longest x5 5.11 us: local_gram(): jnp.dot(moved.T, moved, precision=HIGH, preferred_element_type=jnp.float32)]
    pallas_call x0 -> x7, Pallas kernels: none -> 6.97 us  [call(): pl.pallas_call(kernel, out_shape=outs, in_specs=specs, out_specs=[pl.Bloc...]
    gather x3 -> x0, local copies, waits for them, and re-layouts: 4.5 us -> none  [rescale(): scales = jnp.sqrt(jnp.diagonal(gram) / row_count + 1e-06)]
  transfers between devices with their start and end apart: 3 -> 12, of which waited for: 3 -> 12; matrix products, arithmetic and copies ran while one was open for 0% -> 0% of each run, Pallas kernels for 0% -> 4%
where the time goes in v3:
time: 46.6 us; the launch traced here: 46.5 us
  waiting for transfers between devices  20 us (43%)
  starting transfers between devices  18.6 us (40%)
  Pallas kernels  6.97 us (15%)
  between operations  0.78 us (2%)
    ppermute x12, waiting for transfers between devices, partner(): return lax.ppermute(values, axes, [(i, i ^ bit) for i in range(count)])  20 us
    ppermute x12, starting transfers between devices, partner(): return lax.ppermute(values, axes, [(i, i ^ bit) for i in range(count)])  18.6 us
    pallas_call x7, Pallas kernels, call(): pl.pallas_call(kernel, out_shape=outs, in_specs=specs, out_specs=[pl.Bloc...  6.97 us
  transfers between devices with their start and end apart: 12, of which 12 were waited for; matrix products, arithmetic and copies ran while one was open for 0% of the time, Pallas kernels for 4%

profile of v3, /device:TPU:0, one launch (start us, length us, event | category | flops | bytes accessed | tf_op | source)
XLA Modules:
  0.0 46.5 jit_solution(2520581103022808027)
XLA Ops:
  0.6 3.1 %shard_map.84 = (f32[1024,128]{1,0:T(8,128)S(1)}, f32[136,128]{1,0:T(8,128)S(1)}, f32[8,128,128]{2,1,0:T(8,128)S(1)}) custom-call(f32[1024,128]{1,0:T(8,128)} %bitcast.7, f32[128,128]{1,0:T(8,128)} %c.3, f32[8,128]{1,0:T(8,128)} %b.1), custom_call_target="tpu_custom_call" | custom-call | flops 201326592 | bytes 65536 | tf_op jit(solution)/shard_map/pallas_call | solution.py:36
  3.8 0.5 %collective-permute-start = (f32[136,128]{1,0:T(8,128)S(1)}, f32[136,128]{1,0:T(8,128)S(1)}, u32[]{:S(2)}, u32[]{:S(2)}) collective-permute-start(f32[136,128]{1,0:T(8,128)S(1)} %get-tuple-element.21), channel_id=1, source_target_pairs={{0,1},{1,0},{2,3},{3,2},{4,5},{5,4},{6,7},{7,6},{8,9},{9,8},{10,11... | collective-permute-start | bytes 208904 | tf_op jit(solution)/shard_map/ppermute | solution.py:68
  4.3 0.9 %collective-permute-done = f32[136,128]{1,0:T(8,128)S(1)} collective-permute-done((f32[136,128]{1,0:T(8,128)S(1)}, f32[136,128]{1,0:T(8,128)S(1)}, u32[]{:S(2)}, u32[]{:S(2)}) %collective-permute-start) | collective-permute-done | bytes 69664 | tf_op jit(solution)/shard_map/ppermute | solution.py:68
  5.2 0.0 copy-start
  5.2 0.0 copy-start.2
  5.2 0.0 copy-start.1
  5.3 2.9 %collective-permute-start.1 = (f32[144,128]{1,0:T(8,128)S(1)}, f32[144,128]{1,0:T(8,128)S(1)}, u32[]{:S(2)}, u32[]{:S(2)}) collective-permute-start(f32[144,128]{1,0:T(8,128)S(1)} %pad_maximum_fusion.own), channel_id=1, source_target_pairs={{0,2},{1,3},{2,0},{3,1},{4,6},{5,7},{6,4},{7,5},{8,10},{9,11},{10,... | collective-permute-start | bytes 221192 | tf_op jit(solution)/shard_map/ppermute | solution.py:68
  8.2 0.0 copy-done
  8.2 0.0 copy-done.2
  8.2 0.3 shard_map.85
  8.5 2.2 %collective-permute-done.1.other = f32[144,128]{1,0:T(8,128)S(1)} collective-permute-done((f32[144,128]{1,0:T(8,128)S(1)}, f32[144,128]{1,0:T(8,128)S(1)}, u32[]{:S(2)}, u32[]{:S(2)}) %collective-permute-start.1) | collective-permute-done | bytes 73760 | tf_op jit(solution)/shard_map/ppermute | solution.py:68
  10.8 0.0 copy-done.1
  10.8 0.8 %shard_map.86 = (f32[128,128]{1,0:T(8,128)S(1)}, f32[72,128]{1,0:T(8,128)S(1)}) custom-call(f32[144,128]{1,0:T(8,128)S(1)} %pad_maximum_fusion.own, f32[144,128]{1,0:T(8,128)S(1)} %collective-permute-done.1.other, f32[128,128]{1,0:T(8,128)S(1)} %copy-done.1, f32[1,128]{1,0:T(1,128)S(1)} %bitcast.4, f32[128,128]{1,0:T(8,128)S(1)} %get-tuple-element.22.outer_c, ...), custom_call_target="tpu_custom_call" | custom-call | flops 50331648 | bytes 65536 | tf_op jit(solution)/shard_map/pallas_call | solution.py:36
  11.6 1.8 %collective-permute-start.2 = (f32[72,128]{1,0:T(8,128)S(1)}, f32[72,128]{1,0:T(8,128)S(1)}, u32[]{:S(2)}, u32[]{:S(2)}) collective-permute-start(f32[72,128]{1,0:T(8,128)S(1)} %get-tuple-element.24), channel_id=1, source_target_pairs={{0,4},{4,0},{8,12},{12,8},{16,20},{20,16},{24,28},{28,24},{1,5},{5... | collective-permute-start | bytes 110600 | tf_op jit(solution)/shard_map/ppermute | solution.py:68
  13.4 2.2 %collective-permute-done.2 = f32[72,128]{1,0:T(8,128)S(1)} collective-permute-done((f32[72,128]{1,0:T(8,128)S(1)}, f32[72,128]{1,0:T(8,128)S(1)}, u32[]{:S(2)}, u32[]{:S(2)}) %collective-permute-start.2) | collective-permute-done | bytes 36896 | tf_op jit(solution)/shard_map/ppermute | solution.py:68
  15.6 1.8 %collective-permute-start.3 = (f32[72,128]{1,0:T(8,128)S(1)}, f32[72,128]{1,0:T(8,128)S(1)}, u32[]{:S(2)}, u32[]{:S(2)}) collective-permute-start(f32[72,128]{1,0:T(8,128)S(1)} %add.28), channel_id=1, source_target_pairs={{0,8},{4,12},{8,0},{12,4},{16,24},{20,28},{24,16},{28,20},{1,9},{5... | collective-permute-start | bytes 110600 | tf_op jit(solution)/shard_map/ppermute | solution.py:68
  17.4 2.1 %collective-permute-done.3 = f32[72,128]{1,0:T(8,128)S(1)} collective-permute-done((f32[72,128]{1,0:T(8,128)S(1)}, f32[72,128]{1,0:T(8,128)S(1)}, u32[]{:S(2)}, u32[]{:S(2)}) %collective-permute-start.3) | collective-permute-done | bytes 36896 | tf_op jit(solution)/shard_map/ppermute | solution.py:68
  19.6 2.8 %collective-permute-start.4 = (f32[72,128]{1,0:T(8,128)S(1)}, f32[72,128]{1,0:T(8,128)S(1)}, u32[]{:S(2)}, u32[]{:S(2)}) collective-permute-start(f32[72,128]{1,0:T(8,128)S(1)} %add.29), channel_id=1, source_target_pairs={{0,16},{4,20},{8,24},{12,28},{16,0},{20,4},{24,8},{28,12},{1,17},{... | collective-permute-start | bytes 110600 | tf_op jit(solution)/shard_map/ppermute | solution.py:68
  22.4 2.0 %collective-permute-done.4 = f32[72,128]{1,0:T(8,128)S(1)} collective-permute-done((f32[72,128]{1,0:T(8,128)S(1)}, f32[72,128]{1,0:T(8,128)S(1)}, u32[]{:S(2)}, u32[]{:S(2)}) %collective-permute-start.4) | collective-permute-done | bytes 36896 | tf_op jit(solution)/shard_map/ppermute | solution.py:68
  24.4 0.1 collective-permute-start.5
  24.5 0.0 copy-start.3
  24.5 0.6 %shard_map.87.each = f32[8,128,128]{2,1,0:T(8,128)S(1)} custom-call(f32[1024,128]{1,0:T(8,128)S(1)} %get-tuple-element.25.x, f32[128,128]{1,0:T(8,128)S(1)} %get-tuple-element.26.moved), custom_call_target="tpu_custom_call" | custom-call | flops 201326592 | bytes 65536 | tf_op jit(solution)/shard_map/pallas_call | solution.py:36
  25.2 0.5 %collective-permute-done.5.half = f32[64,128]{1,0:T(8,128)S(1)} collective-permute-done((f32[64,128]{1,0:T(8,128)S(1)}, f32[64,128]{1,0:T(8,128)S(1)}, u32[]{:S(2)}, u32[]{:S(2)}) %collective-permute-start.5) | collective-permute-done | bytes 32800 | tf_op jit(solution)/shard_map/ppermute | solution.py:68
  25.7 0.0 copy-done.3
  25.7 0.2 shard_map.88
  25.9 0.2 collective-permute-start.6
  26.2 1.1 %collective-permute-done.6 = f32[72,128]{1,0:T(8,128)S(1)} collective-permute-done((f32[72,128]{1,0:T(8,128)S(1)}, f32[72,128]{1,0:T(8,128)S(1)}, u32[]{:S(2)}, u32[]{:S(2)}) %collective-permute-start.6) | collective-permute-done | bytes 36896 | tf_op jit(solution)/shard_map/ppermute | solution.py:68
  27.2 1.8 %collective-permute-start.7 = (f32[80,128]{1,0:T(8,128)S(1)}, f32[80,128]{1,0:T(8,128)S(1)}, u32[]{:S(2)}, u32[]{:S(2)}) collective-permute-start(f32[80,128]{1,0:T(8,128)S(1)} %pad_maximum_fusion.1), channel_id=1, source_target_pairs={{0,2},{1,3},{2,0},{3,1},{4,6},{5,7},{6,4},{7,5},{8,10},{9,11},{10,... | collective-permute-start | bytes 122888 | tf_op jit(solution)/shard_map/ppermute | solution.py:68
  29.1 2.2 %collective-permute-done.7 = f32[80,128]{1,0:T(8,128)S(1)} collective-permute-done((f32[80,128]{1,0:T(8,128)S(1)}, f32[80,128]{1,0:T(8,128)S(1)}, u32[]{:S(2)}, u32[]{:S(2)}) %collective-permute-start.7) | collective-permute-done | bytes 40992 | tf_op jit(solution)/shard_map/ppermute | solution.py:68
  31.3 0.0 copy-start.4
  31.3 1.8 %collective-permute-start.8 = (f32[64,128]{1,0:T(8,128)S(1)}, f32[64,128]{1,0:T(8,128)S(1)}, u32[]{:S(2)}, u32[]{:S(2)}) collective-permute-start(f32[64,128]{1,0:T(8,128)S(1)} %slice_add_fusion.1), channel_id=1, source_target_pairs={{0,4},{4,0},{8,12},{12,8},{16,20},{20,16},{24,28},{28,24},{1,5},{5... | collective-permute-start | bytes 98312 | tf_op jit(solution)/shard_map/ppermute | solution.py:68
  33.1 2.2 %collective-permute-done.8 = f32[64,128]{1,0:T(8,128)S(1)} collective-permute-done((f32[64,128]{1,0:T(8,128)S(1)}, f32[64,128]{1,0:T(8,128)S(1)}, u32[]{:S(2)}, u32[]{:S(2)}) %collective-permute-start.8) | collective-permute-done | bytes 32800 | tf_op jit(solution)/shard_map/ppermute | solution.py:68
  35.3 1.8 %collective-permute-start.9 = (f32[64,128]{1,0:T(8,128)S(1)}, f32[64,128]{1,0:T(8,128)S(1)}, u32[]{:S(2)}, u32[]{:S(2)}) collective-permute-start(f32[64,128]{1,0:T(8,128)S(1)} %add.33), channel_id=1, source_target_pairs={{0,8},{4,12},{8,0},{12,4},{16,24},{20,28},{24,16},{28,20},{1,9},{5... | collective-permute-start | bytes 98312 | tf_op jit(solution)/shard_map/ppermute | solution.py:68
  37.1 2.1 %collective-permute-done.9 = f32[64,128]{1,0:T(8,128)S(1)} collective-permute-done((f32[64,128]{1,0:T(8,128)S(1)}, f32[64,128]{1,0:T(8,128)S(1)}, u32[]{:S(2)}, u32[]{:S(2)}) %collective-permute-start.9) | collective-permute-done | bytes 32800 | tf_op jit(solution)/shard_map/ppermute | solution.py:68
  39.2 3.0 %collective-permute-start.10 = (f32[64,128]{1,0:T(8,128)S(1)}, f32[64,128]{1,0:T(8,128)S(1)}, u32[]{:S(2)}, u32[]{:S(2)}) collective-permute-start(f32[64,128]{1,0:T(8,128)S(1)} %add.34), channel_id=1, source_target_pairs={{0,16},{4,20},{8,24},{12,28},{16,0},{20,4},{24,8},{28,12},{1,17},{... | collective-permute-start | bytes 98312 | tf_op jit(solution)/shard_map/ppermute | solution.py:68
  42.2 0.7 %shard_map.89 = (f32[128,128]{1,0:T(8,128)}, f32[1,128]{1,0:T(1,128)S(1)}, f32[128,128]{1,0:T(8,128)S(1)}) custom-call(f32[128,128]{1,0:T(8,128)S(1)} %get-tuple-element.27.gram, f32[128,128]{1,0:T(8,128)S(1)} %get-tuple-element.26.moved, f32[128,128]{1,0:T(8,128)S(1)} %get-tuple-element.28.outer), custom_call_target="tpu_custom_call" | custom-call | flops 131072 | bytes 65536 | tf_op jit(solution)/shard_map/pallas_call | solution.py:36
  42.9 0.0 copy-done.4
  42.9 0.0 slice-start
  42.9 1.2 %collective-permute-done.10 = f32[64,128]{1,0:T(8,128)S(1)} collective-permute-done((f32[64,128]{1,0:T(8,128)S(1)}, f32[64,128]{1,0:T(8,128)S(1)}, u32[]{:S(2)}, u32[]{:S(2)}) %collective-permute-start.10) | collective-permute-done | bytes 32800 | tf_op jit(solution)/shard_map/ppermute | solution.py:68
  44.1 0.0 collective-permute-start.11
  44.1 0.0 slice-done
  44.1 1.2 %collective-permute-done.11.half = f32[64,128]{1,0:T(8,128)S(1)} collective-permute-done((f32[64,128]{1,0:T(8,128)S(1)}, f32[64,128]{1,0:T(8,128)S(1)}, u32[]{:S(2)}, u32[]{:S(2)}) %collective-permute-start.11) | collective-permute-done | bytes 32800 | tf_op jit(solution)/shard_map/ppermute | solution.py:68
  45.3 1.2 %shard_map.90 = (f32[8,128]{1,0:T(8,128)}, f32[128,128]{1,0:T(8,128)}, f32[1,128]{1,0:T(1,128)}) custom-call(f32[64,128]{1,0:T(8,128)S(1)} %add.35.kept, f32[64,128]{1,0:T(8,128)S(1)} %collective-permute-done.11.half, f32[32,128]{1,0:T(8,128)S(1)} %pad_maximum_fusion.2.rows, f32[8,128]{1,0:T(8,128)S(1)} %get-tuple-element.32.moved_b, ...), custom_call_target="tpu_custom_call" | custom-call | flops 25165824 | bytes 65536 | tf_op jit(solution)/shard_map/pallas_call | solution.py:36
  (16 shorter events, 0.1 us)
Async XLA Ops:
  3.8 1.4 %collective-permute-start = (f32[136,128]{1,0:T(8,128)S(1)}, f32[136,128]{1,0:T(8,128)S(1)}, u32[]{:S(2)}, u32[]{:S(2)}) collective-permute-start(f32[136,128]{1,0:T(8,128)S(1)} %get-tuple-element.21), channel_id=1, source_target_pairs={{0,1},{1,0},{2,3},{3,2},{4,5},{5,4},{6,7},{7,6},{8,9},{9,8},{10,11... | collective-permute-start | bytes 208904 | tf_op jit(solution)/shard_map/ppermute | solution.py:68
  5.2 3.0 %copy-start = (f32[128,128]{1,0:T(8,128)S(1)}, f32[128,128]{1,0:T(8,128)}, u32[]{:S(2)}) copy-start(f32[128,128]{1,0:T(8,128)} %c.3) | copy-start | bytes 196612
  5.2 3.0 %copy-start.2 = (f32[128]{0:T(128)S(1)}, f32[128]{0:T(128)}, u32[]{:S(2)}) copy-start(f32[128]{0:T(128)} %param.9) | copy-start | bytes 1540
  5.2 5.5 %copy-start.1 = (f32[128,128]{1,0:T(8,128)S(1)}, f32[128,128]{1,0:T(8,128)}, u32[]{:S(2)}) copy-start(f32[128,128]{1,0:T(8,128)} %a.1) | copy-start | bytes 196612
  5.3 5.5 %collective-permute-start.1 = (f32[144,128]{1,0:T(8,128)S(1)}, f32[144,128]{1,0:T(8,128)S(1)}, u32[]{:S(2)}, u32[]{:S(2)}) collective-permute-start(f32[144,128]{1,0:T(8,128)S(1)} %pad_maximum_fusion.own), channel_id=1, source_target_pairs={{0,2},{1,3},{2,0},{3,1},{4,6},{5,7},{6,4},{7,5},{8,10},{9,11},{10,... | collective-permute-start | bytes 221192 | tf_op jit(solution)/shard_map/ppermute | solution.py:68
  11.6 4.0 %collective-permute-start.2 = (f32[72,128]{1,0:T(8,128)S(1)}, f32[72,128]{1,0:T(8,128)S(1)}, u32[]{:S(2)}, u32[]{:S(2)}) collective-permute-start(f32[72,128]{1,0:T(8,128)S(1)} %get-tuple-element.24), channel_id=1, source_target_pairs={{0,4},{4,0},{8,12},{12,8},{16,20},{20,16},{24,28},{28,24},{1,5},{5... | collective-permute-start | bytes 110600 | tf_op jit(solution)/shard_map/ppermute | solution.py:68
  15.6 4.0 %collective-permute-start.3 = (f32[72,128]{1,0:T(8,128)S(1)}, f32[72,128]{1,0:T(8,128)S(1)}, u32[]{:S(2)}, u32[]{:S(2)}) collective-permute-start(f32[72,128]{1,0:T(8,128)S(1)} %add.28), channel_id=1, source_target_pairs={{0,8},{4,12},{8,0},{12,4},{16,24},{20,28},{24,16},{28,20},{1,9},{5... | collective-permute-start | bytes 110600 | tf_op jit(solution)/shard_map/ppermute | solution.py:68
  19.6 4.9 %collective-permute-start.4 = (f32[72,128]{1,0:T(8,128)S(1)}, f32[72,128]{1,0:T(8,128)S(1)}, u32[]{:S(2)}, u32[]{:S(2)}) collective-permute-start(f32[72,128]{1,0:T(8,128)S(1)} %add.29), channel_id=1, source_target_pairs={{0,16},{4,20},{8,24},{12,28},{16,0},{20,4},{24,8},{28,12},{1,17},{... | collective-permute-start | bytes 110600 | tf_op jit(solution)/shard_map/ppermute | solution.py:68
  24.4 1.3 %collective-permute-start.5 = (f32[64,128]{1,0:T(8,128)S(1)}, f32[64,128]{1,0:T(8,128)S(1)}, u32[]{:S(2)}, u32[]{:S(2)}) collective-permute-start(f32[64,128]{1,0:T(8,128)S(1)} %slice.38), channel_id=1, source_target_pairs={{0,1},{1,0},{2,3},{3,2},{4,5},{5,4},{6,7},{7,6},{8,9},{9,8},{10,11... | collective-permute-start | bytes 98312 | tf_op jit(solution)/shard_map/ppermute | solution.py:68
  24.5 1.2 %copy-start.3 = (f32[8,128]{1,0:T(8,128)S(1)}, f32[8,128]{1,0:T(8,128)}, u32[]{:S(2)}) copy-start(f32[8,128]{1,0:T(8,128)} %b.1) | copy-start | bytes 12292
  25.9 1.3 %collective-permute-start.6 = (f32[72,128]{1,0:T(8,128)S(1)}, f32[72,128]{1,0:T(8,128)S(1)}, u32[]{:S(2)}, u32[]{:S(2)}) collective-permute-start(f32[72,128]{1,0:T(8,128)S(1)} %get-tuple-element.31), channel_id=1, source_target_pairs={{0,1},{1,0},{2,3},{3,2},{4,5},{5,4},{6,7},{7,6},{8,9},{9,8},{10,11... | collective-permute-start | bytes 110600 | tf_op jit(solution)/shard_map/ppermute | solution.py:68
  27.2 4.1 %collective-permute-start.7 = (f32[80,128]{1,0:T(8,128)S(1)}, f32[80,128]{1,0:T(8,128)S(1)}, u32[]{:S(2)}, u32[]{:S(2)}) collective-permute-start(f32[80,128]{1,0:T(8,128)S(1)} %pad_maximum_fusion.1), channel_id=1, source_target_pairs={{0,2},{1,3},{2,0},{3,1},{4,6},{5,7},{6,4},{7,5},{8,10},{9,11},{10,... | collective-permute-start | bytes 122888 | tf_op jit(solution)/shard_map/ppermute | solution.py:68
  31.3 11.6 %copy-start.4 = (f32[80,128]{1,0:T(8,128)}, f32[80,128]{1,0:T(8,128)S(1)}, u32[]{:S(2)}) copy-start(f32[80,128]{1,0:T(8,128)S(1)} %collective-permute-done.7) | copy-start | bytes 122884
  31.3 4.0 %collective-permute-start.8 = (f32[64,128]{1,0:T(8,128)S(1)}, f32[64,128]{1,0:T(8,128)S(1)}, u32[]{:S(2)}, u32[]{:S(2)}) collective-permute-start(f32[64,128]{1,0:T(8,128)S(1)} %slice_add_fusion.1), channel_id=1, source_target_pairs={{0,4},{4,0},{8,12},{12,8},{16,20},{20,16},{24,28},{28,24},{1,5},{5... | collective-permute-start | bytes 98312 | tf_op jit(solution)/shard_map/ppermute | solution.py:68
  35.3 3.9 %collective-permute-start.9 = (f32[64,128]{1,0:T(8,128)S(1)}, f32[64,128]{1,0:T(8,128)S(1)}, u32[]{:S(2)}, u32[]{:S(2)}) collective-permute-start(f32[64,128]{1,0:T(8,128)S(1)} %add.33), channel_id=1, source_target_pairs={{0,8},{4,12},{8,0},{12,4},{16,24},{20,28},{24,16},{28,20},{1,9},{5... | collective-permute-start | bytes 98312 | tf_op jit(solution)/shard_map/ppermute | solution.py:68
  39.2 4.9 %collective-permute-start.10 = (f32[64,128]{1,0:T(8,128)S(1)}, f32[64,128]{1,0:T(8,128)S(1)}, u32[]{:S(2)}, u32[]{:S(2)}) collective-permute-start(f32[64,128]{1,0:T(8,128)S(1)} %add.34), channel_id=1, source_target_pairs={{0,16},{4,20},{8,24},{12,28},{16,0},{20,4},{24,8},{28,12},{1,17},{... | collective-permute-start | bytes 98312 | tf_op jit(solution)/shard_map/ppermute | solution.py:68
  42.9 1.2 %slice-start = ((f32[80,128]{1,0:T(8,128)}), f32[16,128]{1,0:T(8,128)S(1)}, s32[]{:S(2)}) async-start(f32[80,128]{1,0:T(8,128)} %copy-done.4), calls=%async_computation | async-start | bytes 16384 | tf_op jit(solution)/shard_map/slice | solution.py:213
  44.1 1.2 %collective-permute-start.11 = (f32[64,128]{1,0:T(8,128)S(1)}, f32[64,128]{1,0:T(8,128)S(1)}, u32[]{:S(2)}, u32[]{:S(2)}) collective-permute-start(f32[64,128]{1,0:T(8,128)S(1)} %add.35.kept), channel_id=1, source_target_pairs={{0,1},{1,0},{2,3},{3,2},{4,5},{5,4},{6,7},{7,6},{8,9},{9,8},{10,11... | collective-permute-start | bytes 98312 | tf_op jit(solution)/shard_map/ppermute | solution.py:68

commit v4 on v3

v4 whole, which is shorter than its diff:
```python
import jax
import jax.numpy as jnp
from jax import lax
from jax.experimental import pallas as pl
from jax.experimental.pallas import tpu as pltpu
from jax.sharding import PartitionSpec as P

HIGH = lax.Precision.HIGHEST
F32 = jnp.float32
VMEM_LIMIT = 12 * 1024 * 1024
ALL = ("vox", "smp")


def dot(a, b):
    return jnp.dot(a, b, precision=HIGH, preferred_element_type=F32)


def dot_rows(a, b):
    return lax.dot_general(a, b, (((0,), (0,)), ((), ())), precision=HIGH, preferred_element_type=F32)


def step_of(coupled):
    sums = jnp.sum(jnp.abs(coupled), axis=0, keepdims=True)
    return 1.0 / jnp.max(sums, axis=1, keepdims=True)


def diagonal_row(gram):
    rows = lax.broadcasted_iota(jnp.int32, gram.shape, 0)
    columns = lax.broadcasted_iota(jnp.int32, gram.shape, 1)
    return jnp.sum(jnp.where(rows == columns, gram, 0.0), axis=0, keepdims=True)


def call(kernel, outs, operands, flops, scratch=(), in_hbm=0):
    spaces = [pltpu.HBM if i < in_hbm else pltpu.VMEM for i in range(len(operands))]
    placed = [pltpu.with_memory_space_constraint(x, space) for x, space in zip(operands, spaces)]
    specs = [pl.BlockSpec(memory_space=space) for space in spaces]
    return pl.pallas_call(
        kernel,
        out_shape=outs,
        in_specs=specs,
        out_specs=[pl.BlockSpec(memory_space=pltpu.VMEM)] * len(outs),
        scratch_shapes=list(scratch),
        compiler_params=pltpu.CompilerParams(vmem_limit_bytes=VMEM_LIMIT),
        cost_estimate=pl.CostEstimate(flops=flops, bytes_accessed=1 << 16, transcendentals=0),
    )(*placed)


def near(*shape):
    return pltpu.VMEM(shape, F32)


def far(*shape):
    return jax.ShapeDtypeStruct(shape, F32)


def bits_of(count):
    if count & (count - 1):
        raise ValueError("axis size")
    return [1 << b for b in range(count.bit_length() - 1)]


def groups_of(bits, size=2):
    return [bits[i : i + size] for i in range(0, len(bits), size)]


def masks_of(group):
    masks = [0]
    for bit in group:
        masks = masks + [mask | bit for mask in masks]
    return masks


def send(values, holder, mask=0):
    count = lax.axis_size(ALL)
    pairs = [(i, i ^ 1 ^ mask) for i in range(count) if i & 1 == holder]
    return lax.ppermute(values, ALL, pairs)


def fan(values, holder, masks):
    sent = [send(values, holder, mask) for mask in reversed(masks)]
    return sent[::-1]


def tree(parts):
    while len(parts) > 1:
        parts = [a + b for a, b in zip(parts[::2], parts[1::2])]
    return parts[0]


def smp_index():
    return lax.axis_index("smp")


def on_core(core, own, got):
    return jnp.where(smp_index() & 1 == core, own, got)


def in_order(rows, scratch, chips):
    block = scratch.shape[0] // chips
    chip = smp_index() // 2
    for p in range(chips):
        scratch[pl.ds(pl.multiple_of((chip ^ p) * block, block), block), :] = rows[p * block : (p + 1) * block, :]
    return scratch[...]


def per_device(ensemble, voxel_factor, sample_factor, time_factor, weights):
    vox_rows, smp_rows, times = ensemble.shape
    rank = voxel_factor.shape[1]
    flat_rows = vox_rows * smp_rows
    vox_count, smp_count = lax.axis_size("vox"), lax.axis_size("smp")
    vox_total, smp_total = vox_rows * vox_count, smp_rows * smp_count
    chips, chip_rows = smp_count // 2, 2 * smp_rows
    chip_bits = bits_of(smp_count)[1:]
    vox_bits = [bit * smp_count for bit in bits_of(vox_count)]
    chunks = 4 if vox_rows % 32 == 0 else 1
    chunk_vox = vox_rows // chunks
    chunk_rows = chunk_vox * smp_rows
    w_row = weights.reshape(1, rank)

    def open_kernel(x_hbm, c_hbm, b_hbm, x, out, con, c, sems):
        copies = [pltpu.make_async_copy(c_hbm, c, sems.at[0])]
        copies += [pltpu.make_async_copy(b_hbm, out.at[pl.ds(vox_rows, smp_rows), :], sems.at[1])]
        for n in range(chunks):
            part = pl.ds(n * chunk_rows, chunk_rows)
            copies.append(pltpu.make_async_copy(x_hbm.at[part, :], x.at[part, :], sems.at[2 + n]))
        for copy in copies:
            copy.start()
        copies[0].wait()
        copies[1].wait()
        factor = c[...]
        b = out[pl.ds(vox_rows, smp_rows), :]
        for n in range(chunks):
            copies[2 + n].wait()
            total = None
            rows = pl.ds(n * chunk_vox, chunk_vox)
            for j in range(smp_rows):
                block = x[pl.ds(n * chunk_rows + j, chunk_vox, stride=smp_rows), :]
                made = dot(block, factor)
                con[j, rows, :] = made
                made = made * b[j : j + 1, :]
                total = made if total is None else total + made
            out[rows, :] = total

    x, opened, con = call(
        open_kernel,
        (near(flat_rows, times), near(vox_rows + smp_rows, rank), near(smp_rows, vox_rows, rank)),
        (ensemble.reshape(flat_rows, times), time_factor, sample_factor),
        2 * flat_rows * times * rank * 6,
        scratch=(near(times, rank), pltpu.SemaphoreType.DMA((2 + chunks,))),
        in_hbm=3,
    )

    def weigh_kernel(c, w, outer, outer_c):
        squared = dot_rows(w[...], w[...])
        outer[...] = squared
        outer_c[...] = squared * dot_rows(c[...], c[...])

    outer, outer_c = call(
        weigh_kernel, (near(rank, rank), near(rank, rank)), (time_factor, w_row), 2 * rank * rank * times * 6
    )

    got = send(opened, 0)
    terms = opened[:vox_rows] + got[:vox_rows]
    rows_b = jnp.concatenate([got[vox_rows:], opened[vox_rows:]], axis=0)
    holder = 1
    for group in groups_of(chip_bits):
        parts = fan(jnp.concatenate([terms, rows_b], axis=0), holder, masks_of(group))
        terms = tree([part[:vox_rows] for part in parts])
        rows_b = jnp.concatenate([part[vox_rows:] for part in parts], axis=0)
        holder ^= 1
    voxel_core = holder
    mate_con = send(con, 1 - voxel_core)

    def voxel_kernel(terms, rows, a, w, outer_c, con, mate_con, moved_out, chip_b, out, all_b):
        b = in_order(rows, all_b, chips)
        chip_b[...] = all_b[pl.ds(pl.multiple_of(smp_index() // 2 * chip_rows, chip_rows), chip_rows), :]
        coupled = outer_c[...] * dot_rows(b, b)
        moved = a[...] - step_of(coupled) * (dot(a[...], coupled) - terms[...] * w[...])
        moved_out[...] = moved
        out[:rank, :] = dot_rows(moved, moved)
        for core in range(2):
            for j in range(smp_rows):
                block = con[j] if core == voxel_core else mate_con[j]
                row = rank + core * smp_rows + j
                out[row : row + 1, :] = jnp.sum(block * moved, axis=0, keepdims=True)

    moved_a, chip_b, sums = call(
        voxel_kernel,
        (near(vox_rows, rank), near(chip_rows, rank), near(rank + chip_rows, rank)),
        (terms, rows_b, voxel_factor, w_row, outer_c, con, mate_con),
        2 * rank * rank * vox_rows * 12,
        scratch=(near(smp_total, rank),),
    )
    mate_moved_a = send(moved_a, voxel_core)

    for group in groups_of(vox_bits):
        sums = tree(fan(sums, holder, masks_of(group)))
        holder ^= 1
    sample_core = holder
    if sample_core != voxel_core:
        chip_b = send(chip_b, voxel_core)
    mate_x = send(x, 1 - sample_core)

    def time_kernel(x, mate_x, moved, mate_moved, each):
        moved = on_core(voxel_core, moved[...], mate_moved[...])
        for core in range(2):
            for j in range(smp_rows):
                source = x if core == sample_core else mate_x
                each[core * smp_rows + j] = dot_rows(source[pl.ds(j, vox_rows, stride=smp_rows), :], moved)

    (each,) = call(
        time_kernel,
        (near(chip_rows, times, rank),),
        (x, mate_x, moved_a, mate_moved_a),
        4 * flat_rows * times * rank * 6,
    )

    def sample_kernel(sums, b, w, outer_c, each, out):
        coupled = outer_c[...] * sums[:rank, :]
        moved = b[...] - step_of(coupled) * (dot(b[...], coupled) - sums[rank:, :] * w[...])
        out[times:, :] = moved
        total = None
        for j in range(chip_rows):
            made = each[j] * moved[j : j + 1, :]
            total = made if total is None else total + made
        out[:times, :] = total

    (payload,) = call(
        sample_kernel,
        (near(times + chip_rows, rank),),
        (sums, chip_b, w_row, outer_c, each),
        2 * rank * rank * chip_rows * 6,
    )
    mate_sums = send(sums, sample_core)

    def scale_kernel(sums, mate_sums, moved, mate_moved, outer, result, scales_out, weighed):
        gram = on_core(sample_core, sums[:rank, :], mate_sums[:rank, :])
        scales = jnp.sqrt(diagonal_row(gram) / vox_total + 1e-06)
        scales_out[...] = scales
        result[...] = on_core(voxel_core, moved[...], mate_moved[...]) / scales
        weighed[...] = outer[...] * gram

    voxel_result, scales_a, weighed = call(
        scale_kernel,
        (far(vox_rows, rank), near(1, rank), near(rank, rank)),
        (sums, mate_sums, moved_a, mate_moved_a, outer),
        vox_rows * rank * 8,
    )

    terms, rows_b, rows_core = payload[:times], payload[times:], holder
    smp_mask = sum(chip_bits)
    for group in groups_of(chip_bits + vox_bits):
        masks = masks_of(group)
        with_rows = any(mask & smp_mask for mask in masks)
        parts = fan(jnp.concatenate([terms, rows_b], axis=0) if with_rows else terms, holder, masks)
        terms = tree([part[:times] for part in parts])
        holder ^= 1
        if with_rows:
            parts = [part for part, mask in zip(parts, masks) if not mask & ~smp_mask]
            rows_b = jnp.concatenate([part[times:] for part in parts], axis=0)
            rows_core = holder
    last_core = holder
    mate_rows_b = send(rows_b, rows_core)
    mate_terms = send(terms, last_core)

    def last_kernel(terms, mate_terms, rows, mate_rows, c, w, weighed, scales_a, b_out, c_out, w_out, all_b):
        b = in_order(on_core(rows_core, rows[...], mate_rows[...]), all_b, chips)
        coupled = weighed[...] * dot_rows(b, b)
        scales_b = jnp.sqrt(jnp.sum(b * b, axis=0, keepdims=True) / smp_total + 1e-06)
        b_out[...] = all_b[pl.ds(pl.multiple_of(smp_index() * smp_rows, smp_rows), smp_rows), :] / scales_b
        summed = on_core(last_core, terms[...], mate_terms[...])
        moved = c[...] - step_of(coupled) * (dot(c[...], coupled) - summed * w[...])
        scales_c = jnp.sqrt(jnp.sum(moved * moved, axis=0, keepdims=True) / times + 1e-06)
        c_out[...] = moved / scales_c
        w_out[...] = w[...] * scales_a[...] * scales_b * scales_c

    sample_result, time_result, scale_result = call(
        last_kernel,
        (far(smp_rows, rank), far(times, rank), far(1, rank)),
        (terms, mate_terms, rows_b, mate_rows_b, time_factor, w_row, weighed, scales_a),
        2 * rank * rank * times * 6,
        scratch=(near(smp_total, rank),),
    )
    return voxel_result, sample_result, time_result, scale_result.reshape(rank)


def solution(mesh):
    return jax.shard_map(
        per_device,
        mesh=mesh,
        in_specs=(P("vox", "smp", None), P("vox", None), P("smp", None), P(), P()),
        out_specs=(P("vox", None), P("smp", None), P(), P()),
        check_vma=False,
    )
```

time: 46.6 us -> 60.3 us (1.29)
  starting transfers between devices: 18.6 us -> 36.3 us
  waiting for transfers between devices: 20 us -> 13.7 us
  local copies, waits for them, and re-layouts: 0.04 us -> 0.86 us
    ppermute x12 -> x23, starting transfers between devices: 18.6 us -> 36.3 us  [send(): return lax.ppermute(values, ALL, pairs)]
    ppermute x12 -> x23, waiting for transfers between devices: 20 us -> 13.7 us  [send(): return lax.ppermute(values, ALL, pairs)]
    unnamed x10, local copies, waits for them, and re-layouts: 0.03 us -> 0.84 us
  transfers between devices with their start and end apart: 12 -> 23, of which waited for: 12 -> 8; matrix products, arithmetic and copies ran while one was open for 0% -> 0% of each run, Pallas kernels for 4% -> 5%
where the time goes in v4:
time: 60.3 us; the launch traced here: 59.6 us
  starting transfers between devices  36.3 us (60%)
  waiting for transfers between devices  13.7 us (23%)
  Pallas kernels  7.5 us (12%)
  between operations  1.12 us (2%)
  local copies, waits for them, and re-layouts  0.86 us (1%)
    ppermute x23, starting transfers between devices, send(): return lax.ppermute(values, ALL, pairs)  36.3 us
    ppermute x23, waiting for transfers between devices, send(): return lax.ppermute(values, ALL, pairs)  13.7 us
    pallas_call x7, Pallas kernels, call(): pl.pallas_call(kernel, out_shape=outs, in_specs=specs, out_specs=[pl.Bloc...  7.5 us
  transfers between devices with their start and end apart: 23, of which 8 were waited for; matrix products, arithmetic and copies ran while one was open for 0% of the time, Pallas kernels for 5%

profile of v4, /device:TPU:0, one launch (start us, length us, event | category | flops | bytes accessed | tf_op | source)
XLA Modules:
  0.0 59.6 jit_solution(11731808224716767512)
XLA Ops:
  0.6 3.1 %shard_map.84 = (f32[1024,128]{1,0:T(8,128)S(1)}, f32[136,128]{1,0:T(8,128)S(1)}, f32[8,128,128]{2,1,0:T(8,128)S(1)}) custom-call(f32[1024,128]{1,0:T(8,128)} %bitcast.7, f32[128,128]{1,0:T(8,128)} %c.3, f32[8,128]{1,0:T(8,128)} %b_hbm.1), custom_call_target="tpu_custom_call" | custom-call | flops 201326592 | bytes 65536 | tf_op jit(solution)/shard_map/pallas_call | solution.py:37
  3.8 2.4 %collective-permute-start = (f32[136,128]{1,0:T(8,128)S(1)}, f32[136,128]{1,0:T(8,128)S(1)}, u32[]{:S(2)}, u32[]{:S(2)}) collective-permute-start(f32[136,128]{1,0:T(8,128)S(1)} %get-tuple-element.18), channel_id=1, source_target_pairs={{0,1},{2,3},{4,5},{6,7},{8,9},{10,11},{12,13},{14,15},{16,17},{18,... | collective-permute-start | bytes 208904 | tf_op jit(solution)/shard_map/ppermute | solution.py:76
  6.1 1.3 %collective-permute-start.3 = (f32[8,128,128]{2,1,0:T(8,128)S(1)}, f32[8,128,128]{2,1,0:T(8,128)S(1)}, u32[]{:S(2)}, u32[]{:S(2)}) collective-permute-start(f32[8,128,128]{2,1,0:T(8,128)S(1)} %get-tuple-element.20.con), channel_id=1, source_target_pairs={{1,0},{3,2},{5,4},{7,6},{9,8},{11,10},{13,12},{15,14},{17,16},{19,... | collective-permute-start | bytes 1572872 | tf_op jit(solution)/shard_map/ppermute | solution.py:76
  7.4 0.0 collective-permute-done
  7.5 0.0 copy-start.1
  7.5 1.3 %collective-permute-start.1 = (f32[144,128]{1,0:T(8,128)S(1)}, f32[144,128]{1,0:T(8,128)S(1)}, u32[]{:S(2)}, u32[]{:S(2)}) collective-permute-start(f32[144,128]{1,0:T(8,128)S(1)} %pad_maximum_fusion), channel_id=1, source_target_pairs={{1,0},{3,2},{5,4},{7,6},{9,8},{11,10},{13,12},{15,14},{17,16},{19,... | collective-permute-start | bytes 221192 | tf_op jit(solution)/shard_map/ppermute | solution.py:76
  8.8 1.3 %collective-permute-start.2 = (f32[144,128]{1,0:T(8,128)S(1)}, f32[144,128]{1,0:T(8,128)S(1)}, u32[]{:S(2)}, u32[]{:S(2)}) collective-permute-start(f32[144,128]{1,0:T(8,128)S(1)} %pad_maximum_fusion), channel_id=1, source_target_pairs={{1,2},{3,0},{5,6},{7,4},{9,10},{11,8},{13,14},{15,12},{17,18},{19,... | collective-permute-start | bytes 221192 | tf_op jit(solution)/shard_map/ppermute | solution.py:76
  10.1 0.0 copy-start.2
  10.1 1.3 %collective-permute-start.12 = (f32[1024,128]{1,0:T(8,128)S(1)}, f32[1024,128]{1,0:T(8,128)S(1)}, u32[]{:S(2)}, u32[]{:S(2)}) collective-permute-start(f32[1024,128]{1,0:T(8,128)S(1)} %get-tuple-element.26.x), channel_id=1, source_target_pairs={{1,0},{3,2},{5,4},{7,6},{9,8},{11,10},{13,12},{15,14},{17,16},{19,... | collective-permute-start | bytes 1572872 | tf_op jit(solution)/shard_map/ppermute | solution.py:76
  11.4 0.3 shard_map.85
  11.8 3.4 %collective-permute-done.2 = f32[144,128]{1,0:T(8,128)S(1)} collective-permute-done((f32[144,128]{1,0:T(8,128)S(1)}, f32[144,128]{1,0:T(8,128)S(1)}, u32[]{:S(2)}, u32[]{:S(2)}) %collective-permute-start.2) | collective-permute-done | bytes 73760 | tf_op jit(solution)/shard_map/ppermute | solution.py:76
  15.2 0.0 collective-permute-done.3.mate_con
  15.3 0.8 %copy-done = f32[128,128]{1,0:T(8,128)S(1)} copy-done((f32[128,128]{1,0:T(8,128)S(1)}, f32[128,128]{1,0:T(8,128)}, u32[]{:S(2)}) %copy-start) | copy-done | bytes 65560
  16.1 0.8 %shard_map.86 = (f32[128,128]{1,0:T(8,128)S(1)}, f32[16,128]{1,0:T(8,128)S(1)}, f32[144,128]{1,0:T(8,128)S(1)}) custom-call(f32[128,128]{1,0:T(8,128)S(1)} %slice_add_fusion.2.terms, f32[32,128]{1,0:T(8,128)S(1)} %pad_maximum_fusion.1.rows, f32[128,128]{1,0:T(8,128)S(1)} %copy-done, f32[1,128]{1,0:T(1,128)S(1)} %bitcast.4, ...), custom_call_target="tpu_custom_call" | custom-call | flops 50331648 | bytes 65536 | tf_op jit(solution)/shard_map/pallas_call | solution.py:37
  16.9 1.6 %collective-permute-start.4 = (f32[144,128]{1,0:T(8,128)S(1)}, f32[144,128]{1,0:T(8,128)S(1)}, u32[]{:S(2)}, u32[]{:S(2)}) collective-permute-start(f32[144,128]{1,0:T(8,128)S(1)} %get-tuple-element.21), channel_id=1, source_target_pairs={{0,1},{2,3},{4,5},{6,7},{8,9},{10,11},{12,13},{14,15},{16,17},{18,... | collective-permute-start | bytes 221192 | tf_op jit(solution)/shard_map/ppermute | solution.py:76
  18.5 2.4 %collective-permute-start.5 = (f32[144,128]{1,0:T(8,128)S(1)}, f32[144,128]{1,0:T(8,128)S(1)}, u32[]{:S(2)}, u32[]{:S(2)}) collective-permute-start(f32[144,128]{1,0:T(8,128)S(1)} %get-tuple-element.21), channel_id=1, source_target_pairs={{0,5},{2,7},{4,1},{6,3},{8,13},{10,15},{12,9},{14,11},{16,21},{18,... | collective-permute-start | bytes 221192 | tf_op jit(solution)/shard_map/ppermute | solution.py:76
  20.9 1.4 %collective-permute-start.6 = (f32[144,128]{1,0:T(8,128)S(1)}, f32[144,128]{1,0:T(8,128)S(1)}, u32[]{:S(2)}, u32[]{:S(2)}) collective-permute-start(f32[144,128]{1,0:T(8,128)S(1)} %get-tuple-element.21), channel_id=1, source_target_pairs={{0,9},{2,11},{4,13},{6,15},{8,1},{10,3},{12,5},{14,7},{16,25},{18,... | collective-permute-start | bytes 221192 | tf_op jit(solution)/shard_map/ppermute | solution.py:76
  22.3 2.2 %collective-permute-start.7 = (f32[144,128]{1,0:T(8,128)S(1)}, f32[144,128]{1,0:T(8,128)S(1)}, u32[]{:S(2)}, u32[]{:S(2)}) collective-permute-start(f32[144,128]{1,0:T(8,128)S(1)} %get-tuple-element.21), channel_id=1, source_target_pairs={{0,13},{2,15},{4,9},{6,11},{8,5},{10,7},{12,1},{14,3},{16,29},{18,... | collective-permute-start | bytes 221192 | tf_op jit(solution)/shard_map/ppermute | solution.py:76
  24.5 1.3 %collective-permute-start.11 = (f32[128,128]{1,0:T(8,128)S(1)}, f32[128,128]{1,0:T(8,128)S(1)}, u32[]{:S(2)}, u32[]{:S(2)}) collective-permute-start(f32[128,128]{1,0:T(8,128)S(1)} %get-tuple-element.22.moved), channel_id=1, source_target_pairs={{0,1},{2,3},{4,5},{6,7},{8,9},{10,11},{12,13},{14,15},{16,17},{18,... | collective-permute-start | bytes 196616 | tf_op jit(solution)/shard_map/ppermute | solution.py:76
  25.9 0.0 collective-permute-done.6
  25.9 0.6 %collective-permute-done.7 = f32[144,128]{1,0:T(8,128)S(1)} collective-permute-done((f32[144,128]{1,0:T(8,128)S(1)}, f32[144,128]{1,0:T(8,128)S(1)}, u32[]{:S(2)}, u32[]{:S(2)}) %collective-permute-start.7) | collective-permute-done | bytes 73760 | tf_op jit(solution)/shard_map/ppermute | solution.py:76
  26.5 1.3 %collective-permute-start.8 = (f32[144,128]{1,0:T(8,128)S(1)}, f32[144,128]{1,0:T(8,128)S(1)}, u32[]{:S(2)}, u32[]{:S(2)}) collective-permute-start(f32[144,128]{1,0:T(8,128)S(1)} %add_add_fusion), channel_id=1, source_target_pairs={{1,0},{3,2},{5,4},{7,6},{9,8},{11,10},{13,12},{15,14},{17,16},{19,... | collective-permute-start | bytes 221192 | tf_op jit(solution)/shard_map/ppermute | solution.py:76
  27.8 1.3 %collective-permute-start.9 = (f32[144,128]{1,0:T(8,128)S(1)}, f32[144,128]{1,0:T(8,128)S(1)}, u32[]{:S(2)}, u32[]{:S(2)}) collective-permute-start(f32[144,128]{1,0:T(8,128)S(1)} %add_add_fusion), channel_id=1, source_target_pairs={{1,16},{3,18},{5,20},{7,22},{9,24},{11,26},{13,28},{15,30},{17,0},... | collective-permute-start | bytes 221192 | tf_op jit(solution)/shard_map/ppermute | solution.py:76
  29.1 0.0 collective-permute-done.12.mate_x
  29.1 1.1 %shard_map.88.each = f32[16,128,128]{2,1,0:T(8,128)S(1)} custom-call(f32[1024,128]{1,0:T(8,128)S(1)} %get-tuple-element.26.x, f32[1024,128]{1,0:T(8,128)S(1)} %collective-permute-done.12.mate_x, f32[128,128]{1,0:T(8,128)S(1)} %get-tuple-element.22.moved, f32[128,128]{1,0:T(8,128)S(1)} %collective-permute-done.11.mate_moved), custom_call_target="tpu_custom_call" | custom-call | flops 402653184 | bytes 65536 | tf_op jit(solution)/shard_map/pallas_call | solution.py:37
  30.2 0.0 collective-permute-done.8
  30.2 5.0 %collective-permute-done.9 = f32[144,128]{1,0:T(8,128)S(1)} collective-permute-done((f32[144,128]{1,0:T(8,128)S(1)}, f32[144,128]{1,0:T(8,128)S(1)}, u32[]{:S(2)}, u32[]{:S(2)}) %collective-permute-start.9) | collective-permute-done | bytes 73760 | tf_op jit(solution)/shard_map/ppermute | solution.py:76
  35.3 0.3 shard_map.89
  35.5 1.3 %collective-permute-start.13 = (f32[144,128]{1,0:T(8,128)S(1)}, f32[144,128]{1,0:T(8,128)S(1)}, u32[]{:S(2)}, u32[]{:S(2)}) collective-permute-start(f32[144,128]{1,0:T(8,128)S(1)} %shard_map.89), channel_id=1, source_target_pairs={{0,1},{2,3},{4,5},{6,7},{8,9},{10,11},{12,13},{14,15},{16,17},{18,... | collective-permute-start | bytes 221192 | tf_op jit(solution)/shard_map/ppermute | solution.py:76
  36.8 1.3 %collective-permute-start.14 = (f32[144,128]{1,0:T(8,128)S(1)}, f32[144,128]{1,0:T(8,128)S(1)}, u32[]{:S(2)}, u32[]{:S(2)}) collective-permute-start(f32[144,128]{1,0:T(8,128)S(1)} %shard_map.89), channel_id=1, source_target_pairs={{0,3},{2,1},{4,7},{6,5},{8,11},{10,9},{12,15},{14,13},{16,19},{18,... | collective-permute-start | bytes 221192 | tf_op jit(solution)/shard_map/ppermute | solution.py:76
  38.1 1.3 %collective-permute-start.15 = (f32[144,128]{1,0:T(8,128)S(1)}, f32[144,128]{1,0:T(8,128)S(1)}, u32[]{:S(2)}, u32[]{:S(2)}) collective-permute-start(f32[144,128]{1,0:T(8,128)S(1)} %shard_map.89), channel_id=1, source_target_pairs={{0,5},{2,7},{4,1},{6,3},{8,13},{10,15},{12,9},{14,11},{16,21},{18,... | collective-permute-start | bytes 221192 | tf_op jit(solution)/shard_map/ppermute | solution.py:76
  39.4 1.3 %collective-permute-start.16 = (f32[144,128]{1,0:T(8,128)S(1)}, f32[144,128]{1,0:T(8,128)S(1)}, u32[]{:S(2)}, u32[]{:S(2)}) collective-permute-start(f32[144,128]{1,0:T(8,128)S(1)} %shard_map.89), channel_id=1, source_target_pairs={{0,7},{2,5},{4,3},{6,1},{8,15},{10,13},{12,11},{14,9},{16,23},{18,... | collective-permute-start | bytes 221192 | tf_op jit(solution)/shard_map/ppermute | solution.py:76
  40.7 0.0 collective-permute-done.13
  40.8 0.6 %collective-permute-done.15 = f32[144,128]{1,0:T(8,128)S(1)} collective-permute-done((f32[144,128]{1,0:T(8,128)S(1)}, f32[144,128]{1,0:T(8,128)S(1)}, u32[]{:S(2)}, u32[]{:S(2)}) %collective-permute-start.15) | collective-permute-done | bytes 73760 | tf_op jit(solution)/shard_map/ppermute | solution.py:76
  41.4 1.3 %collective-permute-done.16 = f32[144,128]{1,0:T(8,128)S(1)} collective-permute-done((f32[144,128]{1,0:T(8,128)S(1)}, f32[144,128]{1,0:T(8,128)S(1)}, u32[]{:S(2)}, u32[]{:S(2)}) %collective-permute-start.16) | collective-permute-done | bytes 73760 | tf_op jit(solution)/shard_map/ppermute | solution.py:76
  42.7 1.3 %collective-permute-start.17 = (f32[128,128]{1,0:T(8,128)S(1)}, f32[128,128]{1,0:T(8,128)S(1)}, u32[]{:S(2)}, u32[]{:S(2)}) collective-permute-start(f32[128,128]{1,0:T(8,128)S(1)} %fusion), channel_id=1, source_target_pairs={{1,0},{3,2},{5,4},{7,6},{9,8},{11,10},{13,12},{15,14},{17,16},{19,... | collective-permute-start | bytes 196616 | tf_op jit(solution)/shard_map/ppermute | solution.py:76
  44.0 1.3 %collective-permute-start.18 = (f32[128,128]{1,0:T(8,128)S(1)}, f32[128,128]{1,0:T(8,128)S(1)}, u32[]{:S(2)}, u32[]{:S(2)}) collective-permute-start(f32[128,128]{1,0:T(8,128)S(1)} %fusion), channel_id=1, source_target_pairs={{1,8},{3,10},{5,12},{7,14},{9,0},{11,2},{13,4},{15,6},{17,24},{19,... | collective-permute-start | bytes 196616 | tf_op jit(solution)/shard_map/ppermute | solution.py:76
  45.3 1.3 %collective-permute-start.19 = (f32[128,128]{1,0:T(8,128)S(1)}, f32[128,128]{1,0:T(8,128)S(1)}, u32[]{:S(2)}, u32[]{:S(2)}) collective-permute-start(f32[128,128]{1,0:T(8,128)S(1)} %fusion), channel_id=1, source_target_pairs={{1,16},{3,18},{5,20},{7,22},{9,24},{11,26},{13,28},{15,30},{17,0},... | collective-permute-start | bytes 196616 | tf_op jit(solution)/shard_map/ppermute | solution.py:76
  46.6 1.3 %collective-permute-start.20 = (f32[128,128]{1,0:T(8,128)S(1)}, f32[128,128]{1,0:T(8,128)S(1)}, u32[]{:S(2)}, u32[]{:S(2)}) collective-permute-start(f32[128,128]{1,0:T(8,128)S(1)} %fusion), channel_id=1, source_target_pairs={{1,24},{3,26},{5,28},{7,30},{9,16},{11,18},{13,20},{15,22},{17,8},... | collective-permute-start | bytes 196616 | tf_op jit(solution)/shard_map/ppermute | solution.py:76
  47.9 4.4 %collective-permute-start.10 = (f32[144,128]{1,0:T(8,128)S(1)}, f32[144,128]{1,0:T(8,128)S(1)}, u32[]{:S(2)}, u32[]{:S(2)}) collective-permute-start(f32[144,128]{1,0:T(8,128)S(1)} %add.41.sums), channel_id=1, source_target_pairs={{0,1},{2,3},{4,5},{6,7},{8,9},{10,11},{12,13},{14,15},{16,17},{18,... | collective-permute-start | bytes 221192 | tf_op jit(solution)/shard_map/ppermute | solution.py:76
  52.3 0.0 slice-start
  52.4 0.1 collective-permute-done.19
  52.5 1.5 %collective-permute-done.20 = f32[128,128]{1,0:T(8,128)S(1)} collective-permute-done((f32[128,128]{1,0:T(8,128)S(1)}, f32[128,128]{1,0:T(8,128)S(1)}, u32[]{:S(2)}, u32[]{:S(2)}) %collective-permute-start.20) | collective-permute-done | bytes 65568 | tf_op jit(solution)/shard_map/ppermute | solution.py:76
  54.0 1.3 %collective-permute-start.21 = (f32[128,128]{1,0:T(8,128)S(1)}, f32[128,128]{1,0:T(8,128)S(1)}, u32[]{:S(2)}, u32[]{:S(2)}) collective-permute-start(f32[128,128]{1,0:T(8,128)S(1)} %add_add_fusion.1.terms), channel_id=1, source_target_pairs={{0,1},{2,3},{4,5},{6,7},{8,9},{10,11},{12,13},{14,15},{16,17},{18,... | collective-permute-start | bytes 196616 | tf_op jit(solution)/shard_map/ppermute | solution.py:76
  55.3 1.3 %collective-permute-start.22 = (f32[32,128]{1,0:T(8,128)S(1)}, f32[32,128]{1,0:T(8,128)S(1)}, u32[]{:S(2)}, u32[]{:S(2)}) collective-permute-start(f32[32,128]{1,0:T(8,128)S(1)} %pad_maximum_fusion.2.rows), channel_id=1, source_target_pairs={{1,0},{3,2},{5,4},{7,6},{9,8},{11,10},{13,12},{15,14},{17,16},{19,... | collective-permute-start | bytes 49160 | tf_op jit(solution)/shard_map/ppermute | solution.py:76
  56.7 0.7 %shard_map.87 = (f32[128,128]{1,0:T(8,128)}, f32[1,128]{1,0:T(1,128)S(1)}, f32[128,128]{1,0:T(8,128)S(1)}) custom-call(f32[144,128]{1,0:T(8,128)S(1)} %add.41.sums, f32[144,128]{1,0:T(8,128)S(1)} %collective-permute-done.10.mate_sums, f32[128,128]{1,0:T(8,128)S(1)} %get-tuple-element.22.moved, f32[128,128]{1,0:T(8,128)S(1)} %collective-permute-done.11.mate_moved, ...), custom_call_target="tpu_custom_call" | custom-call | flops 131072 | bytes 65536 | tf_op jit(solution)/shard_map/pallas_call | solution.py:37
  57.3 1.1 %collective-permute-done.22.mate_rows = f32[32,128]{1,0:T(8,128)S(1)} collective-permute-done((f32[32,128]{1,0:T(8,128)S(1)}, f32[32,128]{1,0:T(8,128)S(1)}, u32[]{:S(2)}, u32[]{:S(2)}) %collective-permute-start.22) | collective-permute-done | bytes 16416 | tf_op jit(solution)/shard_map/ppermute | solution.py:76
  58.4 1.2 %shard_map.90 = (f32[8,128]{1,0:T(8,128)}, f32[128,128]{1,0:T(8,128)}, f32[1,128]{1,0:T(1,128)}) custom-call(f32[128,128]{1,0:T(8,128)S(1)} %add_add_fusion.1.terms, f32[128,128]{1,0:T(8,128)S(1)} %collective-permute-done.21.mate_terms, f32[32,128]{1,0:T(8,128)S(1)} %pad_maximum_fusion.2.rows, f32[32,128]{1,0:T(8,128)S(1)} %collective-permute-done.22.mate_rows, ...), custom_call_target="tpu_custom_call" | custom-call | flops 25165824 | bytes 65536 | tf_op jit(solution)/shard_map/pallas_call | solution.py:37
  (32 shorter events, 0.2 us)
Async XLA Ops:
  3.8 3.7 %collective-permute-start = (f32[136,128]{1,0:T(8,128)S(1)}, f32[136,128]{1,0:T(8,128)S(1)}, u32[]{:S(2)}, u32[]{:S(2)}) collective-permute-start(f32[136,128]{1,0:T(8,128)S(1)} %get-tuple-element.18), channel_id=1, source_target_pairs={{0,1},{2,3},{4,5},{6,7},{8,9},{10,11},{12,13},{14,15},{16,17},{18,... | collective-permute-start | bytes 208904 | tf_op jit(solution)/shard_map/ppermute | solution.py:76
  6.1 9.1 %collective-permute-start.3 = (f32[8,128,128]{2,1,0:T(8,128)S(1)}, f32[8,128,128]{2,1,0:T(8,128)S(1)}, u32[]{:S(2)}, u32[]{:S(2)}) collective-permute-start(f32[8,128,128]{2,1,0:T(8,128)S(1)} %get-tuple-element.20.con), channel_id=1, source_target_pairs={{1,0},{3,2},{5,4},{7,6},{9,8},{11,10},{13,12},{15,14},{17,16},{19,... | collective-permute-start | bytes 1572872 | tf_op jit(solution)/shard_map/ppermute | solution.py:76
  7.5 3.9 %copy-start.1 = (f32[128,128]{1,0:T(8,128)S(1)}, f32[128,128]{1,0:T(8,128)}, u32[]{:S(2)}) copy-start(f32[128,128]{1,0:T(8,128)} %c.3) | copy-start | bytes 196612
  7.5 4.3 %collective-permute-start.1 = (f32[144,128]{1,0:T(8,128)S(1)}, f32[144,128]{1,0:T(8,128)S(1)}, u32[]{:S(2)}, u32[]{:S(2)}) collective-permute-start(f32[144,128]{1,0:T(8,128)S(1)} %pad_maximum_fusion), channel_id=1, source_target_pairs={{1,0},{3,2},{5,4},{7,6},{9,8},{11,10},{13,12},{15,14},{17,16},{19,... | collective-permute-start | bytes 221192 | tf_op jit(solution)/shard_map/ppermute | solution.py:76
  8.8 6.4 %collective-permute-start.2 = (f32[144,128]{1,0:T(8,128)S(1)}, f32[144,128]{1,0:T(8,128)S(1)}, u32[]{:S(2)}, u32[]{:S(2)}) collective-permute-start(f32[144,128]{1,0:T(8,128)S(1)} %pad_maximum_fusion), channel_id=1, source_target_pairs={{1,2},{3,0},{5,6},{7,4},{9,10},{11,8},{13,14},{15,12},{17,18},{19,... | collective-permute-start | bytes 221192 | tf_op jit(solution)/shard_map/ppermute | solution.py:76
  10.1 1.3 %copy-start.2 = (f32[128]{0:T(128)S(1)}, f32[128]{0:T(128)}, u32[]{:S(2)}) copy-start(f32[128]{0:T(128)} %param.9) | copy-start | bytes 1540
  10.1 19.0 %collective-permute-start.12 = (f32[1024,128]{1,0:T(8,128)S(1)}, f32[1024,128]{1,0:T(8,128)S(1)}, u32[]{:S(2)}, u32[]{:S(2)}) collective-permute-start(f32[1024,128]{1,0:T(8,128)S(1)} %get-tuple-element.26.x), channel_id=1, source_target_pairs={{1,0},{3,2},{5,4},{7,6},{9,8},{11,10},{13,12},{15,14},{17,16},{19,... | collective-permute-start | bytes 1572872 | tf_op jit(solution)/shard_map/ppermute | solution.py:76
  15.2 0.8 %copy-start = (f32[128,128]{1,0:T(8,128)S(1)}, f32[128,128]{1,0:T(8,128)}, u32[]{:S(2)}) copy-start(f32[128,128]{1,0:T(8,128)} %a.1) | copy-start | bytes 196612
  16.9 7.6 %collective-permute-start.4 = (f32[144,128]{1,0:T(8,128)S(1)}, f32[144,128]{1,0:T(8,128)S(1)}, u32[]{:S(2)}, u32[]{:S(2)}) collective-permute-start(f32[144,128]{1,0:T(8,128)S(1)} %get-tuple-element.21), channel_id=1, source_target_pairs={{0,1},{2,3},{4,5},{6,7},{8,9},{10,11},{12,13},{14,15},{16,17},{18,... | collective-permute-start | bytes 221192 | tf_op jit(solution)/shard_map/ppermute | solution.py:76
  18.5 7.3 %collective-permute-start.5 = (f32[144,128]{1,0:T(8,128)S(1)}, f32[144,128]{1,0:T(8,128)S(1)}, u32[]{:S(2)}, u32[]{:S(2)}) collective-permute-start(f32[144,128]{1,0:T(8,128)S(1)} %get-tuple-element.21), channel_id=1, source_target_pairs={{0,5},{2,7},{4,1},{6,3},{8,13},{10,15},{12,9},{14,11},{16,21},{18,... | collective-permute-start | bytes 221192 | tf_op jit(solution)/shard_map/ppermute | solution.py:76
  20.9 4.9 %collective-permute-start.6 = (f32[144,128]{1,0:T(8,128)S(1)}, f32[144,128]{1,0:T(8,128)S(1)}, u32[]{:S(2)}, u32[]{:S(2)}) collective-permute-start(f32[144,128]{1,0:T(8,128)S(1)} %get-tuple-element.21), channel_id=1, source_target_pairs={{0,9},{2,11},{4,13},{6,15},{8,1},{10,3},{12,5},{14,7},{16,25},{18,... | collective-permute-start | bytes 221192 | tf_op jit(solution)/shard_map/ppermute | solution.py:76
  22.3 4.2 %collective-permute-start.7 = (f32[144,128]{1,0:T(8,128)S(1)}, f32[144,128]{1,0:T(8,128)S(1)}, u32[]{:S(2)}, u32[]{:S(2)}) collective-permute-start(f32[144,128]{1,0:T(8,128)S(1)} %get-tuple-element.21), channel_id=1, source_target_pairs={{0,13},{2,15},{4,9},{6,11},{8,5},{10,7},{12,1},{14,3},{16,29},{18,... | collective-permute-start | bytes 221192 | tf_op jit(solution)/shard_map/ppermute | solution.py:76
  24.5 4.6 %collective-permute-start.11 = (f32[128,128]{1,0:T(8,128)S(1)}, f32[128,128]{1,0:T(8,128)S(1)}, u32[]{:S(2)}, u32[]{:S(2)}) collective-permute-start(f32[128,128]{1,0:T(8,128)S(1)} %get-tuple-element.22.moved), channel_id=1, source_target_pairs={{0,1},{2,3},{4,5},{6,7},{8,9},{10,11},{12,13},{14,15},{16,17},{18,... | collective-permute-start | bytes 196616 | tf_op jit(solution)/shard_map/ppermute | solution.py:76
  26.5 3.7 %collective-permute-start.8 = (f32[144,128]{1,0:T(8,128)S(1)}, f32[144,128]{1,0:T(8,128)S(1)}, u32[]{:S(2)}, u32[]{:S(2)}) collective-permute-start(f32[144,128]{1,0:T(8,128)S(1)} %add_add_fusion), channel_id=1, source_target_pairs={{1,0},{3,2},{5,4},{7,6},{9,8},{11,10},{13,12},{15,14},{17,16},{19,... | collective-permute-start | bytes 221192 | tf_op jit(solution)/shard_map/ppermute | solution.py:76
  27.8 7.4 %collective-permute-start.9 = (f32[144,128]{1,0:T(8,128)S(1)}, f32[144,128]{1,0:T(8,128)S(1)}, u32[]{:S(2)}, u32[]{:S(2)}) collective-permute-start(f32[144,128]{1,0:T(8,128)S(1)} %add_add_fusion), channel_id=1, source_target_pairs={{1,16},{3,18},{5,20},{7,22},{9,24},{11,26},{13,28},{15,30},{17,0},... | collective-permute-start | bytes 221192 | tf_op jit(solution)/shard_map/ppermute | solution.py:76
  35.5 5.2 %collective-permute-start.13 = (f32[144,128]{1,0:T(8,128)S(1)}, f32[144,128]{1,0:T(8,128)S(1)}, u32[]{:S(2)}, u32[]{:S(2)}) collective-permute-start(f32[144,128]{1,0:T(8,128)S(1)} %shard_map.89), channel_id=1, source_target_pairs={{0,1},{2,3},{4,5},{6,7},{8,9},{10,11},{12,13},{14,15},{16,17},{18,... | collective-permute-start | bytes 221192 | tf_op jit(solution)/shard_map/ppermute | solution.py:76
  36.8 3.9 %collective-permute-start.14 = (f32[144,128]{1,0:T(8,128)S(1)}, f32[144,128]{1,0:T(8,128)S(1)}, u32[]{:S(2)}, u32[]{:S(2)}) collective-permute-start(f32[144,128]{1,0:T(8,128)S(1)} %shard_map.89), channel_id=1, source_target_pairs={{0,3},{2,1},{4,7},{6,5},{8,11},{10,9},{12,15},{14,13},{16,19},{18,... | collective-permute-start | bytes 221192 | tf_op jit(solution)/shard_map/ppermute | solution.py:76
  38.1 3.3 %collective-permute-start.15 = (f32[144,128]{1,0:T(8,128)S(1)}, f32[144,128]{1,0:T(8,128)S(1)}, u32[]{:S(2)}, u32[]{:S(2)}) collective-permute-start(f32[144,128]{1,0:T(8,128)S(1)} %shard_map.89), channel_id=1, source_target_pairs={{0,5},{2,7},{4,1},{6,3},{8,13},{10,15},{12,9},{14,11},{16,21},{18,... | collective-permute-start | bytes 221192 | tf_op jit(solution)/shard_map/ppermute | solution.py:76
  39.4 3.3 %collective-permute-start.16 = (f32[144,128]{1,0:T(8,128)S(1)}, f32[144,128]{1,0:T(8,128)S(1)}, u32[]{:S(2)}, u32[]{:S(2)}) collective-permute-start(f32[144,128]{1,0:T(8,128)S(1)} %shard_map.89), channel_id=1, source_target_pairs={{0,7},{2,5},{4,3},{6,1},{8,15},{10,13},{12,11},{14,9},{16,23},{18,... | collective-permute-start | bytes 221192 | tf_op jit(solution)/shard_map/ppermute | solution.py:76
  40.7 11.6 %copy-start.3 = (f32[144,128]{1,0:T(8,128)}, f32[144,128]{1,0:T(8,128)S(1)}, u32[]{:S(2)}) copy-start(f32[144,128]{1,0:T(8,128)S(1)} %collective-permute-done.13) | copy-start | bytes 221188
  40.8 11.6 %copy-start.4 = (f32[144,128]{1,0:T(8,128)}, f32[144,128]{1,0:T(8,128)S(1)}, u32[]{:S(2)}) copy-start(f32[144,128]{1,0:T(8,128)S(1)} %collective-permute-done.14) | copy-start | bytes 221188
  42.7 9.6 %collective-permute-start.17 = (f32[128,128]{1,0:T(8,128)S(1)}, f32[128,128]{1,0:T(8,128)S(1)}, u32[]{:S(2)}, u32[]{:S(2)}) collective-permute-start(f32[128,128]{1,0:T(8,128)S(1)} %fusion), channel_id=1, source_target_pairs={{1,0},{3,2},{5,4},{7,6},{9,8},{11,10},{13,12},{15,14},{17,16},{19,... | collective-permute-start | bytes 196616 | tf_op jit(solution)/shard_map/ppermute | solution.py:76
  44.0 8.3 %collective-permute-start.18 = (f32[128,128]{1,0:T(8,128)S(1)}, f32[128,128]{1,0:T(8,128)S(1)}, u32[]{:S(2)}, u32[]{:S(2)}) collective-permute-start(f32[128,128]{1,0:T(8,128)S(1)} %fusion), channel_id=1, source_target_pairs={{1,8},{3,10},{5,12},{7,14},{9,0},{11,2},{13,4},{15,6},{17,24},{19,... | collective-permute-start | bytes 196616 | tf_op jit(solution)/shard_map/ppermute | solution.py:76
  45.3 7.2 %collective-permute-start.19 = (f32[128,128]{1,0:T(8,128)S(1)}, f32[128,128]{1,0:T(8,128)S(1)}, u32[]{:S(2)}, u32[]{:S(2)}) collective-permute-start(f32[128,128]{1,0:T(8,128)S(1)} %fusion), channel_id=1, source_target_pairs={{1,16},{3,18},{5,20},{7,22},{9,24},{11,26},{13,28},{15,30},{17,0},... | collective-permute-start | bytes 196616 | tf_op jit(solution)/shard_map/ppermute | solution.py:76
  46.6 7.4 %collective-permute-start.20 = (f32[128,128]{1,0:T(8,128)S(1)}, f32[128,128]{1,0:T(8,128)S(1)}, u32[]{:S(2)}, u32[]{:S(2)}) collective-permute-start(f32[128,128]{1,0:T(8,128)S(1)} %fusion), channel_id=1, source_target_pairs={{1,24},{3,26},{5,28},{7,30},{9,16},{11,18},{13,20},{15,22},{17,8},... | collective-permute-start | bytes 196616 | tf_op jit(solution)/shard_map/ppermute | solution.py:76
  47.9 8.7 %collective-permute-start.10 = (f32[144,128]{1,0:T(8,128)S(1)}, f32[144,128]{1,0:T(8,128)S(1)}, u32[]{:S(2)}, u32[]{:S(2)}) collective-permute-start(f32[144,128]{1,0:T(8,128)S(1)} %add.41.sums), channel_id=1, source_target_pairs={{0,1},{2,3},{4,5},{6,7},{8,9},{10,11},{12,13},{14,15},{16,17},{18,... | collective-permute-start | bytes 221192 | tf_op jit(solution)/shard_map/ppermute | solution.py:76
  52.3 3.0 %slice-start = ((f32[144,128]{1,0:T(8,128)}), f32[16,128]{1,0:T(8,128)S(1)}, s32[]{:S(2)}) async-start(f32[144,128]{1,0:T(8,128)} %copy-done.3), calls=%async_computation | async-start | bytes 16384 | tf_op jit(solution)/shard_map/slice | solution.py:260
  52.3 3.0 %slice-start.1 = ((f32[144,128]{1,0:T(8,128)}), f32[16,128]{1,0:T(8,128)S(1)}, s32[]{:S(2)}) async-start(f32[144,128]{1,0:T(8,128)} %copy-done.4), calls=%async_computation.1 | async-start | bytes 16384 | tf_op jit(solution)/shard_map/slice | solution.py:260
  54.0 4.4 %collective-permute-start.21 = (f32[128,128]{1,0:T(8,128)S(1)}, f32[128,128]{1,0:T(8,128)S(1)}, u32[]{:S(2)}, u32[]{:S(2)}) collective-permute-start(f32[128,128]{1,0:T(8,128)S(1)} %add_add_fusion.1.terms), channel_id=1, source_target_pairs={{0,1},{2,3},{4,5},{6,7},{8,9},{10,11},{12,13},{14,15},{16,17},{18,... | collective-permute-start | bytes 196616 | tf_op jit(solution)/shard_map/ppermute | solution.py:76
  55.3 3.1 %collective-permute-start.22 = (f32[32,128]{1,0:T(8,128)S(1)}, f32[32,128]{1,0:T(8,128)S(1)}, u32[]{:S(2)}, u32[]{:S(2)}) collective-permute-start(f32[32,128]{1,0:T(8,128)S(1)} %pad_maximum_fusion.2.rows), channel_id=1, source_target_pairs={{1,0},{3,2},{5,4},{7,6},{9,8},{11,10},{13,12},{15,14},{17,16},{19,... | collective-permute-start | bytes 49160 | tf_op jit(solution)/shard_map/ppermute | solution.py:76

commit v5 on v4

--- a/solution.py
+++ b/solution.py
@@ -59,7 +59,7 @@
     return [1 << b for b in range(count.bit_length() - 1)]
 
 
-def groups_of(bits, size=2):
+def groups_of(bits, size=1):
     return [bits[i : i + size] for i in range(0, len(bits), size)]
 
 
@@ -72,16 +72,16 @@
 
 def send(values, holder, mask=0):
     count = lax.axis_size(ALL)
-    pairs = [(i, i ^ 1 ^ mask) for i in range(count) if i & 1 == holder]
+    pairs = [(i, i ^ 1 ^ mask if i & 1 == holder else i ^ 1) for i in range(count)]
     return lax.ppermute(values, ALL, pairs)
 
 
 def fan(values, holder, masks):
-    sent = [send(values, holder, mask) for mask in reversed(masks)]
-    return sent[::-1]
+    return [send(values, holder, mask) for mask in masks]
 
 
 def tree(parts):
+    parts = parts[::-1]
     while len(parts) > 1:
         parts = [a + b for a, b in zip(parts[::2], parts[1::2])]
     return parts[0]
@@ -99,7 +99,7 @@
     block = scratch.shape[0] // chips
     chip = smp_index() // 2
     for p in range(chips):
-        scratch[pl.ds(pl.multiple_of((chip ^ p) * block, block), block), :] = rows[p * block : (p + 1) * block, :]
+        scratch[pl.ds(pl.multiple_of((chip ^ (chips - 1 - p)) * block, block), block), :] = rows[p * block : (p + 1) * block, :]
     return scratch[...]
 
 
@@ -166,7 +166,7 @@
     for group in groups_of(chip_bits):
         parts = fan(jnp.concatenate([terms, rows_b], axis=0), holder, masks_of(group))
         terms = tree([part[:vox_rows] for part in parts])
-        rows_b = jnp.concatenate([part[vox_rows:] for part in parts], axis=0)
+        rows_b = jnp.concatenate([part[vox_rows:] for part in parts[::-1]], axis=0)
         holder ^= 1
     voxel_core = holder
     mate_con = send(con, 1 - voxel_core)
@@ -257,7 +257,7 @@
         holder ^= 1
         if with_rows:
             parts = [part for part, mask in zip(parts, masks) if not mask & ~smp_mask]
-            rows_b = jnp.concatenate([part[times:] for part in parts], axis=0)
+            rows_b = jnp.concatenate([part[times:] for part in parts[::-1]], axis=0)
             rows_core = holder
     last_core = holder
     mate_rows_b = send(rows_b, rows_core)

time: 60.3 us -> 39.2 us (0.65)
  starting transfers between devices: 36.3 us -> 12.8 us
  waiting for transfers between devices: 13.7 us -> 16.3 us
  local copies, waits for them, and re-layouts: 0.86 us -> 1.48 us
    ppermute x23 -> x24, starting transfers between devices: 36.3 us -> 12.8 us  [send(): return lax.ppermute(values, ALL, pairs)]
    ppermute x23 -> x24, waiting for transfers between devices: 13.7 us -> 16.3 us  [send(): return lax.ppermute(values, ALL, pairs)]
    unnamed x10, local copies, waits for them, and re-layouts: 0.84 us -> 1.47 us
  transfers between devices with their start and end apart: 23 -> 24, of which waited for: 8 -> 10; matrix products, arithmetic and copies ran while one was open for 0% -> 0% of each run, Pallas kernels for 5% -> 8%
where the time goes in v5:
time: 39.2 us; the launch traced here: 39 us
  waiting for transfers between devices  16.3 us (42%)
  starting transfers between devices  12.8 us (33%)
  Pallas kernels  7.49 us (19%)
  local copies, waits for them, and re-layouts  1.48 us (4%)
  between operations  0.8 us (2%)
    ppermute x24, waiting for transfers between devices, send(): return lax.ppermute(values, ALL, pairs)  16.3 us
    ppermute x24, starting transfers between devices, send(): return lax.ppermute(values, ALL, pairs)  12.8 us
    pallas_call x7, Pallas kernels, call(): pl.pallas_call(kernel, out_shape=outs, in_specs=specs, out_specs=[pl.Bloc...  7.49 us
    unnamed x10, local copies, waits for them, and re-layouts  1.47 us
  transfers between devices with their start and end apart: 24, of which 10 were waited for; matrix products, arithmetic and copies ran while one was open for 0% of the time, Pallas kernels for 8%

profile of v5, /device:TPU:0, one launch (start us, length us, event | category | flops | bytes accessed | tf_op | source)
XLA Modules:
  0.0 39.0 jit_solution(703703541044378196)
XLA Ops:
  0.6 3.1 %shard_map.84 = (f32[1024,128]{1,0:T(8,128)S(1)}, f32[136,128]{1,0:T(8,128)S(1)}, f32[8,128,128]{2,1,0:T(8,128)S(1)}) custom-call(f32[1024,128]{1,0:T(8,128)} %bitcast.7, f32[128,128]{1,0:T(8,128)} %c.3, f32[8,128]{1,0:T(8,128)} %b_hbm.1), custom_call_target="tpu_custom_call" | custom-call | flops 201326592 | bytes 65536 | tf_op jit(solution)/shard_map/pallas_call | solution.py:37
  3.8 0.5 %collective-permute-start = (f32[136,128]{1,0:T(8,128)S(1)}, f32[136,128]{1,0:T(8,128)S(1)}, u32[]{:S(2)}, u32[]{:S(2)}) collective-permute-start(f32[136,128]{1,0:T(8,128)S(1)} %get-tuple-element.18), channel_id=1, source_target_pairs={{0,1},{1,0},{2,3},{3,2},{4,5},{5,4},{6,7},{7,6},{8,9},{9,8},{10,11... | collective-permute-start | bytes 208904 | tf_op jit(solution)/shard_map/ppermute | solution.py:76
  4.3 0.1 collective-permute-start.3
  4.4 0.8 %collective-permute-done = f32[136,128]{1,0:T(8,128)S(1)} collective-permute-done((f32[136,128]{1,0:T(8,128)S(1)}, f32[136,128]{1,0:T(8,128)S(1)}, u32[]{:S(2)}, u32[]{:S(2)}) %collective-permute-start) | collective-permute-done | bytes 69664 | tf_op jit(solution)/shard_map/ppermute | solution.py:76
  5.2 0.0 copy-start.1
  5.2 0.4 %collective-permute-start.1 = (f32[144,128]{1,0:T(8,128)S(1)}, f32[144,128]{1,0:T(8,128)S(1)}, u32[]{:S(2)}, u32[]{:S(2)}) collective-permute-start(f32[144,128]{1,0:T(8,128)S(1)} %pad_maximum_fusion), channel_id=1, source_target_pairs={{0,1},{1,2},{2,3},{3,0},{4,5},{5,6},{6,7},{7,4},{8,9},{9,10},{10,1... | collective-permute-start | bytes 221192 | tf_op jit(solution)/shard_map/ppermute | solution.py:76
  5.6 2.6 %collective-permute-start.2 = (f32[144,128]{1,0:T(8,128)S(1)}, f32[144,128]{1,0:T(8,128)S(1)}, u32[]{:S(2)}, u32[]{:S(2)}) collective-permute-start(f32[144,128]{1,0:T(8,128)S(1)} %pad_maximum_fusion), channel_id=1, source_target_pairs={{0,1},{1,0},{2,3},{3,2},{4,5},{5,4},{6,7},{7,6},{8,9},{9,8},{10,11... | collective-permute-start | bytes 221192 | tf_op jit(solution)/shard_map/ppermute | solution.py:76
  8.3 0.0 collective-permute-start.13
  8.3 0.6 %copy-done.2 = f32[128]{0:T(128)S(1)} copy-done((f32[128]{0:T(128)S(1)}, f32[128]{0:T(128)}, u32[]{:S(2)}) %copy-start.2) | copy-done | bytes 536
  8.9 0.3 shard_map.85
  9.3 0.7 %collective-permute-done.1 = f32[144,128]{1,0:T(8,128)S(1)} collective-permute-done((f32[144,128]{1,0:T(8,128)S(1)}, f32[144,128]{1,0:T(8,128)S(1)}, u32[]{:S(2)}, u32[]{:S(2)}) %collective-permute-start.1) | collective-permute-done | bytes 73760 | tf_op jit(solution)/shard_map/ppermute | solution.py:76
  10.0 0.0 copy-start
  10.0 0.8 %copy-done = f32[128,128]{1,0:T(8,128)S(1)} copy-done((f32[128,128]{1,0:T(8,128)S(1)}, f32[128,128]{1,0:T(8,128)}, u32[]{:S(2)}) %copy-start) | copy-done | bytes 65560
  10.8 0.8 %shard_map.86 = (f32[128,128]{1,0:T(8,128)S(1)}, f32[16,128]{1,0:T(8,128)S(1)}, f32[144,128]{1,0:T(8,128)S(1)}) custom-call(f32[128,128]{1,0:T(8,128)S(1)} %slice_add_fusion.1.terms, f32[32,128]{1,0:T(8,128)S(1)} %pad_maximum_fusion.1.rows, f32[128,128]{1,0:T(8,128)S(1)} %copy-done, f32[1,128]{1,0:T(1,128)S(1)} %bitcast.4, ...), custom_call_target="tpu_custom_call" | custom-call | flops 50331648 | bytes 65536 | tf_op jit(solution)/shard_map/pallas_call | solution.py:37
  11.6 0.9 %collective-permute-start.4 = (f32[144,128]{1,0:T(8,128)S(1)}, f32[144,128]{1,0:T(8,128)S(1)}, u32[]{:S(2)}, u32[]{:S(2)}) collective-permute-start(f32[144,128]{1,0:T(8,128)S(1)} %get-tuple-element.21), channel_id=1, source_target_pairs={{0,5},{1,0},{2,7},{3,2},{4,1},{5,4},{6,3},{7,6},{8,13},{9,8},{10,1... | collective-permute-start | bytes 221192 | tf_op jit(solution)/shard_map/ppermute | solution.py:76
  12.5 2.0 %collective-permute-done.4 = f32[144,128]{1,0:T(8,128)S(1)} collective-permute-done((f32[144,128]{1,0:T(8,128)S(1)}, f32[144,128]{1,0:T(8,128)S(1)}, u32[]{:S(2)}, u32[]{:S(2)}) %collective-permute-start.4) | collective-permute-done | bytes 73760 | tf_op jit(solution)/shard_map/ppermute | solution.py:76
  14.5 0.0 collective-permute-done.5
  14.5 1.4 %collective-permute-start.6 = (f32[144,128]{1,0:T(8,128)S(1)}, f32[144,128]{1,0:T(8,128)S(1)}, u32[]{:S(2)}, u32[]{:S(2)}) collective-permute-start(f32[144,128]{1,0:T(8,128)S(1)} %add.29), channel_id=1, source_target_pairs={{0,1},{1,8},{2,3},{3,10},{4,5},{5,12},{6,7},{7,14},{8,9},{9,0},{10... | collective-permute-start | bytes 221192 | tf_op jit(solution)/shard_map/ppermute | solution.py:76
  15.9 0.4 collective-permute-start.7
  16.3 0.1 collective-permute-start.11
  16.4 2.7 %collective-permute-done.6 = f32[144,128]{1,0:T(8,128)S(1)} collective-permute-done((f32[144,128]{1,0:T(8,128)S(1)}, f32[144,128]{1,0:T(8,128)S(1)}, u32[]{:S(2)}, u32[]{:S(2)}) %collective-permute-start.6) | collective-permute-done | bytes 73760 | tf_op jit(solution)/shard_map/ppermute | solution.py:76
  19.1 0.0 collective-permute-done.7
  19.1 0.8 %collective-permute-start.8 = (f32[144,128]{1,0:T(8,128)S(1)}, f32[144,128]{1,0:T(8,128)S(1)}, u32[]{:S(2)}, u32[]{:S(2)}) collective-permute-start(f32[144,128]{1,0:T(8,128)S(1)} %add.30), channel_id=1, source_target_pairs={{0,17},{1,0},{2,19},{3,2},{4,21},{5,4},{6,23},{7,6},{8,25},{9,8},{... | collective-permute-start | bytes 221192 | tf_op jit(solution)/shard_map/ppermute | solution.py:76
  19.9 0.0 collective-permute-start.9
  19.9 0.5 %collective-permute-start.12 = (f32[16,128]{1,0:T(8,128)S(1)}, f32[16,128]{1,0:T(8,128)S(1)}, u32[]{:S(2)}, u32[]{:S(2)}) collective-permute-start(f32[16,128]{1,0:T(8,128)S(1)} %get-tuple-element.25), channel_id=1, source_target_pairs={{0,1},{1,0},{2,3},{3,2},{4,5},{5,4},{6,7},{7,6},{8,9},{9,8},{10,11... | collective-permute-start | bytes 24584 | tf_op jit(solution)/shard_map/ppermute | solution.py:76
  20.4 0.0 collective-permute-done.13.mate_x
  20.4 1.1 %shard_map.88.each = f32[16,128,128]{2,1,0:T(8,128)S(1)} custom-call(f32[1024,128]{1,0:T(8,128)S(1)} %get-tuple-element.26.x, f32[1024,128]{1,0:T(8,128)S(1)} %collective-permute-done.13.mate_x, f32[128,128]{1,0:T(8,128)S(1)} %get-tuple-element.22.moved, f32[128,128]{1,0:T(8,128)S(1)} %collective-permute-done.11.mate_moved), custom_call_target="tpu_custom_call" | custom-call | flops 402653184 | bytes 65536 | tf_op jit(solution)/shard_map/pallas_call | solution.py:37
  21.5 0.4 collective-permute-done.8
  21.9 0.0 collective-permute-done.9
  21.9 0.3 shard_map.89
  22.2 2.8 %collective-permute-start.14 = (f32[144,128]{1,0:T(8,128)S(1)}, f32[144,128]{1,0:T(8,128)S(1)}, u32[]{:S(2)}, u32[]{:S(2)}) collective-permute-start(f32[144,128]{1,0:T(8,128)S(1)} %shard_map.89), channel_id=1, source_target_pairs={{0,1},{1,2},{2,3},{3,0},{4,5},{5,6},{6,7},{7,4},{8,9},{9,10},{10,1... | collective-permute-start | bytes 221192 | tf_op jit(solution)/shard_map/ppermute | solution.py:76
  25.0 0.1 collective-permute-start.15
  25.1 3.0 %collective-permute-done.14 = f32[144,128]{1,0:T(8,128)S(1)} collective-permute-done((f32[144,128]{1,0:T(8,128)S(1)}, f32[144,128]{1,0:T(8,128)S(1)}, u32[]{:S(2)}, u32[]{:S(2)}) %collective-permute-start.14) | collective-permute-done | bytes 73760 | tf_op jit(solution)/shard_map/ppermute | solution.py:76
  28.1 0.1 collective-permute-start.16
  28.2 0.5 %collective-permute-start.17 = (f32[128,128]{1,0:T(8,128)S(1)}, f32[128,128]{1,0:T(8,128)S(1)}, u32[]{:S(2)}, u32[]{:S(2)}) collective-permute-start(f32[128,128]{1,0:T(8,128)S(1)} %slice_add_fusion), channel_id=1, source_target_pairs={{0,1},{1,0},{2,3},{3,2},{4,5},{5,4},{6,7},{7,6},{8,9},{9,8},{10,11... | collective-permute-start | bytes 196616 | tf_op jit(solution)/shard_map/ppermute | solution.py:76
  28.7 1.4 %collective-permute-done.16 = f32[128,128]{1,0:T(8,128)S(1)} collective-permute-done((f32[128,128]{1,0:T(8,128)S(1)}, f32[128,128]{1,0:T(8,128)S(1)}, u32[]{:S(2)}, u32[]{:S(2)}) %collective-permute-start.16) | collective-permute-done | bytes 65568 | tf_op jit(solution)/shard_map/ppermute | solution.py:76
  30.1 0.2 collective-permute-start.18
  30.3 0.1 collective-permute-start.19
  30.4 3.5 %collective-permute-done.18 = f32[128,128]{1,0:T(8,128)S(1)} collective-permute-done((f32[128,128]{1,0:T(8,128)S(1)}, f32[128,128]{1,0:T(8,128)S(1)}, u32[]{:S(2)}, u32[]{:S(2)}) %collective-permute-start.18) | collective-permute-done | bytes 65568 | tf_op jit(solution)/shard_map/ppermute | solution.py:76
  33.9 0.1 collective-permute-start.20
  33.9 0.5 %collective-permute-start.21 = (f32[128,128]{1,0:T(8,128)S(1)}, f32[128,128]{1,0:T(8,128)S(1)}, u32[]{:S(2)}, u32[]{:S(2)}) collective-permute-start(f32[128,128]{1,0:T(8,128)S(1)} %add.34), channel_id=1, source_target_pairs={{0,1},{1,0},{2,3},{3,2},{4,5},{5,4},{6,7},{7,6},{8,9},{9,8},{10,11... | collective-permute-start | bytes 196616 | tf_op jit(solution)/shard_map/ppermute | solution.py:76
  34.4 0.1 collective-permute-start.10
  34.5 1.3 %collective-permute-done.20 = f32[128,128]{1,0:T(8,128)S(1)} collective-permute-done((f32[128,128]{1,0:T(8,128)S(1)}, f32[128,128]{1,0:T(8,128)S(1)}, u32[]{:S(2)}, u32[]{:S(2)}) %collective-permute-start.20) | collective-permute-done | bytes 65568 | tf_op jit(solution)/shard_map/ppermute | solution.py:76
  35.9 0.7 %collective-permute-start.22 = (f32[128,128]{1,0:T(8,128)S(1)}, f32[128,128]{1,0:T(8,128)S(1)}, u32[]{:S(2)}, u32[]{:S(2)}) collective-permute-start(f32[128,128]{1,0:T(8,128)S(1)} %add.35.terms), channel_id=1, source_target_pairs={{0,1},{1,0},{2,3},{3,2},{4,5},{5,4},{6,7},{7,6},{8,9},{9,8},{10,11... | collective-permute-start | bytes 196616 | tf_op jit(solution)/shard_map/ppermute | solution.py:76
  36.5 0.1 collective-permute-start.23
  36.7 0.7 %shard_map.87 = (f32[128,128]{1,0:T(8,128)}, f32[1,128]{1,0:T(1,128)S(1)}, f32[128,128]{1,0:T(8,128)S(1)}) custom-call(f32[144,128]{1,0:T(8,128)S(1)} %add.31.sums, f32[144,128]{1,0:T(8,128)S(1)} %collective-permute-done.10.mate_sums, f32[128,128]{1,0:T(8,128)S(1)} %get-tuple-element.22.moved, f32[128,128]{1,0:T(8,128)S(1)} %collective-permute-done.11.mate_moved, ...), custom_call_target="tpu_custom_call" | custom-call | flops 131072 | bytes 65536 | tf_op jit(solution)/shard_map/pallas_call | solution.py:37
  37.3 0.5 %collective-permute-done.23.mate_rows = f32[32,128]{1,0:T(8,128)S(1)} collective-permute-done((f32[32,128]{1,0:T(8,128)S(1)}, f32[32,128]{1,0:T(8,128)S(1)}, u32[]{:S(2)}, u32[]{:S(2)}) %collective-permute-start.23) | collective-permute-done | bytes 16416 | tf_op jit(solution)/shard_map/ppermute | solution.py:76
  37.8 1.2 %shard_map.90 = (f32[8,128]{1,0:T(8,128)}, f32[128,128]{1,0:T(8,128)}, f32[1,128]{1,0:T(1,128)}) custom-call(f32[128,128]{1,0:T(8,128)S(1)} %add.35.terms, f32[128,128]{1,0:T(8,128)S(1)} %collective-permute-done.22.mate_terms, f32[32,128]{1,0:T(8,128)S(1)} %pad_maximum_fusion.2.rows, f32[32,128]{1,0:T(8,128)S(1)} %collective-permute-done.23.mate_rows, ...), custom_call_target="tpu_custom_call" | custom-call | flops 25165824 | bytes 65536 | tf_op jit(solution)/shard_map/pallas_call | solution.py:37
  (37 shorter events, 0.2 us)
Async XLA Ops:
  3.8 1.4 %collective-permute-start = (f32[136,128]{1,0:T(8,128)S(1)}, f32[136,128]{1,0:T(8,128)S(1)}, u32[]{:S(2)}, u32[]{:S(2)}) collective-permute-start(f32[136,128]{1,0:T(8,128)S(1)} %get-tuple-element.18), channel_id=1, source_target_pairs={{0,1},{1,0},{2,3},{3,2},{4,5},{5,4},{6,7},{7,6},{8,9},{9,8},{10,11... | collective-permute-start | bytes 208904 | tf_op jit(solution)/shard_map/ppermute | solution.py:76
  4.3 5.7 %collective-permute-start.3 = (f32[8,128,128]{2,1,0:T(8,128)S(1)}, f32[8,128,128]{2,1,0:T(8,128)S(1)}, u32[]{:S(2)}, u32[]{:S(2)}) collective-permute-start(f32[8,128,128]{2,1,0:T(8,128)S(1)} %get-tuple-element.20.con), channel_id=1, source_target_pairs={{0,1},{1,0},{2,3},{3,2},{4,5},{5,4},{6,7},{7,6},{8,9},{9,8},{10,11... | collective-permute-start | bytes 1572872 | tf_op jit(solution)/shard_map/ppermute | solution.py:76
  5.2 3.1 %copy-start.1 = (f32[128,128]{1,0:T(8,128)S(1)}, f32[128,128]{1,0:T(8,128)}, u32[]{:S(2)}) copy-start(f32[128,128]{1,0:T(8,128)} %c.3) | copy-start | bytes 196612
  5.2 4.7 %collective-permute-start.1 = (f32[144,128]{1,0:T(8,128)S(1)}, f32[144,128]{1,0:T(8,128)S(1)}, u32[]{:S(2)}, u32[]{:S(2)}) collective-permute-start(f32[144,128]{1,0:T(8,128)S(1)} %pad_maximum_fusion), channel_id=1, source_target_pairs={{0,1},{1,2},{2,3},{3,0},{4,5},{5,6},{6,7},{7,4},{8,9},{9,10},{10,1... | collective-permute-start | bytes 221192 | tf_op jit(solution)/shard_map/ppermute | solution.py:76
  5.6 4.3 %collective-permute-start.2 = (f32[144,128]{1,0:T(8,128)S(1)}, f32[144,128]{1,0:T(8,128)S(1)}, u32[]{:S(2)}, u32[]{:S(2)}) collective-permute-start(f32[144,128]{1,0:T(8,128)S(1)} %pad_maximum_fusion), channel_id=1, source_target_pairs={{0,1},{1,0},{2,3},{3,2},{4,5},{5,4},{6,7},{7,6},{8,9},{9,8},{10,11... | collective-permute-start | bytes 221192 | tf_op jit(solution)/shard_map/ppermute | solution.py:76
  8.3 0.7 %copy-start.2 = (f32[128]{0:T(128)S(1)}, f32[128]{0:T(128)}, u32[]{:S(2)}) copy-start(f32[128]{0:T(128)} %param.9) | copy-start | bytes 1540
  8.3 12.2 %collective-permute-start.13 = (f32[1024,128]{1,0:T(8,128)S(1)}, f32[1024,128]{1,0:T(8,128)S(1)}, u32[]{:S(2)}, u32[]{:S(2)}) collective-permute-start(f32[1024,128]{1,0:T(8,128)S(1)} %get-tuple-element.26.x), channel_id=1, source_target_pairs={{0,1},{1,0},{2,3},{3,2},{4,5},{5,4},{6,7},{7,6},{8,9},{9,8},{10,11... | collective-permute-start | bytes 1572872 | tf_op jit(solution)/shard_map/ppermute | solution.py:76
  10.0 0.8 %copy-start = (f32[128,128]{1,0:T(8,128)S(1)}, f32[128,128]{1,0:T(8,128)}, u32[]{:S(2)}) copy-start(f32[128,128]{1,0:T(8,128)} %a.1) | copy-start | bytes 196612
  11.6 2.9 %collective-permute-start.4 = (f32[144,128]{1,0:T(8,128)S(1)}, f32[144,128]{1,0:T(8,128)S(1)}, u32[]{:S(2)}, u32[]{:S(2)}) collective-permute-start(f32[144,128]{1,0:T(8,128)S(1)} %get-tuple-element.21), channel_id=1, source_target_pairs={{0,5},{1,0},{2,7},{3,2},{4,1},{5,4},{6,3},{7,6},{8,13},{9,8},{10,1... | collective-permute-start | bytes 221192 | tf_op jit(solution)/shard_map/ppermute | solution.py:76
  12.5 2.0 %collective-permute-start.5 = (f32[144,128]{1,0:T(8,128)S(1)}, f32[144,128]{1,0:T(8,128)S(1)}, u32[]{:S(2)}, u32[]{:S(2)}) collective-permute-start(f32[144,128]{1,0:T(8,128)S(1)} %get-tuple-element.21), channel_id=1, source_target_pairs={{0,1},{1,0},{2,3},{3,2},{4,5},{5,4},{6,7},{7,6},{8,9},{9,8},{10,11... | collective-permute-start | bytes 221192 | tf_op jit(solution)/shard_map/ppermute | solution.py:76
  14.5 4.6 %collective-permute-start.6 = (f32[144,128]{1,0:T(8,128)S(1)}, f32[144,128]{1,0:T(8,128)S(1)}, u32[]{:S(2)}, u32[]{:S(2)}) collective-permute-start(f32[144,128]{1,0:T(8,128)S(1)} %add.29), channel_id=1, source_target_pairs={{0,1},{1,8},{2,3},{3,10},{4,5},{5,12},{6,7},{7,14},{8,9},{9,0},{10... | collective-permute-start | bytes 221192 | tf_op jit(solution)/shard_map/ppermute | solution.py:76
  15.9 3.2 %collective-permute-start.7 = (f32[144,128]{1,0:T(8,128)S(1)}, f32[144,128]{1,0:T(8,128)S(1)}, u32[]{:S(2)}, u32[]{:S(2)}) collective-permute-start(f32[144,128]{1,0:T(8,128)S(1)} %add.29), channel_id=1, source_target_pairs={{0,1},{1,0},{2,3},{3,2},{4,5},{5,4},{6,7},{7,6},{8,9},{9,8},{10,11... | collective-permute-start | bytes 221192 | tf_op jit(solution)/shard_map/ppermute | solution.py:76
  16.3 4.2 %collective-permute-start.11 = (f32[128,128]{1,0:T(8,128)S(1)}, f32[128,128]{1,0:T(8,128)S(1)}, u32[]{:S(2)}, u32[]{:S(2)}) collective-permute-start(f32[128,128]{1,0:T(8,128)S(1)} %get-tuple-element.22.moved), channel_id=1, source_target_pairs={{0,1},{1,0},{2,3},{3,2},{4,5},{5,4},{6,7},{7,6},{8,9},{9,8},{10,11... | collective-permute-start | bytes 196616 | tf_op jit(solution)/shard_map/ppermute | solution.py:76
  19.1 2.8 %collective-permute-start.8 = (f32[144,128]{1,0:T(8,128)S(1)}, f32[144,128]{1,0:T(8,128)S(1)}, u32[]{:S(2)}, u32[]{:S(2)}) collective-permute-start(f32[144,128]{1,0:T(8,128)S(1)} %add.30), channel_id=1, source_target_pairs={{0,17},{1,0},{2,19},{3,2},{4,21},{5,4},{6,23},{7,6},{8,25},{9,8},{... | collective-permute-start | bytes 221192 | tf_op jit(solution)/shard_map/ppermute | solution.py:76
  19.9 2.0 %collective-permute-start.9 = (f32[144,128]{1,0:T(8,128)S(1)}, f32[144,128]{1,0:T(8,128)S(1)}, u32[]{:S(2)}, u32[]{:S(2)}) collective-permute-start(f32[144,128]{1,0:T(8,128)S(1)} %add.30), channel_id=1, source_target_pairs={{0,1},{1,0},{2,3},{3,2},{4,5},{5,4},{6,7},{7,6},{8,9},{9,8},{10,11... | collective-permute-start | bytes 221192 | tf_op jit(solution)/shard_map/ppermute | solution.py:76
  19.9 2.0 %collective-permute-start.12 = (f32[16,128]{1,0:T(8,128)S(1)}, f32[16,128]{1,0:T(8,128)S(1)}, u32[]{:S(2)}, u32[]{:S(2)}) collective-permute-start(f32[16,128]{1,0:T(8,128)S(1)} %get-tuple-element.25), channel_id=1, source_target_pairs={{0,1},{1,0},{2,3},{3,2},{4,5},{5,4},{6,7},{7,6},{8,9},{9,8},{10,11... | collective-permute-start | bytes 24584 | tf_op jit(solution)/shard_map/ppermute | solution.py:76
  22.2 5.9 %collective-permute-start.14 = (f32[144,128]{1,0:T(8,128)S(1)}, f32[144,128]{1,0:T(8,128)S(1)}, u32[]{:S(2)}, u32[]{:S(2)}) collective-permute-start(f32[144,128]{1,0:T(8,128)S(1)} %shard_map.89), channel_id=1, source_target_pairs={{0,1},{1,2},{2,3},{3,0},{4,5},{5,6},{6,7},{7,4},{8,9},{9,10},{10,1... | collective-permute-start | bytes 221192 | tf_op jit(solution)/shard_map/ppermute | solution.py:76
  25.0 3.1 %collective-permute-start.15 = (f32[144,128]{1,0:T(8,128)S(1)}, f32[144,128]{1,0:T(8,128)S(1)}, u32[]{:S(2)}, u32[]{:S(2)}) collective-permute-start(f32[144,128]{1,0:T(8,128)S(1)} %shard_map.89), channel_id=1, source_target_pairs={{0,1},{1,0},{2,3},{3,2},{4,5},{5,4},{6,7},{7,6},{8,9},{9,8},{10,11... | collective-permute-start | bytes 221192 | tf_op jit(solution)/shard_map/ppermute | solution.py:76
  28.1 6.4 %copy-start.3 = (f32[144,128]{1,0:T(8,128)}, f32[144,128]{1,0:T(8,128)S(1)}, u32[]{:S(2)}) copy-start(f32[144,128]{1,0:T(8,128)S(1)} %collective-permute-done.14) | copy-start | bytes 221188
  28.1 6.4 %copy-start.4 = (f32[144,128]{1,0:T(8,128)}, f32[144,128]{1,0:T(8,128)S(1)}, u32[]{:S(2)}) copy-start(f32[144,128]{1,0:T(8,128)S(1)} %collective-permute-done.15) | copy-start | bytes 221188
  28.1 2.0 %collective-permute-start.16 = (f32[128,128]{1,0:T(8,128)S(1)}, f32[128,128]{1,0:T(8,128)S(1)}, u32[]{:S(2)}, u32[]{:S(2)}) collective-permute-start(f32[128,128]{1,0:T(8,128)S(1)} %slice_add_fusion), channel_id=1, source_target_pairs={{0,5},{1,0},{2,7},{3,2},{4,1},{5,4},{6,3},{7,6},{8,13},{9,8},{10,1... | collective-permute-start | bytes 196616 | tf_op jit(solution)/shard_map/ppermute | solution.py:76
  28.2 1.9 %collective-permute-start.17 = (f32[128,128]{1,0:T(8,128)S(1)}, f32[128,128]{1,0:T(8,128)S(1)}, u32[]{:S(2)}, u32[]{:S(2)}) collective-permute-start(f32[128,128]{1,0:T(8,128)S(1)} %slice_add_fusion), channel_id=1, source_target_pairs={{0,1},{1,0},{2,3},{3,2},{4,5},{5,4},{6,7},{7,6},{8,9},{9,8},{10,11... | collective-permute-start | bytes 196616 | tf_op jit(solution)/shard_map/ppermute | solution.py:76
  30.1 3.7 %collective-permute-start.18 = (f32[128,128]{1,0:T(8,128)S(1)}, f32[128,128]{1,0:T(8,128)S(1)}, u32[]{:S(2)}, u32[]{:S(2)}) collective-permute-start(f32[128,128]{1,0:T(8,128)S(1)} %add.33), channel_id=1, source_target_pairs={{0,1},{1,8},{2,3},{3,10},{4,5},{5,12},{6,7},{7,14},{8,9},{9,0},{10... | collective-permute-start | bytes 196616 | tf_op jit(solution)/shard_map/ppermute | solution.py:76
  30.3 3.6 %collective-permute-start.19 = (f32[128,128]{1,0:T(8,128)S(1)}, f32[128,128]{1,0:T(8,128)S(1)}, u32[]{:S(2)}, u32[]{:S(2)}) collective-permute-start(f32[128,128]{1,0:T(8,128)S(1)} %add.33), channel_id=1, source_target_pairs={{0,1},{1,0},{2,3},{3,2},{4,5},{5,4},{6,7},{7,6},{8,9},{9,8},{10,11... | collective-permute-start | bytes 196616 | tf_op jit(solution)/shard_map/ppermute | solution.py:76
  33.9 2.0 %collective-permute-start.20 = (f32[128,128]{1,0:T(8,128)S(1)}, f32[128,128]{1,0:T(8,128)S(1)}, u32[]{:S(2)}, u32[]{:S(2)}) collective-permute-start(f32[128,128]{1,0:T(8,128)S(1)} %add.34), channel_id=1, source_target_pairs={{0,17},{1,0},{2,19},{3,2},{4,21},{5,4},{6,23},{7,6},{8,25},{9,8},{... | collective-permute-start | bytes 196616 | tf_op jit(solution)/shard_map/ppermute | solution.py:76
  33.9 1.9 %collective-permute-start.21 = (f32[128,128]{1,0:T(8,128)S(1)}, f32[128,128]{1,0:T(8,128)S(1)}, u32[]{:S(2)}, u32[]{:S(2)}) collective-permute-start(f32[128,128]{1,0:T(8,128)S(1)} %add.34), channel_id=1, source_target_pairs={{0,1},{1,0},{2,3},{3,2},{4,5},{5,4},{6,7},{7,6},{8,9},{9,8},{10,11... | collective-permute-start | bytes 196616 | tf_op jit(solution)/shard_map/ppermute | solution.py:76
  34.4 2.2 %collective-permute-start.10 = (f32[144,128]{1,0:T(8,128)S(1)}, f32[144,128]{1,0:T(8,128)S(1)}, u32[]{:S(2)}, u32[]{:S(2)}) collective-permute-start(f32[144,128]{1,0:T(8,128)S(1)} %add.31.sums), channel_id=1, source_target_pairs={{0,1},{1,0},{2,3},{3,2},{4,5},{5,4},{6,7},{7,6},{8,9},{9,8},{10,11... | collective-permute-start | bytes 221192 | tf_op jit(solution)/shard_map/ppermute | solution.py:76
  34.5 2.0 %slice-start = ((f32[144,128]{1,0:T(8,128)}), f32[16,128]{1,0:T(8,128)S(1)}, s32[]{:S(2)}) async-start(f32[144,128]{1,0:T(8,128)} %copy-done.3), calls=%async_computation | async-start | bytes 16384 | tf_op jit(solution)/shard_map/slice | solution.py:260
  34.5 2.0 %slice-start.1 = ((f32[144,128]{1,0:T(8,128)}), f32[16,128]{1,0:T(8,128)S(1)}, s32[]{:S(2)}) async-start(f32[144,128]{1,0:T(8,128)} %copy-done.4), calls=%async_computation.1 | async-start | bytes 16384 | tf_op jit(solution)/shard_map/slice | solution.py:260
  35.9 1.9 %collective-permute-start.22 = (f32[128,128]{1,0:T(8,128)S(1)}, f32[128,128]{1,0:T(8,128)S(1)}, u32[]{:S(2)}, u32[]{:S(2)}) collective-permute-start(f32[128,128]{1,0:T(8,128)S(1)} %add.35.terms), channel_id=1, source_target_pairs={{0,1},{1,0},{2,3},{3,2},{4,5},{5,4},{6,7},{7,6},{8,9},{9,8},{10,11... | collective-permute-start | bytes 196616 | tf_op jit(solution)/shard_map/ppermute | solution.py:76
  36.5 1.2 %collective-permute-start.23 = (f32[32,128]{1,0:T(8,128)S(1)}, f32[32,128]{1,0:T(8,128)S(1)}, u32[]{:S(2)}, u32[]{:S(2)}) collective-permute-start(f32[32,128]{1,0:T(8,128)S(1)} %pad_maximum_fusion.2.rows), channel_id=1, source_target_pairs={{0,1},{1,0},{2,3},{3,2},{4,5},{5,4},{6,7},{7,6},{8,9},{9,8},{10,11... | collective-permute-start | bytes 49160 | tf_op jit(solution)/shard_map/ppermute | solution.py:76

commit v6 on v4

--- a/solution.py
+++ b/solution.py
@@ -70,15 +70,13 @@
     return masks
 
 
-def send(values, holder, mask=0):
-    count = lax.axis_size(ALL)
-    pairs = [(i, i ^ 1 ^ mask) for i in range(count) if i & 1 == holder]
+def swap(values):
+    return lax.ppermute(values, ALL, [(i, i ^ 1) for i in range(lax.axis_size(ALL))])
+
+
+def cross(values, mask):
+    pairs = [(i, i ^ 1 ^ mask if i & 1 else i ^ 1) for i in range(lax.axis_size(ALL))]
     return lax.ppermute(values, ALL, pairs)
-
-
-def fan(values, holder, masks):
-    sent = [send(values, holder, mask) for mask in reversed(masks)]
-    return sent[::-1]
 
 
 def tree(parts):
@@ -91,8 +89,8 @@
     return lax.axis_index("smp")
 
 
-def on_core(core, own, got):
-    return jnp.where(smp_index() & 1 == core, own, got)
+def from_core_0(own, got):
+    return jnp.where(smp_index() & 1 == 0, own, got)
 
 
 def in_order(rows, scratch, chips):
@@ -115,14 +113,15 @@
     chunks = 4 if vox_rows % 32 == 0 else 1
     chunk_vox = vox_rows // chunks
     chunk_rows = chunk_vox * smp_rows
-    w_row = weights.reshape(1, rank)
-
-    def open_kernel(x_hbm, c_hbm, b_hbm, x, out, con, c, sems):
+
+    def open_kernel(x_hbm, c_hbm, b_hbm, a_hbm, w_hbm, x, c, a, w, out, con, sems):
         copies = [pltpu.make_async_copy(c_hbm, c, sems.at[0])]
         copies += [pltpu.make_async_copy(b_hbm, out.at[pl.ds(vox_rows, smp_rows), :], sems.at[1])]
         for n in range(chunks):
             part = pl.ds(n * chunk_rows, chunk_rows)
             copies.append(pltpu.make_async_copy(x_hbm.at[part, :], x.at[part, :], sems.at[2 + n]))
+        copies.append(pltpu.make_async_copy(a_hbm, a, sems.at[2 + chunks]))
+        copies.append(pltpu.make_async_copy(w_hbm, w, sems.at[3 + chunks]))
         for copy in copies:
             copy.start()
         copies[0].wait()
@@ -140,14 +139,23 @@
                 made = made * b[j : j + 1, :]
                 total = made if total is None else total + made
             out[rows, :] = total
-
-    x, opened, con = call(
+        copies[2 + chunks].wait()
+        copies[3 + chunks].wait()
+
+    x, c_near, a_near, w_row, opened, con = call(
         open_kernel,
-        (near(flat_rows, times), near(vox_rows + smp_rows, rank), near(smp_rows, vox_rows, rank)),
-        (ensemble.reshape(flat_rows, times), time_factor, sample_factor),
+        (
+            near(flat_rows, times),
+            near(times, rank),
+            near(vox_rows, rank),
+            near(1, rank),
+            near(vox_rows + smp_rows, rank),
+            near(smp_rows, vox_rows, rank),
+        ),
+        (ensemble.reshape(flat_rows, times), time_factor, sample_factor, voxel_factor, weights.reshape(1, rank)),
         2 * flat_rows * times * rank * 6,
-        scratch=(near(times, rank), pltpu.SemaphoreType.DMA((2 + chunks,))),
-        in_hbm=3,
+        scratch=(pltpu.SemaphoreType.DMA((4 + chunks,)),),
+        in_hbm=5,
     )
 
     def weigh_kernel(c, w, outer, outer_c):
@@ -156,20 +164,22 @@
         outer_c[...] = squared * dot_rows(c[...], c[...])
 
     outer, outer_c = call(
-        weigh_kernel, (near(rank, rank), near(rank, rank)), (time_factor, w_row), 2 * rank * rank * times * 6
-    )
-
-    got = send(opened, 0)
+        weigh_kernel, (near(rank, rank), near(rank, rank)), (c_near, w_row), 2 * rank * rank * times * 6
+    )
+
+    got = swap(opened)
     terms = opened[:vox_rows] + got[:vox_rows]
     rows_b = jnp.concatenate([got[vox_rows:], opened[vox_rows:]], axis=0)
-    holder = 1
+    handed = jnp.concatenate([terms, rows_b], axis=0)
+    rows_b = jnp.concatenate([opened[vox_rows:], got[vox_rows:]], axis=0)
     for group in groups_of(chip_bits):
-        parts = fan(jnp.concatenate([terms, rows_b], axis=0), holder, masks_of(group))
-        terms = tree([part[:vox_rows] for part in parts])
-        rows_b = jnp.concatenate([part[vox_rows:] for part in parts], axis=0)
-        holder ^= 1
-    voxel_core = holder
-    mate_con = send(con, 1 - voxel_core)
+        if handed is None:
+            handed = swap(jnp.concatenate([terms, rows_b], axis=0))
+        parts = [cross(handed, mask) for mask in masks_of(group)[1:]]
+        terms = tree([terms] + [part[:vox_rows] for part in parts])
+        rows_b = jnp.concatenate([rows_b] + [part[vox_rows:] for part in parts], axis=0)
+        handed = None
+    mate_con = swap(con)
 
     def voxel_kernel(terms, rows, a, w, outer_c, con, mate_con, moved_out, chip_b, out, all_b):
         b = in_order(rows, all_b, chips)
@@ -180,39 +190,30 @@
         out[:rank, :] = dot_rows(moved, moved)
         for core in range(2):
             for j in range(smp_rows):
-                block = con[j] if core == voxel_core else mate_con[j]
                 row = rank + core * smp_rows + j
-                out[row : row + 1, :] = jnp.sum(block * moved, axis=0, keepdims=True)
+                out[row : row + 1, :] = jnp.sum((con, mate_con)[core][j] * moved, axis=0, keepdims=True)
 
     moved_a, chip_b, sums = call(
         voxel_kernel,
         (near(vox_rows, rank), near(chip_rows, rank), near(rank + chip_rows, rank)),
-        (terms, rows_b, voxel_factor, w_row, outer_c, con, mate_con),
+        (terms, rows_b, a_near, w_row, outer_c, con, mate_con),
         2 * rank * rank * vox_rows * 12,
         scratch=(near(smp_total, rank),),
     )
-    mate_moved_a = send(moved_a, voxel_core)
 
     for group in groups_of(vox_bits):
-        sums = tree(fan(sums, holder, masks_of(group)))
-        holder ^= 1
-    sample_core = holder
-    if sample_core != voxel_core:
-        chip_b = send(chip_b, voxel_core)
-    mate_x = send(x, 1 - sample_core)
-
-    def time_kernel(x, mate_x, moved, mate_moved, each):
-        moved = on_core(voxel_core, moved[...], mate_moved[...])
+        handed = swap(sums)
+        sums = tree([sums] + [cross(handed, mask) for mask in masks_of(group)[1:]])
+    mate_x = swap(x)
+
+    def time_kernel(x, mate_x, moved, each):
         for core in range(2):
             for j in range(smp_rows):
-                source = x if core == sample_core else mate_x
-                each[core * smp_rows + j] = dot_rows(source[pl.ds(j, vox_rows, stride=smp_rows), :], moved)
+                block = (x, mate_x)[core][pl.ds(j, vox_rows, stride=smp_rows), :]
+                each[core * smp_rows + j] = dot_rows(block, moved[...])
 
     (each,) = call(
-        time_kernel,
-        (near(chip_rows, times, rank),),
-        (x, mate_x, moved_a, mate_moved_a),
-        4 * flat_rows * times * rank * 6,
+        time_kernel, (near(chip_rows, times, rank),), (x, mate_x, moved_a), 4 * flat_rows * times * rank * 6
     )
 
     def sample_kernel(sums, b, w, outer_c, each, out):
@@ -231,13 +232,14 @@
         (sums, chip_b, w_row, outer_c, each),
         2 * rank * rank * chip_rows * 6,
     )
-    mate_sums = send(sums, sample_core)
+    mate_sums = swap(sums)
+    mate_moved_a = swap(moved_a)
 
     def scale_kernel(sums, mate_sums, moved, mate_moved, outer, result, scales_out, weighed):
-        gram = on_core(sample_core, sums[:rank, :], mate_sums[:rank, :])
+        gram = from_core_0(sums[:rank, :], mate_sums[:rank, :])
         scales = jnp.sqrt(diagonal_row(gram) / vox_total + 1e-06)
         scales_out[...] = scales
-        result[...] = on_core(voxel_core, moved[...], mate_moved[...]) / scales
+        result[...] = from_core_0(moved[...], mate_moved[...]) / scales
         weighed[...] = outer[...] * gram
 
     voxel_result, scales_a, weighed = call(
@@ -247,28 +249,26 @@
         vox_rows * rank * 8,
     )
 
-    terms, rows_b, rows_core = payload[:times], payload[times:], holder
+    terms, rows_b = payload[:times], payload[times:]
     smp_mask = sum(chip_bits)
     for group in groups_of(chip_bits + vox_bits):
-        masks = masks_of(group)
+        masks = masks_of(group)[1:]
         with_rows = any(mask & smp_mask for mask in masks)
-        parts = fan(jnp.concatenate([terms, rows_b], axis=0) if with_rows else terms, holder, masks)
-        terms = tree([part[:times] for part in parts])
-        holder ^= 1
+        handed = swap(jnp.concatenate([terms, rows_b], axis=0) if with_rows else terms)
+        parts = [cross(handed, mask) for mask in masks]
+        terms = tree([terms] + [part[:times] for part in parts])
         if with_rows:
             parts = [part for part, mask in zip(parts, masks) if not mask & ~smp_mask]
-            rows_b = jnp.concatenate([part[times:] for part in parts], axis=0)
-            rows_core = holder
-    last_core = holder
-    mate_rows_b = send(rows_b, rows_core)
-    mate_terms = send(terms, last_core)
+            rows_b = jnp.concatenate([rows_b] + [part[times:] for part in parts], axis=0)
+    mate_rows_b = swap(rows_b)
+    mate_terms = swap(terms)
 
     def last_kernel(terms, mate_terms, rows, mate_rows, c, w, weighed, scales_a, b_out, c_out, w_out, all_b):
-        b = in_order(on_core(rows_core, rows[...], mate_rows[...]), all_b, chips)
+        b = in_order(from_core_0(rows[...], mate_rows[...]), all_b, chips)
         coupled = weighed[...] * dot_rows(b, b)
         scales_b = jnp.sqrt(jnp.sum(b * b, axis=0, keepdims=True) / smp_total + 1e-06)
         b_out[...] = all_b[pl.ds(pl.multiple_of(smp_index() * smp_rows, smp_rows), smp_rows), :] / scales_b
-        summed = on_core(last_core, terms[...], mate_terms[...])
+        summed = from_core_0(terms[...], mate_terms[...])
         moved = c[...] - step_of(coupled) * (dot(c[...], coupled) - summed * w[...])
         scales_c = jnp.sqrt(jnp.sum(moved * moved, axis=0, keepdims=True) / times + 1e-06)
         c_out[...] = moved / scales_c
@@ -277,7 +277,7 @@
     sample_result, time_result, scale_result = call(
         last_kernel,
         (far(smp_rows, rank), far(times, rank), far(1, rank)),
-        (terms, mate_terms, rows_b, mate_rows_b, time_factor, w_row, weighed, scales_a),
+        (terms, mate_terms, rows_b, mate_rows_b, c_near, w_row, weighed, scales_a),
         2 * rank * rank * times * 6,
         scratch=(near(smp_total, rank),),
     )

time: 60.3 us -> 44.9 us (0.74)
  starting transfers between devices: 36.3 us -> 13.1 us
  waiting for transfers between devices: 13.7 us -> 23.2 us
  local copies, waits for them, and re-layouts: 0.86 us -> 0.01 us
    ppermute x23 -> x22, starting transfers between devices: 36.3 us -> 13.1 us  [the longest x11 7.44 us: cross(): return lax.ppermute(values, ALL, pairs)]
    ppermute x23 -> x22, waiting for transfers between devices: 13.7 us -> 23.2 us  [the longest x11 17.2 us: cross(): return lax.ppermute(values, ALL, pairs)]
    unnamed x10 -> x2, local copies, waits for them, and re-layouts: 0.84 us -> 0.01 us
  transfers between devices with their start and end apart: 23 -> 22, of which waited for: 8 -> 15; matrix products, arithmetic and copies ran while one was open for 0% -> 0% of each run, Pallas kernels for 5% -> 7%
where the time goes in v6:
time: 44.9 us; the launch traced here: 44.8 us
  waiting for transfers between devices  23.2 us (52%)
  starting transfers between devices  13.1 us (29%)
  Pallas kernels  7.55 us (17%)
  between operations  0.81 us (2%)
    ppermute x11, waiting for transfers between devices, cross(): return lax.ppermute(values, ALL, pairs)  17.2 us
    pallas_call x7, Pallas kernels, call(): pl.pallas_call(kernel, out_shape=outs, in_specs=specs, out_specs=[pl.Bloc...  7.55 us
    ppermute x11, starting transfers between devices, cross(): return lax.ppermute(values, ALL, pairs)  7.44 us
    ppermute x11, waiting for transfers between devices, swap(): lax.ppermute(values, ALL, [(i, i ^ 1) for i in range(lax.axis_size(ALL))])  5.98 us
    ppermute x11, starting transfers between devices, swap(): lax.ppermute(values, ALL, [(i, i ^ 1) for i in range(lax.axis_size(ALL))])  5.68 us
  transfers between devices with their start and end apart: 22, of which 15 were waited for; matrix products, arithmetic and copies ran while one was open for 0% of the time, Pallas kernels for 7%

profile of v6, /device:TPU:0, one launch (start us, length us, event | category | flops | bytes accessed | tf_op | source)
XLA Modules:
  0.0 44.8 jit_solution(4906324416913262181)
XLA Ops:
  0.6 3.1 %shard_map.84 = (f32[1024,128]{1,0:T(8,128)S(1)}, f32[128,128]{1,0:T(8,128)S(1)}, f32[128,128]{1,0:T(8,128)S(1)}, f32[1,128]{1,0:T(1,128)S(1)}, f32[136,128]{1,0:T(8,128)S(1)}, /*index=5*/f32[8,128,128]{2,1,0:T(8,128)S(1)}) custom-call(f32[1024,128]{1,0:T(8,128)} %bitcast.3, f32[128,128]{1,0:T(8,128)} %c_hbm.1, f32[8,128]{1,0:T(8,128)} %b_hbm.1, ...), custom_call_target="tpu_custom_call" | custom-call | flops 201326592 | bytes 65536 | tf_op jit(solution)/shard_map/pallas_call | solution.py:37
  3.8 0.5 %collective-permute-start = (f32[136,128]{1,0:T(8,128)S(1)}, f32[136,128]{1,0:T(8,128)S(1)}, u32[]{:S(2)}, u32[]{:S(2)}) collective-permute-start(f32[136,128]{1,0:T(8,128)S(1)} %get-tuple-element.21), channel_id=1, source_target_pairs={{0,1},{1,0},{2,3},{3,2},{4,5},{5,4},{6,7},{7,6},{8,9},{9,8},{10,11... | collective-permute-start | bytes 208904 | tf_op jit(solution)/shard_map/ppermute | solution.py:74
  4.3 0.1 collective-permute-start.2
  4.4 0.8 %collective-permute-done = f32[136,128]{1,0:T(8,128)S(1)} collective-permute-done((f32[136,128]{1,0:T(8,128)S(1)}, f32[136,128]{1,0:T(8,128)S(1)}, u32[]{:S(2)}, u32[]{:S(2)}) %collective-permute-start) | collective-permute-done | bytes 69664 | tf_op jit(solution)/shard_map/ppermute | solution.py:74
  5.2 0.4 collective-permute-start.1
  5.6 2.6 %collective-permute-start.11 = (f32[1024,128]{1,0:T(8,128)S(1)}, f32[1024,128]{1,0:T(8,128)S(1)}, u32[]{:S(2)}, u32[]{:S(2)}) collective-permute-start(f32[1024,128]{1,0:T(8,128)S(1)} %get-tuple-element.32.x), channel_id=1, source_target_pairs={{0,1},{1,0},{2,3},{3,2},{4,5},{5,4},{6,7},{7,6},{8,9},{9,8},{10,11... | collective-permute-start | bytes 1572872 | tf_op jit(solution)/shard_map/ppermute | solution.py:74
  8.3 0.3 shard_map.85
  8.6 1.3 %collective-permute-done.1 = f32[144,128]{1,0:T(8,128)S(1)} collective-permute-done((f32[144,128]{1,0:T(8,128)S(1)}, f32[144,128]{1,0:T(8,128)S(1)}, u32[]{:S(2)}, u32[]{:S(2)}) %collective-permute-start.1) | collective-permute-done | bytes 73760 | tf_op jit(solution)/shard_map/ppermute | solution.py:79
  10.0 0.0 collective-permute-done.2.mate_con
  10.0 0.8 %shard_map.86 = (f32[128,128]{1,0:T(8,128)S(1)}, f32[16,128]{1,0:T(8,128)S(1)}, f32[144,128]{1,0:T(8,128)S(1)}) custom-call(f32[128,128]{1,0:T(8,128)S(1)} %slice_add_fusion.2.terms, f32[32,128]{1,0:T(8,128)S(1)} %pad_maximum_fusion.1.rows, f32[128,128]{1,0:T(8,128)S(1)} %get-tuple-element.22.a, f32[1,128]{1,0:T(1,128)S(1)} %get-tuple-element.23.w, ...), custom_call_target="tpu_custom_call" | custom-call | flops 50331648 | bytes 65536 | tf_op jit(solution)/shard_map/pallas_call | solution.py:37
  10.8 0.1 collective-permute-start.3
  10.9 1.3 %collective-permute-done.3 = f32[144,128]{1,0:T(8,128)S(1)} collective-permute-done((f32[144,128]{1,0:T(8,128)S(1)}, f32[144,128]{1,0:T(8,128)S(1)}, u32[]{:S(2)}, u32[]{:S(2)}) %collective-permute-start.3) | collective-permute-done | bytes 73760 | tf_op jit(solution)/shard_map/ppermute | solution.py:74
  12.2 0.2 collective-permute-start.4
  12.3 1.9 %collective-permute-start.5 = (f32[144,128]{1,0:T(8,128)S(1)}, f32[144,128]{1,0:T(8,128)S(1)}, u32[]{:S(2)}, u32[]{:S(2)}) collective-permute-start(f32[144,128]{1,0:T(8,128)S(1)} %collective-permute-done.3), channel_id=1, source_target_pairs={{0,1},{1,8},{2,3},{3,10},{4,5},{5,12},{6,7},{7,14},{8,9},{9,0},{10... | collective-permute-start | bytes 221192 | tf_op jit(solution)/shard_map/ppermute | solution.py:79
  14.2 0.2 collective-permute-start.6
  14.5 1.5 %collective-permute-done.4 = f32[144,128]{1,0:T(8,128)S(1)} collective-permute-done((f32[144,128]{1,0:T(8,128)S(1)}, f32[144,128]{1,0:T(8,128)S(1)}, u32[]{:S(2)}, u32[]{:S(2)}) %collective-permute-start.4) | collective-permute-done | bytes 73760 | tf_op jit(solution)/shard_map/ppermute | solution.py:79
  16.0 1.5 %collective-permute-done.5 = f32[144,128]{1,0:T(8,128)S(1)} collective-permute-done((f32[144,128]{1,0:T(8,128)S(1)}, f32[144,128]{1,0:T(8,128)S(1)}, u32[]{:S(2)}, u32[]{:S(2)}) %collective-permute-start.5) | collective-permute-done | bytes 73760 | tf_op jit(solution)/shard_map/ppermute | solution.py:79
  17.5 1.5 %collective-permute-done.6 = f32[144,128]{1,0:T(8,128)S(1)} collective-permute-done((f32[144,128]{1,0:T(8,128)S(1)}, f32[144,128]{1,0:T(8,128)S(1)}, u32[]{:S(2)}, u32[]{:S(2)}) %collective-permute-start.6) | collective-permute-done | bytes 73760 | tf_op jit(solution)/shard_map/ppermute | solution.py:79
  18.9 0.1 collective-permute-start.7
  19.0 1.3 %collective-permute-done.7 = f32[144,128]{1,0:T(8,128)S(1)} collective-permute-done((f32[144,128]{1,0:T(8,128)S(1)}, f32[144,128]{1,0:T(8,128)S(1)}, u32[]{:S(2)}, u32[]{:S(2)}) %collective-permute-start.7) | collective-permute-done | bytes 73760 | tf_op jit(solution)/shard_map/ppermute | solution.py:74
  20.3 0.2 collective-permute-start.8
  20.4 0.0 collective-permute-done.11.mate_x
  20.4 1.1 %shard_map.88.each = f32[16,128,128]{2,1,0:T(8,128)S(1)} custom-call(f32[1024,128]{1,0:T(8,128)S(1)} %get-tuple-element.32.x, f32[1024,128]{1,0:T(8,128)S(1)} %collective-permute-done.11.mate_x, f32[128,128]{1,0:T(8,128)S(1)} %get-tuple-element.28.moved), custom_call_target="tpu_custom_call" | custom-call | flops 402653184 | bytes 65536 | tf_op jit(solution)/shard_map/pallas_call | solution.py:37
  21.5 3.4 %collective-permute-done.8 = f32[144,128]{1,0:T(8,128)S(1)} collective-permute-done((f32[144,128]{1,0:T(8,128)S(1)}, f32[144,128]{1,0:T(8,128)S(1)}, u32[]{:S(2)}, u32[]{:S(2)}) %collective-permute-start.8) | collective-permute-done | bytes 73760 | tf_op jit(solution)/shard_map/ppermute | solution.py:79
  25.0 0.3 shard_map.89
  25.2 0.1 collective-permute-start.12
  25.3 1.3 %collective-permute-done.12 = f32[144,128]{1,0:T(8,128)S(1)} collective-permute-done((f32[144,128]{1,0:T(8,128)S(1)}, f32[144,128]{1,0:T(8,128)S(1)}, u32[]{:S(2)}, u32[]{:S(2)}) %collective-permute-start.12) | collective-permute-done | bytes 73760 | tf_op jit(solution)/shard_map/ppermute | solution.py:74
  26.6 0.2 collective-permute-start.13
  26.7 1.5 %collective-permute-start.14 = (f32[144,128]{1,0:T(8,128)S(1)}, f32[144,128]{1,0:T(8,128)S(1)}, u32[]{:S(2)}, u32[]{:S(2)}) collective-permute-start(f32[144,128]{1,0:T(8,128)S(1)} %collective-permute-done.12), channel_id=1, source_target_pairs={{0,1},{1,4},{2,3},{3,6},{4,5},{5,0},{6,7},{7,2},{8,9},{9,12},{10,1... | collective-permute-start | bytes 221192 | tf_op jit(solution)/shard_map/ppermute | solution.py:79
  28.2 2.1 %collective-permute-done.13 = f32[144,128]{1,0:T(8,128)S(1)} collective-permute-done((f32[144,128]{1,0:T(8,128)S(1)}, f32[144,128]{1,0:T(8,128)S(1)}, u32[]{:S(2)}, u32[]{:S(2)}) %collective-permute-start.13) | collective-permute-done | bytes 73760 | tf_op jit(solution)/shard_map/ppermute | solution.py:79
  30.3 0.3 collective-permute-done.14
  30.6 2.2 %collective-permute-done.15 = f32[144,128]{1,0:T(8,128)S(1)} collective-permute-done((f32[144,128]{1,0:T(8,128)S(1)}, f32[144,128]{1,0:T(8,128)S(1)}, u32[]{:S(2)}, u32[]{:S(2)}) %collective-permute-start.15) | collective-permute-done | bytes 73760 | tf_op jit(solution)/shard_map/ppermute | solution.py:79
  32.9 0.1 collective-permute-start.16
  33.0 1.2 %collective-permute-done.16 = f32[128,128]{1,0:T(8,128)S(1)} collective-permute-done((f32[128,128]{1,0:T(8,128)S(1)}, f32[128,128]{1,0:T(8,128)S(1)}, u32[]{:S(2)}, u32[]{:S(2)}) %collective-permute-start.16) | collective-permute-done | bytes 65568 | tf_op jit(solution)/shard_map/ppermute | solution.py:74
  34.2 0.2 collective-permute-start.17
  34.4 1.5 %collective-permute-start.18 = (f32[128,128]{1,0:T(8,128)S(1)}, f32[128,128]{1,0:T(8,128)S(1)}, u32[]{:S(2)}, u32[]{:S(2)}) collective-permute-start(f32[128,128]{1,0:T(8,128)S(1)} %collective-permute-done.16), channel_id=1, source_target_pairs={{0,1},{1,16},{2,3},{3,18},{4,5},{5,20},{6,7},{7,22},{8,9},{9,24},{... | collective-permute-start | bytes 196616 | tf_op jit(solution)/shard_map/ppermute | solution.py:79
  35.9 1.2 %collective-permute-start.19 = (f32[128,128]{1,0:T(8,128)S(1)}, f32[128,128]{1,0:T(8,128)S(1)}, u32[]{:S(2)}, u32[]{:S(2)}) collective-permute-start(f32[128,128]{1,0:T(8,128)S(1)} %collective-permute-done.16), channel_id=1, source_target_pairs={{0,1},{1,24},{2,3},{3,26},{4,5},{5,28},{6,7},{7,30},{8,9},{9,16},{... | collective-permute-start | bytes 196616 | tf_op jit(solution)/shard_map/ppermute | solution.py:79
  37.2 1.6 %collective-permute-start.10 = (f32[128,128]{1,0:T(8,128)S(1)}, f32[128,128]{1,0:T(8,128)S(1)}, u32[]{:S(2)}, u32[]{:S(2)}) collective-permute-start(f32[128,128]{1,0:T(8,128)S(1)} %get-tuple-element.28.moved), channel_id=1, source_target_pairs={{0,1},{1,0},{2,3},{3,2},{4,5},{5,4},{6,7},{7,6},{8,9},{9,8},{10,11... | collective-permute-start | bytes 196616 | tf_op jit(solution)/shard_map/ppermute | solution.py:74
  38.8 0.0 collective-permute-start.9
  38.8 3.3 %collective-permute-done.18 = f32[128,128]{1,0:T(8,128)S(1)} collective-permute-done((f32[128,128]{1,0:T(8,128)S(1)}, f32[128,128]{1,0:T(8,128)S(1)}, u32[]{:S(2)}, u32[]{:S(2)}) %collective-permute-start.18) | collective-permute-done | bytes 65568 | tf_op jit(solution)/shard_map/ppermute | solution.py:79
  42.1 0.0 collective-permute-done.19
  42.2 0.1 collective-permute-start.20
  42.3 0.5 %collective-permute-start.21 = (f32[32,128]{1,0:T(8,128)S(1)}, f32[32,128]{1,0:T(8,128)S(1)}, u32[]{:S(2)}, u32[]{:S(2)}) collective-permute-start(f32[32,128]{1,0:T(8,128)S(1)} %pad_maximum_fusion.2.rows), channel_id=1, source_target_pairs={{0,1},{1,0},{2,3},{3,2},{4,5},{5,4},{6,7},{7,6},{8,9},{9,8},{10,11... | collective-permute-start | bytes 49160 | tf_op jit(solution)/shard_map/ppermute | solution.py:74
  42.7 0.0 collective-permute-done.9.mate_sums
  42.7 0.7 %shard_map.87 = (f32[128,128]{1,0:T(8,128)}, f32[1,128]{1,0:T(1,128)S(1)}, f32[128,128]{1,0:T(8,128)S(1)}) custom-call(f32[144,128]{1,0:T(8,128)S(1)} %add.41.sums, f32[144,128]{1,0:T(8,128)S(1)} %collective-permute-done.9.mate_sums, f32[128,128]{1,0:T(8,128)S(1)} %get-tuple-element.28.moved, f32[128,128]{1,0:T(8,128)S(1)} %collective-permute-done.10.mate_moved, ...), custom_call_target="tpu_custom_call" | custom-call | flops 131072 | bytes 65536 | tf_op jit(solution)/shard_map/pallas_call | solution.py:37
  43.4 0.1 collective-permute-done.21.mate_rows
  43.6 0.0 collective-permute-done.20.mate_terms
  43.6 1.2 %shard_map.90 = (f32[8,128]{1,0:T(8,128)}, f32[128,128]{1,0:T(8,128)}, f32[1,128]{1,0:T(1,128)}) custom-call(f32[128,128]{1,0:T(8,128)S(1)} %add_add_fusion.1.terms, f32[128,128]{1,0:T(8,128)S(1)} %collective-permute-done.20.mate_terms, f32[32,128]{1,0:T(8,128)S(1)} %pad_maximum_fusion.2.rows, f32[32,128]{1,0:T(8,128)S(1)} %collective-permute-done.21.mate_rows, ...), custom_call_target="tpu_custom_call" | custom-call | flops 25165824 | bytes 65536 | tf_op jit(solution)/shard_map/pallas_call | solution.py:37
  (20 shorter events, 0.1 us)
Async XLA Ops:
  3.8 1.4 %collective-permute-start = (f32[136,128]{1,0:T(8,128)S(1)}, f32[136,128]{1,0:T(8,128)S(1)}, u32[]{:S(2)}, u32[]{:S(2)}) collective-permute-start(f32[136,128]{1,0:T(8,128)S(1)} %get-tuple-element.21), channel_id=1, source_target_pairs={{0,1},{1,0},{2,3},{3,2},{4,5},{5,4},{6,7},{7,6},{8,9},{9,8},{10,11... | collective-permute-start | bytes 208904 | tf_op jit(solution)/shard_map/ppermute | solution.py:74
  4.3 5.7 %collective-permute-start.2 = (f32[8,128,128]{2,1,0:T(8,128)S(1)}, f32[8,128,128]{2,1,0:T(8,128)S(1)}, u32[]{:S(2)}, u32[]{:S(2)}) collective-permute-start(f32[8,128,128]{2,1,0:T(8,128)S(1)} %get-tuple-element.26.con), channel_id=1, source_target_pairs={{0,1},{1,0},{2,3},{3,2},{4,5},{5,4},{6,7},{7,6},{8,9},{9,8},{10,11... | collective-permute-start | bytes 1572872 | tf_op jit(solution)/shard_map/ppermute | solution.py:74
  5.2 4.7 %collective-permute-start.1 = (f32[144,128]{1,0:T(8,128)S(1)}, f32[144,128]{1,0:T(8,128)S(1)}, u32[]{:S(2)}, u32[]{:S(2)}) collective-permute-start(f32[144,128]{1,0:T(8,128)S(1)} %pad_maximum_fusion), channel_id=1, source_target_pairs={{0,1},{1,2},{2,3},{3,0},{4,5},{5,6},{6,7},{7,4},{8,9},{9,10},{10,1... | collective-permute-start | bytes 221192 | tf_op jit(solution)/shard_map/ppermute | solution.py:79
  5.6 14.8 %collective-permute-start.11 = (f32[1024,128]{1,0:T(8,128)S(1)}, f32[1024,128]{1,0:T(8,128)S(1)}, u32[]{:S(2)}, u32[]{:S(2)}) collective-permute-start(f32[1024,128]{1,0:T(8,128)S(1)} %get-tuple-element.32.x), channel_id=1, source_target_pairs={{0,1},{1,0},{2,3},{3,2},{4,5},{5,4},{6,7},{7,6},{8,9},{9,8},{10,11... | collective-permute-start | bytes 1572872 | tf_op jit(solution)/shard_map/ppermute | solution.py:74
  10.8 1.3 %collective-permute-start.3 = (f32[144,128]{1,0:T(8,128)S(1)}, f32[144,128]{1,0:T(8,128)S(1)}, u32[]{:S(2)}, u32[]{:S(2)}) collective-permute-start(f32[144,128]{1,0:T(8,128)S(1)} %get-tuple-element.27), channel_id=1, source_target_pairs={{0,1},{1,0},{2,3},{3,2},{4,5},{5,4},{6,7},{7,6},{8,9},{9,8},{10,11... | collective-permute-start | bytes 221192 | tf_op jit(solution)/shard_map/ppermute | solution.py:74
  12.2 3.8 %collective-permute-start.4 = (f32[144,128]{1,0:T(8,128)S(1)}, f32[144,128]{1,0:T(8,128)S(1)}, u32[]{:S(2)}, u32[]{:S(2)}) collective-permute-start(f32[144,128]{1,0:T(8,128)S(1)} %collective-permute-done.3), channel_id=1, source_target_pairs={{0,1},{1,4},{2,3},{3,6},{4,5},{5,0},{6,7},{7,2},{8,9},{9,12},{10,1... | collective-permute-start | bytes 221192 | tf_op jit(solution)/shard_map/ppermute | solution.py:79
  12.3 5.1 %collective-permute-start.5 = (f32[144,128]{1,0:T(8,128)S(1)}, f32[144,128]{1,0:T(8,128)S(1)}, u32[]{:S(2)}, u32[]{:S(2)}) collective-permute-start(f32[144,128]{1,0:T(8,128)S(1)} %collective-permute-done.3), channel_id=1, source_target_pairs={{0,1},{1,8},{2,3},{3,10},{4,5},{5,12},{6,7},{7,14},{8,9},{9,0},{10... | collective-permute-start | bytes 221192 | tf_op jit(solution)/shard_map/ppermute | solution.py:79
  14.2 4.7 %collective-permute-start.6 = (f32[144,128]{1,0:T(8,128)S(1)}, f32[144,128]{1,0:T(8,128)S(1)}, u32[]{:S(2)}, u32[]{:S(2)}) collective-permute-start(f32[144,128]{1,0:T(8,128)S(1)} %collective-permute-done.3), channel_id=1, source_target_pairs={{0,1},{1,12},{2,3},{3,14},{4,5},{5,8},{6,7},{7,10},{8,9},{9,4},{10... | collective-permute-start | bytes 221192 | tf_op jit(solution)/shard_map/ppermute | solution.py:79
  18.9 1.3 %collective-permute-start.7 = (f32[144,128]{1,0:T(8,128)S(1)}, f32[144,128]{1,0:T(8,128)S(1)}, u32[]{:S(2)}, u32[]{:S(2)}) collective-permute-start(f32[144,128]{1,0:T(8,128)S(1)} %add_add_fusion), channel_id=1, source_target_pairs={{0,1},{1,0},{2,3},{3,2},{4,5},{5,4},{6,7},{7,6},{8,9},{9,8},{10,11... | collective-permute-start | bytes 221192 | tf_op jit(solution)/shard_map/ppermute | solution.py:74
  20.3 4.7 %collective-permute-start.8 = (f32[144,128]{1,0:T(8,128)S(1)}, f32[144,128]{1,0:T(8,128)S(1)}, u32[]{:S(2)}, u32[]{:S(2)}) collective-permute-start(f32[144,128]{1,0:T(8,128)S(1)} %collective-permute-done.7), channel_id=1, source_target_pairs={{0,1},{1,16},{2,3},{3,18},{4,5},{5,20},{6,7},{7,22},{8,9},{9,24},{... | collective-permute-start | bytes 221192 | tf_op jit(solution)/shard_map/ppermute | solution.py:79
  25.2 1.3 %collective-permute-start.12 = (f32[144,128]{1,0:T(8,128)S(1)}, f32[144,128]{1,0:T(8,128)S(1)}, u32[]{:S(2)}, u32[]{:S(2)}) collective-permute-start(f32[144,128]{1,0:T(8,128)S(1)} %shard_map.89), channel_id=1, source_target_pairs={{0,1},{1,0},{2,3},{3,2},{4,5},{5,4},{6,7},{7,6},{8,9},{9,8},{10,11... | collective-permute-start | bytes 221192 | tf_op jit(solution)/shard_map/ppermute | solution.py:74
  26.6 3.8 %collective-permute-start.13 = (f32[144,128]{1,0:T(8,128)S(1)}, f32[144,128]{1,0:T(8,128)S(1)}, u32[]{:S(2)}, u32[]{:S(2)}) collective-permute-start(f32[144,128]{1,0:T(8,128)S(1)} %collective-permute-done.12), channel_id=1, source_target_pairs={{0,1},{1,2},{2,3},{3,0},{4,5},{5,6},{6,7},{7,4},{8,9},{9,10},{10,1... | collective-permute-start | bytes 221192 | tf_op jit(solution)/shard_map/ppermute | solution.py:79
  26.7 3.9 %collective-permute-start.14 = (f32[144,128]{1,0:T(8,128)S(1)}, f32[144,128]{1,0:T(8,128)S(1)}, u32[]{:S(2)}, u32[]{:S(2)}) collective-permute-start(f32[144,128]{1,0:T(8,128)S(1)} %collective-permute-done.12), channel_id=1, source_target_pairs={{0,1},{1,4},{2,3},{3,6},{4,5},{5,0},{6,7},{7,2},{8,9},{9,12},{10,1... | collective-permute-start | bytes 221192 | tf_op jit(solution)/shard_map/ppermute | solution.py:79
  28.2 4.7 %collective-permute-start.15 = (f32[144,128]{1,0:T(8,128)S(1)}, f32[144,128]{1,0:T(8,128)S(1)}, u32[]{:S(2)}, u32[]{:S(2)}) collective-permute-start(f32[144,128]{1,0:T(8,128)S(1)} %collective-permute-done.12), channel_id=1, source_target_pairs={{0,1},{1,6},{2,3},{3,4},{4,5},{5,2},{6,7},{7,0},{8,9},{9,14},{10,1... | collective-permute-start | bytes 221192 | tf_op jit(solution)/shard_map/ppermute | solution.py:79
  30.3 8.4 %copy-start = (f32[144,128]{1,0:T(8,128)}, f32[144,128]{1,0:T(8,128)S(1)}, u32[]{:S(2)}) copy-start(f32[144,128]{1,0:T(8,128)S(1)} %collective-permute-done.13) | copy-start | bytes 221188
  32.9 1.3 %collective-permute-start.16 = (f32[128,128]{1,0:T(8,128)S(1)}, f32[128,128]{1,0:T(8,128)S(1)}, u32[]{:S(2)}, u32[]{:S(2)}) collective-permute-start(f32[128,128]{1,0:T(8,128)S(1)} %fusion), channel_id=1, source_target_pairs={{0,1},{1,0},{2,3},{3,2},{4,5},{5,4},{6,7},{7,6},{8,9},{9,8},{10,11... | collective-permute-start | bytes 196616 | tf_op jit(solution)/shard_map/ppermute | solution.py:74
  34.2 4.6 %collective-permute-start.17 = (f32[128,128]{1,0:T(8,128)S(1)}, f32[128,128]{1,0:T(8,128)S(1)}, u32[]{:S(2)}, u32[]{:S(2)}) collective-permute-start(f32[128,128]{1,0:T(8,128)S(1)} %collective-permute-done.16), channel_id=1, source_target_pairs={{0,1},{1,8},{2,3},{3,10},{4,5},{5,12},{6,7},{7,14},{8,9},{9,0},{10... | collective-permute-start | bytes 196616 | tf_op jit(solution)/shard_map/ppermute | solution.py:79
  34.4 7.8 %collective-permute-start.18 = (f32[128,128]{1,0:T(8,128)S(1)}, f32[128,128]{1,0:T(8,128)S(1)}, u32[]{:S(2)}, u32[]{:S(2)}) collective-permute-start(f32[128,128]{1,0:T(8,128)S(1)} %collective-permute-done.16), channel_id=1, source_target_pairs={{0,1},{1,16},{2,3},{3,18},{4,5},{5,20},{6,7},{7,22},{8,9},{9,24},{... | collective-permute-start | bytes 196616 | tf_op jit(solution)/shard_map/ppermute | solution.py:79
  35.9 6.2 %collective-permute-start.19 = (f32[128,128]{1,0:T(8,128)S(1)}, f32[128,128]{1,0:T(8,128)S(1)}, u32[]{:S(2)}, u32[]{:S(2)}) collective-permute-start(f32[128,128]{1,0:T(8,128)S(1)} %collective-permute-done.16), channel_id=1, source_target_pairs={{0,1},{1,24},{2,3},{3,26},{4,5},{5,28},{6,7},{7,30},{8,9},{9,16},{... | collective-permute-start | bytes 196616 | tf_op jit(solution)/shard_map/ppermute | solution.py:79
  37.2 5.6 %collective-permute-start.10 = (f32[128,128]{1,0:T(8,128)S(1)}, f32[128,128]{1,0:T(8,128)S(1)}, u32[]{:S(2)}, u32[]{:S(2)}) collective-permute-start(f32[128,128]{1,0:T(8,128)S(1)} %get-tuple-element.28.moved), channel_id=1, source_target_pairs={{0,1},{1,0},{2,3},{3,2},{4,5},{5,4},{6,7},{7,6},{8,9},{9,8},{10,11... | collective-permute-start | bytes 196616 | tf_op jit(solution)/shard_map/ppermute | solution.py:74
  38.8 4.0 %collective-permute-start.9 = (f32[144,128]{1,0:T(8,128)S(1)}, f32[144,128]{1,0:T(8,128)S(1)}, u32[]{:S(2)}, u32[]{:S(2)}) collective-permute-start(f32[144,128]{1,0:T(8,128)S(1)} %add.41.sums), channel_id=1, source_target_pairs={{0,1},{1,0},{2,3},{3,2},{4,5},{5,4},{6,7},{7,6},{8,9},{9,8},{10,11... | collective-permute-start | bytes 221192 | tf_op jit(solution)/shard_map/ppermute | solution.py:74
  38.8 3.5 %slice-start = ((f32[144,128]{1,0:T(8,128)}), f32[16,128]{1,0:T(8,128)S(1)}, s32[]{:S(2)}) async-start(f32[144,128]{1,0:T(8,128)} %copy-done), calls=%async_computation | async-start | bytes 16384 | tf_op jit(solution)/shard_map/slice | solution.py:262
  42.2 1.4 %collective-permute-start.20 = (f32[128,128]{1,0:T(8,128)S(1)}, f32[128,128]{1,0:T(8,128)S(1)}, u32[]{:S(2)}, u32[]{:S(2)}) collective-permute-start(f32[128,128]{1,0:T(8,128)S(1)} %add_add_fusion.1.terms), channel_id=1, source_target_pairs={{0,1},{1,0},{2,3},{3,2},{4,5},{5,4},{6,7},{7,6},{8,9},{9,8},{10,11... | collective-permute-start | bytes 196616 | tf_op jit(solution)/shard_map/ppermute | solution.py:74
  42.3 1.3 %collective-permute-start.21 = (f32[32,128]{1,0:T(8,128)S(1)}, f32[32,128]{1,0:T(8,128)S(1)}, u32[]{:S(2)}, u32[]{:S(2)}) collective-permute-start(f32[32,128]{1,0:T(8,128)S(1)} %pad_maximum_fusion.2.rows), channel_id=1, source_target_pairs={{0,1},{1,0},{2,3},{3,2},{4,5},{5,4},{6,7},{7,6},{8,9},{9,8},{10,11... | collective-permute-start | bytes 49160 | tf_op jit(solution)/shard_map/ppermute | solution.py:74

commit v7 on v6

--- a/solution.py
+++ b/solution.py
@@ -74,9 +74,13 @@
     return lax.ppermute(values, ALL, [(i, i ^ 1) for i in range(lax.axis_size(ALL))])
 
 
-def cross(values, mask):
-    pairs = [(i, i ^ 1 ^ mask if i & 1 else i ^ 1) for i in range(lax.axis_size(ALL))]
+def exchange(values, mask):
+    pairs = [(i, i ^ mask if i & 1 else i) for i in range(lax.axis_size(ALL))]
     return lax.ppermute(values, ALL, pairs)
+
+
+def exchange_sum(values, group):
+    return tree([values] + [exchange(values, mask) for mask in masks_of(group)[1:]])
 
 
 def tree(parts):
@@ -89,8 +93,28 @@
     return lax.axis_index("smp")
 
 
-def from_core_0(own, got):
-    return jnp.where(smp_index() & 1 == 0, own, got)
+def from_core_1(own, got):
+    return jnp.where(smp_index() & 1 == 1, own, got)
+
+
+def pack(gram):
+    half = gram.shape[0] // 2
+    rows = lax.broadcasted_iota(jnp.int32, (half, 2 * half), 0)
+    columns = lax.broadcasted_iota(jnp.int32, (half, 2 * half), 1)
+    top, bottom = gram[:half], gram[half:]
+    packed = jnp.where(rows <= columns, top, pltpu.roll(bottom, half, 1))
+    return packed, jnp.sum(jnp.where(columns == rows + half, bottom, 0.0), axis=0, keepdims=True)
+
+
+def unpack(packed, diagonal):
+    half = packed.shape[0]
+    rows = lax.broadcasted_iota(jnp.int32, packed.shape, 0)
+    columns = lax.broadcasted_iota(jnp.int32, packed.shape, 1)
+    turned = jnp.concatenate([packed, packed], axis=0).T
+    top = jnp.where(rows <= columns, packed, turned[:half])
+    corner = jnp.where(columns < rows + half, pltpu.roll(packed, half, 1), turned[:half])
+    corner = jnp.where(columns == rows + half, diagonal, corner)
+    return jnp.concatenate([top, jnp.where(columns < half, turned[half:], corner)], axis=0)
 
 
 def in_order(rows, scratch, chips):
@@ -170,16 +194,14 @@
     got = swap(opened)
     terms = opened[:vox_rows] + got[:vox_rows]
     rows_b = jnp.concatenate([got[vox_rows:], opened[vox_rows:]], axis=0)
-    handed = jnp.concatenate([terms, rows_b], axis=0)
-    rows_b = jnp.concatenate([opened[vox_rows:], got[vox_rows:]], axis=0)
     for group in groups_of(chip_bits):
-        if handed is None:
-            handed = swap(jnp.concatenate([terms, rows_b], axis=0))
-        parts = [cross(handed, mask) for mask in masks_of(group)[1:]]
+        packet = jnp.concatenate([terms, rows_b], axis=0)
+        parts = [exchange(packet, mask) for mask in masks_of(group)[1:]]
         terms = tree([terms] + [part[:vox_rows] for part in parts])
         rows_b = jnp.concatenate([rows_b] + [part[vox_rows:] for part in parts], axis=0)
-        handed = None
     mate_con = swap(con)
+
+    half, sums_rows = rank // 2, rank // 2 + chip_rows
 
     def voxel_kernel(terms, rows, a, w, outer_c, con, mate_con, moved_out, chip_b, out, all_b):
         b = in_order(rows, all_b, chips)
@@ -187,38 +209,40 @@
         coupled = outer_c[...] * dot_rows(b, b)
         moved = a[...] - step_of(coupled) * (dot(a[...], coupled) - terms[...] * w[...])
         moved_out[...] = moved
-        out[:rank, :] = dot_rows(moved, moved)
+        packed, diagonal = pack(dot_rows(moved, moved))
+        out[:half, :] = packed
         for core in range(2):
             for j in range(smp_rows):
-                row = rank + core * smp_rows + j
-                out[row : row + 1, :] = jnp.sum((con, mate_con)[core][j] * moved, axis=0, keepdims=True)
+                row = half + core * smp_rows + j
+                out[row : row + 1, :] = jnp.sum((mate_con, con)[core][j] * moved, axis=0, keepdims=True)
+        out[sums_rows:, :] = jnp.broadcast_to(diagonal, (8, rank))
 
     moved_a, chip_b, sums = call(
         voxel_kernel,
-        (near(vox_rows, rank), near(chip_rows, rank), near(rank + chip_rows, rank)),
+        (near(vox_rows, rank), near(chip_rows, rank), near(sums_rows + 8, rank)),
         (terms, rows_b, a_near, w_row, outer_c, con, mate_con),
         2 * rank * rank * vox_rows * 12,
         scratch=(near(smp_total, rank),),
     )
 
     for group in groups_of(vox_bits):
-        handed = swap(sums)
-        sums = tree([sums] + [cross(handed, mask) for mask in masks_of(group)[1:]])
+        sums = exchange_sum(sums, group)
     mate_x = swap(x)
 
     def time_kernel(x, mate_x, moved, each):
         for core in range(2):
             for j in range(smp_rows):
-                block = (x, mate_x)[core][pl.ds(j, vox_rows, stride=smp_rows), :]
+                block = (mate_x, x)[core][pl.ds(j, vox_rows, stride=smp_rows), :]
                 each[core * smp_rows + j] = dot_rows(block, moved[...])
 
     (each,) = call(
         time_kernel, (near(chip_rows, times, rank),), (x, mate_x, moved_a), 4 * flat_rows * times * rank * 6
     )
 
-    def sample_kernel(sums, b, w, outer_c, each, out):
-        coupled = outer_c[...] * sums[:rank, :]
-        moved = b[...] - step_of(coupled) * (dot(b[...], coupled) - sums[rank:, :] * w[...])
+    def sample_kernel(sums, b, w, outer_c, each, gram_out, out):
+        gram_out[...] = unpack(sums[:half, :], sums[sums_rows : sums_rows + 1, :])
+        coupled = outer_c[...] * gram_out[...]
+        moved = b[...] - step_of(coupled) * (dot(b[...], coupled) - sums[half:sums_rows, :] * w[...])
         out[times:, :] = moved
         total = None
         for j in range(chip_rows):
@@ -226,26 +250,26 @@
             total = made if total is None else total + made
         out[:times, :] = total
 
-    (payload,) = call(
+    gram_a, payload = call(
         sample_kernel,
-        (near(times + chip_rows, rank),),
+        (near(rank, rank), near(times + chip_rows, rank)),
         (sums, chip_b, w_row, outer_c, each),
         2 * rank * rank * chip_rows * 6,
     )
-    mate_sums = swap(sums)
+    mate_gram_a = swap(gram_a)
     mate_moved_a = swap(moved_a)
 
-    def scale_kernel(sums, mate_sums, moved, mate_moved, outer, result, scales_out, weighed):
-        gram = from_core_0(sums[:rank, :], mate_sums[:rank, :])
+    def scale_kernel(gram, mate_gram, moved, mate_moved, outer, result, scales_out, weighed):
+        gram = from_core_1(gram[...], mate_gram[...])
         scales = jnp.sqrt(diagonal_row(gram) / vox_total + 1e-06)
         scales_out[...] = scales
-        result[...] = from_core_0(moved[...], mate_moved[...]) / scales
+        result[...] = from_core_1(moved[...], mate_moved[...]) / scales
         weighed[...] = outer[...] * gram
 
     voxel_result, scales_a, weighed = call(
         scale_kernel,
         (far(vox_rows, rank), near(1, rank), near(rank, rank)),
-        (sums, mate_sums, moved_a, mate_moved_a, outer),
+        (gram_a, mate_gram_a, moved_a, mate_moved_a, outer),
         vox_rows * rank * 8,
     )
 
@@ -253,22 +277,23 @@
     smp_mask = sum(chip_bits)
     for group in groups_of(chip_bits + vox_bits):
         masks = masks_of(group)[1:]
-        with_rows = any(mask & smp_mask for mask in masks)
-        handed = swap(jnp.concatenate([terms, rows_b], axis=0) if with_rows else terms)
-        parts = [cross(handed, mask) for mask in masks]
-        terms = tree([terms] + [part[:times] for part in parts])
-        if with_rows:
+        if any(mask & smp_mask for mask in masks):
+            packet = jnp.concatenate([terms, rows_b], axis=0)
+            parts = [exchange(packet, mask) for mask in masks]
+            terms = tree([terms] + [part[:times] for part in parts])
             parts = [part for part, mask in zip(parts, masks) if not mask & ~smp_mask]
             rows_b = jnp.concatenate([rows_b] + [part[times:] for part in parts], axis=0)
+        else:
+            terms = exchange_sum(terms, group)
     mate_rows_b = swap(rows_b)
     mate_terms = swap(terms)
 
     def last_kernel(terms, mate_terms, rows, mate_rows, c, w, weighed, scales_a, b_out, c_out, w_out, all_b):
-        b = in_order(from_core_0(rows[...], mate_rows[...]), all_b, chips)
+        b = in_order(from_core_1(rows[...], mate_rows[...]), all_b, chips)
         coupled = weighed[...] * dot_rows(b, b)
         scales_b = jnp.sqrt(jnp.sum(b * b, axis=0, keepdims=True) / smp_total + 1e-06)
         b_out[...] = all_b[pl.ds(pl.multiple_of(smp_index() * smp_rows, smp_rows), smp_rows), :] / scales_b
-        summed = from_core_0(terms[...], mate_terms[...])
+        summed = from_core_1(terms[...], mate_terms[...])
         moved = c[...] - step_of(coupled) * (dot(c[...], coupled) - summed * w[...])
         scales_c = jnp.sqrt(jnp.sum(moved * moved, axis=0, keepdims=True) / times + 1e-06)
         c_out[...] = moved / scales_c

time: 44.9 us -> 56.7 us (1.26)
  starting transfers between devices: 13.1 us -> 46.3 us
  waiting for transfers between devices: 23.2 us -> 1.27 us
    ppermute x11 -> x7, starting transfers between devices: 5.68 us -> 38.9 us  [swap(): lax.ppermute(values, ALL, [(i, i ^ 1) for i in range(lax.axis_size(ALL))])]
    ppermute x11, waiting for transfers between devices: 17.2 us -> 0.03 us  [exchange(): return lax.ppermute(values, ALL, pairs)]
    ppermute x11 -> x7, waiting for transfers between devices: 5.98 us -> 1.24 us  [swap(): lax.ppermute(values, ALL, [(i, i ^ 1) for i in range(lax.axis_size(ALL))])]
  transfers between devices with their start and end apart: 22 -> 18, of which waited for: 15 -> 2; matrix products, arithmetic and copies ran while one was open for 0% -> 0% of each run, Pallas kernels for 7% -> 5%
where the time goes in v7:
time: 56.7 us; the launch traced here: 56.3 us
  starting transfers between devices  46.3 us (82%)
  Pallas kernels  7.72 us (14%)
  waiting for transfers between devices  1.27 us (2%)
  between operations  0.93 us (2%)
    ppermute x7, starting transfers between devices, swap(): lax.ppermute(values, ALL, [(i, i ^ 1) for i in range(lax.axis_size(ALL))])  38.9 us
    pallas_call x7, Pallas kernels, call(): pl.pallas_call(kernel, out_shape=outs, in_specs=specs, out_specs=[pl.Bloc...  7.72 us
    ppermute x11, starting transfers between devices, exchange(): return lax.ppermute(values, ALL, pairs)  7.31 us
    ppermute x7, waiting for transfers between devices, swap(): lax.ppermute(values, ALL, [(i, i ^ 1) for i in range(lax.axis_size(ALL))])  1.24 us
  transfers between devices with their start and end apart: 18, of which 2 were waited for; matrix products, arithmetic and copies ran while one was open for 0% of the time, Pallas kernels for 5%

profile of v7, /device:TPU:0, one launch (start us, length us, event | category | flops | bytes accessed | tf_op | source)
XLA Modules:
  0.0 56.3 jit_solution(7232887815706584853)
XLA Ops:
  0.6 3.1 %shard_map.84 = (f32[1024,128]{1,0:T(8,128)S(1)}, f32[128,128]{1,0:T(8,128)S(1)}, f32[128,128]{1,0:T(8,128)S(1)}, f32[1,128]{1,0:T(1,128)S(1)}, f32[136,128]{1,0:T(8,128)S(1)}, /*index=5*/f32[8,128,128]{2,1,0:T(8,128)S(1)}) custom-call(f32[1024,128]{1,0:T(8,128)} %bitcast.3, f32[128,128]{1,0:T(8,128)} %c_hbm.1, f32[8,128]{1,0:T(8,128)} %b_hbm.1, ...), custom_call_target="tpu_custom_call" | custom-call | flops 201326592 | bytes 65536 | tf_op jit(solution)/shard_map/pallas_call | solution.py:37
  3.8 0.5 collective-permute-start
  4.3 0.1 collective-permute-start.2
  4.4 0.8 %collective-permute-done = f32[136,128]{1,0:T(8,128)S(1)} collective-permute-done((f32[136,128]{1,0:T(8,128)S(1)}, f32[136,128]{1,0:T(8,128)S(1)}, u32[]{:S(2)}, u32[]{:S(2)}) %collective-permute-start) | collective-permute-done | bytes 69664 | tf_op jit(solution)/shard_map/ppermute | solution.py:74
  5.2 0.7 %collective-permute-start.1 = (f32[144,128]{1,0:T(8,128)S(1)}, f32[144,128]{1,0:T(8,128)S(1)}, u32[]{:S(2)}, u32[]{:S(2)}) collective-permute-start(f32[144,128]{1,0:T(8,128)S(1)} %pad_maximum_fusion), channel_id=1, source_target_pairs={{0,0},{1,3},{2,2},{3,1},{4,4},{5,7},{6,6},{7,5},{8,8},{9,11},{10,1... | collective-permute-start | bytes 221192 | tf_op jit(solution)/shard_map/ppermute | solution.py:79
  5.9 4.1 %collective-permute-start.7 = (f32[1024,128]{1,0:T(8,128)S(1)}, f32[1024,128]{1,0:T(8,128)S(1)}, u32[]{:S(2)}, u32[]{:S(2)}) collective-permute-start(f32[1024,128]{1,0:T(8,128)S(1)} %get-tuple-element.31.x), channel_id=1, source_target_pairs={{0,1},{1,0},{2,3},{3,2},{4,5},{5,4},{6,7},{7,6},{8,9},{9,8},{10,11... | collective-permute-start | bytes 1572872 | tf_op jit(solution)/shard_map/ppermute | solution.py:74
  10.0 0.3 shard_map.85
  10.3 0.0 collective-permute-done.1
  10.4 0.0 collective-permute-done.2.mate_con
  10.4 0.9 %shard_map.86 = (f32[128,128]{1,0:T(8,128)S(1)}, f32[16,128]{1,0:T(8,128)S(1)}, f32[88,128]{1,0:T(8,128)S(1)}) custom-call(f32[128,128]{1,0:T(8,128)S(1)} %slice_add_fusion.2.terms, f32[32,128]{1,0:T(8,128)S(1)} %pad_maximum_fusion.1.rows, f32[128,128]{1,0:T(8,128)S(1)} %get-tuple-element.24.a, f32[1,128]{1,0:T(1,128)S(1)} %get-tuple-element.25.w, ...), custom_call_target="tpu_custom_call" | custom-call | flops 50331648 | bytes 65536 | tf_op jit(solution)/shard_map/pallas_call | solution.py:37
  11.3 0.7 %collective-permute-start.4 = (f32[88,128]{1,0:T(8,128)S(1)}, f32[88,128]{1,0:T(8,128)S(1)}, u32[]{:S(2)}, u32[]{:S(2)}) collective-permute-start(f32[88,128]{1,0:T(8,128)S(1)} %get-tuple-element.29), channel_id=1, source_target_pairs={{0,0},{1,9},{2,2},{3,11},{4,4},{5,13},{6,6},{7,15},{8,8},{9,1},{10... | collective-permute-start | bytes 135176 | tf_op jit(solution)/shard_map/ppermute | solution.py:79
  12.0 0.7 %collective-permute-start.5 = (f32[88,128]{1,0:T(8,128)S(1)}, f32[88,128]{1,0:T(8,128)S(1)}, u32[]{:S(2)}, u32[]{:S(2)}) collective-permute-start(f32[88,128]{1,0:T(8,128)S(1)} %get-tuple-element.29), channel_id=1, source_target_pairs={{0,0},{1,13},{2,2},{3,15},{4,4},{5,9},{6,6},{7,11},{8,8},{9,5},{10... | collective-permute-start | bytes 135176 | tf_op jit(solution)/shard_map/ppermute | solution.py:79
  12.6 0.7 %collective-permute-start.3 = (f32[88,128]{1,0:T(8,128)S(1)}, f32[88,128]{1,0:T(8,128)S(1)}, u32[]{:S(2)}, u32[]{:S(2)}) collective-permute-start(f32[88,128]{1,0:T(8,128)S(1)} %get-tuple-element.29), channel_id=1, source_target_pairs={{0,0},{1,5},{2,2},{3,7},{4,4},{5,1},{6,6},{7,3},{8,8},{9,13},{10,1... | collective-permute-start | bytes 135176 | tf_op jit(solution)/shard_map/ppermute | solution.py:79
  13.3 0.0 collective-permute-done.4
  13.3 0.0 collective-permute-done.5
  13.3 0.0 collective-permute-done.3
  13.4 0.7 %collective-permute-start.6 = (f32[88,128]{1,0:T(8,128)S(1)}, f32[88,128]{1,0:T(8,128)S(1)}, u32[]{:S(2)}, u32[]{:S(2)}) collective-permute-start(f32[88,128]{1,0:T(8,128)S(1)} %add_add_fusion.1), channel_id=1, source_target_pairs={{0,0},{1,17},{2,2},{3,19},{4,4},{5,21},{6,6},{7,23},{8,8},{9,25},{... | collective-permute-start | bytes 135176 | tf_op jit(solution)/shard_map/ppermute | solution.py:79
  14.0 0.0 collective-permute-done.7.mate_x
  14.0 1.1 %shard_map.87.each = f32[16,128,128]{2,1,0:T(8,128)S(1)} custom-call(f32[1024,128]{1,0:T(8,128)S(1)} %get-tuple-element.31.x, f32[1024,128]{1,0:T(8,128)S(1)} %collective-permute-done.7.mate_x, f32[128,128]{1,0:T(8,128)S(1)} %get-tuple-element.32.moved), custom_call_target="tpu_custom_call" | custom-call | flops 402653184 | bytes 65536 | tf_op jit(solution)/shard_map/pallas_call | solution.py:37
  15.1 0.0 collective-permute-done.6
  15.2 0.4 shard_map.88
  15.5 0.7 %collective-permute-start.12 = (f32[144,128]{1,0:T(8,128)S(1)}, f32[144,128]{1,0:T(8,128)S(1)}, u32[]{:S(2)}, u32[]{:S(2)}) collective-permute-start(f32[144,128]{1,0:T(8,128)S(1)} %get-tuple-element.36), channel_id=1, source_target_pairs={{0,0},{1,7},{2,2},{3,5},{4,4},{5,3},{6,6},{7,1},{8,8},{9,15},{10,1... | collective-permute-start | bytes 221192 | tf_op jit(solution)/shard_map/ppermute | solution.py:79
  16.2 0.7 %collective-permute-start.11 = (f32[144,128]{1,0:T(8,128)S(1)}, f32[144,128]{1,0:T(8,128)S(1)}, u32[]{:S(2)}, u32[]{:S(2)}) collective-permute-start(f32[144,128]{1,0:T(8,128)S(1)} %get-tuple-element.36), channel_id=1, source_target_pairs={{0,0},{1,5},{2,2},{3,7},{4,4},{5,1},{6,6},{7,3},{8,8},{9,13},{10,1... | collective-permute-start | bytes 221192 | tf_op jit(solution)/shard_map/ppermute | solution.py:79
  16.9 0.7 %collective-permute-start.10 = (f32[144,128]{1,0:T(8,128)S(1)}, f32[144,128]{1,0:T(8,128)S(1)}, u32[]{:S(2)}, u32[]{:S(2)}) collective-permute-start(f32[144,128]{1,0:T(8,128)S(1)} %get-tuple-element.36), channel_id=1, source_target_pairs={{0,0},{1,3},{2,2},{3,1},{4,4},{5,7},{6,6},{7,5},{8,8},{9,11},{10,1... | collective-permute-start | bytes 221192 | tf_op jit(solution)/shard_map/ppermute | solution.py:79
  17.6 0.0 collective-permute-done.12
  17.6 0.0 collective-permute-done.11
  17.6 0.0 collective-permute-done.10
  17.6 0.0 copy-start
  17.6 0.7 %collective-permute-start.14 = (f32[128,128]{1,0:T(8,128)S(1)}, f32[128,128]{1,0:T(8,128)S(1)}, u32[]{:S(2)}, u32[]{:S(2)}) collective-permute-start(f32[128,128]{1,0:T(8,128)S(1)} %fusion), channel_id=1, source_target_pairs={{0,0},{1,17},{2,2},{3,19},{4,4},{5,21},{6,6},{7,23},{8,8},{9,25},{... | collective-permute-start | bytes 196616 | tf_op jit(solution)/shard_map/ppermute | solution.py:79
  18.3 0.7 %collective-permute-start.15 = (f32[128,128]{1,0:T(8,128)S(1)}, f32[128,128]{1,0:T(8,128)S(1)}, u32[]{:S(2)}, u32[]{:S(2)}) collective-permute-start(f32[128,128]{1,0:T(8,128)S(1)} %fusion), channel_id=1, source_target_pairs={{0,0},{1,25},{2,2},{3,27},{4,4},{5,29},{6,6},{7,31},{8,8},{9,17},{... | collective-permute-start | bytes 196616 | tf_op jit(solution)/shard_map/ppermute | solution.py:79
  19.0 0.7 %collective-permute-start.13 = (f32[128,128]{1,0:T(8,128)S(1)}, f32[128,128]{1,0:T(8,128)S(1)}, u32[]{:S(2)}, u32[]{:S(2)}) collective-permute-start(f32[128,128]{1,0:T(8,128)S(1)} %fusion), channel_id=1, source_target_pairs={{0,0},{1,9},{2,2},{3,11},{4,4},{5,13},{6,6},{7,15},{8,8},{9,1},{10... | collective-permute-start | bytes 196616 | tf_op jit(solution)/shard_map/ppermute | solution.py:79
  19.6 31.4 %collective-permute-start.9 = (f32[128,128]{1,0:T(8,128)S(1)}, f32[128,128]{1,0:T(8,128)S(1)}, u32[]{:S(2)}, u32[]{:S(2)}) collective-permute-start(f32[128,128]{1,0:T(8,128)S(1)} %get-tuple-element.32.moved), channel_id=1, source_target_pairs={{0,1},{1,0},{2,3},{3,2},{4,5},{5,4},{6,7},{7,6},{8,9},{9,8},{10,11... | collective-permute-start | bytes 196616 | tf_op jit(solution)/shard_map/ppermute | solution.py:74
  51.1 0.1 collective-permute-start.8
  51.2 0.0 copy-done
  51.2 0.0 slice-start
  51.2 0.0 collective-permute-done.14
  51.2 0.0 collective-permute-done.15
  51.2 0.0 collective-permute-done.13
  51.2 2.7 %collective-permute-start.16 = (f32[128,128]{1,0:T(8,128)S(1)}, f32[128,128]{1,0:T(8,128)S(1)}, u32[]{:S(2)}, u32[]{:S(2)}) collective-permute-start(f32[128,128]{1,0:T(8,128)S(1)} %add_add_fusion.terms), channel_id=1, source_target_pairs={{0,1},{1,0},{2,3},{3,2},{4,5},{5,4},{6,7},{7,6},{8,9},{9,8},{10,11... | collective-permute-start | bytes 196616 | tf_op jit(solution)/shard_map/ppermute | solution.py:74
  53.9 0.0 slice-done
  53.9 0.1 collective-permute-start.17
  54.0 0.0 collective-permute-done.9.mate_moved
  54.0 0.0 collective-permute-done.8.mate_gram
  54.0 0.7 %shard_map.89 = (f32[128,128]{1,0:T(8,128)}, f32[1,128]{1,0:T(1,128)S(1)}, f32[128,128]{1,0:T(8,128)S(1)}) custom-call(f32[128,128]{1,0:T(8,128)S(1)} %get-tuple-element.33.gram, f32[128,128]{1,0:T(8,128)S(1)} %collective-permute-done.8.mate_gram, f32[128,128]{1,0:T(8,128)S(1)} %get-tuple-element.32.moved, f32[128,128]{1,0:T(8,128)S(1)} %collective-permute-done.9.mate_moved, ...), custom_call_target="tpu_custom_call" | custom-call | flops 131072 | bytes 65536 | tf_op jit(solution)/shard_map/pallas_call | solution.py:37
  54.7 0.4 collective-permute-done.17.mate_rows
  55.1 0.0 collective-permute-done.16.mate_terms
  55.1 1.2 %shard_map.90 = (f32[8,128]{1,0:T(8,128)}, f32[128,128]{1,0:T(8,128)}, f32[1,128]{1,0:T(1,128)}) custom-call(f32[128,128]{1,0:T(8,128)S(1)} %add_add_fusion.terms, f32[128,128]{1,0:T(8,128)S(1)} %collective-permute-done.16.mate_terms, f32[32,128]{1,0:T(8,128)S(1)} %pad_maximum_fusion.2.rows, f32[32,128]{1,0:T(8,128)S(1)} %collective-permute-done.17.mate_rows, ...), custom_call_target="tpu_custom_call" | custom-call | flops 25165824 | bytes 65536 | tf_op jit(solution)/shard_map/pallas_call | solution.py:37
  (13 shorter events, 0.1 us)
Async XLA Ops:
  3.8 1.4 %collective-permute-start = (f32[136,128]{1,0:T(8,128)S(1)}, f32[136,128]{1,0:T(8,128)S(1)}, u32[]{:S(2)}, u32[]{:S(2)}) collective-permute-start(f32[136,128]{1,0:T(8,128)S(1)} %get-tuple-element.23), channel_id=1, source_target_pairs={{0,1},{1,0},{2,3},{3,2},{4,5},{5,4},{6,7},{7,6},{8,9},{9,8},{10,11... | collective-permute-start | bytes 208904 | tf_op jit(solution)/shard_map/ppermute | solution.py:74
  4.3 6.1 %collective-permute-start.2 = (f32[8,128,128]{2,1,0:T(8,128)S(1)}, f32[8,128,128]{2,1,0:T(8,128)S(1)}, u32[]{:S(2)}, u32[]{:S(2)}) collective-permute-start(f32[8,128,128]{2,1,0:T(8,128)S(1)} %get-tuple-element.28.con), channel_id=1, source_target_pairs={{0,1},{1,0},{2,3},{3,2},{4,5},{5,4},{6,7},{7,6},{8,9},{9,8},{10,11... | collective-permute-start | bytes 1572872 | tf_op jit(solution)/shard_map/ppermute | solution.py:74
  5.2 5.1 %collective-permute-start.1 = (f32[144,128]{1,0:T(8,128)S(1)}, f32[144,128]{1,0:T(8,128)S(1)}, u32[]{:S(2)}, u32[]{:S(2)}) collective-permute-start(f32[144,128]{1,0:T(8,128)S(1)} %pad_maximum_fusion), channel_id=1, source_target_pairs={{0,0},{1,3},{2,2},{3,1},{4,4},{5,7},{6,6},{7,5},{8,8},{9,11},{10,1... | collective-permute-start | bytes 221192 | tf_op jit(solution)/shard_map/ppermute | solution.py:79
  5.9 8.1 %collective-permute-start.7 = (f32[1024,128]{1,0:T(8,128)S(1)}, f32[1024,128]{1,0:T(8,128)S(1)}, u32[]{:S(2)}, u32[]{:S(2)}) collective-permute-start(f32[1024,128]{1,0:T(8,128)S(1)} %get-tuple-element.31.x), channel_id=1, source_target_pairs={{0,1},{1,0},{2,3},{3,2},{4,5},{5,4},{6,7},{7,6},{8,9},{9,8},{10,11... | collective-permute-start | bytes 1572872 | tf_op jit(solution)/shard_map/ppermute | solution.py:74
  11.3 2.0 %collective-permute-start.4 = (f32[88,128]{1,0:T(8,128)S(1)}, f32[88,128]{1,0:T(8,128)S(1)}, u32[]{:S(2)}, u32[]{:S(2)}) collective-permute-start(f32[88,128]{1,0:T(8,128)S(1)} %get-tuple-element.29), channel_id=1, source_target_pairs={{0,0},{1,9},{2,2},{3,11},{4,4},{5,13},{6,6},{7,15},{8,8},{9,1},{10... | collective-permute-start | bytes 135176 | tf_op jit(solution)/shard_map/ppermute | solution.py:79
  12.0 1.4 %collective-permute-start.5 = (f32[88,128]{1,0:T(8,128)S(1)}, f32[88,128]{1,0:T(8,128)S(1)}, u32[]{:S(2)}, u32[]{:S(2)}) collective-permute-start(f32[88,128]{1,0:T(8,128)S(1)} %get-tuple-element.29), channel_id=1, source_target_pairs={{0,0},{1,13},{2,2},{3,15},{4,4},{5,9},{6,6},{7,11},{8,8},{9,5},{10... | collective-permute-start | bytes 135176 | tf_op jit(solution)/shard_map/ppermute | solution.py:79
  12.6 0.7 %collective-permute-start.3 = (f32[88,128]{1,0:T(8,128)S(1)}, f32[88,128]{1,0:T(8,128)S(1)}, u32[]{:S(2)}, u32[]{:S(2)}) collective-permute-start(f32[88,128]{1,0:T(8,128)S(1)} %get-tuple-element.29), channel_id=1, source_target_pairs={{0,0},{1,5},{2,2},{3,7},{4,4},{5,1},{6,6},{7,3},{8,8},{9,13},{10,1... | collective-permute-start | bytes 135176 | tf_op jit(solution)/shard_map/ppermute | solution.py:79
  13.4 1.8 %collective-permute-start.6 = (f32[88,128]{1,0:T(8,128)S(1)}, f32[88,128]{1,0:T(8,128)S(1)}, u32[]{:S(2)}, u32[]{:S(2)}) collective-permute-start(f32[88,128]{1,0:T(8,128)S(1)} %add_add_fusion.1), channel_id=1, source_target_pairs={{0,0},{1,17},{2,2},{3,19},{4,4},{5,21},{6,6},{7,23},{8,8},{9,25},{... | collective-permute-start | bytes 135176 | tf_op jit(solution)/shard_map/ppermute | solution.py:79
  15.5 2.0 %collective-permute-start.12 = (f32[144,128]{1,0:T(8,128)S(1)}, f32[144,128]{1,0:T(8,128)S(1)}, u32[]{:S(2)}, u32[]{:S(2)}) collective-permute-start(f32[144,128]{1,0:T(8,128)S(1)} %get-tuple-element.36), channel_id=1, source_target_pairs={{0,0},{1,7},{2,2},{3,5},{4,4},{5,3},{6,6},{7,1},{8,8},{9,15},{10,1... | collective-permute-start | bytes 221192 | tf_op jit(solution)/shard_map/ppermute | solution.py:79
  16.2 1.4 %collective-permute-start.11 = (f32[144,128]{1,0:T(8,128)S(1)}, f32[144,128]{1,0:T(8,128)S(1)}, u32[]{:S(2)}, u32[]{:S(2)}) collective-permute-start(f32[144,128]{1,0:T(8,128)S(1)} %get-tuple-element.36), channel_id=1, source_target_pairs={{0,0},{1,5},{2,2},{3,7},{4,4},{5,1},{6,6},{7,3},{8,8},{9,13},{10,1... | collective-permute-start | bytes 221192 | tf_op jit(solution)/shard_map/ppermute | solution.py:79
  16.9 0.7 %collective-permute-start.10 = (f32[144,128]{1,0:T(8,128)S(1)}, f32[144,128]{1,0:T(8,128)S(1)}, u32[]{:S(2)}, u32[]{:S(2)}) collective-permute-start(f32[144,128]{1,0:T(8,128)S(1)} %get-tuple-element.36), channel_id=1, source_target_pairs={{0,0},{1,3},{2,2},{3,1},{4,4},{5,7},{6,6},{7,5},{8,8},{9,11},{10,1... | collective-permute-start | bytes 221192 | tf_op jit(solution)/shard_map/ppermute | solution.py:79
  17.6 33.6 %copy-start = (f32[144,128]{1,0:T(8,128)}, f32[144,128]{1,0:T(8,128)S(1)}, u32[]{:S(2)}) copy-start(f32[144,128]{1,0:T(8,128)S(1)} %collective-permute-done.10) | copy-start | bytes 221188
  17.6 33.5 %collective-permute-start.14 = (f32[128,128]{1,0:T(8,128)S(1)}, f32[128,128]{1,0:T(8,128)S(1)}, u32[]{:S(2)}, u32[]{:S(2)}) collective-permute-start(f32[128,128]{1,0:T(8,128)S(1)} %fusion), channel_id=1, source_target_pairs={{0,0},{1,17},{2,2},{3,19},{4,4},{5,21},{6,6},{7,23},{8,8},{9,25},{... | collective-permute-start | bytes 196616 | tf_op jit(solution)/shard_map/ppermute | solution.py:79
  18.3 32.9 %collective-permute-start.15 = (f32[128,128]{1,0:T(8,128)S(1)}, f32[128,128]{1,0:T(8,128)S(1)}, u32[]{:S(2)}, u32[]{:S(2)}) collective-permute-start(f32[128,128]{1,0:T(8,128)S(1)} %fusion), channel_id=1, source_target_pairs={{0,0},{1,25},{2,2},{3,27},{4,4},{5,29},{6,6},{7,31},{8,8},{9,17},{... | collective-permute-start | bytes 196616 | tf_op jit(solution)/shard_map/ppermute | solution.py:79
  19.0 32.2 %collective-permute-start.13 = (f32[128,128]{1,0:T(8,128)S(1)}, f32[128,128]{1,0:T(8,128)S(1)}, u32[]{:S(2)}, u32[]{:S(2)}) collective-permute-start(f32[128,128]{1,0:T(8,128)S(1)} %fusion), channel_id=1, source_target_pairs={{0,0},{1,9},{2,2},{3,11},{4,4},{5,13},{6,6},{7,15},{8,8},{9,1},{10... | collective-permute-start | bytes 196616 | tf_op jit(solution)/shard_map/ppermute | solution.py:79
  19.6 34.4 %collective-permute-start.9 = (f32[128,128]{1,0:T(8,128)S(1)}, f32[128,128]{1,0:T(8,128)S(1)}, u32[]{:S(2)}, u32[]{:S(2)}) collective-permute-start(f32[128,128]{1,0:T(8,128)S(1)} %get-tuple-element.32.moved), channel_id=1, source_target_pairs={{0,1},{1,0},{2,3},{3,2},{4,5},{5,4},{6,7},{7,6},{8,9},{9,8},{10,11... | collective-permute-start | bytes 196616 | tf_op jit(solution)/shard_map/ppermute | solution.py:74
  51.1 2.9 %collective-permute-start.8 = (f32[128,128]{1,0:T(8,128)S(1)}, f32[128,128]{1,0:T(8,128)S(1)}, u32[]{:S(2)}, u32[]{:S(2)}) collective-permute-start(f32[128,128]{1,0:T(8,128)S(1)} %get-tuple-element.33.gram), channel_id=1, source_target_pairs={{0,1},{1,0},{2,3},{3,2},{4,5},{5,4},{6,7},{7,6},{8,9},{9,8},{10,11... | collective-permute-start | bytes 196616 | tf_op jit(solution)/shard_map/ppermute | solution.py:74
  51.2 2.7 %slice-start = ((f32[144,128]{1,0:T(8,128)}), f32[16,128]{1,0:T(8,128)S(1)}, s32[]{:S(2)}) async-start(f32[144,128]{1,0:T(8,128)} %copy-done), calls=%async_computation | async-start | bytes 16384 | tf_op jit(solution)/shard_map/slice | solution.py:285
  51.2 3.9 %collective-permute-start.16 = (f32[128,128]{1,0:T(8,128)S(1)}, f32[128,128]{1,0:T(8,128)S(1)}, u32[]{:S(2)}, u32[]{:S(2)}) collective-permute-start(f32[128,128]{1,0:T(8,128)S(1)} %add_add_fusion.terms), channel_id=1, source_target_pairs={{0,1},{1,0},{2,3},{3,2},{4,5},{5,4},{6,7},{7,6},{8,9},{9,8},{10,11... | collective-permute-start | bytes 196616 | tf_op jit(solution)/shard_map/ppermute | solution.py:74
  53.9 1.2 %collective-permute-start.17 = (f32[32,128]{1,0:T(8,128)S(1)}, f32[32,128]{1,0:T(8,128)S(1)}, u32[]{:S(2)}, u32[]{:S(2)}) collective-permute-start(f32[32,128]{1,0:T(8,128)S(1)} %pad_maximum_fusion.2.rows), channel_id=1, source_target_pairs={{0,1},{1,0},{2,3},{3,2},{4,5},{5,4},{6,7},{7,6},{8,9},{9,8},{10,11... | collective-permute-start | bytes 49160 | tf_op jit(solution)/shard_map/ppermute | solution.py:74

commit v8 on v7

--- a/solution.py
+++ b/solution.py
@@ -66,7 +66,7 @@
 def masks_of(group):
     masks = [0]
     for bit in group:
-        masks = masks + [mask | bit for mask in masks]
+        masks = [mask | bit for mask in masks] + masks
     return masks
 
 
@@ -74,16 +74,19 @@
     return lax.ppermute(values, ALL, [(i, i ^ 1) for i in range(lax.axis_size(ALL))])
 
 
-def exchange(values, mask):
-    pairs = [(i, i ^ mask if i & 1 else i) for i in range(lax.axis_size(ALL))]
+def send(values, holder, mask):
+    count = lax.axis_size(ALL)
+    pairs = [(i, i ^ 1 ^ mask if i & 1 == holder else i ^ 1) for i in range(count)]
     return lax.ppermute(values, ALL, pairs)
 
 
-def exchange_sum(values, group):
-    return tree([values] + [exchange(values, mask) for mask in masks_of(group)[1:]])
+def fan(values, holder, masks):
+    sent = [send(values, holder, mask) if mask else swap(values) for mask in reversed(masks)]
+    return sent[::-1]
 
 
 def tree(parts):
+    parts = parts[::-1]
     while len(parts) > 1:
         parts = [a + b for a, b in zip(parts[::2], parts[1::2])]
     return parts[0]
@@ -93,8 +96,8 @@
     return lax.axis_index("smp")
 
 
-def from_core_1(own, got):
-    return jnp.where(smp_index() & 1 == 1, own, got)
+def on_core(core, own, got):
+    return jnp.where(smp_index() & 1 == core, own, got)
 
 
 def pack(gram):
@@ -121,7 +124,7 @@
     block = scratch.shape[0] // chips
     chip = smp_index() // 2
     for p in range(chips):
-        scratch[pl.ds(pl.multiple_of((chip ^ p) * block, block), block), :] = rows[p * block : (p + 1) * block, :]
+        scratch[pl.ds(pl.multiple_of((chip ^ (chips - 1 - p)) * block, block), block), :] = rows[p * block : (p + 1) * block, :]
     return scratch[...]
 
 
@@ -194,11 +197,13 @@
     got = swap(opened)
     terms = opened[:vox_rows] + got[:vox_rows]
     rows_b = jnp.concatenate([got[vox_rows:], opened[vox_rows:]], axis=0)
+    holder = 1
     for group in groups_of(chip_bits):
-        packet = jnp.concatenate([terms, rows_b], axis=0)
-        parts = [exchange(packet, mask) for mask in masks_of(group)[1:]]
-        terms = tree([terms] + [part[:vox_rows] for part in parts])
-        rows_b = jnp.concatenate([rows_b] + [part[vox_rows:] for part in parts], axis=0)
+        parts = fan(jnp.concatenate([terms, rows_b], axis=0), holder, masks_of(group))
+        terms = tree([part[:vox_rows] for part in parts])
+        rows_b = jnp.concatenate([part[vox_rows:] for part in parts], axis=0)
+        holder ^= 1
+    voxel_core = holder
     mate_con = swap(con)
 
     half, sums_rows = rank // 2, rank // 2 + chip_rows
@@ -214,7 +219,7 @@
         for core in range(2):
             for j in range(smp_rows):
                 row = half + core * smp_rows + j
-                out[row : row + 1, :] = jnp.sum((mate_con, con)[core][j] * moved, axis=0, keepdims=True)
+                out[row : row + 1, :] = jnp.sum((con if core == voxel_core else mate_con)[j] * moved, axis=0, keepdims=True)
         out[sums_rows:, :] = jnp.broadcast_to(diagonal, (8, rank))
 
     moved_a, chip_b, sums = call(
@@ -225,18 +230,28 @@
         scratch=(near(smp_total, rank),),
     )
 
+    mate_moved_a = swap(moved_a)
+
     for group in groups_of(vox_bits):
-        sums = exchange_sum(sums, group)
+        sums = tree(fan(sums, holder, masks_of(group)))
+        holder ^= 1
+    sample_core = holder
+    if sample_core != voxel_core:
+        chip_b = swap(chip_b)
     mate_x = swap(x)
 
-    def time_kernel(x, mate_x, moved, each):
+    def time_kernel(x, mate_x, moved, mate_moved, each):
+        moved = on_core(voxel_core, moved[...], mate_moved[...])
         for core in range(2):
             for j in range(smp_rows):
-                block = (mate_x, x)[core][pl.ds(j, vox_rows, stride=smp_rows), :]
-                each[core * smp_rows + j] = dot_rows(block, moved[...])
+                block = (x if core == sample_core else mate_x)[pl.ds(j, vox_rows, stride=smp_rows), :]
+                each[core * smp_rows + j] = dot_rows(block, moved)
 
     (each,) = call(
-        time_kernel, (near(chip_rows, times, rank),), (x, mate_x, moved_a), 4 * flat_rows * times * rank * 6
+        time_kernel,
+        (near(chip_rows, times, rank),),
+        (x, mate_x, moved_a, mate_moved_a),
+        4 * flat_rows * times * rank * 6,
     )
 
     def sample_kernel(sums, b, w, outer_c, each, gram_out, out):
@@ -257,13 +272,12 @@
         2 * rank * rank * chip_rows * 6,
     )
     mate_gram_a = swap(gram_a)
-    mate_moved_a = swap(moved_a)
 
     def scale_kernel(gram, mate_gram, moved, mate_moved, outer, result, scales_out, weighed):
-        gram = from_core_1(gram[...], mate_gram[...])
+        gram = on_core(sample_core, gram[...], mate_gram[...])
         scales = jnp.sqrt(diagonal_row(gram) / vox_total + 1e-06)
         scales_out[...] = scales
-        result[...] = from_core_1(moved[...], mate_moved[...]) / scales
+        result[...] = on_core(voxel_core, moved[...], mate_moved[...]) / scales
         weighed[...] = outer[...] * gram
 
     voxel_result, scales_a, weighed = call(
@@ -273,27 +287,31 @@
         vox_rows * rank * 8,
     )
 
-    terms, rows_b = payload[:times], payload[times:]
+    terms, rows_b, rows_core = payload[:times], payload[times:], holder
     smp_mask = sum(chip_bits)
     for group in groups_of(chip_bits + vox_bits):
-        masks = masks_of(group)[1:]
-        if any(mask & smp_mask for mask in masks):
-            packet = jnp.concatenate([terms, rows_b], axis=0)
-            parts = [exchange(packet, mask) for mask in masks]
-            terms = tree([terms] + [part[:times] for part in parts])
+        masks = masks_of(group)
+        with_rows = any(mask & smp_mask for mask in masks)
+        parts = fan(jnp.concatenate([terms, rows_b], axis=0) if with_rows else terms, holder, masks)
+        terms = tree([part[:times] for part in parts])
+        holder ^= 1
+        if with_rows:
             parts = [part for part, mask in zip(parts, masks) if not mask & ~smp_mask]
-            rows_b = jnp.concatenate([rows_b] + [part[times:] for part in parts], axis=0)
-        else:
-            terms = exchange_sum(terms, group)
+            rows_b = jnp.concatenate([part[times:] for part in parts], axis=0)
+            rows_core = holder
+    last_core = holder
     mate_rows_b = swap(rows_b)
+    terms, mate_rows_b, voxel_result, scales_a, weighed = lax.optimization_barrier(
+        (terms, mate_rows_b, voxel_result, scales_a, weighed)
+    )
     mate_terms = swap(terms)
 
     def last_kernel(terms, mate_terms, rows, mate_rows, c, w, weighed, scales_a, b_out, c_out, w_out, all_b):
-        b = in_order(from_core_1(rows[...], mate_rows[...]), all_b, chips)
+        b = in_order(on_core(rows_core, rows[...], mate_rows[...]), all_b, chips)
         coupled = weighed[...] * dot_rows(b, b)
         scales_b = jnp.sqrt(jnp.sum(b * b, axis=0, keepdims=True) / smp_total + 1e-06)
         b_out[...] = all_b[pl.ds(pl.multiple_of(smp_index() * smp_rows, smp_rows), smp_rows), :] / scales_b
-        summed = from_core_1(terms[...], mate_terms[...])
+        summed = on_core(last_core, terms[...], mate_terms[...])
         moved = c[...] - step_of(coupled) * (dot(c[...], coupled) - summed * w[...])
         scales_c = jnp.sqrt(jnp.sum(moved * moved, axis=0, keepdims=True) / times + 1e-06)
         c_out[...] = moved / scales_c

time: 56.7 us -> 35.2 us (0.62)
  starting transfers between devices: 46.3 us -> 16.1 us
  waiting for transfers between devices: 1.27 us -> 9.63 us
  local copies, waits for them, and re-layouts: 0.02 us -> 0.69 us
    ppermute x7 -> x12, starting transfers between devices: 38.9 us -> 7.48 us  [swap(): lax.ppermute(values, ALL, [(i, i ^ 1) for i in range(lax.axis_size(ALL))])]
    ppermute x11, waiting for transfers between devices: 0.03 us -> 6.64 us  [send(): return lax.ppermute(values, ALL, pairs)]
    ppermute x7 -> x12, waiting for transfers between devices: 1.24 us -> 2.99 us  [swap(): lax.ppermute(values, ALL, [(i, i ^ 1) for i in range(lax.axis_size(ALL))])]
    ppermute x11, starting transfers between devices: 7.31 us -> 8.58 us  [send(): return lax.ppermute(values, ALL, pairs)]
    slice x4 -> x5, local copies, waits for them, and re-layouts: 0.01 us -> 0.69 us  [the longest x3 0.68 us: per_device(): rows_b = jnp.concatenate([part[times:] for part in parts], axis=0)]
  transfers between devices with their start and end apart: 18 -> 23, of which waited for: 2 -> 9; matrix products, arithmetic and copies ran while one was open for 0% -> 0% of each run, Pallas kernels for 5% -> 9%
where the time goes in v8:
time: 35.2 us; the launch traced here: 35 us
  starting transfers between devices  16.1 us (46%)
  waiting for transfers between devices  9.63 us (27%)
  Pallas kernels  7.7 us (22%)
  between operations  0.81 us (2%)
  local copies, waits for them, and re-layouts  0.69 us (2%)
    ppermute x11, starting transfers between devices, send(): return lax.ppermute(values, ALL, pairs)  8.58 us
    pallas_call x7, Pallas kernels, call(): pl.pallas_call(kernel, out_shape=outs, in_specs=specs, out_specs=[pl.Bloc...  7.7 us
    ppermute x12, starting transfers between devices, swap(): lax.ppermute(values, ALL, [(i, i ^ 1) for i in range(lax.axis_size(ALL))])  7.48 us
    ppermute x11, waiting for transfers between devices, send(): return lax.ppermute(values, ALL, pairs)  6.64 us
    ppermute x12, waiting for transfers between devices, swap(): lax.ppermute(values, ALL, [(i, i ^ 1) for i in range(lax.axis_size(ALL))])  2.99 us
  transfers between devices with their start and end apart: 23, of which 9 were waited for; matrix products, arithmetic and copies ran while one was open for 0% of the time, Pallas kernels for 9%

profile of v8, /device:TPU:0, one launch (start us, length us, event | category | flops | bytes accessed | tf_op | source)
XLA Modules:
  0.0 35.0 jit_solution(2783426125904832921)
XLA Ops:
  0.6 3.1 %shard_map.84 = (f32[1024,128]{1,0:T(8,128)S(1)}, f32[128,128]{1,0:T(8,128)S(1)}, f32[128,128]{1,0:T(8,128)S(1)}, f32[1,128]{1,0:T(1,128)S(1)}, f32[136,128]{1,0:T(8,128)S(1)}, /*index=5*/f32[8,128,128]{2,1,0:T(8,128)S(1)}) custom-call(f32[1024,128]{1,0:T(8,128)} %bitcast.3, f32[128,128]{1,0:T(8,128)} %c_hbm.1, f32[8,128]{1,0:T(8,128)} %b_hbm.1, ...), custom_call_target="tpu_custom_call" | custom-call | flops 201326592 | bytes 65536 | tf_op jit(solution)/shard_map/pallas_call | solution.py:37
  3.8 0.5 %collective-permute-start = (f32[136,128]{1,0:T(8,128)S(1)}, f32[136,128]{1,0:T(8,128)S(1)}, u32[]{:S(2)}, u32[]{:S(2)}) collective-permute-start(f32[136,128]{1,0:T(8,128)S(1)} %get-tuple-element.28), channel_id=1, source_target_pairs={{0,1},{1,0},{2,3},{3,2},{4,5},{5,4},{6,7},{7,6},{8,9},{9,8},{10,11... | collective-permute-start | bytes 208904 | tf_op jit(solution)/shard_map/ppermute | solution.py:74
  4.3 0.1 collective-permute-start.3
  4.4 0.8 %collective-permute-done = f32[136,128]{1,0:T(8,128)S(1)} collective-permute-done((f32[136,128]{1,0:T(8,128)S(1)}, f32[136,128]{1,0:T(8,128)S(1)}, u32[]{:S(2)}, u32[]{:S(2)}) %collective-permute-start) | collective-permute-done | bytes 69664 | tf_op jit(solution)/shard_map/ppermute | solution.py:74
  5.2 0.4 %collective-permute-start.2 = (f32[144,128]{1,0:T(8,128)S(1)}, f32[144,128]{1,0:T(8,128)S(1)}, u32[]{:S(2)}, u32[]{:S(2)}) collective-permute-start(f32[144,128]{1,0:T(8,128)S(1)} %pad_maximum_fusion), channel_id=1, source_target_pairs={{0,1},{1,2},{2,3},{3,0},{4,5},{5,6},{6,7},{7,4},{8,9},{9,10},{10,1... | collective-permute-start | bytes 221192 | tf_op jit(solution)/shard_map/ppermute | solution.py:80
  5.6 2.6 %collective-permute-start.1 = (f32[144,128]{1,0:T(8,128)S(1)}, f32[144,128]{1,0:T(8,128)S(1)}, u32[]{:S(2)}, u32[]{:S(2)}) collective-permute-start(f32[144,128]{1,0:T(8,128)S(1)} %pad_maximum_fusion), channel_id=1, source_target_pairs={{0,1},{1,0},{2,3},{3,2},{4,5},{5,4},{6,7},{7,6},{8,9},{9,8},{10,11... | collective-permute-start | bytes 221192 | tf_op jit(solution)/shard_map/ppermute | solution.py:74
  8.3 0.0 collective-permute-start.10
  8.3 0.3 shard_map.85
  8.6 1.3 %collective-permute-done.2 = f32[144,128]{1,0:T(8,128)S(1)} collective-permute-done((f32[144,128]{1,0:T(8,128)S(1)}, f32[144,128]{1,0:T(8,128)S(1)}, u32[]{:S(2)}, u32[]{:S(2)}) %collective-permute-start.2) | collective-permute-done | bytes 73760 | tf_op jit(solution)/shard_map/ppermute | solution.py:80
  10.0 0.0 collective-permute-done.1
  10.0 0.0 collective-permute-done.3.mate_con
  10.0 0.9 %shard_map.86 = (f32[128,128]{1,0:T(8,128)S(1)}, f32[16,128]{1,0:T(8,128)S(1)}, f32[88,128]{1,0:T(8,128)S(1)}) custom-call(f32[128,128]{1,0:T(8,128)S(1)} %slice_add_fusion.2.terms, f32[32,128]{1,0:T(8,128)S(1)} %pad_maximum_fusion.1.rows, f32[128,128]{1,0:T(8,128)S(1)} %get-tuple-element.29.a, f32[1,128]{1,0:T(1,128)S(1)} %get-tuple-element.30.w, ...), custom_call_target="tpu_custom_call" | custom-call | flops 50331648 | bytes 65536 | tf_op jit(solution)/shard_map/pallas_call | solution.py:37
  10.9 1.9 %collective-permute-start.7 = (f32[88,128]{1,0:T(8,128)S(1)}, f32[88,128]{1,0:T(8,128)S(1)}, u32[]{:S(2)}, u32[]{:S(2)}) collective-permute-start(f32[88,128]{1,0:T(8,128)S(1)} %get-tuple-element.34), channel_id=1, source_target_pairs={{0,13},{1,0},{2,15},{3,2},{4,9},{5,4},{6,11},{7,6},{8,5},{9,8},{10... | collective-permute-start | bytes 135176 | tf_op jit(solution)/shard_map/ppermute | solution.py:80
  12.8 0.3 collective-permute-start.6
  13.1 0.3 collective-permute-start.5
  13.5 0.2 collective-permute-start.4
  13.6 0.9 %collective-permute-done.7 = f32[88,128]{1,0:T(8,128)S(1)} collective-permute-done((f32[88,128]{1,0:T(8,128)S(1)}, f32[88,128]{1,0:T(8,128)S(1)}, u32[]{:S(2)}, u32[]{:S(2)}) %collective-permute-start.7) | collective-permute-done | bytes 45088 | tf_op jit(solution)/shard_map/ppermute | solution.py:80
  14.5 1.3 %collective-permute-start.11 = (f32[128,128]{1,0:T(8,128)S(1)}, f32[128,128]{1,0:T(8,128)S(1)}, u32[]{:S(2)}, u32[]{:S(2)}) collective-permute-start(f32[128,128]{1,0:T(8,128)S(1)} %get-tuple-element.37.moved), channel_id=1, source_target_pairs={{0,1},{1,0},{2,3},{3,2},{4,5},{5,4},{6,7},{7,6},{8,9},{9,8},{10,11... | collective-permute-start | bytes 196616 | tf_op jit(solution)/shard_map/ppermute | solution.py:74
  15.8 0.0 collective-permute-done.6
  15.8 1.0 %collective-permute-start.9 = (f32[88,128]{1,0:T(8,128)S(1)}, f32[88,128]{1,0:T(8,128)S(1)}, u32[]{:S(2)}, u32[]{:S(2)}) collective-permute-start(f32[88,128]{1,0:T(8,128)S(1)} %add_add_fusion.1), channel_id=1, source_target_pairs={{0,1},{1,16},{2,3},{3,18},{4,5},{5,20},{6,7},{7,22},{8,9},{9,24},{... | collective-permute-start | bytes 135176 | tf_op jit(solution)/shard_map/ppermute | solution.py:80
  16.9 1.7 %collective-permute-start.8 = (f32[88,128]{1,0:T(8,128)S(1)}, f32[88,128]{1,0:T(8,128)S(1)}, u32[]{:S(2)}, u32[]{:S(2)}) collective-permute-start(f32[88,128]{1,0:T(8,128)S(1)} %add_add_fusion.1), channel_id=1, source_target_pairs={{0,1},{1,0},{2,3},{3,2},{4,5},{5,4},{6,7},{7,6},{8,9},{9,8},{10,11... | collective-permute-start | bytes 135176 | tf_op jit(solution)/shard_map/ppermute | solution.py:74
  18.6 0.0 collective-permute-done.11.mate_moved
  18.6 1.1 %shard_map.87.each = f32[16,128,128]{2,1,0:T(8,128)S(1)} custom-call(f32[1024,128]{1,0:T(8,128)S(1)} %get-tuple-element.36.x, f32[1024,128]{1,0:T(8,128)S(1)} %collective-permute-done.10.mate_x, f32[128,128]{1,0:T(8,128)S(1)} %get-tuple-element.37.moved, f32[128,128]{1,0:T(8,128)S(1)} %collective-permute-done.11.mate_moved), custom_call_target="tpu_custom_call" | custom-call | flops 402653184 | bytes 65536 | tf_op jit(solution)/shard_map/pallas_call | solution.py:37
  19.7 1.5 %collective-permute-done.9 = f32[88,128]{1,0:T(8,128)S(1)} collective-permute-done((f32[88,128]{1,0:T(8,128)S(1)}, f32[88,128]{1,0:T(8,128)S(1)}, u32[]{:S(2)}, u32[]{:S(2)}) %collective-permute-start.9) | collective-permute-done | bytes 45088 | tf_op jit(solution)/shard_map/ppermute | solution.py:80
  21.2 0.4 %shard_map.88 = (f32[128,128]{1,0:T(8,128)S(1)}, f32[144,128]{1,0:T(8,128)S(1)}) custom-call(f32[88,128]{1,0:T(8,128)S(1)} %add.41.sums, f32[16,128]{1,0:T(8,128)S(1)} %get-tuple-element.35.b, f32[1,128]{1,0:T(1,128)S(1)} %get-tuple-element.30.w, f32[128,128]{1,0:T(8,128)S(1)} %get-tuple-element.32.outer_c, f32[16,128,128]{2,1,0:T(8,128)S(1)} %shard_map.87.each), custom_call_target="tpu_custom_call" | custom-call | flops 3145728 | bytes 65536 | tf_op jit(solution)/shard_map/pallas_call | solution.py:37
  21.5 0.1 collective-permute-start.15
  21.6 0.3 collective-permute-start.14
  21.9 1.2 %collective-permute-start.13 = (f32[144,128]{1,0:T(8,128)S(1)}, f32[144,128]{1,0:T(8,128)S(1)}, u32[]{:S(2)}, u32[]{:S(2)}) collective-permute-start(f32[144,128]{1,0:T(8,128)S(1)} %get-tuple-element.38), channel_id=1, source_target_pairs={{0,3},{1,0},{2,1},{3,2},{4,7},{5,4},{6,5},{7,6},{8,11},{9,8},{10,9... | collective-permute-start | bytes 221192 | tf_op jit(solution)/shard_map/ppermute | solution.py:80
  23.1 0.0 collective-permute-start.12
  23.1 0.5 %collective-permute-start.21 = (f32[128,128]{1,0:T(8,128)S(1)}, f32[128,128]{1,0:T(8,128)S(1)}, u32[]{:S(2)}, u32[]{:S(2)}) collective-permute-start(f32[128,128]{1,0:T(8,128)S(1)} %get-tuple-element.39.gram), channel_id=1, source_target_pairs={{0,1},{1,0},{2,3},{3,2},{4,5},{5,4},{6,7},{7,6},{8,9},{9,8},{10,11... | collective-permute-start | bytes 196616 | tf_op jit(solution)/shard_map/ppermute | solution.py:74
  23.6 0.9 %collective-permute-done.21.mate_gram = f32[128,128]{1,0:T(8,128)S(1)} collective-permute-done((f32[128,128]{1,0:T(8,128)S(1)}, f32[128,128]{1,0:T(8,128)S(1)}, u32[]{:S(2)}, u32[]{:S(2)}) %collective-permute-start.21) | collective-permute-done | bytes 65568 | tf_op jit(solution)/shard_map/ppermute | solution.py:74
  24.5 0.7 %shard_map.89 = (f32[128,128]{1,0:T(8,128)}, f32[1,128]{1,0:T(1,128)S(1)}, f32[128,128]{1,0:T(8,128)S(1)}) custom-call(f32[128,128]{1,0:T(8,128)S(1)} %get-tuple-element.39.gram, f32[128,128]{1,0:T(8,128)S(1)} %collective-permute-done.21.mate_gram, f32[128,128]{1,0:T(8,128)S(1)} %get-tuple-element.37.moved, ...), custom_call_target="tpu_custom_call" | custom-call | flops 131072 | bytes 65536 | tf_op jit(solution)/shard_map/pallas_call | solution.py:37
  25.2 0.0 collective-permute-done.13
  25.2 0.0 collective-permute-done.12
  25.2 0.8 %collective-permute-start.19 = (f32[128,128]{1,0:T(8,128)S(1)}, f32[128,128]{1,0:T(8,128)S(1)}, u32[]{:S(2)}, u32[]{:S(2)}) collective-permute-start(f32[128,128]{1,0:T(8,128)S(1)} %fusion), channel_id=1, source_target_pairs={{0,1},{1,24},{2,3},{3,26},{4,5},{5,28},{6,7},{7,30},{8,9},{9,16},{... | collective-permute-start | bytes 196616 | tf_op jit(solution)/shard_map/ppermute | solution.py:80
  26.0 2.3 %collective-permute-start.18 = (f32[128,128]{1,0:T(8,128)S(1)}, f32[128,128]{1,0:T(8,128)S(1)}, u32[]{:S(2)}, u32[]{:S(2)}) collective-permute-start(f32[128,128]{1,0:T(8,128)S(1)} %fusion), channel_id=1, source_target_pairs={{0,1},{1,16},{2,3},{3,18},{4,5},{5,20},{6,7},{7,22},{8,9},{9,24},{... | collective-permute-start | bytes 196616 | tf_op jit(solution)/shard_map/ppermute | solution.py:80
  28.3 0.0 collective-permute-start.17
  28.3 0.0 collective-permute-start.16
  28.3 0.0 slice-start
  28.3 0.7 %slice-done = f32[16,128]{1,0:T(8,128)S(1)} async-done(((f32[144,128]{1,0:T(8,128)}), f32[16,128]{1,0:T(8,128)S(1)}, s32[]{:S(2)}) %slice-start) | async-done | bytes 8216 | tf_op jit(solution)/shard_map/slice | solution.py:300
  29.0 0.5 %collective-permute-start.20 = (f32[32,128]{1,0:T(8,128)S(1)}, f32[32,128]{1,0:T(8,128)S(1)}, u32[]{:S(2)}, u32[]{:S(2)}) collective-permute-start(f32[32,128]{1,0:T(8,128)S(1)} %pad_maximum_fusion.2.rows), channel_id=1, source_target_pairs={{0,1},{1,0},{2,3},{3,2},{4,5},{5,4},{6,7},{7,6},{8,9},{9,8},{10,11... | collective-permute-start | bytes 49160 | tf_op jit(solution)/shard_map/ppermute | solution.py:74
  29.5 1.4 %collective-permute-done.19 = f32[128,128]{1,0:T(8,128)S(1)} collective-permute-done((f32[128,128]{1,0:T(8,128)S(1)}, f32[128,128]{1,0:T(8,128)S(1)}, u32[]{:S(2)}, u32[]{:S(2)}) %collective-permute-start.19) | collective-permute-done | bytes 65568 | tf_op jit(solution)/shard_map/ppermute | solution.py:80
  30.9 1.3 %collective-permute-done.18 = f32[128,128]{1,0:T(8,128)S(1)} collective-permute-done((f32[128,128]{1,0:T(8,128)S(1)}, f32[128,128]{1,0:T(8,128)S(1)}, u32[]{:S(2)}, u32[]{:S(2)}) %collective-permute-start.18) | collective-permute-done | bytes 65568 | tf_op jit(solution)/shard_map/ppermute | solution.py:80
  32.1 0.3 collective-permute-done.17
  32.5 0.0 collective-permute-done.20.mate_rows
  32.5 0.1 collective-permute-start.22
  32.6 1.2 %collective-permute-done.22.mate_terms = f32[128,128]{1,0:T(8,128)S(1)} collective-permute-done((f32[128,128]{1,0:T(8,128)S(1)}, f32[128,128]{1,0:T(8,128)S(1)}, u32[]{:S(2)}, u32[]{:S(2)}) %collective-permute-start.22) | collective-permute-done | bytes 65568 | tf_op jit(solution)/shard_map/ppermute | solution.py:74
  33.8 1.2 %shard_map.90 = (f32[8,128]{1,0:T(8,128)}, f32[128,128]{1,0:T(8,128)}, f32[1,128]{1,0:T(1,128)}) custom-call(f32[128,128]{1,0:T(8,128)S(1)} %add_add_fusion.terms, f32[128,128]{1,0:T(8,128)S(1)} %collective-permute-done.22.mate_terms, f32[32,128]{1,0:T(8,128)S(1)} %pad_maximum_fusion.2.rows, f32[32,128]{1,0:T(8,128)S(1)} %collective-permute-done.20.mate_rows, ...), custom_call_target="tpu_custom_call" | custom-call | flops 25165824 | bytes 65536 | tf_op jit(solution)/shard_map/pallas_call | solution.py:37
  (23 shorter events, 0.1 us)
Async XLA Ops:
  3.8 1.4 %collective-permute-start = (f32[136,128]{1,0:T(8,128)S(1)}, f32[136,128]{1,0:T(8,128)S(1)}, u32[]{:S(2)}, u32[]{:S(2)}) collective-permute-start(f32[136,128]{1,0:T(8,128)S(1)} %get-tuple-element.28), channel_id=1, source_target_pairs={{0,1},{1,0},{2,3},{3,2},{4,5},{5,4},{6,7},{7,6},{8,9},{9,8},{10,11... | collective-permute-start | bytes 208904 | tf_op jit(solution)/shard_map/ppermute | solution.py:74
  4.3 5.7 %collective-permute-start.3 = (f32[8,128,128]{2,1,0:T(8,128)S(1)}, f32[8,128,128]{2,1,0:T(8,128)S(1)}, u32[]{:S(2)}, u32[]{:S(2)}) collective-permute-start(f32[8,128,128]{2,1,0:T(8,128)S(1)} %get-tuple-element.33.con), channel_id=1, source_target_pairs={{0,1},{1,0},{2,3},{3,2},{4,5},{5,4},{6,7},{7,6},{8,9},{9,8},{10,11... | collective-permute-start | bytes 1572872 | tf_op jit(solution)/shard_map/ppermute | solution.py:74
  5.2 4.7 %collective-permute-start.2 = (f32[144,128]{1,0:T(8,128)S(1)}, f32[144,128]{1,0:T(8,128)S(1)}, u32[]{:S(2)}, u32[]{:S(2)}) collective-permute-start(f32[144,128]{1,0:T(8,128)S(1)} %pad_maximum_fusion), channel_id=1, source_target_pairs={{0,1},{1,2},{2,3},{3,0},{4,5},{5,6},{6,7},{7,4},{8,9},{9,10},{10,1... | collective-permute-start | bytes 221192 | tf_op jit(solution)/shard_map/ppermute | solution.py:80
  5.6 4.3 %collective-permute-start.1 = (f32[144,128]{1,0:T(8,128)S(1)}, f32[144,128]{1,0:T(8,128)S(1)}, u32[]{:S(2)}, u32[]{:S(2)}) collective-permute-start(f32[144,128]{1,0:T(8,128)S(1)} %pad_maximum_fusion), channel_id=1, source_target_pairs={{0,1},{1,0},{2,3},{3,2},{4,5},{5,4},{6,7},{7,6},{8,9},{9,8},{10,11... | collective-permute-start | bytes 221192 | tf_op jit(solution)/shard_map/ppermute | solution.py:74
  8.3 10.3 %collective-permute-start.10 = (f32[1024,128]{1,0:T(8,128)S(1)}, f32[1024,128]{1,0:T(8,128)S(1)}, u32[]{:S(2)}, u32[]{:S(2)}) collective-permute-start(f32[1024,128]{1,0:T(8,128)S(1)} %get-tuple-element.36.x), channel_id=1, source_target_pairs={{0,1},{1,0},{2,3},{3,2},{4,5},{5,4},{6,7},{7,6},{8,9},{9,8},{10,11... | collective-permute-start | bytes 1572872 | tf_op jit(solution)/shard_map/ppermute | solution.py:74
  10.9 3.6 %collective-permute-start.7 = (f32[88,128]{1,0:T(8,128)S(1)}, f32[88,128]{1,0:T(8,128)S(1)}, u32[]{:S(2)}, u32[]{:S(2)}) collective-permute-start(f32[88,128]{1,0:T(8,128)S(1)} %get-tuple-element.34), channel_id=1, source_target_pairs={{0,13},{1,0},{2,15},{3,2},{4,9},{5,4},{6,11},{7,6},{8,5},{9,8},{10... | collective-permute-start | bytes 135176 | tf_op jit(solution)/shard_map/ppermute | solution.py:80
  12.8 3.0 %collective-permute-start.6 = (f32[88,128]{1,0:T(8,128)S(1)}, f32[88,128]{1,0:T(8,128)S(1)}, u32[]{:S(2)}, u32[]{:S(2)}) collective-permute-start(f32[88,128]{1,0:T(8,128)S(1)} %get-tuple-element.34), channel_id=1, source_target_pairs={{0,9},{1,0},{2,11},{3,2},{4,13},{5,4},{6,15},{7,6},{8,1},{9,8},{10... | collective-permute-start | bytes 135176 | tf_op jit(solution)/shard_map/ppermute | solution.py:80
  13.1 2.7 %collective-permute-start.5 = (f32[88,128]{1,0:T(8,128)S(1)}, f32[88,128]{1,0:T(8,128)S(1)}, u32[]{:S(2)}, u32[]{:S(2)}) collective-permute-start(f32[88,128]{1,0:T(8,128)S(1)} %get-tuple-element.34), channel_id=1, source_target_pairs={{0,5},{1,0},{2,7},{3,2},{4,1},{5,4},{6,3},{7,6},{8,13},{9,8},{10,1... | collective-permute-start | bytes 135176 | tf_op jit(solution)/shard_map/ppermute | solution.py:80
  13.5 2.3 %collective-permute-start.4 = (f32[88,128]{1,0:T(8,128)S(1)}, f32[88,128]{1,0:T(8,128)S(1)}, u32[]{:S(2)}, u32[]{:S(2)}) collective-permute-start(f32[88,128]{1,0:T(8,128)S(1)} %get-tuple-element.34), channel_id=1, source_target_pairs={{0,1},{1,0},{2,3},{3,2},{4,5},{5,4},{6,7},{7,6},{8,9},{9,8},{10,11... | collective-permute-start | bytes 135176 | tf_op jit(solution)/shard_map/ppermute | solution.py:74
  14.5 4.1 %collective-permute-start.11 = (f32[128,128]{1,0:T(8,128)S(1)}, f32[128,128]{1,0:T(8,128)S(1)}, u32[]{:S(2)}, u32[]{:S(2)}) collective-permute-start(f32[128,128]{1,0:T(8,128)S(1)} %get-tuple-element.37.moved), channel_id=1, source_target_pairs={{0,1},{1,0},{2,3},{3,2},{4,5},{5,4},{6,7},{7,6},{8,9},{9,8},{10,11... | collective-permute-start | bytes 196616 | tf_op jit(solution)/shard_map/ppermute | solution.py:74
  15.8 5.3 %collective-permute-start.9 = (f32[88,128]{1,0:T(8,128)S(1)}, f32[88,128]{1,0:T(8,128)S(1)}, u32[]{:S(2)}, u32[]{:S(2)}) collective-permute-start(f32[88,128]{1,0:T(8,128)S(1)} %add_add_fusion.1), channel_id=1, source_target_pairs={{0,1},{1,16},{2,3},{3,18},{4,5},{5,20},{6,7},{7,22},{8,9},{9,24},{... | collective-permute-start | bytes 135176 | tf_op jit(solution)/shard_map/ppermute | solution.py:80
  16.9 4.3 %collective-permute-start.8 = (f32[88,128]{1,0:T(8,128)S(1)}, f32[88,128]{1,0:T(8,128)S(1)}, u32[]{:S(2)}, u32[]{:S(2)}) collective-permute-start(f32[88,128]{1,0:T(8,128)S(1)} %add_add_fusion.1), channel_id=1, source_target_pairs={{0,1},{1,0},{2,3},{3,2},{4,5},{5,4},{6,7},{7,6},{8,9},{9,8},{10,11... | collective-permute-start | bytes 135176 | tf_op jit(solution)/shard_map/ppermute | solution.py:74
  21.5 3.6 %collective-permute-start.15 = (f32[144,128]{1,0:T(8,128)S(1)}, f32[144,128]{1,0:T(8,128)S(1)}, u32[]{:S(2)}, u32[]{:S(2)}) collective-permute-start(f32[144,128]{1,0:T(8,128)S(1)} %get-tuple-element.38), channel_id=1, source_target_pairs={{0,7},{1,0},{2,5},{3,2},{4,3},{5,4},{6,1},{7,6},{8,15},{9,8},{10,1... | collective-permute-start | bytes 221192 | tf_op jit(solution)/shard_map/ppermute | solution.py:80
  21.6 3.6 %collective-permute-start.14 = (f32[144,128]{1,0:T(8,128)S(1)}, f32[144,128]{1,0:T(8,128)S(1)}, u32[]{:S(2)}, u32[]{:S(2)}) collective-permute-start(f32[144,128]{1,0:T(8,128)S(1)} %get-tuple-element.38), channel_id=1, source_target_pairs={{0,5},{1,0},{2,7},{3,2},{4,1},{5,4},{6,3},{7,6},{8,13},{9,8},{10,1... | collective-permute-start | bytes 221192 | tf_op jit(solution)/shard_map/ppermute | solution.py:80
  21.9 3.3 %collective-permute-start.13 = (f32[144,128]{1,0:T(8,128)S(1)}, f32[144,128]{1,0:T(8,128)S(1)}, u32[]{:S(2)}, u32[]{:S(2)}) collective-permute-start(f32[144,128]{1,0:T(8,128)S(1)} %get-tuple-element.38), channel_id=1, source_target_pairs={{0,3},{1,0},{2,1},{3,2},{4,7},{5,4},{6,5},{7,6},{8,11},{9,8},{10,9... | collective-permute-start | bytes 221192 | tf_op jit(solution)/shard_map/ppermute | solution.py:80
  23.1 2.1 %collective-permute-start.12 = (f32[144,128]{1,0:T(8,128)S(1)}, f32[144,128]{1,0:T(8,128)S(1)}, u32[]{:S(2)}, u32[]{:S(2)}) collective-permute-start(f32[144,128]{1,0:T(8,128)S(1)} %get-tuple-element.38), channel_id=1, source_target_pairs={{0,1},{1,0},{2,3},{3,2},{4,5},{5,4},{6,7},{7,6},{8,9},{9,8},{10,11... | collective-permute-start | bytes 221192 | tf_op jit(solution)/shard_map/ppermute | solution.py:74
  23.1 1.4 %collective-permute-start.21 = (f32[128,128]{1,0:T(8,128)S(1)}, f32[128,128]{1,0:T(8,128)S(1)}, u32[]{:S(2)}, u32[]{:S(2)}) collective-permute-start(f32[128,128]{1,0:T(8,128)S(1)} %get-tuple-element.39.gram), channel_id=1, source_target_pairs={{0,1},{1,0},{2,3},{3,2},{4,5},{5,4},{6,7},{7,6},{8,9},{9,8},{10,11... | collective-permute-start | bytes 196616 | tf_op jit(solution)/shard_map/ppermute | solution.py:74
  25.2 3.1 %copy-start = (f32[144,128]{1,0:T(8,128)}, f32[144,128]{1,0:T(8,128)S(1)}, u32[]{:S(2)}) copy-start(f32[144,128]{1,0:T(8,128)S(1)} %collective-permute-done.13) | copy-start | bytes 221188
  25.2 5.6 %collective-permute-start.19 = (f32[128,128]{1,0:T(8,128)S(1)}, f32[128,128]{1,0:T(8,128)S(1)}, u32[]{:S(2)}, u32[]{:S(2)}) collective-permute-start(f32[128,128]{1,0:T(8,128)S(1)} %fusion), channel_id=1, source_target_pairs={{0,1},{1,24},{2,3},{3,26},{4,5},{5,28},{6,7},{7,30},{8,9},{9,16},{... | collective-permute-start | bytes 196616 | tf_op jit(solution)/shard_map/ppermute | solution.py:80
  26.0 6.1 %collective-permute-start.18 = (f32[128,128]{1,0:T(8,128)S(1)}, f32[128,128]{1,0:T(8,128)S(1)}, u32[]{:S(2)}, u32[]{:S(2)}) collective-permute-start(f32[128,128]{1,0:T(8,128)S(1)} %fusion), channel_id=1, source_target_pairs={{0,1},{1,16},{2,3},{3,18},{4,5},{5,20},{6,7},{7,22},{8,9},{9,24},{... | collective-permute-start | bytes 196616 | tf_op jit(solution)/shard_map/ppermute | solution.py:80
  28.3 4.1 %collective-permute-start.17 = (f32[128,128]{1,0:T(8,128)S(1)}, f32[128,128]{1,0:T(8,128)S(1)}, u32[]{:S(2)}, u32[]{:S(2)}) collective-permute-start(f32[128,128]{1,0:T(8,128)S(1)} %fusion), channel_id=1, source_target_pairs={{0,1},{1,8},{2,3},{3,10},{4,5},{5,12},{6,7},{7,14},{8,9},{9,0},{10... | collective-permute-start | bytes 196616 | tf_op jit(solution)/shard_map/ppermute | solution.py:80
  28.3 4.1 %collective-permute-start.16 = (f32[128,128]{1,0:T(8,128)S(1)}, f32[128,128]{1,0:T(8,128)S(1)}, u32[]{:S(2)}, u32[]{:S(2)}) collective-permute-start(f32[128,128]{1,0:T(8,128)S(1)} %fusion), channel_id=1, source_target_pairs={{0,1},{1,0},{2,3},{3,2},{4,5},{5,4},{6,7},{7,6},{8,9},{9,8},{10,11... | collective-permute-start | bytes 196616 | tf_op jit(solution)/shard_map/ppermute | solution.py:74
  28.3 0.7 %slice-start = ((f32[144,128]{1,0:T(8,128)}), f32[16,128]{1,0:T(8,128)S(1)}, s32[]{:S(2)}) async-start(f32[144,128]{1,0:T(8,128)} %copy-done), calls=%async_computation | async-start | bytes 16384 | tf_op jit(solution)/shard_map/slice | solution.py:300
  29.0 3.4 %collective-permute-start.20 = (f32[32,128]{1,0:T(8,128)S(1)}, f32[32,128]{1,0:T(8,128)S(1)}, u32[]{:S(2)}, u32[]{:S(2)}) collective-permute-start(f32[32,128]{1,0:T(8,128)S(1)} %pad_maximum_fusion.2.rows), channel_id=1, source_target_pairs={{0,1},{1,0},{2,3},{3,2},{4,5},{5,4},{6,7},{7,6},{8,9},{9,8},{10,11... | collective-permute-start | bytes 49160 | tf_op jit(solution)/shard_map/ppermute | solution.py:74
  32.5 1.3 %collective-permute-start.22 = (f32[128,128]{1,0:T(8,128)S(1)}, f32[128,128]{1,0:T(8,128)S(1)}, u32[]{:S(2)}, u32[]{:S(2)}) collective-permute-start(f32[128,128]{1,0:T(8,128)S(1)} %add_add_fusion.terms), channel_id=1, source_target_pairs={{0,1},{1,0},{2,3},{3,2},{4,5},{5,4},{6,7},{7,6},{8,9},{9,8},{10,11... | collective-permute-start | bytes 196616 | tf_op jit(solution)/shard_map/ppermute | solution.py:74

commit v9 on v8

--- a/solution.py
+++ b/solution.py
@@ -5,18 +5,33 @@
 from jax.experimental.pallas import tpu as pltpu
 from jax.sharding import PartitionSpec as P
 
-HIGH = lax.Precision.HIGHEST
 F32 = jnp.float32
+BF16 = jnp.bfloat16
 VMEM_LIMIT = 12 * 1024 * 1024
 ALL = ("vox", "smp")
 
 
+def halves(a, axis):
+    high = a.astype(BF16)
+    return jnp.concatenate([high, (a - high.astype(F32)).astype(BF16)], axis=axis)
+
+
+def both(b):
+    parts = halves(b, 1)
+    return jnp.concatenate([parts, parts], axis=0)
+
+
+def fold(product):
+    width = product.shape[1] // 2
+    return product[:, :width] + product[:, width:]
+
+
 def dot(a, b):
-    return jnp.dot(a, b, precision=HIGH, preferred_element_type=F32)
+    return fold(jnp.dot(halves(a, 1), both(b), preferred_element_type=F32))
 
 
 def dot_rows(a, b):
-    return lax.dot_general(a, b, (((0,), (0,)), ((), ())), precision=HIGH, preferred_element_type=F32)
+    return fold(lax.dot_general(halves(a, 0), both(b), (((0,), (0,)), ((), ())), preferred_element_type=F32))
 
 
 def step_of(coupled):
@@ -153,18 +168,18 @@
             copy.start()
         copies[0].wait()
         copies[1].wait()
-        factor = c[...]
+        factor = both(c[...])
         b = out[pl.ds(vox_rows, smp_rows), :]
         for n in range(chunks):
             copies[2 + n].wait()
-            total = None
             rows = pl.ds(n * chunk_vox, chunk_vox)
-            for j in range(smp_rows):
-                block = x[pl.ds(n * chunk_rows + j, chunk_vox, stride=smp_rows), :]
-                made = dot(block, factor)
-                con[j, rows, :] = made
-                made = made * b[j : j + 1, :]
-                total = made if total is None else total + made
+            blocks = [x[pl.ds(n * chunk_rows + j, chunk_vox, stride=smp_rows), :] for j in range(smp_rows)]
+            blocks = jnp.concatenate([halves(block, 1) for block in blocks], axis=0)
+            made = fold(jnp.dot(blocks, factor, preferred_element_type=F32)).reshape(smp_rows, chunk_vox, rank)
+            con[:, rows, :] = made
+            total = made[0] * b[:1, :]
+            for j in range(1, smp_rows):
+                total = total + made[j] * b[j : j + 1, :]
             out[rows, :] = total
         copies[2 + chunks].wait()
         copies[3 + chunks].wait()
@@ -301,28 +316,40 @@
             rows_core = holder
     last_core = holder
     mate_rows_b = swap(rows_b)
-    terms, mate_rows_b, voxel_result, scales_a, weighed = lax.optimization_barrier(
-        (terms, mate_rows_b, voxel_result, scales_a, weighed)
-    )
-    mate_terms = swap(terms)
-
-    def last_kernel(terms, mate_terms, rows, mate_rows, c, w, weighed, scales_a, b_out, c_out, w_out, all_b):
+
+    def ready_kernel(rows, mate_rows, c, w, weighed, scales_a, b_out, base, gain, scale, all_b):
         b = in_order(on_core(rows_core, rows[...], mate_rows[...]), all_b, chips)
         coupled = weighed[...] * dot_rows(b, b)
+        step = step_of(coupled)
+        base[...] = c[...] - step * dot(c[...], coupled)
+        gain[...] = step * w[...]
         scales_b = jnp.sqrt(jnp.sum(b * b, axis=0, keepdims=True) / smp_total + 1e-06)
+        scale[...] = w[...] * scales_a[...] * scales_b
         b_out[...] = all_b[pl.ds(pl.multiple_of(smp_index() * smp_rows, smp_rows), smp_rows), :] / scales_b
-        summed = on_core(last_core, terms[...], mate_terms[...])
-        moved = c[...] - step_of(coupled) * (dot(c[...], coupled) - summed * w[...])
+
+    sample_result, base, gain, scale = call(
+        ready_kernel,
+        (far(smp_rows, rank), near(times, rank), near(1, rank), near(1, rank)),
+        (rows_b, mate_rows_b, c_near, w_row, weighed, scales_a),
+        2 * rank * rank * times * 4,
+        scratch=(near(smp_total, rank),),
+    )
+    terms, base, gain, scale, voxel_result, sample_result = lax.optimization_barrier(
+        (terms, base, gain, scale, voxel_result, sample_result)
+    )
+    mate_terms = swap(terms)
+
+    def last_kernel(terms, mate_terms, base, gain, scale, c_out, w_out):
+        moved = base[...] + on_core(last_core, terms[...], mate_terms[...]) * gain[...]
         scales_c = jnp.sqrt(jnp.sum(moved * moved, axis=0, keepdims=True) / times + 1e-06)
         c_out[...] = moved / scales_c
-        w_out[...] = w[...] * scales_a[...] * scales_b * scales_c
-
-    sample_result, time_result, scale_result = call(
+        w_out[...] = scale[...] * scales_c
+
+    time_result, scale_result = call(
         last_kernel,
-        (far(smp_rows, rank), far(times, rank), far(1, rank)),
-        (terms, mate_terms, rows_b, mate_rows_b, c_near, w_row, weighed, scales_a),
-        2 * rank * rank * times * 6,
-        scratch=(near(smp_total, rank),),
+        (far(times, rank), far(1, rank)),
+        (terms, mate_terms, base, gain, scale),
+        rank * times * 8,
     )
     return voxel_result, sample_result, time_result, scale_result.reshape(rank)
 

time: 35.2 us -> 32.9 us (0.935)
  Pallas kernels: 7.7 us -> 5.93 us
    pallas_call x7 -> x8, Pallas kernels: 7.7 us -> 5.93 us  [call(): pl.pallas_call(kernel, out_shape=outs, in_specs=specs, out_specs=[pl.Bloc...]
    ppermute x12, waiting for transfers between devices: 2.99 us -> 2.25 us  [swap(): lax.ppermute(values, ALL, [(i, i ^ 1) for i in range(lax.axis_size(ALL))])]
    ppermute x11, waiting for transfers between devices: 6.64 us -> 7.16 us  [send(): return lax.ppermute(values, ALL, pairs)]
where the time goes in v9:
time: 32.9 us; the launch traced here: 32.7 us
  starting transfers between devices  15.8 us (48%)
  waiting for transfers between devices  9.41 us (29%)
  Pallas kernels  5.93 us (18%)
  between operations  0.76 us (2%)
  local copies, waits for them, and re-layouts  0.7 us (2%)
    ppermute x11, starting transfers between devices, send(): return lax.ppermute(values, ALL, pairs)  8.32 us
    ppermute x12, starting transfers between devices, swap(): lax.ppermute(values, ALL, [(i, i ^ 1) for i in range(lax.axis_size(ALL))])  7.48 us
    ppermute x11, waiting for transfers between devices, send(): return lax.ppermute(values, ALL, pairs)  7.16 us
    pallas_call x8, Pallas kernels, call(): pl.pallas_call(kernel, out_shape=outs, in_specs=specs, out_specs=[pl.Bloc...  5.93 us
    ppermute x12, waiting for transfers between devices, swap(): lax.ppermute(values, ALL, [(i, i ^ 1) for i in range(lax.axis_size(ALL))])  2.25 us
    slice x3, local copies, waits for them, and re-layouts, per_device(): rows_b = jnp.concatenate([part[times:] for part in parts], axis=0)  0.69 us
  transfers between devices with their start and end apart: 23, of which 9 were waited for; matrix products, arithmetic and copies ran while one was open for 0% of the time, Pallas kernels for 9%

profile of v9, /device:TPU:0, one launch (start us, length us, event | category | flops | bytes accessed | tf_op | source)
XLA Modules:
  0.0 32.7 jit_solution(722461022906164635)
XLA Ops:
  0.6 1.9 %shard_map.84 = (f32[1024,128]{1,0:T(8,128)S(1)}, f32[128,128]{1,0:T(8,128)S(1)}, f32[128,128]{1,0:T(8,128)S(1)}, f32[1,128]{1,0:T(1,128)S(1)}, f32[136,128]{1,0:T(8,128)S(1)}, /*index=5*/f32[8,128,128]{2,1,0:T(8,128)S(1)}) custom-call(f32[1024,128]{1,0:T(8,128)} %bitcast.3, f32[128,128]{1,0:T(8,128)} %c_hbm.1, f32[8,128]{1,0:T(8,128)} %b_hbm.1, ...), custom_call_target="tpu_custom_call" | custom-call | flops 201326592 | bytes 65536 | tf_op jit(solution)/shard_map/pallas_call | solution.py:52
  2.6 0.5 %collective-permute-start = (f32[136,128]{1,0:T(8,128)S(1)}, f32[136,128]{1,0:T(8,128)S(1)}, u32[]{:S(2)}, u32[]{:S(2)}) collective-permute-start(f32[136,128]{1,0:T(8,128)S(1)} %get-tuple-element.32), channel_id=1, source_target_pairs={{0,1},{1,0},{2,3},{3,2},{4,5},{5,4},{6,7},{7,6},{8,9},{9,8},{10,11... | collective-permute-start | bytes 208904 | tf_op jit(solution)/shard_map/ppermute | solution.py:89
  3.1 0.1 collective-permute-start.3
  3.2 0.8 %collective-permute-done = f32[136,128]{1,0:T(8,128)S(1)} collective-permute-done((f32[136,128]{1,0:T(8,128)S(1)}, f32[136,128]{1,0:T(8,128)S(1)}, u32[]{:S(2)}, u32[]{:S(2)}) %collective-permute-start) | collective-permute-done | bytes 69664 | tf_op jit(solution)/shard_map/ppermute | solution.py:89
  4.0 0.4 %collective-permute-start.2 = (f32[144,128]{1,0:T(8,128)S(1)}, f32[144,128]{1,0:T(8,128)S(1)}, u32[]{:S(2)}, u32[]{:S(2)}) collective-permute-start(f32[144,128]{1,0:T(8,128)S(1)} %pad_maximum_fusion), channel_id=1, source_target_pairs={{0,1},{1,2},{2,3},{3,0},{4,5},{5,6},{6,7},{7,4},{8,9},{9,10},{10,1... | collective-permute-start | bytes 221192 | tf_op jit(solution)/shard_map/ppermute | solution.py:95
  4.4 2.6 %collective-permute-start.1 = (f32[144,128]{1,0:T(8,128)S(1)}, f32[144,128]{1,0:T(8,128)S(1)}, u32[]{:S(2)}, u32[]{:S(2)}) collective-permute-start(f32[144,128]{1,0:T(8,128)S(1)} %pad_maximum_fusion), channel_id=1, source_target_pairs={{0,1},{1,0},{2,3},{3,2},{4,5},{5,4},{6,7},{7,6},{8,9},{9,8},{10,11... | collective-permute-start | bytes 221192 | tf_op jit(solution)/shard_map/ppermute | solution.py:89
  7.1 0.0 collective-permute-start.10
  7.1 0.2 shard_map.85
  7.3 1.5 %collective-permute-done.2 = f32[144,128]{1,0:T(8,128)S(1)} collective-permute-done((f32[144,128]{1,0:T(8,128)S(1)}, f32[144,128]{1,0:T(8,128)S(1)}, u32[]{:S(2)}, u32[]{:S(2)}) %collective-permute-start.2) | collective-permute-done | bytes 73760 | tf_op jit(solution)/shard_map/ppermute | solution.py:95
  8.8 0.0 collective-permute-done.3.mate_con
  8.8 0.7 %shard_map.86 = (f32[128,128]{1,0:T(8,128)S(1)}, f32[16,128]{1,0:T(8,128)S(1)}, f32[88,128]{1,0:T(8,128)S(1)}) custom-call(f32[128,128]{1,0:T(8,128)S(1)} %slice_add_fusion.2.terms, f32[32,128]{1,0:T(8,128)S(1)} %pad_maximum_fusion.1.rows, f32[128,128]{1,0:T(8,128)S(1)} %get-tuple-element.33.a, f32[1,128]{1,0:T(1,128)S(1)} %get-tuple-element.34.w, ...), custom_call_target="tpu_custom_call" | custom-call | flops 50331648 | bytes 65536 | tf_op jit(solution)/shard_map/pallas_call | solution.py:52
  9.5 1.9 %collective-permute-start.7 = (f32[88,128]{1,0:T(8,128)S(1)}, f32[88,128]{1,0:T(8,128)S(1)}, u32[]{:S(2)}, u32[]{:S(2)}) collective-permute-start(f32[88,128]{1,0:T(8,128)S(1)} %get-tuple-element.38), channel_id=1, source_target_pairs={{0,13},{1,0},{2,15},{3,2},{4,9},{5,4},{6,11},{7,6},{8,5},{9,8},{10... | collective-permute-start | bytes 135176 | tf_op jit(solution)/shard_map/ppermute | solution.py:95
  11.4 0.3 collective-permute-start.6
  11.7 0.3 %collective-permute-start.5 = (f32[88,128]{1,0:T(8,128)S(1)}, f32[88,128]{1,0:T(8,128)S(1)}, u32[]{:S(2)}, u32[]{:S(2)}) collective-permute-start(f32[88,128]{1,0:T(8,128)S(1)} %get-tuple-element.38), channel_id=1, source_target_pairs={{0,5},{1,0},{2,7},{3,2},{4,1},{5,4},{6,3},{7,6},{8,13},{9,8},{10,1... | collective-permute-start | bytes 135176 | tf_op jit(solution)/shard_map/ppermute | solution.py:95
  12.0 0.2 collective-permute-start.4
  12.2 0.9 %collective-permute-done.7 = f32[88,128]{1,0:T(8,128)S(1)} collective-permute-done((f32[88,128]{1,0:T(8,128)S(1)}, f32[88,128]{1,0:T(8,128)S(1)}, u32[]{:S(2)}, u32[]{:S(2)}) %collective-permute-start.7) | collective-permute-done | bytes 45088 | tf_op jit(solution)/shard_map/ppermute | solution.py:95
  13.1 1.3 %collective-permute-start.11 = (f32[128,128]{1,0:T(8,128)S(1)}, f32[128,128]{1,0:T(8,128)S(1)}, u32[]{:S(2)}, u32[]{:S(2)}) collective-permute-start(f32[128,128]{1,0:T(8,128)S(1)} %get-tuple-element.41.moved), channel_id=1, source_target_pairs={{0,1},{1,0},{2,3},{3,2},{4,5},{5,4},{6,7},{7,6},{8,9},{9,8},{10,11... | collective-permute-start | bytes 196616 | tf_op jit(solution)/shard_map/ppermute | solution.py:89
  14.4 0.0 collective-permute-done.6
  14.4 0.0 collective-permute-done.5
  14.4 0.0 collective-permute-done.4
  14.4 1.0 %collective-permute-start.9 = (f32[88,128]{1,0:T(8,128)S(1)}, f32[88,128]{1,0:T(8,128)S(1)}, u32[]{:S(2)}, u32[]{:S(2)}) collective-permute-start(f32[88,128]{1,0:T(8,128)S(1)} %add_add_fusion.1), channel_id=1, source_target_pairs={{0,1},{1,16},{2,3},{3,18},{4,5},{5,20},{6,7},{7,22},{8,9},{9,24},{... | collective-permute-start | bytes 135176 | tf_op jit(solution)/shard_map/ppermute | solution.py:95
  15.5 1.7 %collective-permute-start.8 = (f32[88,128]{1,0:T(8,128)S(1)}, f32[88,128]{1,0:T(8,128)S(1)}, u32[]{:S(2)}, u32[]{:S(2)}) collective-permute-start(f32[88,128]{1,0:T(8,128)S(1)} %add_add_fusion.1), channel_id=1, source_target_pairs={{0,1},{1,0},{2,3},{3,2},{4,5},{5,4},{6,7},{7,6},{8,9},{9,8},{10,11... | collective-permute-start | bytes 135176 | tf_op jit(solution)/shard_map/ppermute | solution.py:89
  17.2 0.0 collective-permute-done.10.mate_x
  17.2 0.0 collective-permute-done.11.mate_moved
  17.2 0.5 %shard_map.87.each = f32[16,128,128]{2,1,0:T(8,128)S(1)} custom-call(f32[1024,128]{1,0:T(8,128)S(1)} %get-tuple-element.40.x, f32[1024,128]{1,0:T(8,128)S(1)} %collective-permute-done.10.mate_x, f32[128,128]{1,0:T(8,128)S(1)} %get-tuple-element.41.moved, f32[128,128]{1,0:T(8,128)S(1)} %collective-permute-done.11.mate_moved), custom_call_target="tpu_custom_call" | custom-call | flops 402653184 | bytes 65536 | tf_op jit(solution)/shard_map/pallas_call | solution.py:52
  17.7 2.1 %collective-permute-done.9 = f32[88,128]{1,0:T(8,128)S(1)} collective-permute-done((f32[88,128]{1,0:T(8,128)S(1)}, f32[88,128]{1,0:T(8,128)S(1)}, u32[]{:S(2)}, u32[]{:S(2)}) %collective-permute-start.9) | collective-permute-done | bytes 45088 | tf_op jit(solution)/shard_map/ppermute | solution.py:95
  19.8 0.3 %shard_map.88 = (f32[128,128]{1,0:T(8,128)S(1)}, f32[144,128]{1,0:T(8,128)S(1)}) custom-call(f32[88,128]{1,0:T(8,128)S(1)} %add.41.sums, f32[16,128]{1,0:T(8,128)S(1)} %get-tuple-element.39.b, f32[1,128]{1,0:T(1,128)S(1)} %get-tuple-element.34.w, f32[128,128]{1,0:T(8,128)S(1)} %get-tuple-element.36.outer_c, f32[16,128,128]{2,1,0:T(8,128)S(1)} %shard_map.87.each), custom_call_target="tpu_custom_call" | custom-call | flops 3145728 | bytes 65536 | tf_op jit(solution)/shard_map/pallas_call | solution.py:52
  20.1 0.1 collective-permute-start.15
  20.2 0.3 collective-permute-start.14
  20.4 1.2 %collective-permute-start.13 = (f32[144,128]{1,0:T(8,128)S(1)}, f32[144,128]{1,0:T(8,128)S(1)}, u32[]{:S(2)}, u32[]{:S(2)}) collective-permute-start(f32[144,128]{1,0:T(8,128)S(1)} %get-tuple-element.42), channel_id=1, source_target_pairs={{0,3},{1,0},{2,1},{3,2},{4,7},{5,4},{6,5},{7,6},{8,11},{9,8},{10,9... | collective-permute-start | bytes 221192 | tf_op jit(solution)/shard_map/ppermute | solution.py:95
  21.6 0.5 %collective-permute-start.21 = (f32[128,128]{1,0:T(8,128)S(1)}, f32[128,128]{1,0:T(8,128)S(1)}, u32[]{:S(2)}, u32[]{:S(2)}) collective-permute-start(f32[128,128]{1,0:T(8,128)S(1)} %get-tuple-element.43.gram), channel_id=1, source_target_pairs={{0,1},{1,0},{2,3},{3,2},{4,5},{5,4},{6,7},{7,6},{8,9},{9,8},{10,11... | collective-permute-start | bytes 196616 | tf_op jit(solution)/shard_map/ppermute | solution.py:89
  22.1 0.0 collective-permute-done.15
  22.2 0.7 %collective-permute-done.14 = f32[144,128]{1,0:T(8,128)S(1)} collective-permute-done((f32[144,128]{1,0:T(8,128)S(1)}, f32[144,128]{1,0:T(8,128)S(1)}, u32[]{:S(2)}, u32[]{:S(2)}) %collective-permute-start.14) | collective-permute-done | bytes 73760 | tf_op jit(solution)/shard_map/ppermute | solution.py:95
  22.8 0.8 %collective-permute-done.13 = f32[144,128]{1,0:T(8,128)S(1)} collective-permute-done((f32[144,128]{1,0:T(8,128)S(1)}, f32[144,128]{1,0:T(8,128)S(1)}, u32[]{:S(2)}, u32[]{:S(2)}) %collective-permute-start.13) | collective-permute-done | bytes 73760 | tf_op jit(solution)/shard_map/ppermute | solution.py:95
  23.6 0.0 collective-permute-done.12
  23.6 0.9 %collective-permute-start.19 = (f32[128,128]{1,0:T(8,128)S(1)}, f32[128,128]{1,0:T(8,128)S(1)}, u32[]{:S(2)}, u32[]{:S(2)}) collective-permute-start(f32[128,128]{1,0:T(8,128)S(1)} %fusion), channel_id=1, source_target_pairs={{0,1},{1,24},{2,3},{3,26},{4,5},{5,28},{6,7},{7,30},{8,9},{9,16},{... | collective-permute-start | bytes 196616 | tf_op jit(solution)/shard_map/ppermute | solution.py:95
  24.6 1.8 %collective-permute-start.18 = (f32[128,128]{1,0:T(8,128)S(1)}, f32[128,128]{1,0:T(8,128)S(1)}, u32[]{:S(2)}, u32[]{:S(2)}) collective-permute-start(f32[128,128]{1,0:T(8,128)S(1)} %fusion), channel_id=1, source_target_pairs={{0,1},{1,16},{2,3},{3,18},{4,5},{5,20},{6,7},{7,22},{8,9},{9,24},{... | collective-permute-start | bytes 196616 | tf_op jit(solution)/shard_map/ppermute | solution.py:95
  26.4 0.1 collective-permute-start.17
  26.5 0.7 %slice-done = f32[16,128]{1,0:T(8,128)S(1)} async-done(((f32[144,128]{1,0:T(8,128)}), f32[16,128]{1,0:T(8,128)S(1)}, s32[]{:S(2)}) %slice-start) | async-done | bytes 8216 | tf_op jit(solution)/shard_map/slice | solution.py:315
  27.2 0.5 %collective-permute-start.20 = (f32[32,128]{1,0:T(8,128)S(1)}, f32[32,128]{1,0:T(8,128)S(1)}, u32[]{:S(2)}, u32[]{:S(2)}) collective-permute-start(f32[32,128]{1,0:T(8,128)S(1)} %pad_maximum_fusion.2.rows), channel_id=1, source_target_pairs={{0,1},{1,0},{2,3},{3,2},{4,5},{5,4},{6,7},{7,6},{8,9},{9,8},{10,11... | collective-permute-start | bytes 49160 | tf_op jit(solution)/shard_map/ppermute | solution.py:89
  27.7 0.7 %shard_map.89 = (f32[128,128]{1,0:T(8,128)}, f32[1,128]{1,0:T(1,128)S(1)}, f32[128,128]{1,0:T(8,128)S(1)}) custom-call(f32[128,128]{1,0:T(8,128)S(1)} %get-tuple-element.43.gram, f32[128,128]{1,0:T(8,128)S(1)} %collective-permute-done.21.mate_gram, f32[128,128]{1,0:T(8,128)S(1)} %get-tuple-element.41.moved, ...), custom_call_target="tpu_custom_call" | custom-call | flops 131072 | bytes 65536 | tf_op jit(solution)/shard_map/pallas_call | solution.py:52
  28.4 0.2 collective-permute-done.20.mate_rows
  28.5 0.9 %shard_map.90 = (f32[8,128]{1,0:T(8,128)}, f32[128,128]{1,0:T(8,128)S(1)}, f32[1,128]{1,0:T(1,128)S(1)}, f32[1,128]{1,0:T(1,128)S(1)}) custom-call(f32[32,128]{1,0:T(8,128)S(1)} %pad_maximum_fusion.2.rows, f32[32,128]{1,0:T(8,128)S(1)} %collective-permute-done.20.mate_rows, f32[128,128]{1,0:T(8,128)S(1)} %get-tuple-element.35.c, ...), custom_call_target="tpu_custom_call" | custom-call | flops 16777216 | bytes 65536 | tf_op jit(solution)/shard_map/pallas_call | solution.py:52
  29.4 1.3 %collective-permute-done.18 = f32[128,128]{1,0:T(8,128)S(1)} collective-permute-done((f32[128,128]{1,0:T(8,128)S(1)}, f32[128,128]{1,0:T(8,128)S(1)}, u32[]{:S(2)}, u32[]{:S(2)}) %collective-permute-start.18) | collective-permute-done | bytes 65568 | tf_op jit(solution)/shard_map/ppermute | solution.py:95
  30.7 0.0 collective-permute-done.17
  30.7 0.1 collective-permute-start.22
  30.8 1.2 %collective-permute-done.22.mate_terms = f32[128,128]{1,0:T(8,128)S(1)} collective-permute-done((f32[128,128]{1,0:T(8,128)S(1)}, f32[128,128]{1,0:T(8,128)S(1)}, u32[]{:S(2)}, u32[]{:S(2)}) %collective-permute-start.22) | collective-permute-done | bytes 65568 | tf_op jit(solution)/shard_map/ppermute | solution.py:89
  32.0 0.7 %shard_map.91 = (f32[128,128]{1,0:T(8,128)}, f32[1,128]{1,0:T(1,128)}) custom-call(f32[128,128]{1,0:T(8,128)S(1)} %add_add_fusion.terms, f32[128,128]{1,0:T(8,128)S(1)} %collective-permute-done.22.mate_terms, f32[128,128]{1,0:T(8,128)S(1)} %get-tuple-element.55.base, f32[1,128]{1,0:T(1,128)S(1)} %get-tuple-element.56.gain, f32[1,128]{1,0:T(1,128)S(1)} %get-tuple-element.57.scale), custom_call_target="tpu_custom_call" | custom-call | flops 131072 | bytes 65536 | tf_op jit(solution)/shard_map/pallas_call | solution.py:52
  (24 shorter events, 0.1 us)
Async XLA Ops:
  2.6 1.4 %collective-permute-start = (f32[136,128]{1,0:T(8,128)S(1)}, f32[136,128]{1,0:T(8,128)S(1)}, u32[]{:S(2)}, u32[]{:S(2)}) collective-permute-start(f32[136,128]{1,0:T(8,128)S(1)} %get-tuple-element.32), channel_id=1, source_target_pairs={{0,1},{1,0},{2,3},{3,2},{4,5},{5,4},{6,7},{7,6},{8,9},{9,8},{10,11... | collective-permute-start | bytes 208904 | tf_op jit(solution)/shard_map/ppermute | solution.py:89
  3.1 5.7 %collective-permute-start.3 = (f32[8,128,128]{2,1,0:T(8,128)S(1)}, f32[8,128,128]{2,1,0:T(8,128)S(1)}, u32[]{:S(2)}, u32[]{:S(2)}) collective-permute-start(f32[8,128,128]{2,1,0:T(8,128)S(1)} %get-tuple-element.37.con), channel_id=1, source_target_pairs={{0,1},{1,0},{2,3},{3,2},{4,5},{5,4},{6,7},{7,6},{8,9},{9,8},{10,11... | collective-permute-start | bytes 1572872 | tf_op jit(solution)/shard_map/ppermute | solution.py:89
  4.0 4.7 %collective-permute-start.2 = (f32[144,128]{1,0:T(8,128)S(1)}, f32[144,128]{1,0:T(8,128)S(1)}, u32[]{:S(2)}, u32[]{:S(2)}) collective-permute-start(f32[144,128]{1,0:T(8,128)S(1)} %pad_maximum_fusion), channel_id=1, source_target_pairs={{0,1},{1,2},{2,3},{3,0},{4,5},{5,6},{6,7},{7,4},{8,9},{9,10},{10,1... | collective-permute-start | bytes 221192 | tf_op jit(solution)/shard_map/ppermute | solution.py:95
  4.4 4.3 %collective-permute-start.1 = (f32[144,128]{1,0:T(8,128)S(1)}, f32[144,128]{1,0:T(8,128)S(1)}, u32[]{:S(2)}, u32[]{:S(2)}) collective-permute-start(f32[144,128]{1,0:T(8,128)S(1)} %pad_maximum_fusion), channel_id=1, source_target_pairs={{0,1},{1,0},{2,3},{3,2},{4,5},{5,4},{6,7},{7,6},{8,9},{9,8},{10,11... | collective-permute-start | bytes 221192 | tf_op jit(solution)/shard_map/ppermute | solution.py:89
  7.1 10.1 %collective-permute-start.10 = (f32[1024,128]{1,0:T(8,128)S(1)}, f32[1024,128]{1,0:T(8,128)S(1)}, u32[]{:S(2)}, u32[]{:S(2)}) collective-permute-start(f32[1024,128]{1,0:T(8,128)S(1)} %get-tuple-element.40.x), channel_id=1, source_target_pairs={{0,1},{1,0},{2,3},{3,2},{4,5},{5,4},{6,7},{7,6},{8,9},{9,8},{10,11... | collective-permute-start | bytes 1572872 | tf_op jit(solution)/shard_map/ppermute | solution.py:89
  9.5 3.6 %collective-permute-start.7 = (f32[88,128]{1,0:T(8,128)S(1)}, f32[88,128]{1,0:T(8,128)S(1)}, u32[]{:S(2)}, u32[]{:S(2)}) collective-permute-start(f32[88,128]{1,0:T(8,128)S(1)} %get-tuple-element.38), channel_id=1, source_target_pairs={{0,13},{1,0},{2,15},{3,2},{4,9},{5,4},{6,11},{7,6},{8,5},{9,8},{10... | collective-permute-start | bytes 135176 | tf_op jit(solution)/shard_map/ppermute | solution.py:95
  11.4 3.0 %collective-permute-start.6 = (f32[88,128]{1,0:T(8,128)S(1)}, f32[88,128]{1,0:T(8,128)S(1)}, u32[]{:S(2)}, u32[]{:S(2)}) collective-permute-start(f32[88,128]{1,0:T(8,128)S(1)} %get-tuple-element.38), channel_id=1, source_target_pairs={{0,9},{1,0},{2,11},{3,2},{4,13},{5,4},{6,15},{7,6},{8,1},{9,8},{10... | collective-permute-start | bytes 135176 | tf_op jit(solution)/shard_map/ppermute | solution.py:95
  11.7 2.7 %collective-permute-start.5 = (f32[88,128]{1,0:T(8,128)S(1)}, f32[88,128]{1,0:T(8,128)S(1)}, u32[]{:S(2)}, u32[]{:S(2)}) collective-permute-start(f32[88,128]{1,0:T(8,128)S(1)} %get-tuple-element.38), channel_id=1, source_target_pairs={{0,5},{1,0},{2,7},{3,2},{4,1},{5,4},{6,3},{7,6},{8,13},{9,8},{10,1... | collective-permute-start | bytes 135176 | tf_op jit(solution)/shard_map/ppermute | solution.py:95
  12.0 2.3 %collective-permute-start.4 = (f32[88,128]{1,0:T(8,128)S(1)}, f32[88,128]{1,0:T(8,128)S(1)}, u32[]{:S(2)}, u32[]{:S(2)}) collective-permute-start(f32[88,128]{1,0:T(8,128)S(1)} %get-tuple-element.38), channel_id=1, source_target_pairs={{0,1},{1,0},{2,3},{3,2},{4,5},{5,4},{6,7},{7,6},{8,9},{9,8},{10,11... | collective-permute-start | bytes 135176 | tf_op jit(solution)/shard_map/ppermute | solution.py:89
  13.1 4.1 %collective-permute-start.11 = (f32[128,128]{1,0:T(8,128)S(1)}, f32[128,128]{1,0:T(8,128)S(1)}, u32[]{:S(2)}, u32[]{:S(2)}) collective-permute-start(f32[128,128]{1,0:T(8,128)S(1)} %get-tuple-element.41.moved), channel_id=1, source_target_pairs={{0,1},{1,0},{2,3},{3,2},{4,5},{5,4},{6,7},{7,6},{8,9},{9,8},{10,11... | collective-permute-start | bytes 196616 | tf_op jit(solution)/shard_map/ppermute | solution.py:89
  14.4 5.3 %collective-permute-start.9 = (f32[88,128]{1,0:T(8,128)S(1)}, f32[88,128]{1,0:T(8,128)S(1)}, u32[]{:S(2)}, u32[]{:S(2)}) collective-permute-start(f32[88,128]{1,0:T(8,128)S(1)} %add_add_fusion.1), channel_id=1, source_target_pairs={{0,1},{1,16},{2,3},{3,18},{4,5},{5,20},{6,7},{7,22},{8,9},{9,24},{... | collective-permute-start | bytes 135176 | tf_op jit(solution)/shard_map/ppermute | solution.py:95
  15.5 4.3 %collective-permute-start.8 = (f32[88,128]{1,0:T(8,128)S(1)}, f32[88,128]{1,0:T(8,128)S(1)}, u32[]{:S(2)}, u32[]{:S(2)}) collective-permute-start(f32[88,128]{1,0:T(8,128)S(1)} %add_add_fusion.1), channel_id=1, source_target_pairs={{0,1},{1,0},{2,3},{3,2},{4,5},{5,4},{6,7},{7,6},{8,9},{9,8},{10,11... | collective-permute-start | bytes 135176 | tf_op jit(solution)/shard_map/ppermute | solution.py:89
  20.1 2.0 %collective-permute-start.15 = (f32[144,128]{1,0:T(8,128)S(1)}, f32[144,128]{1,0:T(8,128)S(1)}, u32[]{:S(2)}, u32[]{:S(2)}) collective-permute-start(f32[144,128]{1,0:T(8,128)S(1)} %get-tuple-element.42), channel_id=1, source_target_pairs={{0,7},{1,0},{2,5},{3,2},{4,3},{5,4},{6,1},{7,6},{8,15},{9,8},{10,1... | collective-permute-start | bytes 221192 | tf_op jit(solution)/shard_map/ppermute | solution.py:95
  20.2 2.7 %collective-permute-start.14 = (f32[144,128]{1,0:T(8,128)S(1)}, f32[144,128]{1,0:T(8,128)S(1)}, u32[]{:S(2)}, u32[]{:S(2)}) collective-permute-start(f32[144,128]{1,0:T(8,128)S(1)} %get-tuple-element.42), channel_id=1, source_target_pairs={{0,5},{1,0},{2,7},{3,2},{4,1},{5,4},{6,3},{7,6},{8,13},{9,8},{10,1... | collective-permute-start | bytes 221192 | tf_op jit(solution)/shard_map/ppermute | solution.py:95
  20.4 3.2 %collective-permute-start.13 = (f32[144,128]{1,0:T(8,128)S(1)}, f32[144,128]{1,0:T(8,128)S(1)}, u32[]{:S(2)}, u32[]{:S(2)}) collective-permute-start(f32[144,128]{1,0:T(8,128)S(1)} %get-tuple-element.42), channel_id=1, source_target_pairs={{0,3},{1,0},{2,1},{3,2},{4,7},{5,4},{6,5},{7,6},{8,11},{9,8},{10,9... | collective-permute-start | bytes 221192 | tf_op jit(solution)/shard_map/ppermute | solution.py:95
  21.6 2.0 %collective-permute-start.12 = (f32[144,128]{1,0:T(8,128)S(1)}, f32[144,128]{1,0:T(8,128)S(1)}, u32[]{:S(2)}, u32[]{:S(2)}) collective-permute-start(f32[144,128]{1,0:T(8,128)S(1)} %get-tuple-element.42), channel_id=1, source_target_pairs={{0,1},{1,0},{2,3},{3,2},{4,5},{5,4},{6,7},{7,6},{8,9},{9,8},{10,11... | collective-permute-start | bytes 221192 | tf_op jit(solution)/shard_map/ppermute | solution.py:89
  21.6 5.5 %collective-permute-start.21 = (f32[128,128]{1,0:T(8,128)S(1)}, f32[128,128]{1,0:T(8,128)S(1)}, u32[]{:S(2)}, u32[]{:S(2)}) collective-permute-start(f32[128,128]{1,0:T(8,128)S(1)} %get-tuple-element.43.gram), channel_id=1, source_target_pairs={{0,1},{1,0},{2,3},{3,2},{4,5},{5,4},{6,7},{7,6},{8,9},{9,8},{10,11... | collective-permute-start | bytes 196616 | tf_op jit(solution)/shard_map/ppermute | solution.py:89
  23.6 2.8 %copy-start = (f32[144,128]{1,0:T(8,128)}, f32[144,128]{1,0:T(8,128)S(1)}, u32[]{:S(2)}) copy-start(f32[144,128]{1,0:T(8,128)S(1)} %collective-permute-done.13) | copy-start | bytes 221188
  23.6 5.7 %collective-permute-start.19 = (f32[128,128]{1,0:T(8,128)S(1)}, f32[128,128]{1,0:T(8,128)S(1)}, u32[]{:S(2)}, u32[]{:S(2)}) collective-permute-start(f32[128,128]{1,0:T(8,128)S(1)} %fusion), channel_id=1, source_target_pairs={{0,1},{1,24},{2,3},{3,26},{4,5},{5,28},{6,7},{7,30},{8,9},{9,16},{... | collective-permute-start | bytes 196616 | tf_op jit(solution)/shard_map/ppermute | solution.py:95
  24.6 6.1 %collective-permute-start.18 = (f32[128,128]{1,0:T(8,128)S(1)}, f32[128,128]{1,0:T(8,128)S(1)}, u32[]{:S(2)}, u32[]{:S(2)}) collective-permute-start(f32[128,128]{1,0:T(8,128)S(1)} %fusion), channel_id=1, source_target_pairs={{0,1},{1,16},{2,3},{3,18},{4,5},{5,20},{6,7},{7,22},{8,9},{9,24},{... | collective-permute-start | bytes 196616 | tf_op jit(solution)/shard_map/ppermute | solution.py:95
  26.4 4.3 %collective-permute-start.17 = (f32[128,128]{1,0:T(8,128)S(1)}, f32[128,128]{1,0:T(8,128)S(1)}, u32[]{:S(2)}, u32[]{:S(2)}) collective-permute-start(f32[128,128]{1,0:T(8,128)S(1)} %fusion), channel_id=1, source_target_pairs={{0,1},{1,8},{2,3},{3,10},{4,5},{5,12},{6,7},{7,14},{8,9},{9,0},{10... | collective-permute-start | bytes 196616 | tf_op jit(solution)/shard_map/ppermute | solution.py:95
  26.5 4.2 %collective-permute-start.16 = (f32[128,128]{1,0:T(8,128)S(1)}, f32[128,128]{1,0:T(8,128)S(1)}, u32[]{:S(2)}, u32[]{:S(2)}) collective-permute-start(f32[128,128]{1,0:T(8,128)S(1)} %fusion), channel_id=1, source_target_pairs={{0,1},{1,0},{2,3},{3,2},{4,5},{5,4},{6,7},{7,6},{8,9},{9,8},{10,11... | collective-permute-start | bytes 196616 | tf_op jit(solution)/shard_map/ppermute | solution.py:89
  26.5 0.7 %slice-start = ((f32[144,128]{1,0:T(8,128)}), f32[16,128]{1,0:T(8,128)S(1)}, s32[]{:S(2)}) async-start(f32[144,128]{1,0:T(8,128)} %copy-done), calls=%async_computation | async-start | bytes 16384 | tf_op jit(solution)/shard_map/slice | solution.py:315
  27.2 1.3 %collective-permute-start.20 = (f32[32,128]{1,0:T(8,128)S(1)}, f32[32,128]{1,0:T(8,128)S(1)}, u32[]{:S(2)}, u32[]{:S(2)}) collective-permute-start(f32[32,128]{1,0:T(8,128)S(1)} %pad_maximum_fusion.2.rows), channel_id=1, source_target_pairs={{0,1},{1,0},{2,3},{3,2},{4,5},{5,4},{6,7},{7,6},{8,9},{9,8},{10,11... | collective-permute-start | bytes 49160 | tf_op jit(solution)/shard_map/ppermute | solution.py:89
  30.7 1.3 %collective-permute-start.22 = (f32[128,128]{1,0:T(8,128)S(1)}, f32[128,128]{1,0:T(8,128)S(1)}, u32[]{:S(2)}, u32[]{:S(2)}) collective-permute-start(f32[128,128]{1,0:T(8,128)S(1)} %add_add_fusion.terms), channel_id=1, source_target_pairs={{0,1},{1,0},{2,3},{3,2},{4,5},{5,4},{6,7},{7,6},{8,9},{9,8},{10,11... | collective-permute-start | bytes 196616 | tf_op jit(solution)/shard_map/ppermute | solution.py:89

commit v10 on v9

--- a/solution.py
+++ b/solution.py
@@ -211,8 +211,8 @@
 
     got = swap(opened)
     terms = opened[:vox_rows] + got[:vox_rows]
-    rows_b = jnp.concatenate([got[vox_rows:], opened[vox_rows:]], axis=0)
-    holder = 1
+    rows_b = jnp.concatenate([opened[vox_rows:], got[vox_rows:]], axis=0)
+    holder = 0
     for group in groups_of(chip_bits):
         parts = fan(jnp.concatenate([terms, rows_b], axis=0), holder, masks_of(group))
         terms = tree([part[:vox_rows] for part in parts])
@@ -314,6 +314,9 @@
             parts = [part for part, mask in zip(parts, masks) if not mask & ~smp_mask]
             rows_b = jnp.concatenate([part[times:] for part in parts], axis=0)
             rows_core = holder
+            terms, rows_b, voxel_result, scales_a, weighed = lax.optimization_barrier(
+                (terms, rows_b, voxel_result, scales_a, weighed)
+            )
     last_core = holder
     mate_rows_b = swap(rows_b)
 
@@ -334,9 +337,7 @@
         2 * rank * rank * times * 4,
         scratch=(near(smp_total, rank),),
     )
-    terms, base, gain, scale, voxel_result, sample_result = lax.optimization_barrier(
-        (terms, base, gain, scale, voxel_result, sample_result)
-    )
+    terms, base, gain, scale, sample_result = lax.optimization_barrier((terms, base, gain, scale, sample_result))
     mate_terms = swap(terms)
 
     def last_kernel(terms, mate_terms, base, gain, scale, c_out, w_out):

time: 32.9 us -> 34.1 us (1.036)
  waiting for transfers between devices: 9.41 us -> 11.7 us
  local copies, waits for them, and re-layouts: 0.7 us -> 0.01 us
    ppermute x12, starting transfers between devices: 7.48 us -> 4.32 us  [swap(): lax.ppermute(values, ALL, [(i, i ^ 1) for i in range(lax.axis_size(ALL))])]
    ppermute x11, starting transfers between devices: 8.32 us -> 11.2 us  [send(): return lax.ppermute(values, ALL, pairs)]
    ppermute x11, waiting for transfers between devices: 7.16 us -> 8.4 us  [send(): return lax.ppermute(values, ALL, pairs)]
    ppermute x12, waiting for transfers between devices: 2.25 us -> 3.25 us  [swap(): lax.ppermute(values, ALL, [(i, i ^ 1) for i in range(lax.axis_size(ALL))])]
    slice x3 -> x2, local copies, waits for them, and re-layouts: 0.69 us -> 0.01 us  [per_device(): rows_b = jnp.concatenate([part[times:] for part in parts], axis=0)]
  transfers between devices with their start and end apart: 23 -> 23, of which waited for: 9 -> 12; matrix products, arithmetic and copies ran while one was open for 0% -> 0% of each run, Pallas kernels for 9% -> 9%
where the time goes in v10:
time: 34.1 us; the launch traced here: 33.9 us
  starting transfers between devices  15.5 us (45%)
  waiting for transfers between devices  11.7 us (34%)
  Pallas kernels  5.93 us (17%)
  between operations  0.75 us (2%)
    ppermute x11, starting transfers between devices, send(): return lax.ppermute(values, ALL, pairs)  11.2 us
    ppermute x11, waiting for transfers between devices, send(): return lax.ppermute(values, ALL, pairs)  8.4 us
    pallas_call x8, Pallas kernels, call(): pl.pallas_call(kernel, out_shape=outs, in_specs=specs, out_specs=[pl.Bloc...  5.93 us
    ppermute x12, starting transfers between devices, swap(): lax.ppermute(values, ALL, [(i, i ^ 1) for i in range(lax.axis_size(ALL))])  4.32 us
    ppermute x12, waiting for transfers between devices, swap(): lax.ppermute(values, ALL, [(i, i ^ 1) for i in range(lax.axis_size(ALL))])  3.25 us
  transfers between devices with their start and end apart: 23, of which 12 were waited for; matrix products, arithmetic and copies ran while one was open for 0% of the time, Pallas kernels for 9%

profile of v10, /device:TPU:0, one launch (start us, length us, event | category | flops | bytes accessed | tf_op | source)
XLA Modules:
  0.0 33.9 jit_solution(1047191242199099946)
XLA Ops:
  0.6 1.9 %shard_map.84 = (f32[1024,128]{1,0:T(8,128)S(1)}, f32[128,128]{1,0:T(8,128)S(1)}, f32[128,128]{1,0:T(8,128)S(1)}, f32[1,128]{1,0:T(1,128)S(1)}, f32[136,128]{1,0:T(8,128)S(1)}, /*index=5*/f32[8,128,128]{2,1,0:T(8,128)S(1)}) custom-call(f32[1024,128]{1,0:T(8,128)} %bitcast.3, f32[128,128]{1,0:T(8,128)} %c_hbm.1, f32[8,128]{1,0:T(8,128)} %b_hbm.1, ...), custom_call_target="tpu_custom_call" | custom-call | flops 201326592 | bytes 65536 | tf_op jit(solution)/shard_map/pallas_call | solution.py:52
  2.6 0.5 %collective-permute-start = (f32[136,128]{1,0:T(8,128)S(1)}, f32[136,128]{1,0:T(8,128)S(1)}, u32[]{:S(2)}, u32[]{:S(2)}) collective-permute-start(f32[136,128]{1,0:T(8,128)S(1)} %get-tuple-element.36), channel_id=1, source_target_pairs={{0,1},{1,0},{2,3},{3,2},{4,5},{5,4},{6,7},{7,6},{8,9},{9,8},{10,11... | collective-permute-start | bytes 208904 | tf_op jit(solution)/shard_map/ppermute | solution.py:89
  3.1 0.1 collective-permute-start.3
  3.2 0.8 %collective-permute-done = f32[136,128]{1,0:T(8,128)S(1)} collective-permute-done((f32[136,128]{1,0:T(8,128)S(1)}, f32[136,128]{1,0:T(8,128)S(1)}, u32[]{:S(2)}, u32[]{:S(2)}) %collective-permute-start) | collective-permute-done | bytes 69664 | tf_op jit(solution)/shard_map/ppermute | solution.py:89
  4.0 2.7 %collective-permute-start.2 = (f32[144,128]{1,0:T(8,128)S(1)}, f32[144,128]{1,0:T(8,128)S(1)}, u32[]{:S(2)}, u32[]{:S(2)}) collective-permute-start(f32[144,128]{1,0:T(8,128)S(1)} %pad_maximum_fusion), channel_id=1, source_target_pairs={{0,3},{1,0},{2,1},{3,2},{4,7},{5,4},{6,5},{7,6},{8,11},{9,8},{10,9... | collective-permute-start | bytes 221192 | tf_op jit(solution)/shard_map/ppermute | solution.py:95
  6.7 0.0 collective-permute-start.1
  6.7 0.5 %collective-permute-start.10 = (f32[1024,128]{1,0:T(8,128)S(1)}, f32[1024,128]{1,0:T(8,128)S(1)}, u32[]{:S(2)}, u32[]{:S(2)}) collective-permute-start(f32[1024,128]{1,0:T(8,128)S(1)} %get-tuple-element.44.x), channel_id=1, source_target_pairs={{0,1},{1,0},{2,3},{3,2},{4,5},{5,4},{6,7},{7,6},{8,9},{9,8},{10,11... | collective-permute-start | bytes 1572872 | tf_op jit(solution)/shard_map/ppermute | solution.py:89
  7.2 0.2 shard_map.85
  7.4 1.2 %collective-permute-done.2 = f32[144,128]{1,0:T(8,128)S(1)} collective-permute-done((f32[144,128]{1,0:T(8,128)S(1)}, f32[144,128]{1,0:T(8,128)S(1)}, u32[]{:S(2)}, u32[]{:S(2)}) %collective-permute-start.2) | collective-permute-done | bytes 73760 | tf_op jit(solution)/shard_map/ppermute | solution.py:95
  8.7 0.0 collective-permute-done.1
  8.7 0.0 collective-permute-done.3.mate_con
  8.7 0.7 %shard_map.86 = (f32[128,128]{1,0:T(8,128)S(1)}, f32[16,128]{1,0:T(8,128)S(1)}, f32[88,128]{1,0:T(8,128)S(1)}) custom-call(f32[128,128]{1,0:T(8,128)S(1)} %slice_add_fusion.2.terms, f32[32,128]{1,0:T(8,128)S(1)} %pad_maximum_fusion.1.rows, f32[128,128]{1,0:T(8,128)S(1)} %get-tuple-element.37.a, f32[1,128]{1,0:T(1,128)S(1)} %get-tuple-element.38.w, ...), custom_call_target="tpu_custom_call" | custom-call | flops 50331648 | bytes 65536 | tf_op jit(solution)/shard_map/pallas_call | solution.py:52
  9.5 0.5 %collective-permute-start.7 = (f32[88,128]{1,0:T(8,128)S(1)}, f32[88,128]{1,0:T(8,128)S(1)}, u32[]{:S(2)}, u32[]{:S(2)}) collective-permute-start(f32[88,128]{1,0:T(8,128)S(1)} %get-tuple-element.42), channel_id=1, source_target_pairs={{0,1},{1,12},{2,3},{3,14},{4,5},{5,8},{6,7},{7,10},{8,9},{9,4},{10... | collective-permute-start | bytes 135176 | tf_op jit(solution)/shard_map/ppermute | solution.py:95
  9.9 2.2 %collective-permute-start.6 = (f32[88,128]{1,0:T(8,128)S(1)}, f32[88,128]{1,0:T(8,128)S(1)}, u32[]{:S(2)}, u32[]{:S(2)}) collective-permute-start(f32[88,128]{1,0:T(8,128)S(1)} %get-tuple-element.42), channel_id=1, source_target_pairs={{0,1},{1,8},{2,3},{3,10},{4,5},{5,12},{6,7},{7,14},{8,9},{9,0},{10... | collective-permute-start | bytes 135176 | tf_op jit(solution)/shard_map/ppermute | solution.py:95
  12.1 0.0 collective-permute-start.5
  12.1 0.6 %collective-permute-start.4 = (f32[88,128]{1,0:T(8,128)S(1)}, f32[88,128]{1,0:T(8,128)S(1)}, u32[]{:S(2)}, u32[]{:S(2)}) collective-permute-start(f32[88,128]{1,0:T(8,128)S(1)} %get-tuple-element.42), channel_id=1, source_target_pairs={{0,1},{1,0},{2,3},{3,2},{4,5},{5,4},{6,7},{7,6},{8,9},{9,8},{10,11... | collective-permute-start | bytes 135176 | tf_op jit(solution)/shard_map/ppermute | solution.py:89
  12.8 1.2 %collective-permute-done.7 = f32[88,128]{1,0:T(8,128)S(1)} collective-permute-done((f32[88,128]{1,0:T(8,128)S(1)}, f32[88,128]{1,0:T(8,128)S(1)}, u32[]{:S(2)}, u32[]{:S(2)}) %collective-permute-start.7) | collective-permute-done | bytes 45088 | tf_op jit(solution)/shard_map/ppermute | solution.py:95
  14.0 0.0 collective-permute-start.11
  14.0 0.4 %collective-permute-done.6 = f32[88,128]{1,0:T(8,128)S(1)} collective-permute-done((f32[88,128]{1,0:T(8,128)S(1)}, f32[88,128]{1,0:T(8,128)S(1)}, u32[]{:S(2)}, u32[]{:S(2)}) %collective-permute-start.6) | collective-permute-done | bytes 45088 | tf_op jit(solution)/shard_map/ppermute | solution.py:95
  14.4 1.2 %collective-permute-done.5 = f32[88,128]{1,0:T(8,128)S(1)} collective-permute-done((f32[88,128]{1,0:T(8,128)S(1)}, f32[88,128]{1,0:T(8,128)S(1)}, u32[]{:S(2)}, u32[]{:S(2)}) %collective-permute-start.5) | collective-permute-done | bytes 45088 | tf_op jit(solution)/shard_map/ppermute | solution.py:95
  15.6 0.0 collective-permute-done.4
  15.6 1.2 %collective-permute-start.9 = (f32[88,128]{1,0:T(8,128)S(1)}, f32[88,128]{1,0:T(8,128)S(1)}, u32[]{:S(2)}, u32[]{:S(2)}) collective-permute-start(f32[88,128]{1,0:T(8,128)S(1)} %add_add_fusion.1), channel_id=1, source_target_pairs={{0,17},{1,0},{2,19},{3,2},{4,21},{5,4},{6,23},{7,6},{8,25},{9,8},{... | collective-permute-start | bytes 135176 | tf_op jit(solution)/shard_map/ppermute | solution.py:95
  16.8 0.5 %shard_map.87.each = f32[16,128,128]{2,1,0:T(8,128)S(1)} custom-call(f32[1024,128]{1,0:T(8,128)S(1)} %get-tuple-element.44.x, f32[1024,128]{1,0:T(8,128)S(1)} %collective-permute-done.10.mate_x, f32[128,128]{1,0:T(8,128)S(1)} %get-tuple-element.45.moved, f32[128,128]{1,0:T(8,128)S(1)} %collective-permute-done.11.mate_moved), custom_call_target="tpu_custom_call" | custom-call | flops 402653184 | bytes 65536 | tf_op jit(solution)/shard_map/pallas_call | solution.py:52
  17.3 1.2 %collective-permute-done.9 = f32[88,128]{1,0:T(8,128)S(1)} collective-permute-done((f32[88,128]{1,0:T(8,128)S(1)}, f32[88,128]{1,0:T(8,128)S(1)}, u32[]{:S(2)}, u32[]{:S(2)}) %collective-permute-start.9) | collective-permute-done | bytes 45088 | tf_op jit(solution)/shard_map/ppermute | solution.py:95
  18.5 0.0 collective-permute-done.8
  18.5 0.3 shard_map.88
  18.9 2.0 %collective-permute-start.13 = (f32[144,128]{1,0:T(8,128)S(1)}, f32[144,128]{1,0:T(8,128)S(1)}, u32[]{:S(2)}, u32[]{:S(2)}) collective-permute-start(f32[144,128]{1,0:T(8,128)S(1)} %get-tuple-element.46), channel_id=1, source_target_pairs={{0,1},{1,2},{2,3},{3,0},{4,5},{5,6},{6,7},{7,4},{8,9},{9,10},{10,1... | collective-permute-start | bytes 221192 | tf_op jit(solution)/shard_map/ppermute | solution.py:95
  20.9 0.1 collective-permute-start.12
  21.0 0.4 %collective-permute-start.16 = (f32[128,128]{1,0:T(8,128)S(1)}, f32[128,128]{1,0:T(8,128)S(1)}, u32[]{:S(2)}, u32[]{:S(2)}) collective-permute-start(f32[128,128]{1,0:T(8,128)S(1)} %get-tuple-element.47.gram), channel_id=1, source_target_pairs={{0,1},{1,0},{2,3},{3,2},{4,5},{5,4},{6,7},{7,6},{8,9},{9,8},{10,11... | collective-permute-start | bytes 196616 | tf_op jit(solution)/shard_map/ppermute | solution.py:89
  21.4 0.1 collective-permute-start.15
  21.5 0.5 %collective-permute-start.14 = (f32[144,128]{1,0:T(8,128)S(1)}, f32[144,128]{1,0:T(8,128)S(1)}, u32[]{:S(2)}, u32[]{:S(2)}) collective-permute-start(f32[144,128]{1,0:T(8,128)S(1)} %get-tuple-element.46), channel_id=1, source_target_pairs={{0,1},{1,4},{2,3},{3,6},{4,5},{5,0},{6,7},{7,2},{8,9},{9,12},{10,1... | collective-permute-start | bytes 221192 | tf_op jit(solution)/shard_map/ppermute | solution.py:95
  22.0 0.3 collective-permute-done.16.mate_gram
  22.3 0.7 %shard_map.89 = (f32[128,128]{1,0:T(8,128)}, f32[1,128]{1,0:T(1,128)S(1)}, f32[128,128]{1,0:T(8,128)S(1)}) custom-call(f32[128,128]{1,0:T(8,128)S(1)} %get-tuple-element.47.gram, f32[128,128]{1,0:T(8,128)S(1)} %collective-permute-done.16.mate_gram, f32[128,128]{1,0:T(8,128)S(1)} %get-tuple-element.45.moved, ...), custom_call_target="tpu_custom_call" | custom-call | flops 131072 | bytes 65536 | tf_op jit(solution)/shard_map/pallas_call | solution.py:52
  23.0 0.3 collective-permute-done.13
  23.3 2.8 %collective-permute-done.15 = f32[144,128]{1,0:T(8,128)S(1)} collective-permute-done((f32[144,128]{1,0:T(8,128)S(1)}, f32[144,128]{1,0:T(8,128)S(1)}, u32[]{:S(2)}, u32[]{:S(2)}) %collective-permute-start.15) | collective-permute-done | bytes 73760 | tf_op jit(solution)/shard_map/ppermute | solution.py:95
  26.1 0.1 collective-permute-done.14
  26.1 1.0 %collective-permute-start.20 = (f32[128,128]{1,0:T(8,128)S(1)}, f32[128,128]{1,0:T(8,128)S(1)}, u32[]{:S(2)}, u32[]{:S(2)}) collective-permute-start(f32[128,128]{1,0:T(8,128)S(1)} %fusion), channel_id=1, source_target_pairs={{0,25},{1,0},{2,27},{3,2},{4,29},{5,4},{6,31},{7,6},{8,17},{9,8},{... | collective-permute-start | bytes 196616 | tf_op jit(solution)/shard_map/ppermute | solution.py:95
  27.2 1.0 %collective-permute-start.19 = (f32[128,128]{1,0:T(8,128)S(1)}, f32[128,128]{1,0:T(8,128)S(1)}, u32[]{:S(2)}, u32[]{:S(2)}) collective-permute-start(f32[128,128]{1,0:T(8,128)S(1)} %fusion), channel_id=1, source_target_pairs={{0,17},{1,0},{2,19},{3,2},{4,21},{5,4},{6,23},{7,6},{8,25},{9,8},{... | collective-permute-start | bytes 196616 | tf_op jit(solution)/shard_map/ppermute | solution.py:95
  28.2 0.5 %collective-permute-start.17 = (f32[128,128]{1,0:T(8,128)S(1)}, f32[128,128]{1,0:T(8,128)S(1)}, u32[]{:S(2)}, u32[]{:S(2)}) collective-permute-start(f32[128,128]{1,0:T(8,128)S(1)} %fusion), channel_id=1, source_target_pairs={{0,1},{1,0},{2,3},{3,2},{4,5},{5,4},{6,7},{7,6},{8,9},{9,8},{10,11... | collective-permute-start | bytes 196616 | tf_op jit(solution)/shard_map/ppermute | solution.py:89
  28.7 0.0 collective-permute-start.21
  28.7 1.2 %collective-permute-done.21.mate_rows = f32[32,128]{1,0:T(8,128)S(1)} collective-permute-done((f32[32,128]{1,0:T(8,128)S(1)}, f32[32,128]{1,0:T(8,128)S(1)}, u32[]{:S(2)}, u32[]{:S(2)}) %collective-permute-start.21) | collective-permute-done | bytes 16416 | tf_op jit(solution)/shard_map/ppermute | solution.py:89
  29.9 0.9 %shard_map.90 = (f32[8,128]{1,0:T(8,128)}, f32[128,128]{1,0:T(8,128)S(1)}, f32[1,128]{1,0:T(1,128)S(1)}, f32[1,128]{1,0:T(1,128)S(1)}) custom-call(f32[32,128]{1,0:T(8,128)S(1)} %pad_maximum_fusion.2.rows, f32[32,128]{1,0:T(8,128)S(1)} %collective-permute-done.21.mate_rows, f32[128,128]{1,0:T(8,128)S(1)} %get-tuple-element.39.c, ...), custom_call_target="tpu_custom_call" | custom-call | flops 16777216 | bytes 65536 | tf_op jit(solution)/shard_map/pallas_call | solution.py:52
  30.8 0.0 collective-permute-done.20
  30.8 0.0 collective-permute-done.19
  30.8 0.0 collective-permute-done.18
  30.8 1.5 %collective-permute-start.22 = (f32[128,128]{1,0:T(8,128)S(1)}, f32[128,128]{1,0:T(8,128)S(1)}, u32[]{:S(2)}, u32[]{:S(2)}) collective-permute-start(f32[128,128]{1,0:T(8,128)S(1)} %add_add_fusion.terms), channel_id=1, source_target_pairs={{0,1},{1,0},{2,3},{3,2},{4,5},{5,4},{6,7},{7,6},{8,9},{9,8},{10,11... | collective-permute-start | bytes 196616 | tf_op jit(solution)/shard_map/ppermute | solution.py:89
  32.4 0.9 %collective-permute-done.22.mate_terms = f32[128,128]{1,0:T(8,128)S(1)} collective-permute-done((f32[128,128]{1,0:T(8,128)S(1)}, f32[128,128]{1,0:T(8,128)S(1)}, u32[]{:S(2)}, u32[]{:S(2)}) %collective-permute-start.22) | collective-permute-done | bytes 65568 | tf_op jit(solution)/shard_map/ppermute | solution.py:89
  33.3 0.7 %shard_map.91 = (f32[128,128]{1,0:T(8,128)}, f32[1,128]{1,0:T(1,128)}) custom-call(f32[128,128]{1,0:T(8,128)S(1)} %add_add_fusion.terms, f32[128,128]{1,0:T(8,128)S(1)} %collective-permute-done.22.mate_terms, f32[128,128]{1,0:T(8,128)S(1)} %get-tuple-element.63.base, f32[1,128]{1,0:T(1,128)S(1)} %get-tuple-element.64.gain, f32[1,128]{1,0:T(1,128)S(1)} %get-tuple-element.65.scale), custom_call_target="tpu_custom_call" | custom-call | flops 131072 | bytes 65536 | tf_op jit(solution)/shard_map/pallas_call | solution.py:52
  (21 shorter events, 0.1 us)
Async XLA Ops:
  2.6 1.4 %collective-permute-start = (f32[136,128]{1,0:T(8,128)S(1)}, f32[136,128]{1,0:T(8,128)S(1)}, u32[]{:S(2)}, u32[]{:S(2)}) collective-permute-start(f32[136,128]{1,0:T(8,128)S(1)} %get-tuple-element.36), channel_id=1, source_target_pairs={{0,1},{1,0},{2,3},{3,2},{4,5},{5,4},{6,7},{7,6},{8,9},{9,8},{10,11... | collective-permute-start | bytes 208904 | tf_op jit(solution)/shard_map/ppermute | solution.py:89
  3.1 5.6 %collective-permute-start.3 = (f32[8,128,128]{2,1,0:T(8,128)S(1)}, f32[8,128,128]{2,1,0:T(8,128)S(1)}, u32[]{:S(2)}, u32[]{:S(2)}) collective-permute-start(f32[8,128,128]{2,1,0:T(8,128)S(1)} %get-tuple-element.41.con), channel_id=1, source_target_pairs={{0,1},{1,0},{2,3},{3,2},{4,5},{5,4},{6,7},{7,6},{8,9},{9,8},{10,11... | collective-permute-start | bytes 1572872 | tf_op jit(solution)/shard_map/ppermute | solution.py:89
  4.0 4.7 %collective-permute-start.2 = (f32[144,128]{1,0:T(8,128)S(1)}, f32[144,128]{1,0:T(8,128)S(1)}, u32[]{:S(2)}, u32[]{:S(2)}) collective-permute-start(f32[144,128]{1,0:T(8,128)S(1)} %pad_maximum_fusion), channel_id=1, source_target_pairs={{0,3},{1,0},{2,1},{3,2},{4,7},{5,4},{6,5},{7,6},{8,11},{9,8},{10,9... | collective-permute-start | bytes 221192 | tf_op jit(solution)/shard_map/ppermute | solution.py:95
  6.7 2.0 %collective-permute-start.1 = (f32[144,128]{1,0:T(8,128)S(1)}, f32[144,128]{1,0:T(8,128)S(1)}, u32[]{:S(2)}, u32[]{:S(2)}) collective-permute-start(f32[144,128]{1,0:T(8,128)S(1)} %pad_maximum_fusion), channel_id=1, source_target_pairs={{0,1},{1,0},{2,3},{3,2},{4,5},{5,4},{6,7},{7,6},{8,9},{9,8},{10,11... | collective-permute-start | bytes 221192 | tf_op jit(solution)/shard_map/ppermute | solution.py:89
  6.7 10.1 %collective-permute-start.10 = (f32[1024,128]{1,0:T(8,128)S(1)}, f32[1024,128]{1,0:T(8,128)S(1)}, u32[]{:S(2)}, u32[]{:S(2)}) collective-permute-start(f32[1024,128]{1,0:T(8,128)S(1)} %get-tuple-element.44.x), channel_id=1, source_target_pairs={{0,1},{1,0},{2,3},{3,2},{4,5},{5,4},{6,7},{7,6},{8,9},{9,8},{10,11... | collective-permute-start | bytes 1572872 | tf_op jit(solution)/shard_map/ppermute | solution.py:89
  9.5 4.6 %collective-permute-start.7 = (f32[88,128]{1,0:T(8,128)S(1)}, f32[88,128]{1,0:T(8,128)S(1)}, u32[]{:S(2)}, u32[]{:S(2)}) collective-permute-start(f32[88,128]{1,0:T(8,128)S(1)} %get-tuple-element.42), channel_id=1, source_target_pairs={{0,1},{1,12},{2,3},{3,14},{4,5},{5,8},{6,7},{7,10},{8,9},{9,4},{10... | collective-permute-start | bytes 135176 | tf_op jit(solution)/shard_map/ppermute | solution.py:95
  9.9 4.5 %collective-permute-start.6 = (f32[88,128]{1,0:T(8,128)S(1)}, f32[88,128]{1,0:T(8,128)S(1)}, u32[]{:S(2)}, u32[]{:S(2)}) collective-permute-start(f32[88,128]{1,0:T(8,128)S(1)} %get-tuple-element.42), channel_id=1, source_target_pairs={{0,1},{1,8},{2,3},{3,10},{4,5},{5,12},{6,7},{7,14},{8,9},{9,0},{10... | collective-permute-start | bytes 135176 | tf_op jit(solution)/shard_map/ppermute | solution.py:95
  12.1 3.5 %collective-permute-start.5 = (f32[88,128]{1,0:T(8,128)S(1)}, f32[88,128]{1,0:T(8,128)S(1)}, u32[]{:S(2)}, u32[]{:S(2)}) collective-permute-start(f32[88,128]{1,0:T(8,128)S(1)} %get-tuple-element.42), channel_id=1, source_target_pairs={{0,1},{1,4},{2,3},{3,6},{4,5},{5,0},{6,7},{7,2},{8,9},{9,12},{10,1... | collective-permute-start | bytes 135176 | tf_op jit(solution)/shard_map/ppermute | solution.py:95
  12.1 3.5 %collective-permute-start.4 = (f32[88,128]{1,0:T(8,128)S(1)}, f32[88,128]{1,0:T(8,128)S(1)}, u32[]{:S(2)}, u32[]{:S(2)}) collective-permute-start(f32[88,128]{1,0:T(8,128)S(1)} %get-tuple-element.42), channel_id=1, source_target_pairs={{0,1},{1,0},{2,3},{3,2},{4,5},{5,4},{6,7},{7,6},{8,9},{9,8},{10,11... | collective-permute-start | bytes 135176 | tf_op jit(solution)/shard_map/ppermute | solution.py:89
  14.0 2.8 %collective-permute-start.11 = (f32[128,128]{1,0:T(8,128)S(1)}, f32[128,128]{1,0:T(8,128)S(1)}, u32[]{:S(2)}, u32[]{:S(2)}) collective-permute-start(f32[128,128]{1,0:T(8,128)S(1)} %get-tuple-element.45.moved), channel_id=1, source_target_pairs={{0,1},{1,0},{2,3},{3,2},{4,5},{5,4},{6,7},{7,6},{8,9},{9,8},{10,11... | collective-permute-start | bytes 196616 | tf_op jit(solution)/shard_map/ppermute | solution.py:89
  15.6 2.9 %collective-permute-start.9 = (f32[88,128]{1,0:T(8,128)S(1)}, f32[88,128]{1,0:T(8,128)S(1)}, u32[]{:S(2)}, u32[]{:S(2)}) collective-permute-start(f32[88,128]{1,0:T(8,128)S(1)} %add_add_fusion.1), channel_id=1, source_target_pairs={{0,17},{1,0},{2,19},{3,2},{4,21},{5,4},{6,23},{7,6},{8,25},{9,8},{... | collective-permute-start | bytes 135176 | tf_op jit(solution)/shard_map/ppermute | solution.py:95
  16.8 1.7 %collective-permute-start.8 = (f32[88,128]{1,0:T(8,128)S(1)}, f32[88,128]{1,0:T(8,128)S(1)}, u32[]{:S(2)}, u32[]{:S(2)}) collective-permute-start(f32[88,128]{1,0:T(8,128)S(1)} %add_add_fusion.1), channel_id=1, source_target_pairs={{0,1},{1,0},{2,3},{3,2},{4,5},{5,4},{6,7},{7,6},{8,9},{9,8},{10,11... | collective-permute-start | bytes 135176 | tf_op jit(solution)/shard_map/ppermute | solution.py:89
  18.9 4.4 %collective-permute-start.13 = (f32[144,128]{1,0:T(8,128)S(1)}, f32[144,128]{1,0:T(8,128)S(1)}, u32[]{:S(2)}, u32[]{:S(2)}) collective-permute-start(f32[144,128]{1,0:T(8,128)S(1)} %get-tuple-element.46), channel_id=1, source_target_pairs={{0,1},{1,2},{2,3},{3,0},{4,5},{5,6},{6,7},{7,4},{8,9},{9,10},{10,1... | collective-permute-start | bytes 221192 | tf_op jit(solution)/shard_map/ppermute | solution.py:95
  20.9 2.4 %collective-permute-start.12 = (f32[144,128]{1,0:T(8,128)S(1)}, f32[144,128]{1,0:T(8,128)S(1)}, u32[]{:S(2)}, u32[]{:S(2)}) collective-permute-start(f32[144,128]{1,0:T(8,128)S(1)} %get-tuple-element.46), channel_id=1, source_target_pairs={{0,1},{1,0},{2,3},{3,2},{4,5},{5,4},{6,7},{7,6},{8,9},{9,8},{10,11... | collective-permute-start | bytes 221192 | tf_op jit(solution)/shard_map/ppermute | solution.py:89
  21.0 1.3 %collective-permute-start.16 = (f32[128,128]{1,0:T(8,128)S(1)}, f32[128,128]{1,0:T(8,128)S(1)}, u32[]{:S(2)}, u32[]{:S(2)}) collective-permute-start(f32[128,128]{1,0:T(8,128)S(1)} %get-tuple-element.47.gram), channel_id=1, source_target_pairs={{0,1},{1,0},{2,3},{3,2},{4,5},{5,4},{6,7},{7,6},{8,9},{9,8},{10,11... | collective-permute-start | bytes 196616 | tf_op jit(solution)/shard_map/ppermute | solution.py:89
  21.4 4.7 %collective-permute-start.15 = (f32[144,128]{1,0:T(8,128)S(1)}, f32[144,128]{1,0:T(8,128)S(1)}, u32[]{:S(2)}, u32[]{:S(2)}) collective-permute-start(f32[144,128]{1,0:T(8,128)S(1)} %get-tuple-element.46), channel_id=1, source_target_pairs={{0,1},{1,6},{2,3},{3,4},{4,5},{5,2},{6,7},{7,0},{8,9},{9,14},{10,1... | collective-permute-start | bytes 221192 | tf_op jit(solution)/shard_map/ppermute | solution.py:95
  21.5 4.7 %collective-permute-start.14 = (f32[144,128]{1,0:T(8,128)S(1)}, f32[144,128]{1,0:T(8,128)S(1)}, u32[]{:S(2)}, u32[]{:S(2)}) collective-permute-start(f32[144,128]{1,0:T(8,128)S(1)} %get-tuple-element.46), channel_id=1, source_target_pairs={{0,1},{1,4},{2,3},{3,6},{4,5},{5,0},{6,7},{7,2},{8,9},{9,12},{10,1... | collective-permute-start | bytes 221192 | tf_op jit(solution)/shard_map/ppermute | solution.py:95
  26.1 4.6 %collective-permute-start.20 = (f32[128,128]{1,0:T(8,128)S(1)}, f32[128,128]{1,0:T(8,128)S(1)}, u32[]{:S(2)}, u32[]{:S(2)}) collective-permute-start(f32[128,128]{1,0:T(8,128)S(1)} %fusion), channel_id=1, source_target_pairs={{0,25},{1,0},{2,27},{3,2},{4,29},{5,4},{6,31},{7,6},{8,17},{9,8},{... | collective-permute-start | bytes 196616 | tf_op jit(solution)/shard_map/ppermute | solution.py:95
  27.2 3.6 %collective-permute-start.19 = (f32[128,128]{1,0:T(8,128)S(1)}, f32[128,128]{1,0:T(8,128)S(1)}, u32[]{:S(2)}, u32[]{:S(2)}) collective-permute-start(f32[128,128]{1,0:T(8,128)S(1)} %fusion), channel_id=1, source_target_pairs={{0,17},{1,0},{2,19},{3,2},{4,21},{5,4},{6,23},{7,6},{8,25},{9,8},{... | collective-permute-start | bytes 196616 | tf_op jit(solution)/shard_map/ppermute | solution.py:95
  28.2 2.6 %collective-permute-start.18 = (f32[128,128]{1,0:T(8,128)S(1)}, f32[128,128]{1,0:T(8,128)S(1)}, u32[]{:S(2)}, u32[]{:S(2)}) collective-permute-start(f32[128,128]{1,0:T(8,128)S(1)} %fusion), channel_id=1, source_target_pairs={{0,9},{1,0},{2,11},{3,2},{4,13},{5,4},{6,15},{7,6},{8,1},{9,8},{10... | collective-permute-start | bytes 196616 | tf_op jit(solution)/shard_map/ppermute | solution.py:95
  28.2 2.6 %collective-permute-start.17 = (f32[128,128]{1,0:T(8,128)S(1)}, f32[128,128]{1,0:T(8,128)S(1)}, u32[]{:S(2)}, u32[]{:S(2)}) collective-permute-start(f32[128,128]{1,0:T(8,128)S(1)} %fusion), channel_id=1, source_target_pairs={{0,1},{1,0},{2,3},{3,2},{4,5},{5,4},{6,7},{7,6},{8,9},{9,8},{10,11... | collective-permute-start | bytes 196616 | tf_op jit(solution)/shard_map/ppermute | solution.py:89
  28.7 1.2 %collective-permute-start.21 = (f32[32,128]{1,0:T(8,128)S(1)}, f32[32,128]{1,0:T(8,128)S(1)}, u32[]{:S(2)}, u32[]{:S(2)}) collective-permute-start(f32[32,128]{1,0:T(8,128)S(1)} %pad_maximum_fusion.2.rows), channel_id=1, source_target_pairs={{0,1},{1,0},{2,3},{3,2},{4,5},{5,4},{6,7},{7,6},{8,9},{9,8},{10,11... | collective-permute-start | bytes 49160 | tf_op jit(solution)/shard_map/ppermute | solution.py:89
  30.8 2.4 %collective-permute-start.22 = (f32[128,128]{1,0:T(8,128)S(1)}, f32[128,128]{1,0:T(8,128)S(1)}, u32[]{:S(2)}, u32[]{:S(2)}) collective-permute-start(f32[128,128]{1,0:T(8,128)S(1)} %add_add_fusion.terms), channel_id=1, source_target_pairs={{0,1},{1,0},{2,3},{3,2},{4,5},{5,4},{6,7},{7,6},{8,9},{9,8},{10,11... | collective-permute-start | bytes 196616 | tf_op jit(solution)/shard_map/ppermute | solution.py:89

commit v11 on v9

--- a/solution.py
+++ b/solution.py
@@ -89,19 +89,11 @@
     return lax.ppermute(values, ALL, [(i, i ^ 1) for i in range(lax.axis_size(ALL))])
 
 
-def send(values, holder, mask):
-    count = lax.axis_size(ALL)
-    pairs = [(i, i ^ 1 ^ mask if i & 1 == holder else i ^ 1) for i in range(count)]
-    return lax.ppermute(values, ALL, pairs)
-
-
-def fan(values, holder, masks):
-    sent = [send(values, holder, mask) if mask else swap(values) for mask in reversed(masks)]
-    return sent[::-1]
+def exchange(values, mask, other_core=True):
+    return lax.ppermute(values, ALL, [(i, i ^ mask ^ other_core) for i in range(lax.axis_size(ALL))])
 
 
 def tree(parts):
-    parts = parts[::-1]
     while len(parts) > 1:
         parts = [a + b for a, b in zip(parts[::2], parts[1::2])]
     return parts[0]
@@ -109,10 +101,6 @@
 
 def smp_index():
     return lax.axis_index("smp")
-
-
-def on_core(core, own, got):
-    return jnp.where(smp_index() & 1 == core, own, got)
 
 
 def pack(gram):
@@ -135,12 +123,8 @@
     return jnp.concatenate([top, jnp.where(columns < half, turned[half:], corner)], axis=0)
 
 
-def in_order(rows, scratch, chips):
-    block = scratch.shape[0] // chips
-    chip = smp_index() // 2
-    for p in range(chips):
-        scratch[pl.ds(pl.multiple_of((chip ^ (chips - 1 - p)) * block, block), block), :] = rows[p * block : (p + 1) * block, :]
-    return scratch[...]
+def core_rows(core, rows, block=0):
+    return pl.ds(pl.multiple_of((2 * block + core) * rows, rows), rows)
 
 
 def per_device(ensemble, voxel_factor, sample_factor, time_factor, weights):
@@ -211,121 +195,135 @@
 
     got = swap(opened)
     terms = opened[:vox_rows] + got[:vox_rows]
-    rows_b = jnp.concatenate([got[vox_rows:], opened[vox_rows:]], axis=0)
-    holder = 1
+    own_b = jnp.concatenate([opened[vox_rows:], got[vox_rows:]], axis=0)
     for group in groups_of(chip_bits):
-        parts = fan(jnp.concatenate([terms, rows_b], axis=0), holder, masks_of(group))
+        packet = jnp.concatenate([terms, own_b], axis=0)
+        parts = [exchange(packet, mask) for mask in masks_of(group)[:-1]] + [packet]
         terms = tree([part[:vox_rows] for part in parts])
-        rows_b = jnp.concatenate([part[vox_rows:] for part in parts], axis=0)
-        holder ^= 1
-    voxel_core = holder
-    mate_con = swap(con)
-
-    half, sums_rows = rank // 2, rank // 2 + chip_rows
-
-    def voxel_kernel(terms, rows, a, w, outer_c, con, mate_con, moved_out, chip_b, out, all_b):
-        b = in_order(rows, all_b, chips)
-        chip_b[...] = all_b[pl.ds(pl.multiple_of(smp_index() // 2 * chip_rows, chip_rows), chip_rows), :]
+        own_b = jnp.concatenate([part[vox_rows:] for part in parts], axis=0)
+
+    half, rail = rank // 2, rank // 4
+
+    def voxel_kernel(terms, rows, a, w, outer_c, con, moved_out, chip_b, out, all_b, packed_all):
+        core, chip = smp_index() & 1, smp_index() // 2
+        for p in range(chips):
+            flip = chips - 1 - p
+            hops = sum(1 for group in groups_of(bits_of(chips)) if flip & sum(group))
+            for q in range(2):
+                place = core_rows(core ^ (hops & 1) ^ q, smp_rows, block=chip ^ flip)
+                start = (2 * p + q) * smp_rows
+                all_b[place, :] = rows[start : start + smp_rows, :]
+        b = all_b[...]
+        chip_b[...] = all_b[pl.ds(pl.multiple_of(chip * chip_rows, chip_rows), chip_rows), :]
         coupled = outer_c[...] * dot_rows(b, b)
         moved = a[...] - step_of(coupled) * (dot(a[...], coupled) - terms[...] * w[...])
         moved_out[...] = moved
         packed, diagonal = pack(dot_rows(moved, moved))
-        out[:half, :] = packed
-        for core in range(2):
-            for j in range(smp_rows):
-                row = half + core * smp_rows + j
-                out[row : row + 1, :] = jnp.sum((con if core == voxel_core else mate_con)[j] * moved, axis=0, keepdims=True)
-        out[sums_rows:, :] = jnp.broadcast_to(diagonal, (8, rank))
+        packed_all[...] = packed
+        out[:rail, :] = packed_all[core_rows(core, rail), :]
+        for j in range(smp_rows):
+            out[rail + j : rail + j + 1, :] = jnp.sum(con[j] * moved, axis=0, keepdims=True)
+        out[rail + smp_rows :, :] = jnp.broadcast_to(diagonal, (8, rank))
 
     moved_a, chip_b, sums = call(
         voxel_kernel,
-        (near(vox_rows, rank), near(chip_rows, rank), near(sums_rows + 8, rank)),
-        (terms, rows_b, a_near, w_row, outer_c, con, mate_con),
+        (near(vox_rows, rank), near(chip_rows, rank), near(rail + smp_rows + 8, rank)),
+        (terms, own_b, a_near, w_row, outer_c, con),
         2 * rank * rank * vox_rows * 12,
-        scratch=(near(smp_total, rank),),
-    )
-
-    mate_moved_a = swap(moved_a)
-
-    for group in groups_of(vox_bits):
-        sums = tree(fan(sums, holder, masks_of(group)))
-        holder ^= 1
-    sample_core = holder
-    if sample_core != voxel_core:
-        chip_b = swap(chip_b)
+        scratch=(near(smp_total, rank), near(half, rank)),
+    )
     mate_x = swap(x)
 
-    def time_kernel(x, mate_x, moved, mate_moved, each):
-        moved = on_core(voxel_core, moved[...], mate_moved[...])
-        for core in range(2):
+    turns = 0
+    groups = groups_of(vox_bits)
+    for group in groups[:-1]:
+        sums = tree([exchange(sums, mask) for mask in masks_of(group)])
+        turns ^= 1
+    masks = masks_of(groups[-1])
+    same = tree([exchange(sums, mask, False) for mask in masks[:-1]] + [sums])
+    other = tree([exchange(sums, mask) for mask in masks])
+
+    def time_kernel(x, mate_x, moved, each):
+        for i, source in enumerate((x, mate_x)):
             for j in range(smp_rows):
-                block = (x if core == sample_core else mate_x)[pl.ds(j, vox_rows, stride=smp_rows), :]
-                each[core * smp_rows + j] = dot_rows(block, moved)
+                block = source[pl.ds(j, vox_rows, stride=smp_rows), :]
+                each[i * smp_rows + j] = dot_rows(block, moved[...])
 
     (each,) = call(
-        time_kernel,
-        (near(chip_rows, times, rank),),
-        (x, mate_x, moved_a, mate_moved_a),
-        4 * flat_rows * times * rank * 6,
-    )
-
-    def sample_kernel(sums, b, w, outer_c, each, gram_out, out):
-        gram_out[...] = unpack(sums[:half, :], sums[sums_rows : sums_rows + 1, :])
+        time_kernel, (near(chip_rows, times, rank),), (x, mate_x, moved_a), 4 * flat_rows * times * rank * 4
+    )
+
+    time_half = times // 2
+
+    def sample_kernel(same, other, b, w, outer_c, each, gram_out, out, packed, raw, moved_all):
+        core = smp_index() & 1
+        for part, owner in ((same, core ^ turns), (other, core ^ turns ^ 1)):
+            packed[core_rows(owner, rail), :] = part[:rail, :]
+            raw[core_rows(owner, smp_rows), :] = part[rail : rail + smp_rows, :]
+        gram_out[...] = unpack(packed[...], same[rail + smp_rows : rail + smp_rows + 1, :])
         coupled = outer_c[...] * gram_out[...]
-        moved = b[...] - step_of(coupled) * (dot(b[...], coupled) - sums[half:sums_rows, :] * w[...])
-        out[times:, :] = moved
+        moved_all[...] = b[...] - step_of(coupled) * (dot(b[...], coupled) - raw[...] * w[...])
         total = None
-        for j in range(chip_rows):
-            made = each[j] * moved[j : j + 1, :]
-            total = made if total is None else total + made
-        out[:times, :] = total
+        for i in range(2):
+            moved = moved_all[core_rows(core ^ i, smp_rows), :]
+            if i == 0:
+                out[time_half:, :] = moved
+            for j in range(smp_rows):
+                made = each[i * smp_rows + j, core_rows(core, time_half), :] * moved[j : j + 1, :]
+                total = made if total is None else total + made
+        out[:time_half, :] = total
 
     gram_a, payload = call(
         sample_kernel,
-        (near(rank, rank), near(times + chip_rows, rank)),
-        (sums, chip_b, w_row, outer_c, each),
-        2 * rank * rank * chip_rows * 6,
-    )
-    mate_gram_a = swap(gram_a)
-
-    def scale_kernel(gram, mate_gram, moved, mate_moved, outer, result, scales_out, weighed):
-        gram = on_core(sample_core, gram[...], mate_gram[...])
-        scales = jnp.sqrt(diagonal_row(gram) / vox_total + 1e-06)
+        (near(rank, rank), near(time_half + smp_rows, rank)),
+        (same, other, chip_b, w_row, outer_c, each),
+        2 * rank * rank * chip_rows * 4,
+        scratch=(near(half, rank), near(chip_rows, rank), near(chip_rows, rank)),
+    )
+
+    def scale_kernel(gram, moved, outer, result, scales_out, weighed):
+        scales = jnp.sqrt(diagonal_row(gram[...]) / vox_total + 1e-06)
         scales_out[...] = scales
-        result[...] = on_core(voxel_core, moved[...], mate_moved[...]) / scales
-        weighed[...] = outer[...] * gram
+        result[...] = moved[...] / scales
+        weighed[...] = outer[...] * gram[...]
 
     voxel_result, scales_a, weighed = call(
         scale_kernel,
         (far(vox_rows, rank), near(1, rank), near(rank, rank)),
-        (gram_a, mate_gram_a, moved_a, mate_moved_a, outer),
+        (gram_a, moved_a, outer),
         vox_rows * rank * 8,
     )
 
-    terms, rows_b, rows_core = payload[:times], payload[times:], holder
+    terms, rows_b = payload[:time_half], payload[time_half:]
+    turns = rows_turns = 0
     smp_mask = sum(chip_bits)
     for group in groups_of(chip_bits + vox_bits):
         masks = masks_of(group)
         with_rows = any(mask & smp_mask for mask in masks)
-        parts = fan(jnp.concatenate([terms, rows_b], axis=0) if with_rows else terms, holder, masks)
-        terms = tree([part[:times] for part in parts])
-        holder ^= 1
+        packet = jnp.concatenate([terms, rows_b], axis=0) if with_rows else terms
+        parts = [exchange(packet, mask) for mask in masks]
+        terms = tree([part[:time_half] for part in parts])
+        turns ^= 1
         if with_rows:
             parts = [part for part, mask in zip(parts, masks) if not mask & ~smp_mask]
-            rows_b = jnp.concatenate([part[times:] for part in parts], axis=0)
-            rows_core = holder
-    last_core = holder
+            rows_b = jnp.concatenate([part[time_half:] for part in parts], axis=0)
+            rows_turns ^= 1
     mate_rows_b = swap(rows_b)
 
     def ready_kernel(rows, mate_rows, c, w, weighed, scales_a, b_out, base, gain, scale, all_b):
-        b = in_order(on_core(rows_core, rows[...], mate_rows[...]), all_b, chips)
+        core, chip = smp_index() & 1, smp_index() // 2
+        for part, owner in ((rows, core ^ rows_turns), (mate_rows, core ^ rows_turns ^ 1)):
+            for p in range(chips):
+                place = core_rows(owner, smp_rows, block=chip ^ (chips - 1 - p))
+                all_b[place, :] = part[p * smp_rows : (p + 1) * smp_rows, :]
+        b = all_b[...]
         coupled = weighed[...] * dot_rows(b, b)
         step = step_of(coupled)
         base[...] = c[...] - step * dot(c[...], coupled)
         gain[...] = step * w[...]
         scales_b = jnp.sqrt(jnp.sum(b * b, axis=0, keepdims=True) / smp_total + 1e-06)
         scale[...] = w[...] * scales_a[...] * scales_b
-        b_out[...] = all_b[pl.ds(pl.multiple_of(smp_index() * smp_rows, smp_rows), smp_rows), :] / scales_b
+        b_out[...] = all_b[core_rows(core, smp_rows, block=chip), :] / scales_b
 
     sample_result, base, gain, scale = call(
         ready_kernel,
@@ -339,8 +337,11 @@
     )
     mate_terms = swap(terms)
 
-    def last_kernel(terms, mate_terms, base, gain, scale, c_out, w_out):
-        moved = base[...] + on_core(last_core, terms[...], mate_terms[...]) * gain[...]
+    def last_kernel(terms, mate_terms, base, gain, scale, c_out, w_out, summed):
+        owner = smp_index() & 1 ^ turns
+        summed[core_rows(owner, time_half), :] = terms[...]
+        summed[core_rows(owner ^ 1, time_half), :] = mate_terms[...]
+        moved = base[...] + summed[...] * gain[...]
         scales_c = jnp.sqrt(jnp.sum(moved * moved, axis=0, keepdims=True) / times + 1e-06)
         c_out[...] = moved / scales_c
         w_out[...] = scale[...] * scales_c
@@ -350,6 +351,7 @@
         (far(times, rank), far(1, rank)),
         (terms, mate_terms, base, gain, scale),
         rank * times * 8,
+        scratch=(near(times, rank),),
     )
     return voxel_result, sample_result, time_result, scale_result.reshape(rank)
 

time: 32.9 us -> 39.7 us (1.21)
  waiting for transfers between devices: 9.41 us -> 13.2 us
  starting transfers between devices: 15.8 us -> 18.9 us
    ppermute x11 -> x16, starting transfers between devices: 8.32 us -> 17.2 us  [exchange(): lax.ppermute(values, ALL, [(i, i ^ mask ^ other_core) for i in range(lax....]
    ppermute x12 -> x4, starting transfers between devices: 7.48 us -> 1.73 us  [swap(): lax.ppermute(values, ALL, [(i, i ^ 1) for i in range(lax.axis_size(ALL))])]
    ppermute x11 -> x16, waiting for transfers between devices: 7.16 us -> 11.3 us  [exchange(): lax.ppermute(values, ALL, [(i, i ^ mask ^ other_core) for i in range(lax....]
    ppermute x12 -> x4, waiting for transfers between devices: 2.25 us -> 1.92 us  [swap(): lax.ppermute(values, ALL, [(i, i ^ 1) for i in range(lax.axis_size(ALL))])]
  transfers between devices with their start and end apart: 23 -> 20, of which waited for: 9 -> 11; matrix products, arithmetic and copies ran while one was open for 0% -> 0% of each run, Pallas kernels for 9% -> 6%
where the time goes in v11:
time: 39.7 us; the launch traced here: 39.5 us
  starting transfers between devices  18.9 us (48%)
  waiting for transfers between devices  13.2 us (33%)
  Pallas kernels  5.88 us (15%)
  between operations  0.75 us (2%)
  local copies, waits for them, and re-layouts  0.7 us (2%)
    ppermute x16, starting transfers between devices, exchange(): lax.ppermute(values, ALL, [(i, i ^ mask ^ other_core) for i in range(lax....  17.2 us
    ppermute x16, waiting for transfers between devices, exchange(): lax.ppermute(values, ALL, [(i, i ^ mask ^ other_core) for i in range(lax....  11.3 us
    pallas_call x8, Pallas kernels, call(): pl.pallas_call(kernel, out_shape=outs, in_specs=specs, out_specs=[pl.Bloc...  5.88 us
    ppermute x4, waiting for transfers between devices, swap(): lax.ppermute(values, ALL, [(i, i ^ 1) for i in range(lax.axis_size(ALL))])  1.92 us
    ppermute x4, starting transfers between devices, swap(): lax.ppermute(values, ALL, [(i, i ^ 1) for i in range(lax.axis_size(ALL))])  1.73 us
  transfers between devices with their start and end apart: 20, of which 11 were waited for; matrix products, arithmetic and copies ran while one was open for 0% of the time, Pallas kernels for 6%

profile of v11, /device:TPU:0, one launch (start us, length us, event | category | flops | bytes accessed | tf_op | source)
XLA Modules:
  0.0 39.5 jit_solution(12952186457928971676)
XLA Ops:
  0.6 1.9 %shard_map.84 = (f32[1024,128]{1,0:T(8,128)S(1)}, f32[128,128]{1,0:T(8,128)S(1)}, f32[128,128]{1,0:T(8,128)S(1)}, f32[1,128]{1,0:T(1,128)S(1)}, f32[136,128]{1,0:T(8,128)S(1)}, /*index=5*/f32[8,128,128]{2,1,0:T(8,128)S(1)}) custom-call(f32[1024,128]{1,0:T(8,128)} %bitcast.3, f32[128,128]{1,0:T(8,128)} %c_hbm.1, f32[8,128]{1,0:T(8,128)} %b_hbm.1, ...), custom_call_target="tpu_custom_call" | custom-call | flops 201326592 | bytes 65536 | tf_op jit(solution)/shard_map/pallas_call | solution.py:52
  2.6 0.5 %collective-permute-start = (f32[136,128]{1,0:T(8,128)S(1)}, f32[136,128]{1,0:T(8,128)S(1)}, u32[]{:S(2)}, u32[]{:S(2)}) collective-permute-start(f32[136,128]{1,0:T(8,128)S(1)} %get-tuple-element.32), channel_id=1, source_target_pairs={{0,1},{1,0},{2,3},{3,2},{4,5},{5,4},{6,7},{7,6},{8,9},{9,8},{10,11... | collective-permute-start | bytes 208904 | tf_op jit(solution)/shard_map/ppermute | solution.py:89
  3.1 0.9 %collective-permute-done = f32[136,128]{1,0:T(8,128)S(1)} collective-permute-done((f32[136,128]{1,0:T(8,128)S(1)}, f32[136,128]{1,0:T(8,128)S(1)}, u32[]{:S(2)}, u32[]{:S(2)}) %collective-permute-start) | collective-permute-done | bytes 69664 | tf_op jit(solution)/shard_map/ppermute | solution.py:89
  4.0 2.7 %collective-permute-start.1 = (f32[144,128]{1,0:T(8,128)S(1)}, f32[144,128]{1,0:T(8,128)S(1)}, u32[]{:S(2)}, u32[]{:S(2)}) collective-permute-start(f32[144,128]{1,0:T(8,128)S(1)} %pad_maximum_fusion), channel_id=1, source_target_pairs={{0,3},{1,2},{2,1},{3,0},{4,7},{5,6},{6,5},{7,4},{8,11},{9,10},{10,... | collective-permute-start | bytes 221192 | tf_op jit(solution)/shard_map/ppermute | solution.py:93
  6.7 0.4 collective-permute-start.9
  7.1 0.2 shard_map.85
  7.3 1.8 %collective-permute-done.1 = f32[144,128]{1,0:T(8,128)S(1)} collective-permute-done((f32[144,128]{1,0:T(8,128)S(1)}, f32[144,128]{1,0:T(8,128)S(1)}, u32[]{:S(2)}, u32[]{:S(2)}) %collective-permute-start.1) | collective-permute-done | bytes 73760 | tf_op jit(solution)/shard_map/ppermute | solution.py:93
  9.1 0.7 %shard_map.86 = (f32[128,128]{1,0:T(8,128)S(1)}, f32[16,128]{1,0:T(8,128)S(1)}, f32[48,128]{1,0:T(8,128)S(1)}) custom-call(f32[128,128]{1,0:T(8,128)S(1)} %slice_add_fusion.terms, f32[32,128]{1,0:T(8,128)S(1)} %pad_maximum_fusion.1.rows, f32[128,128]{1,0:T(8,128)S(1)} %get-tuple-element.33.a, f32[1,128]{1,0:T(1,128)S(1)} %get-tuple-element.34.w, ...), custom_call_target="tpu_custom_call" | custom-call | flops 50331648 | bytes 65536 | tf_op jit(solution)/shard_map/pallas_call | solution.py:52
  9.8 2.9 %collective-permute-start.2 = (f32[48,128]{1,0:T(8,128)S(1)}, f32[48,128]{1,0:T(8,128)S(1)}, u32[]{:S(2)}, u32[]{:S(2)}) collective-permute-start(f32[48,128]{1,0:T(8,128)S(1)} %get-tuple-element.38), channel_id=1, source_target_pairs={{0,13},{1,12},{2,15},{3,14},{4,9},{5,8},{6,11},{7,10},{8,5},{9,4},... | collective-permute-start | bytes 73736 | tf_op jit(solution)/shard_map/ppermute | solution.py:93
  12.7 0.4 %collective-permute-start.3 = (f32[48,128]{1,0:T(8,128)S(1)}, f32[48,128]{1,0:T(8,128)S(1)}, u32[]{:S(2)}, u32[]{:S(2)}) collective-permute-start(f32[48,128]{1,0:T(8,128)S(1)} %get-tuple-element.38), channel_id=1, source_target_pairs={{0,9},{1,8},{2,11},{3,10},{4,13},{5,12},{6,15},{7,14},{8,1},{9,0},... | collective-permute-start | bytes 73736 | tf_op jit(solution)/shard_map/ppermute | solution.py:93
  13.1 0.2 collective-permute-start.4
  13.3 0.2 collective-permute-start.5
  13.5 0.8 %collective-permute-done.2 = f32[48,128]{1,0:T(8,128)S(1)} collective-permute-done((f32[48,128]{1,0:T(8,128)S(1)}, f32[48,128]{1,0:T(8,128)S(1)}, u32[]{:S(2)}, u32[]{:S(2)}) %collective-permute-start.2) | collective-permute-done | bytes 24608 | tf_op jit(solution)/shard_map/ppermute | solution.py:93
  14.2 1.7 %collective-permute-done.3 = f32[48,128]{1,0:T(8,128)S(1)} collective-permute-done((f32[48,128]{1,0:T(8,128)S(1)}, f32[48,128]{1,0:T(8,128)S(1)}, u32[]{:S(2)}, u32[]{:S(2)}) %collective-permute-start.3) | collective-permute-done | bytes 24608 | tf_op jit(solution)/shard_map/ppermute | solution.py:93
  16.0 0.4 %collective-permute-done.4 = f32[48,128]{1,0:T(8,128)S(1)} collective-permute-done((f32[48,128]{1,0:T(8,128)S(1)}, f32[48,128]{1,0:T(8,128)S(1)}, u32[]{:S(2)}, u32[]{:S(2)}) %collective-permute-start.4) | collective-permute-done | bytes 24608 | tf_op jit(solution)/shard_map/ppermute | solution.py:93
  16.4 0.0 collective-permute-done.5
  16.4 2.6 %collective-permute-start.6 = (f32[48,128]{1,0:T(8,128)S(1)}, f32[48,128]{1,0:T(8,128)S(1)}, u32[]{:S(2)}, u32[]{:S(2)}) collective-permute-start(f32[48,128]{1,0:T(8,128)S(1)} %add_add_fusion.1), channel_id=1, source_target_pairs={{0,16},{1,17},{2,18},{3,19},{4,20},{5,21},{6,22},{7,23},{8,24},{9,... | collective-permute-start | bytes 73736 | tf_op jit(solution)/shard_map/ppermute | solution.py:93
  19.0 0.0 collective-permute-start.7
  19.0 0.5 %collective-permute-start.8 = (f32[48,128]{1,0:T(8,128)S(1)}, f32[48,128]{1,0:T(8,128)S(1)}, u32[]{:S(2)}, u32[]{:S(2)}) collective-permute-start(f32[48,128]{1,0:T(8,128)S(1)} %add_add_fusion.1), channel_id=1, source_target_pairs={{0,1},{1,0},{2,3},{3,2},{4,5},{5,4},{6,7},{7,6},{8,9},{9,8},{10,11... | collective-permute-start | bytes 73736 | tf_op jit(solution)/shard_map/ppermute | solution.py:93
  19.5 1.7 %collective-permute-done.6 = f32[48,128]{1,0:T(8,128)S(1)} collective-permute-done((f32[48,128]{1,0:T(8,128)S(1)}, f32[48,128]{1,0:T(8,128)S(1)}, u32[]{:S(2)}, u32[]{:S(2)}) %collective-permute-start.6) | collective-permute-done | bytes 24608 | tf_op jit(solution)/shard_map/ppermute | solution.py:93
  21.2 2.2 %collective-permute-done.7 = f32[48,128]{1,0:T(8,128)S(1)} collective-permute-done((f32[48,128]{1,0:T(8,128)S(1)}, f32[48,128]{1,0:T(8,128)S(1)}, u32[]{:S(2)}, u32[]{:S(2)}) %collective-permute-start.7) | collective-permute-done | bytes 24608 | tf_op jit(solution)/shard_map/ppermute | solution.py:93
  23.4 0.0 collective-permute-done.8
  23.4 0.0 collective-permute-done.9.mate_x
  23.4 0.5 %shard_map.87.each = f32[16,128,128]{2,1,0:T(8,128)S(1)} custom-call(f32[1024,128]{1,0:T(8,128)S(1)} %get-tuple-element.40.x, f32[1024,128]{1,0:T(8,128)S(1)} %collective-permute-done.9.mate_x, f32[128,128]{1,0:T(8,128)S(1)} %get-tuple-element.41.moved), custom_call_target="tpu_custom_call" | custom-call | flops 268435456 | bytes 65536 | tf_op jit(solution)/shard_map/pallas_call | solution.py:52
  23.9 0.3 shard_map.88
  24.3 1.3 %collective-permute-start.12 = (f32[72,128]{1,0:T(8,128)S(1)}, f32[72,128]{1,0:T(8,128)S(1)}, u32[]{:S(2)}, u32[]{:S(2)}) collective-permute-start(f32[72,128]{1,0:T(8,128)S(1)} %get-tuple-element.42), channel_id=1, source_target_pairs={{0,3},{1,2},{2,1},{3,0},{4,7},{5,6},{6,5},{7,4},{8,11},{9,10},{10,... | collective-permute-start | bytes 110600 | tf_op jit(solution)/shard_map/ppermute | solution.py:93
  25.6 0.4 collective-permute-start.13
  26.0 0.2 collective-permute-start.10
  26.2 1.5 %collective-permute-start.11 = (f32[72,128]{1,0:T(8,128)S(1)}, f32[72,128]{1,0:T(8,128)S(1)}, u32[]{:S(2)}, u32[]{:S(2)}) collective-permute-start(f32[72,128]{1,0:T(8,128)S(1)} %get-tuple-element.42), channel_id=1, source_target_pairs={{0,5},{1,4},{2,7},{3,6},{4,1},{5,0},{6,3},{7,2},{8,13},{9,12},{10,... | collective-permute-start | bytes 110600 | tf_op jit(solution)/shard_map/ppermute | solution.py:93
  27.6 0.1 collective-permute-done.12
  27.8 0.0 collective-permute-done.13
  27.8 2.5 %collective-permute-done.10 = f32[72,128]{1,0:T(8,128)S(1)} collective-permute-done((f32[72,128]{1,0:T(8,128)S(1)}, f32[72,128]{1,0:T(8,128)S(1)}, u32[]{:S(2)}, u32[]{:S(2)}) %collective-permute-start.10) | collective-permute-done | bytes 36896 | tf_op jit(solution)/shard_map/ppermute | solution.py:93
  30.3 0.0 collective-permute-done.11
  30.3 2.2 %collective-permute-start.14 = (f32[64,128]{1,0:T(8,128)S(1)}, f32[64,128]{1,0:T(8,128)S(1)}, u32[]{:S(2)}, u32[]{:S(2)}) collective-permute-start(f32[64,128]{1,0:T(8,128)S(1)} %fusion), channel_id=1, source_target_pairs={{0,25},{1,24},{2,27},{3,26},{4,29},{5,28},{6,31},{7,30},{8,17},{9,... | collective-permute-start | bytes 98312 | tf_op jit(solution)/shard_map/ppermute | solution.py:93
  32.5 0.6 %collective-permute-start.15 = (f32[64,128]{1,0:T(8,128)S(1)}, f32[64,128]{1,0:T(8,128)S(1)}, u32[]{:S(2)}, u32[]{:S(2)}) collective-permute-start(f32[64,128]{1,0:T(8,128)S(1)} %fusion), channel_id=1, source_target_pairs={{0,17},{1,16},{2,19},{3,18},{4,21},{5,20},{6,23},{7,22},{8,25},{9,... | collective-permute-start | bytes 98312 | tf_op jit(solution)/shard_map/ppermute | solution.py:93
  33.2 1.4 %collective-permute-start.16 = (f32[64,128]{1,0:T(8,128)S(1)}, f32[64,128]{1,0:T(8,128)S(1)}, u32[]{:S(2)}, u32[]{:S(2)}) collective-permute-start(f32[64,128]{1,0:T(8,128)S(1)} %fusion), channel_id=1, source_target_pairs={{0,9},{1,8},{2,11},{3,10},{4,13},{5,12},{6,15},{7,14},{8,1},{9,0},... | collective-permute-start | bytes 98312 | tf_op jit(solution)/shard_map/ppermute | solution.py:93
  34.6 0.1 collective-permute-start.17
  34.6 0.7 %slice-done = f32[8,128]{1,0:T(8,128)S(1)} async-done(((f32[72,128]{1,0:T(8,128)}), f32[8,128]{1,0:T(8,128)S(1)}, s32[]{:S(2)}) %slice-start) | async-done | bytes 4120 | tf_op jit(solution)/shard_map/slice | solution.py:309
  35.3 0.4 %collective-permute-start.18 = (f32[16,128]{1,0:T(8,128)S(1)}, f32[16,128]{1,0:T(8,128)S(1)}, u32[]{:S(2)}, u32[]{:S(2)}) collective-permute-start(f32[16,128]{1,0:T(8,128)S(1)} %pad_maximum_fusion.2.rows), channel_id=1, source_target_pairs={{0,1},{1,0},{2,3},{3,2},{4,5},{5,4},{6,7},{7,6},{8,9},{9,8},{10,11... | collective-permute-start | bytes 24584 | tf_op jit(solution)/shard_map/ppermute | solution.py:89
  35.8 0.7 %shard_map.89 = (f32[128,128]{1,0:T(8,128)}, f32[1,128]{1,0:T(1,128)S(1)}, f32[128,128]{1,0:T(8,128)S(1)}) custom-call(f32[128,128]{1,0:T(8,128)S(1)} %get-tuple-element.43.gram, f32[128,128]{1,0:T(8,128)S(1)} %get-tuple-element.41.moved, f32[128,128]{1,0:T(8,128)S(1)} %get-tuple-element.44.outer), custom_call_target="tpu_custom_call" | custom-call | flops 131072 | bytes 65536 | tf_op jit(solution)/shard_map/pallas_call | solution.py:52
  36.5 0.2 collective-permute-done.18.mate_rows
  36.6 0.9 %shard_map.90 = (f32[8,128]{1,0:T(8,128)}, f32[128,128]{1,0:T(8,128)S(1)}, f32[1,128]{1,0:T(1,128)S(1)}, f32[1,128]{1,0:T(1,128)S(1)}) custom-call(f32[16,128]{1,0:T(8,128)S(1)} %pad_maximum_fusion.2.rows, f32[16,128]{1,0:T(8,128)S(1)} %collective-permute-done.18.mate_rows, f32[128,128]{1,0:T(8,128)S(1)} %get-tuple-element.35.c, ...), custom_call_target="tpu_custom_call" | custom-call | flops 16777216 | bytes 65536 | tf_op jit(solution)/shard_map/pallas_call | solution.py:52
  37.5 0.0 collective-permute-done.14
  37.5 0.0 collective-permute-done.15
  37.5 0.0 collective-permute-done.17
  37.5 0.4 %collective-permute-start.19 = (f32[64,128]{1,0:T(8,128)S(1)}, f32[64,128]{1,0:T(8,128)S(1)}, u32[]{:S(2)}, u32[]{:S(2)}) collective-permute-start(f32[64,128]{1,0:T(8,128)S(1)} %add_add_fusion.terms), channel_id=1, source_target_pairs={{0,1},{1,0},{2,3},{3,2},{4,5},{5,4},{6,7},{7,6},{8,9},{9,8},{10,11... | collective-permute-start | bytes 98312 | tf_op jit(solution)/shard_map/ppermute | solution.py:89
  37.9 0.9 %collective-permute-done.19.mate_terms = f32[64,128]{1,0:T(8,128)S(1)} collective-permute-done((f32[64,128]{1,0:T(8,128)S(1)}, f32[64,128]{1,0:T(8,128)S(1)}, u32[]{:S(2)}, u32[]{:S(2)}) %collective-permute-start.19) | collective-permute-done | bytes 32800 | tf_op jit(solution)/shard_map/ppermute | solution.py:89
  38.8 0.7 %shard_map.91 = (f32[128,128]{1,0:T(8,128)}, f32[1,128]{1,0:T(1,128)}) custom-call(f32[64,128]{1,0:T(8,128)S(1)} %add_add_fusion.terms, f32[64,128]{1,0:T(8,128)S(1)} %collective-permute-done.19.mate_terms, f32[128,128]{1,0:T(8,128)S(1)} %get-tuple-element.55.base, f32[1,128]{1,0:T(1,128)S(1)} %get-tuple-element.56.gain, f32[1,128]{1,0:T(1,128)S(1)} %get-tuple-element.57.scale), custom_call_target="tpu_custom_call" | custom-call | flops 131072 | bytes 65536 | tf_op jit(solution)/shard_map/pallas_call | solution.py:52
  (18 shorter events, 0.1 us)
Async XLA Ops:
  2.6 1.4 %collective-permute-start = (f32[136,128]{1,0:T(8,128)S(1)}, f32[136,128]{1,0:T(8,128)S(1)}, u32[]{:S(2)}, u32[]{:S(2)}) collective-permute-start(f32[136,128]{1,0:T(8,128)S(1)} %get-tuple-element.32), channel_id=1, source_target_pairs={{0,1},{1,0},{2,3},{3,2},{4,5},{5,4},{6,7},{7,6},{8,9},{9,8},{10,11... | collective-permute-start | bytes 208904 | tf_op jit(solution)/shard_map/ppermute | solution.py:89
  4.0 5.1 %collective-permute-start.1 = (f32[144,128]{1,0:T(8,128)S(1)}, f32[144,128]{1,0:T(8,128)S(1)}, u32[]{:S(2)}, u32[]{:S(2)}) collective-permute-start(f32[144,128]{1,0:T(8,128)S(1)} %pad_maximum_fusion), channel_id=1, source_target_pairs={{0,3},{1,2},{2,1},{3,0},{4,7},{5,6},{6,5},{7,4},{8,11},{9,10},{10,... | collective-permute-start | bytes 221192 | tf_op jit(solution)/shard_map/ppermute | solution.py:93
  6.7 16.7 %collective-permute-start.9 = (f32[1024,128]{1,0:T(8,128)S(1)}, f32[1024,128]{1,0:T(8,128)S(1)}, u32[]{:S(2)}, u32[]{:S(2)}) collective-permute-start(f32[1024,128]{1,0:T(8,128)S(1)} %get-tuple-element.40.x), channel_id=1, source_target_pairs={{0,1},{1,0},{2,3},{3,2},{4,5},{5,4},{6,7},{7,6},{8,9},{9,8},{10,11... | collective-permute-start | bytes 1572872 | tf_op jit(solution)/shard_map/ppermute | solution.py:89
  9.8 4.5 %collective-permute-start.2 = (f32[48,128]{1,0:T(8,128)S(1)}, f32[48,128]{1,0:T(8,128)S(1)}, u32[]{:S(2)}, u32[]{:S(2)}) collective-permute-start(f32[48,128]{1,0:T(8,128)S(1)} %get-tuple-element.38), channel_id=1, source_target_pairs={{0,13},{1,12},{2,15},{3,14},{4,9},{5,8},{6,11},{7,10},{8,5},{9,4},... | collective-permute-start | bytes 73736 | tf_op jit(solution)/shard_map/ppermute | solution.py:93
  12.7 3.3 %collective-permute-start.3 = (f32[48,128]{1,0:T(8,128)S(1)}, f32[48,128]{1,0:T(8,128)S(1)}, u32[]{:S(2)}, u32[]{:S(2)}) collective-permute-start(f32[48,128]{1,0:T(8,128)S(1)} %get-tuple-element.38), channel_id=1, source_target_pairs={{0,9},{1,8},{2,11},{3,10},{4,13},{5,12},{6,15},{7,14},{8,1},{9,0},... | collective-permute-start | bytes 73736 | tf_op jit(solution)/shard_map/ppermute | solution.py:93
  13.1 3.3 %collective-permute-start.4 = (f32[48,128]{1,0:T(8,128)S(1)}, f32[48,128]{1,0:T(8,128)S(1)}, u32[]{:S(2)}, u32[]{:S(2)}) collective-permute-start(f32[48,128]{1,0:T(8,128)S(1)} %get-tuple-element.38), channel_id=1, source_target_pairs={{0,5},{1,4},{2,7},{3,6},{4,1},{5,0},{6,3},{7,2},{8,13},{9,12},{10,... | collective-permute-start | bytes 73736 | tf_op jit(solution)/shard_map/ppermute | solution.py:93
  13.3 3.1 %collective-permute-start.5 = (f32[48,128]{1,0:T(8,128)S(1)}, f32[48,128]{1,0:T(8,128)S(1)}, u32[]{:S(2)}, u32[]{:S(2)}) collective-permute-start(f32[48,128]{1,0:T(8,128)S(1)} %get-tuple-element.38), channel_id=1, source_target_pairs={{0,1},{1,0},{2,3},{3,2},{4,5},{5,4},{6,7},{7,6},{8,9},{9,8},{10,11... | collective-permute-start | bytes 73736 | tf_op jit(solution)/shard_map/ppermute | solution.py:93
  16.4 4.8 %collective-permute-start.6 = (f32[48,128]{1,0:T(8,128)S(1)}, f32[48,128]{1,0:T(8,128)S(1)}, u32[]{:S(2)}, u32[]{:S(2)}) collective-permute-start(f32[48,128]{1,0:T(8,128)S(1)} %add_add_fusion.1), channel_id=1, source_target_pairs={{0,16},{1,17},{2,18},{3,19},{4,20},{5,21},{6,22},{7,23},{8,24},{9,... | collective-permute-start | bytes 73736 | tf_op jit(solution)/shard_map/ppermute | solution.py:93
  19.0 4.4 %collective-permute-start.7 = (f32[48,128]{1,0:T(8,128)S(1)}, f32[48,128]{1,0:T(8,128)S(1)}, u32[]{:S(2)}, u32[]{:S(2)}) collective-permute-start(f32[48,128]{1,0:T(8,128)S(1)} %add_add_fusion.1), channel_id=1, source_target_pairs={{0,17},{1,16},{2,19},{3,18},{4,21},{5,20},{6,23},{7,22},{8,25},{9,... | collective-permute-start | bytes 73736 | tf_op jit(solution)/shard_map/ppermute | solution.py:93
  19.0 4.4 %collective-permute-start.8 = (f32[48,128]{1,0:T(8,128)S(1)}, f32[48,128]{1,0:T(8,128)S(1)}, u32[]{:S(2)}, u32[]{:S(2)}) collective-permute-start(f32[48,128]{1,0:T(8,128)S(1)} %add_add_fusion.1), channel_id=1, source_target_pairs={{0,1},{1,0},{2,3},{3,2},{4,5},{5,4},{6,7},{7,6},{8,9},{9,8},{10,11... | collective-permute-start | bytes 73736 | tf_op jit(solution)/shard_map/ppermute | solution.py:93
  24.3 3.5 %collective-permute-start.12 = (f32[72,128]{1,0:T(8,128)S(1)}, f32[72,128]{1,0:T(8,128)S(1)}, u32[]{:S(2)}, u32[]{:S(2)}) collective-permute-start(f32[72,128]{1,0:T(8,128)S(1)} %get-tuple-element.42), channel_id=1, source_target_pairs={{0,3},{1,2},{2,1},{3,0},{4,7},{5,6},{6,5},{7,4},{8,11},{9,10},{10,... | collective-permute-start | bytes 110600 | tf_op jit(solution)/shard_map/ppermute | solution.py:93
  25.6 2.2 %collective-permute-start.13 = (f32[72,128]{1,0:T(8,128)S(1)}, f32[72,128]{1,0:T(8,128)S(1)}, u32[]{:S(2)}, u32[]{:S(2)}) collective-permute-start(f32[72,128]{1,0:T(8,128)S(1)} %get-tuple-element.42), channel_id=1, source_target_pairs={{0,1},{1,0},{2,3},{3,2},{4,5},{5,4},{6,7},{7,6},{8,9},{9,8},{10,11... | collective-permute-start | bytes 110600 | tf_op jit(solution)/shard_map/ppermute | solution.py:93
  26.0 4.4 %collective-permute-start.10 = (f32[72,128]{1,0:T(8,128)S(1)}, f32[72,128]{1,0:T(8,128)S(1)}, u32[]{:S(2)}, u32[]{:S(2)}) collective-permute-start(f32[72,128]{1,0:T(8,128)S(1)} %get-tuple-element.42), channel_id=1, source_target_pairs={{0,7},{1,6},{2,5},{3,4},{4,3},{5,2},{6,1},{7,0},{8,15},{9,14},{10,... | collective-permute-start | bytes 110600 | tf_op jit(solution)/shard_map/ppermute | solution.py:93
  26.2 4.2 %collective-permute-start.11 = (f32[72,128]{1,0:T(8,128)S(1)}, f32[72,128]{1,0:T(8,128)S(1)}, u32[]{:S(2)}, u32[]{:S(2)}) collective-permute-start(f32[72,128]{1,0:T(8,128)S(1)} %get-tuple-element.42), channel_id=1, source_target_pairs={{0,5},{1,4},{2,7},{3,6},{4,1},{5,0},{6,3},{7,2},{8,13},{9,12},{10,... | collective-permute-start | bytes 110600 | tf_op jit(solution)/shard_map/ppermute | solution.py:93
  27.8 6.8 %copy-start = (f32[72,128]{1,0:T(8,128)}, f32[72,128]{1,0:T(8,128)S(1)}, u32[]{:S(2)}) copy-start(f32[72,128]{1,0:T(8,128)S(1)} %collective-permute-done.12) | copy-start | bytes 110596
  30.3 7.1 %collective-permute-start.14 = (f32[64,128]{1,0:T(8,128)S(1)}, f32[64,128]{1,0:T(8,128)S(1)}, u32[]{:S(2)}, u32[]{:S(2)}) collective-permute-start(f32[64,128]{1,0:T(8,128)S(1)} %fusion), channel_id=1, source_target_pairs={{0,25},{1,24},{2,27},{3,26},{4,29},{5,28},{6,31},{7,30},{8,17},{9,... | collective-permute-start | bytes 98312 | tf_op jit(solution)/shard_map/ppermute | solution.py:93
  32.5 4.9 %collective-permute-start.15 = (f32[64,128]{1,0:T(8,128)S(1)}, f32[64,128]{1,0:T(8,128)S(1)}, u32[]{:S(2)}, u32[]{:S(2)}) collective-permute-start(f32[64,128]{1,0:T(8,128)S(1)} %fusion), channel_id=1, source_target_pairs={{0,17},{1,16},{2,19},{3,18},{4,21},{5,20},{6,23},{7,22},{8,25},{9,... | collective-permute-start | bytes 98312 | tf_op jit(solution)/shard_map/ppermute | solution.py:93
  33.2 4.3 %collective-permute-start.16 = (f32[64,128]{1,0:T(8,128)S(1)}, f32[64,128]{1,0:T(8,128)S(1)}, u32[]{:S(2)}, u32[]{:S(2)}) collective-permute-start(f32[64,128]{1,0:T(8,128)S(1)} %fusion), channel_id=1, source_target_pairs={{0,9},{1,8},{2,11},{3,10},{4,13},{5,12},{6,15},{7,14},{8,1},{9,0},... | collective-permute-start | bytes 98312 | tf_op jit(solution)/shard_map/ppermute | solution.py:93
  34.6 2.9 %collective-permute-start.17 = (f32[64,128]{1,0:T(8,128)S(1)}, f32[64,128]{1,0:T(8,128)S(1)}, u32[]{:S(2)}, u32[]{:S(2)}) collective-permute-start(f32[64,128]{1,0:T(8,128)S(1)} %fusion), channel_id=1, source_target_pairs={{0,1},{1,0},{2,3},{3,2},{4,5},{5,4},{6,7},{7,6},{8,9},{9,8},{10,11... | collective-permute-start | bytes 98312 | tf_op jit(solution)/shard_map/ppermute | solution.py:93
  34.6 0.7 %slice-start = ((f32[72,128]{1,0:T(8,128)}), f32[8,128]{1,0:T(8,128)S(1)}, s32[]{:S(2)}) async-start(f32[72,128]{1,0:T(8,128)} %copy-done), calls=%async_computation | async-start | bytes 8192 | tf_op jit(solution)/shard_map/slice | solution.py:309
  35.3 1.3 %collective-permute-start.18 = (f32[16,128]{1,0:T(8,128)S(1)}, f32[16,128]{1,0:T(8,128)S(1)}, u32[]{:S(2)}, u32[]{:S(2)}) collective-permute-start(f32[16,128]{1,0:T(8,128)S(1)} %pad_maximum_fusion.2.rows), channel_id=1, source_target_pairs={{0,1},{1,0},{2,3},{3,2},{4,5},{5,4},{6,7},{7,6},{8,9},{9,8},{10,11... | collective-permute-start | bytes 24584 | tf_op jit(solution)/shard_map/ppermute | solution.py:89
  37.5 1.3 %collective-permute-start.19 = (f32[64,128]{1,0:T(8,128)S(1)}, f32[64,128]{1,0:T(8,128)S(1)}, u32[]{:S(2)}, u32[]{:S(2)}) collective-permute-start(f32[64,128]{1,0:T(8,128)S(1)} %add_add_fusion.terms), channel_id=1, source_target_pairs={{0,1},{1,0},{2,3},{3,2},{4,5},{5,4},{6,7},{7,6},{8,9},{9,8},{10,11... | collective-permute-start | bytes 98312 | tf_op jit(solution)/shard_map/ppermute | solution.py:89

commit v12 on v9

--- a/solution.py
+++ b/solution.py
@@ -211,19 +211,23 @@
 
     got = swap(opened)
     terms = opened[:vox_rows] + got[:vox_rows]
-    rows_b = jnp.concatenate([got[vox_rows:], opened[vox_rows:]], axis=0)
+    mate_con, mate_x = swap(con), swap(x)
+    packet = jnp.concatenate([terms, got[vox_rows:], opened[vox_rows:]], axis=0)
+    own = jnp.concatenate([terms, opened[vox_rows:], got[vox_rows:]], axis=0)
+    rows_b = own[vox_rows:]
     holder = 1
     for group in groups_of(chip_bits):
-        parts = fan(jnp.concatenate([terms, rows_b], axis=0), holder, masks_of(group))
+        parts = [send(packet, holder, mask) for mask in masks_of(group)[:-1]] + [own]
         terms = tree([part[:vox_rows] for part in parts])
         rows_b = jnp.concatenate([part[vox_rows:] for part in parts], axis=0)
+        packet = jnp.concatenate([terms, rows_b], axis=0)
+        own = swap(packet)
         holder ^= 1
     voxel_core = holder
-    mate_con = swap(con)
 
     half, sums_rows = rank // 2, rank // 2 + chip_rows
 
-    def voxel_kernel(terms, rows, a, w, outer_c, con, mate_con, moved_out, chip_b, out, all_b):
+    def voxel_kernel(terms, rows, a, w, outer_c, con, mate_con, mate_x, moved_out, chip_b, out, all_b):
         b = in_order(rows, all_b, chips)
         chip_b[...] = all_b[pl.ds(pl.multiple_of(smp_index() // 2 * chip_rows, chip_rows), chip_rows), :]
         coupled = outer_c[...] * dot_rows(b, b)
@@ -240,7 +244,7 @@
     moved_a, chip_b, sums = call(
         voxel_kernel,
         (near(vox_rows, rank), near(chip_rows, rank), near(sums_rows + 8, rank)),
-        (terms, rows_b, a_near, w_row, outer_c, con, mate_con),
+        (terms, rows_b, a_near, w_row, outer_c, con, mate_con, mate_x),
         2 * rank * rank * vox_rows * 12,
         scratch=(near(smp_total, rank),),
     )
@@ -253,7 +257,6 @@
     sample_core = holder
     if sample_core != voxel_core:
         chip_b = swap(chip_b)
-    mate_x = swap(x)
 
     def time_kernel(x, mate_x, moved, mate_moved, each):
         moved = on_core(voxel_core, moved[...], mate_moved[...])
@@ -270,8 +273,9 @@
     )
 
     def sample_kernel(sums, b, w, outer_c, each, gram_out, out):
-        gram_out[...] = unpack(sums[:half, :], sums[sums_rows : sums_rows + 1, :])
-        coupled = outer_c[...] * gram_out[...]
+        gram = unpack(sums[:half, :], sums[sums_rows : sums_rows + 1, :])
+        gram_out[...] = gram
+        coupled = outer_c[...] * gram
         moved = b[...] - step_of(coupled) * (dot(b[...], coupled) - sums[half:sums_rows, :] * w[...])
         out[times:, :] = moved
         total = None
@@ -306,14 +310,28 @@
     smp_mask = sum(chip_bits)
     for group in groups_of(chip_bits + vox_bits):
         masks = masks_of(group)
-        with_rows = any(mask & smp_mask for mask in masks)
-        parts = fan(jnp.concatenate([terms, rows_b], axis=0) if with_rows else terms, holder, masks)
-        terms = tree([part[:times] for part in parts])
+        if any(mask & smp_mask for mask in masks):
+            packet = payload if rows_b.shape[0] == chip_rows else jnp.concatenate([terms, rows_b], axis=0)
+            parts = fan(packet, holder, masks)
+            gathered = [i for i, mask in enumerate(masks) if not mask & ~smp_mask]
+            rows = rows_b.shape[0]
+
+            def gather_kernel(*refs, gathered=gathered, rows=rows):
+                parts, (terms, rows_out) = refs[-3::-1], refs[-2:]
+                terms[...] = tree([part[:times, :] for part in parts])
+                for p, i in enumerate(gathered):
+                    rows_out[p * rows : (p + 1) * rows, :] = parts[i][times:, :]
+
+            terms, rows_b = call(
+                gather_kernel,
+                (near(times, rank), near(len(gathered) * rows, rank)),
+                parts[::-1],
+                len(masks) * times * rank,
+            )
+            rows_core = holder ^ 1
+        else:
+            terms = tree(fan(terms, holder, masks))
         holder ^= 1
-        if with_rows:
-            parts = [part for part, mask in zip(parts, masks) if not mask & ~smp_mask]
-            rows_b = jnp.concatenate([part[times:] for part in parts], axis=0)
-            rows_core = holder
     last_core = holder
     mate_rows_b = swap(rows_b)
 

time: 32.9 us -> 32.8 us (level)
  waiting for transfers between devices: 9.41 us -> 13.2 us
  starting transfers between devices: 15.8 us -> 12.7 us
  local copies, waits for them, and re-layouts: 0.7 us -> 0.01 us
    ppermute x11, waiting for transfers between devices: 7.16 us -> 11.4 us  [send(): return lax.ppermute(values, ALL, pairs)]
    ppermute x12 -> x11, starting transfers between devices: 7.48 us -> 3.71 us  [swap(): lax.ppermute(values, ALL, [(i, i ^ 1) for i in range(lax.axis_size(ALL))])]
    slice x5 -> x2, local copies, waits for them, and re-layouts: 0.7 us -> 0.01 us  [per_device(): packet = jnp.concatenate([terms, got[vox_rows:], opened[vox_rows:]], axis=0)]
    ppermute x11, starting transfers between devices: 8.32 us -> 8.94 us  [send(): return lax.ppermute(values, ALL, pairs)]
    ppermute x12 -> x11, waiting for transfers between devices: 2.25 us -> 1.81 us  [swap(): lax.ppermute(values, ALL, [(i, i ^ 1) for i in range(lax.axis_size(ALL))])]
    pallas_call x8 -> x9, Pallas kernels: 5.93 us -> 5.94 us  [call(): pl.pallas_call(kernel, out_shape=outs, in_specs=specs, out_specs=[pl.Bloc...]
  transfers between devices with their start and end apart: 23 -> 22, of which waited for: 9 -> 12; matrix products, arithmetic and copies ran while one was open for 0% -> 0% of each run, Pallas kernels for 9% -> 7%
where the time goes in v12:
time: 32.8 us; the launch traced here: 32.6 us
  waiting for transfers between devices  13.2 us (40%)
  starting transfers between devices  12.7 us (39%)
  Pallas kernels  5.94 us (18%)
  between operations  0.74 us (2%)
    ppermute x11, waiting for transfers between devices, send(): return lax.ppermute(values, ALL, pairs)  11.4 us
    ppermute x11, starting transfers between devices, send(): return lax.ppermute(values, ALL, pairs)  8.94 us
    pallas_call x9, Pallas kernels, call(): pl.pallas_call(kernel, out_shape=outs, in_specs=specs, out_specs=[pl.Bloc...  5.94 us
    ppermute x11, starting transfers between devices, swap(): lax.ppermute(values, ALL, [(i, i ^ 1) for i in range(lax.axis_size(ALL))])  3.71 us
    ppermute x11, waiting for transfers between devices, swap(): lax.ppermute(values, ALL, [(i, i ^ 1) for i in range(lax.axis_size(ALL))])  1.81 us
  transfers between devices with their start and end apart: 22, of which 12 were waited for; matrix products, arithmetic and copies ran while one was open for 0% of the time, Pallas kernels for 7%

profile of v12, /device:TPU:0, one launch (start us, length us, event | category | flops | bytes accessed | tf_op | source)
XLA Modules:
  0.0 32.6 jit_solution(14043228700331938174)
XLA Ops:
  0.6 1.9 %shard_map.84 = (f32[1024,128]{1,0:T(8,128)S(1)}, f32[128,128]{1,0:T(8,128)S(1)}, f32[128,128]{1,0:T(8,128)S(1)}, f32[1,128]{1,0:T(1,128)S(1)}, f32[136,128]{1,0:T(8,128)S(1)}, /*index=5*/f32[8,128,128]{2,1,0:T(8,128)S(1)}) custom-call(f32[1024,128]{1,0:T(8,128)} %bitcast.3, f32[128,128]{1,0:T(8,128)} %c_hbm.1, f32[8,128]{1,0:T(8,128)} %b_hbm.1, ...), custom_call_target="tpu_custom_call" | custom-call | flops 201326592 | bytes 65536 | tf_op jit(solution)/shard_map/pallas_call | solution.py:52
  2.6 0.5 %collective-permute-start = (f32[136,128]{1,0:T(8,128)S(1)}, f32[136,128]{1,0:T(8,128)S(1)}, u32[]{:S(2)}, u32[]{:S(2)}) collective-permute-start(f32[136,128]{1,0:T(8,128)S(1)} %get-tuple-element.34), channel_id=1, source_target_pairs={{0,1},{1,0},{2,3},{3,2},{4,5},{5,4},{6,7},{7,6},{8,9},{9,8},{10,11... | collective-permute-start | bytes 208904 | tf_op jit(solution)/shard_map/ppermute | solution.py:89
  3.1 0.1 collective-permute-start.2
  3.1 0.4 %collective-permute-start.3 = (f32[1024,128]{1,0:T(8,128)S(1)}, f32[1024,128]{1,0:T(8,128)S(1)}, u32[]{:S(2)}, u32[]{:S(2)}) collective-permute-start(f32[1024,128]{1,0:T(8,128)S(1)} %get-tuple-element.40.x), channel_id=1, source_target_pairs={{0,1},{1,0},{2,3},{3,2},{4,5},{5,4},{6,7},{7,6},{8,9},{9,8},{10,11... | collective-permute-start | bytes 1572872 | tf_op jit(solution)/shard_map/ppermute | solution.py:89
  3.6 0.4 %collective-permute-done = f32[136,128]{1,0:T(8,128)S(1)} collective-permute-done((f32[136,128]{1,0:T(8,128)S(1)}, f32[136,128]{1,0:T(8,128)S(1)}, u32[]{:S(2)}, u32[]{:S(2)}) %collective-permute-start) | collective-permute-done | bytes 69664 | tf_op jit(solution)/shard_map/ppermute | solution.py:89
  4.0 0.4 %collective-permute-start.1 = (f32[144,128]{1,0:T(8,128)S(1)}, f32[144,128]{1,0:T(8,128)S(1)}, u32[]{:S(2)}, u32[]{:S(2)}) collective-permute-start(f32[144,128]{1,0:T(8,128)S(1)} %pad_maximum_fusion), channel_id=1, source_target_pairs={{0,1},{1,2},{2,3},{3,0},{4,5},{5,6},{6,7},{7,4},{8,9},{9,10},{10,1... | collective-permute-start | bytes 221192 | tf_op jit(solution)/shard_map/ppermute | solution.py:95
  4.4 0.2 shard_map.85
  4.7 4.1 %collective-permute-done.1 = f32[144,128]{1,0:T(8,128)S(1)} collective-permute-done((f32[144,128]{1,0:T(8,128)S(1)}, f32[144,128]{1,0:T(8,128)S(1)}, u32[]{:S(2)}, u32[]{:S(2)}) %collective-permute-start.1) | collective-permute-done | bytes 73760 | tf_op jit(solution)/shard_map/ppermute | solution.py:95
  8.8 0.0 collective-permute-done.2.mate_con
  8.8 0.0 collective-permute-done.3.mate_x
  8.8 0.7 %shard_map.86 = (f32[128,128]{1,0:T(8,128)S(1)}, f32[16,128]{1,0:T(8,128)S(1)}, f32[88,128]{1,0:T(8,128)S(1)}) custom-call(f32[128,128]{1,0:T(8,128)S(1)} %slice_add_fusion.terms, f32[32,128]{1,0:T(8,128)S(1)} %pad_maximum_fusion.1.rows, f32[128,128]{1,0:T(8,128)S(1)} %get-tuple-element.35.a, f32[1,128]{1,0:T(1,128)S(1)} %get-tuple-element.36.w, ...), custom_call_target="tpu_custom_call" | custom-call | flops 50331648 | bytes 65536 | tf_op jit(solution)/shard_map/pallas_call | solution.py:52
  9.5 1.9 %collective-permute-start.7 = (f32[88,128]{1,0:T(8,128)S(1)}, f32[88,128]{1,0:T(8,128)S(1)}, u32[]{:S(2)}, u32[]{:S(2)}) collective-permute-start(f32[88,128]{1,0:T(8,128)S(1)} %get-tuple-element.41), channel_id=1, source_target_pairs={{0,13},{1,0},{2,15},{3,2},{4,9},{5,4},{6,11},{7,6},{8,5},{9,8},{10... | collective-permute-start | bytes 135176 | tf_op jit(solution)/shard_map/ppermute | solution.py:95
  11.4 0.3 collective-permute-start.6
  11.7 0.3 %collective-permute-start.5 = (f32[88,128]{1,0:T(8,128)S(1)}, f32[88,128]{1,0:T(8,128)S(1)}, u32[]{:S(2)}, u32[]{:S(2)}) collective-permute-start(f32[88,128]{1,0:T(8,128)S(1)} %get-tuple-element.41), channel_id=1, source_target_pairs={{0,5},{1,0},{2,7},{3,2},{4,1},{5,4},{6,3},{7,6},{8,13},{9,8},{10,1... | collective-permute-start | bytes 135176 | tf_op jit(solution)/shard_map/ppermute | solution.py:95
  12.0 0.2 collective-permute-start.4
  12.2 0.3 %collective-permute-start.10 = (f32[128,128]{1,0:T(8,128)S(1)}, f32[128,128]{1,0:T(8,128)S(1)}, u32[]{:S(2)}, u32[]{:S(2)}) collective-permute-start(f32[128,128]{1,0:T(8,128)S(1)} %get-tuple-element.43.moved), channel_id=1, source_target_pairs={{0,1},{1,0},{2,3},{3,2},{4,5},{5,4},{6,7},{7,6},{8,9},{9,8},{10,11... | collective-permute-start | bytes 196616 | tf_op jit(solution)/shard_map/ppermute | solution.py:89
  12.6 0.6 %collective-permute-done.7 = f32[88,128]{1,0:T(8,128)S(1)} collective-permute-done((f32[88,128]{1,0:T(8,128)S(1)}, f32[88,128]{1,0:T(8,128)S(1)}, u32[]{:S(2)}, u32[]{:S(2)}) %collective-permute-start.7) | collective-permute-done | bytes 45088 | tf_op jit(solution)/shard_map/ppermute | solution.py:95
  13.1 0.4 %collective-permute-done.6 = f32[88,128]{1,0:T(8,128)S(1)} collective-permute-done((f32[88,128]{1,0:T(8,128)S(1)}, f32[88,128]{1,0:T(8,128)S(1)}, u32[]{:S(2)}, u32[]{:S(2)}) %collective-permute-start.6) | collective-permute-done | bytes 45088 | tf_op jit(solution)/shard_map/ppermute | solution.py:95
  13.5 0.2 collective-permute-done.5
  13.8 0.0 collective-permute-done.4
  13.8 1.7 %collective-permute-start.9 = (f32[88,128]{1,0:T(8,128)S(1)}, f32[88,128]{1,0:T(8,128)S(1)}, u32[]{:S(2)}, u32[]{:S(2)}) collective-permute-start(f32[88,128]{1,0:T(8,128)S(1)} %add_add_fusion.1), channel_id=1, source_target_pairs={{0,1},{1,16},{2,3},{3,18},{4,5},{5,20},{6,7},{7,22},{8,9},{9,24},{... | collective-permute-start | bytes 135176 | tf_op jit(solution)/shard_map/ppermute | solution.py:95
  15.4 1.1 %collective-permute-start.8 = (f32[88,128]{1,0:T(8,128)S(1)}, f32[88,128]{1,0:T(8,128)S(1)}, u32[]{:S(2)}, u32[]{:S(2)}) collective-permute-start(f32[88,128]{1,0:T(8,128)S(1)} %add_add_fusion.1), channel_id=1, source_target_pairs={{0,1},{1,0},{2,3},{3,2},{4,5},{5,4},{6,7},{7,6},{8,9},{9,8},{10,11... | collective-permute-start | bytes 135176 | tf_op jit(solution)/shard_map/ppermute | solution.py:89
  16.5 0.0 collective-permute-done.10.mate_moved
  16.5 0.5 %shard_map.87.each = f32[16,128,128]{2,1,0:T(8,128)S(1)} custom-call(f32[1024,128]{1,0:T(8,128)S(1)} %get-tuple-element.40.x, f32[1024,128]{1,0:T(8,128)S(1)} %collective-permute-done.3.mate_x, f32[128,128]{1,0:T(8,128)S(1)} %get-tuple-element.43.moved, f32[128,128]{1,0:T(8,128)S(1)} %collective-permute-done.10.mate_moved), custom_call_target="tpu_custom_call" | custom-call | flops 402653184 | bytes 65536 | tf_op jit(solution)/shard_map/pallas_call | solution.py:52
  17.0 2.7 %collective-permute-done.9 = f32[88,128]{1,0:T(8,128)S(1)} collective-permute-done((f32[88,128]{1,0:T(8,128)S(1)}, f32[88,128]{1,0:T(8,128)S(1)}, u32[]{:S(2)}, u32[]{:S(2)}) %collective-permute-start.9) | collective-permute-done | bytes 45088 | tf_op jit(solution)/shard_map/ppermute | solution.py:95
  19.7 0.0 collective-permute-done.8
  19.8 0.3 %shard_map.88 = (f32[128,128]{1,0:T(8,128)S(1)}, f32[144,128]{1,0:T(8,128)S(1)}) custom-call(f32[88,128]{1,0:T(8,128)S(1)} %add.32.sums, f32[16,128]{1,0:T(8,128)S(1)} %get-tuple-element.42.b, f32[1,128]{1,0:T(1,128)S(1)} %get-tuple-element.36.w, f32[128,128]{1,0:T(8,128)S(1)} %get-tuple-element.38.outer_c, f32[16,128,128]{2,1,0:T(8,128)S(1)} %shard_map.87.each), custom_call_target="tpu_custom_call" | custom-call | flops 3145728 | bytes 65536 | tf_op jit(solution)/shard_map/pallas_call | solution.py:52
  20.1 0.1 collective-permute-start.14
  20.2 0.3 collective-permute-start.13
  20.4 1.2 %collective-permute-start.12 = (f32[144,128]{1,0:T(8,128)S(1)}, f32[144,128]{1,0:T(8,128)S(1)}, u32[]{:S(2)}, u32[]{:S(2)}) collective-permute-start(f32[144,128]{1,0:T(8,128)S(1)} %get-tuple-element.44), channel_id=1, source_target_pairs={{0,3},{1,0},{2,1},{3,2},{4,7},{5,4},{6,5},{7,6},{8,11},{9,8},{10,9... | collective-permute-start | bytes 221192 | tf_op jit(solution)/shard_map/ppermute | solution.py:95
  21.6 0.0 collective-permute-start.11
  21.6 0.5 %collective-permute-start.20 = (f32[128,128]{1,0:T(8,128)S(1)}, f32[128,128]{1,0:T(8,128)S(1)}, u32[]{:S(2)}, u32[]{:S(2)}) collective-permute-start(f32[128,128]{1,0:T(8,128)S(1)} %get-tuple-element.47.gram), channel_id=1, source_target_pairs={{0,1},{1,0},{2,3},{3,2},{4,5},{5,4},{6,7},{7,6},{8,9},{9,8},{10,11... | collective-permute-start | bytes 196616 | tf_op jit(solution)/shard_map/ppermute | solution.py:89
  22.1 0.7 %collective-permute-done.13.refs_2_ = f32[144,128]{1,0:T(8,128)S(1)} collective-permute-done((f32[144,128]{1,0:T(8,128)S(1)}, f32[144,128]{1,0:T(8,128)S(1)}, u32[]{:S(2)}, u32[]{:S(2)}) %collective-permute-start.13) | collective-permute-done | bytes 73760 | tf_op jit(solution)/shard_map/ppermute | solution.py:95
  22.8 0.8 %collective-permute-done.12.refs_1_ = f32[144,128]{1,0:T(8,128)S(1)} collective-permute-done((f32[144,128]{1,0:T(8,128)S(1)}, f32[144,128]{1,0:T(8,128)S(1)}, u32[]{:S(2)}, u32[]{:S(2)}) %collective-permute-start.12) | collective-permute-done | bytes 73760 | tf_op jit(solution)/shard_map/ppermute | solution.py:95
  23.6 0.0 collective-permute-done.11.refs_0_
  23.6 0.9 %collective-permute-start.18 = (f32[128,128]{1,0:T(8,128)S(1)}, f32[128,128]{1,0:T(8,128)S(1)}, u32[]{:S(2)}, u32[]{:S(2)}) collective-permute-start(f32[128,128]{1,0:T(8,128)S(1)} %get-tuple-element.45), channel_id=1, source_target_pairs={{0,1},{1,24},{2,3},{3,26},{4,5},{5,28},{6,7},{7,30},{8,9},{9,16},{... | collective-permute-start | bytes 196616 | tf_op jit(solution)/shard_map/ppermute | solution.py:95
  24.6 1.5 %collective-permute-start.17 = (f32[128,128]{1,0:T(8,128)S(1)}, f32[128,128]{1,0:T(8,128)S(1)}, u32[]{:S(2)}, u32[]{:S(2)}) collective-permute-start(f32[128,128]{1,0:T(8,128)S(1)} %get-tuple-element.45), channel_id=1, source_target_pairs={{0,1},{1,16},{2,3},{3,18},{4,5},{5,20},{6,7},{7,22},{8,9},{9,24},{... | collective-permute-start | bytes 196616 | tf_op jit(solution)/shard_map/ppermute | solution.py:95
  26.1 0.3 collective-permute-start.16
  26.5 0.5 %collective-permute-start.19 = (f32[32,128]{1,0:T(8,128)S(1)}, f32[32,128]{1,0:T(8,128)S(1)}, u32[]{:S(2)}, u32[]{:S(2)}) collective-permute-start(f32[32,128]{1,0:T(8,128)S(1)} %get-tuple-element.46.rows), channel_id=1, source_target_pairs={{0,1},{1,0},{2,3},{3,2},{4,5},{5,4},{6,7},{7,6},{8,9},{9,8},{10,11... | collective-permute-start | bytes 49160 | tf_op jit(solution)/shard_map/ppermute | solution.py:89
  27.0 0.7 %shard_map.90 = (f32[128,128]{1,0:T(8,128)}, f32[1,128]{1,0:T(1,128)S(1)}, f32[128,128]{1,0:T(8,128)S(1)}) custom-call(f32[128,128]{1,0:T(8,128)S(1)} %get-tuple-element.47.gram, f32[128,128]{1,0:T(8,128)S(1)} %collective-permute-done.20.mate_gram, f32[128,128]{1,0:T(8,128)S(1)} %get-tuple-element.43.moved, ...), custom_call_target="tpu_custom_call" | custom-call | flops 131072 | bytes 65536 | tf_op jit(solution)/shard_map/pallas_call | solution.py:52
  27.6 0.2 collective-permute-done.19.mate_rows
  27.8 0.9 %shard_map.91 = (f32[8,128]{1,0:T(8,128)}, f32[128,128]{1,0:T(8,128)S(1)}, f32[1,128]{1,0:T(1,128)S(1)}, f32[1,128]{1,0:T(1,128)S(1)}) custom-call(f32[32,128]{1,0:T(8,128)S(1)} %get-tuple-element.46.rows, f32[32,128]{1,0:T(8,128)S(1)} %collective-permute-done.19.mate_rows, f32[128,128]{1,0:T(8,128)S(1)} %get-tuple-element.37.c, ...), custom_call_target="tpu_custom_call" | custom-call | flops 16777216 | bytes 65536 | tf_op jit(solution)/shard_map/pallas_call | solution.py:52
  28.7 0.6 %collective-permute-done.18 = f32[128,128]{1,0:T(8,128)S(1)} collective-permute-done((f32[128,128]{1,0:T(8,128)S(1)}, f32[128,128]{1,0:T(8,128)S(1)}, u32[]{:S(2)}, u32[]{:S(2)}) %collective-permute-start.18) | collective-permute-done | bytes 65568 | tf_op jit(solution)/shard_map/ppermute | solution.py:95
  29.3 1.3 %collective-permute-done.17 = f32[128,128]{1,0:T(8,128)S(1)} collective-permute-done((f32[128,128]{1,0:T(8,128)S(1)}, f32[128,128]{1,0:T(8,128)S(1)}, u32[]{:S(2)}, u32[]{:S(2)}) %collective-permute-start.17) | collective-permute-done | bytes 65568 | tf_op jit(solution)/shard_map/ppermute | solution.py:95
  30.6 0.0 collective-permute-done.16
  30.6 0.1 collective-permute-start.21
  30.7 1.2 %collective-permute-done.21.mate_terms = f32[128,128]{1,0:T(8,128)S(1)} collective-permute-done((f32[128,128]{1,0:T(8,128)S(1)}, f32[128,128]{1,0:T(8,128)S(1)}, u32[]{:S(2)}, u32[]{:S(2)}) %collective-permute-start.21) | collective-permute-done | bytes 65568 | tf_op jit(solution)/shard_map/ppermute | solution.py:89
  31.9 0.7 %shard_map.92 = (f32[128,128]{1,0:T(8,128)}, f32[1,128]{1,0:T(1,128)}) custom-call(f32[128,128]{1,0:T(8,128)S(1)} %add_add_fusion.terms, f32[128,128]{1,0:T(8,128)S(1)} %collective-permute-done.21.mate_terms, f32[128,128]{1,0:T(8,128)S(1)} %get-tuple-element.59.base, f32[1,128]{1,0:T(1,128)S(1)} %get-tuple-element.60.gain, f32[1,128]{1,0:T(1,128)S(1)} %get-tuple-element.61.scale), custom_call_target="tpu_custom_call" | custom-call | flops 131072 | bytes 65536 | tf_op jit(solution)/shard_map/pallas_call | solution.py:52
  (15 shorter events, 0.1 us)
Async XLA Ops:
  2.6 1.4 %collective-permute-start = (f32[136,128]{1,0:T(8,128)S(1)}, f32[136,128]{1,0:T(8,128)S(1)}, u32[]{:S(2)}, u32[]{:S(2)}) collective-permute-start(f32[136,128]{1,0:T(8,128)S(1)} %get-tuple-element.34), channel_id=1, source_target_pairs={{0,1},{1,0},{2,3},{3,2},{4,5},{5,4},{6,7},{7,6},{8,9},{9,8},{10,11... | collective-permute-start | bytes 208904 | tf_op jit(solution)/shard_map/ppermute | solution.py:89
  3.1 5.7 %collective-permute-start.2 = (f32[8,128,128]{2,1,0:T(8,128)S(1)}, f32[8,128,128]{2,1,0:T(8,128)S(1)}, u32[]{:S(2)}, u32[]{:S(2)}) collective-permute-start(f32[8,128,128]{2,1,0:T(8,128)S(1)} %get-tuple-element.39.con), channel_id=1, source_target_pairs={{0,1},{1,0},{2,3},{3,2},{4,5},{5,4},{6,7},{7,6},{8,9},{9,8},{10,11... | collective-permute-start | bytes 1572872 | tf_op jit(solution)/shard_map/ppermute | solution.py:89
  3.1 5.6 %collective-permute-start.3 = (f32[1024,128]{1,0:T(8,128)S(1)}, f32[1024,128]{1,0:T(8,128)S(1)}, u32[]{:S(2)}, u32[]{:S(2)}) collective-permute-start(f32[1024,128]{1,0:T(8,128)S(1)} %get-tuple-element.40.x), channel_id=1, source_target_pairs={{0,1},{1,0},{2,3},{3,2},{4,5},{5,4},{6,7},{7,6},{8,9},{9,8},{10,11... | collective-permute-start | bytes 1572872 | tf_op jit(solution)/shard_map/ppermute | solution.py:89
  4.0 4.7 %collective-permute-start.1 = (f32[144,128]{1,0:T(8,128)S(1)}, f32[144,128]{1,0:T(8,128)S(1)}, u32[]{:S(2)}, u32[]{:S(2)}) collective-permute-start(f32[144,128]{1,0:T(8,128)S(1)} %pad_maximum_fusion), channel_id=1, source_target_pairs={{0,1},{1,2},{2,3},{3,0},{4,5},{5,6},{6,7},{7,4},{8,9},{9,10},{10,1... | collective-permute-start | bytes 221192 | tf_op jit(solution)/shard_map/ppermute | solution.py:95
  9.5 3.6 %collective-permute-start.7 = (f32[88,128]{1,0:T(8,128)S(1)}, f32[88,128]{1,0:T(8,128)S(1)}, u32[]{:S(2)}, u32[]{:S(2)}) collective-permute-start(f32[88,128]{1,0:T(8,128)S(1)} %get-tuple-element.41), channel_id=1, source_target_pairs={{0,13},{1,0},{2,15},{3,2},{4,9},{5,4},{6,11},{7,6},{8,5},{9,8},{10... | collective-permute-start | bytes 135176 | tf_op jit(solution)/shard_map/ppermute | solution.py:95
  11.4 2.1 %collective-permute-start.6 = (f32[88,128]{1,0:T(8,128)S(1)}, f32[88,128]{1,0:T(8,128)S(1)}, u32[]{:S(2)}, u32[]{:S(2)}) collective-permute-start(f32[88,128]{1,0:T(8,128)S(1)} %get-tuple-element.41), channel_id=1, source_target_pairs={{0,9},{1,0},{2,11},{3,2},{4,13},{5,4},{6,15},{7,6},{8,1},{9,8},{10... | collective-permute-start | bytes 135176 | tf_op jit(solution)/shard_map/ppermute | solution.py:95
  11.7 2.0 %collective-permute-start.5 = (f32[88,128]{1,0:T(8,128)S(1)}, f32[88,128]{1,0:T(8,128)S(1)}, u32[]{:S(2)}, u32[]{:S(2)}) collective-permute-start(f32[88,128]{1,0:T(8,128)S(1)} %get-tuple-element.41), channel_id=1, source_target_pairs={{0,5},{1,0},{2,7},{3,2},{4,1},{5,4},{6,3},{7,6},{8,13},{9,8},{10,1... | collective-permute-start | bytes 135176 | tf_op jit(solution)/shard_map/ppermute | solution.py:95
  12.0 1.7 %collective-permute-start.4 = (f32[88,128]{1,0:T(8,128)S(1)}, f32[88,128]{1,0:T(8,128)S(1)}, u32[]{:S(2)}, u32[]{:S(2)}) collective-permute-start(f32[88,128]{1,0:T(8,128)S(1)} %get-tuple-element.41), channel_id=1, source_target_pairs={{0,1},{1,0},{2,3},{3,2},{4,5},{5,4},{6,7},{7,6},{8,9},{9,8},{10,11... | collective-permute-start | bytes 135176 | tf_op jit(solution)/shard_map/ppermute | solution.py:89
  12.2 4.3 %collective-permute-start.10 = (f32[128,128]{1,0:T(8,128)S(1)}, f32[128,128]{1,0:T(8,128)S(1)}, u32[]{:S(2)}, u32[]{:S(2)}) collective-permute-start(f32[128,128]{1,0:T(8,128)S(1)} %get-tuple-element.43.moved), channel_id=1, source_target_pairs={{0,1},{1,0},{2,3},{3,2},{4,5},{5,4},{6,7},{7,6},{8,9},{9,8},{10,11... | collective-permute-start | bytes 196616 | tf_op jit(solution)/shard_map/ppermute | solution.py:89
  13.8 6.0 %collective-permute-start.9 = (f32[88,128]{1,0:T(8,128)S(1)}, f32[88,128]{1,0:T(8,128)S(1)}, u32[]{:S(2)}, u32[]{:S(2)}) collective-permute-start(f32[88,128]{1,0:T(8,128)S(1)} %add_add_fusion.1), channel_id=1, source_target_pairs={{0,1},{1,16},{2,3},{3,18},{4,5},{5,20},{6,7},{7,22},{8,9},{9,24},{... | collective-permute-start | bytes 135176 | tf_op jit(solution)/shard_map/ppermute | solution.py:95
  15.4 4.3 %collective-permute-start.8 = (f32[88,128]{1,0:T(8,128)S(1)}, f32[88,128]{1,0:T(8,128)S(1)}, u32[]{:S(2)}, u32[]{:S(2)}) collective-permute-start(f32[88,128]{1,0:T(8,128)S(1)} %add_add_fusion.1), channel_id=1, source_target_pairs={{0,1},{1,0},{2,3},{3,2},{4,5},{5,4},{6,7},{7,6},{8,9},{9,8},{10,11... | collective-permute-start | bytes 135176 | tf_op jit(solution)/shard_map/ppermute | solution.py:89
  20.1 2.0 %collective-permute-start.14 = (f32[144,128]{1,0:T(8,128)S(1)}, f32[144,128]{1,0:T(8,128)S(1)}, u32[]{:S(2)}, u32[]{:S(2)}) collective-permute-start(f32[144,128]{1,0:T(8,128)S(1)} %get-tuple-element.44), channel_id=1, source_target_pairs={{0,7},{1,0},{2,5},{3,2},{4,3},{5,4},{6,1},{7,6},{8,15},{9,8},{10,1... | collective-permute-start | bytes 221192 | tf_op jit(solution)/shard_map/ppermute | solution.py:95
  20.2 2.7 %collective-permute-start.13 = (f32[144,128]{1,0:T(8,128)S(1)}, f32[144,128]{1,0:T(8,128)S(1)}, u32[]{:S(2)}, u32[]{:S(2)}) collective-permute-start(f32[144,128]{1,0:T(8,128)S(1)} %get-tuple-element.44), channel_id=1, source_target_pairs={{0,5},{1,0},{2,7},{3,2},{4,1},{5,4},{6,3},{7,6},{8,13},{9,8},{10,1... | collective-permute-start | bytes 221192 | tf_op jit(solution)/shard_map/ppermute | solution.py:95
  20.4 3.2 %collective-permute-start.12 = (f32[144,128]{1,0:T(8,128)S(1)}, f32[144,128]{1,0:T(8,128)S(1)}, u32[]{:S(2)}, u32[]{:S(2)}) collective-permute-start(f32[144,128]{1,0:T(8,128)S(1)} %get-tuple-element.44), channel_id=1, source_target_pairs={{0,3},{1,0},{2,1},{3,2},{4,7},{5,4},{6,5},{7,6},{8,11},{9,8},{10,9... | collective-permute-start | bytes 221192 | tf_op jit(solution)/shard_map/ppermute | solution.py:95
  21.6 2.0 %collective-permute-start.11 = (f32[144,128]{1,0:T(8,128)S(1)}, f32[144,128]{1,0:T(8,128)S(1)}, u32[]{:S(2)}, u32[]{:S(2)}) collective-permute-start(f32[144,128]{1,0:T(8,128)S(1)} %get-tuple-element.44), channel_id=1, source_target_pairs={{0,1},{1,0},{2,3},{3,2},{4,5},{5,4},{6,7},{7,6},{8,9},{9,8},{10,11... | collective-permute-start | bytes 221192 | tf_op jit(solution)/shard_map/ppermute | solution.py:89
  21.6 4.8 %collective-permute-start.20 = (f32[128,128]{1,0:T(8,128)S(1)}, f32[128,128]{1,0:T(8,128)S(1)}, u32[]{:S(2)}, u32[]{:S(2)}) collective-permute-start(f32[128,128]{1,0:T(8,128)S(1)} %get-tuple-element.47.gram), channel_id=1, source_target_pairs={{0,1},{1,0},{2,3},{3,2},{4,5},{5,4},{6,7},{7,6},{8,9},{9,8},{10,11... | collective-permute-start | bytes 196616 | tf_op jit(solution)/shard_map/ppermute | solution.py:89
  23.6 5.7 %collective-permute-start.18 = (f32[128,128]{1,0:T(8,128)S(1)}, f32[128,128]{1,0:T(8,128)S(1)}, u32[]{:S(2)}, u32[]{:S(2)}) collective-permute-start(f32[128,128]{1,0:T(8,128)S(1)} %get-tuple-element.45), channel_id=1, source_target_pairs={{0,1},{1,24},{2,3},{3,26},{4,5},{5,28},{6,7},{7,30},{8,9},{9,16},{... | collective-permute-start | bytes 196616 | tf_op jit(solution)/shard_map/ppermute | solution.py:95
  24.6 6.0 %collective-permute-start.17 = (f32[128,128]{1,0:T(8,128)S(1)}, f32[128,128]{1,0:T(8,128)S(1)}, u32[]{:S(2)}, u32[]{:S(2)}) collective-permute-start(f32[128,128]{1,0:T(8,128)S(1)} %get-tuple-element.45), channel_id=1, source_target_pairs={{0,1},{1,16},{2,3},{3,18},{4,5},{5,20},{6,7},{7,22},{8,9},{9,24},{... | collective-permute-start | bytes 196616 | tf_op jit(solution)/shard_map/ppermute | solution.py:95
  26.1 4.5 %collective-permute-start.16 = (f32[128,128]{1,0:T(8,128)S(1)}, f32[128,128]{1,0:T(8,128)S(1)}, u32[]{:S(2)}, u32[]{:S(2)}) collective-permute-start(f32[128,128]{1,0:T(8,128)S(1)} %get-tuple-element.45), channel_id=1, source_target_pairs={{0,1},{1,8},{2,3},{3,10},{4,5},{5,12},{6,7},{7,14},{8,9},{9,0},{10... | collective-permute-start | bytes 196616 | tf_op jit(solution)/shard_map/ppermute | solution.py:95
  26.5 4.1 %collective-permute-start.15 = (f32[128,128]{1,0:T(8,128)S(1)}, f32[128,128]{1,0:T(8,128)S(1)}, u32[]{:S(2)}, u32[]{:S(2)}) collective-permute-start(f32[128,128]{1,0:T(8,128)S(1)} %get-tuple-element.45), channel_id=1, source_target_pairs={{0,1},{1,0},{2,3},{3,2},{4,5},{5,4},{6,7},{7,6},{8,9},{9,8},{10,11... | collective-permute-start | bytes 196616 | tf_op jit(solution)/shard_map/ppermute | solution.py:89
  26.5 1.3 %collective-permute-start.19 = (f32[32,128]{1,0:T(8,128)S(1)}, f32[32,128]{1,0:T(8,128)S(1)}, u32[]{:S(2)}, u32[]{:S(2)}) collective-permute-start(f32[32,128]{1,0:T(8,128)S(1)} %get-tuple-element.46.rows), channel_id=1, source_target_pairs={{0,1},{1,0},{2,3},{3,2},{4,5},{5,4},{6,7},{7,6},{8,9},{9,8},{10,11... | collective-permute-start | bytes 49160 | tf_op jit(solution)/shard_map/ppermute | solution.py:89
  30.6 1.3 %collective-permute-start.21 = (f32[128,128]{1,0:T(8,128)S(1)}, f32[128,128]{1,0:T(8,128)S(1)}, u32[]{:S(2)}, u32[]{:S(2)}) collective-permute-start(f32[128,128]{1,0:T(8,128)S(1)} %add_add_fusion.terms), channel_id=1, source_target_pairs={{0,1},{1,0},{2,3},{3,2},{4,5},{5,4},{6,7},{7,6},{8,9},{9,8},{10,11... | collective-permute-start | bytes 196616 | tf_op jit(solution)/shard_map/ppermute | solution.py:89

commit v13 on v12

--- a/solution.py
+++ b/solution.py
@@ -152,7 +152,7 @@
     chips, chip_rows = smp_count // 2, 2 * smp_rows
     chip_bits = bits_of(smp_count)[1:]
     vox_bits = [bit * smp_count for bit in bits_of(vox_count)]
-    chunks = 4 if vox_rows % 32 == 0 else 1
+    chunks = 1
     chunk_vox = vox_rows // chunks
     chunk_rows = chunk_vox * smp_rows
 

time: 32.8 us -> 32.3 us (0.985)
  Pallas kernels: 5.94 us -> 5.51 us
    pallas_call x9, Pallas kernels: 5.94 us -> 5.51 us  [call(): pl.pallas_call(kernel, out_shape=outs, in_specs=specs, out_specs=[pl.Bloc...]
where the time goes in v13:
time: 32.3 us; the launch traced here: 32.2 us
  waiting for transfers between devices  13.2 us (41%)
  starting transfers between devices  12.6 us (39%)
  Pallas kernels  5.51 us (17%)
  between operations  0.74 us (2%)
    ppermute x11, waiting for transfers between devices, send(): return lax.ppermute(values, ALL, pairs)  11.4 us
    ppermute x11, starting transfers between devices, send(): return lax.ppermute(values, ALL, pairs)  8.93 us
    pallas_call x9, Pallas kernels, call(): pl.pallas_call(kernel, out_shape=outs, in_specs=specs, out_specs=[pl.Bloc...  5.51 us
    ppermute x11, starting transfers between devices, swap(): lax.ppermute(values, ALL, [(i, i ^ 1) for i in range(lax.axis_size(ALL))])  3.7 us
    ppermute x11, waiting for transfers between devices, swap(): lax.ppermute(values, ALL, [(i, i ^ 1) for i in range(lax.axis_size(ALL))])  1.81 us
  transfers between devices with their start and end apart: 22, of which 12 were waited for; matrix products, arithmetic and copies ran while one was open for 0% of the time, Pallas kernels for 7%

profile of v13, /device:TPU:0, one launch (start us, length us, event | category | flops | bytes accessed | tf_op | source)
XLA Modules:
  0.0 32.2 jit_solution(6945104911877566862)
XLA Ops:
  0.6 1.5 %shard_map.84 = (f32[1024,128]{1,0:T(8,128)S(1)}, f32[128,128]{1,0:T(8,128)S(1)}, f32[128,128]{1,0:T(8,128)S(1)}, f32[1,128]{1,0:T(1,128)S(1)}, f32[136,128]{1,0:T(8,128)S(1)}, /*index=5*/f32[8,128,128]{2,1,0:T(8,128)S(1)}) custom-call(f32[1024,128]{1,0:T(8,128)} %bitcast.3, f32[128,128]{1,0:T(8,128)} %c_hbm.1, f32[8,128]{1,0:T(8,128)} %b_hbm.1, ...), custom_call_target="tpu_custom_call" | custom-call | flops 201326592 | bytes 65536 | tf_op jit(solution)/shard_map/pallas_call | solution.py:52
  2.1 0.5 %collective-permute-start = (f32[136,128]{1,0:T(8,128)S(1)}, f32[136,128]{1,0:T(8,128)S(1)}, u32[]{:S(2)}, u32[]{:S(2)}) collective-permute-start(f32[136,128]{1,0:T(8,128)S(1)} %get-tuple-element.34), channel_id=1, source_target_pairs={{0,1},{1,0},{2,3},{3,2},{4,5},{5,4},{6,7},{7,6},{8,9},{9,8},{10,11... | collective-permute-start | bytes 208904 | tf_op jit(solution)/shard_map/ppermute | solution.py:89
  2.6 0.1 collective-permute-start.2
  2.7 0.4 %collective-permute-start.3 = (f32[1024,128]{1,0:T(8,128)S(1)}, f32[1024,128]{1,0:T(8,128)S(1)}, u32[]{:S(2)}, u32[]{:S(2)}) collective-permute-start(f32[1024,128]{1,0:T(8,128)S(1)} %get-tuple-element.40.x), channel_id=1, source_target_pairs={{0,1},{1,0},{2,3},{3,2},{4,5},{5,4},{6,7},{7,6},{8,9},{9,8},{10,11... | collective-permute-start | bytes 1572872 | tf_op jit(solution)/shard_map/ppermute | solution.py:89
  3.1 0.4 %collective-permute-done = f32[136,128]{1,0:T(8,128)S(1)} collective-permute-done((f32[136,128]{1,0:T(8,128)S(1)}, f32[136,128]{1,0:T(8,128)S(1)}, u32[]{:S(2)}, u32[]{:S(2)}) %collective-permute-start) | collective-permute-done | bytes 69664 | tf_op jit(solution)/shard_map/ppermute | solution.py:89
  3.6 0.4 %collective-permute-start.1 = (f32[144,128]{1,0:T(8,128)S(1)}, f32[144,128]{1,0:T(8,128)S(1)}, u32[]{:S(2)}, u32[]{:S(2)}) collective-permute-start(f32[144,128]{1,0:T(8,128)S(1)} %pad_maximum_fusion), channel_id=1, source_target_pairs={{0,1},{1,2},{2,3},{3,0},{4,5},{5,6},{6,7},{7,4},{8,9},{9,10},{10,1... | collective-permute-start | bytes 221192 | tf_op jit(solution)/shard_map/ppermute | solution.py:95
  4.0 0.2 shard_map.85
  4.2 4.1 %collective-permute-done.1 = f32[144,128]{1,0:T(8,128)S(1)} collective-permute-done((f32[144,128]{1,0:T(8,128)S(1)}, f32[144,128]{1,0:T(8,128)S(1)}, u32[]{:S(2)}, u32[]{:S(2)}) %collective-permute-start.1) | collective-permute-done | bytes 73760 | tf_op jit(solution)/shard_map/ppermute | solution.py:95
  8.3 0.0 collective-permute-done.3.mate_x
  8.3 0.7 %shard_map.86 = (f32[128,128]{1,0:T(8,128)S(1)}, f32[16,128]{1,0:T(8,128)S(1)}, f32[88,128]{1,0:T(8,128)S(1)}) custom-call(f32[128,128]{1,0:T(8,128)S(1)} %slice_add_fusion.terms, f32[32,128]{1,0:T(8,128)S(1)} %pad_maximum_fusion.1.rows, f32[128,128]{1,0:T(8,128)S(1)} %get-tuple-element.35.a, f32[1,128]{1,0:T(1,128)S(1)} %get-tuple-element.36.w, ...), custom_call_target="tpu_custom_call" | custom-call | flops 50331648 | bytes 65536 | tf_op jit(solution)/shard_map/pallas_call | solution.py:52
  9.1 1.9 %collective-permute-start.7 = (f32[88,128]{1,0:T(8,128)S(1)}, f32[88,128]{1,0:T(8,128)S(1)}, u32[]{:S(2)}, u32[]{:S(2)}) collective-permute-start(f32[88,128]{1,0:T(8,128)S(1)} %get-tuple-element.41), channel_id=1, source_target_pairs={{0,13},{1,0},{2,15},{3,2},{4,9},{5,4},{6,11},{7,6},{8,5},{9,8},{10... | collective-permute-start | bytes 135176 | tf_op jit(solution)/shard_map/ppermute | solution.py:95
  11.0 0.3 collective-permute-start.6
  11.3 0.3 %collective-permute-start.5 = (f32[88,128]{1,0:T(8,128)S(1)}, f32[88,128]{1,0:T(8,128)S(1)}, u32[]{:S(2)}, u32[]{:S(2)}) collective-permute-start(f32[88,128]{1,0:T(8,128)S(1)} %get-tuple-element.41), channel_id=1, source_target_pairs={{0,5},{1,0},{2,7},{3,2},{4,1},{5,4},{6,3},{7,6},{8,13},{9,8},{10,1... | collective-permute-start | bytes 135176 | tf_op jit(solution)/shard_map/ppermute | solution.py:95
  11.6 0.2 collective-permute-start.4
  11.8 0.3 %collective-permute-start.10 = (f32[128,128]{1,0:T(8,128)S(1)}, f32[128,128]{1,0:T(8,128)S(1)}, u32[]{:S(2)}, u32[]{:S(2)}) collective-permute-start(f32[128,128]{1,0:T(8,128)S(1)} %get-tuple-element.43.moved), channel_id=1, source_target_pairs={{0,1},{1,0},{2,3},{3,2},{4,5},{5,4},{6,7},{7,6},{8,9},{9,8},{10,11... | collective-permute-start | bytes 196616 | tf_op jit(solution)/shard_map/ppermute | solution.py:89
  12.1 0.6 %collective-permute-done.7 = f32[88,128]{1,0:T(8,128)S(1)} collective-permute-done((f32[88,128]{1,0:T(8,128)S(1)}, f32[88,128]{1,0:T(8,128)S(1)}, u32[]{:S(2)}, u32[]{:S(2)}) %collective-permute-start.7) | collective-permute-done | bytes 45088 | tf_op jit(solution)/shard_map/ppermute | solution.py:95
  12.7 0.4 %collective-permute-done.6 = f32[88,128]{1,0:T(8,128)S(1)} collective-permute-done((f32[88,128]{1,0:T(8,128)S(1)}, f32[88,128]{1,0:T(8,128)S(1)}, u32[]{:S(2)}, u32[]{:S(2)}) %collective-permute-start.6) | collective-permute-done | bytes 45088 | tf_op jit(solution)/shard_map/ppermute | solution.py:95
  13.1 0.2 collective-permute-done.5
  13.3 1.7 %collective-permute-start.9 = (f32[88,128]{1,0:T(8,128)S(1)}, f32[88,128]{1,0:T(8,128)S(1)}, u32[]{:S(2)}, u32[]{:S(2)}) collective-permute-start(f32[88,128]{1,0:T(8,128)S(1)} %add_add_fusion.1), channel_id=1, source_target_pairs={{0,1},{1,16},{2,3},{3,18},{4,5},{5,20},{6,7},{7,22},{8,9},{9,24},{... | collective-permute-start | bytes 135176 | tf_op jit(solution)/shard_map/ppermute | solution.py:95
  15.0 1.1 %collective-permute-start.8 = (f32[88,128]{1,0:T(8,128)S(1)}, f32[88,128]{1,0:T(8,128)S(1)}, u32[]{:S(2)}, u32[]{:S(2)}) collective-permute-start(f32[88,128]{1,0:T(8,128)S(1)} %add_add_fusion.1), channel_id=1, source_target_pairs={{0,1},{1,0},{2,3},{3,2},{4,5},{5,4},{6,7},{7,6},{8,9},{9,8},{10,11... | collective-permute-start | bytes 135176 | tf_op jit(solution)/shard_map/ppermute | solution.py:89
  16.1 0.0 collective-permute-done.10.mate_moved
  16.1 0.5 %shard_map.87.each = f32[16,128,128]{2,1,0:T(8,128)S(1)} custom-call(f32[1024,128]{1,0:T(8,128)S(1)} %get-tuple-element.40.x, f32[1024,128]{1,0:T(8,128)S(1)} %collective-permute-done.3.mate_x, f32[128,128]{1,0:T(8,128)S(1)} %get-tuple-element.43.moved, f32[128,128]{1,0:T(8,128)S(1)} %collective-permute-done.10.mate_moved), custom_call_target="tpu_custom_call" | custom-call | flops 402653184 | bytes 65536 | tf_op jit(solution)/shard_map/pallas_call | solution.py:52
  16.6 2.7 %collective-permute-done.9 = f32[88,128]{1,0:T(8,128)S(1)} collective-permute-done((f32[88,128]{1,0:T(8,128)S(1)}, f32[88,128]{1,0:T(8,128)S(1)}, u32[]{:S(2)}, u32[]{:S(2)}) %collective-permute-start.9) | collective-permute-done | bytes 45088 | tf_op jit(solution)/shard_map/ppermute | solution.py:95
  19.3 0.0 collective-permute-done.8
  19.3 0.3 %shard_map.88 = (f32[128,128]{1,0:T(8,128)S(1)}, f32[144,128]{1,0:T(8,128)S(1)}) custom-call(f32[88,128]{1,0:T(8,128)S(1)} %add.32.sums, f32[16,128]{1,0:T(8,128)S(1)} %get-tuple-element.42.b, f32[1,128]{1,0:T(1,128)S(1)} %get-tuple-element.36.w, f32[128,128]{1,0:T(8,128)S(1)} %get-tuple-element.38.outer_c, f32[16,128,128]{2,1,0:T(8,128)S(1)} %shard_map.87.each), custom_call_target="tpu_custom_call" | custom-call | flops 3145728 | bytes 65536 | tf_op jit(solution)/shard_map/pallas_call | solution.py:52
  19.7 0.1 collective-permute-start.14
  19.7 0.3 collective-permute-start.13
  20.0 1.2 %collective-permute-start.12 = (f32[144,128]{1,0:T(8,128)S(1)}, f32[144,128]{1,0:T(8,128)S(1)}, u32[]{:S(2)}, u32[]{:S(2)}) collective-permute-start(f32[144,128]{1,0:T(8,128)S(1)} %get-tuple-element.44), channel_id=1, source_target_pairs={{0,3},{1,0},{2,1},{3,2},{4,7},{5,4},{6,5},{7,6},{8,11},{9,8},{10,9... | collective-permute-start | bytes 221192 | tf_op jit(solution)/shard_map/ppermute | solution.py:95
  21.2 0.0 collective-permute-start.11
  21.2 0.5 %collective-permute-start.20 = (f32[128,128]{1,0:T(8,128)S(1)}, f32[128,128]{1,0:T(8,128)S(1)}, u32[]{:S(2)}, u32[]{:S(2)}) collective-permute-start(f32[128,128]{1,0:T(8,128)S(1)} %get-tuple-element.47.gram), channel_id=1, source_target_pairs={{0,1},{1,0},{2,3},{3,2},{4,5},{5,4},{6,7},{7,6},{8,9},{9,8},{10,11... | collective-permute-start | bytes 196616 | tf_op jit(solution)/shard_map/ppermute | solution.py:89
  21.7 0.0 collective-permute-done.14.refs_3_
  21.7 0.7 %collective-permute-done.13.refs_2_ = f32[144,128]{1,0:T(8,128)S(1)} collective-permute-done((f32[144,128]{1,0:T(8,128)S(1)}, f32[144,128]{1,0:T(8,128)S(1)}, u32[]{:S(2)}, u32[]{:S(2)}) %collective-permute-start.13) | collective-permute-done | bytes 73760 | tf_op jit(solution)/shard_map/ppermute | solution.py:95
  22.4 0.8 %collective-permute-done.12.refs_1_ = f32[144,128]{1,0:T(8,128)S(1)} collective-permute-done((f32[144,128]{1,0:T(8,128)S(1)}, f32[144,128]{1,0:T(8,128)S(1)}, u32[]{:S(2)}, u32[]{:S(2)}) %collective-permute-start.12) | collective-permute-done | bytes 73760 | tf_op jit(solution)/shard_map/ppermute | solution.py:95
  23.2 0.0 collective-permute-done.11.refs_0_
  23.2 0.9 %collective-permute-start.18 = (f32[128,128]{1,0:T(8,128)S(1)}, f32[128,128]{1,0:T(8,128)S(1)}, u32[]{:S(2)}, u32[]{:S(2)}) collective-permute-start(f32[128,128]{1,0:T(8,128)S(1)} %get-tuple-element.45), channel_id=1, source_target_pairs={{0,1},{1,24},{2,3},{3,26},{4,5},{5,28},{6,7},{7,30},{8,9},{9,16},{... | collective-permute-start | bytes 196616 | tf_op jit(solution)/shard_map/ppermute | solution.py:95
  24.1 1.5 %collective-permute-start.17 = (f32[128,128]{1,0:T(8,128)S(1)}, f32[128,128]{1,0:T(8,128)S(1)}, u32[]{:S(2)}, u32[]{:S(2)}) collective-permute-start(f32[128,128]{1,0:T(8,128)S(1)} %get-tuple-element.45), channel_id=1, source_target_pairs={{0,1},{1,16},{2,3},{3,18},{4,5},{5,20},{6,7},{7,22},{8,9},{9,24},{... | collective-permute-start | bytes 196616 | tf_op jit(solution)/shard_map/ppermute | solution.py:95
  25.7 0.3 %collective-permute-start.16 = (f32[128,128]{1,0:T(8,128)S(1)}, f32[128,128]{1,0:T(8,128)S(1)}, u32[]{:S(2)}, u32[]{:S(2)}) collective-permute-start(f32[128,128]{1,0:T(8,128)S(1)} %get-tuple-element.45), channel_id=1, source_target_pairs={{0,1},{1,8},{2,3},{3,10},{4,5},{5,12},{6,7},{7,14},{8,9},{9,0},{10... | collective-permute-start | bytes 196616 | tf_op jit(solution)/shard_map/ppermute | solution.py:95
  26.0 0.5 %collective-permute-start.19 = (f32[32,128]{1,0:T(8,128)S(1)}, f32[32,128]{1,0:T(8,128)S(1)}, u32[]{:S(2)}, u32[]{:S(2)}) collective-permute-start(f32[32,128]{1,0:T(8,128)S(1)} %get-tuple-element.46.rows), channel_id=1, source_target_pairs={{0,1},{1,0},{2,3},{3,2},{4,5},{5,4},{6,7},{7,6},{8,9},{9,8},{10,11... | collective-permute-start | bytes 49160 | tf_op jit(solution)/shard_map/ppermute | solution.py:89
  26.5 0.7 %shard_map.90 = (f32[128,128]{1,0:T(8,128)}, f32[1,128]{1,0:T(1,128)S(1)}, f32[128,128]{1,0:T(8,128)S(1)}) custom-call(f32[128,128]{1,0:T(8,128)S(1)} %get-tuple-element.47.gram, f32[128,128]{1,0:T(8,128)S(1)} %collective-permute-done.20.mate_gram, f32[128,128]{1,0:T(8,128)S(1)} %get-tuple-element.43.moved, ...), custom_call_target="tpu_custom_call" | custom-call | flops 131072 | bytes 65536 | tf_op jit(solution)/shard_map/pallas_call | solution.py:52
  27.2 0.2 collective-permute-done.19.mate_rows
  27.4 0.9 %shard_map.91 = (f32[8,128]{1,0:T(8,128)}, f32[128,128]{1,0:T(8,128)S(1)}, f32[1,128]{1,0:T(1,128)S(1)}, f32[1,128]{1,0:T(1,128)S(1)}) custom-call(f32[32,128]{1,0:T(8,128)S(1)} %get-tuple-element.46.rows, f32[32,128]{1,0:T(8,128)S(1)} %collective-permute-done.19.mate_rows, f32[128,128]{1,0:T(8,128)S(1)} %get-tuple-element.37.c, ...), custom_call_target="tpu_custom_call" | custom-call | flops 16777216 | bytes 65536 | tf_op jit(solution)/shard_map/pallas_call | solution.py:52
  28.2 0.6 %collective-permute-done.18 = f32[128,128]{1,0:T(8,128)S(1)} collective-permute-done((f32[128,128]{1,0:T(8,128)S(1)}, f32[128,128]{1,0:T(8,128)S(1)}, u32[]{:S(2)}, u32[]{:S(2)}) %collective-permute-start.18) | collective-permute-done | bytes 65568 | tf_op jit(solution)/shard_map/ppermute | solution.py:95
  28.8 1.3 %collective-permute-done.17 = f32[128,128]{1,0:T(8,128)S(1)} collective-permute-done((f32[128,128]{1,0:T(8,128)S(1)}, f32[128,128]{1,0:T(8,128)S(1)}, u32[]{:S(2)}, u32[]{:S(2)}) %collective-permute-start.17) | collective-permute-done | bytes 65568 | tf_op jit(solution)/shard_map/ppermute | solution.py:95
  30.1 0.0 collective-permute-done.16
  30.1 0.0 collective-permute-done.15
  30.2 0.1 collective-permute-start.21
  30.3 1.2 %collective-permute-done.21.mate_terms = f32[128,128]{1,0:T(8,128)S(1)} collective-permute-done((f32[128,128]{1,0:T(8,128)S(1)}, f32[128,128]{1,0:T(8,128)S(1)}, u32[]{:S(2)}, u32[]{:S(2)}) %collective-permute-start.21) | collective-permute-done | bytes 65568 | tf_op jit(solution)/shard_map/ppermute | solution.py:89
  31.5 0.7 %shard_map.92 = (f32[128,128]{1,0:T(8,128)}, f32[1,128]{1,0:T(1,128)}) custom-call(f32[128,128]{1,0:T(8,128)S(1)} %add_add_fusion.terms, f32[128,128]{1,0:T(8,128)S(1)} %collective-permute-done.21.mate_terms, f32[128,128]{1,0:T(8,128)S(1)} %get-tuple-element.59.base, f32[1,128]{1,0:T(1,128)S(1)} %get-tuple-element.60.gain, f32[1,128]{1,0:T(1,128)S(1)} %get-tuple-element.61.scale), custom_call_target="tpu_custom_call" | custom-call | flops 131072 | bytes 65536 | tf_op jit(solution)/shard_map/pallas_call | solution.py:52
  (15 shorter events, 0.1 us)
Async XLA Ops:
  2.1 1.4 %collective-permute-start = (f32[136,128]{1,0:T(8,128)S(1)}, f32[136,128]{1,0:T(8,128)S(1)}, u32[]{:S(2)}, u32[]{:S(2)}) collective-permute-start(f32[136,128]{1,0:T(8,128)S(1)} %get-tuple-element.34), channel_id=1, source_target_pairs={{0,1},{1,0},{2,3},{3,2},{4,5},{5,4},{6,7},{7,6},{8,9},{9,8},{10,11... | collective-permute-start | bytes 208904 | tf_op jit(solution)/shard_map/ppermute | solution.py:89
  2.6 5.7 %collective-permute-start.2 = (f32[8,128,128]{2,1,0:T(8,128)S(1)}, f32[8,128,128]{2,1,0:T(8,128)S(1)}, u32[]{:S(2)}, u32[]{:S(2)}) collective-permute-start(f32[8,128,128]{2,1,0:T(8,128)S(1)} %get-tuple-element.39.con), channel_id=1, source_target_pairs={{0,1},{1,0},{2,3},{3,2},{4,5},{5,4},{6,7},{7,6},{8,9},{9,8},{10,11... | collective-permute-start | bytes 1572872 | tf_op jit(solution)/shard_map/ppermute | solution.py:89
  2.7 5.6 %collective-permute-start.3 = (f32[1024,128]{1,0:T(8,128)S(1)}, f32[1024,128]{1,0:T(8,128)S(1)}, u32[]{:S(2)}, u32[]{:S(2)}) collective-permute-start(f32[1024,128]{1,0:T(8,128)S(1)} %get-tuple-element.40.x), channel_id=1, source_target_pairs={{0,1},{1,0},{2,3},{3,2},{4,5},{5,4},{6,7},{7,6},{8,9},{9,8},{10,11... | collective-permute-start | bytes 1572872 | tf_op jit(solution)/shard_map/ppermute | solution.py:89
  3.6 4.7 %collective-permute-start.1 = (f32[144,128]{1,0:T(8,128)S(1)}, f32[144,128]{1,0:T(8,128)S(1)}, u32[]{:S(2)}, u32[]{:S(2)}) collective-permute-start(f32[144,128]{1,0:T(8,128)S(1)} %pad_maximum_fusion), channel_id=1, source_target_pairs={{0,1},{1,2},{2,3},{3,0},{4,5},{5,6},{6,7},{7,4},{8,9},{9,10},{10,1... | collective-permute-start | bytes 221192 | tf_op jit(solution)/shard_map/ppermute | solution.py:95
  9.1 3.6 %collective-permute-start.7 = (f32[88,128]{1,0:T(8,128)S(1)}, f32[88,128]{1,0:T(8,128)S(1)}, u32[]{:S(2)}, u32[]{:S(2)}) collective-permute-start(f32[88,128]{1,0:T(8,128)S(1)} %get-tuple-element.41), channel_id=1, source_target_pairs={{0,13},{1,0},{2,15},{3,2},{4,9},{5,4},{6,11},{7,6},{8,5},{9,8},{10... | collective-permute-start | bytes 135176 | tf_op jit(solution)/shard_map/ppermute | solution.py:95
  11.0 2.1 %collective-permute-start.6 = (f32[88,128]{1,0:T(8,128)S(1)}, f32[88,128]{1,0:T(8,128)S(1)}, u32[]{:S(2)}, u32[]{:S(2)}) collective-permute-start(f32[88,128]{1,0:T(8,128)S(1)} %get-tuple-element.41), channel_id=1, source_target_pairs={{0,9},{1,0},{2,11},{3,2},{4,13},{5,4},{6,15},{7,6},{8,1},{9,8},{10... | collective-permute-start | bytes 135176 | tf_op jit(solution)/shard_map/ppermute | solution.py:95
  11.3 2.0 %collective-permute-start.5 = (f32[88,128]{1,0:T(8,128)S(1)}, f32[88,128]{1,0:T(8,128)S(1)}, u32[]{:S(2)}, u32[]{:S(2)}) collective-permute-start(f32[88,128]{1,0:T(8,128)S(1)} %get-tuple-element.41), channel_id=1, source_target_pairs={{0,5},{1,0},{2,7},{3,2},{4,1},{5,4},{6,3},{7,6},{8,13},{9,8},{10,1... | collective-permute-start | bytes 135176 | tf_op jit(solution)/shard_map/ppermute | solution.py:95
  11.6 1.7 %collective-permute-start.4 = (f32[88,128]{1,0:T(8,128)S(1)}, f32[88,128]{1,0:T(8,128)S(1)}, u32[]{:S(2)}, u32[]{:S(2)}) collective-permute-start(f32[88,128]{1,0:T(8,128)S(1)} %get-tuple-element.41), channel_id=1, source_target_pairs={{0,1},{1,0},{2,3},{3,2},{4,5},{5,4},{6,7},{7,6},{8,9},{9,8},{10,11... | collective-permute-start | bytes 135176 | tf_op jit(solution)/shard_map/ppermute | solution.py:89
  11.8 4.3 %collective-permute-start.10 = (f32[128,128]{1,0:T(8,128)S(1)}, f32[128,128]{1,0:T(8,128)S(1)}, u32[]{:S(2)}, u32[]{:S(2)}) collective-permute-start(f32[128,128]{1,0:T(8,128)S(1)} %get-tuple-element.43.moved), channel_id=1, source_target_pairs={{0,1},{1,0},{2,3},{3,2},{4,5},{5,4},{6,7},{7,6},{8,9},{9,8},{10,11... | collective-permute-start | bytes 196616 | tf_op jit(solution)/shard_map/ppermute | solution.py:89
  13.3 6.0 %collective-permute-start.9 = (f32[88,128]{1,0:T(8,128)S(1)}, f32[88,128]{1,0:T(8,128)S(1)}, u32[]{:S(2)}, u32[]{:S(2)}) collective-permute-start(f32[88,128]{1,0:T(8,128)S(1)} %add_add_fusion.1), channel_id=1, source_target_pairs={{0,1},{1,16},{2,3},{3,18},{4,5},{5,20},{6,7},{7,22},{8,9},{9,24},{... | collective-permute-start | bytes 135176 | tf_op jit(solution)/shard_map/ppermute | solution.py:95
  15.0 4.3 %collective-permute-start.8 = (f32[88,128]{1,0:T(8,128)S(1)}, f32[88,128]{1,0:T(8,128)S(1)}, u32[]{:S(2)}, u32[]{:S(2)}) collective-permute-start(f32[88,128]{1,0:T(8,128)S(1)} %add_add_fusion.1), channel_id=1, source_target_pairs={{0,1},{1,0},{2,3},{3,2},{4,5},{5,4},{6,7},{7,6},{8,9},{9,8},{10,11... | collective-permute-start | bytes 135176 | tf_op jit(solution)/shard_map/ppermute | solution.py:89
  19.7 2.0 %collective-permute-start.14 = (f32[144,128]{1,0:T(8,128)S(1)}, f32[144,128]{1,0:T(8,128)S(1)}, u32[]{:S(2)}, u32[]{:S(2)}) collective-permute-start(f32[144,128]{1,0:T(8,128)S(1)} %get-tuple-element.44), channel_id=1, source_target_pairs={{0,7},{1,0},{2,5},{3,2},{4,3},{5,4},{6,1},{7,6},{8,15},{9,8},{10,1... | collective-permute-start | bytes 221192 | tf_op jit(solution)/shard_map/ppermute | solution.py:95
  19.7 2.7 %collective-permute-start.13 = (f32[144,128]{1,0:T(8,128)S(1)}, f32[144,128]{1,0:T(8,128)S(1)}, u32[]{:S(2)}, u32[]{:S(2)}) collective-permute-start(f32[144,128]{1,0:T(8,128)S(1)} %get-tuple-element.44), channel_id=1, source_target_pairs={{0,5},{1,0},{2,7},{3,2},{4,1},{5,4},{6,3},{7,6},{8,13},{9,8},{10,1... | collective-permute-start | bytes 221192 | tf_op jit(solution)/shard_map/ppermute | solution.py:95
  20.0 3.2 %collective-permute-start.12 = (f32[144,128]{1,0:T(8,128)S(1)}, f32[144,128]{1,0:T(8,128)S(1)}, u32[]{:S(2)}, u32[]{:S(2)}) collective-permute-start(f32[144,128]{1,0:T(8,128)S(1)} %get-tuple-element.44), channel_id=1, source_target_pairs={{0,3},{1,0},{2,1},{3,2},{4,7},{5,4},{6,5},{7,6},{8,11},{9,8},{10,9... | collective-permute-start | bytes 221192 | tf_op jit(solution)/shard_map/ppermute | solution.py:95
  21.2 2.0 %collective-permute-start.11 = (f32[144,128]{1,0:T(8,128)S(1)}, f32[144,128]{1,0:T(8,128)S(1)}, u32[]{:S(2)}, u32[]{:S(2)}) collective-permute-start(f32[144,128]{1,0:T(8,128)S(1)} %get-tuple-element.44), channel_id=1, source_target_pairs={{0,1},{1,0},{2,3},{3,2},{4,5},{5,4},{6,7},{7,6},{8,9},{9,8},{10,11... | collective-permute-start | bytes 221192 | tf_op jit(solution)/shard_map/ppermute | solution.py:89
  21.2 4.8 %collective-permute-start.20 = (f32[128,128]{1,0:T(8,128)S(1)}, f32[128,128]{1,0:T(8,128)S(1)}, u32[]{:S(2)}, u32[]{:S(2)}) collective-permute-start(f32[128,128]{1,0:T(8,128)S(1)} %get-tuple-element.47.gram), channel_id=1, source_target_pairs={{0,1},{1,0},{2,3},{3,2},{4,5},{5,4},{6,7},{7,6},{8,9},{9,8},{10,11... | collective-permute-start | bytes 196616 | tf_op jit(solution)/shard_map/ppermute | solution.py:89
  23.2 5.6 %collective-permute-start.18 = (f32[128,128]{1,0:T(8,128)S(1)}, f32[128,128]{1,0:T(8,128)S(1)}, u32[]{:S(2)}, u32[]{:S(2)}) collective-permute-start(f32[128,128]{1,0:T(8,128)S(1)} %get-tuple-element.45), channel_id=1, source_target_pairs={{0,1},{1,24},{2,3},{3,26},{4,5},{5,28},{6,7},{7,30},{8,9},{9,16},{... | collective-permute-start | bytes 196616 | tf_op jit(solution)/shard_map/ppermute | solution.py:95
  24.1 6.0 %collective-permute-start.17 = (f32[128,128]{1,0:T(8,128)S(1)}, f32[128,128]{1,0:T(8,128)S(1)}, u32[]{:S(2)}, u32[]{:S(2)}) collective-permute-start(f32[128,128]{1,0:T(8,128)S(1)} %get-tuple-element.45), channel_id=1, source_target_pairs={{0,1},{1,16},{2,3},{3,18},{4,5},{5,20},{6,7},{7,22},{8,9},{9,24},{... | collective-permute-start | bytes 196616 | tf_op jit(solution)/shard_map/ppermute | solution.py:95
  25.7 4.5 %collective-permute-start.16 = (f32[128,128]{1,0:T(8,128)S(1)}, f32[128,128]{1,0:T(8,128)S(1)}, u32[]{:S(2)}, u32[]{:S(2)}) collective-permute-start(f32[128,128]{1,0:T(8,128)S(1)} %get-tuple-element.45), channel_id=1, source_target_pairs={{0,1},{1,8},{2,3},{3,10},{4,5},{5,12},{6,7},{7,14},{8,9},{9,0},{10... | collective-permute-start | bytes 196616 | tf_op jit(solution)/shard_map/ppermute | solution.py:95
  26.0 4.1 %collective-permute-start.15 = (f32[128,128]{1,0:T(8,128)S(1)}, f32[128,128]{1,0:T(8,128)S(1)}, u32[]{:S(2)}, u32[]{:S(2)}) collective-permute-start(f32[128,128]{1,0:T(8,128)S(1)} %get-tuple-element.45), channel_id=1, source_target_pairs={{0,1},{1,0},{2,3},{3,2},{4,5},{5,4},{6,7},{7,6},{8,9},{9,8},{10,11... | collective-permute-start | bytes 196616 | tf_op jit(solution)/shard_map/ppermute | solution.py:89
  26.0 1.3 %collective-permute-start.19 = (f32[32,128]{1,0:T(8,128)S(1)}, f32[32,128]{1,0:T(8,128)S(1)}, u32[]{:S(2)}, u32[]{:S(2)}) collective-permute-start(f32[32,128]{1,0:T(8,128)S(1)} %get-tuple-element.46.rows), channel_id=1, source_target_pairs={{0,1},{1,0},{2,3},{3,2},{4,5},{5,4},{6,7},{7,6},{8,9},{9,8},{10,11... | collective-permute-start | bytes 49160 | tf_op jit(solution)/shard_map/ppermute | solution.py:89
  30.2 1.3 %collective-permute-start.21 = (f32[128,128]{1,0:T(8,128)S(1)}, f32[128,128]{1,0:T(8,128)S(1)}, u32[]{:S(2)}, u32[]{:S(2)}) collective-permute-start(f32[128,128]{1,0:T(8,128)S(1)} %add_add_fusion.terms), channel_id=1, source_target_pairs={{0,1},{1,0},{2,3},{3,2},{4,5},{5,4},{6,7},{7,6},{8,9},{9,8},{10,11... | collective-permute-start | bytes 196616 | tf_op jit(solution)/shard_map/ppermute | solution.py:89

commit v14 on v13

--- a/solution.py
+++ b/solution.py
@@ -309,7 +309,7 @@
     terms, rows_b, rows_core = payload[:times], payload[times:], holder
     smp_mask = sum(chip_bits)
     for group in groups_of(chip_bits + vox_bits):
-        masks = masks_of(group)
+        masks = masks_of(group if smp_mask & sum(group) else group[::-1])
         if any(mask & smp_mask for mask in masks):
             packet = payload if rows_b.shape[0] == chip_rows else jnp.concatenate([terms, rows_b], axis=0)
             parts = fan(packet, holder, masks)

time: 32.3 us -> 33 us (1.022)
  waiting for transfers between devices: 13.2 us -> 14.2 us
    ppermute x11, waiting for transfers between devices: 11.4 us -> 12.2 us  [send(): return lax.ppermute(values, ALL, pairs)]
where the time goes in v14:
time: 33 us; the launch traced here: 32.9 us
  waiting for transfers between devices  14.2 us (43%)
  starting transfers between devices  12.3 us (37%)
  Pallas kernels  5.51 us (17%)
  between operations  0.74 us (2%)
    ppermute x11, waiting for transfers between devices, send(): return lax.ppermute(values, ALL, pairs)  12.2 us
    ppermute x11, starting transfers between devices, send(): return lax.ppermute(values, ALL, pairs)  8.61 us
    pallas_call x9, Pallas kernels, call(): pl.pallas_call(kernel, out_shape=outs, in_specs=specs, out_specs=[pl.Bloc...  5.51 us
    ppermute x11, starting transfers between devices, swap(): lax.ppermute(values, ALL, [(i, i ^ 1) for i in range(lax.axis_size(ALL))])  3.7 us
    ppermute x11, waiting for transfers between devices, swap(): lax.ppermute(values, ALL, [(i, i ^ 1) for i in range(lax.axis_size(ALL))])  2.04 us
  transfers between devices with their start and end apart: 22, of which 12 were waited for; matrix products, arithmetic and copies ran while one was open for 0% of the time, Pallas kernels for 7%

profile of v14, /device:TPU:0, one launch (start us, length us, event | category | flops | bytes accessed | tf_op | source)
XLA Modules:
  0.0 32.9 jit_solution(14057585517503486027)
XLA Ops:
  0.6 1.5 %shard_map.84 = (f32[1024,128]{1,0:T(8,128)S(1)}, f32[128,128]{1,0:T(8,128)S(1)}, f32[128,128]{1,0:T(8,128)S(1)}, f32[1,128]{1,0:T(1,128)S(1)}, f32[136,128]{1,0:T(8,128)S(1)}, /*index=5*/f32[8,128,128]{2,1,0:T(8,128)S(1)}) custom-call(f32[1024,128]{1,0:T(8,128)} %bitcast.3, f32[128,128]{1,0:T(8,128)} %c_hbm.1, f32[8,128]{1,0:T(8,128)} %b_hbm.1, ...), custom_call_target="tpu_custom_call" | custom-call | flops 201326592 | bytes 65536 | tf_op jit(solution)/shard_map/pallas_call | solution.py:52
  2.1 0.5 %collective-permute-start = (f32[136,128]{1,0:T(8,128)S(1)}, f32[136,128]{1,0:T(8,128)S(1)}, u32[]{:S(2)}, u32[]{:S(2)}) collective-permute-start(f32[136,128]{1,0:T(8,128)S(1)} %get-tuple-element.34), channel_id=1, source_target_pairs={{0,1},{1,0},{2,3},{3,2},{4,5},{5,4},{6,7},{7,6},{8,9},{9,8},{10,11... | collective-permute-start | bytes 208904 | tf_op jit(solution)/shard_map/ppermute | solution.py:89
  2.6 0.1 collective-permute-start.2
  2.7 0.4 %collective-permute-start.3 = (f32[1024,128]{1,0:T(8,128)S(1)}, f32[1024,128]{1,0:T(8,128)S(1)}, u32[]{:S(2)}, u32[]{:S(2)}) collective-permute-start(f32[1024,128]{1,0:T(8,128)S(1)} %get-tuple-element.40.x), channel_id=1, source_target_pairs={{0,1},{1,0},{2,3},{3,2},{4,5},{5,4},{6,7},{7,6},{8,9},{9,8},{10,11... | collective-permute-start | bytes 1572872 | tf_op jit(solution)/shard_map/ppermute | solution.py:89
  3.1 0.4 %collective-permute-done = f32[136,128]{1,0:T(8,128)S(1)} collective-permute-done((f32[136,128]{1,0:T(8,128)S(1)}, f32[136,128]{1,0:T(8,128)S(1)}, u32[]{:S(2)}, u32[]{:S(2)}) %collective-permute-start) | collective-permute-done | bytes 69664 | tf_op jit(solution)/shard_map/ppermute | solution.py:89
  3.6 0.4 %collective-permute-start.1 = (f32[144,128]{1,0:T(8,128)S(1)}, f32[144,128]{1,0:T(8,128)S(1)}, u32[]{:S(2)}, u32[]{:S(2)}) collective-permute-start(f32[144,128]{1,0:T(8,128)S(1)} %pad_maximum_fusion), channel_id=1, source_target_pairs={{0,1},{1,2},{2,3},{3,0},{4,5},{5,6},{6,7},{7,4},{8,9},{9,10},{10,1... | collective-permute-start | bytes 221192 | tf_op jit(solution)/shard_map/ppermute | solution.py:95
  4.0 0.2 shard_map.85
  4.2 4.1 %collective-permute-done.1 = f32[144,128]{1,0:T(8,128)S(1)} collective-permute-done((f32[144,128]{1,0:T(8,128)S(1)}, f32[144,128]{1,0:T(8,128)S(1)}, u32[]{:S(2)}, u32[]{:S(2)}) %collective-permute-start.1) | collective-permute-done | bytes 73760 | tf_op jit(solution)/shard_map/ppermute | solution.py:95
  8.3 0.0 collective-permute-done.2.mate_con
  8.3 0.0 collective-permute-done.3.mate_x
  8.3 0.7 %shard_map.86 = (f32[128,128]{1,0:T(8,128)S(1)}, f32[16,128]{1,0:T(8,128)S(1)}, f32[88,128]{1,0:T(8,128)S(1)}) custom-call(f32[128,128]{1,0:T(8,128)S(1)} %slice_add_fusion.terms, f32[32,128]{1,0:T(8,128)S(1)} %pad_maximum_fusion.1.rows, f32[128,128]{1,0:T(8,128)S(1)} %get-tuple-element.35.a, f32[1,128]{1,0:T(1,128)S(1)} %get-tuple-element.36.w, ...), custom_call_target="tpu_custom_call" | custom-call | flops 50331648 | bytes 65536 | tf_op jit(solution)/shard_map/pallas_call | solution.py:52
  9.1 1.9 %collective-permute-start.7 = (f32[88,128]{1,0:T(8,128)S(1)}, f32[88,128]{1,0:T(8,128)S(1)}, u32[]{:S(2)}, u32[]{:S(2)}) collective-permute-start(f32[88,128]{1,0:T(8,128)S(1)} %get-tuple-element.41), channel_id=1, source_target_pairs={{0,13},{1,0},{2,15},{3,2},{4,9},{5,4},{6,11},{7,6},{8,5},{9,8},{10... | collective-permute-start | bytes 135176 | tf_op jit(solution)/shard_map/ppermute | solution.py:95
  11.0 0.3 collective-permute-start.6
  11.3 0.3 collective-permute-start.5
  11.6 0.2 collective-permute-start.4
  11.8 0.3 collective-permute-start.10
  12.1 0.6 %collective-permute-done.7 = f32[88,128]{1,0:T(8,128)S(1)} collective-permute-done((f32[88,128]{1,0:T(8,128)S(1)}, f32[88,128]{1,0:T(8,128)S(1)}, u32[]{:S(2)}, u32[]{:S(2)}) %collective-permute-start.7) | collective-permute-done | bytes 45088 | tf_op jit(solution)/shard_map/ppermute | solution.py:95
  12.7 0.4 %collective-permute-done.6 = f32[88,128]{1,0:T(8,128)S(1)} collective-permute-done((f32[88,128]{1,0:T(8,128)S(1)}, f32[88,128]{1,0:T(8,128)S(1)}, u32[]{:S(2)}, u32[]{:S(2)}) %collective-permute-start.6) | collective-permute-done | bytes 45088 | tf_op jit(solution)/shard_map/ppermute | solution.py:95
  13.1 0.2 collective-permute-done.5
  13.3 0.0 collective-permute-done.4
  13.3 1.7 %collective-permute-start.9 = (f32[88,128]{1,0:T(8,128)S(1)}, f32[88,128]{1,0:T(8,128)S(1)}, u32[]{:S(2)}, u32[]{:S(2)}) collective-permute-start(f32[88,128]{1,0:T(8,128)S(1)} %add_add_fusion.1), channel_id=1, source_target_pairs={{0,1},{1,16},{2,3},{3,18},{4,5},{5,20},{6,7},{7,22},{8,9},{9,24},{... | collective-permute-start | bytes 135176 | tf_op jit(solution)/shard_map/ppermute | solution.py:95
  15.0 1.1 %collective-permute-start.8 = (f32[88,128]{1,0:T(8,128)S(1)}, f32[88,128]{1,0:T(8,128)S(1)}, u32[]{:S(2)}, u32[]{:S(2)}) collective-permute-start(f32[88,128]{1,0:T(8,128)S(1)} %add_add_fusion.1), channel_id=1, source_target_pairs={{0,1},{1,0},{2,3},{3,2},{4,5},{5,4},{6,7},{7,6},{8,9},{9,8},{10,11... | collective-permute-start | bytes 135176 | tf_op jit(solution)/shard_map/ppermute | solution.py:89
  16.1 0.0 collective-permute-done.10.mate_moved
  16.1 0.5 %shard_map.87.each = f32[16,128,128]{2,1,0:T(8,128)S(1)} custom-call(f32[1024,128]{1,0:T(8,128)S(1)} %get-tuple-element.40.x, f32[1024,128]{1,0:T(8,128)S(1)} %collective-permute-done.3.mate_x, f32[128,128]{1,0:T(8,128)S(1)} %get-tuple-element.43.moved, f32[128,128]{1,0:T(8,128)S(1)} %collective-permute-done.10.mate_moved), custom_call_target="tpu_custom_call" | custom-call | flops 402653184 | bytes 65536 | tf_op jit(solution)/shard_map/pallas_call | solution.py:52
  16.6 2.7 %collective-permute-done.9 = f32[88,128]{1,0:T(8,128)S(1)} collective-permute-done((f32[88,128]{1,0:T(8,128)S(1)}, f32[88,128]{1,0:T(8,128)S(1)}, u32[]{:S(2)}, u32[]{:S(2)}) %collective-permute-start.9) | collective-permute-done | bytes 45088 | tf_op jit(solution)/shard_map/ppermute | solution.py:95
  19.3 0.0 collective-permute-done.8
  19.3 0.3 %shard_map.88 = (f32[128,128]{1,0:T(8,128)S(1)}, f32[144,128]{1,0:T(8,128)S(1)}) custom-call(f32[88,128]{1,0:T(8,128)S(1)} %add.32.sums, f32[16,128]{1,0:T(8,128)S(1)} %get-tuple-element.42.b, f32[1,128]{1,0:T(1,128)S(1)} %get-tuple-element.36.w, f32[128,128]{1,0:T(8,128)S(1)} %get-tuple-element.38.outer_c, f32[16,128,128]{2,1,0:T(8,128)S(1)} %shard_map.87.each), custom_call_target="tpu_custom_call" | custom-call | flops 3145728 | bytes 65536 | tf_op jit(solution)/shard_map/pallas_call | solution.py:52
  19.7 0.1 collective-permute-start.14
  19.7 0.3 collective-permute-start.13
  20.0 1.2 %collective-permute-start.12 = (f32[144,128]{1,0:T(8,128)S(1)}, f32[144,128]{1,0:T(8,128)S(1)}, u32[]{:S(2)}, u32[]{:S(2)}) collective-permute-start(f32[144,128]{1,0:T(8,128)S(1)} %get-tuple-element.44), channel_id=1, source_target_pairs={{0,3},{1,0},{2,1},{3,2},{4,7},{5,4},{6,5},{7,6},{8,11},{9,8},{10,9... | collective-permute-start | bytes 221192 | tf_op jit(solution)/shard_map/ppermute | solution.py:95
  21.2 0.5 %collective-permute-start.20 = (f32[128,128]{1,0:T(8,128)S(1)}, f32[128,128]{1,0:T(8,128)S(1)}, u32[]{:S(2)}, u32[]{:S(2)}) collective-permute-start(f32[128,128]{1,0:T(8,128)S(1)} %get-tuple-element.47.gram), channel_id=1, source_target_pairs={{0,1},{1,0},{2,3},{3,2},{4,5},{5,4},{6,7},{7,6},{8,9},{9,8},{10,11... | collective-permute-start | bytes 196616 | tf_op jit(solution)/shard_map/ppermute | solution.py:89
  21.7 0.0 collective-permute-done.14.refs_3_
  21.7 0.7 %collective-permute-done.13.refs_2_ = f32[144,128]{1,0:T(8,128)S(1)} collective-permute-done((f32[144,128]{1,0:T(8,128)S(1)}, f32[144,128]{1,0:T(8,128)S(1)}, u32[]{:S(2)}, u32[]{:S(2)}) %collective-permute-start.13) | collective-permute-done | bytes 73760 | tf_op jit(solution)/shard_map/ppermute | solution.py:95
  22.4 0.8 %collective-permute-done.12.refs_1_ = f32[144,128]{1,0:T(8,128)S(1)} collective-permute-done((f32[144,128]{1,0:T(8,128)S(1)}, f32[144,128]{1,0:T(8,128)S(1)}, u32[]{:S(2)}, u32[]{:S(2)}) %collective-permute-start.12) | collective-permute-done | bytes 73760 | tf_op jit(solution)/shard_map/ppermute | solution.py:95
  23.2 0.9 %collective-permute-start.18 = (f32[128,128]{1,0:T(8,128)S(1)}, f32[128,128]{1,0:T(8,128)S(1)}, u32[]{:S(2)}, u32[]{:S(2)}) collective-permute-start(f32[128,128]{1,0:T(8,128)S(1)} %get-tuple-element.45), channel_id=1, source_target_pairs={{0,1},{1,24},{2,3},{3,26},{4,5},{5,28},{6,7},{7,30},{8,9},{9,16},{... | collective-permute-start | bytes 196616 | tf_op jit(solution)/shard_map/ppermute | solution.py:95
  24.1 1.5 %collective-permute-start.17 = (f32[128,128]{1,0:T(8,128)S(1)}, f32[128,128]{1,0:T(8,128)S(1)}, u32[]{:S(2)}, u32[]{:S(2)}) collective-permute-start(f32[128,128]{1,0:T(8,128)S(1)} %get-tuple-element.45), channel_id=1, source_target_pairs={{0,1},{1,8},{2,3},{3,10},{4,5},{5,12},{6,7},{7,14},{8,9},{9,0},{10... | collective-permute-start | bytes 196616 | tf_op jit(solution)/shard_map/ppermute | solution.py:95
  25.7 0.4 %collective-permute-start.15 = (f32[128,128]{1,0:T(8,128)S(1)}, f32[128,128]{1,0:T(8,128)S(1)}, u32[]{:S(2)}, u32[]{:S(2)}) collective-permute-start(f32[128,128]{1,0:T(8,128)S(1)} %get-tuple-element.45), channel_id=1, source_target_pairs={{0,1},{1,0},{2,3},{3,2},{4,5},{5,4},{6,7},{7,6},{8,9},{9,8},{10,11... | collective-permute-start | bytes 196616 | tf_op jit(solution)/shard_map/ppermute | solution.py:89
  26.1 0.0 collective-permute-done.20.mate_gram
  26.1 0.1 collective-permute-start.19
  26.2 0.7 %shard_map.90 = (f32[128,128]{1,0:T(8,128)}, f32[1,128]{1,0:T(1,128)S(1)}, f32[128,128]{1,0:T(8,128)S(1)}) custom-call(f32[128,128]{1,0:T(8,128)S(1)} %get-tuple-element.47.gram, f32[128,128]{1,0:T(8,128)S(1)} %collective-permute-done.20.mate_gram, f32[128,128]{1,0:T(8,128)S(1)} %get-tuple-element.43.moved, ...), custom_call_target="tpu_custom_call" | custom-call | flops 131072 | bytes 65536 | tf_op jit(solution)/shard_map/pallas_call | solution.py:52
  26.9 0.4 %collective-permute-done.19.mate_rows = f32[32,128]{1,0:T(8,128)S(1)} collective-permute-done((f32[32,128]{1,0:T(8,128)S(1)}, f32[32,128]{1,0:T(8,128)S(1)}, u32[]{:S(2)}, u32[]{:S(2)}) %collective-permute-start.19) | collective-permute-done | bytes 16416 | tf_op jit(solution)/shard_map/ppermute | solution.py:89
  27.3 0.9 %shard_map.91 = (f32[8,128]{1,0:T(8,128)}, f32[128,128]{1,0:T(8,128)S(1)}, f32[1,128]{1,0:T(1,128)S(1)}, f32[1,128]{1,0:T(1,128)S(1)}) custom-call(f32[32,128]{1,0:T(8,128)S(1)} %get-tuple-element.46.rows, f32[32,128]{1,0:T(8,128)S(1)} %collective-permute-done.19.mate_rows, f32[128,128]{1,0:T(8,128)S(1)} %get-tuple-element.37.c, ...), custom_call_target="tpu_custom_call" | custom-call | flops 16777216 | bytes 65536 | tf_op jit(solution)/shard_map/pallas_call | solution.py:52
  28.1 0.6 %collective-permute-done.18 = f32[128,128]{1,0:T(8,128)S(1)} collective-permute-done((f32[128,128]{1,0:T(8,128)S(1)}, f32[128,128]{1,0:T(8,128)S(1)}, u32[]{:S(2)}, u32[]{:S(2)}) %collective-permute-start.18) | collective-permute-done | bytes 65568 | tf_op jit(solution)/shard_map/ppermute | solution.py:95
  28.7 2.1 %collective-permute-done.16 = f32[128,128]{1,0:T(8,128)S(1)} collective-permute-done((f32[128,128]{1,0:T(8,128)S(1)}, f32[128,128]{1,0:T(8,128)S(1)}, u32[]{:S(2)}, u32[]{:S(2)}) %collective-permute-start.16) | collective-permute-done | bytes 65568 | tf_op jit(solution)/shard_map/ppermute | solution.py:95
  30.8 0.0 collective-permute-done.15
  30.9 0.1 collective-permute-start.21
  30.9 1.2 %collective-permute-done.21.mate_terms = f32[128,128]{1,0:T(8,128)S(1)} collective-permute-done((f32[128,128]{1,0:T(8,128)S(1)}, f32[128,128]{1,0:T(8,128)S(1)}, u32[]{:S(2)}, u32[]{:S(2)}) %collective-permute-start.21) | collective-permute-done | bytes 65568 | tf_op jit(solution)/shard_map/ppermute | solution.py:89
  32.2 0.7 %shard_map.92 = (f32[128,128]{1,0:T(8,128)}, f32[1,128]{1,0:T(1,128)}) custom-call(f32[128,128]{1,0:T(8,128)S(1)} %add_add_fusion.terms, f32[128,128]{1,0:T(8,128)S(1)} %collective-permute-done.21.mate_terms, f32[128,128]{1,0:T(8,128)S(1)} %get-tuple-element.59.base, f32[1,128]{1,0:T(1,128)S(1)} %get-tuple-element.60.gain, f32[1,128]{1,0:T(1,128)S(1)} %get-tuple-element.61.scale), custom_call_target="tpu_custom_call" | custom-call | flops 131072 | bytes 65536 | tf_op jit(solution)/shard_map/pallas_call | solution.py:52
  (15 shorter events, 0.1 us)
Async XLA Ops:
  2.1 1.4 %collective-permute-start = (f32[136,128]{1,0:T(8,128)S(1)}, f32[136,128]{1,0:T(8,128)S(1)}, u32[]{:S(2)}, u32[]{:S(2)}) collective-permute-start(f32[136,128]{1,0:T(8,128)S(1)} %get-tuple-element.34), channel_id=1, source_target_pairs={{0,1},{1,0},{2,3},{3,2},{4,5},{5,4},{6,7},{7,6},{8,9},{9,8},{10,11... | collective-permute-start | bytes 208904 | tf_op jit(solution)/shard_map/ppermute | solution.py:89
  2.6 5.7 %collective-permute-start.2 = (f32[8,128,128]{2,1,0:T(8,128)S(1)}, f32[8,128,128]{2,1,0:T(8,128)S(1)}, u32[]{:S(2)}, u32[]{:S(2)}) collective-permute-start(f32[8,128,128]{2,1,0:T(8,128)S(1)} %get-tuple-element.39.con), channel_id=1, source_target_pairs={{0,1},{1,0},{2,3},{3,2},{4,5},{5,4},{6,7},{7,6},{8,9},{9,8},{10,11... | collective-permute-start | bytes 1572872 | tf_op jit(solution)/shard_map/ppermute | solution.py:89
  2.7 5.6 %collective-permute-start.3 = (f32[1024,128]{1,0:T(8,128)S(1)}, f32[1024,128]{1,0:T(8,128)S(1)}, u32[]{:S(2)}, u32[]{:S(2)}) collective-permute-start(f32[1024,128]{1,0:T(8,128)S(1)} %get-tuple-element.40.x), channel_id=1, source_target_pairs={{0,1},{1,0},{2,3},{3,2},{4,5},{5,4},{6,7},{7,6},{8,9},{9,8},{10,11... | collective-permute-start | bytes 1572872 | tf_op jit(solution)/shard_map/ppermute | solution.py:89
  3.6 4.7 %collective-permute-start.1 = (f32[144,128]{1,0:T(8,128)S(1)}, f32[144,128]{1,0:T(8,128)S(1)}, u32[]{:S(2)}, u32[]{:S(2)}) collective-permute-start(f32[144,128]{1,0:T(8,128)S(1)} %pad_maximum_fusion), channel_id=1, source_target_pairs={{0,1},{1,2},{2,3},{3,0},{4,5},{5,6},{6,7},{7,4},{8,9},{9,10},{10,1... | collective-permute-start | bytes 221192 | tf_op jit(solution)/shard_map/ppermute | solution.py:95
  9.1 3.6 %collective-permute-start.7 = (f32[88,128]{1,0:T(8,128)S(1)}, f32[88,128]{1,0:T(8,128)S(1)}, u32[]{:S(2)}, u32[]{:S(2)}) collective-permute-start(f32[88,128]{1,0:T(8,128)S(1)} %get-tuple-element.41), channel_id=1, source_target_pairs={{0,13},{1,0},{2,15},{3,2},{4,9},{5,4},{6,11},{7,6},{8,5},{9,8},{10... | collective-permute-start | bytes 135176 | tf_op jit(solution)/shard_map/ppermute | solution.py:95
  11.0 2.1 %collective-permute-start.6 = (f32[88,128]{1,0:T(8,128)S(1)}, f32[88,128]{1,0:T(8,128)S(1)}, u32[]{:S(2)}, u32[]{:S(2)}) collective-permute-start(f32[88,128]{1,0:T(8,128)S(1)} %get-tuple-element.41), channel_id=1, source_target_pairs={{0,9},{1,0},{2,11},{3,2},{4,13},{5,4},{6,15},{7,6},{8,1},{9,8},{10... | collective-permute-start | bytes 135176 | tf_op jit(solution)/shard_map/ppermute | solution.py:95
  11.3 2.0 %collective-permute-start.5 = (f32[88,128]{1,0:T(8,128)S(1)}, f32[88,128]{1,0:T(8,128)S(1)}, u32[]{:S(2)}, u32[]{:S(2)}) collective-permute-start(f32[88,128]{1,0:T(8,128)S(1)} %get-tuple-element.41), channel_id=1, source_target_pairs={{0,5},{1,0},{2,7},{3,2},{4,1},{5,4},{6,3},{7,6},{8,13},{9,8},{10,1... | collective-permute-start | bytes 135176 | tf_op jit(solution)/shard_map/ppermute | solution.py:95
  11.6 1.7 %collective-permute-start.4 = (f32[88,128]{1,0:T(8,128)S(1)}, f32[88,128]{1,0:T(8,128)S(1)}, u32[]{:S(2)}, u32[]{:S(2)}) collective-permute-start(f32[88,128]{1,0:T(8,128)S(1)} %get-tuple-element.41), channel_id=1, source_target_pairs={{0,1},{1,0},{2,3},{3,2},{4,5},{5,4},{6,7},{7,6},{8,9},{9,8},{10,11... | collective-permute-start | bytes 135176 | tf_op jit(solution)/shard_map/ppermute | solution.py:89
  11.8 4.3 %collective-permute-start.10 = (f32[128,128]{1,0:T(8,128)S(1)}, f32[128,128]{1,0:T(8,128)S(1)}, u32[]{:S(2)}, u32[]{:S(2)}) collective-permute-start(f32[128,128]{1,0:T(8,128)S(1)} %get-tuple-element.43.moved), channel_id=1, source_target_pairs={{0,1},{1,0},{2,3},{3,2},{4,5},{5,4},{6,7},{7,6},{8,9},{9,8},{10,11... | collective-permute-start | bytes 196616 | tf_op jit(solution)/shard_map/ppermute | solution.py:89
  13.3 6.0 %collective-permute-start.9 = (f32[88,128]{1,0:T(8,128)S(1)}, f32[88,128]{1,0:T(8,128)S(1)}, u32[]{:S(2)}, u32[]{:S(2)}) collective-permute-start(f32[88,128]{1,0:T(8,128)S(1)} %add_add_fusion.1), channel_id=1, source_target_pairs={{0,1},{1,16},{2,3},{3,18},{4,5},{5,20},{6,7},{7,22},{8,9},{9,24},{... | collective-permute-start | bytes 135176 | tf_op jit(solution)/shard_map/ppermute | solution.py:95
  15.0 4.3 %collective-permute-start.8 = (f32[88,128]{1,0:T(8,128)S(1)}, f32[88,128]{1,0:T(8,128)S(1)}, u32[]{:S(2)}, u32[]{:S(2)}) collective-permute-start(f32[88,128]{1,0:T(8,128)S(1)} %add_add_fusion.1), channel_id=1, source_target_pairs={{0,1},{1,0},{2,3},{3,2},{4,5},{5,4},{6,7},{7,6},{8,9},{9,8},{10,11... | collective-permute-start | bytes 135176 | tf_op jit(solution)/shard_map/ppermute | solution.py:89
  19.7 2.0 %collective-permute-start.14 = (f32[144,128]{1,0:T(8,128)S(1)}, f32[144,128]{1,0:T(8,128)S(1)}, u32[]{:S(2)}, u32[]{:S(2)}) collective-permute-start(f32[144,128]{1,0:T(8,128)S(1)} %get-tuple-element.44), channel_id=1, source_target_pairs={{0,7},{1,0},{2,5},{3,2},{4,3},{5,4},{6,1},{7,6},{8,15},{9,8},{10,1... | collective-permute-start | bytes 221192 | tf_op jit(solution)/shard_map/ppermute | solution.py:95
  19.7 2.7 %collective-permute-start.13 = (f32[144,128]{1,0:T(8,128)S(1)}, f32[144,128]{1,0:T(8,128)S(1)}, u32[]{:S(2)}, u32[]{:S(2)}) collective-permute-start(f32[144,128]{1,0:T(8,128)S(1)} %get-tuple-element.44), channel_id=1, source_target_pairs={{0,5},{1,0},{2,7},{3,2},{4,1},{5,4},{6,3},{7,6},{8,13},{9,8},{10,1... | collective-permute-start | bytes 221192 | tf_op jit(solution)/shard_map/ppermute | solution.py:95
  20.0 3.2 %collective-permute-start.12 = (f32[144,128]{1,0:T(8,128)S(1)}, f32[144,128]{1,0:T(8,128)S(1)}, u32[]{:S(2)}, u32[]{:S(2)}) collective-permute-start(f32[144,128]{1,0:T(8,128)S(1)} %get-tuple-element.44), channel_id=1, source_target_pairs={{0,3},{1,0},{2,1},{3,2},{4,7},{5,4},{6,5},{7,6},{8,11},{9,8},{10,9... | collective-permute-start | bytes 221192 | tf_op jit(solution)/shard_map/ppermute | solution.py:95
  21.2 2.0 %collective-permute-start.11 = (f32[144,128]{1,0:T(8,128)S(1)}, f32[144,128]{1,0:T(8,128)S(1)}, u32[]{:S(2)}, u32[]{:S(2)}) collective-permute-start(f32[144,128]{1,0:T(8,128)S(1)} %get-tuple-element.44), channel_id=1, source_target_pairs={{0,1},{1,0},{2,3},{3,2},{4,5},{5,4},{6,7},{7,6},{8,9},{9,8},{10,11... | collective-permute-start | bytes 221192 | tf_op jit(solution)/shard_map/ppermute | solution.py:89
  21.2 4.9 %collective-permute-start.20 = (f32[128,128]{1,0:T(8,128)S(1)}, f32[128,128]{1,0:T(8,128)S(1)}, u32[]{:S(2)}, u32[]{:S(2)}) collective-permute-start(f32[128,128]{1,0:T(8,128)S(1)} %get-tuple-element.47.gram), channel_id=1, source_target_pairs={{0,1},{1,0},{2,3},{3,2},{4,5},{5,4},{6,7},{7,6},{8,9},{9,8},{10,11... | collective-permute-start | bytes 196616 | tf_op jit(solution)/shard_map/ppermute | solution.py:89
  23.2 5.5 %collective-permute-start.18 = (f32[128,128]{1,0:T(8,128)S(1)}, f32[128,128]{1,0:T(8,128)S(1)}, u32[]{:S(2)}, u32[]{:S(2)}) collective-permute-start(f32[128,128]{1,0:T(8,128)S(1)} %get-tuple-element.45), channel_id=1, source_target_pairs={{0,1},{1,24},{2,3},{3,26},{4,5},{5,28},{6,7},{7,30},{8,9},{9,16},{... | collective-permute-start | bytes 196616 | tf_op jit(solution)/shard_map/ppermute | solution.py:95
  24.1 4.6 %collective-permute-start.17 = (f32[128,128]{1,0:T(8,128)S(1)}, f32[128,128]{1,0:T(8,128)S(1)}, u32[]{:S(2)}, u32[]{:S(2)}) collective-permute-start(f32[128,128]{1,0:T(8,128)S(1)} %get-tuple-element.45), channel_id=1, source_target_pairs={{0,1},{1,8},{2,3},{3,10},{4,5},{5,12},{6,7},{7,14},{8,9},{9,0},{10... | collective-permute-start | bytes 196616 | tf_op jit(solution)/shard_map/ppermute | solution.py:95
  25.7 5.2 %collective-permute-start.16 = (f32[128,128]{1,0:T(8,128)S(1)}, f32[128,128]{1,0:T(8,128)S(1)}, u32[]{:S(2)}, u32[]{:S(2)}) collective-permute-start(f32[128,128]{1,0:T(8,128)S(1)} %get-tuple-element.45), channel_id=1, source_target_pairs={{0,1},{1,16},{2,3},{3,18},{4,5},{5,20},{6,7},{7,22},{8,9},{9,24},{... | collective-permute-start | bytes 196616 | tf_op jit(solution)/shard_map/ppermute | solution.py:95
  25.7 5.2 %collective-permute-start.15 = (f32[128,128]{1,0:T(8,128)S(1)}, f32[128,128]{1,0:T(8,128)S(1)}, u32[]{:S(2)}, u32[]{:S(2)}) collective-permute-start(f32[128,128]{1,0:T(8,128)S(1)} %get-tuple-element.45), channel_id=1, source_target_pairs={{0,1},{1,0},{2,3},{3,2},{4,5},{5,4},{6,7},{7,6},{8,9},{9,8},{10,11... | collective-permute-start | bytes 196616 | tf_op jit(solution)/shard_map/ppermute | solution.py:89
  26.1 1.2 %collective-permute-start.19 = (f32[32,128]{1,0:T(8,128)S(1)}, f32[32,128]{1,0:T(8,128)S(1)}, u32[]{:S(2)}, u32[]{:S(2)}) collective-permute-start(f32[32,128]{1,0:T(8,128)S(1)} %get-tuple-element.46.rows), channel_id=1, source_target_pairs={{0,1},{1,0},{2,3},{3,2},{4,5},{5,4},{6,7},{7,6},{8,9},{9,8},{10,11... | collective-permute-start | bytes 49160 | tf_op jit(solution)/shard_map/ppermute | solution.py:89
  30.9 1.3 %collective-permute-start.21 = (f32[128,128]{1,0:T(8,128)S(1)}, f32[128,128]{1,0:T(8,128)S(1)}, u32[]{:S(2)}, u32[]{:S(2)}) collective-permute-start(f32[128,128]{1,0:T(8,128)S(1)} %add_add_fusion.terms), channel_id=1, source_target_pairs={{0,1},{1,0},{2,3},{3,2},{4,5},{5,4},{6,7},{7,6},{8,9},{9,8},{10,11... | collective-permute-start | bytes 196616 | tf_op jit(solution)/shard_map/ppermute | solution.py:89

commit v15 on v13

--- a/solution.py
+++ b/solution.py
@@ -251,7 +251,7 @@
 
     mate_moved_a = swap(moved_a)
 
-    for group in groups_of(vox_bits):
+    for group in groups_of(vox_bits[:1] + vox_bits[:0:-1]):
         sums = tree(fan(sums, holder, masks_of(group)))
         holder ^= 1
     sample_core = holder

time: 32.3 us -> 32.1 us (level)
  waiting for transfers between devices: 13.2 us -> 11.7 us
  starting transfers between devices: 12.6 us -> 14 us
    ppermute x11, starting transfers between devices: 8.93 us -> 10.7 us  [send(): return lax.ppermute(values, ALL, pairs)]
    ppermute x11, waiting for transfers between devices: 11.4 us -> 9.88 us  [send(): return lax.ppermute(values, ALL, pairs)]
    ppermute x11, starting transfers between devices: 3.7 us -> 3.24 us  [swap(): lax.ppermute(values, ALL, [(i, i ^ 1) for i in range(lax.axis_size(ALL))])]
where the time goes in v15:
time: 32.1 us; the launch traced here: 32 us
  starting transfers between devices  14 us (44%)
  waiting for transfers between devices  11.7 us (36%)
  Pallas kernels  5.51 us (17%)
  between operations  0.74 us (2%)
    ppermute x11, starting transfers between devices, send(): return lax.ppermute(values, ALL, pairs)  10.7 us
    ppermute x11, waiting for transfers between devices, send(): return lax.ppermute(values, ALL, pairs)  9.88 us
    pallas_call x9, Pallas kernels, call(): pl.pallas_call(kernel, out_shape=outs, in_specs=specs, out_specs=[pl.Bloc...  5.51 us
    ppermute x11, starting transfers between devices, swap(): lax.ppermute(values, ALL, [(i, i ^ 1) for i in range(lax.axis_size(ALL))])  3.24 us
    ppermute x11, waiting for transfers between devices, swap(): lax.ppermute(values, ALL, [(i, i ^ 1) for i in range(lax.axis_size(ALL))])  1.81 us
  transfers between devices with their start and end apart: 22, of which 12 were waited for; matrix products, arithmetic and copies ran while one was open for 0% of the time, Pallas kernels for 7%

profile of v15, /device:TPU:0, one launch (start us, length us, event | category | flops | bytes accessed | tf_op | source)
XLA Modules:
  0.0 32.0 jit_solution(12878925937804489796)
XLA Ops:
  0.6 1.5 %shard_map.84 = (f32[1024,128]{1,0:T(8,128)S(1)}, f32[128,128]{1,0:T(8,128)S(1)}, f32[128,128]{1,0:T(8,128)S(1)}, f32[1,128]{1,0:T(1,128)S(1)}, f32[136,128]{1,0:T(8,128)S(1)}, /*index=5*/f32[8,128,128]{2,1,0:T(8,128)S(1)}) custom-call(f32[1024,128]{1,0:T(8,128)} %bitcast.3, f32[128,128]{1,0:T(8,128)} %c_hbm.1, f32[8,128]{1,0:T(8,128)} %b_hbm.1, ...), custom_call_target="tpu_custom_call" | custom-call | flops 201326592 | bytes 65536 | tf_op jit(solution)/shard_map/pallas_call | solution.py:52
  2.1 0.5 %collective-permute-start = (f32[136,128]{1,0:T(8,128)S(1)}, f32[136,128]{1,0:T(8,128)S(1)}, u32[]{:S(2)}, u32[]{:S(2)}) collective-permute-start(f32[136,128]{1,0:T(8,128)S(1)} %get-tuple-element.34), channel_id=1, source_target_pairs={{0,1},{1,0},{2,3},{3,2},{4,5},{5,4},{6,7},{7,6},{8,9},{9,8},{10,11... | collective-permute-start | bytes 208904 | tf_op jit(solution)/shard_map/ppermute | solution.py:89
  2.6 0.1 collective-permute-start.2
  2.7 0.4 %collective-permute-start.3 = (f32[1024,128]{1,0:T(8,128)S(1)}, f32[1024,128]{1,0:T(8,128)S(1)}, u32[]{:S(2)}, u32[]{:S(2)}) collective-permute-start(f32[1024,128]{1,0:T(8,128)S(1)} %get-tuple-element.40.x), channel_id=1, source_target_pairs={{0,1},{1,0},{2,3},{3,2},{4,5},{5,4},{6,7},{7,6},{8,9},{9,8},{10,11... | collective-permute-start | bytes 1572872 | tf_op jit(solution)/shard_map/ppermute | solution.py:89
  3.1 0.4 %collective-permute-done = f32[136,128]{1,0:T(8,128)S(1)} collective-permute-done((f32[136,128]{1,0:T(8,128)S(1)}, f32[136,128]{1,0:T(8,128)S(1)}, u32[]{:S(2)}, u32[]{:S(2)}) %collective-permute-start) | collective-permute-done | bytes 69664 | tf_op jit(solution)/shard_map/ppermute | solution.py:89
  3.6 0.4 %collective-permute-start.1 = (f32[144,128]{1,0:T(8,128)S(1)}, f32[144,128]{1,0:T(8,128)S(1)}, u32[]{:S(2)}, u32[]{:S(2)}) collective-permute-start(f32[144,128]{1,0:T(8,128)S(1)} %pad_maximum_fusion), channel_id=1, source_target_pairs={{0,1},{1,2},{2,3},{3,0},{4,5},{5,6},{6,7},{7,4},{8,9},{9,10},{10,1... | collective-permute-start | bytes 221192 | tf_op jit(solution)/shard_map/ppermute | solution.py:95
  4.0 0.2 shard_map.85
  4.2 4.1 %collective-permute-done.1 = f32[144,128]{1,0:T(8,128)S(1)} collective-permute-done((f32[144,128]{1,0:T(8,128)S(1)}, f32[144,128]{1,0:T(8,128)S(1)}, u32[]{:S(2)}, u32[]{:S(2)}) %collective-permute-start.1) | collective-permute-done | bytes 73760 | tf_op jit(solution)/shard_map/ppermute | solution.py:95
  8.3 0.0 collective-permute-done.2.mate_con
  8.3 0.0 collective-permute-done.3.mate_x
  8.3 0.7 %shard_map.86 = (f32[128,128]{1,0:T(8,128)S(1)}, f32[16,128]{1,0:T(8,128)S(1)}, f32[88,128]{1,0:T(8,128)S(1)}) custom-call(f32[128,128]{1,0:T(8,128)S(1)} %slice_add_fusion.terms, f32[32,128]{1,0:T(8,128)S(1)} %pad_maximum_fusion.1.rows, f32[128,128]{1,0:T(8,128)S(1)} %get-tuple-element.35.a, f32[1,128]{1,0:T(1,128)S(1)} %get-tuple-element.36.w, ...), custom_call_target="tpu_custom_call" | custom-call | flops 50331648 | bytes 65536 | tf_op jit(solution)/shard_map/pallas_call | solution.py:52
  9.1 2.9 %collective-permute-start.7 = (f32[88,128]{1,0:T(8,128)S(1)}, f32[88,128]{1,0:T(8,128)S(1)}, u32[]{:S(2)}, u32[]{:S(2)}) collective-permute-start(f32[88,128]{1,0:T(8,128)S(1)} %get-tuple-element.41), channel_id=1, source_target_pairs={{0,21},{1,0},{2,23},{3,2},{4,17},{5,4},{6,19},{7,6},{8,29},{9,8},{... | collective-permute-start | bytes 135176 | tf_op jit(solution)/shard_map/ppermute | solution.py:95
  12.0 0.3 collective-permute-start.6
  12.3 0.3 %collective-permute-start.5 = (f32[88,128]{1,0:T(8,128)S(1)}, f32[88,128]{1,0:T(8,128)S(1)}, u32[]{:S(2)}, u32[]{:S(2)}) collective-permute-start(f32[88,128]{1,0:T(8,128)S(1)} %get-tuple-element.41), channel_id=1, source_target_pairs={{0,5},{1,0},{2,7},{3,2},{4,1},{5,4},{6,3},{7,6},{8,13},{9,8},{10,1... | collective-permute-start | bytes 135176 | tf_op jit(solution)/shard_map/ppermute | solution.py:95
  12.6 0.2 collective-permute-start.4
  12.8 0.3 %collective-permute-start.10 = (f32[128,128]{1,0:T(8,128)S(1)}, f32[128,128]{1,0:T(8,128)S(1)}, u32[]{:S(2)}, u32[]{:S(2)}) collective-permute-start(f32[128,128]{1,0:T(8,128)S(1)} %get-tuple-element.43.moved), channel_id=1, source_target_pairs={{0,1},{1,0},{2,3},{3,2},{4,5},{5,4},{6,7},{7,6},{8,9},{9,8},{10,11... | collective-permute-start | bytes 196616 | tf_op jit(solution)/shard_map/ppermute | solution.py:89
  13.1 0.6 %collective-permute-done.7 = f32[88,128]{1,0:T(8,128)S(1)} collective-permute-done((f32[88,128]{1,0:T(8,128)S(1)}, f32[88,128]{1,0:T(8,128)S(1)}, u32[]{:S(2)}, u32[]{:S(2)}) %collective-permute-start.7) | collective-permute-done | bytes 45088 | tf_op jit(solution)/shard_map/ppermute | solution.py:95
  13.7 0.4 %collective-permute-done.6 = f32[88,128]{1,0:T(8,128)S(1)} collective-permute-done((f32[88,128]{1,0:T(8,128)S(1)}, f32[88,128]{1,0:T(8,128)S(1)}, u32[]{:S(2)}, u32[]{:S(2)}) %collective-permute-start.6) | collective-permute-done | bytes 45088 | tf_op jit(solution)/shard_map/ppermute | solution.py:95
  14.1 0.2 collective-permute-done.5
  14.3 0.0 collective-permute-done.4
  14.4 1.7 %collective-permute-start.9 = (f32[88,128]{1,0:T(8,128)S(1)}, f32[88,128]{1,0:T(8,128)S(1)}, u32[]{:S(2)}, u32[]{:S(2)}) collective-permute-start(f32[88,128]{1,0:T(8,128)S(1)} %add_add_fusion.1), channel_id=1, source_target_pairs={{0,1},{1,8},{2,3},{3,10},{4,5},{5,12},{6,7},{7,14},{8,9},{9,0},{10... | collective-permute-start | bytes 135176 | tf_op jit(solution)/shard_map/ppermute | solution.py:95
  16.0 0.6 %collective-permute-start.8 = (f32[88,128]{1,0:T(8,128)S(1)}, f32[88,128]{1,0:T(8,128)S(1)}, u32[]{:S(2)}, u32[]{:S(2)}) collective-permute-start(f32[88,128]{1,0:T(8,128)S(1)} %add_add_fusion.1), channel_id=1, source_target_pairs={{0,1},{1,0},{2,3},{3,2},{4,5},{5,4},{6,7},{7,6},{8,9},{9,8},{10,11... | collective-permute-start | bytes 135176 | tf_op jit(solution)/shard_map/ppermute | solution.py:89
  16.6 0.0 collective-permute-done.10.mate_moved
  16.6 0.5 %shard_map.87.each = f32[16,128,128]{2,1,0:T(8,128)S(1)} custom-call(f32[1024,128]{1,0:T(8,128)S(1)} %get-tuple-element.40.x, f32[1024,128]{1,0:T(8,128)S(1)} %collective-permute-done.3.mate_x, f32[128,128]{1,0:T(8,128)S(1)} %get-tuple-element.43.moved, f32[128,128]{1,0:T(8,128)S(1)} %collective-permute-done.10.mate_moved), custom_call_target="tpu_custom_call" | custom-call | flops 402653184 | bytes 65536 | tf_op jit(solution)/shard_map/pallas_call | solution.py:52
  17.1 1.8 %collective-permute-done.9 = f32[88,128]{1,0:T(8,128)S(1)} collective-permute-done((f32[88,128]{1,0:T(8,128)S(1)}, f32[88,128]{1,0:T(8,128)S(1)}, u32[]{:S(2)}, u32[]{:S(2)}) %collective-permute-start.9) | collective-permute-done | bytes 45088 | tf_op jit(solution)/shard_map/ppermute | solution.py:95
  18.9 0.0 collective-permute-done.8
  18.9 0.3 %shard_map.88 = (f32[128,128]{1,0:T(8,128)S(1)}, f32[144,128]{1,0:T(8,128)S(1)}) custom-call(f32[88,128]{1,0:T(8,128)S(1)} %add.32.sums, f32[16,128]{1,0:T(8,128)S(1)} %get-tuple-element.42.b, f32[1,128]{1,0:T(1,128)S(1)} %get-tuple-element.36.w, f32[128,128]{1,0:T(8,128)S(1)} %get-tuple-element.38.outer_c, f32[16,128,128]{2,1,0:T(8,128)S(1)} %shard_map.87.each), custom_call_target="tpu_custom_call" | custom-call | flops 3145728 | bytes 65536 | tf_op jit(solution)/shard_map/pallas_call | solution.py:52
  19.3 0.4 %collective-permute-start.14 = (f32[144,128]{1,0:T(8,128)S(1)}, f32[144,128]{1,0:T(8,128)S(1)}, u32[]{:S(2)}, u32[]{:S(2)}) collective-permute-start(f32[144,128]{1,0:T(8,128)S(1)} %get-tuple-element.44), channel_id=1, source_target_pairs={{0,7},{1,0},{2,5},{3,2},{4,3},{5,4},{6,1},{7,6},{8,15},{9,8},{10,1... | collective-permute-start | bytes 221192 | tf_op jit(solution)/shard_map/ppermute | solution.py:95
  19.7 0.3 collective-permute-start.13
  20.0 0.7 %collective-permute-start.12 = (f32[144,128]{1,0:T(8,128)S(1)}, f32[144,128]{1,0:T(8,128)S(1)}, u32[]{:S(2)}, u32[]{:S(2)}) collective-permute-start(f32[144,128]{1,0:T(8,128)S(1)} %get-tuple-element.44), channel_id=1, source_target_pairs={{0,3},{1,0},{2,1},{3,2},{4,7},{5,4},{6,5},{7,6},{8,11},{9,8},{10,9... | collective-permute-start | bytes 221192 | tf_op jit(solution)/shard_map/ppermute | solution.py:95
  20.7 0.0 collective-permute-start.11
  20.7 0.5 %collective-permute-start.20 = (f32[128,128]{1,0:T(8,128)S(1)}, f32[128,128]{1,0:T(8,128)S(1)}, u32[]{:S(2)}, u32[]{:S(2)}) collective-permute-start(f32[128,128]{1,0:T(8,128)S(1)} %get-tuple-element.47.gram), channel_id=1, source_target_pairs={{0,1},{1,0},{2,3},{3,2},{4,5},{5,4},{6,7},{7,6},{8,9},{9,8},{10,11... | collective-permute-start | bytes 196616 | tf_op jit(solution)/shard_map/ppermute | solution.py:89
  21.2 0.5 %collective-permute-done.14.refs_3_ = f32[144,128]{1,0:T(8,128)S(1)} collective-permute-done((f32[144,128]{1,0:T(8,128)S(1)}, f32[144,128]{1,0:T(8,128)S(1)}, u32[]{:S(2)}, u32[]{:S(2)}) %collective-permute-start.14) | collective-permute-done | bytes 73760 | tf_op jit(solution)/shard_map/ppermute | solution.py:95
  21.7 0.7 %collective-permute-done.13.refs_2_ = f32[144,128]{1,0:T(8,128)S(1)} collective-permute-done((f32[144,128]{1,0:T(8,128)S(1)}, f32[144,128]{1,0:T(8,128)S(1)}, u32[]{:S(2)}, u32[]{:S(2)}) %collective-permute-start.13) | collective-permute-done | bytes 73760 | tf_op jit(solution)/shard_map/ppermute | solution.py:95
  22.4 0.3 collective-permute-done.12.refs_1_
  22.7 1.4 %collective-permute-start.18 = (f32[128,128]{1,0:T(8,128)S(1)}, f32[128,128]{1,0:T(8,128)S(1)}, u32[]{:S(2)}, u32[]{:S(2)}) collective-permute-start(f32[128,128]{1,0:T(8,128)S(1)} %get-tuple-element.45), channel_id=1, source_target_pairs={{0,1},{1,24},{2,3},{3,26},{4,5},{5,28},{6,7},{7,30},{8,9},{9,16},{... | collective-permute-start | bytes 196616 | tf_op jit(solution)/shard_map/ppermute | solution.py:95
  24.1 1.2 %collective-permute-start.17 = (f32[128,128]{1,0:T(8,128)S(1)}, f32[128,128]{1,0:T(8,128)S(1)}, u32[]{:S(2)}, u32[]{:S(2)}) collective-permute-start(f32[128,128]{1,0:T(8,128)S(1)} %get-tuple-element.45), channel_id=1, source_target_pairs={{0,1},{1,16},{2,3},{3,18},{4,5},{5,20},{6,7},{7,22},{8,9},{9,24},{... | collective-permute-start | bytes 196616 | tf_op jit(solution)/shard_map/ppermute | solution.py:95
  25.3 1.1 %collective-permute-start.16 = (f32[128,128]{1,0:T(8,128)S(1)}, f32[128,128]{1,0:T(8,128)S(1)}, u32[]{:S(2)}, u32[]{:S(2)}) collective-permute-start(f32[128,128]{1,0:T(8,128)S(1)} %get-tuple-element.45), channel_id=1, source_target_pairs={{0,1},{1,8},{2,3},{3,10},{4,5},{5,12},{6,7},{7,14},{8,9},{9,0},{10... | collective-permute-start | bytes 196616 | tf_op jit(solution)/shard_map/ppermute | solution.py:95
  26.4 0.5 %collective-permute-start.19 = (f32[32,128]{1,0:T(8,128)S(1)}, f32[32,128]{1,0:T(8,128)S(1)}, u32[]{:S(2)}, u32[]{:S(2)}) collective-permute-start(f32[32,128]{1,0:T(8,128)S(1)} %get-tuple-element.46.rows), channel_id=1, source_target_pairs={{0,1},{1,0},{2,3},{3,2},{4,5},{5,4},{6,7},{7,6},{8,9},{9,8},{10,11... | collective-permute-start | bytes 49160 | tf_op jit(solution)/shard_map/ppermute | solution.py:89
  26.9 0.7 %shard_map.90 = (f32[128,128]{1,0:T(8,128)}, f32[1,128]{1,0:T(1,128)S(1)}, f32[128,128]{1,0:T(8,128)S(1)}) custom-call(f32[128,128]{1,0:T(8,128)S(1)} %get-tuple-element.47.gram, f32[128,128]{1,0:T(8,128)S(1)} %collective-permute-done.20.mate_gram, f32[128,128]{1,0:T(8,128)S(1)} %get-tuple-element.43.moved, ...), custom_call_target="tpu_custom_call" | custom-call | flops 131072 | bytes 65536 | tf_op jit(solution)/shard_map/pallas_call | solution.py:52
  27.6 0.2 collective-permute-done.19.mate_rows
  27.8 0.9 %shard_map.91 = (f32[8,128]{1,0:T(8,128)}, f32[128,128]{1,0:T(8,128)S(1)}, f32[1,128]{1,0:T(1,128)S(1)}, f32[1,128]{1,0:T(1,128)S(1)}) custom-call(f32[32,128]{1,0:T(8,128)S(1)} %get-tuple-element.46.rows, f32[32,128]{1,0:T(8,128)S(1)} %collective-permute-done.19.mate_rows, f32[128,128]{1,0:T(8,128)S(1)} %get-tuple-element.37.c, ...), custom_call_target="tpu_custom_call" | custom-call | flops 16777216 | bytes 65536 | tf_op jit(solution)/shard_map/pallas_call | solution.py:52
  28.6 1.3 %collective-permute-done.17 = f32[128,128]{1,0:T(8,128)S(1)} collective-permute-done((f32[128,128]{1,0:T(8,128)S(1)}, f32[128,128]{1,0:T(8,128)S(1)}, u32[]{:S(2)}, u32[]{:S(2)}) %collective-permute-start.17) | collective-permute-done | bytes 65568 | tf_op jit(solution)/shard_map/ppermute | solution.py:95
  30.0 0.0 collective-permute-done.16
  30.0 0.0 collective-permute-done.15
  30.0 0.1 collective-permute-start.21
  30.1 1.2 %collective-permute-done.21.mate_terms = f32[128,128]{1,0:T(8,128)S(1)} collective-permute-done((f32[128,128]{1,0:T(8,128)S(1)}, f32[128,128]{1,0:T(8,128)S(1)}, u32[]{:S(2)}, u32[]{:S(2)}) %collective-permute-start.21) | collective-permute-done | bytes 65568 | tf_op jit(solution)/shard_map/ppermute | solution.py:89
  31.3 0.7 %shard_map.92 = (f32[128,128]{1,0:T(8,128)}, f32[1,128]{1,0:T(1,128)}) custom-call(f32[128,128]{1,0:T(8,128)S(1)} %add_add_fusion.terms, f32[128,128]{1,0:T(8,128)S(1)} %collective-permute-done.21.mate_terms, f32[128,128]{1,0:T(8,128)S(1)} %get-tuple-element.59.base, f32[1,128]{1,0:T(1,128)S(1)} %get-tuple-element.60.gain, f32[1,128]{1,0:T(1,128)S(1)} %get-tuple-element.61.scale), custom_call_target="tpu_custom_call" | custom-call | flops 131072 | bytes 65536 | tf_op jit(solution)/shard_map/pallas_call | solution.py:52
  (15 shorter events, 0.1 us)
Async XLA Ops:
  2.1 1.4 %collective-permute-start = (f32[136,128]{1,0:T(8,128)S(1)}, f32[136,128]{1,0:T(8,128)S(1)}, u32[]{:S(2)}, u32[]{:S(2)}) collective-permute-start(f32[136,128]{1,0:T(8,128)S(1)} %get-tuple-element.34), channel_id=1, source_target_pairs={{0,1},{1,0},{2,3},{3,2},{4,5},{5,4},{6,7},{7,6},{8,9},{9,8},{10,11... | collective-permute-start | bytes 208904 | tf_op jit(solution)/shard_map/ppermute | solution.py:89
  2.6 5.7 %collective-permute-start.2 = (f32[8,128,128]{2,1,0:T(8,128)S(1)}, f32[8,128,128]{2,1,0:T(8,128)S(1)}, u32[]{:S(2)}, u32[]{:S(2)}) collective-permute-start(f32[8,128,128]{2,1,0:T(8,128)S(1)} %get-tuple-element.39.con), channel_id=1, source_target_pairs={{0,1},{1,0},{2,3},{3,2},{4,5},{5,4},{6,7},{7,6},{8,9},{9,8},{10,11... | collective-permute-start | bytes 1572872 | tf_op jit(solution)/shard_map/ppermute | solution.py:89
  2.7 5.6 %collective-permute-start.3 = (f32[1024,128]{1,0:T(8,128)S(1)}, f32[1024,128]{1,0:T(8,128)S(1)}, u32[]{:S(2)}, u32[]{:S(2)}) collective-permute-start(f32[1024,128]{1,0:T(8,128)S(1)} %get-tuple-element.40.x), channel_id=1, source_target_pairs={{0,1},{1,0},{2,3},{3,2},{4,5},{5,4},{6,7},{7,6},{8,9},{9,8},{10,11... | collective-permute-start | bytes 1572872 | tf_op jit(solution)/shard_map/ppermute | solution.py:89
  3.6 4.7 %collective-permute-start.1 = (f32[144,128]{1,0:T(8,128)S(1)}, f32[144,128]{1,0:T(8,128)S(1)}, u32[]{:S(2)}, u32[]{:S(2)}) collective-permute-start(f32[144,128]{1,0:T(8,128)S(1)} %pad_maximum_fusion), channel_id=1, source_target_pairs={{0,1},{1,2},{2,3},{3,0},{4,5},{5,6},{6,7},{7,4},{8,9},{9,10},{10,1... | collective-permute-start | bytes 221192 | tf_op jit(solution)/shard_map/ppermute | solution.py:95
  9.1 4.6 %collective-permute-start.7 = (f32[88,128]{1,0:T(8,128)S(1)}, f32[88,128]{1,0:T(8,128)S(1)}, u32[]{:S(2)}, u32[]{:S(2)}) collective-permute-start(f32[88,128]{1,0:T(8,128)S(1)} %get-tuple-element.41), channel_id=1, source_target_pairs={{0,21},{1,0},{2,23},{3,2},{4,17},{5,4},{6,19},{7,6},{8,29},{9,8},{... | collective-permute-start | bytes 135176 | tf_op jit(solution)/shard_map/ppermute | solution.py:95
  12.0 2.1 %collective-permute-start.6 = (f32[88,128]{1,0:T(8,128)S(1)}, f32[88,128]{1,0:T(8,128)S(1)}, u32[]{:S(2)}, u32[]{:S(2)}) collective-permute-start(f32[88,128]{1,0:T(8,128)S(1)} %get-tuple-element.41), channel_id=1, source_target_pairs={{0,17},{1,0},{2,19},{3,2},{4,21},{5,4},{6,23},{7,6},{8,25},{9,8},{... | collective-permute-start | bytes 135176 | tf_op jit(solution)/shard_map/ppermute | solution.py:95
  12.3 2.1 %collective-permute-start.5 = (f32[88,128]{1,0:T(8,128)S(1)}, f32[88,128]{1,0:T(8,128)S(1)}, u32[]{:S(2)}, u32[]{:S(2)}) collective-permute-start(f32[88,128]{1,0:T(8,128)S(1)} %get-tuple-element.41), channel_id=1, source_target_pairs={{0,5},{1,0},{2,7},{3,2},{4,1},{5,4},{6,3},{7,6},{8,13},{9,8},{10,1... | collective-permute-start | bytes 135176 | tf_op jit(solution)/shard_map/ppermute | solution.py:95
  12.6 1.7 %collective-permute-start.4 = (f32[88,128]{1,0:T(8,128)S(1)}, f32[88,128]{1,0:T(8,128)S(1)}, u32[]{:S(2)}, u32[]{:S(2)}) collective-permute-start(f32[88,128]{1,0:T(8,128)S(1)} %get-tuple-element.41), channel_id=1, source_target_pairs={{0,1},{1,0},{2,3},{3,2},{4,5},{5,4},{6,7},{7,6},{8,9},{9,8},{10,11... | collective-permute-start | bytes 135176 | tf_op jit(solution)/shard_map/ppermute | solution.py:89
  12.8 3.9 %collective-permute-start.10 = (f32[128,128]{1,0:T(8,128)S(1)}, f32[128,128]{1,0:T(8,128)S(1)}, u32[]{:S(2)}, u32[]{:S(2)}) collective-permute-start(f32[128,128]{1,0:T(8,128)S(1)} %get-tuple-element.43.moved), channel_id=1, source_target_pairs={{0,1},{1,0},{2,3},{3,2},{4,5},{5,4},{6,7},{7,6},{8,9},{9,8},{10,11... | collective-permute-start | bytes 196616 | tf_op jit(solution)/shard_map/ppermute | solution.py:89
  14.4 4.6 %collective-permute-start.9 = (f32[88,128]{1,0:T(8,128)S(1)}, f32[88,128]{1,0:T(8,128)S(1)}, u32[]{:S(2)}, u32[]{:S(2)}) collective-permute-start(f32[88,128]{1,0:T(8,128)S(1)} %add_add_fusion.1), channel_id=1, source_target_pairs={{0,1},{1,8},{2,3},{3,10},{4,5},{5,12},{6,7},{7,14},{8,9},{9,0},{10... | collective-permute-start | bytes 135176 | tf_op jit(solution)/shard_map/ppermute | solution.py:95
  16.0 2.9 %collective-permute-start.8 = (f32[88,128]{1,0:T(8,128)S(1)}, f32[88,128]{1,0:T(8,128)S(1)}, u32[]{:S(2)}, u32[]{:S(2)}) collective-permute-start(f32[88,128]{1,0:T(8,128)S(1)} %add_add_fusion.1), channel_id=1, source_target_pairs={{0,1},{1,0},{2,3},{3,2},{4,5},{5,4},{6,7},{7,6},{8,9},{9,8},{10,11... | collective-permute-start | bytes 135176 | tf_op jit(solution)/shard_map/ppermute | solution.py:89
  19.3 2.4 %collective-permute-start.14 = (f32[144,128]{1,0:T(8,128)S(1)}, f32[144,128]{1,0:T(8,128)S(1)}, u32[]{:S(2)}, u32[]{:S(2)}) collective-permute-start(f32[144,128]{1,0:T(8,128)S(1)} %get-tuple-element.44), channel_id=1, source_target_pairs={{0,7},{1,0},{2,5},{3,2},{4,3},{5,4},{6,1},{7,6},{8,15},{9,8},{10,1... | collective-permute-start | bytes 221192 | tf_op jit(solution)/shard_map/ppermute | solution.py:95
  19.7 2.7 %collective-permute-start.13 = (f32[144,128]{1,0:T(8,128)S(1)}, f32[144,128]{1,0:T(8,128)S(1)}, u32[]{:S(2)}, u32[]{:S(2)}) collective-permute-start(f32[144,128]{1,0:T(8,128)S(1)} %get-tuple-element.44), channel_id=1, source_target_pairs={{0,5},{1,0},{2,7},{3,2},{4,1},{5,4},{6,3},{7,6},{8,13},{9,8},{10,1... | collective-permute-start | bytes 221192 | tf_op jit(solution)/shard_map/ppermute | solution.py:95
  20.0 2.7 %collective-permute-start.12 = (f32[144,128]{1,0:T(8,128)S(1)}, f32[144,128]{1,0:T(8,128)S(1)}, u32[]{:S(2)}, u32[]{:S(2)}) collective-permute-start(f32[144,128]{1,0:T(8,128)S(1)} %get-tuple-element.44), channel_id=1, source_target_pairs={{0,3},{1,0},{2,1},{3,2},{4,7},{5,4},{6,5},{7,6},{8,11},{9,8},{10,9... | collective-permute-start | bytes 221192 | tf_op jit(solution)/shard_map/ppermute | solution.py:95
  20.7 2.0 %collective-permute-start.11 = (f32[144,128]{1,0:T(8,128)S(1)}, f32[144,128]{1,0:T(8,128)S(1)}, u32[]{:S(2)}, u32[]{:S(2)}) collective-permute-start(f32[144,128]{1,0:T(8,128)S(1)} %get-tuple-element.44), channel_id=1, source_target_pairs={{0,1},{1,0},{2,3},{3,2},{4,5},{5,4},{6,7},{7,6},{8,9},{9,8},{10,11... | collective-permute-start | bytes 221192 | tf_op jit(solution)/shard_map/ppermute | solution.py:89
  20.7 5.7 %collective-permute-start.20 = (f32[128,128]{1,0:T(8,128)S(1)}, f32[128,128]{1,0:T(8,128)S(1)}, u32[]{:S(2)}, u32[]{:S(2)}) collective-permute-start(f32[128,128]{1,0:T(8,128)S(1)} %get-tuple-element.47.gram), channel_id=1, source_target_pairs={{0,1},{1,0},{2,3},{3,2},{4,5},{5,4},{6,7},{7,6},{8,9},{9,8},{10,11... | collective-permute-start | bytes 196616 | tf_op jit(solution)/shard_map/ppermute | solution.py:89
  22.7 5.9 %collective-permute-start.18 = (f32[128,128]{1,0:T(8,128)S(1)}, f32[128,128]{1,0:T(8,128)S(1)}, u32[]{:S(2)}, u32[]{:S(2)}) collective-permute-start(f32[128,128]{1,0:T(8,128)S(1)} %get-tuple-element.45), channel_id=1, source_target_pairs={{0,1},{1,24},{2,3},{3,26},{4,5},{5,28},{6,7},{7,30},{8,9},{9,16},{... | collective-permute-start | bytes 196616 | tf_op jit(solution)/shard_map/ppermute | solution.py:95
  24.1 5.9 %collective-permute-start.17 = (f32[128,128]{1,0:T(8,128)S(1)}, f32[128,128]{1,0:T(8,128)S(1)}, u32[]{:S(2)}, u32[]{:S(2)}) collective-permute-start(f32[128,128]{1,0:T(8,128)S(1)} %get-tuple-element.45), channel_id=1, source_target_pairs={{0,1},{1,16},{2,3},{3,18},{4,5},{5,20},{6,7},{7,22},{8,9},{9,24},{... | collective-permute-start | bytes 196616 | tf_op jit(solution)/shard_map/ppermute | solution.py:95
  25.3 4.7 %collective-permute-start.16 = (f32[128,128]{1,0:T(8,128)S(1)}, f32[128,128]{1,0:T(8,128)S(1)}, u32[]{:S(2)}, u32[]{:S(2)}) collective-permute-start(f32[128,128]{1,0:T(8,128)S(1)} %get-tuple-element.45), channel_id=1, source_target_pairs={{0,1},{1,8},{2,3},{3,10},{4,5},{5,12},{6,7},{7,14},{8,9},{9,0},{10... | collective-permute-start | bytes 196616 | tf_op jit(solution)/shard_map/ppermute | solution.py:95
  26.4 3.6 %collective-permute-start.15 = (f32[128,128]{1,0:T(8,128)S(1)}, f32[128,128]{1,0:T(8,128)S(1)}, u32[]{:S(2)}, u32[]{:S(2)}) collective-permute-start(f32[128,128]{1,0:T(8,128)S(1)} %get-tuple-element.45), channel_id=1, source_target_pairs={{0,1},{1,0},{2,3},{3,2},{4,5},{5,4},{6,7},{7,6},{8,9},{9,8},{10,11... | collective-permute-start | bytes 196616 | tf_op jit(solution)/shard_map/ppermute | solution.py:89
  26.4 1.3 %collective-permute-start.19 = (f32[32,128]{1,0:T(8,128)S(1)}, f32[32,128]{1,0:T(8,128)S(1)}, u32[]{:S(2)}, u32[]{:S(2)}) collective-permute-start(f32[32,128]{1,0:T(8,128)S(1)} %get-tuple-element.46.rows), channel_id=1, source_target_pairs={{0,1},{1,0},{2,3},{3,2},{4,5},{5,4},{6,7},{7,6},{8,9},{9,8},{10,11... | collective-permute-start | bytes 49160 | tf_op jit(solution)/shard_map/ppermute | solution.py:89
  30.0 1.3 %collective-permute-start.21 = (f32[128,128]{1,0:T(8,128)S(1)}, f32[128,128]{1,0:T(8,128)S(1)}, u32[]{:S(2)}, u32[]{:S(2)}) collective-permute-start(f32[128,128]{1,0:T(8,128)S(1)} %add_add_fusion.terms), channel_id=1, source_target_pairs={{0,1},{1,0},{2,3},{3,2},{4,5},{5,4},{6,7},{7,6},{8,9},{9,8},{10,11... | collective-permute-start | bytes 196616 | tf_op jit(solution)/shard_map/ppermute | solution.py:89

commit v16 on v15

--- a/solution.py
+++ b/solution.py
@@ -43,6 +43,13 @@
     rows = lax.broadcasted_iota(jnp.int32, gram.shape, 0)
     columns = lax.broadcasted_iota(jnp.int32, gram.shape, 1)
     return jnp.sum(jnp.where(rows == columns, gram, 0.0), axis=0, keepdims=True)
+
+
+def only_on(core, kernel):
+    def run(*refs):
+        pl.when(smp_index() & 1 == core)(lambda: kernel(*refs))
+
+    return run
 
 
 def call(kernel, outs, operands, flops, scratch=(), in_hbm=0):
@@ -152,37 +159,35 @@
     chips, chip_rows = smp_count // 2, 2 * smp_rows
     chip_bits = bits_of(smp_count)[1:]
     vox_bits = [bit * smp_count for bit in bits_of(vox_count)]
-    chunks = 1
-    chunk_vox = vox_rows // chunks
-    chunk_rows = chunk_vox * smp_rows
+    pieces = 4 if flat_rows % 32 == 0 else 1
+    piece_rows = flat_rows // pieces
 
     def open_kernel(x_hbm, c_hbm, b_hbm, a_hbm, w_hbm, x, c, a, w, out, con, sems):
         copies = [pltpu.make_async_copy(c_hbm, c, sems.at[0])]
         copies += [pltpu.make_async_copy(b_hbm, out.at[pl.ds(vox_rows, smp_rows), :], sems.at[1])]
-        for n in range(chunks):
-            part = pl.ds(n * chunk_rows, chunk_rows)
-            copies.append(pltpu.make_async_copy(x_hbm.at[part, :], x.at[part, :], sems.at[2 + n]))
-        copies.append(pltpu.make_async_copy(a_hbm, a, sems.at[2 + chunks]))
-        copies.append(pltpu.make_async_copy(w_hbm, w, sems.at[3 + chunks]))
+        for n in range(pieces):
+            piece = pl.ds(n * piece_rows, piece_rows)
+            copies.append(pltpu.make_async_copy(x_hbm.at[piece, :], x.at[piece, :], sems.at[2 + n]))
+        copies.append(pltpu.make_async_copy(a_hbm, a, sems.at[2 + pieces]))
+        copies.append(pltpu.make_async_copy(w_hbm, w, sems.at[3 + pieces]))
         for copy in copies:
             copy.start()
         copies[0].wait()
         copies[1].wait()
         factor = both(c[...])
         b = out[pl.ds(vox_rows, smp_rows), :]
-        for n in range(chunks):
+        for n in range(pieces):
             copies[2 + n].wait()
-            rows = pl.ds(n * chunk_vox, chunk_vox)
-            blocks = [x[pl.ds(n * chunk_rows + j, chunk_vox, stride=smp_rows), :] for j in range(smp_rows)]
-            blocks = jnp.concatenate([halves(block, 1) for block in blocks], axis=0)
-            made = fold(jnp.dot(blocks, factor, preferred_element_type=F32)).reshape(smp_rows, chunk_vox, rank)
-            con[:, rows, :] = made
-            total = made[0] * b[:1, :]
-            for j in range(1, smp_rows):
-                total = total + made[j] * b[j : j + 1, :]
-            out[rows, :] = total
-        copies[2 + chunks].wait()
-        copies[3 + chunks].wait()
+        blocks = [x[pl.ds(j, vox_rows, stride=smp_rows), :] for j in range(smp_rows)]
+        blocks = jnp.concatenate([halves(block, 1) for block in blocks], axis=0)
+        made = fold(jnp.dot(blocks, factor, preferred_element_type=F32)).reshape(smp_rows, vox_rows, rank)
+        con[...] = made
+        total = made[0] * b[:1, :]
+        for j in range(1, smp_rows):
+            total = total + made[j] * b[j : j + 1, :]
+        out[:vox_rows, :] = total
+        copies[2 + pieces].wait()
+        copies[3 + pieces].wait()
 
     x, c_near, a_near, w_row, opened, con = call(
         open_kernel,
@@ -196,7 +201,7 @@
         ),
         (ensemble.reshape(flat_rows, times), time_factor, sample_factor, voxel_factor, weights.reshape(1, rank)),
         2 * flat_rows * times * rank * 6,
-        scratch=(pltpu.SemaphoreType.DMA((4 + chunks,)),),
+        scratch=(pltpu.SemaphoreType.DMA((4 + pieces,)),),
         in_hbm=5,
     )
 
@@ -242,7 +247,7 @@
         out[sums_rows:, :] = jnp.broadcast_to(diagonal, (8, rank))
 
     moved_a, chip_b, sums = call(
-        voxel_kernel,
+        only_on(voxel_core, voxel_kernel),
         (near(vox_rows, rank), near(chip_rows, rank), near(sums_rows + 8, rank)),
         (terms, rows_b, a_near, w_row, outer_c, con, mate_con, mate_x),
         2 * rank * rank * vox_rows * 12,
@@ -266,7 +271,7 @@
                 each[core * smp_rows + j] = dot_rows(block, moved)
 
     (each,) = call(
-        time_kernel,
+        only_on(sample_core, time_kernel),
         (near(chip_rows, times, rank),),
         (x, mate_x, moved_a, mate_moved_a),
         4 * flat_rows * times * rank * 6,
@@ -285,7 +290,7 @@
         out[:times, :] = total
 
     gram_a, payload = call(
-        sample_kernel,
+        only_on(sample_core, sample_kernel),
         (near(rank, rank), near(times + chip_rows, rank)),
         (sums, chip_b, w_row, outer_c, each),
         2 * rank * rank * chip_rows * 6,

time: 32.1 us -> 32.2 us (level)
  transfers between devices with their start and end apart: 22 -> 22, of which waited for: 12 -> 11; matrix products, arithmetic and copies ran while one was open for 0% -> 0% of each run, Pallas kernels for 7% -> 7%
where the time goes in v16:
time: 32.2 us; the launch traced here: 32.1 us
  starting transfers between devices  13.7 us (43%)
  waiting for transfers between devices  12 us (37%)
  Pallas kernels  5.6 us (17%)
  between operations  0.74 us (2%)
    ppermute x11, starting transfers between devices, send(): return lax.ppermute(values, ALL, pairs)  10.7 us
    ppermute x11, waiting for transfers between devices, send(): return lax.ppermute(values, ALL, pairs)  10.2 us
    pallas_call x9, Pallas kernels, call(): pl.pallas_call(kernel, out_shape=outs, in_specs=specs, out_specs=[pl.Bloc...  5.6 us
    ppermute x11, starting transfers between devices, swap(): lax.ppermute(values, ALL, [(i, i ^ 1) for i in range(lax.axis_size(ALL))])  2.95 us
    ppermute x11, waiting for transfers between devices, swap(): lax.ppermute(values, ALL, [(i, i ^ 1) for i in range(lax.axis_size(ALL))])  1.81 us
  transfers between devices with their start and end apart: 22, of which 11 were waited for; matrix products, arithmetic and copies ran while one was open for 0% of the time, Pallas kernels for 7%

profile of v16, /device:TPU:0, one launch (start us, length us, event | category | flops | bytes accessed | tf_op | source)
XLA Modules:
  0.0 32.1 jit_solution(18079063937403909070)
XLA Ops:
  0.6 1.6 %shard_map.84 = (f32[1024,128]{1,0:T(8,128)S(1)}, f32[128,128]{1,0:T(8,128)S(1)}, f32[128,128]{1,0:T(8,128)S(1)}, f32[1,128]{1,0:T(1,128)S(1)}, f32[136,128]{1,0:T(8,128)S(1)}, /*index=5*/f32[8,128,128]{2,1,0:T(8,128)S(1)}) custom-call(f32[1024,128]{1,0:T(8,128)} %bitcast.3, f32[128,128]{1,0:T(8,128)} %c_hbm.1, f32[8,128]{1,0:T(8,128)} %b_hbm.1, ...), custom_call_target="tpu_custom_call" | custom-call | flops 201326592 | bytes 65536 | tf_op jit(solution)/shard_map/pallas_call | solution.py:59
  2.2 0.5 %collective-permute-start = (f32[136,128]{1,0:T(8,128)S(1)}, f32[136,128]{1,0:T(8,128)S(1)}, u32[]{:S(2)}, u32[]{:S(2)}) collective-permute-start(f32[136,128]{1,0:T(8,128)S(1)} %get-tuple-element.34), channel_id=1, source_target_pairs={{0,1},{1,0},{2,3},{3,2},{4,5},{5,4},{6,7},{7,6},{8,9},{9,8},{10,11... | collective-permute-start | bytes 208904 | tf_op jit(solution)/shard_map/ppermute | solution.py:96
  2.7 0.1 collective-permute-start.2
  2.8 0.4 %collective-permute-start.3 = (f32[1024,128]{1,0:T(8,128)S(1)}, f32[1024,128]{1,0:T(8,128)S(1)}, u32[]{:S(2)}, u32[]{:S(2)}) collective-permute-start(f32[1024,128]{1,0:T(8,128)S(1)} %get-tuple-element.40.refs_0_), channel_id=1, source_target_pairs={{0,1},{1,0},{2,3},{3,2},{4,5},{5,4},{6,7},{7,6},{8,9},{9,8},{10,11... | collective-permute-start | bytes 1572872 | tf_op jit(solution)/shard_map/ppermute | solution.py:96
  3.2 0.4 %collective-permute-done = f32[136,128]{1,0:T(8,128)S(1)} collective-permute-done((f32[136,128]{1,0:T(8,128)S(1)}, f32[136,128]{1,0:T(8,128)S(1)}, u32[]{:S(2)}, u32[]{:S(2)}) %collective-permute-start) | collective-permute-done | bytes 69664 | tf_op jit(solution)/shard_map/ppermute | solution.py:96
  3.7 0.4 %collective-permute-start.1 = (f32[144,128]{1,0:T(8,128)S(1)}, f32[144,128]{1,0:T(8,128)S(1)}, u32[]{:S(2)}, u32[]{:S(2)}) collective-permute-start(f32[144,128]{1,0:T(8,128)S(1)} %pad_maximum_fusion), channel_id=1, source_target_pairs={{0,1},{1,2},{2,3},{3,0},{4,5},{5,6},{6,7},{7,4},{8,9},{9,10},{10,1... | collective-permute-start | bytes 221192 | tf_op jit(solution)/shard_map/ppermute | solution.py:102
  4.1 0.2 shard_map.85
  4.3 4.1 %collective-permute-done.1 = f32[144,128]{1,0:T(8,128)S(1)} collective-permute-done((f32[144,128]{1,0:T(8,128)S(1)}, f32[144,128]{1,0:T(8,128)S(1)}, u32[]{:S(2)}, u32[]{:S(2)}) %collective-permute-start.1) | collective-permute-done | bytes 73760 | tf_op jit(solution)/shard_map/ppermute | solution.py:102
  8.4 0.0 collective-permute-done.2.refs_6_
  8.4 0.0 collective-permute-done.3.refs_7_.refs_1_
  8.4 0.7 %shard_map.86 = (f32[128,128]{1,0:T(8,128)S(1)}, f32[16,128]{1,0:T(8,128)S(1)}, f32[88,128]{1,0:T(8,128)S(1)}) custom-call(f32[128,128]{1,0:T(8,128)S(1)} %slice_add_fusion.refs_0_, f32[32,128]{1,0:T(8,128)S(1)} %pad_maximum_fusion.1.refs_1_, f32[128,128]{1,0:T(8,128)S(1)} %get-tuple-element.35.refs_2_, f32[1,128]{1,0:T(1,128)S(1)} %get-tuple-element.36.w.refs_3_.refs_2_, ...), custom_call_target="tpu_custom_call" | custom-call | flops 50331648 | bytes 65536 | tf_op jit(solution)/shard_map/pallas_call | solution.py:59
  9.2 2.2 %collective-permute-start.7 = (f32[88,128]{1,0:T(8,128)S(1)}, f32[88,128]{1,0:T(8,128)S(1)}, u32[]{:S(2)}, u32[]{:S(2)}) collective-permute-start(f32[88,128]{1,0:T(8,128)S(1)} %get-tuple-element.41), channel_id=1, source_target_pairs={{0,21},{1,0},{2,23},{3,2},{4,17},{5,4},{6,19},{7,6},{8,29},{9,8},{... | collective-permute-start | bytes 135176 | tf_op jit(solution)/shard_map/ppermute | solution.py:102
  11.3 1.0 %collective-permute-start.6 = (f32[88,128]{1,0:T(8,128)S(1)}, f32[88,128]{1,0:T(8,128)S(1)}, u32[]{:S(2)}, u32[]{:S(2)}) collective-permute-start(f32[88,128]{1,0:T(8,128)S(1)} %get-tuple-element.41), channel_id=1, source_target_pairs={{0,17},{1,0},{2,19},{3,2},{4,21},{5,4},{6,23},{7,6},{8,25},{9,8},{... | collective-permute-start | bytes 135176 | tf_op jit(solution)/shard_map/ppermute | solution.py:102
  12.4 0.0 collective-permute-start.5
  12.4 0.5 %collective-permute-start.4 = (f32[88,128]{1,0:T(8,128)S(1)}, f32[88,128]{1,0:T(8,128)S(1)}, u32[]{:S(2)}, u32[]{:S(2)}) collective-permute-start(f32[88,128]{1,0:T(8,128)S(1)} %get-tuple-element.41), channel_id=1, source_target_pairs={{0,1},{1,0},{2,3},{3,2},{4,5},{5,4},{6,7},{7,6},{8,9},{9,8},{10,11... | collective-permute-start | bytes 135176 | tf_op jit(solution)/shard_map/ppermute | solution.py:96
  12.9 0.0 collective-permute-start.10
  12.9 0.2 collective-permute-done.7
  13.1 1.0 %collective-permute-done.6 = f32[88,128]{1,0:T(8,128)S(1)} collective-permute-done((f32[88,128]{1,0:T(8,128)S(1)}, f32[88,128]{1,0:T(8,128)S(1)}, u32[]{:S(2)}, u32[]{:S(2)}) %collective-permute-start.6) | collective-permute-done | bytes 45088 | tf_op jit(solution)/shard_map/ppermute | solution.py:102
  14.1 0.0 collective-permute-done.5
  14.1 0.0 collective-permute-done.4
  14.1 1.7 %collective-permute-start.9 = (f32[88,128]{1,0:T(8,128)S(1)}, f32[88,128]{1,0:T(8,128)S(1)}, u32[]{:S(2)}, u32[]{:S(2)}) collective-permute-start(f32[88,128]{1,0:T(8,128)S(1)} %add_add_fusion.1), channel_id=1, source_target_pairs={{0,1},{1,8},{2,3},{3,10},{4,5},{5,12},{6,7},{7,14},{8,9},{9,0},{10... | collective-permute-start | bytes 135176 | tf_op jit(solution)/shard_map/ppermute | solution.py:102
  15.8 0.3 %collective-permute-start.8 = (f32[88,128]{1,0:T(8,128)S(1)}, f32[88,128]{1,0:T(8,128)S(1)}, u32[]{:S(2)}, u32[]{:S(2)}) collective-permute-start(f32[88,128]{1,0:T(8,128)S(1)} %add_add_fusion.1), channel_id=1, source_target_pairs={{0,1},{1,0},{2,3},{3,2},{4,5},{5,4},{6,7},{7,6},{8,9},{9,8},{10,11... | collective-permute-start | bytes 135176 | tf_op jit(solution)/shard_map/ppermute | solution.py:96
  16.1 0.0 collective-permute-done.10.refs_3_.mate_moved
  16.1 0.5 %shard_map.87.refs_4_ = f32[16,128,128]{2,1,0:T(8,128)S(1)} custom-call(f32[1024,128]{1,0:T(8,128)S(1)} %get-tuple-element.40.refs_0_, f32[1024,128]{1,0:T(8,128)S(1)} %collective-permute-done.3.refs_7_.refs_1_, f32[128,128]{1,0:T(8,128)S(1)} %get-tuple-element.43.refs_2_.moved, f32[128,128]{1,0:T(8,128)S(1)} %collective-permute-done.10.refs_3_.mate_moved), custom_call_target="tpu_custom_call" | custom-call | flops 402653184 | bytes 65536 | tf_op jit(solution)/shard_map/pallas_call | solution.py:59
  16.6 2.1 %collective-permute-done.9 = f32[88,128]{1,0:T(8,128)S(1)} collective-permute-done((f32[88,128]{1,0:T(8,128)S(1)}, f32[88,128]{1,0:T(8,128)S(1)}, u32[]{:S(2)}, u32[]{:S(2)}) %collective-permute-start.9) | collective-permute-done | bytes 45088 | tf_op jit(solution)/shard_map/ppermute | solution.py:102
  18.7 0.0 collective-permute-done.8
  18.7 0.3 %shard_map.88 = (f32[128,128]{1,0:T(8,128)S(1)}, f32[144,128]{1,0:T(8,128)S(1)}) custom-call(f32[88,128]{1,0:T(8,128)S(1)} %add.32.refs_0_, f32[16,128]{1,0:T(8,128)S(1)} %get-tuple-element.42.refs_1_, f32[1,128]{1,0:T(1,128)S(1)} %get-tuple-element.36.w.refs_3_.refs_2_, f32[128,128]{1,0:T(8,128)S(1)} %get-tuple-element.38.refs_4_.refs_3_, ...), custom_call_target="tpu_custom_call" | custom-call | flops 3145728 | bytes 65536 | tf_op jit(solution)/shard_map/pallas_call | solution.py:59
  19.1 0.4 %collective-permute-start.14 = (f32[144,128]{1,0:T(8,128)S(1)}, f32[144,128]{1,0:T(8,128)S(1)}, u32[]{:S(2)}, u32[]{:S(2)}) collective-permute-start(f32[144,128]{1,0:T(8,128)S(1)} %get-tuple-element.44), channel_id=1, source_target_pairs={{0,7},{1,0},{2,5},{3,2},{4,3},{5,4},{6,1},{7,6},{8,15},{9,8},{10,1... | collective-permute-start | bytes 221192 | tf_op jit(solution)/shard_map/ppermute | solution.py:102
  19.5 0.3 collective-permute-start.13
  19.7 1.0 %collective-permute-start.12 = (f32[144,128]{1,0:T(8,128)S(1)}, f32[144,128]{1,0:T(8,128)S(1)}, u32[]{:S(2)}, u32[]{:S(2)}) collective-permute-start(f32[144,128]{1,0:T(8,128)S(1)} %get-tuple-element.44), channel_id=1, source_target_pairs={{0,3},{1,0},{2,1},{3,2},{4,7},{5,4},{6,5},{7,6},{8,11},{9,8},{10,9... | collective-permute-start | bytes 221192 | tf_op jit(solution)/shard_map/ppermute | solution.py:102
  20.8 0.0 collective-permute-start.11
  20.8 0.5 %collective-permute-start.20 = (f32[128,128]{1,0:T(8,128)S(1)}, f32[128,128]{1,0:T(8,128)S(1)}, u32[]{:S(2)}, u32[]{:S(2)}) collective-permute-start(f32[128,128]{1,0:T(8,128)S(1)} %get-tuple-element.47.gram), channel_id=1, source_target_pairs={{0,1},{1,0},{2,3},{3,2},{4,5},{5,4},{6,7},{7,6},{8,9},{9,8},{10,11... | collective-permute-start | bytes 196616 | tf_op jit(solution)/shard_map/ppermute | solution.py:96
  21.3 0.1 collective-permute-done.14.refs_3_
  21.4 0.7 %collective-permute-done.13.refs_2_ = f32[144,128]{1,0:T(8,128)S(1)} collective-permute-done((f32[144,128]{1,0:T(8,128)S(1)}, f32[144,128]{1,0:T(8,128)S(1)}, u32[]{:S(2)}, u32[]{:S(2)}) %collective-permute-start.13) | collective-permute-done | bytes 73760 | tf_op jit(solution)/shard_map/ppermute | solution.py:102
  22.1 0.6 %collective-permute-done.12.refs_1_ = f32[144,128]{1,0:T(8,128)S(1)} collective-permute-done((f32[144,128]{1,0:T(8,128)S(1)}, f32[144,128]{1,0:T(8,128)S(1)}, u32[]{:S(2)}, u32[]{:S(2)}) %collective-permute-start.12) | collective-permute-done | bytes 73760 | tf_op jit(solution)/shard_map/ppermute | solution.py:102
  22.8 1.0 %collective-permute-start.18 = (f32[128,128]{1,0:T(8,128)S(1)}, f32[128,128]{1,0:T(8,128)S(1)}, u32[]{:S(2)}, u32[]{:S(2)}) collective-permute-start(f32[128,128]{1,0:T(8,128)S(1)} %get-tuple-element.45), channel_id=1, source_target_pairs={{0,1},{1,24},{2,3},{3,26},{4,5},{5,28},{6,7},{7,30},{8,9},{9,16},{... | collective-permute-start | bytes 196616 | tf_op jit(solution)/shard_map/ppermute | solution.py:102
  23.8 1.1 %collective-permute-start.17 = (f32[128,128]{1,0:T(8,128)S(1)}, f32[128,128]{1,0:T(8,128)S(1)}, u32[]{:S(2)}, u32[]{:S(2)}) collective-permute-start(f32[128,128]{1,0:T(8,128)S(1)} %get-tuple-element.45), channel_id=1, source_target_pairs={{0,1},{1,16},{2,3},{3,18},{4,5},{5,20},{6,7},{7,22},{8,9},{9,24},{... | collective-permute-start | bytes 196616 | tf_op jit(solution)/shard_map/ppermute | solution.py:102
  25.0 1.5 %collective-permute-start.16 = (f32[128,128]{1,0:T(8,128)S(1)}, f32[128,128]{1,0:T(8,128)S(1)}, u32[]{:S(2)}, u32[]{:S(2)}) collective-permute-start(f32[128,128]{1,0:T(8,128)S(1)} %get-tuple-element.45), channel_id=1, source_target_pairs={{0,1},{1,8},{2,3},{3,10},{4,5},{5,12},{6,7},{7,14},{8,9},{9,0},{10... | collective-permute-start | bytes 196616 | tf_op jit(solution)/shard_map/ppermute | solution.py:102
  26.5 0.5 %collective-permute-start.19 = (f32[32,128]{1,0:T(8,128)S(1)}, f32[32,128]{1,0:T(8,128)S(1)}, u32[]{:S(2)}, u32[]{:S(2)}) collective-permute-start(f32[32,128]{1,0:T(8,128)S(1)} %get-tuple-element.46.rows), channel_id=1, source_target_pairs={{0,1},{1,0},{2,3},{3,2},{4,5},{5,4},{6,7},{7,6},{8,9},{9,8},{10,11... | collective-permute-start | bytes 49160 | tf_op jit(solution)/shard_map/ppermute | solution.py:96
  27.0 0.7 %shard_map.90 = (f32[128,128]{1,0:T(8,128)}, f32[1,128]{1,0:T(1,128)S(1)}, f32[128,128]{1,0:T(8,128)S(1)}) custom-call(f32[128,128]{1,0:T(8,128)S(1)} %get-tuple-element.47.gram, f32[128,128]{1,0:T(8,128)S(1)} %collective-permute-done.20.mate_gram, f32[128,128]{1,0:T(8,128)S(1)} %get-tuple-element.43.refs_2_.moved, ...), custom_call_target="tpu_custom_call" | custom-call | flops 131072 | bytes 65536 | tf_op jit(solution)/shard_map/pallas_call | solution.py:59
  27.7 0.2 collective-permute-done.19.mate_rows
  27.9 0.9 %shard_map.91 = (f32[8,128]{1,0:T(8,128)}, f32[128,128]{1,0:T(8,128)S(1)}, f32[1,128]{1,0:T(1,128)S(1)}, f32[1,128]{1,0:T(1,128)S(1)}) custom-call(f32[32,128]{1,0:T(8,128)S(1)} %get-tuple-element.46.rows, f32[32,128]{1,0:T(8,128)S(1)} %collective-permute-done.19.mate_rows, f32[128,128]{1,0:T(8,128)S(1)} %get-tuple-element.37.c, ...), custom_call_target="tpu_custom_call" | custom-call | flops 16777216 | bytes 65536 | tf_op jit(solution)/shard_map/pallas_call | solution.py:59
  28.7 1.3 %collective-permute-done.17 = f32[128,128]{1,0:T(8,128)S(1)} collective-permute-done((f32[128,128]{1,0:T(8,128)S(1)}, f32[128,128]{1,0:T(8,128)S(1)}, u32[]{:S(2)}, u32[]{:S(2)}) %collective-permute-start.17) | collective-permute-done | bytes 65568 | tf_op jit(solution)/shard_map/ppermute | solution.py:102
  30.0 0.0 collective-permute-done.16
  30.0 0.0 collective-permute-done.15
  30.1 0.1 collective-permute-start.21
  30.1 1.2 %collective-permute-done.21.mate_terms = f32[128,128]{1,0:T(8,128)S(1)} collective-permute-done((f32[128,128]{1,0:T(8,128)S(1)}, f32[128,128]{1,0:T(8,128)S(1)}, u32[]{:S(2)}, u32[]{:S(2)}) %collective-permute-start.21) | collective-permute-done | bytes 65568 | tf_op jit(solution)/shard_map/ppermute | solution.py:96
  31.4 0.7 %shard_map.92 = (f32[128,128]{1,0:T(8,128)}, f32[1,128]{1,0:T(1,128)}) custom-call(f32[128,128]{1,0:T(8,128)S(1)} %add_add_fusion.terms, f32[128,128]{1,0:T(8,128)S(1)} %collective-permute-done.21.mate_terms, f32[128,128]{1,0:T(8,128)S(1)} %get-tuple-element.59.base, f32[1,128]{1,0:T(1,128)S(1)} %get-tuple-element.60.gain, f32[1,128]{1,0:T(1,128)S(1)} %get-tuple-element.61.scale), custom_call_target="tpu_custom_call" | custom-call | flops 131072 | bytes 65536 | tf_op jit(solution)/shard_map/pallas_call | solution.py:59
  (15 shorter events, 0.1 us)
Async XLA Ops:
  2.2 1.4 %collective-permute-start = (f32[136,128]{1,0:T(8,128)S(1)}, f32[136,128]{1,0:T(8,128)S(1)}, u32[]{:S(2)}, u32[]{:S(2)}) collective-permute-start(f32[136,128]{1,0:T(8,128)S(1)} %get-tuple-element.34), channel_id=1, source_target_pairs={{0,1},{1,0},{2,3},{3,2},{4,5},{5,4},{6,7},{7,6},{8,9},{9,8},{10,11... | collective-permute-start | bytes 208904 | tf_op jit(solution)/shard_map/ppermute | solution.py:96
  2.7 5.7 %collective-permute-start.2 = (f32[8,128,128]{2,1,0:T(8,128)S(1)}, f32[8,128,128]{2,1,0:T(8,128)S(1)}, u32[]{:S(2)}, u32[]{:S(2)}) collective-permute-start(f32[8,128,128]{2,1,0:T(8,128)S(1)} %get-tuple-element.39.refs_5_), channel_id=1, source_target_pairs={{0,1},{1,0},{2,3},{3,2},{4,5},{5,4},{6,7},{7,6},{8,9},{9,8},{10,11... | collective-permute-start | bytes 1572872 | tf_op jit(solution)/shard_map/ppermute | solution.py:96
  2.8 5.6 %collective-permute-start.3 = (f32[1024,128]{1,0:T(8,128)S(1)}, f32[1024,128]{1,0:T(8,128)S(1)}, u32[]{:S(2)}, u32[]{:S(2)}) collective-permute-start(f32[1024,128]{1,0:T(8,128)S(1)} %get-tuple-element.40.refs_0_), channel_id=1, source_target_pairs={{0,1},{1,0},{2,3},{3,2},{4,5},{5,4},{6,7},{7,6},{8,9},{9,8},{10,11... | collective-permute-start | bytes 1572872 | tf_op jit(solution)/shard_map/ppermute | solution.py:96
  3.7 4.7 %collective-permute-start.1 = (f32[144,128]{1,0:T(8,128)S(1)}, f32[144,128]{1,0:T(8,128)S(1)}, u32[]{:S(2)}, u32[]{:S(2)}) collective-permute-start(f32[144,128]{1,0:T(8,128)S(1)} %pad_maximum_fusion), channel_id=1, source_target_pairs={{0,1},{1,2},{2,3},{3,0},{4,5},{5,6},{6,7},{7,4},{8,9},{9,10},{10,1... | collective-permute-start | bytes 221192 | tf_op jit(solution)/shard_map/ppermute | solution.py:102
  9.2 3.9 %collective-permute-start.7 = (f32[88,128]{1,0:T(8,128)S(1)}, f32[88,128]{1,0:T(8,128)S(1)}, u32[]{:S(2)}, u32[]{:S(2)}) collective-permute-start(f32[88,128]{1,0:T(8,128)S(1)} %get-tuple-element.41), channel_id=1, source_target_pairs={{0,21},{1,0},{2,23},{3,2},{4,17},{5,4},{6,19},{7,6},{8,29},{9,8},{... | collective-permute-start | bytes 135176 | tf_op jit(solution)/shard_map/ppermute | solution.py:102
  11.3 2.7 %collective-permute-start.6 = (f32[88,128]{1,0:T(8,128)S(1)}, f32[88,128]{1,0:T(8,128)S(1)}, u32[]{:S(2)}, u32[]{:S(2)}) collective-permute-start(f32[88,128]{1,0:T(8,128)S(1)} %get-tuple-element.41), channel_id=1, source_target_pairs={{0,17},{1,0},{2,19},{3,2},{4,21},{5,4},{6,23},{7,6},{8,25},{9,8},{... | collective-permute-start | bytes 135176 | tf_op jit(solution)/shard_map/ppermute | solution.py:102
  12.4 1.7 %collective-permute-start.5 = (f32[88,128]{1,0:T(8,128)S(1)}, f32[88,128]{1,0:T(8,128)S(1)}, u32[]{:S(2)}, u32[]{:S(2)}) collective-permute-start(f32[88,128]{1,0:T(8,128)S(1)} %get-tuple-element.41), channel_id=1, source_target_pairs={{0,5},{1,0},{2,7},{3,2},{4,1},{5,4},{6,3},{7,6},{8,13},{9,8},{10,1... | collective-permute-start | bytes 135176 | tf_op jit(solution)/shard_map/ppermute | solution.py:102
  12.4 1.7 %collective-permute-start.4 = (f32[88,128]{1,0:T(8,128)S(1)}, f32[88,128]{1,0:T(8,128)S(1)}, u32[]{:S(2)}, u32[]{:S(2)}) collective-permute-start(f32[88,128]{1,0:T(8,128)S(1)} %get-tuple-element.41), channel_id=1, source_target_pairs={{0,1},{1,0},{2,3},{3,2},{4,5},{5,4},{6,7},{7,6},{8,9},{9,8},{10,11... | collective-permute-start | bytes 135176 | tf_op jit(solution)/shard_map/ppermute | solution.py:96
  12.9 3.2 %collective-permute-start.10 = (f32[128,128]{1,0:T(8,128)S(1)}, f32[128,128]{1,0:T(8,128)S(1)}, u32[]{:S(2)}, u32[]{:S(2)}) collective-permute-start(f32[128,128]{1,0:T(8,128)S(1)} %get-tuple-element.43.refs_2_.moved), channel_id=1, source_target_pairs={{0,1},{1,0},{2,3},{3,2},{4,5},{5,4},{6,7},{7,6},{8,9},{9,8},{10,11... | collective-permute-start | bytes 196616 | tf_op jit(solution)/shard_map/ppermute | solution.py:96
  14.1 4.6 %collective-permute-start.9 = (f32[88,128]{1,0:T(8,128)S(1)}, f32[88,128]{1,0:T(8,128)S(1)}, u32[]{:S(2)}, u32[]{:S(2)}) collective-permute-start(f32[88,128]{1,0:T(8,128)S(1)} %add_add_fusion.1), channel_id=1, source_target_pairs={{0,1},{1,8},{2,3},{3,10},{4,5},{5,12},{6,7},{7,14},{8,9},{9,0},{10... | collective-permute-start | bytes 135176 | tf_op jit(solution)/shard_map/ppermute | solution.py:102
  15.8 2.9 %collective-permute-start.8 = (f32[88,128]{1,0:T(8,128)S(1)}, f32[88,128]{1,0:T(8,128)S(1)}, u32[]{:S(2)}, u32[]{:S(2)}) collective-permute-start(f32[88,128]{1,0:T(8,128)S(1)} %add_add_fusion.1), channel_id=1, source_target_pairs={{0,1},{1,0},{2,3},{3,2},{4,5},{5,4},{6,7},{7,6},{8,9},{9,8},{10,11... | collective-permute-start | bytes 135176 | tf_op jit(solution)/shard_map/ppermute | solution.py:96
  19.1 2.4 %collective-permute-start.14 = (f32[144,128]{1,0:T(8,128)S(1)}, f32[144,128]{1,0:T(8,128)S(1)}, u32[]{:S(2)}, u32[]{:S(2)}) collective-permute-start(f32[144,128]{1,0:T(8,128)S(1)} %get-tuple-element.44), channel_id=1, source_target_pairs={{0,7},{1,0},{2,5},{3,2},{4,3},{5,4},{6,1},{7,6},{8,15},{9,8},{10,1... | collective-permute-start | bytes 221192 | tf_op jit(solution)/shard_map/ppermute | solution.py:102
  19.5 2.7 %collective-permute-start.13 = (f32[144,128]{1,0:T(8,128)S(1)}, f32[144,128]{1,0:T(8,128)S(1)}, u32[]{:S(2)}, u32[]{:S(2)}) collective-permute-start(f32[144,128]{1,0:T(8,128)S(1)} %get-tuple-element.44), channel_id=1, source_target_pairs={{0,5},{1,0},{2,7},{3,2},{4,1},{5,4},{6,3},{7,6},{8,13},{9,8},{10,1... | collective-permute-start | bytes 221192 | tf_op jit(solution)/shard_map/ppermute | solution.py:102
  19.7 3.0 %collective-permute-start.12 = (f32[144,128]{1,0:T(8,128)S(1)}, f32[144,128]{1,0:T(8,128)S(1)}, u32[]{:S(2)}, u32[]{:S(2)}) collective-permute-start(f32[144,128]{1,0:T(8,128)S(1)} %get-tuple-element.44), channel_id=1, source_target_pairs={{0,3},{1,0},{2,1},{3,2},{4,7},{5,4},{6,5},{7,6},{8,11},{9,8},{10,9... | collective-permute-start | bytes 221192 | tf_op jit(solution)/shard_map/ppermute | solution.py:102
  20.8 2.0 %collective-permute-start.11 = (f32[144,128]{1,0:T(8,128)S(1)}, f32[144,128]{1,0:T(8,128)S(1)}, u32[]{:S(2)}, u32[]{:S(2)}) collective-permute-start(f32[144,128]{1,0:T(8,128)S(1)} %get-tuple-element.44), channel_id=1, source_target_pairs={{0,1},{1,0},{2,3},{3,2},{4,5},{5,4},{6,7},{7,6},{8,9},{9,8},{10,11... | collective-permute-start | bytes 221192 | tf_op jit(solution)/shard_map/ppermute | solution.py:96
  20.8 5.7 %collective-permute-start.20 = (f32[128,128]{1,0:T(8,128)S(1)}, f32[128,128]{1,0:T(8,128)S(1)}, u32[]{:S(2)}, u32[]{:S(2)}) collective-permute-start(f32[128,128]{1,0:T(8,128)S(1)} %get-tuple-element.47.gram), channel_id=1, source_target_pairs={{0,1},{1,0},{2,3},{3,2},{4,5},{5,4},{6,7},{7,6},{8,9},{9,8},{10,11... | collective-permute-start | bytes 196616 | tf_op jit(solution)/shard_map/ppermute | solution.py:96
  22.8 5.9 %collective-permute-start.18 = (f32[128,128]{1,0:T(8,128)S(1)}, f32[128,128]{1,0:T(8,128)S(1)}, u32[]{:S(2)}, u32[]{:S(2)}) collective-permute-start(f32[128,128]{1,0:T(8,128)S(1)} %get-tuple-element.45), channel_id=1, source_target_pairs={{0,1},{1,24},{2,3},{3,26},{4,5},{5,28},{6,7},{7,30},{8,9},{9,16},{... | collective-permute-start | bytes 196616 | tf_op jit(solution)/shard_map/ppermute | solution.py:102
  23.8 6.2 %collective-permute-start.17 = (f32[128,128]{1,0:T(8,128)S(1)}, f32[128,128]{1,0:T(8,128)S(1)}, u32[]{:S(2)}, u32[]{:S(2)}) collective-permute-start(f32[128,128]{1,0:T(8,128)S(1)} %get-tuple-element.45), channel_id=1, source_target_pairs={{0,1},{1,16},{2,3},{3,18},{4,5},{5,20},{6,7},{7,22},{8,9},{9,24},{... | collective-permute-start | bytes 196616 | tf_op jit(solution)/shard_map/ppermute | solution.py:102
  25.0 5.1 %collective-permute-start.16 = (f32[128,128]{1,0:T(8,128)S(1)}, f32[128,128]{1,0:T(8,128)S(1)}, u32[]{:S(2)}, u32[]{:S(2)}) collective-permute-start(f32[128,128]{1,0:T(8,128)S(1)} %get-tuple-element.45), channel_id=1, source_target_pairs={{0,1},{1,8},{2,3},{3,10},{4,5},{5,12},{6,7},{7,14},{8,9},{9,0},{10... | collective-permute-start | bytes 196616 | tf_op jit(solution)/shard_map/ppermute | solution.py:102
  26.5 3.6 %collective-permute-start.15 = (f32[128,128]{1,0:T(8,128)S(1)}, f32[128,128]{1,0:T(8,128)S(1)}, u32[]{:S(2)}, u32[]{:S(2)}) collective-permute-start(f32[128,128]{1,0:T(8,128)S(1)} %get-tuple-element.45), channel_id=1, source_target_pairs={{0,1},{1,0},{2,3},{3,2},{4,5},{5,4},{6,7},{7,6},{8,9},{9,8},{10,11... | collective-permute-start | bytes 196616 | tf_op jit(solution)/shard_map/ppermute | solution.py:96
  26.5 1.3 %collective-permute-start.19 = (f32[32,128]{1,0:T(8,128)S(1)}, f32[32,128]{1,0:T(8,128)S(1)}, u32[]{:S(2)}, u32[]{:S(2)}) collective-permute-start(f32[32,128]{1,0:T(8,128)S(1)} %get-tuple-element.46.rows), channel_id=1, source_target_pairs={{0,1},{1,0},{2,3},{3,2},{4,5},{5,4},{6,7},{7,6},{8,9},{9,8},{10,11... | collective-permute-start | bytes 49160 | tf_op jit(solution)/shard_map/ppermute | solution.py:96
  30.1 1.3 %collective-permute-start.21 = (f32[128,128]{1,0:T(8,128)S(1)}, f32[128,128]{1,0:T(8,128)S(1)}, u32[]{:S(2)}, u32[]{:S(2)}) collective-permute-start(f32[128,128]{1,0:T(8,128)S(1)} %add_add_fusion.terms), channel_id=1, source_target_pairs={{0,1},{1,0},{2,3},{3,2},{4,5},{5,4},{6,7},{7,6},{8,9},{9,8},{10,11... | collective-permute-start | bytes 196616 | tf_op jit(solution)/shard_map/ppermute | solution.py:96

commit v17 on v16

--- a/solution.py
+++ b/solution.py
@@ -313,7 +313,7 @@
 
     terms, rows_b, rows_core = payload[:times], payload[times:], holder
     smp_mask = sum(chip_bits)
-    for group in groups_of(chip_bits + vox_bits):
+    for group in groups_of(chip_bits + vox_bits[1:2] + vox_bits[:1] + vox_bits[2:]):
         masks = masks_of(group)
         if any(mask & smp_mask for mask in masks):
             packet = payload if rows_b.shape[0] == chip_rows else jnp.concatenate([terms, rows_b], axis=0)

time: 32.2 us -> 32 us (level)
  starting transfers between devices: 13.7 us -> 13 us
  waiting for transfers between devices: 12 us -> 12.4 us
    ppermute x11, starting transfers between devices: 10.7 us -> 9.94 us  [send(): return lax.ppermute(values, ALL, pairs)]
    ppermute x11, waiting for transfers between devices: 1.81 us -> 2.16 us  [swap(): lax.ppermute(values, ALL, [(i, i ^ 1) for i in range(lax.axis_size(ALL))])]
where the time goes in v17:
time: 32 us; the launch traced here: 31.9 us
  starting transfers between devices  13 us (41%)
  waiting for transfers between devices  12.4 us (39%)
  Pallas kernels  5.6 us (18%)
  between operations  0.74 us (2%)
    ppermute x11, waiting for transfers between devices, send(): return lax.ppermute(values, ALL, pairs)  10.3 us
    ppermute x11, starting transfers between devices, send(): return lax.ppermute(values, ALL, pairs)  9.94 us
    pallas_call x9, Pallas kernels, call(): pl.pallas_call(kernel, out_shape=outs, in_specs=specs, out_specs=[pl.Bloc...  5.6 us
    ppermute x11, starting transfers between devices, swap(): lax.ppermute(values, ALL, [(i, i ^ 1) for i in range(lax.axis_size(ALL))])  3.08 us
    ppermute x11, waiting for transfers between devices, swap(): lax.ppermute(values, ALL, [(i, i ^ 1) for i in range(lax.axis_size(ALL))])  2.16 us
  transfers between devices with their start and end apart: 22, of which 11 were waited for; matrix products, arithmetic and copies ran while one was open for 0% of the time, Pallas kernels for 7%

profile of v17, /device:TPU:0, one launch (start us, length us, event | category | flops | bytes accessed | tf_op | source)
XLA Modules:
  0.0 31.9 jit_solution(9553886360235486165)
XLA Ops:
  0.6 1.6 %shard_map.84 = (f32[1024,128]{1,0:T(8,128)S(1)}, f32[128,128]{1,0:T(8,128)S(1)}, f32[128,128]{1,0:T(8,128)S(1)}, f32[1,128]{1,0:T(1,128)S(1)}, f32[136,128]{1,0:T(8,128)S(1)}, /*index=5*/f32[8,128,128]{2,1,0:T(8,128)S(1)}) custom-call(f32[1024,128]{1,0:T(8,128)} %bitcast.3, f32[128,128]{1,0:T(8,128)} %c_hbm.1, f32[8,128]{1,0:T(8,128)} %b_hbm.1, ...), custom_call_target="tpu_custom_call" | custom-call | flops 201326592 | bytes 65536 | tf_op jit(solution)/shard_map/pallas_call | solution.py:59
  2.2 0.5 %collective-permute-start = (f32[136,128]{1,0:T(8,128)S(1)}, f32[136,128]{1,0:T(8,128)S(1)}, u32[]{:S(2)}, u32[]{:S(2)}) collective-permute-start(f32[136,128]{1,0:T(8,128)S(1)} %get-tuple-element.34), channel_id=1, source_target_pairs={{0,1},{1,0},{2,3},{3,2},{4,5},{5,4},{6,7},{7,6},{8,9},{9,8},{10,11... | collective-permute-start | bytes 208904 | tf_op jit(solution)/shard_map/ppermute | solution.py:96
  2.7 0.1 collective-permute-start.2
  2.8 0.4 %collective-permute-start.3 = (f32[1024,128]{1,0:T(8,128)S(1)}, f32[1024,128]{1,0:T(8,128)S(1)}, u32[]{:S(2)}, u32[]{:S(2)}) collective-permute-start(f32[1024,128]{1,0:T(8,128)S(1)} %get-tuple-element.40.refs_0_), channel_id=1, source_target_pairs={{0,1},{1,0},{2,3},{3,2},{4,5},{5,4},{6,7},{7,6},{8,9},{9,8},{10,11... | collective-permute-start | bytes 1572872 | tf_op jit(solution)/shard_map/ppermute | solution.py:96
  3.2 0.4 %collective-permute-done = f32[136,128]{1,0:T(8,128)S(1)} collective-permute-done((f32[136,128]{1,0:T(8,128)S(1)}, f32[136,128]{1,0:T(8,128)S(1)}, u32[]{:S(2)}, u32[]{:S(2)}) %collective-permute-start) | collective-permute-done | bytes 69664 | tf_op jit(solution)/shard_map/ppermute | solution.py:96
  3.7 0.4 %collective-permute-start.1 = (f32[144,128]{1,0:T(8,128)S(1)}, f32[144,128]{1,0:T(8,128)S(1)}, u32[]{:S(2)}, u32[]{:S(2)}) collective-permute-start(f32[144,128]{1,0:T(8,128)S(1)} %pad_maximum_fusion), channel_id=1, source_target_pairs={{0,1},{1,2},{2,3},{3,0},{4,5},{5,6},{6,7},{7,4},{8,9},{9,10},{10,1... | collective-permute-start | bytes 221192 | tf_op jit(solution)/shard_map/ppermute | solution.py:102
  4.1 0.2 shard_map.85
  4.3 4.1 %collective-permute-done.1 = f32[144,128]{1,0:T(8,128)S(1)} collective-permute-done((f32[144,128]{1,0:T(8,128)S(1)}, f32[144,128]{1,0:T(8,128)S(1)}, u32[]{:S(2)}, u32[]{:S(2)}) %collective-permute-start.1) | collective-permute-done | bytes 73760 | tf_op jit(solution)/shard_map/ppermute | solution.py:102
  8.4 0.0 collective-permute-done.2.refs_6_
  8.4 0.0 collective-permute-done.3.refs_7_.refs_1_
  8.4 0.7 %shard_map.86 = (f32[128,128]{1,0:T(8,128)S(1)}, f32[16,128]{1,0:T(8,128)S(1)}, f32[88,128]{1,0:T(8,128)S(1)}) custom-call(f32[128,128]{1,0:T(8,128)S(1)} %slice_add_fusion.refs_0_, f32[32,128]{1,0:T(8,128)S(1)} %pad_maximum_fusion.1.refs_1_, f32[128,128]{1,0:T(8,128)S(1)} %get-tuple-element.35.refs_2_, f32[1,128]{1,0:T(1,128)S(1)} %get-tuple-element.36.w.refs_3_.refs_2_, ...), custom_call_target="tpu_custom_call" | custom-call | flops 50331648 | bytes 65536 | tf_op jit(solution)/shard_map/pallas_call | solution.py:59
  9.2 2.2 %collective-permute-start.7 = (f32[88,128]{1,0:T(8,128)S(1)}, f32[88,128]{1,0:T(8,128)S(1)}, u32[]{:S(2)}, u32[]{:S(2)}) collective-permute-start(f32[88,128]{1,0:T(8,128)S(1)} %get-tuple-element.41), channel_id=1, source_target_pairs={{0,21},{1,0},{2,23},{3,2},{4,17},{5,4},{6,19},{7,6},{8,29},{9,8},{... | collective-permute-start | bytes 135176 | tf_op jit(solution)/shard_map/ppermute | solution.py:102
  11.3 1.0 %collective-permute-start.6 = (f32[88,128]{1,0:T(8,128)S(1)}, f32[88,128]{1,0:T(8,128)S(1)}, u32[]{:S(2)}, u32[]{:S(2)}) collective-permute-start(f32[88,128]{1,0:T(8,128)S(1)} %get-tuple-element.41), channel_id=1, source_target_pairs={{0,17},{1,0},{2,19},{3,2},{4,21},{5,4},{6,23},{7,6},{8,25},{9,8},{... | collective-permute-start | bytes 135176 | tf_op jit(solution)/shard_map/ppermute | solution.py:102
  12.4 0.5 %collective-permute-start.4 = (f32[88,128]{1,0:T(8,128)S(1)}, f32[88,128]{1,0:T(8,128)S(1)}, u32[]{:S(2)}, u32[]{:S(2)}) collective-permute-start(f32[88,128]{1,0:T(8,128)S(1)} %get-tuple-element.41), channel_id=1, source_target_pairs={{0,1},{1,0},{2,3},{3,2},{4,5},{5,4},{6,7},{7,6},{8,9},{9,8},{10,11... | collective-permute-start | bytes 135176 | tf_op jit(solution)/shard_map/ppermute | solution.py:96
  12.9 0.2 collective-permute-done.7
  13.1 1.0 %collective-permute-done.6 = f32[88,128]{1,0:T(8,128)S(1)} collective-permute-done((f32[88,128]{1,0:T(8,128)S(1)}, f32[88,128]{1,0:T(8,128)S(1)}, u32[]{:S(2)}, u32[]{:S(2)}) %collective-permute-start.6) | collective-permute-done | bytes 45088 | tf_op jit(solution)/shard_map/ppermute | solution.py:102
  14.1 0.0 collective-permute-done.5
  14.1 0.0 collective-permute-done.4
  14.1 1.7 %collective-permute-start.9 = (f32[88,128]{1,0:T(8,128)S(1)}, f32[88,128]{1,0:T(8,128)S(1)}, u32[]{:S(2)}, u32[]{:S(2)}) collective-permute-start(f32[88,128]{1,0:T(8,128)S(1)} %add_add_fusion.1), channel_id=1, source_target_pairs={{0,1},{1,8},{2,3},{3,10},{4,5},{5,12},{6,7},{7,14},{8,9},{9,0},{10... | collective-permute-start | bytes 135176 | tf_op jit(solution)/shard_map/ppermute | solution.py:102
  15.8 0.3 %collective-permute-start.8 = (f32[88,128]{1,0:T(8,128)S(1)}, f32[88,128]{1,0:T(8,128)S(1)}, u32[]{:S(2)}, u32[]{:S(2)}) collective-permute-start(f32[88,128]{1,0:T(8,128)S(1)} %add_add_fusion.1), channel_id=1, source_target_pairs={{0,1},{1,0},{2,3},{3,2},{4,5},{5,4},{6,7},{7,6},{8,9},{9,8},{10,11... | collective-permute-start | bytes 135176 | tf_op jit(solution)/shard_map/ppermute | solution.py:96
  16.1 0.0 collective-permute-done.10.refs_3_.mate_moved
  16.1 0.5 %shard_map.87.refs_4_ = f32[16,128,128]{2,1,0:T(8,128)S(1)} custom-call(f32[1024,128]{1,0:T(8,128)S(1)} %get-tuple-element.40.refs_0_, f32[1024,128]{1,0:T(8,128)S(1)} %collective-permute-done.3.refs_7_.refs_1_, f32[128,128]{1,0:T(8,128)S(1)} %get-tuple-element.43.refs_2_.moved, f32[128,128]{1,0:T(8,128)S(1)} %collective-permute-done.10.refs_3_.mate_moved), custom_call_target="tpu_custom_call" | custom-call | flops 402653184 | bytes 65536 | tf_op jit(solution)/shard_map/pallas_call | solution.py:59
  16.6 2.1 %collective-permute-done.9 = f32[88,128]{1,0:T(8,128)S(1)} collective-permute-done((f32[88,128]{1,0:T(8,128)S(1)}, f32[88,128]{1,0:T(8,128)S(1)}, u32[]{:S(2)}, u32[]{:S(2)}) %collective-permute-start.9) | collective-permute-done | bytes 45088 | tf_op jit(solution)/shard_map/ppermute | solution.py:102
  18.7 0.0 collective-permute-done.8
  18.7 0.3 %shard_map.88 = (f32[128,128]{1,0:T(8,128)S(1)}, f32[144,128]{1,0:T(8,128)S(1)}) custom-call(f32[88,128]{1,0:T(8,128)S(1)} %add.32.refs_0_, f32[16,128]{1,0:T(8,128)S(1)} %get-tuple-element.42.refs_1_, f32[1,128]{1,0:T(1,128)S(1)} %get-tuple-element.36.w.refs_3_.refs_2_, f32[128,128]{1,0:T(8,128)S(1)} %get-tuple-element.38.refs_4_.refs_3_, ...), custom_call_target="tpu_custom_call" | custom-call | flops 3145728 | bytes 65536 | tf_op jit(solution)/shard_map/pallas_call | solution.py:59
  19.1 0.3 collective-permute-start.14
  19.3 0.6 %collective-permute-start.13 = (f32[144,128]{1,0:T(8,128)S(1)}, f32[144,128]{1,0:T(8,128)S(1)}, u32[]{:S(2)}, u32[]{:S(2)}) collective-permute-start(f32[144,128]{1,0:T(8,128)S(1)} %get-tuple-element.44), channel_id=1, source_target_pairs={{0,9},{1,0},{2,11},{3,2},{4,13},{5,4},{6,15},{7,6},{8,1},{9,8},{10... | collective-permute-start | bytes 221192 | tf_op jit(solution)/shard_map/ppermute | solution.py:102
  20.0 0.8 %collective-permute-start.12 = (f32[144,128]{1,0:T(8,128)S(1)}, f32[144,128]{1,0:T(8,128)S(1)}, u32[]{:S(2)}, u32[]{:S(2)}) collective-permute-start(f32[144,128]{1,0:T(8,128)S(1)} %get-tuple-element.44), channel_id=1, source_target_pairs={{0,3},{1,0},{2,1},{3,2},{4,7},{5,4},{6,5},{7,6},{8,11},{9,8},{10,9... | collective-permute-start | bytes 221192 | tf_op jit(solution)/shard_map/ppermute | solution.py:102
  20.8 0.0 collective-permute-start.11
  20.8 0.5 %collective-permute-start.20 = (f32[128,128]{1,0:T(8,128)S(1)}, f32[128,128]{1,0:T(8,128)S(1)}, u32[]{:S(2)}, u32[]{:S(2)}) collective-permute-start(f32[128,128]{1,0:T(8,128)S(1)} %get-tuple-element.47.gram), channel_id=1, source_target_pairs={{0,1},{1,0},{2,3},{3,2},{4,5},{5,4},{6,7},{7,6},{8,9},{9,8},{10,11... | collective-permute-start | bytes 196616 | tf_op jit(solution)/shard_map/ppermute | solution.py:96
  21.3 0.0 collective-permute-done.14.refs_3_
  21.3 0.7 %collective-permute-done.13.refs_2_ = f32[144,128]{1,0:T(8,128)S(1)} collective-permute-done((f32[144,128]{1,0:T(8,128)S(1)}, f32[144,128]{1,0:T(8,128)S(1)}, u32[]{:S(2)}, u32[]{:S(2)}) %collective-permute-start.13) | collective-permute-done | bytes 73760 | tf_op jit(solution)/shard_map/ppermute | solution.py:102
  22.0 0.8 %collective-permute-done.12.refs_1_ = f32[144,128]{1,0:T(8,128)S(1)} collective-permute-done((f32[144,128]{1,0:T(8,128)S(1)}, f32[144,128]{1,0:T(8,128)S(1)}, u32[]{:S(2)}, u32[]{:S(2)}) %collective-permute-start.12) | collective-permute-done | bytes 73760 | tf_op jit(solution)/shard_map/ppermute | solution.py:102
  22.8 0.0 collective-permute-done.11.refs_0_
  22.8 1.0 %collective-permute-start.18 = (f32[128,128]{1,0:T(8,128)S(1)}, f32[128,128]{1,0:T(8,128)S(1)}, u32[]{:S(2)}, u32[]{:S(2)}) collective-permute-start(f32[128,128]{1,0:T(8,128)S(1)} %get-tuple-element.45), channel_id=1, source_target_pairs={{0,1},{1,20},{2,3},{3,22},{4,5},{5,16},{6,7},{7,18},{8,9},{9,28},{... | collective-permute-start | bytes 196616 | tf_op jit(solution)/shard_map/ppermute | solution.py:102
  23.9 1.9 %collective-permute-start.17 = (f32[128,128]{1,0:T(8,128)S(1)}, f32[128,128]{1,0:T(8,128)S(1)}, u32[]{:S(2)}, u32[]{:S(2)}) collective-permute-start(f32[128,128]{1,0:T(8,128)S(1)} %get-tuple-element.45), channel_id=1, source_target_pairs={{0,1},{1,16},{2,3},{3,18},{4,5},{5,20},{6,7},{7,22},{8,9},{9,24},{... | collective-permute-start | bytes 196616 | tf_op jit(solution)/shard_map/ppermute | solution.py:102
  25.7 0.6 %collective-permute-start.15 = (f32[128,128]{1,0:T(8,128)S(1)}, f32[128,128]{1,0:T(8,128)S(1)}, u32[]{:S(2)}, u32[]{:S(2)}) collective-permute-start(f32[128,128]{1,0:T(8,128)S(1)} %get-tuple-element.45), channel_id=1, source_target_pairs={{0,1},{1,0},{2,3},{3,2},{4,5},{5,4},{6,7},{7,6},{8,9},{9,8},{10,11... | collective-permute-start | bytes 196616 | tf_op jit(solution)/shard_map/ppermute | solution.py:96
  26.4 0.0 collective-permute-done.20.mate_gram
  26.4 0.0 collective-permute-start.19
  26.4 0.7 %shard_map.90 = (f32[128,128]{1,0:T(8,128)}, f32[1,128]{1,0:T(1,128)S(1)}, f32[128,128]{1,0:T(8,128)S(1)}) custom-call(f32[128,128]{1,0:T(8,128)S(1)} %get-tuple-element.47.gram, f32[128,128]{1,0:T(8,128)S(1)} %collective-permute-done.20.mate_gram, f32[128,128]{1,0:T(8,128)S(1)} %get-tuple-element.43.refs_2_.moved, ...), custom_call_target="tpu_custom_call" | custom-call | flops 131072 | bytes 65536 | tf_op jit(solution)/shard_map/pallas_call | solution.py:59
  27.1 0.5 %collective-permute-done.19.mate_rows = f32[32,128]{1,0:T(8,128)S(1)} collective-permute-done((f32[32,128]{1,0:T(8,128)S(1)}, f32[32,128]{1,0:T(8,128)S(1)}, u32[]{:S(2)}, u32[]{:S(2)}) %collective-permute-start.19) | collective-permute-done | bytes 16416 | tf_op jit(solution)/shard_map/ppermute | solution.py:96
  27.6 0.9 %shard_map.91 = (f32[8,128]{1,0:T(8,128)}, f32[128,128]{1,0:T(8,128)S(1)}, f32[1,128]{1,0:T(1,128)S(1)}, f32[1,128]{1,0:T(1,128)S(1)}) custom-call(f32[32,128]{1,0:T(8,128)S(1)} %get-tuple-element.46.rows, f32[32,128]{1,0:T(8,128)S(1)} %collective-permute-done.19.mate_rows, f32[128,128]{1,0:T(8,128)S(1)} %get-tuple-element.37.c, ...), custom_call_target="tpu_custom_call" | custom-call | flops 16777216 | bytes 65536 | tf_op jit(solution)/shard_map/pallas_call | solution.py:59
  28.4 1.3 %collective-permute-done.18 = f32[128,128]{1,0:T(8,128)S(1)} collective-permute-done((f32[128,128]{1,0:T(8,128)S(1)}, f32[128,128]{1,0:T(8,128)S(1)}, u32[]{:S(2)}, u32[]{:S(2)}) %collective-permute-start.18) | collective-permute-done | bytes 65568 | tf_op jit(solution)/shard_map/ppermute | solution.py:102
  29.7 0.1 collective-permute-done.17
  29.8 0.0 collective-permute-done.16
  29.9 0.1 collective-permute-start.21
  30.0 1.2 %collective-permute-done.21.mate_terms = f32[128,128]{1,0:T(8,128)S(1)} collective-permute-done((f32[128,128]{1,0:T(8,128)S(1)}, f32[128,128]{1,0:T(8,128)S(1)}, u32[]{:S(2)}, u32[]{:S(2)}) %collective-permute-start.21) | collective-permute-done | bytes 65568 | tf_op jit(solution)/shard_map/ppermute | solution.py:96
  31.2 0.7 %shard_map.92 = (f32[128,128]{1,0:T(8,128)}, f32[1,128]{1,0:T(1,128)}) custom-call(f32[128,128]{1,0:T(8,128)S(1)} %add_add_fusion.terms, f32[128,128]{1,0:T(8,128)S(1)} %collective-permute-done.21.mate_terms, f32[128,128]{1,0:T(8,128)S(1)} %get-tuple-element.59.base, f32[1,128]{1,0:T(1,128)S(1)} %get-tuple-element.60.gain, f32[1,128]{1,0:T(1,128)S(1)} %get-tuple-element.61.scale), custom_call_target="tpu_custom_call" | custom-call | flops 131072 | bytes 65536 | tf_op jit(solution)/shard_map/pallas_call | solution.py:59
  (15 shorter events, 0.1 us)
Async XLA Ops:
  2.2 1.4 %collective-permute-start = (f32[136,128]{1,0:T(8,128)S(1)}, f32[136,128]{1,0:T(8,128)S(1)}, u32[]{:S(2)}, u32[]{:S(2)}) collective-permute-start(f32[136,128]{1,0:T(8,128)S(1)} %get-tuple-element.34), channel_id=1, source_target_pairs={{0,1},{1,0},{2,3},{3,2},{4,5},{5,4},{6,7},{7,6},{8,9},{9,8},{10,11... | collective-permute-start | bytes 208904 | tf_op jit(solution)/shard_map/ppermute | solution.py:96
  2.7 5.7 %collective-permute-start.2 = (f32[8,128,128]{2,1,0:T(8,128)S(1)}, f32[8,128,128]{2,1,0:T(8,128)S(1)}, u32[]{:S(2)}, u32[]{:S(2)}) collective-permute-start(f32[8,128,128]{2,1,0:T(8,128)S(1)} %get-tuple-element.39.refs_5_), channel_id=1, source_target_pairs={{0,1},{1,0},{2,3},{3,2},{4,5},{5,4},{6,7},{7,6},{8,9},{9,8},{10,11... | collective-permute-start | bytes 1572872 | tf_op jit(solution)/shard_map/ppermute | solution.py:96
  2.8 5.6 %collective-permute-start.3 = (f32[1024,128]{1,0:T(8,128)S(1)}, f32[1024,128]{1,0:T(8,128)S(1)}, u32[]{:S(2)}, u32[]{:S(2)}) collective-permute-start(f32[1024,128]{1,0:T(8,128)S(1)} %get-tuple-element.40.refs_0_), channel_id=1, source_target_pairs={{0,1},{1,0},{2,3},{3,2},{4,5},{5,4},{6,7},{7,6},{8,9},{9,8},{10,11... | collective-permute-start | bytes 1572872 | tf_op jit(solution)/shard_map/ppermute | solution.py:96
  3.7 4.7 %collective-permute-start.1 = (f32[144,128]{1,0:T(8,128)S(1)}, f32[144,128]{1,0:T(8,128)S(1)}, u32[]{:S(2)}, u32[]{:S(2)}) collective-permute-start(f32[144,128]{1,0:T(8,128)S(1)} %pad_maximum_fusion), channel_id=1, source_target_pairs={{0,1},{1,2},{2,3},{3,0},{4,5},{5,6},{6,7},{7,4},{8,9},{9,10},{10,1... | collective-permute-start | bytes 221192 | tf_op jit(solution)/shard_map/ppermute | solution.py:102
  9.2 3.9 %collective-permute-start.7 = (f32[88,128]{1,0:T(8,128)S(1)}, f32[88,128]{1,0:T(8,128)S(1)}, u32[]{:S(2)}, u32[]{:S(2)}) collective-permute-start(f32[88,128]{1,0:T(8,128)S(1)} %get-tuple-element.41), channel_id=1, source_target_pairs={{0,21},{1,0},{2,23},{3,2},{4,17},{5,4},{6,19},{7,6},{8,29},{9,8},{... | collective-permute-start | bytes 135176 | tf_op jit(solution)/shard_map/ppermute | solution.py:102
  11.3 2.7 %collective-permute-start.6 = (f32[88,128]{1,0:T(8,128)S(1)}, f32[88,128]{1,0:T(8,128)S(1)}, u32[]{:S(2)}, u32[]{:S(2)}) collective-permute-start(f32[88,128]{1,0:T(8,128)S(1)} %get-tuple-element.41), channel_id=1, source_target_pairs={{0,17},{1,0},{2,19},{3,2},{4,21},{5,4},{6,23},{7,6},{8,25},{9,8},{... | collective-permute-start | bytes 135176 | tf_op jit(solution)/shard_map/ppermute | solution.py:102
  12.4 1.7 %collective-permute-start.5 = (f32[88,128]{1,0:T(8,128)S(1)}, f32[88,128]{1,0:T(8,128)S(1)}, u32[]{:S(2)}, u32[]{:S(2)}) collective-permute-start(f32[88,128]{1,0:T(8,128)S(1)} %get-tuple-element.41), channel_id=1, source_target_pairs={{0,5},{1,0},{2,7},{3,2},{4,1},{5,4},{6,3},{7,6},{8,13},{9,8},{10,1... | collective-permute-start | bytes 135176 | tf_op jit(solution)/shard_map/ppermute | solution.py:102
  12.4 1.7 %collective-permute-start.4 = (f32[88,128]{1,0:T(8,128)S(1)}, f32[88,128]{1,0:T(8,128)S(1)}, u32[]{:S(2)}, u32[]{:S(2)}) collective-permute-start(f32[88,128]{1,0:T(8,128)S(1)} %get-tuple-element.41), channel_id=1, source_target_pairs={{0,1},{1,0},{2,3},{3,2},{4,5},{5,4},{6,7},{7,6},{8,9},{9,8},{10,11... | collective-permute-start | bytes 135176 | tf_op jit(solution)/shard_map/ppermute | solution.py:96
  12.9 3.2 %collective-permute-start.10 = (f32[128,128]{1,0:T(8,128)S(1)}, f32[128,128]{1,0:T(8,128)S(1)}, u32[]{:S(2)}, u32[]{:S(2)}) collective-permute-start(f32[128,128]{1,0:T(8,128)S(1)} %get-tuple-element.43.refs_2_.moved), channel_id=1, source_target_pairs={{0,1},{1,0},{2,3},{3,2},{4,5},{5,4},{6,7},{7,6},{8,9},{9,8},{10,11... | collective-permute-start | bytes 196616 | tf_op jit(solution)/shard_map/ppermute | solution.py:96
  14.1 4.6 %collective-permute-start.9 = (f32[88,128]{1,0:T(8,128)S(1)}, f32[88,128]{1,0:T(8,128)S(1)}, u32[]{:S(2)}, u32[]{:S(2)}) collective-permute-start(f32[88,128]{1,0:T(8,128)S(1)} %add_add_fusion.1), channel_id=1, source_target_pairs={{0,1},{1,8},{2,3},{3,10},{4,5},{5,12},{6,7},{7,14},{8,9},{9,0},{10... | collective-permute-start | bytes 135176 | tf_op jit(solution)/shard_map/ppermute | solution.py:102
  15.8 2.9 %collective-permute-start.8 = (f32[88,128]{1,0:T(8,128)S(1)}, f32[88,128]{1,0:T(8,128)S(1)}, u32[]{:S(2)}, u32[]{:S(2)}) collective-permute-start(f32[88,128]{1,0:T(8,128)S(1)} %add_add_fusion.1), channel_id=1, source_target_pairs={{0,1},{1,0},{2,3},{3,2},{4,5},{5,4},{6,7},{7,6},{8,9},{9,8},{10,11... | collective-permute-start | bytes 135176 | tf_op jit(solution)/shard_map/ppermute | solution.py:96
  19.1 2.3 %collective-permute-start.14 = (f32[144,128]{1,0:T(8,128)S(1)}, f32[144,128]{1,0:T(8,128)S(1)}, u32[]{:S(2)}, u32[]{:S(2)}) collective-permute-start(f32[144,128]{1,0:T(8,128)S(1)} %get-tuple-element.44), channel_id=1, source_target_pairs={{0,11},{1,0},{2,9},{3,2},{4,15},{5,4},{6,13},{7,6},{8,3},{9,8},{10... | collective-permute-start | bytes 221192 | tf_op jit(solution)/shard_map/ppermute | solution.py:102
  19.3 2.7 %collective-permute-start.13 = (f32[144,128]{1,0:T(8,128)S(1)}, f32[144,128]{1,0:T(8,128)S(1)}, u32[]{:S(2)}, u32[]{:S(2)}) collective-permute-start(f32[144,128]{1,0:T(8,128)S(1)} %get-tuple-element.44), channel_id=1, source_target_pairs={{0,9},{1,0},{2,11},{3,2},{4,13},{5,4},{6,15},{7,6},{8,1},{9,8},{10... | collective-permute-start | bytes 221192 | tf_op jit(solution)/shard_map/ppermute | solution.py:102
  20.0 2.8 %collective-permute-start.12 = (f32[144,128]{1,0:T(8,128)S(1)}, f32[144,128]{1,0:T(8,128)S(1)}, u32[]{:S(2)}, u32[]{:S(2)}) collective-permute-start(f32[144,128]{1,0:T(8,128)S(1)} %get-tuple-element.44), channel_id=1, source_target_pairs={{0,3},{1,0},{2,1},{3,2},{4,7},{5,4},{6,5},{7,6},{8,11},{9,8},{10,9... | collective-permute-start | bytes 221192 | tf_op jit(solution)/shard_map/ppermute | solution.py:102
  20.8 2.0 %collective-permute-start.11 = (f32[144,128]{1,0:T(8,128)S(1)}, f32[144,128]{1,0:T(8,128)S(1)}, u32[]{:S(2)}, u32[]{:S(2)}) collective-permute-start(f32[144,128]{1,0:T(8,128)S(1)} %get-tuple-element.44), channel_id=1, source_target_pairs={{0,1},{1,0},{2,3},{3,2},{4,5},{5,4},{6,7},{7,6},{8,9},{9,8},{10,11... | collective-permute-start | bytes 221192 | tf_op jit(solution)/shard_map/ppermute | solution.py:96
  20.8 5.6 %collective-permute-start.20 = (f32[128,128]{1,0:T(8,128)S(1)}, f32[128,128]{1,0:T(8,128)S(1)}, u32[]{:S(2)}, u32[]{:S(2)}) collective-permute-start(f32[128,128]{1,0:T(8,128)S(1)} %get-tuple-element.47.gram), channel_id=1, source_target_pairs={{0,1},{1,0},{2,3},{3,2},{4,5},{5,4},{6,7},{7,6},{8,9},{9,8},{10,11... | collective-permute-start | bytes 196616 | tf_op jit(solution)/shard_map/ppermute | solution.py:96
  22.8 6.9 %collective-permute-start.18 = (f32[128,128]{1,0:T(8,128)S(1)}, f32[128,128]{1,0:T(8,128)S(1)}, u32[]{:S(2)}, u32[]{:S(2)}) collective-permute-start(f32[128,128]{1,0:T(8,128)S(1)} %get-tuple-element.45), channel_id=1, source_target_pairs={{0,1},{1,20},{2,3},{3,22},{4,5},{5,16},{6,7},{7,18},{8,9},{9,28},{... | collective-permute-start | bytes 196616 | tf_op jit(solution)/shard_map/ppermute | solution.py:102
  23.9 6.0 %collective-permute-start.17 = (f32[128,128]{1,0:T(8,128)S(1)}, f32[128,128]{1,0:T(8,128)S(1)}, u32[]{:S(2)}, u32[]{:S(2)}) collective-permute-start(f32[128,128]{1,0:T(8,128)S(1)} %get-tuple-element.45), channel_id=1, source_target_pairs={{0,1},{1,16},{2,3},{3,18},{4,5},{5,20},{6,7},{7,22},{8,9},{9,24},{... | collective-permute-start | bytes 196616 | tf_op jit(solution)/shard_map/ppermute | solution.py:102
  25.7 4.1 %collective-permute-start.16 = (f32[128,128]{1,0:T(8,128)S(1)}, f32[128,128]{1,0:T(8,128)S(1)}, u32[]{:S(2)}, u32[]{:S(2)}) collective-permute-start(f32[128,128]{1,0:T(8,128)S(1)} %get-tuple-element.45), channel_id=1, source_target_pairs={{0,1},{1,4},{2,3},{3,6},{4,5},{5,0},{6,7},{7,2},{8,9},{9,12},{10,1... | collective-permute-start | bytes 196616 | tf_op jit(solution)/shard_map/ppermute | solution.py:102
  25.7 4.1 %collective-permute-start.15 = (f32[128,128]{1,0:T(8,128)S(1)}, f32[128,128]{1,0:T(8,128)S(1)}, u32[]{:S(2)}, u32[]{:S(2)}) collective-permute-start(f32[128,128]{1,0:T(8,128)S(1)} %get-tuple-element.45), channel_id=1, source_target_pairs={{0,1},{1,0},{2,3},{3,2},{4,5},{5,4},{6,7},{7,6},{8,9},{9,8},{10,11... | collective-permute-start | bytes 196616 | tf_op jit(solution)/shard_map/ppermute | solution.py:96
  26.4 1.2 %collective-permute-start.19 = (f32[32,128]{1,0:T(8,128)S(1)}, f32[32,128]{1,0:T(8,128)S(1)}, u32[]{:S(2)}, u32[]{:S(2)}) collective-permute-start(f32[32,128]{1,0:T(8,128)S(1)} %get-tuple-element.46.rows), channel_id=1, source_target_pairs={{0,1},{1,0},{2,3},{3,2},{4,5},{5,4},{6,7},{7,6},{8,9},{9,8},{10,11... | collective-permute-start | bytes 49160 | tf_op jit(solution)/shard_map/ppermute | solution.py:96
  29.9 1.3 %collective-permute-start.21 = (f32[128,128]{1,0:T(8,128)S(1)}, f32[128,128]{1,0:T(8,128)S(1)}, u32[]{:S(2)}, u32[]{:S(2)}) collective-permute-start(f32[128,128]{1,0:T(8,128)S(1)} %add_add_fusion.terms), channel_id=1, source_target_pairs={{0,1},{1,0},{2,3},{3,2},{4,5},{5,4},{6,7},{7,6},{8,9},{9,8},{10,11... | collective-permute-start | bytes 196616 | tf_op jit(solution)/shard_map/ppermute | solution.py:96

commit v18 on v17

--- a/solution.py
+++ b/solution.py
@@ -45,9 +45,13 @@
     return jnp.sum(jnp.where(rows == columns, gram, 0.0), axis=0, keepdims=True)
 
 
-def only_on(core, kernel):
+def role_index():
+    return (smp_index() ^ lax.axis_index("vox")) & 1
+
+
+def only_on(role, kernel):
     def run(*refs):
-        pl.when(smp_index() & 1 == core)(lambda: kernel(*refs))
+        pl.when(role_index() == role)(lambda: kernel(*refs))
 
     return run
 
@@ -97,8 +101,12 @@
 
 
 def send(values, holder, mask):
-    count = lax.axis_size(ALL)
-    pairs = [(i, i ^ 1 ^ mask if i & 1 == holder else i ^ 1) for i in range(count)]
+    smp_count, count = lax.axis_size("smp"), lax.axis_size(ALL)
+    role = lambda i: (i ^ i // smp_count) & 1
+    pairs = []
+    for i in range(count):
+        target = i ^ mask if role(i) == holder else i
+        pairs.append((i, target ^ 1 if role(target) == role(i) else target))
     return lax.ppermute(values, ALL, pairs)
 
 
@@ -118,8 +126,8 @@
     return lax.axis_index("smp")
 
 
-def on_core(core, own, got):
-    return jnp.where(smp_index() & 1 == core, own, got)
+def on_role(role, own, got):
+    return jnp.where(role_index() == role, own, got)
 
 
 def pack(gram):
@@ -142,11 +150,14 @@
     return jnp.concatenate([top, jnp.where(columns < half, turned[half:], corner)], axis=0)
 
 
-def in_order(rows, scratch, chips):
-    block = scratch.shape[0] // chips
+def in_order(rows, scratch, chips, flip=0):
+    size = scratch.shape[0] // chips // 2
     chip = smp_index() // 2
     for p in range(chips):
-        scratch[pl.ds(pl.multiple_of((chip ^ (chips - 1 - p)) * block, block), block), :] = rows[p * block : (p + 1) * block, :]
+        for q in range(2):
+            start = (2 * p + q) * size
+            place = (chip ^ (chips - 1 - p)) * 2 + (q ^ flip)
+            scratch[pl.ds(pl.multiple_of(place * size, size), size), :] = rows[start : start + size, :]
     return scratch[...]
 
 
@@ -228,26 +239,27 @@
         packet = jnp.concatenate([terms, rows_b], axis=0)
         own = swap(packet)
         holder ^= 1
-    voxel_core = holder
+    voxel_role = holder
 
     half, sums_rows = rank // 2, rank // 2 + chip_rows
 
     def voxel_kernel(terms, rows, a, w, outer_c, con, mate_con, mate_x, moved_out, chip_b, out, all_b):
-        b = in_order(rows, all_b, chips)
+        b = in_order(rows, all_b, chips, lax.axis_index("vox") & 1)
         chip_b[...] = all_b[pl.ds(pl.multiple_of(smp_index() // 2 * chip_rows, chip_rows), chip_rows), :]
         coupled = outer_c[...] * dot_rows(b, b)
         moved = a[...] - step_of(coupled) * (dot(a[...], coupled) - terms[...] * w[...])
         moved_out[...] = moved
         packed, diagonal = pack(dot_rows(moved, moved))
         out[:half, :] = packed
-        for core in range(2):
-            for j in range(smp_rows):
-                row = half + core * smp_rows + j
-                out[row : row + 1, :] = jnp.sum((con if core == voxel_core else mate_con)[j] * moved, axis=0, keepdims=True)
+        core = smp_index() & 1
+        for place, source in ((core, con), (1 - core, mate_con)):
+            made = [jnp.sum(source[j] * moved, axis=0, keepdims=True) for j in range(smp_rows)]
+            start = pl.multiple_of(half + place * smp_rows, smp_rows)
+            out[pl.ds(start, smp_rows), :] = jnp.concatenate(made, axis=0)
         out[sums_rows:, :] = jnp.broadcast_to(diagonal, (8, rank))
 
     moved_a, chip_b, sums = call(
-        only_on(voxel_core, voxel_kernel),
+        only_on(voxel_role, voxel_kernel),
         (near(vox_rows, rank), near(chip_rows, rank), near(sums_rows + 8, rank)),
         (terms, rows_b, a_near, w_row, outer_c, con, mate_con, mate_x),
         2 * rank * rank * vox_rows * 12,
@@ -259,19 +271,20 @@
     for group in groups_of(vox_bits[:1] + vox_bits[:0:-1]):
         sums = tree(fan(sums, holder, masks_of(group)))
         holder ^= 1
-    sample_core = holder
-    if sample_core != voxel_core:
+    sample_role = holder
+    if sample_role != voxel_role:
         chip_b = swap(chip_b)
 
     def time_kernel(x, mate_x, moved, mate_moved, each):
-        moved = on_core(voxel_core, moved[...], mate_moved[...])
-        for core in range(2):
+        moved = on_role(voxel_role, moved[...], mate_moved[...])
+        core = smp_index() & 1
+        for place, source in ((core, x), (1 - core, mate_x)):
             for j in range(smp_rows):
-                block = (x if core == sample_core else mate_x)[pl.ds(j, vox_rows, stride=smp_rows), :]
-                each[core * smp_rows + j] = dot_rows(block, moved)
+                block = source[pl.ds(j, vox_rows, stride=smp_rows), :]
+                each[place * smp_rows + j] = dot_rows(block, moved)
 
     (each,) = call(
-        only_on(sample_core, time_kernel),
+        only_on(sample_role, time_kernel),
         (near(chip_rows, times, rank),),
         (x, mate_x, moved_a, mate_moved_a),
         4 * flat_rows * times * rank * 6,
@@ -290,7 +303,7 @@
         out[:times, :] = total
 
     gram_a, payload = call(
-        only_on(sample_core, sample_kernel),
+        only_on(sample_role, sample_kernel),
         (near(rank, rank), near(times + chip_rows, rank)),
         (sums, chip_b, w_row, outer_c, each),
         2 * rank * rank * chip_rows * 6,
@@ -298,10 +311,10 @@
     mate_gram_a = swap(gram_a)
 
     def scale_kernel(gram, mate_gram, moved, mate_moved, outer, result, scales_out, weighed):
-        gram = on_core(sample_core, gram[...], mate_gram[...])
+        gram = on_role(sample_role, gram[...], mate_gram[...])
         scales = jnp.sqrt(diagonal_row(gram) / vox_total + 1e-06)
         scales_out[...] = scales
-        result[...] = on_core(voxel_core, moved[...], mate_moved[...]) / scales
+        result[...] = on_role(voxel_role, moved[...], mate_moved[...]) / scales
         weighed[...] = outer[...] * gram
 
     voxel_result, scales_a, weighed = call(
@@ -311,7 +324,7 @@
         vox_rows * rank * 8,
     )
 
-    terms, rows_b, rows_core = payload[:times], payload[times:], holder
+    terms, rows_b, rows_role = payload[:times], payload[times:], holder
     smp_mask = sum(chip_bits)
     for group in groups_of(chip_bits + vox_bits[1:2] + vox_bits[:1] + vox_bits[2:]):
         masks = masks_of(group)
@@ -333,15 +346,15 @@
                 parts[::-1],
                 len(masks) * times * rank,
             )
-            rows_core = holder ^ 1
+            rows_role = holder ^ 1
         else:
             terms = tree(fan(terms, holder, masks))
         holder ^= 1
-    last_core = holder
+    last_role = holder
     mate_rows_b = swap(rows_b)
 
     def ready_kernel(rows, mate_rows, c, w, weighed, scales_a, b_out, base, gain, scale, all_b):
-        b = in_order(on_core(rows_core, rows[...], mate_rows[...]), all_b, chips)
+        b = in_order(on_role(rows_role, rows[...], mate_rows[...]), all_b, chips)
         coupled = weighed[...] * dot_rows(b, b)
         step = step_of(coupled)
         base[...] = c[...] - step * dot(c[...], coupled)
@@ -363,7 +376,7 @@
     mate_terms = swap(terms)
 
     def last_kernel(terms, mate_terms, base, gain, scale, c_out, w_out):
-        moved = base[...] + on_core(last_core, terms[...], mate_terms[...]) * gain[...]
+        moved = base[...] + on_role(last_role, terms[...], mate_terms[...]) * gain[...]
         scales_c = jnp.sqrt(jnp.sum(moved * moved, axis=0, keepdims=True) / times + 1e-06)
         c_out[...] = moved / scales_c
         w_out[...] = scale[...] * scales_c

time: 32 us -> 31.8 us (level)
  waiting for transfers between devices: 12.4 us -> 11.1 us
  starting transfers between devices: 13 us -> 14.1 us
    ppermute x11, waiting for transfers between devices: 10.3 us -> 9.13 us  [send(): return lax.ppermute(values, ALL, pairs)]
    ppermute x11, starting transfers between devices: 3.08 us -> 3.81 us  [swap(): lax.ppermute(values, ALL, [(i, i ^ 1) for i in range(lax.axis_size(ALL))])]
  transfers between devices with their start and end apart: 22 -> 22, of which waited for: 11 -> 10; matrix products, arithmetic and copies ran while one was open for 0% -> 0% of each run, Pallas kernels for 7% -> 7%
where the time goes in v18:
time: 31.8 us; the launch traced here: 31.6 us
  starting transfers between devices  14.1 us (44%)
  waiting for transfers between devices  11.1 us (35%)
  Pallas kernels  5.62 us (18%)
  between operations  0.74 us (2%)
    ppermute x11, starting transfers between devices, send(): return lax.ppermute(values, ALL, pairs)  10.2 us
    ppermute x11, waiting for transfers between devices, send(): return lax.ppermute(values, ALL, pairs)  9.13 us
    pallas_call x9, Pallas kernels, call(): pl.pallas_call(kernel, out_shape=outs, in_specs=specs, out_specs=[pl.Bloc...  5.62 us
    ppermute x11, starting transfers between devices, swap(): lax.ppermute(values, ALL, [(i, i ^ 1) for i in range(lax.axis_size(ALL))])  3.81 us
    ppermute x11, waiting for transfers between devices, swap(): lax.ppermute(values, ALL, [(i, i ^ 1) for i in range(lax.axis_size(ALL))])  2 us
  transfers between devices with their start and end apart: 22, of which 10 were waited for; matrix products, arithmetic and copies ran while one was open for 0% of the time, Pallas kernels for 7%

profile of v18, /device:TPU:0, one launch (start us, length us, event | category | flops | bytes accessed | tf_op | source)
XLA Modules:
  0.0 31.6 jit_solution(16087996631834505714)
XLA Ops:
  0.6 1.6 %shard_map.84 = (f32[1024,128]{1,0:T(8,128)S(1)}, f32[128,128]{1,0:T(8,128)S(1)}, f32[128,128]{1,0:T(8,128)S(1)}, f32[1,128]{1,0:T(1,128)S(1)}, f32[136,128]{1,0:T(8,128)S(1)}, /*index=5*/f32[8,128,128]{2,1,0:T(8,128)S(1)}) custom-call(f32[1024,128]{1,0:T(8,128)} %bitcast.3, f32[128,128]{1,0:T(8,128)} %c_hbm.1, f32[8,128]{1,0:T(8,128)} %b_hbm.1, ...), custom_call_target="tpu_custom_call" | custom-call | flops 201326592 | bytes 65536 | tf_op jit(solution)/shard_map/pallas_call | solution.py:63
  2.2 0.5 %collective-permute-start = (f32[136,128]{1,0:T(8,128)S(1)}, f32[136,128]{1,0:T(8,128)S(1)}, u32[]{:S(2)}, u32[]{:S(2)}) collective-permute-start(f32[136,128]{1,0:T(8,128)S(1)} %get-tuple-element.34), channel_id=1, source_target_pairs={{0,1},{1,0},{2,3},{3,2},{4,5},{5,4},{6,7},{7,6},{8,9},{9,8},{10,11... | collective-permute-start | bytes 208904 | tf_op jit(solution)/shard_map/ppermute | solution.py:100
  2.7 0.1 collective-permute-start.2
  2.8 0.4 %collective-permute-start.3 = (f32[1024,128]{1,0:T(8,128)S(1)}, f32[1024,128]{1,0:T(8,128)S(1)}, u32[]{:S(2)}, u32[]{:S(2)}) collective-permute-start(f32[1024,128]{1,0:T(8,128)S(1)} %get-tuple-element.40.refs_0_), channel_id=1, source_target_pairs={{0,1},{1,0},{2,3},{3,2},{4,5},{5,4},{6,7},{7,6},{8,9},{9,8},{10,11... | collective-permute-start | bytes 1572872 | tf_op jit(solution)/shard_map/ppermute | solution.py:100
  3.2 0.4 %collective-permute-done = f32[136,128]{1,0:T(8,128)S(1)} collective-permute-done((f32[136,128]{1,0:T(8,128)S(1)}, f32[136,128]{1,0:T(8,128)S(1)}, u32[]{:S(2)}, u32[]{:S(2)}) %collective-permute-start) | collective-permute-done | bytes 69664 | tf_op jit(solution)/shard_map/ppermute | solution.py:100
  3.7 0.4 %collective-permute-start.1 = (f32[144,128]{1,0:T(8,128)S(1)}, f32[144,128]{1,0:T(8,128)S(1)}, u32[]{:S(2)}, u32[]{:S(2)}) collective-permute-start(f32[144,128]{1,0:T(8,128)S(1)} %pad_maximum_fusion), channel_id=1, source_target_pairs={{0,1},{1,2},{2,3},{3,0},{4,7},{5,4},{6,5},{7,6},{8,9},{9,10},{10,1... | collective-permute-start | bytes 221192 | tf_op jit(solution)/shard_map/ppermute | solution.py:110
  4.1 0.2 shard_map.85
  4.3 4.1 %collective-permute-done.1 = f32[144,128]{1,0:T(8,128)S(1)} collective-permute-done((f32[144,128]{1,0:T(8,128)S(1)}, f32[144,128]{1,0:T(8,128)S(1)}, u32[]{:S(2)}, u32[]{:S(2)}) %collective-permute-start.1) | collective-permute-done | bytes 73760 | tf_op jit(solution)/shard_map/ppermute | solution.py:110
  8.4 0.0 collective-permute-done.2.refs_6_
  8.4 0.0 collective-permute-done.3.refs_7_.refs_1_
  8.4 0.7 %shard_map.86 = (f32[128,128]{1,0:T(8,128)S(1)}, f32[16,128]{1,0:T(8,128)S(1)}, f32[88,128]{1,0:T(8,128)S(1)}) custom-call(f32[128,128]{1,0:T(8,128)S(1)} %slice_add_fusion.refs_0_, f32[32,128]{1,0:T(8,128)S(1)} %pad_maximum_fusion.1.refs_1_, f32[128,128]{1,0:T(8,128)S(1)} %get-tuple-element.35.refs_2_, f32[1,128]{1,0:T(1,128)S(1)} %get-tuple-element.36.w.refs_3_.refs_2_, ...), custom_call_target="tpu_custom_call" | custom-call | flops 50331648 | bytes 65536 | tf_op jit(solution)/shard_map/pallas_call | solution.py:63
  9.2 2.8 %collective-permute-start.7 = (f32[88,128]{1,0:T(8,128)S(1)}, f32[88,128]{1,0:T(8,128)S(1)}, u32[]{:S(2)}, u32[]{:S(2)}) collective-permute-start(f32[88,128]{1,0:T(8,128)S(1)} %get-tuple-element.41), channel_id=1, source_target_pairs={{0,20},{1,0},{2,22},{3,2},{4,5},{5,17},{6,7},{7,19},{8,28},{9,8},{... | collective-permute-start | bytes 135176 | tf_op jit(solution)/shard_map/ppermute | solution.py:110
  12.0 0.4 %collective-permute-start.6 = (f32[88,128]{1,0:T(8,128)S(1)}, f32[88,128]{1,0:T(8,128)S(1)}, u32[]{:S(2)}, u32[]{:S(2)}) collective-permute-start(f32[88,128]{1,0:T(8,128)S(1)} %get-tuple-element.41), channel_id=1, source_target_pairs={{0,17},{1,0},{2,19},{3,2},{4,5},{5,20},{6,7},{7,22},{8,25},{9,8},{... | collective-permute-start | bytes 135176 | tf_op jit(solution)/shard_map/ppermute | solution.py:110
  12.4 0.5 %collective-permute-start.4 = (f32[88,128]{1,0:T(8,128)S(1)}, f32[88,128]{1,0:T(8,128)S(1)}, u32[]{:S(2)}, u32[]{:S(2)}) collective-permute-start(f32[88,128]{1,0:T(8,128)S(1)} %get-tuple-element.41), channel_id=1, source_target_pairs={{0,1},{1,0},{2,3},{3,2},{4,5},{5,4},{6,7},{7,6},{8,9},{9,8},{10,11... | collective-permute-start | bytes 135176 | tf_op jit(solution)/shard_map/ppermute | solution.py:100
  12.9 0.0 collective-permute-start.10
  12.9 0.8 %collective-permute-done.7 = f32[88,128]{1,0:T(8,128)S(1)} collective-permute-done((f32[88,128]{1,0:T(8,128)S(1)}, f32[88,128]{1,0:T(8,128)S(1)}, u32[]{:S(2)}, u32[]{:S(2)}) %collective-permute-start.7) | collective-permute-done | bytes 45088 | tf_op jit(solution)/shard_map/ppermute | solution.py:110
  13.7 0.4 %collective-permute-done.6 = f32[88,128]{1,0:T(8,128)S(1)} collective-permute-done((f32[88,128]{1,0:T(8,128)S(1)}, f32[88,128]{1,0:T(8,128)S(1)}, u32[]{:S(2)}, u32[]{:S(2)}) %collective-permute-start.6) | collective-permute-done | bytes 45088 | tf_op jit(solution)/shard_map/ppermute | solution.py:110
  14.1 0.0 collective-permute-done.5
  14.1 0.0 collective-permute-done.4
  14.1 1.3 %collective-permute-start.9 = (f32[88,128]{1,0:T(8,128)S(1)}, f32[88,128]{1,0:T(8,128)S(1)}, u32[]{:S(2)}, u32[]{:S(2)}) collective-permute-start(f32[88,128]{1,0:T(8,128)S(1)} %add_add_fusion.1), channel_id=1, source_target_pairs={{0,1},{1,8},{2,3},{3,10},{4,13},{5,4},{6,15},{7,6},{8,9},{9,0},{10... | collective-permute-start | bytes 135176 | tf_op jit(solution)/shard_map/ppermute | solution.py:110
  15.5 1.2 %collective-permute-start.8 = (f32[88,128]{1,0:T(8,128)S(1)}, f32[88,128]{1,0:T(8,128)S(1)}, u32[]{:S(2)}, u32[]{:S(2)}) collective-permute-start(f32[88,128]{1,0:T(8,128)S(1)} %add_add_fusion.1), channel_id=1, source_target_pairs={{0,1},{1,0},{2,3},{3,2},{4,5},{5,4},{6,7},{7,6},{8,9},{9,8},{10,11... | collective-permute-start | bytes 135176 | tf_op jit(solution)/shard_map/ppermute | solution.py:100
  16.6 0.5 %shard_map.87.refs_4_ = f32[16,128,128]{2,1,0:T(8,128)S(1)} custom-call(f32[1024,128]{1,0:T(8,128)S(1)} %get-tuple-element.40.refs_0_, f32[1024,128]{1,0:T(8,128)S(1)} %collective-permute-done.3.refs_7_.refs_1_, f32[128,128]{1,0:T(8,128)S(1)} %get-tuple-element.43.refs_2_.moved, f32[128,128]{1,0:T(8,128)S(1)} %collective-permute-done.10.refs_3_.mate_moved), custom_call_target="tpu_custom_call" | custom-call | flops 402653184 | bytes 65536 | tf_op jit(solution)/shard_map/pallas_call | solution.py:63
  17.2 1.2 %collective-permute-done.9 = f32[88,128]{1,0:T(8,128)S(1)} collective-permute-done((f32[88,128]{1,0:T(8,128)S(1)}, f32[88,128]{1,0:T(8,128)S(1)}, u32[]{:S(2)}, u32[]{:S(2)}) %collective-permute-start.9) | collective-permute-done | bytes 45088 | tf_op jit(solution)/shard_map/ppermute | solution.py:110
  18.4 0.0 collective-permute-done.8
  18.4 0.3 %shard_map.88 = (f32[128,128]{1,0:T(8,128)S(1)}, f32[144,128]{1,0:T(8,128)S(1)}) custom-call(f32[88,128]{1,0:T(8,128)S(1)} %add.32.refs_0_, f32[16,128]{1,0:T(8,128)S(1)} %get-tuple-element.42.refs_1_, f32[1,128]{1,0:T(1,128)S(1)} %get-tuple-element.36.w.refs_3_.refs_2_, f32[128,128]{1,0:T(8,128)S(1)} %get-tuple-element.38.refs_4_.refs_3_, ...), custom_call_target="tpu_custom_call" | custom-call | flops 3145728 | bytes 65536 | tf_op jit(solution)/shard_map/pallas_call | solution.py:63
  18.7 0.1 collective-permute-start.14
  18.8 1.7 %collective-permute-start.13 = (f32[144,128]{1,0:T(8,128)S(1)}, f32[144,128]{1,0:T(8,128)S(1)}, u32[]{:S(2)}, u32[]{:S(2)}) collective-permute-start(f32[144,128]{1,0:T(8,128)S(1)} %get-tuple-element.44), channel_id=1, source_target_pairs={{0,9},{1,0},{2,11},{3,2},{4,5},{5,12},{6,7},{7,14},{8,1},{9,8},{10... | collective-permute-start | bytes 221192 | tf_op jit(solution)/shard_map/ppermute | solution.py:110
  20.5 0.0 collective-permute-start.12
  20.5 0.5 %collective-permute-start.11 = (f32[144,128]{1,0:T(8,128)S(1)}, f32[144,128]{1,0:T(8,128)S(1)}, u32[]{:S(2)}, u32[]{:S(2)}) collective-permute-start(f32[144,128]{1,0:T(8,128)S(1)} %get-tuple-element.44), channel_id=1, source_target_pairs={{0,1},{1,0},{2,3},{3,2},{4,5},{5,4},{6,7},{7,6},{8,9},{9,8},{10,11... | collective-permute-start | bytes 221192 | tf_op jit(solution)/shard_map/ppermute | solution.py:100
  21.1 1.5 %collective-permute-done.13.refs_2_ = f32[144,128]{1,0:T(8,128)S(1)} collective-permute-done((f32[144,128]{1,0:T(8,128)S(1)}, f32[144,128]{1,0:T(8,128)S(1)}, u32[]{:S(2)}, u32[]{:S(2)}) %collective-permute-start.13) | collective-permute-done | bytes 73760 | tf_op jit(solution)/shard_map/ppermute | solution.py:110
  22.5 0.0 collective-permute-done.12.refs_1_
  22.5 0.0 collective-permute-done.11.refs_0_
  22.5 1.3 %collective-permute-start.18 = (f32[128,128]{1,0:T(8,128)S(1)}, f32[128,128]{1,0:T(8,128)S(1)}, u32[]{:S(2)}, u32[]{:S(2)}) collective-permute-start(f32[128,128]{1,0:T(8,128)S(1)} %get-tuple-element.45), channel_id=1, source_target_pairs={{0,1},{1,21},{2,3},{3,23},{4,16},{5,4},{6,18},{7,6},{8,9},{9,29},{... | collective-permute-start | bytes 196616 | tf_op jit(solution)/shard_map/ppermute | solution.py:110
  23.9 1.2 %collective-permute-start.17 = (f32[128,128]{1,0:T(8,128)S(1)}, f32[128,128]{1,0:T(8,128)S(1)}, u32[]{:S(2)}, u32[]{:S(2)}) collective-permute-start(f32[128,128]{1,0:T(8,128)S(1)} %get-tuple-element.45), channel_id=1, source_target_pairs={{0,1},{1,16},{2,3},{3,18},{4,21},{5,4},{6,23},{7,6},{8,9},{9,24},{... | collective-permute-start | bytes 196616 | tf_op jit(solution)/shard_map/ppermute | solution.py:110
  25.1 1.0 %collective-permute-start.16 = (f32[128,128]{1,0:T(8,128)S(1)}, f32[128,128]{1,0:T(8,128)S(1)}, u32[]{:S(2)}, u32[]{:S(2)}) collective-permute-start(f32[128,128]{1,0:T(8,128)S(1)} %get-tuple-element.45), channel_id=1, source_target_pairs={{0,1},{1,5},{2,3},{3,7},{4,0},{5,4},{6,2},{7,6},{8,9},{9,13},{10,1... | collective-permute-start | bytes 196616 | tf_op jit(solution)/shard_map/ppermute | solution.py:110
  26.0 0.3 %collective-permute-start.15 = (f32[128,128]{1,0:T(8,128)S(1)}, f32[128,128]{1,0:T(8,128)S(1)}, u32[]{:S(2)}, u32[]{:S(2)}) collective-permute-start(f32[128,128]{1,0:T(8,128)S(1)} %get-tuple-element.45), channel_id=1, source_target_pairs={{0,1},{1,0},{2,3},{3,2},{4,5},{5,4},{6,7},{7,6},{8,9},{9,8},{10,11... | collective-permute-start | bytes 196616 | tf_op jit(solution)/shard_map/ppermute | solution.py:100
  26.4 0.0 collective-permute-done.20.mate_gram
  26.4 0.2 collective-permute-start.19
  26.6 0.7 %shard_map.90 = (f32[128,128]{1,0:T(8,128)}, f32[1,128]{1,0:T(1,128)S(1)}, f32[128,128]{1,0:T(8,128)S(1)}) custom-call(f32[128,128]{1,0:T(8,128)S(1)} %get-tuple-element.47.gram, f32[128,128]{1,0:T(8,128)S(1)} %collective-permute-done.20.mate_gram, f32[128,128]{1,0:T(8,128)S(1)} %get-tuple-element.43.refs_2_.moved, ...), custom_call_target="tpu_custom_call" | custom-call | flops 131072 | bytes 65536 | tf_op jit(solution)/shard_map/pallas_call | solution.py:63
  27.2 0.3 %collective-permute-done.19.mate_rows = f32[32,128]{1,0:T(8,128)S(1)} collective-permute-done((f32[32,128]{1,0:T(8,128)S(1)}, f32[32,128]{1,0:T(8,128)S(1)}, u32[]{:S(2)}, u32[]{:S(2)}) %collective-permute-start.19) | collective-permute-done | bytes 16416 | tf_op jit(solution)/shard_map/ppermute | solution.py:100
  27.6 0.9 %shard_map.91 = (f32[8,128]{1,0:T(8,128)}, f32[128,128]{1,0:T(8,128)S(1)}, f32[1,128]{1,0:T(1,128)S(1)}, f32[1,128]{1,0:T(1,128)S(1)}) custom-call(f32[32,128]{1,0:T(8,128)S(1)} %get-tuple-element.46.rows, f32[32,128]{1,0:T(8,128)S(1)} %collective-permute-done.19.mate_rows, f32[128,128]{1,0:T(8,128)S(1)} %get-tuple-element.37.c, ...), custom_call_target="tpu_custom_call" | custom-call | flops 16777216 | bytes 65536 | tf_op jit(solution)/shard_map/pallas_call | solution.py:63
  28.4 0.3 %collective-permute-done.18 = f32[128,128]{1,0:T(8,128)S(1)} collective-permute-done((f32[128,128]{1,0:T(8,128)S(1)}, f32[128,128]{1,0:T(8,128)S(1)}, u32[]{:S(2)}, u32[]{:S(2)}) %collective-permute-start.18) | collective-permute-done | bytes 65568 | tf_op jit(solution)/shard_map/ppermute | solution.py:110
  28.8 0.8 %collective-permute-done.17 = f32[128,128]{1,0:T(8,128)S(1)} collective-permute-done((f32[128,128]{1,0:T(8,128)S(1)}, f32[128,128]{1,0:T(8,128)S(1)}, u32[]{:S(2)}, u32[]{:S(2)}) %collective-permute-start.17) | collective-permute-done | bytes 65568 | tf_op jit(solution)/shard_map/ppermute | solution.py:110
  29.6 0.0 collective-permute-done.16
  29.6 0.0 collective-permute-done.15
  29.6 0.1 collective-permute-start.21
  29.7 1.2 %collective-permute-done.21.mate_terms = f32[128,128]{1,0:T(8,128)S(1)} collective-permute-done((f32[128,128]{1,0:T(8,128)S(1)}, f32[128,128]{1,0:T(8,128)S(1)}, u32[]{:S(2)}, u32[]{:S(2)}) %collective-permute-start.21) | collective-permute-done | bytes 65568 | tf_op jit(solution)/shard_map/ppermute | solution.py:100
  30.9 0.7 %shard_map.92 = (f32[128,128]{1,0:T(8,128)}, f32[1,128]{1,0:T(1,128)}) custom-call(f32[128,128]{1,0:T(8,128)S(1)} %add_add_fusion.terms, f32[128,128]{1,0:T(8,128)S(1)} %collective-permute-done.21.mate_terms, f32[128,128]{1,0:T(8,128)S(1)} %get-tuple-element.59.base, f32[1,128]{1,0:T(1,128)S(1)} %get-tuple-element.60.gain, f32[1,128]{1,0:T(1,128)S(1)} %get-tuple-element.61.scale), custom_call_target="tpu_custom_call" | custom-call | flops 131072 | bytes 65536 | tf_op jit(solution)/shard_map/pallas_call | solution.py:63
  (15 shorter events, 0.1 us)
Async XLA Ops:
  2.2 1.4 %collective-permute-start = (f32[136,128]{1,0:T(8,128)S(1)}, f32[136,128]{1,0:T(8,128)S(1)}, u32[]{:S(2)}, u32[]{:S(2)}) collective-permute-start(f32[136,128]{1,0:T(8,128)S(1)} %get-tuple-element.34), channel_id=1, source_target_pairs={{0,1},{1,0},{2,3},{3,2},{4,5},{5,4},{6,7},{7,6},{8,9},{9,8},{10,11... | collective-permute-start | bytes 208904 | tf_op jit(solution)/shard_map/ppermute | solution.py:100
  2.7 5.7 %collective-permute-start.2 = (f32[8,128,128]{2,1,0:T(8,128)S(1)}, f32[8,128,128]{2,1,0:T(8,128)S(1)}, u32[]{:S(2)}, u32[]{:S(2)}) collective-permute-start(f32[8,128,128]{2,1,0:T(8,128)S(1)} %get-tuple-element.39.refs_5_), channel_id=1, source_target_pairs={{0,1},{1,0},{2,3},{3,2},{4,5},{5,4},{6,7},{7,6},{8,9},{9,8},{10,11... | collective-permute-start | bytes 1572872 | tf_op jit(solution)/shard_map/ppermute | solution.py:100
  2.8 5.6 %collective-permute-start.3 = (f32[1024,128]{1,0:T(8,128)S(1)}, f32[1024,128]{1,0:T(8,128)S(1)}, u32[]{:S(2)}, u32[]{:S(2)}) collective-permute-start(f32[1024,128]{1,0:T(8,128)S(1)} %get-tuple-element.40.refs_0_), channel_id=1, source_target_pairs={{0,1},{1,0},{2,3},{3,2},{4,5},{5,4},{6,7},{7,6},{8,9},{9,8},{10,11... | collective-permute-start | bytes 1572872 | tf_op jit(solution)/shard_map/ppermute | solution.py:100
  3.7 4.7 %collective-permute-start.1 = (f32[144,128]{1,0:T(8,128)S(1)}, f32[144,128]{1,0:T(8,128)S(1)}, u32[]{:S(2)}, u32[]{:S(2)}) collective-permute-start(f32[144,128]{1,0:T(8,128)S(1)} %pad_maximum_fusion), channel_id=1, source_target_pairs={{0,1},{1,2},{2,3},{3,0},{4,7},{5,4},{6,5},{7,6},{8,9},{9,10},{10,1... | collective-permute-start | bytes 221192 | tf_op jit(solution)/shard_map/ppermute | solution.py:110
  9.2 4.5 %collective-permute-start.7 = (f32[88,128]{1,0:T(8,128)S(1)}, f32[88,128]{1,0:T(8,128)S(1)}, u32[]{:S(2)}, u32[]{:S(2)}) collective-permute-start(f32[88,128]{1,0:T(8,128)S(1)} %get-tuple-element.41), channel_id=1, source_target_pairs={{0,20},{1,0},{2,22},{3,2},{4,5},{5,17},{6,7},{7,19},{8,28},{9,8},{... | collective-permute-start | bytes 135176 | tf_op jit(solution)/shard_map/ppermute | solution.py:110
  12.0 2.1 %collective-permute-start.6 = (f32[88,128]{1,0:T(8,128)S(1)}, f32[88,128]{1,0:T(8,128)S(1)}, u32[]{:S(2)}, u32[]{:S(2)}) collective-permute-start(f32[88,128]{1,0:T(8,128)S(1)} %get-tuple-element.41), channel_id=1, source_target_pairs={{0,17},{1,0},{2,19},{3,2},{4,5},{5,20},{6,7},{7,22},{8,25},{9,8},{... | collective-permute-start | bytes 135176 | tf_op jit(solution)/shard_map/ppermute | solution.py:110
  12.4 1.7 %collective-permute-start.5 = (f32[88,128]{1,0:T(8,128)S(1)}, f32[88,128]{1,0:T(8,128)S(1)}, u32[]{:S(2)}, u32[]{:S(2)}) collective-permute-start(f32[88,128]{1,0:T(8,128)S(1)} %get-tuple-element.41), channel_id=1, source_target_pairs={{0,4},{1,0},{2,6},{3,2},{4,5},{5,1},{6,7},{7,3},{8,12},{9,8},{10,1... | collective-permute-start | bytes 135176 | tf_op jit(solution)/shard_map/ppermute | solution.py:110
  12.4 1.7 %collective-permute-start.4 = (f32[88,128]{1,0:T(8,128)S(1)}, f32[88,128]{1,0:T(8,128)S(1)}, u32[]{:S(2)}, u32[]{:S(2)}) collective-permute-start(f32[88,128]{1,0:T(8,128)S(1)} %get-tuple-element.41), channel_id=1, source_target_pairs={{0,1},{1,0},{2,3},{3,2},{4,5},{5,4},{6,7},{7,6},{8,9},{9,8},{10,11... | collective-permute-start | bytes 135176 | tf_op jit(solution)/shard_map/ppermute | solution.py:100
  12.9 3.8 %collective-permute-start.10 = (f32[128,128]{1,0:T(8,128)S(1)}, f32[128,128]{1,0:T(8,128)S(1)}, u32[]{:S(2)}, u32[]{:S(2)}) collective-permute-start(f32[128,128]{1,0:T(8,128)S(1)} %get-tuple-element.43.refs_2_.moved), channel_id=1, source_target_pairs={{0,1},{1,0},{2,3},{3,2},{4,5},{5,4},{6,7},{7,6},{8,9},{9,8},{10,11... | collective-permute-start | bytes 196616 | tf_op jit(solution)/shard_map/ppermute | solution.py:100
  14.1 4.2 %collective-permute-start.9 = (f32[88,128]{1,0:T(8,128)S(1)}, f32[88,128]{1,0:T(8,128)S(1)}, u32[]{:S(2)}, u32[]{:S(2)}) collective-permute-start(f32[88,128]{1,0:T(8,128)S(1)} %add_add_fusion.1), channel_id=1, source_target_pairs={{0,1},{1,8},{2,3},{3,10},{4,13},{5,4},{6,15},{7,6},{8,9},{9,0},{10... | collective-permute-start | bytes 135176 | tf_op jit(solution)/shard_map/ppermute | solution.py:110
  15.5 2.9 %collective-permute-start.8 = (f32[88,128]{1,0:T(8,128)S(1)}, f32[88,128]{1,0:T(8,128)S(1)}, u32[]{:S(2)}, u32[]{:S(2)}) collective-permute-start(f32[88,128]{1,0:T(8,128)S(1)} %add_add_fusion.1), channel_id=1, source_target_pairs={{0,1},{1,0},{2,3},{3,2},{4,5},{5,4},{6,7},{7,6},{8,9},{9,8},{10,11... | collective-permute-start | bytes 135176 | tf_op jit(solution)/shard_map/ppermute | solution.py:100
  18.7 2.3 %collective-permute-start.14 = (f32[144,128]{1,0:T(8,128)S(1)}, f32[144,128]{1,0:T(8,128)S(1)}, u32[]{:S(2)}, u32[]{:S(2)}) collective-permute-start(f32[144,128]{1,0:T(8,128)S(1)} %get-tuple-element.44), channel_id=1, source_target_pairs={{0,11},{1,0},{2,9},{3,2},{4,5},{5,14},{6,7},{7,12},{8,3},{9,8},{10... | collective-permute-start | bytes 221192 | tf_op jit(solution)/shard_map/ppermute | solution.py:110
  18.8 3.7 %collective-permute-start.13 = (f32[144,128]{1,0:T(8,128)S(1)}, f32[144,128]{1,0:T(8,128)S(1)}, u32[]{:S(2)}, u32[]{:S(2)}) collective-permute-start(f32[144,128]{1,0:T(8,128)S(1)} %get-tuple-element.44), channel_id=1, source_target_pairs={{0,9},{1,0},{2,11},{3,2},{4,5},{5,12},{6,7},{7,14},{8,1},{9,8},{10... | collective-permute-start | bytes 221192 | tf_op jit(solution)/shard_map/ppermute | solution.py:110
  20.5 2.0 %collective-permute-start.12 = (f32[144,128]{1,0:T(8,128)S(1)}, f32[144,128]{1,0:T(8,128)S(1)}, u32[]{:S(2)}, u32[]{:S(2)}) collective-permute-start(f32[144,128]{1,0:T(8,128)S(1)} %get-tuple-element.44), channel_id=1, source_target_pairs={{0,3},{1,0},{2,1},{3,2},{4,5},{5,6},{6,7},{7,4},{8,11},{9,8},{10,9... | collective-permute-start | bytes 221192 | tf_op jit(solution)/shard_map/ppermute | solution.py:110
  20.5 2.0 %collective-permute-start.11 = (f32[144,128]{1,0:T(8,128)S(1)}, f32[144,128]{1,0:T(8,128)S(1)}, u32[]{:S(2)}, u32[]{:S(2)}) collective-permute-start(f32[144,128]{1,0:T(8,128)S(1)} %get-tuple-element.44), channel_id=1, source_target_pairs={{0,1},{1,0},{2,3},{3,2},{4,5},{5,4},{6,7},{7,6},{8,9},{9,8},{10,11... | collective-permute-start | bytes 221192 | tf_op jit(solution)/shard_map/ppermute | solution.py:100
  21.0 5.4 %collective-permute-start.20 = (f32[128,128]{1,0:T(8,128)S(1)}, f32[128,128]{1,0:T(8,128)S(1)}, u32[]{:S(2)}, u32[]{:S(2)}) collective-permute-start(f32[128,128]{1,0:T(8,128)S(1)} %get-tuple-element.47.gram), channel_id=1, source_target_pairs={{0,1},{1,0},{2,3},{3,2},{4,5},{5,4},{6,7},{7,6},{8,9},{9,8},{10,11... | collective-permute-start | bytes 196616 | tf_op jit(solution)/shard_map/ppermute | solution.py:100
  22.5 6.2 %collective-permute-start.18 = (f32[128,128]{1,0:T(8,128)S(1)}, f32[128,128]{1,0:T(8,128)S(1)}, u32[]{:S(2)}, u32[]{:S(2)}) collective-permute-start(f32[128,128]{1,0:T(8,128)S(1)} %get-tuple-element.45), channel_id=1, source_target_pairs={{0,1},{1,21},{2,3},{3,23},{4,16},{5,4},{6,18},{7,6},{8,9},{9,29},{... | collective-permute-start | bytes 196616 | tf_op jit(solution)/shard_map/ppermute | solution.py:110
  23.9 5.7 %collective-permute-start.17 = (f32[128,128]{1,0:T(8,128)S(1)}, f32[128,128]{1,0:T(8,128)S(1)}, u32[]{:S(2)}, u32[]{:S(2)}) collective-permute-start(f32[128,128]{1,0:T(8,128)S(1)} %get-tuple-element.45), channel_id=1, source_target_pairs={{0,1},{1,16},{2,3},{3,18},{4,21},{5,4},{6,23},{7,6},{8,9},{9,24},{... | collective-permute-start | bytes 196616 | tf_op jit(solution)/shard_map/ppermute | solution.py:110
  25.1 4.5 %collective-permute-start.16 = (f32[128,128]{1,0:T(8,128)S(1)}, f32[128,128]{1,0:T(8,128)S(1)}, u32[]{:S(2)}, u32[]{:S(2)}) collective-permute-start(f32[128,128]{1,0:T(8,128)S(1)} %get-tuple-element.45), channel_id=1, source_target_pairs={{0,1},{1,5},{2,3},{3,7},{4,0},{5,4},{6,2},{7,6},{8,9},{9,13},{10,1... | collective-permute-start | bytes 196616 | tf_op jit(solution)/shard_map/ppermute | solution.py:110
  26.0 3.6 %collective-permute-start.15 = (f32[128,128]{1,0:T(8,128)S(1)}, f32[128,128]{1,0:T(8,128)S(1)}, u32[]{:S(2)}, u32[]{:S(2)}) collective-permute-start(f32[128,128]{1,0:T(8,128)S(1)} %get-tuple-element.45), channel_id=1, source_target_pairs={{0,1},{1,0},{2,3},{3,2},{4,5},{5,4},{6,7},{7,6},{8,9},{9,8},{10,11... | collective-permute-start | bytes 196616 | tf_op jit(solution)/shard_map/ppermute | solution.py:100
  26.4 1.2 %collective-permute-start.19 = (f32[32,128]{1,0:T(8,128)S(1)}, f32[32,128]{1,0:T(8,128)S(1)}, u32[]{:S(2)}, u32[]{:S(2)}) collective-permute-start(f32[32,128]{1,0:T(8,128)S(1)} %get-tuple-element.46.rows), channel_id=1, source_target_pairs={{0,1},{1,0},{2,3},{3,2},{4,5},{5,4},{6,7},{7,6},{8,9},{9,8},{10,11... | collective-permute-start | bytes 49160 | tf_op jit(solution)/shard_map/ppermute | solution.py:100
  29.6 1.3 %collective-permute-start.21 = (f32[128,128]{1,0:T(8,128)S(1)}, f32[128,128]{1,0:T(8,128)S(1)}, u32[]{:S(2)}, u32[]{:S(2)}) collective-permute-start(f32[128,128]{1,0:T(8,128)S(1)} %add_add_fusion.terms), channel_id=1, source_target_pairs={{0,1},{1,0},{2,3},{3,2},{4,5},{5,4},{6,7},{7,6},{8,9},{9,8},{10,11... | collective-permute-start | bytes 196616 | tf_op jit(solution)/shard_map/ppermute | solution.py:100

commit v19 on v18

--- a/solution.py
+++ b/solution.py
@@ -46,7 +46,7 @@
 
 
 def role_index():
-    return (smp_index() ^ lax.axis_index("vox")) & 1
+    return (smp_index() ^ lax.axis_index("vox") // 2) & 1
 
 
 def only_on(role, kernel):
@@ -102,7 +102,7 @@
 
 def send(values, holder, mask):
     smp_count, count = lax.axis_size("smp"), lax.axis_size(ALL)
-    role = lambda i: (i ^ i // smp_count) & 1
+    role = lambda i: (i ^ i // (2 * smp_count)) & 1
     pairs = []
     for i in range(count):
         target = i ^ mask if role(i) == holder else i
@@ -244,7 +244,7 @@
     half, sums_rows = rank // 2, rank // 2 + chip_rows
 
     def voxel_kernel(terms, rows, a, w, outer_c, con, mate_con, mate_x, moved_out, chip_b, out, all_b):
-        b = in_order(rows, all_b, chips, lax.axis_index("vox") & 1)
+        b = in_order(rows, all_b, chips, lax.axis_index("vox") // 2 & 1)
         chip_b[...] = all_b[pl.ds(pl.multiple_of(smp_index() // 2 * chip_rows, chip_rows), chip_rows), :]
         coupled = outer_c[...] * dot_rows(b, b)
         moved = a[...] - step_of(coupled) * (dot(a[...], coupled) - terms[...] * w[...])

time: 31.8 us -> 31.6 us (level)
  starting transfers between devices: 14.1 us -> 12.7 us
  waiting for transfers between devices: 11.1 us -> 12.3 us
    ppermute x11, waiting for transfers between devices: 9.13 us -> 10.5 us  [send(): return lax.ppermute(values, ALL, pairs)]
    ppermute x11, starting transfers between devices: 3.81 us -> 2.7 us  [swap(): lax.ppermute(values, ALL, [(i, i ^ 1) for i in range(lax.axis_size(ALL))])]
  transfers between devices with their start and end apart: 22 -> 22, of which waited for: 10 -> 12; matrix products, arithmetic and copies ran while one was open for 0% -> 0% of each run, Pallas kernels for 7% -> 7%
where the time goes in v19:
time: 31.6 us; the launch traced here: 31.5 us
  starting transfers between devices  12.7 us (40%)
  waiting for transfers between devices  12.3 us (39%)
  Pallas kernels  5.63 us (18%)
  between operations  0.74 us (2%)
    ppermute x11, waiting for transfers between devices, send(): return lax.ppermute(values, ALL, pairs)  10.5 us
    ppermute x11, starting transfers between devices, send(): return lax.ppermute(values, ALL, pairs)  10 us
    pallas_call x9, Pallas kernels, call(): pl.pallas_call(kernel, out_shape=outs, in_specs=specs, out_specs=[pl.Bloc...  5.63 us
    ppermute x11, starting transfers between devices, swap(): lax.ppermute(values, ALL, [(i, i ^ 1) for i in range(lax.axis_size(ALL))])  2.7 us
    ppermute x11, waiting for transfers between devices, swap(): lax.ppermute(values, ALL, [(i, i ^ 1) for i in range(lax.axis_size(ALL))])  1.81 us
  transfers between devices with their start and end apart: 22, of which 12 were waited for; matrix products, arithmetic and copies ran while one was open for 0% of the time, Pallas kernels for 7%

profile of v19, /device:TPU:0, one launch (start us, length us, event | category | flops | bytes accessed | tf_op | source)
XLA Modules:
  0.0 31.5 jit_solution(1259251832281847625)
XLA Ops:
  0.6 1.6 %shard_map.84 = (f32[1024,128]{1,0:T(8,128)S(1)}, f32[128,128]{1,0:T(8,128)S(1)}, f32[128,128]{1,0:T(8,128)S(1)}, f32[1,128]{1,0:T(1,128)S(1)}, f32[136,128]{1,0:T(8,128)S(1)}, /*index=5*/f32[8,128,128]{2,1,0:T(8,128)S(1)}) custom-call(f32[1024,128]{1,0:T(8,128)} %bitcast.3, f32[128,128]{1,0:T(8,128)} %c_hbm.1, f32[8,128]{1,0:T(8,128)} %b_hbm.1, ...), custom_call_target="tpu_custom_call" | custom-call | flops 201326592 | bytes 65536 | tf_op jit(solution)/shard_map/pallas_call | solution.py:63
  2.2 0.5 %collective-permute-start = (f32[136,128]{1,0:T(8,128)S(1)}, f32[136,128]{1,0:T(8,128)S(1)}, u32[]{:S(2)}, u32[]{:S(2)}) collective-permute-start(f32[136,128]{1,0:T(8,128)S(1)} %get-tuple-element.34), channel_id=1, source_target_pairs={{0,1},{1,0},{2,3},{3,2},{4,5},{5,4},{6,7},{7,6},{8,9},{9,8},{10,11... | collective-permute-start | bytes 208904 | tf_op jit(solution)/shard_map/ppermute | solution.py:100
  2.7 0.1 collective-permute-start.2
  2.8 0.4 %collective-permute-start.3 = (f32[1024,128]{1,0:T(8,128)S(1)}, f32[1024,128]{1,0:T(8,128)S(1)}, u32[]{:S(2)}, u32[]{:S(2)}) collective-permute-start(f32[1024,128]{1,0:T(8,128)S(1)} %get-tuple-element.40.refs_0_), channel_id=1, source_target_pairs={{0,1},{1,0},{2,3},{3,2},{4,5},{5,4},{6,7},{7,6},{8,9},{9,8},{10,11... | collective-permute-start | bytes 1572872 | tf_op jit(solution)/shard_map/ppermute | solution.py:100
  3.2 0.4 %collective-permute-done = f32[136,128]{1,0:T(8,128)S(1)} collective-permute-done((f32[136,128]{1,0:T(8,128)S(1)}, f32[136,128]{1,0:T(8,128)S(1)}, u32[]{:S(2)}, u32[]{:S(2)}) %collective-permute-start) | collective-permute-done | bytes 69664 | tf_op jit(solution)/shard_map/ppermute | solution.py:100
  3.7 0.4 %collective-permute-start.1 = (f32[144,128]{1,0:T(8,128)S(1)}, f32[144,128]{1,0:T(8,128)S(1)}, u32[]{:S(2)}, u32[]{:S(2)}) collective-permute-start(f32[144,128]{1,0:T(8,128)S(1)} %pad_maximum_fusion), channel_id=1, source_target_pairs={{0,1},{1,2},{2,3},{3,0},{4,5},{5,6},{6,7},{7,4},{8,11},{9,8},{10,9... | collective-permute-start | bytes 221192 | tf_op jit(solution)/shard_map/ppermute | solution.py:110
  4.1 0.2 shard_map.85
  4.3 4.1 %collective-permute-done.1 = f32[144,128]{1,0:T(8,128)S(1)} collective-permute-done((f32[144,128]{1,0:T(8,128)S(1)}, f32[144,128]{1,0:T(8,128)S(1)}, u32[]{:S(2)}, u32[]{:S(2)}) %collective-permute-start.1) | collective-permute-done | bytes 73760 | tf_op jit(solution)/shard_map/ppermute | solution.py:110
  8.4 0.0 collective-permute-done.2.refs_6_
  8.4 0.0 collective-permute-done.3.refs_7_.refs_1_
  8.4 0.7 %shard_map.86 = (f32[128,128]{1,0:T(8,128)S(1)}, f32[16,128]{1,0:T(8,128)S(1)}, f32[88,128]{1,0:T(8,128)S(1)}) custom-call(f32[128,128]{1,0:T(8,128)S(1)} %slice_add_fusion.refs_0_, f32[32,128]{1,0:T(8,128)S(1)} %pad_maximum_fusion.1.refs_1_, f32[128,128]{1,0:T(8,128)S(1)} %get-tuple-element.35.refs_2_, f32[1,128]{1,0:T(1,128)S(1)} %get-tuple-element.36.w.refs_3_.refs_2_, ...), custom_call_target="tpu_custom_call" | custom-call | flops 50331648 | bytes 65536 | tf_op jit(solution)/shard_map/pallas_call | solution.py:63
  9.2 2.2 %collective-permute-start.7 = (f32[88,128]{1,0:T(8,128)S(1)}, f32[88,128]{1,0:T(8,128)S(1)}, u32[]{:S(2)}, u32[]{:S(2)}) collective-permute-start(f32[88,128]{1,0:T(8,128)S(1)} %get-tuple-element.41), channel_id=1, source_target_pairs={{0,21},{1,0},{2,23},{3,2},{4,17},{5,4},{6,19},{7,6},{8,9},{9,28},{... | collective-permute-start | bytes 135176 | tf_op jit(solution)/shard_map/ppermute | solution.py:110
  11.4 1.0 %collective-permute-start.6 = (f32[88,128]{1,0:T(8,128)S(1)}, f32[88,128]{1,0:T(8,128)S(1)}, u32[]{:S(2)}, u32[]{:S(2)}) collective-permute-start(f32[88,128]{1,0:T(8,128)S(1)} %get-tuple-element.41), channel_id=1, source_target_pairs={{0,17},{1,0},{2,19},{3,2},{4,21},{5,4},{6,23},{7,6},{8,9},{9,24},{... | collective-permute-start | bytes 135176 | tf_op jit(solution)/shard_map/ppermute | solution.py:110
  12.4 0.0 collective-permute-start.5
  12.4 0.5 %collective-permute-start.4 = (f32[88,128]{1,0:T(8,128)S(1)}, f32[88,128]{1,0:T(8,128)S(1)}, u32[]{:S(2)}, u32[]{:S(2)}) collective-permute-start(f32[88,128]{1,0:T(8,128)S(1)} %get-tuple-element.41), channel_id=1, source_target_pairs={{0,1},{1,0},{2,3},{3,2},{4,5},{5,4},{6,7},{7,6},{8,9},{9,8},{10,11... | collective-permute-start | bytes 135176 | tf_op jit(solution)/shard_map/ppermute | solution.py:100
  12.9 0.0 collective-permute-start.10
  12.9 0.2 collective-permute-done.7
  13.1 1.0 %collective-permute-done.6 = f32[88,128]{1,0:T(8,128)S(1)} collective-permute-done((f32[88,128]{1,0:T(8,128)S(1)}, f32[88,128]{1,0:T(8,128)S(1)}, u32[]{:S(2)}, u32[]{:S(2)}) %collective-permute-start.6) | collective-permute-done | bytes 45088 | tf_op jit(solution)/shard_map/ppermute | solution.py:110
  14.1 0.0 collective-permute-done.4
  14.1 1.7 %collective-permute-start.9 = (f32[88,128]{1,0:T(8,128)S(1)}, f32[88,128]{1,0:T(8,128)S(1)}, u32[]{:S(2)}, u32[]{:S(2)}) collective-permute-start(f32[88,128]{1,0:T(8,128)S(1)} %add_add_fusion.1), channel_id=1, source_target_pairs={{0,1},{1,9},{2,3},{3,11},{4,5},{5,13},{6,7},{7,15},{8,0},{9,8},{10... | collective-permute-start | bytes 135176 | tf_op jit(solution)/shard_map/ppermute | solution.py:110
  15.8 0.1 collective-permute-start.8
  15.9 0.5 %shard_map.87.refs_4_ = f32[16,128,128]{2,1,0:T(8,128)S(1)} custom-call(f32[1024,128]{1,0:T(8,128)S(1)} %get-tuple-element.40.refs_0_, f32[1024,128]{1,0:T(8,128)S(1)} %collective-permute-done.3.refs_7_.refs_1_, f32[128,128]{1,0:T(8,128)S(1)} %get-tuple-element.43.refs_2_.moved, f32[128,128]{1,0:T(8,128)S(1)} %collective-permute-done.10.refs_3_.mate_moved), custom_call_target="tpu_custom_call" | custom-call | flops 402653184 | bytes 65536 | tf_op jit(solution)/shard_map/pallas_call | solution.py:63
  16.4 2.9 %collective-permute-done.9 = f32[88,128]{1,0:T(8,128)S(1)} collective-permute-done((f32[88,128]{1,0:T(8,128)S(1)}, f32[88,128]{1,0:T(8,128)S(1)}, u32[]{:S(2)}, u32[]{:S(2)}) %collective-permute-start.9) | collective-permute-done | bytes 45088 | tf_op jit(solution)/shard_map/ppermute | solution.py:110
  19.2 0.0 collective-permute-done.8
  19.2 0.4 %shard_map.88 = (f32[128,128]{1,0:T(8,128)S(1)}, f32[144,128]{1,0:T(8,128)S(1)}) custom-call(f32[88,128]{1,0:T(8,128)S(1)} %add.32.refs_0_, f32[16,128]{1,0:T(8,128)S(1)} %get-tuple-element.42.refs_1_, f32[1,128]{1,0:T(1,128)S(1)} %get-tuple-element.36.w.refs_3_.refs_2_, f32[128,128]{1,0:T(8,128)S(1)} %get-tuple-element.38.refs_4_.refs_3_, ...), custom_call_target="tpu_custom_call" | custom-call | flops 3145728 | bytes 65536 | tf_op jit(solution)/shard_map/pallas_call | solution.py:63
  19.6 0.2 collective-permute-start.14
  19.8 0.0 collective-permute-start.13
  19.8 1.4 %collective-permute-start.12 = (f32[144,128]{1,0:T(8,128)S(1)}, f32[144,128]{1,0:T(8,128)S(1)}, u32[]{:S(2)}, u32[]{:S(2)}) collective-permute-start(f32[144,128]{1,0:T(8,128)S(1)} %get-tuple-element.44), channel_id=1, source_target_pairs={{0,3},{1,0},{2,1},{3,2},{4,7},{5,4},{6,5},{7,6},{8,9},{9,10},{10,1... | collective-permute-start | bytes 221192 | tf_op jit(solution)/shard_map/ppermute | solution.py:110
  21.2 0.0 collective-permute-start.11
  21.2 0.5 %collective-permute-start.20 = (f32[128,128]{1,0:T(8,128)S(1)}, f32[128,128]{1,0:T(8,128)S(1)}, u32[]{:S(2)}, u32[]{:S(2)}) collective-permute-start(f32[128,128]{1,0:T(8,128)S(1)} %get-tuple-element.47.gram), channel_id=1, source_target_pairs={{0,1},{1,0},{2,3},{3,2},{4,5},{5,4},{6,7},{7,6},{8,9},{9,8},{10,11... | collective-permute-start | bytes 196616 | tf_op jit(solution)/shard_map/ppermute | solution.py:100
  21.7 0.1 collective-permute-done.14.refs_3_
  21.8 0.7 %collective-permute-done.13.refs_2_ = f32[144,128]{1,0:T(8,128)S(1)} collective-permute-done((f32[144,128]{1,0:T(8,128)S(1)}, f32[144,128]{1,0:T(8,128)S(1)}, u32[]{:S(2)}, u32[]{:S(2)}) %collective-permute-start.13) | collective-permute-done | bytes 73760 | tf_op jit(solution)/shard_map/ppermute | solution.py:110
  22.5 0.7 %collective-permute-done.12.refs_1_ = f32[144,128]{1,0:T(8,128)S(1)} collective-permute-done((f32[144,128]{1,0:T(8,128)S(1)}, f32[144,128]{1,0:T(8,128)S(1)}, u32[]{:S(2)}, u32[]{:S(2)}) %collective-permute-start.12) | collective-permute-done | bytes 73760 | tf_op jit(solution)/shard_map/ppermute | solution.py:110
  23.2 0.0 collective-permute-done.11.refs_0_
  23.2 1.0 %collective-permute-start.18 = (f32[128,128]{1,0:T(8,128)S(1)}, f32[128,128]{1,0:T(8,128)S(1)}, u32[]{:S(2)}, u32[]{:S(2)}) collective-permute-start(f32[128,128]{1,0:T(8,128)S(1)} %get-tuple-element.45), channel_id=1, source_target_pairs={{0,1},{1,20},{2,3},{3,22},{4,5},{5,16},{6,7},{7,18},{8,29},{9,8},{... | collective-permute-start | bytes 196616 | tf_op jit(solution)/shard_map/ppermute | solution.py:110
  24.2 1.6 %collective-permute-start.17 = (f32[128,128]{1,0:T(8,128)S(1)}, f32[128,128]{1,0:T(8,128)S(1)}, u32[]{:S(2)}, u32[]{:S(2)}) collective-permute-start(f32[128,128]{1,0:T(8,128)S(1)} %get-tuple-element.45), channel_id=1, source_target_pairs={{0,1},{1,16},{2,3},{3,18},{4,5},{5,20},{6,7},{7,22},{8,25},{9,8},{... | collective-permute-start | bytes 196616 | tf_op jit(solution)/shard_map/ppermute | solution.py:110
  25.7 0.6 %collective-permute-start.16 = (f32[128,128]{1,0:T(8,128)S(1)}, f32[128,128]{1,0:T(8,128)S(1)}, u32[]{:S(2)}, u32[]{:S(2)}) collective-permute-start(f32[128,128]{1,0:T(8,128)S(1)} %get-tuple-element.45), channel_id=1, source_target_pairs={{0,1},{1,4},{2,3},{3,6},{4,5},{5,0},{6,7},{7,2},{8,13},{9,8},{10,1... | collective-permute-start | bytes 196616 | tf_op jit(solution)/shard_map/ppermute | solution.py:110
  26.3 0.1 collective-permute-start.15
  26.5 0.0 collective-permute-done.20.mate_gram
  26.5 0.4 %collective-permute-start.19 = (f32[32,128]{1,0:T(8,128)S(1)}, f32[32,128]{1,0:T(8,128)S(1)}, u32[]{:S(2)}, u32[]{:S(2)}) collective-permute-start(f32[32,128]{1,0:T(8,128)S(1)} %get-tuple-element.46.rows), channel_id=1, source_target_pairs={{0,1},{1,0},{2,3},{3,2},{4,5},{5,4},{6,7},{7,6},{8,9},{9,8},{10,11... | collective-permute-start | bytes 49160 | tf_op jit(solution)/shard_map/ppermute | solution.py:100
  26.8 0.7 %shard_map.90 = (f32[128,128]{1,0:T(8,128)}, f32[1,128]{1,0:T(1,128)S(1)}, f32[128,128]{1,0:T(8,128)S(1)}) custom-call(f32[128,128]{1,0:T(8,128)S(1)} %get-tuple-element.47.gram, f32[128,128]{1,0:T(8,128)S(1)} %collective-permute-done.20.mate_gram, f32[128,128]{1,0:T(8,128)S(1)} %get-tuple-element.43.refs_2_.moved, ...), custom_call_target="tpu_custom_call" | custom-call | flops 131072 | bytes 65536 | tf_op jit(solution)/shard_map/pallas_call | solution.py:63
  27.5 0.2 collective-permute-done.19.mate_rows
  27.7 0.9 %shard_map.91 = (f32[8,128]{1,0:T(8,128)}, f32[128,128]{1,0:T(8,128)S(1)}, f32[1,128]{1,0:T(1,128)S(1)}, f32[1,128]{1,0:T(1,128)S(1)}) custom-call(f32[32,128]{1,0:T(8,128)S(1)} %get-tuple-element.46.rows, f32[32,128]{1,0:T(8,128)S(1)} %collective-permute-done.19.mate_rows, f32[128,128]{1,0:T(8,128)S(1)} %get-tuple-element.37.c, ...), custom_call_target="tpu_custom_call" | custom-call | flops 16777216 | bytes 65536 | tf_op jit(solution)/shard_map/pallas_call | solution.py:63
  28.5 0.2 collective-permute-done.18
  28.7 0.7 %collective-permute-done.17 = f32[128,128]{1,0:T(8,128)S(1)} collective-permute-done((f32[128,128]{1,0:T(8,128)S(1)}, f32[128,128]{1,0:T(8,128)S(1)}, u32[]{:S(2)}, u32[]{:S(2)}) %collective-permute-start.17) | collective-permute-done | bytes 65568 | tf_op jit(solution)/shard_map/ppermute | solution.py:110
  29.5 0.1 collective-permute-start.21
  29.6 1.2 %collective-permute-done.21.mate_terms = f32[128,128]{1,0:T(8,128)S(1)} collective-permute-done((f32[128,128]{1,0:T(8,128)S(1)}, f32[128,128]{1,0:T(8,128)S(1)}, u32[]{:S(2)}, u32[]{:S(2)}) %collective-permute-start.21) | collective-permute-done | bytes 65568 | tf_op jit(solution)/shard_map/ppermute | solution.py:100
  30.8 0.7 %shard_map.92 = (f32[128,128]{1,0:T(8,128)}, f32[1,128]{1,0:T(1,128)}) custom-call(f32[128,128]{1,0:T(8,128)S(1)} %add_add_fusion.terms, f32[128,128]{1,0:T(8,128)S(1)} %collective-permute-done.21.mate_terms, f32[128,128]{1,0:T(8,128)S(1)} %get-tuple-element.59.base, f32[1,128]{1,0:T(1,128)S(1)} %get-tuple-element.60.gain, f32[1,128]{1,0:T(1,128)S(1)} %get-tuple-element.61.scale), custom_call_target="tpu_custom_call" | custom-call | flops 131072 | bytes 65536 | tf_op jit(solution)/shard_map/pallas_call | solution.py:63
  (15 shorter events, 0.1 us)
Async XLA Ops:
  2.2 1.4 %collective-permute-start = (f32[136,128]{1,0:T(8,128)S(1)}, f32[136,128]{1,0:T(8,128)S(1)}, u32[]{:S(2)}, u32[]{:S(2)}) collective-permute-start(f32[136,128]{1,0:T(8,128)S(1)} %get-tuple-element.34), channel_id=1, source_target_pairs={{0,1},{1,0},{2,3},{3,2},{4,5},{5,4},{6,7},{7,6},{8,9},{9,8},{10,11... | collective-permute-start | bytes 208904 | tf_op jit(solution)/shard_map/ppermute | solution.py:100
  2.7 5.7 %collective-permute-start.2 = (f32[8,128,128]{2,1,0:T(8,128)S(1)}, f32[8,128,128]{2,1,0:T(8,128)S(1)}, u32[]{:S(2)}, u32[]{:S(2)}) collective-permute-start(f32[8,128,128]{2,1,0:T(8,128)S(1)} %get-tuple-element.39.refs_5_), channel_id=1, source_target_pairs={{0,1},{1,0},{2,3},{3,2},{4,5},{5,4},{6,7},{7,6},{8,9},{9,8},{10,11... | collective-permute-start | bytes 1572872 | tf_op jit(solution)/shard_map/ppermute | solution.py:100
  2.8 5.6 %collective-permute-start.3 = (f32[1024,128]{1,0:T(8,128)S(1)}, f32[1024,128]{1,0:T(8,128)S(1)}, u32[]{:S(2)}, u32[]{:S(2)}) collective-permute-start(f32[1024,128]{1,0:T(8,128)S(1)} %get-tuple-element.40.refs_0_), channel_id=1, source_target_pairs={{0,1},{1,0},{2,3},{3,2},{4,5},{5,4},{6,7},{7,6},{8,9},{9,8},{10,11... | collective-permute-start | bytes 1572872 | tf_op jit(solution)/shard_map/ppermute | solution.py:100
  3.7 4.7 %collective-permute-start.1 = (f32[144,128]{1,0:T(8,128)S(1)}, f32[144,128]{1,0:T(8,128)S(1)}, u32[]{:S(2)}, u32[]{:S(2)}) collective-permute-start(f32[144,128]{1,0:T(8,128)S(1)} %pad_maximum_fusion), channel_id=1, source_target_pairs={{0,1},{1,2},{2,3},{3,0},{4,5},{5,6},{6,7},{7,4},{8,11},{9,8},{10,9... | collective-permute-start | bytes 221192 | tf_op jit(solution)/shard_map/ppermute | solution.py:110
  9.2 3.9 %collective-permute-start.7 = (f32[88,128]{1,0:T(8,128)S(1)}, f32[88,128]{1,0:T(8,128)S(1)}, u32[]{:S(2)}, u32[]{:S(2)}) collective-permute-start(f32[88,128]{1,0:T(8,128)S(1)} %get-tuple-element.41), channel_id=1, source_target_pairs={{0,21},{1,0},{2,23},{3,2},{4,17},{5,4},{6,19},{7,6},{8,9},{9,28},{... | collective-permute-start | bytes 135176 | tf_op jit(solution)/shard_map/ppermute | solution.py:110
  11.4 2.7 %collective-permute-start.6 = (f32[88,128]{1,0:T(8,128)S(1)}, f32[88,128]{1,0:T(8,128)S(1)}, u32[]{:S(2)}, u32[]{:S(2)}) collective-permute-start(f32[88,128]{1,0:T(8,128)S(1)} %get-tuple-element.41), channel_id=1, source_target_pairs={{0,17},{1,0},{2,19},{3,2},{4,21},{5,4},{6,23},{7,6},{8,9},{9,24},{... | collective-permute-start | bytes 135176 | tf_op jit(solution)/shard_map/ppermute | solution.py:110
  12.4 1.7 %collective-permute-start.5 = (f32[88,128]{1,0:T(8,128)S(1)}, f32[88,128]{1,0:T(8,128)S(1)}, u32[]{:S(2)}, u32[]{:S(2)}) collective-permute-start(f32[88,128]{1,0:T(8,128)S(1)} %get-tuple-element.41), channel_id=1, source_target_pairs={{0,5},{1,0},{2,7},{3,2},{4,1},{5,4},{6,3},{7,6},{8,9},{9,12},{10,1... | collective-permute-start | bytes 135176 | tf_op jit(solution)/shard_map/ppermute | solution.py:110
  12.4 1.7 %collective-permute-start.4 = (f32[88,128]{1,0:T(8,128)S(1)}, f32[88,128]{1,0:T(8,128)S(1)}, u32[]{:S(2)}, u32[]{:S(2)}) collective-permute-start(f32[88,128]{1,0:T(8,128)S(1)} %get-tuple-element.41), channel_id=1, source_target_pairs={{0,1},{1,0},{2,3},{3,2},{4,5},{5,4},{6,7},{7,6},{8,9},{9,8},{10,11... | collective-permute-start | bytes 135176 | tf_op jit(solution)/shard_map/ppermute | solution.py:100
  12.9 3.0 %collective-permute-start.10 = (f32[128,128]{1,0:T(8,128)S(1)}, f32[128,128]{1,0:T(8,128)S(1)}, u32[]{:S(2)}, u32[]{:S(2)}) collective-permute-start(f32[128,128]{1,0:T(8,128)S(1)} %get-tuple-element.43.refs_2_.moved), channel_id=1, source_target_pairs={{0,1},{1,0},{2,3},{3,2},{4,5},{5,4},{6,7},{7,6},{8,9},{9,8},{10,11... | collective-permute-start | bytes 196616 | tf_op jit(solution)/shard_map/ppermute | solution.py:100
  14.1 5.1 %collective-permute-start.9 = (f32[88,128]{1,0:T(8,128)S(1)}, f32[88,128]{1,0:T(8,128)S(1)}, u32[]{:S(2)}, u32[]{:S(2)}) collective-permute-start(f32[88,128]{1,0:T(8,128)S(1)} %add_add_fusion.1), channel_id=1, source_target_pairs={{0,1},{1,9},{2,3},{3,11},{4,5},{5,13},{6,7},{7,15},{8,0},{9,8},{10... | collective-permute-start | bytes 135176 | tf_op jit(solution)/shard_map/ppermute | solution.py:110
  15.8 3.4 %collective-permute-start.8 = (f32[88,128]{1,0:T(8,128)S(1)}, f32[88,128]{1,0:T(8,128)S(1)}, u32[]{:S(2)}, u32[]{:S(2)}) collective-permute-start(f32[88,128]{1,0:T(8,128)S(1)} %add_add_fusion.1), channel_id=1, source_target_pairs={{0,1},{1,0},{2,3},{3,2},{4,5},{5,4},{6,7},{7,6},{8,9},{9,8},{10,11... | collective-permute-start | bytes 135176 | tf_op jit(solution)/shard_map/ppermute | solution.py:100
  19.6 2.2 %collective-permute-start.14 = (f32[144,128]{1,0:T(8,128)S(1)}, f32[144,128]{1,0:T(8,128)S(1)}, u32[]{:S(2)}, u32[]{:S(2)}) collective-permute-start(f32[144,128]{1,0:T(8,128)S(1)} %get-tuple-element.44), channel_id=1, source_target_pairs={{0,10},{1,0},{2,8},{3,2},{4,14},{5,4},{6,12},{7,6},{8,9},{9,3},{10... | collective-permute-start | bytes 221192 | tf_op jit(solution)/shard_map/ppermute | solution.py:110
  19.8 2.7 %collective-permute-start.13 = (f32[144,128]{1,0:T(8,128)S(1)}, f32[144,128]{1,0:T(8,128)S(1)}, u32[]{:S(2)}, u32[]{:S(2)}) collective-permute-start(f32[144,128]{1,0:T(8,128)S(1)} %get-tuple-element.44), channel_id=1, source_target_pairs={{0,8},{1,0},{2,10},{3,2},{4,12},{5,4},{6,14},{7,6},{8,9},{9,1},{10... | collective-permute-start | bytes 221192 | tf_op jit(solution)/shard_map/ppermute | solution.py:110
  19.8 3.4 %collective-permute-start.12 = (f32[144,128]{1,0:T(8,128)S(1)}, f32[144,128]{1,0:T(8,128)S(1)}, u32[]{:S(2)}, u32[]{:S(2)}) collective-permute-start(f32[144,128]{1,0:T(8,128)S(1)} %get-tuple-element.44), channel_id=1, source_target_pairs={{0,3},{1,0},{2,1},{3,2},{4,7},{5,4},{6,5},{7,6},{8,9},{9,10},{10,1... | collective-permute-start | bytes 221192 | tf_op jit(solution)/shard_map/ppermute | solution.py:110
  21.2 2.0 %collective-permute-start.11 = (f32[144,128]{1,0:T(8,128)S(1)}, f32[144,128]{1,0:T(8,128)S(1)}, u32[]{:S(2)}, u32[]{:S(2)}) collective-permute-start(f32[144,128]{1,0:T(8,128)S(1)} %get-tuple-element.44), channel_id=1, source_target_pairs={{0,1},{1,0},{2,3},{3,2},{4,5},{5,4},{6,7},{7,6},{8,9},{9,8},{10,11... | collective-permute-start | bytes 221192 | tf_op jit(solution)/shard_map/ppermute | solution.py:100
  21.2 5.3 %collective-permute-start.20 = (f32[128,128]{1,0:T(8,128)S(1)}, f32[128,128]{1,0:T(8,128)S(1)}, u32[]{:S(2)}, u32[]{:S(2)}) collective-permute-start(f32[128,128]{1,0:T(8,128)S(1)} %get-tuple-element.47.gram), channel_id=1, source_target_pairs={{0,1},{1,0},{2,3},{3,2},{4,5},{5,4},{6,7},{7,6},{8,9},{9,8},{10,11... | collective-permute-start | bytes 196616 | tf_op jit(solution)/shard_map/ppermute | solution.py:100
  23.2 5.5 %collective-permute-start.18 = (f32[128,128]{1,0:T(8,128)S(1)}, f32[128,128]{1,0:T(8,128)S(1)}, u32[]{:S(2)}, u32[]{:S(2)}) collective-permute-start(f32[128,128]{1,0:T(8,128)S(1)} %get-tuple-element.45), channel_id=1, source_target_pairs={{0,1},{1,20},{2,3},{3,22},{4,5},{5,16},{6,7},{7,18},{8,29},{9,8},{... | collective-permute-start | bytes 196616 | tf_op jit(solution)/shard_map/ppermute | solution.py:110
  24.2 5.3 %collective-permute-start.17 = (f32[128,128]{1,0:T(8,128)S(1)}, f32[128,128]{1,0:T(8,128)S(1)}, u32[]{:S(2)}, u32[]{:S(2)}) collective-permute-start(f32[128,128]{1,0:T(8,128)S(1)} %get-tuple-element.45), channel_id=1, source_target_pairs={{0,1},{1,16},{2,3},{3,18},{4,5},{5,20},{6,7},{7,22},{8,25},{9,8},{... | collective-permute-start | bytes 196616 | tf_op jit(solution)/shard_map/ppermute | solution.py:110
  25.7 3.7 %collective-permute-start.16 = (f32[128,128]{1,0:T(8,128)S(1)}, f32[128,128]{1,0:T(8,128)S(1)}, u32[]{:S(2)}, u32[]{:S(2)}) collective-permute-start(f32[128,128]{1,0:T(8,128)S(1)} %get-tuple-element.45), channel_id=1, source_target_pairs={{0,1},{1,4},{2,3},{3,6},{4,5},{5,0},{6,7},{7,2},{8,13},{9,8},{10,1... | collective-permute-start | bytes 196616 | tf_op jit(solution)/shard_map/ppermute | solution.py:110
  26.3 3.1 %collective-permute-start.15 = (f32[128,128]{1,0:T(8,128)S(1)}, f32[128,128]{1,0:T(8,128)S(1)}, u32[]{:S(2)}, u32[]{:S(2)}) collective-permute-start(f32[128,128]{1,0:T(8,128)S(1)} %get-tuple-element.45), channel_id=1, source_target_pairs={{0,1},{1,0},{2,3},{3,2},{4,5},{5,4},{6,7},{7,6},{8,9},{9,8},{10,11... | collective-permute-start | bytes 196616 | tf_op jit(solution)/shard_map/ppermute | solution.py:100
  26.5 1.2 %collective-permute-start.19 = (f32[32,128]{1,0:T(8,128)S(1)}, f32[32,128]{1,0:T(8,128)S(1)}, u32[]{:S(2)}, u32[]{:S(2)}) collective-permute-start(f32[32,128]{1,0:T(8,128)S(1)} %get-tuple-element.46.rows), channel_id=1, source_target_pairs={{0,1},{1,0},{2,3},{3,2},{4,5},{5,4},{6,7},{7,6},{8,9},{9,8},{10,11... | collective-permute-start | bytes 49160 | tf_op jit(solution)/shard_map/ppermute | solution.py:100
  29.5 1.3 %collective-permute-start.21 = (f32[128,128]{1,0:T(8,128)S(1)}, f32[128,128]{1,0:T(8,128)S(1)}, u32[]{:S(2)}, u32[]{:S(2)}) collective-permute-start(f32[128,128]{1,0:T(8,128)S(1)} %add_add_fusion.terms), channel_id=1, source_target_pairs={{0,1},{1,0},{2,3},{3,2},{4,5},{5,4},{6,7},{7,6},{8,9},{9,8},{10,11... | collective-permute-start | bytes 196616 | tf_op jit(solution)/shard_map/ppermute | solution.py:100

commit v20 on v19

--- a/solution.py
+++ b/solution.py
@@ -326,7 +326,7 @@
 
     terms, rows_b, rows_role = payload[:times], payload[times:], holder
     smp_mask = sum(chip_bits)
-    for group in groups_of(chip_bits + vox_bits[1:2] + vox_bits[:1] + vox_bits[2:]):
+    for group in groups_of(chip_bits + vox_bits[-1:] + vox_bits[:-1]):
         masks = masks_of(group)
         if any(mask & smp_mask for mask in masks):
             packet = payload if rows_b.shape[0] == chip_rows else jnp.concatenate([terms, rows_b], axis=0)

time: 31.6 us -> 32.6 us (1.032)
  waiting for transfers between devices: 12.3 us -> 13.1 us
    ppermute x11, waiting for transfers between devices: 10.5 us -> 11 us  [send(): return lax.ppermute(values, ALL, pairs)]
    ppermute x11, waiting for transfers between devices: 1.81 us -> 2.15 us  [swap(): lax.ppermute(values, ALL, [(i, i ^ 1) for i in range(lax.axis_size(ALL))])]
  transfers between devices with their start and end apart: 22 -> 22, of which waited for: 12 -> 9; matrix products, arithmetic and copies ran while one was open for 0% -> 0% of each run, Pallas kernels for 7% -> 7%
where the time goes in v20:
time: 32.6 us; the launch traced here: 32.5 us
  waiting for transfers between devices  13.1 us (40%)
  starting transfers between devices  12.9 us (40%)
  Pallas kernels  5.64 us (17%)
  between operations  0.75 us (2%)
    ppermute x11, waiting for transfers between devices, send(): return lax.ppermute(values, ALL, pairs)  11 us
    ppermute x11, starting transfers between devices, send(): return lax.ppermute(values, ALL, pairs)  9.99 us
    pallas_call x9, Pallas kernels, call(): pl.pallas_call(kernel, out_shape=outs, in_specs=specs, out_specs=[pl.Bloc...  5.64 us
    ppermute x11, starting transfers between devices, swap(): lax.ppermute(values, ALL, [(i, i ^ 1) for i in range(lax.axis_size(ALL))])  2.93 us
    ppermute x11, waiting for transfers between devices, swap(): lax.ppermute(values, ALL, [(i, i ^ 1) for i in range(lax.axis_size(ALL))])  2.15 us
  transfers between devices with their start and end apart: 22, of which 9 were waited for; matrix products, arithmetic and copies ran while one was open for 0% of the time, Pallas kernels for 7%

profile of v20, /device:TPU:0, one launch (start us, length us, event | category | flops | bytes accessed | tf_op | source)
XLA Modules:
  0.0 32.5 jit_solution(11346077535283509156)
XLA Ops:
  0.6 1.6 %shard_map.84 = (f32[1024,128]{1,0:T(8,128)S(1)}, f32[128,128]{1,0:T(8,128)S(1)}, f32[128,128]{1,0:T(8,128)S(1)}, f32[1,128]{1,0:T(1,128)S(1)}, f32[136,128]{1,0:T(8,128)S(1)}, /*index=5*/f32[8,128,128]{2,1,0:T(8,128)S(1)}) custom-call(f32[1024,128]{1,0:T(8,128)} %bitcast.3, f32[128,128]{1,0:T(8,128)} %c_hbm.1, f32[8,128]{1,0:T(8,128)} %b_hbm.1, ...), custom_call_target="tpu_custom_call" | custom-call | flops 201326592 | bytes 65536 | tf_op jit(solution)/shard_map/pallas_call | solution.py:63
  2.2 0.5 %collective-permute-start = (f32[136,128]{1,0:T(8,128)S(1)}, f32[136,128]{1,0:T(8,128)S(1)}, u32[]{:S(2)}, u32[]{:S(2)}) collective-permute-start(f32[136,128]{1,0:T(8,128)S(1)} %get-tuple-element.34), channel_id=1, source_target_pairs={{0,1},{1,0},{2,3},{3,2},{4,5},{5,4},{6,7},{7,6},{8,9},{9,8},{10,11... | collective-permute-start | bytes 208904 | tf_op jit(solution)/shard_map/ppermute | solution.py:100
  2.7 0.1 collective-permute-start.2
  2.8 0.4 %collective-permute-start.3 = (f32[1024,128]{1,0:T(8,128)S(1)}, f32[1024,128]{1,0:T(8,128)S(1)}, u32[]{:S(2)}, u32[]{:S(2)}) collective-permute-start(f32[1024,128]{1,0:T(8,128)S(1)} %get-tuple-element.40.refs_0_), channel_id=1, source_target_pairs={{0,1},{1,0},{2,3},{3,2},{4,5},{5,4},{6,7},{7,6},{8,9},{9,8},{10,11... | collective-permute-start | bytes 1572872 | tf_op jit(solution)/shard_map/ppermute | solution.py:100
  3.2 0.4 %collective-permute-done = f32[136,128]{1,0:T(8,128)S(1)} collective-permute-done((f32[136,128]{1,0:T(8,128)S(1)}, f32[136,128]{1,0:T(8,128)S(1)}, u32[]{:S(2)}, u32[]{:S(2)}) %collective-permute-start) | collective-permute-done | bytes 69664 | tf_op jit(solution)/shard_map/ppermute | solution.py:100
  3.7 0.4 %collective-permute-start.1 = (f32[144,128]{1,0:T(8,128)S(1)}, f32[144,128]{1,0:T(8,128)S(1)}, u32[]{:S(2)}, u32[]{:S(2)}) collective-permute-start(f32[144,128]{1,0:T(8,128)S(1)} %pad_maximum_fusion), channel_id=1, source_target_pairs={{0,1},{1,2},{2,3},{3,0},{4,5},{5,6},{6,7},{7,4},{8,11},{9,8},{10,9... | collective-permute-start | bytes 221192 | tf_op jit(solution)/shard_map/ppermute | solution.py:110
  4.1 0.2 shard_map.85
  4.3 4.1 %collective-permute-done.1 = f32[144,128]{1,0:T(8,128)S(1)} collective-permute-done((f32[144,128]{1,0:T(8,128)S(1)}, f32[144,128]{1,0:T(8,128)S(1)}, u32[]{:S(2)}, u32[]{:S(2)}) %collective-permute-start.1) | collective-permute-done | bytes 73760 | tf_op jit(solution)/shard_map/ppermute | solution.py:110
  8.4 0.0 collective-permute-done.2.refs_6_
  8.4 0.0 collective-permute-done.3.refs_7_.refs_1_
  8.4 0.7 %shard_map.86 = (f32[128,128]{1,0:T(8,128)S(1)}, f32[16,128]{1,0:T(8,128)S(1)}, f32[88,128]{1,0:T(8,128)S(1)}) custom-call(f32[128,128]{1,0:T(8,128)S(1)} %slice_add_fusion.refs_0_, f32[32,128]{1,0:T(8,128)S(1)} %pad_maximum_fusion.1.refs_1_, f32[128,128]{1,0:T(8,128)S(1)} %get-tuple-element.35.refs_2_, f32[1,128]{1,0:T(1,128)S(1)} %get-tuple-element.36.w.refs_3_.refs_2_, ...), custom_call_target="tpu_custom_call" | custom-call | flops 50331648 | bytes 65536 | tf_op jit(solution)/shard_map/pallas_call | solution.py:63
  9.2 2.2 %collective-permute-start.7 = (f32[88,128]{1,0:T(8,128)S(1)}, f32[88,128]{1,0:T(8,128)S(1)}, u32[]{:S(2)}, u32[]{:S(2)}) collective-permute-start(f32[88,128]{1,0:T(8,128)S(1)} %get-tuple-element.41), channel_id=1, source_target_pairs={{0,21},{1,0},{2,23},{3,2},{4,17},{5,4},{6,19},{7,6},{8,9},{9,28},{... | collective-permute-start | bytes 135176 | tf_op jit(solution)/shard_map/ppermute | solution.py:110
  11.4 1.0 %collective-permute-start.6 = (f32[88,128]{1,0:T(8,128)S(1)}, f32[88,128]{1,0:T(8,128)S(1)}, u32[]{:S(2)}, u32[]{:S(2)}) collective-permute-start(f32[88,128]{1,0:T(8,128)S(1)} %get-tuple-element.41), channel_id=1, source_target_pairs={{0,17},{1,0},{2,19},{3,2},{4,21},{5,4},{6,23},{7,6},{8,9},{9,24},{... | collective-permute-start | bytes 135176 | tf_op jit(solution)/shard_map/ppermute | solution.py:110
  12.4 0.0 collective-permute-start.5
  12.4 0.5 %collective-permute-start.4 = (f32[88,128]{1,0:T(8,128)S(1)}, f32[88,128]{1,0:T(8,128)S(1)}, u32[]{:S(2)}, u32[]{:S(2)}) collective-permute-start(f32[88,128]{1,0:T(8,128)S(1)} %get-tuple-element.41), channel_id=1, source_target_pairs={{0,1},{1,0},{2,3},{3,2},{4,5},{5,4},{6,7},{7,6},{8,9},{9,8},{10,11... | collective-permute-start | bytes 135176 | tf_op jit(solution)/shard_map/ppermute | solution.py:100
  12.9 0.0 collective-permute-start.10
  12.9 0.2 collective-permute-done.7
  13.1 1.0 %collective-permute-done.6 = f32[88,128]{1,0:T(8,128)S(1)} collective-permute-done((f32[88,128]{1,0:T(8,128)S(1)}, f32[88,128]{1,0:T(8,128)S(1)}, u32[]{:S(2)}, u32[]{:S(2)}) %collective-permute-start.6) | collective-permute-done | bytes 45088 | tf_op jit(solution)/shard_map/ppermute | solution.py:110
  14.1 0.0 collective-permute-done.5
  14.1 0.0 collective-permute-done.4
  14.1 1.7 %collective-permute-start.9 = (f32[88,128]{1,0:T(8,128)S(1)}, f32[88,128]{1,0:T(8,128)S(1)}, u32[]{:S(2)}, u32[]{:S(2)}) collective-permute-start(f32[88,128]{1,0:T(8,128)S(1)} %add_add_fusion.1), channel_id=1, source_target_pairs={{0,1},{1,9},{2,3},{3,11},{4,5},{5,13},{6,7},{7,15},{8,0},{9,8},{10... | collective-permute-start | bytes 135176 | tf_op jit(solution)/shard_map/ppermute | solution.py:110
  15.8 0.1 collective-permute-start.8
  15.9 0.0 collective-permute-done.10.refs_3_.mate_moved
  15.9 0.5 %shard_map.87.refs_4_ = f32[16,128,128]{2,1,0:T(8,128)S(1)} custom-call(f32[1024,128]{1,0:T(8,128)S(1)} %get-tuple-element.40.refs_0_, f32[1024,128]{1,0:T(8,128)S(1)} %collective-permute-done.3.refs_7_.refs_1_, f32[128,128]{1,0:T(8,128)S(1)} %get-tuple-element.43.refs_2_.moved, f32[128,128]{1,0:T(8,128)S(1)} %collective-permute-done.10.refs_3_.mate_moved), custom_call_target="tpu_custom_call" | custom-call | flops 402653184 | bytes 65536 | tf_op jit(solution)/shard_map/pallas_call | solution.py:63
  16.4 2.9 %collective-permute-done.9 = f32[88,128]{1,0:T(8,128)S(1)} collective-permute-done((f32[88,128]{1,0:T(8,128)S(1)}, f32[88,128]{1,0:T(8,128)S(1)}, u32[]{:S(2)}, u32[]{:S(2)}) %collective-permute-start.9) | collective-permute-done | bytes 45088 | tf_op jit(solution)/shard_map/ppermute | solution.py:110
  19.2 0.0 collective-permute-done.8
  19.2 0.4 %shard_map.88 = (f32[128,128]{1,0:T(8,128)S(1)}, f32[144,128]{1,0:T(8,128)S(1)}) custom-call(f32[88,128]{1,0:T(8,128)S(1)} %add.32.refs_0_, f32[16,128]{1,0:T(8,128)S(1)} %get-tuple-element.42.refs_1_, f32[1,128]{1,0:T(1,128)S(1)} %get-tuple-element.36.w.refs_3_.refs_2_, f32[128,128]{1,0:T(8,128)S(1)} %get-tuple-element.38.refs_4_.refs_3_, ...), custom_call_target="tpu_custom_call" | custom-call | flops 3145728 | bytes 65536 | tf_op jit(solution)/shard_map/pallas_call | solution.py:63
  19.6 0.1 collective-permute-start.14
  19.7 2.2 %collective-permute-start.13 = (f32[144,128]{1,0:T(8,128)S(1)}, f32[144,128]{1,0:T(8,128)S(1)}, u32[]{:S(2)}, u32[]{:S(2)}) collective-permute-start(f32[144,128]{1,0:T(8,128)S(1)} %get-tuple-element.44), channel_id=1, source_target_pairs={{0,17},{1,0},{2,19},{3,2},{4,21},{5,4},{6,23},{7,6},{8,9},{9,24},{... | collective-permute-start | bytes 221192 | tf_op jit(solution)/shard_map/ppermute | solution.py:110
  21.9 0.0 collective-permute-start.12
  21.9 0.5 %collective-permute-start.11 = (f32[144,128]{1,0:T(8,128)S(1)}, f32[144,128]{1,0:T(8,128)S(1)}, u32[]{:S(2)}, u32[]{:S(2)}) collective-permute-start(f32[144,128]{1,0:T(8,128)S(1)} %get-tuple-element.44), channel_id=1, source_target_pairs={{0,1},{1,0},{2,3},{3,2},{4,5},{5,4},{6,7},{7,6},{8,9},{9,8},{10,11... | collective-permute-start | bytes 221192 | tf_op jit(solution)/shard_map/ppermute | solution.py:100
  22.4 0.0 collective-permute-start.20
  22.4 0.0 collective-permute-done.14.refs_3_
  22.4 1.5 %collective-permute-done.13.refs_2_ = f32[144,128]{1,0:T(8,128)S(1)} collective-permute-done((f32[144,128]{1,0:T(8,128)S(1)}, f32[144,128]{1,0:T(8,128)S(1)}, u32[]{:S(2)}, u32[]{:S(2)}) %collective-permute-start.13) | collective-permute-done | bytes 73760 | tf_op jit(solution)/shard_map/ppermute | solution.py:110
  23.8 0.0 collective-permute-done.12.refs_1_
  23.9 2.3 %collective-permute-start.18 = (f32[128,128]{1,0:T(8,128)S(1)}, f32[128,128]{1,0:T(8,128)S(1)}, u32[]{:S(2)}, u32[]{:S(2)}) collective-permute-start(f32[128,128]{1,0:T(8,128)S(1)} %get-tuple-element.45), channel_id=1, source_target_pairs={{0,1},{1,13},{2,3},{3,15},{4,5},{5,9},{6,7},{7,11},{8,4},{9,8},{10... | collective-permute-start | bytes 196616 | tf_op jit(solution)/shard_map/ppermute | solution.py:110
  26.2 0.1 collective-permute-start.17
  26.3 0.1 collective-permute-start.16
  26.3 0.7 %collective-permute-start.15 = (f32[128,128]{1,0:T(8,128)S(1)}, f32[128,128]{1,0:T(8,128)S(1)}, u32[]{:S(2)}, u32[]{:S(2)}) collective-permute-start(f32[128,128]{1,0:T(8,128)S(1)} %get-tuple-element.45), channel_id=1, source_target_pairs={{0,1},{1,0},{2,3},{3,2},{4,5},{5,4},{6,7},{7,6},{8,9},{9,8},{10,11... | collective-permute-start | bytes 196616 | tf_op jit(solution)/shard_map/ppermute | solution.py:100
  27.1 0.0 collective-permute-done.20.mate_gram
  27.1 0.0 collective-permute-start.19
  27.1 0.7 %shard_map.90 = (f32[128,128]{1,0:T(8,128)}, f32[1,128]{1,0:T(1,128)S(1)}, f32[128,128]{1,0:T(8,128)S(1)}) custom-call(f32[128,128]{1,0:T(8,128)S(1)} %get-tuple-element.47.gram, f32[128,128]{1,0:T(8,128)S(1)} %collective-permute-done.20.mate_gram, f32[128,128]{1,0:T(8,128)S(1)} %get-tuple-element.43.refs_2_.moved, ...), custom_call_target="tpu_custom_call" | custom-call | flops 131072 | bytes 65536 | tf_op jit(solution)/shard_map/pallas_call | solution.py:63
  27.7 0.5 %collective-permute-done.19.mate_rows = f32[32,128]{1,0:T(8,128)S(1)} collective-permute-done((f32[32,128]{1,0:T(8,128)S(1)}, f32[32,128]{1,0:T(8,128)S(1)}, u32[]{:S(2)}, u32[]{:S(2)}) %collective-permute-start.19) | collective-permute-done | bytes 16416 | tf_op jit(solution)/shard_map/ppermute | solution.py:100
  28.2 0.9 %shard_map.91 = (f32[8,128]{1,0:T(8,128)}, f32[128,128]{1,0:T(8,128)S(1)}, f32[1,128]{1,0:T(1,128)S(1)}, f32[1,128]{1,0:T(1,128)S(1)}) custom-call(f32[32,128]{1,0:T(8,128)S(1)} %get-tuple-element.46.rows, f32[32,128]{1,0:T(8,128)S(1)} %collective-permute-done.19.mate_rows, f32[128,128]{1,0:T(8,128)S(1)} %get-tuple-element.37.c, ...), custom_call_target="tpu_custom_call" | custom-call | flops 16777216 | bytes 65536 | tf_op jit(solution)/shard_map/pallas_call | solution.py:63
  29.1 1.3 %collective-permute-done.17 = f32[128,128]{1,0:T(8,128)S(1)} collective-permute-done((f32[128,128]{1,0:T(8,128)S(1)}, f32[128,128]{1,0:T(8,128)S(1)}, u32[]{:S(2)}, u32[]{:S(2)}) %collective-permute-start.17) | collective-permute-done | bytes 65568 | tf_op jit(solution)/shard_map/ppermute | solution.py:110
  30.5 0.1 collective-permute-start.21
  30.6 1.2 %collective-permute-done.21.mate_terms = f32[128,128]{1,0:T(8,128)S(1)} collective-permute-done((f32[128,128]{1,0:T(8,128)S(1)}, f32[128,128]{1,0:T(8,128)S(1)}, u32[]{:S(2)}, u32[]{:S(2)}) %collective-permute-start.21) | collective-permute-done | bytes 65568 | tf_op jit(solution)/shard_map/ppermute | solution.py:100
  31.8 0.7 %shard_map.92 = (f32[128,128]{1,0:T(8,128)}, f32[1,128]{1,0:T(1,128)}) custom-call(f32[128,128]{1,0:T(8,128)S(1)} %add_add_fusion.terms, f32[128,128]{1,0:T(8,128)S(1)} %collective-permute-done.21.mate_terms, f32[128,128]{1,0:T(8,128)S(1)} %get-tuple-element.59.base, f32[1,128]{1,0:T(1,128)S(1)} %get-tuple-element.60.gain, f32[1,128]{1,0:T(1,128)S(1)} %get-tuple-element.61.scale), custom_call_target="tpu_custom_call" | custom-call | flops 131072 | bytes 65536 | tf_op jit(solution)/shard_map/pallas_call | solution.py:63
  (15 shorter events, 0.1 us)
Async XLA Ops:
  2.2 1.4 %collective-permute-start = (f32[136,128]{1,0:T(8,128)S(1)}, f32[136,128]{1,0:T(8,128)S(1)}, u32[]{:S(2)}, u32[]{:S(2)}) collective-permute-start(f32[136,128]{1,0:T(8,128)S(1)} %get-tuple-element.34), channel_id=1, source_target_pairs={{0,1},{1,0},{2,3},{3,2},{4,5},{5,4},{6,7},{7,6},{8,9},{9,8},{10,11... | collective-permute-start | bytes 208904 | tf_op jit(solution)/shard_map/ppermute | solution.py:100
  2.7 5.7 %collective-permute-start.2 = (f32[8,128,128]{2,1,0:T(8,128)S(1)}, f32[8,128,128]{2,1,0:T(8,128)S(1)}, u32[]{:S(2)}, u32[]{:S(2)}) collective-permute-start(f32[8,128,128]{2,1,0:T(8,128)S(1)} %get-tuple-element.39.refs_5_), channel_id=1, source_target_pairs={{0,1},{1,0},{2,3},{3,2},{4,5},{5,4},{6,7},{7,6},{8,9},{9,8},{10,11... | collective-permute-start | bytes 1572872 | tf_op jit(solution)/shard_map/ppermute | solution.py:100
  2.8 5.6 %collective-permute-start.3 = (f32[1024,128]{1,0:T(8,128)S(1)}, f32[1024,128]{1,0:T(8,128)S(1)}, u32[]{:S(2)}, u32[]{:S(2)}) collective-permute-start(f32[1024,128]{1,0:T(8,128)S(1)} %get-tuple-element.40.refs_0_), channel_id=1, source_target_pairs={{0,1},{1,0},{2,3},{3,2},{4,5},{5,4},{6,7},{7,6},{8,9},{9,8},{10,11... | collective-permute-start | bytes 1572872 | tf_op jit(solution)/shard_map/ppermute | solution.py:100
  3.7 4.7 %collective-permute-start.1 = (f32[144,128]{1,0:T(8,128)S(1)}, f32[144,128]{1,0:T(8,128)S(1)}, u32[]{:S(2)}, u32[]{:S(2)}) collective-permute-start(f32[144,128]{1,0:T(8,128)S(1)} %pad_maximum_fusion), channel_id=1, source_target_pairs={{0,1},{1,2},{2,3},{3,0},{4,5},{5,6},{6,7},{7,4},{8,11},{9,8},{10,9... | collective-permute-start | bytes 221192 | tf_op jit(solution)/shard_map/ppermute | solution.py:110
  9.2 3.9 %collective-permute-start.7 = (f32[88,128]{1,0:T(8,128)S(1)}, f32[88,128]{1,0:T(8,128)S(1)}, u32[]{:S(2)}, u32[]{:S(2)}) collective-permute-start(f32[88,128]{1,0:T(8,128)S(1)} %get-tuple-element.41), channel_id=1, source_target_pairs={{0,21},{1,0},{2,23},{3,2},{4,17},{5,4},{6,19},{7,6},{8,9},{9,28},{... | collective-permute-start | bytes 135176 | tf_op jit(solution)/shard_map/ppermute | solution.py:110
  11.4 2.7 %collective-permute-start.6 = (f32[88,128]{1,0:T(8,128)S(1)}, f32[88,128]{1,0:T(8,128)S(1)}, u32[]{:S(2)}, u32[]{:S(2)}) collective-permute-start(f32[88,128]{1,0:T(8,128)S(1)} %get-tuple-element.41), channel_id=1, source_target_pairs={{0,17},{1,0},{2,19},{3,2},{4,21},{5,4},{6,23},{7,6},{8,9},{9,24},{... | collective-permute-start | bytes 135176 | tf_op jit(solution)/shard_map/ppermute | solution.py:110
  12.4 1.7 %collective-permute-start.5 = (f32[88,128]{1,0:T(8,128)S(1)}, f32[88,128]{1,0:T(8,128)S(1)}, u32[]{:S(2)}, u32[]{:S(2)}) collective-permute-start(f32[88,128]{1,0:T(8,128)S(1)} %get-tuple-element.41), channel_id=1, source_target_pairs={{0,5},{1,0},{2,7},{3,2},{4,1},{5,4},{6,3},{7,6},{8,9},{9,12},{10,1... | collective-permute-start | bytes 135176 | tf_op jit(solution)/shard_map/ppermute | solution.py:110
  12.4 1.7 %collective-permute-start.4 = (f32[88,128]{1,0:T(8,128)S(1)}, f32[88,128]{1,0:T(8,128)S(1)}, u32[]{:S(2)}, u32[]{:S(2)}) collective-permute-start(f32[88,128]{1,0:T(8,128)S(1)} %get-tuple-element.41), channel_id=1, source_target_pairs={{0,1},{1,0},{2,3},{3,2},{4,5},{5,4},{6,7},{7,6},{8,9},{9,8},{10,11... | collective-permute-start | bytes 135176 | tf_op jit(solution)/shard_map/ppermute | solution.py:100
  12.9 3.0 %collective-permute-start.10 = (f32[128,128]{1,0:T(8,128)S(1)}, f32[128,128]{1,0:T(8,128)S(1)}, u32[]{:S(2)}, u32[]{:S(2)}) collective-permute-start(f32[128,128]{1,0:T(8,128)S(1)} %get-tuple-element.43.refs_2_.moved), channel_id=1, source_target_pairs={{0,1},{1,0},{2,3},{3,2},{4,5},{5,4},{6,7},{7,6},{8,9},{9,8},{10,11... | collective-permute-start | bytes 196616 | tf_op jit(solution)/shard_map/ppermute | solution.py:100
  14.1 5.1 %collective-permute-start.9 = (f32[88,128]{1,0:T(8,128)S(1)}, f32[88,128]{1,0:T(8,128)S(1)}, u32[]{:S(2)}, u32[]{:S(2)}) collective-permute-start(f32[88,128]{1,0:T(8,128)S(1)} %add_add_fusion.1), channel_id=1, source_target_pairs={{0,1},{1,9},{2,3},{3,11},{4,5},{5,13},{6,7},{7,15},{8,0},{9,8},{10... | collective-permute-start | bytes 135176 | tf_op jit(solution)/shard_map/ppermute | solution.py:110
  15.8 3.4 %collective-permute-start.8 = (f32[88,128]{1,0:T(8,128)S(1)}, f32[88,128]{1,0:T(8,128)S(1)}, u32[]{:S(2)}, u32[]{:S(2)}) collective-permute-start(f32[88,128]{1,0:T(8,128)S(1)} %add_add_fusion.1), channel_id=1, source_target_pairs={{0,1},{1,0},{2,3},{3,2},{4,5},{5,4},{6,7},{7,6},{8,9},{9,8},{10,11... | collective-permute-start | bytes 135176 | tf_op jit(solution)/shard_map/ppermute | solution.py:100
  19.6 2.8 %collective-permute-start.14 = (f32[144,128]{1,0:T(8,128)S(1)}, f32[144,128]{1,0:T(8,128)S(1)}, u32[]{:S(2)}, u32[]{:S(2)}) collective-permute-start(f32[144,128]{1,0:T(8,128)S(1)} %get-tuple-element.44), channel_id=1, source_target_pairs={{0,19},{1,0},{2,17},{3,2},{4,23},{5,4},{6,21},{7,6},{8,9},{9,26},{... | collective-permute-start | bytes 221192 | tf_op jit(solution)/shard_map/ppermute | solution.py:110
  19.7 4.2 %collective-permute-start.13 = (f32[144,128]{1,0:T(8,128)S(1)}, f32[144,128]{1,0:T(8,128)S(1)}, u32[]{:S(2)}, u32[]{:S(2)}) collective-permute-start(f32[144,128]{1,0:T(8,128)S(1)} %get-tuple-element.44), channel_id=1, source_target_pairs={{0,17},{1,0},{2,19},{3,2},{4,21},{5,4},{6,23},{7,6},{8,9},{9,24},{... | collective-permute-start | bytes 221192 | tf_op jit(solution)/shard_map/ppermute | solution.py:110
  21.9 2.0 %collective-permute-start.12 = (f32[144,128]{1,0:T(8,128)S(1)}, f32[144,128]{1,0:T(8,128)S(1)}, u32[]{:S(2)}, u32[]{:S(2)}) collective-permute-start(f32[144,128]{1,0:T(8,128)S(1)} %get-tuple-element.44), channel_id=1, source_target_pairs={{0,3},{1,0},{2,1},{3,2},{4,7},{5,4},{6,5},{7,6},{8,9},{9,10},{10,1... | collective-permute-start | bytes 221192 | tf_op jit(solution)/shard_map/ppermute | solution.py:110
  21.9 2.0 %collective-permute-start.11 = (f32[144,128]{1,0:T(8,128)S(1)}, f32[144,128]{1,0:T(8,128)S(1)}, u32[]{:S(2)}, u32[]{:S(2)}) collective-permute-start(f32[144,128]{1,0:T(8,128)S(1)} %get-tuple-element.44), channel_id=1, source_target_pairs={{0,1},{1,0},{2,3},{3,2},{4,5},{5,4},{6,7},{7,6},{8,9},{9,8},{10,11... | collective-permute-start | bytes 221192 | tf_op jit(solution)/shard_map/ppermute | solution.py:100
  22.4 4.7 %collective-permute-start.20 = (f32[128,128]{1,0:T(8,128)S(1)}, f32[128,128]{1,0:T(8,128)S(1)}, u32[]{:S(2)}, u32[]{:S(2)}) collective-permute-start(f32[128,128]{1,0:T(8,128)S(1)} %get-tuple-element.47.gram), channel_id=1, source_target_pairs={{0,1},{1,0},{2,3},{3,2},{4,5},{5,4},{6,7},{7,6},{8,9},{9,8},{10,11... | collective-permute-start | bytes 196616 | tf_op jit(solution)/shard_map/ppermute | solution.py:100
  23.9 5.2 %collective-permute-start.18 = (f32[128,128]{1,0:T(8,128)S(1)}, f32[128,128]{1,0:T(8,128)S(1)}, u32[]{:S(2)}, u32[]{:S(2)}) collective-permute-start(f32[128,128]{1,0:T(8,128)S(1)} %get-tuple-element.45), channel_id=1, source_target_pairs={{0,1},{1,13},{2,3},{3,15},{4,5},{5,9},{6,7},{7,11},{8,4},{9,8},{10... | collective-permute-start | bytes 196616 | tf_op jit(solution)/shard_map/ppermute | solution.py:110
  26.2 4.3 %collective-permute-start.17 = (f32[128,128]{1,0:T(8,128)S(1)}, f32[128,128]{1,0:T(8,128)S(1)}, u32[]{:S(2)}, u32[]{:S(2)}) collective-permute-start(f32[128,128]{1,0:T(8,128)S(1)} %get-tuple-element.45), channel_id=1, source_target_pairs={{0,1},{1,9},{2,3},{3,11},{4,5},{5,13},{6,7},{7,15},{8,0},{9,8},{10... | collective-permute-start | bytes 196616 | tf_op jit(solution)/shard_map/ppermute | solution.py:110
  26.3 4.2 %collective-permute-start.16 = (f32[128,128]{1,0:T(8,128)S(1)}, f32[128,128]{1,0:T(8,128)S(1)}, u32[]{:S(2)}, u32[]{:S(2)}) collective-permute-start(f32[128,128]{1,0:T(8,128)S(1)} %get-tuple-element.45), channel_id=1, source_target_pairs={{0,1},{1,4},{2,3},{3,6},{4,5},{5,0},{6,7},{7,2},{8,13},{9,8},{10,1... | collective-permute-start | bytes 196616 | tf_op jit(solution)/shard_map/ppermute | solution.py:110
  26.3 4.1 %collective-permute-start.15 = (f32[128,128]{1,0:T(8,128)S(1)}, f32[128,128]{1,0:T(8,128)S(1)}, u32[]{:S(2)}, u32[]{:S(2)}) collective-permute-start(f32[128,128]{1,0:T(8,128)S(1)} %get-tuple-element.45), channel_id=1, source_target_pairs={{0,1},{1,0},{2,3},{3,2},{4,5},{5,4},{6,7},{7,6},{8,9},{9,8},{10,11... | collective-permute-start | bytes 196616 | tf_op jit(solution)/shard_map/ppermute | solution.py:100
  27.1 1.2 %collective-permute-start.19 = (f32[32,128]{1,0:T(8,128)S(1)}, f32[32,128]{1,0:T(8,128)S(1)}, u32[]{:S(2)}, u32[]{:S(2)}) collective-permute-start(f32[32,128]{1,0:T(8,128)S(1)} %get-tuple-element.46.rows), channel_id=1, source_target_pairs={{0,1},{1,0},{2,3},{3,2},{4,5},{5,4},{6,7},{7,6},{8,9},{9,8},{10,11... | collective-permute-start | bytes 49160 | tf_op jit(solution)/shard_map/ppermute | solution.py:100
  30.5 1.3 %collective-permute-start.21 = (f32[128,128]{1,0:T(8,128)S(1)}, f32[128,128]{1,0:T(8,128)S(1)}, u32[]{:S(2)}, u32[]{:S(2)}) collective-permute-start(f32[128,128]{1,0:T(8,128)S(1)} %add_add_fusion.terms), channel_id=1, source_target_pairs={{0,1},{1,0},{2,3},{3,2},{4,5},{5,4},{6,7},{7,6},{8,9},{9,8},{10,11... | collective-permute-start | bytes 196616 | tf_op jit(solution)/shard_map/ppermute | solution.py:100

commit v21 on v20

--- a/solution.py
+++ b/solution.py
@@ -326,7 +326,7 @@
 
     terms, rows_b, rows_role = payload[:times], payload[times:], holder
     smp_mask = sum(chip_bits)
-    for group in groups_of(chip_bits + vox_bits[-1:] + vox_bits[:-1]):
+    for group in groups_of(chip_bits + vox_bits):
         masks = masks_of(group)
         if any(mask & smp_mask for mask in masks):
             packet = payload if rows_b.shape[0] == chip_rows else jnp.concatenate([terms, rows_b], axis=0)

time: 32.6 us -> 32.3 us (level)
    ppermute x11, waiting for transfers between devices: 2.15 us -> 1.81 us  [swap(): lax.ppermute(values, ALL, [(i, i ^ 1) for i in range(lax.axis_size(ALL))])]
  transfers between devices with their start and end apart: 22 -> 22, of which waited for: 9 -> 11; matrix products, arithmetic and copies ran while one was open for 0% -> 0% of each run, Pallas kernels for 7% -> 7%
where the time goes in v21:
time: 32.3 us; the launch traced here: 32.2 us
  starting transfers between devices  12.9 us (40%)
  waiting for transfers between devices  12.8 us (40%)
  Pallas kernels  5.63 us (17%)
  between operations  0.75 us (2%)
    ppermute x11, waiting for transfers between devices, send(): return lax.ppermute(values, ALL, pairs)  11 us
    ppermute x11, starting transfers between devices, send(): return lax.ppermute(values, ALL, pairs)  10.2 us
    pallas_call x9, Pallas kernels, call(): pl.pallas_call(kernel, out_shape=outs, in_specs=specs, out_specs=[pl.Bloc...  5.63 us
    ppermute x11, starting transfers between devices, swap(): lax.ppermute(values, ALL, [(i, i ^ 1) for i in range(lax.axis_size(ALL))])  2.7 us
    ppermute x11, waiting for transfers between devices, swap(): lax.ppermute(values, ALL, [(i, i ^ 1) for i in range(lax.axis_size(ALL))])  1.81 us
  transfers between devices with their start and end apart: 22, of which 11 were waited for; matrix products, arithmetic and copies ran while one was open for 0% of the time, Pallas kernels for 7%

profile of v21, /device:TPU:0, one launch (start us, length us, event | category | flops | bytes accessed | tf_op | source)
XLA Modules:
  0.0 32.2 jit_solution(12573309682346962345)
XLA Ops:
  0.6 1.6 %shard_map.84 = (f32[1024,128]{1,0:T(8,128)S(1)}, f32[128,128]{1,0:T(8,128)S(1)}, f32[128,128]{1,0:T(8,128)S(1)}, f32[1,128]{1,0:T(1,128)S(1)}, f32[136,128]{1,0:T(8,128)S(1)}, /*index=5*/f32[8,128,128]{2,1,0:T(8,128)S(1)}) custom-call(f32[1024,128]{1,0:T(8,128)} %bitcast.3, f32[128,128]{1,0:T(8,128)} %c_hbm.1, f32[8,128]{1,0:T(8,128)} %b_hbm.1, ...), custom_call_target="tpu_custom_call" | custom-call | flops 201326592 | bytes 65536 | tf_op jit(solution)/shard_map/pallas_call | solution.py:63
  2.2 0.5 %collective-permute-start = (f32[136,128]{1,0:T(8,128)S(1)}, f32[136,128]{1,0:T(8,128)S(1)}, u32[]{:S(2)}, u32[]{:S(2)}) collective-permute-start(f32[136,128]{1,0:T(8,128)S(1)} %get-tuple-element.34), channel_id=1, source_target_pairs={{0,1},{1,0},{2,3},{3,2},{4,5},{5,4},{6,7},{7,6},{8,9},{9,8},{10,11... | collective-permute-start | bytes 208904 | tf_op jit(solution)/shard_map/ppermute | solution.py:100
  2.7 0.1 collective-permute-start.2
  2.8 0.4 %collective-permute-start.3 = (f32[1024,128]{1,0:T(8,128)S(1)}, f32[1024,128]{1,0:T(8,128)S(1)}, u32[]{:S(2)}, u32[]{:S(2)}) collective-permute-start(f32[1024,128]{1,0:T(8,128)S(1)} %get-tuple-element.40.refs_0_), channel_id=1, source_target_pairs={{0,1},{1,0},{2,3},{3,2},{4,5},{5,4},{6,7},{7,6},{8,9},{9,8},{10,11... | collective-permute-start | bytes 1572872 | tf_op jit(solution)/shard_map/ppermute | solution.py:100
  3.2 0.4 %collective-permute-done = f32[136,128]{1,0:T(8,128)S(1)} collective-permute-done((f32[136,128]{1,0:T(8,128)S(1)}, f32[136,128]{1,0:T(8,128)S(1)}, u32[]{:S(2)}, u32[]{:S(2)}) %collective-permute-start) | collective-permute-done | bytes 69664 | tf_op jit(solution)/shard_map/ppermute | solution.py:100
  3.7 0.4 %collective-permute-start.1 = (f32[144,128]{1,0:T(8,128)S(1)}, f32[144,128]{1,0:T(8,128)S(1)}, u32[]{:S(2)}, u32[]{:S(2)}) collective-permute-start(f32[144,128]{1,0:T(8,128)S(1)} %pad_maximum_fusion), channel_id=1, source_target_pairs={{0,1},{1,2},{2,3},{3,0},{4,5},{5,6},{6,7},{7,4},{8,11},{9,8},{10,9... | collective-permute-start | bytes 221192 | tf_op jit(solution)/shard_map/ppermute | solution.py:110
  4.1 0.2 shard_map.85
  4.3 4.1 %collective-permute-done.1 = f32[144,128]{1,0:T(8,128)S(1)} collective-permute-done((f32[144,128]{1,0:T(8,128)S(1)}, f32[144,128]{1,0:T(8,128)S(1)}, u32[]{:S(2)}, u32[]{:S(2)}) %collective-permute-start.1) | collective-permute-done | bytes 73760 | tf_op jit(solution)/shard_map/ppermute | solution.py:110
  8.4 0.0 collective-permute-done.2.refs_6_
  8.4 0.0 collective-permute-done.3.refs_7_.refs_1_
  8.4 0.7 %shard_map.86 = (f32[128,128]{1,0:T(8,128)S(1)}, f32[16,128]{1,0:T(8,128)S(1)}, f32[88,128]{1,0:T(8,128)S(1)}) custom-call(f32[128,128]{1,0:T(8,128)S(1)} %slice_add_fusion.refs_0_, f32[32,128]{1,0:T(8,128)S(1)} %pad_maximum_fusion.1.refs_1_, f32[128,128]{1,0:T(8,128)S(1)} %get-tuple-element.35.refs_2_, f32[1,128]{1,0:T(1,128)S(1)} %get-tuple-element.36.w.refs_3_.refs_2_, ...), custom_call_target="tpu_custom_call" | custom-call | flops 50331648 | bytes 65536 | tf_op jit(solution)/shard_map/pallas_call | solution.py:63
  9.2 2.2 %collective-permute-start.7 = (f32[88,128]{1,0:T(8,128)S(1)}, f32[88,128]{1,0:T(8,128)S(1)}, u32[]{:S(2)}, u32[]{:S(2)}) collective-permute-start(f32[88,128]{1,0:T(8,128)S(1)} %get-tuple-element.41), channel_id=1, source_target_pairs={{0,21},{1,0},{2,23},{3,2},{4,17},{5,4},{6,19},{7,6},{8,9},{9,28},{... | collective-permute-start | bytes 135176 | tf_op jit(solution)/shard_map/ppermute | solution.py:110
  11.4 1.0 %collective-permute-start.6 = (f32[88,128]{1,0:T(8,128)S(1)}, f32[88,128]{1,0:T(8,128)S(1)}, u32[]{:S(2)}, u32[]{:S(2)}) collective-permute-start(f32[88,128]{1,0:T(8,128)S(1)} %get-tuple-element.41), channel_id=1, source_target_pairs={{0,17},{1,0},{2,19},{3,2},{4,21},{5,4},{6,23},{7,6},{8,9},{9,24},{... | collective-permute-start | bytes 135176 | tf_op jit(solution)/shard_map/ppermute | solution.py:110
  12.4 0.0 collective-permute-start.5
  12.4 0.5 %collective-permute-start.4 = (f32[88,128]{1,0:T(8,128)S(1)}, f32[88,128]{1,0:T(8,128)S(1)}, u32[]{:S(2)}, u32[]{:S(2)}) collective-permute-start(f32[88,128]{1,0:T(8,128)S(1)} %get-tuple-element.41), channel_id=1, source_target_pairs={{0,1},{1,0},{2,3},{3,2},{4,5},{5,4},{6,7},{7,6},{8,9},{9,8},{10,11... | collective-permute-start | bytes 135176 | tf_op jit(solution)/shard_map/ppermute | solution.py:100
  12.9 0.0 collective-permute-start.10
  12.9 0.2 collective-permute-done.7
  13.1 1.0 %collective-permute-done.6 = f32[88,128]{1,0:T(8,128)S(1)} collective-permute-done((f32[88,128]{1,0:T(8,128)S(1)}, f32[88,128]{1,0:T(8,128)S(1)}, u32[]{:S(2)}, u32[]{:S(2)}) %collective-permute-start.6) | collective-permute-done | bytes 45088 | tf_op jit(solution)/shard_map/ppermute | solution.py:110
  14.1 0.0 collective-permute-done.4
  14.1 1.7 %collective-permute-start.9 = (f32[88,128]{1,0:T(8,128)S(1)}, f32[88,128]{1,0:T(8,128)S(1)}, u32[]{:S(2)}, u32[]{:S(2)}) collective-permute-start(f32[88,128]{1,0:T(8,128)S(1)} %add_add_fusion.1), channel_id=1, source_target_pairs={{0,1},{1,9},{2,3},{3,11},{4,5},{5,13},{6,7},{7,15},{8,0},{9,8},{10... | collective-permute-start | bytes 135176 | tf_op jit(solution)/shard_map/ppermute | solution.py:110
  15.8 0.1 collective-permute-start.8
  15.9 0.5 %shard_map.87.refs_4_ = f32[16,128,128]{2,1,0:T(8,128)S(1)} custom-call(f32[1024,128]{1,0:T(8,128)S(1)} %get-tuple-element.40.refs_0_, f32[1024,128]{1,0:T(8,128)S(1)} %collective-permute-done.3.refs_7_.refs_1_, f32[128,128]{1,0:T(8,128)S(1)} %get-tuple-element.43.refs_2_.moved, f32[128,128]{1,0:T(8,128)S(1)} %collective-permute-done.10.refs_3_.mate_moved), custom_call_target="tpu_custom_call" | custom-call | flops 402653184 | bytes 65536 | tf_op jit(solution)/shard_map/pallas_call | solution.py:63
  16.4 2.9 %collective-permute-done.9 = f32[88,128]{1,0:T(8,128)S(1)} collective-permute-done((f32[88,128]{1,0:T(8,128)S(1)}, f32[88,128]{1,0:T(8,128)S(1)}, u32[]{:S(2)}, u32[]{:S(2)}) %collective-permute-start.9) | collective-permute-done | bytes 45088 | tf_op jit(solution)/shard_map/ppermute | solution.py:110
  19.2 0.4 %shard_map.88 = (f32[128,128]{1,0:T(8,128)S(1)}, f32[144,128]{1,0:T(8,128)S(1)}) custom-call(f32[88,128]{1,0:T(8,128)S(1)} %add.32.refs_0_, f32[16,128]{1,0:T(8,128)S(1)} %get-tuple-element.42.refs_1_, f32[1,128]{1,0:T(1,128)S(1)} %get-tuple-element.36.w.refs_3_.refs_2_, f32[128,128]{1,0:T(8,128)S(1)} %get-tuple-element.38.refs_4_.refs_3_, ...), custom_call_target="tpu_custom_call" | custom-call | flops 3145728 | bytes 65536 | tf_op jit(solution)/shard_map/pallas_call | solution.py:63
  19.6 0.1 collective-permute-start.14
  19.7 0.6 %collective-permute-start.13 = (f32[144,128]{1,0:T(8,128)S(1)}, f32[144,128]{1,0:T(8,128)S(1)}, u32[]{:S(2)}, u32[]{:S(2)}) collective-permute-start(f32[144,128]{1,0:T(8,128)S(1)} %get-tuple-element.44), channel_id=1, source_target_pairs={{0,5},{1,0},{2,7},{3,2},{4,1},{5,4},{6,3},{7,6},{8,9},{9,12},{10,1... | collective-permute-start | bytes 221192 | tf_op jit(solution)/shard_map/ppermute | solution.py:110
  20.3 0.9 %collective-permute-start.12 = (f32[144,128]{1,0:T(8,128)S(1)}, f32[144,128]{1,0:T(8,128)S(1)}, u32[]{:S(2)}, u32[]{:S(2)}) collective-permute-start(f32[144,128]{1,0:T(8,128)S(1)} %get-tuple-element.44), channel_id=1, source_target_pairs={{0,3},{1,0},{2,1},{3,2},{4,7},{5,4},{6,5},{7,6},{8,9},{9,10},{10,1... | collective-permute-start | bytes 221192 | tf_op jit(solution)/shard_map/ppermute | solution.py:110
  21.2 0.0 collective-permute-start.11
  21.2 0.5 %collective-permute-start.20 = (f32[128,128]{1,0:T(8,128)S(1)}, f32[128,128]{1,0:T(8,128)S(1)}, u32[]{:S(2)}, u32[]{:S(2)}) collective-permute-start(f32[128,128]{1,0:T(8,128)S(1)} %get-tuple-element.47.gram), channel_id=1, source_target_pairs={{0,1},{1,0},{2,3},{3,2},{4,5},{5,4},{6,7},{7,6},{8,9},{9,8},{10,11... | collective-permute-start | bytes 196616 | tf_op jit(solution)/shard_map/ppermute | solution.py:100
  21.7 0.7 %collective-permute-done.13.refs_2_ = f32[144,128]{1,0:T(8,128)S(1)} collective-permute-done((f32[144,128]{1,0:T(8,128)S(1)}, f32[144,128]{1,0:T(8,128)S(1)}, u32[]{:S(2)}, u32[]{:S(2)}) %collective-permute-start.13) | collective-permute-done | bytes 73760 | tf_op jit(solution)/shard_map/ppermute | solution.py:110
  22.3 0.8 %collective-permute-done.12.refs_1_ = f32[144,128]{1,0:T(8,128)S(1)} collective-permute-done((f32[144,128]{1,0:T(8,128)S(1)}, f32[144,128]{1,0:T(8,128)S(1)}, u32[]{:S(2)}, u32[]{:S(2)}) %collective-permute-start.12) | collective-permute-done | bytes 73760 | tf_op jit(solution)/shard_map/ppermute | solution.py:110
  23.1 0.0 collective-permute-done.11.refs_0_
  23.2 1.0 %collective-permute-start.18 = (f32[128,128]{1,0:T(8,128)S(1)}, f32[128,128]{1,0:T(8,128)S(1)}, u32[]{:S(2)}, u32[]{:S(2)}) collective-permute-start(f32[128,128]{1,0:T(8,128)S(1)} %get-tuple-element.45), channel_id=1, source_target_pairs={{0,1},{1,25},{2,3},{3,27},{4,5},{5,29},{6,7},{7,31},{8,16},{9,8},{... | collective-permute-start | bytes 196616 | tf_op jit(solution)/shard_map/ppermute | solution.py:110
  24.1 0.1 collective-permute-start.17
  24.2 2.3 %collective-permute-start.16 = (f32[128,128]{1,0:T(8,128)S(1)}, f32[128,128]{1,0:T(8,128)S(1)}, u32[]{:S(2)}, u32[]{:S(2)}) collective-permute-start(f32[128,128]{1,0:T(8,128)S(1)} %get-tuple-element.45), channel_id=1, source_target_pairs={{0,1},{1,9},{2,3},{3,11},{4,5},{5,13},{6,7},{7,15},{8,0},{9,8},{10... | collective-permute-start | bytes 196616 | tf_op jit(solution)/shard_map/ppermute | solution.py:110
  26.5 0.0 collective-permute-start.15
  26.5 0.0 collective-permute-done.20.mate_gram
  26.5 0.5 %collective-permute-start.19 = (f32[32,128]{1,0:T(8,128)S(1)}, f32[32,128]{1,0:T(8,128)S(1)}, u32[]{:S(2)}, u32[]{:S(2)}) collective-permute-start(f32[32,128]{1,0:T(8,128)S(1)} %get-tuple-element.46.rows), channel_id=1, source_target_pairs={{0,1},{1,0},{2,3},{3,2},{4,5},{5,4},{6,7},{7,6},{8,9},{9,8},{10,11... | collective-permute-start | bytes 49160 | tf_op jit(solution)/shard_map/ppermute | solution.py:100
  27.0 0.7 %shard_map.90 = (f32[128,128]{1,0:T(8,128)}, f32[1,128]{1,0:T(1,128)S(1)}, f32[128,128]{1,0:T(8,128)S(1)}) custom-call(f32[128,128]{1,0:T(8,128)S(1)} %get-tuple-element.47.gram, f32[128,128]{1,0:T(8,128)S(1)} %collective-permute-done.20.mate_gram, f32[128,128]{1,0:T(8,128)S(1)} %get-tuple-element.43.refs_2_.moved, ...), custom_call_target="tpu_custom_call" | custom-call | flops 131072 | bytes 65536 | tf_op jit(solution)/shard_map/pallas_call | solution.py:63
  27.7 0.2 collective-permute-done.19.mate_rows
  27.9 0.9 %shard_map.91 = (f32[8,128]{1,0:T(8,128)}, f32[128,128]{1,0:T(8,128)S(1)}, f32[1,128]{1,0:T(1,128)S(1)}, f32[1,128]{1,0:T(1,128)S(1)}) custom-call(f32[32,128]{1,0:T(8,128)S(1)} %get-tuple-element.46.rows, f32[32,128]{1,0:T(8,128)S(1)} %collective-permute-done.19.mate_rows, f32[128,128]{1,0:T(8,128)S(1)} %get-tuple-element.37.c, ...), custom_call_target="tpu_custom_call" | custom-call | flops 16777216 | bytes 65536 | tf_op jit(solution)/shard_map/pallas_call | solution.py:63
  28.7 0.8 %collective-permute-done.18 = f32[128,128]{1,0:T(8,128)S(1)} collective-permute-done((f32[128,128]{1,0:T(8,128)S(1)}, f32[128,128]{1,0:T(8,128)S(1)}, u32[]{:S(2)}, u32[]{:S(2)}) %collective-permute-start.18) | collective-permute-done | bytes 65568 | tf_op jit(solution)/shard_map/ppermute | solution.py:110
  29.5 0.6 %collective-permute-done.17 = f32[128,128]{1,0:T(8,128)S(1)} collective-permute-done((f32[128,128]{1,0:T(8,128)S(1)}, f32[128,128]{1,0:T(8,128)S(1)}, u32[]{:S(2)}, u32[]{:S(2)}) %collective-permute-start.17) | collective-permute-done | bytes 65568 | tf_op jit(solution)/shard_map/ppermute | solution.py:110
  30.1 0.0 collective-permute-done.16
  30.1 0.0 collective-permute-done.15
  30.2 0.1 collective-permute-start.21
  30.2 1.2 %collective-permute-done.21.mate_terms = f32[128,128]{1,0:T(8,128)S(1)} collective-permute-done((f32[128,128]{1,0:T(8,128)S(1)}, f32[128,128]{1,0:T(8,128)S(1)}, u32[]{:S(2)}, u32[]{:S(2)}) %collective-permute-start.21) | collective-permute-done | bytes 65568 | tf_op jit(solution)/shard_map/ppermute | solution.py:100
  31.5 0.7 %shard_map.92 = (f32[128,128]{1,0:T(8,128)}, f32[1,128]{1,0:T(1,128)}) custom-call(f32[128,128]{1,0:T(8,128)S(1)} %add_add_fusion.terms, f32[128,128]{1,0:T(8,128)S(1)} %collective-permute-done.21.mate_terms, f32[128,128]{1,0:T(8,128)S(1)} %get-tuple-element.59.base, f32[1,128]{1,0:T(1,128)S(1)} %get-tuple-element.60.gain, f32[1,128]{1,0:T(1,128)S(1)} %get-tuple-element.61.scale), custom_call_target="tpu_custom_call" | custom-call | flops 131072 | bytes 65536 | tf_op jit(solution)/shard_map/pallas_call | solution.py:63
  (15 shorter events, 0.1 us)
Async XLA Ops:
  2.2 1.4 %collective-permute-start = (f32[136,128]{1,0:T(8,128)S(1)}, f32[136,128]{1,0:T(8,128)S(1)}, u32[]{:S(2)}, u32[]{:S(2)}) collective-permute-start(f32[136,128]{1,0:T(8,128)S(1)} %get-tuple-element.34), channel_id=1, source_target_pairs={{0,1},{1,0},{2,3},{3,2},{4,5},{5,4},{6,7},{7,6},{8,9},{9,8},{10,11... | collective-permute-start | bytes 208904 | tf_op jit(solution)/shard_map/ppermute | solution.py:100
  2.7 5.7 %collective-permute-start.2 = (f32[8,128,128]{2,1,0:T(8,128)S(1)}, f32[8,128,128]{2,1,0:T(8,128)S(1)}, u32[]{:S(2)}, u32[]{:S(2)}) collective-permute-start(f32[8,128,128]{2,1,0:T(8,128)S(1)} %get-tuple-element.39.refs_5_), channel_id=1, source_target_pairs={{0,1},{1,0},{2,3},{3,2},{4,5},{5,4},{6,7},{7,6},{8,9},{9,8},{10,11... | collective-permute-start | bytes 1572872 | tf_op jit(solution)/shard_map/ppermute | solution.py:100
  2.8 5.6 %collective-permute-start.3 = (f32[1024,128]{1,0:T(8,128)S(1)}, f32[1024,128]{1,0:T(8,128)S(1)}, u32[]{:S(2)}, u32[]{:S(2)}) collective-permute-start(f32[1024,128]{1,0:T(8,128)S(1)} %get-tuple-element.40.refs_0_), channel_id=1, source_target_pairs={{0,1},{1,0},{2,3},{3,2},{4,5},{5,4},{6,7},{7,6},{8,9},{9,8},{10,11... | collective-permute-start | bytes 1572872 | tf_op jit(solution)/shard_map/ppermute | solution.py:100
  3.7 4.7 %collective-permute-start.1 = (f32[144,128]{1,0:T(8,128)S(1)}, f32[144,128]{1,0:T(8,128)S(1)}, u32[]{:S(2)}, u32[]{:S(2)}) collective-permute-start(f32[144,128]{1,0:T(8,128)S(1)} %pad_maximum_fusion), channel_id=1, source_target_pairs={{0,1},{1,2},{2,3},{3,0},{4,5},{5,6},{6,7},{7,4},{8,11},{9,8},{10,9... | collective-permute-start | bytes 221192 | tf_op jit(solution)/shard_map/ppermute | solution.py:110
  9.2 3.9 %collective-permute-start.7 = (f32[88,128]{1,0:T(8,128)S(1)}, f32[88,128]{1,0:T(8,128)S(1)}, u32[]{:S(2)}, u32[]{:S(2)}) collective-permute-start(f32[88,128]{1,0:T(8,128)S(1)} %get-tuple-element.41), channel_id=1, source_target_pairs={{0,21},{1,0},{2,23},{3,2},{4,17},{5,4},{6,19},{7,6},{8,9},{9,28},{... | collective-permute-start | bytes 135176 | tf_op jit(solution)/shard_map/ppermute | solution.py:110
  11.4 2.7 %collective-permute-start.6 = (f32[88,128]{1,0:T(8,128)S(1)}, f32[88,128]{1,0:T(8,128)S(1)}, u32[]{:S(2)}, u32[]{:S(2)}) collective-permute-start(f32[88,128]{1,0:T(8,128)S(1)} %get-tuple-element.41), channel_id=1, source_target_pairs={{0,17},{1,0},{2,19},{3,2},{4,21},{5,4},{6,23},{7,6},{8,9},{9,24},{... | collective-permute-start | bytes 135176 | tf_op jit(solution)/shard_map/ppermute | solution.py:110
  12.4 1.7 %collective-permute-start.5 = (f32[88,128]{1,0:T(8,128)S(1)}, f32[88,128]{1,0:T(8,128)S(1)}, u32[]{:S(2)}, u32[]{:S(2)}) collective-permute-start(f32[88,128]{1,0:T(8,128)S(1)} %get-tuple-element.41), channel_id=1, source_target_pairs={{0,5},{1,0},{2,7},{3,2},{4,1},{5,4},{6,3},{7,6},{8,9},{9,12},{10,1... | collective-permute-start | bytes 135176 | tf_op jit(solution)/shard_map/ppermute | solution.py:110
  12.4 1.7 %collective-permute-start.4 = (f32[88,128]{1,0:T(8,128)S(1)}, f32[88,128]{1,0:T(8,128)S(1)}, u32[]{:S(2)}, u32[]{:S(2)}) collective-permute-start(f32[88,128]{1,0:T(8,128)S(1)} %get-tuple-element.41), channel_id=1, source_target_pairs={{0,1},{1,0},{2,3},{3,2},{4,5},{5,4},{6,7},{7,6},{8,9},{9,8},{10,11... | collective-permute-start | bytes 135176 | tf_op jit(solution)/shard_map/ppermute | solution.py:100
  12.9 3.0 %collective-permute-start.10 = (f32[128,128]{1,0:T(8,128)S(1)}, f32[128,128]{1,0:T(8,128)S(1)}, u32[]{:S(2)}, u32[]{:S(2)}) collective-permute-start(f32[128,128]{1,0:T(8,128)S(1)} %get-tuple-element.43.refs_2_.moved), channel_id=1, source_target_pairs={{0,1},{1,0},{2,3},{3,2},{4,5},{5,4},{6,7},{7,6},{8,9},{9,8},{10,11... | collective-permute-start | bytes 196616 | tf_op jit(solution)/shard_map/ppermute | solution.py:100
  14.1 5.1 %collective-permute-start.9 = (f32[88,128]{1,0:T(8,128)S(1)}, f32[88,128]{1,0:T(8,128)S(1)}, u32[]{:S(2)}, u32[]{:S(2)}) collective-permute-start(f32[88,128]{1,0:T(8,128)S(1)} %add_add_fusion.1), channel_id=1, source_target_pairs={{0,1},{1,9},{2,3},{3,11},{4,5},{5,13},{6,7},{7,15},{8,0},{9,8},{10... | collective-permute-start | bytes 135176 | tf_op jit(solution)/shard_map/ppermute | solution.py:110
  15.8 3.4 %collective-permute-start.8 = (f32[88,128]{1,0:T(8,128)S(1)}, f32[88,128]{1,0:T(8,128)S(1)}, u32[]{:S(2)}, u32[]{:S(2)}) collective-permute-start(f32[88,128]{1,0:T(8,128)S(1)} %add_add_fusion.1), channel_id=1, source_target_pairs={{0,1},{1,0},{2,3},{3,2},{4,5},{5,4},{6,7},{7,6},{8,9},{9,8},{10,11... | collective-permute-start | bytes 135176 | tf_op jit(solution)/shard_map/ppermute | solution.py:100
  19.6 2.1 %collective-permute-start.14 = (f32[144,128]{1,0:T(8,128)S(1)}, f32[144,128]{1,0:T(8,128)S(1)}, u32[]{:S(2)}, u32[]{:S(2)}) collective-permute-start(f32[144,128]{1,0:T(8,128)S(1)} %get-tuple-element.44), channel_id=1, source_target_pairs={{0,7},{1,0},{2,5},{3,2},{4,3},{5,4},{6,1},{7,6},{8,9},{9,14},{10,1... | collective-permute-start | bytes 221192 | tf_op jit(solution)/shard_map/ppermute | solution.py:110
  19.7 2.7 %collective-permute-start.13 = (f32[144,128]{1,0:T(8,128)S(1)}, f32[144,128]{1,0:T(8,128)S(1)}, u32[]{:S(2)}, u32[]{:S(2)}) collective-permute-start(f32[144,128]{1,0:T(8,128)S(1)} %get-tuple-element.44), channel_id=1, source_target_pairs={{0,5},{1,0},{2,7},{3,2},{4,1},{5,4},{6,3},{7,6},{8,9},{9,12},{10,1... | collective-permute-start | bytes 221192 | tf_op jit(solution)/shard_map/ppermute | solution.py:110
  20.3 2.8 %collective-permute-start.12 = (f32[144,128]{1,0:T(8,128)S(1)}, f32[144,128]{1,0:T(8,128)S(1)}, u32[]{:S(2)}, u32[]{:S(2)}) collective-permute-start(f32[144,128]{1,0:T(8,128)S(1)} %get-tuple-element.44), channel_id=1, source_target_pairs={{0,3},{1,0},{2,1},{3,2},{4,7},{5,4},{6,5},{7,6},{8,9},{9,10},{10,1... | collective-permute-start | bytes 221192 | tf_op jit(solution)/shard_map/ppermute | solution.py:110
  21.2 2.0 %collective-permute-start.11 = (f32[144,128]{1,0:T(8,128)S(1)}, f32[144,128]{1,0:T(8,128)S(1)}, u32[]{:S(2)}, u32[]{:S(2)}) collective-permute-start(f32[144,128]{1,0:T(8,128)S(1)} %get-tuple-element.44), channel_id=1, source_target_pairs={{0,1},{1,0},{2,3},{3,2},{4,5},{5,4},{6,7},{7,6},{8,9},{9,8},{10,11... | collective-permute-start | bytes 221192 | tf_op jit(solution)/shard_map/ppermute | solution.py:100
  21.2 5.3 %collective-permute-start.20 = (f32[128,128]{1,0:T(8,128)S(1)}, f32[128,128]{1,0:T(8,128)S(1)}, u32[]{:S(2)}, u32[]{:S(2)}) collective-permute-start(f32[128,128]{1,0:T(8,128)S(1)} %get-tuple-element.47.gram), channel_id=1, source_target_pairs={{0,1},{1,0},{2,3},{3,2},{4,5},{5,4},{6,7},{7,6},{8,9},{9,8},{10,11... | collective-permute-start | bytes 196616 | tf_op jit(solution)/shard_map/ppermute | solution.py:100
  23.2 6.3 %collective-permute-start.18 = (f32[128,128]{1,0:T(8,128)S(1)}, f32[128,128]{1,0:T(8,128)S(1)}, u32[]{:S(2)}, u32[]{:S(2)}) collective-permute-start(f32[128,128]{1,0:T(8,128)S(1)} %get-tuple-element.45), channel_id=1, source_target_pairs={{0,1},{1,25},{2,3},{3,27},{4,5},{5,29},{6,7},{7,31},{8,16},{9,8},{... | collective-permute-start | bytes 196616 | tf_op jit(solution)/shard_map/ppermute | solution.py:110
  24.1 6.0 %collective-permute-start.17 = (f32[128,128]{1,0:T(8,128)S(1)}, f32[128,128]{1,0:T(8,128)S(1)}, u32[]{:S(2)}, u32[]{:S(2)}) collective-permute-start(f32[128,128]{1,0:T(8,128)S(1)} %get-tuple-element.45), channel_id=1, source_target_pairs={{0,1},{1,16},{2,3},{3,18},{4,5},{5,20},{6,7},{7,22},{8,25},{9,8},{... | collective-permute-start | bytes 196616 | tf_op jit(solution)/shard_map/ppermute | solution.py:110
  24.2 5.9 %collective-permute-start.16 = (f32[128,128]{1,0:T(8,128)S(1)}, f32[128,128]{1,0:T(8,128)S(1)}, u32[]{:S(2)}, u32[]{:S(2)}) collective-permute-start(f32[128,128]{1,0:T(8,128)S(1)} %get-tuple-element.45), channel_id=1, source_target_pairs={{0,1},{1,9},{2,3},{3,11},{4,5},{5,13},{6,7},{7,15},{8,0},{9,8},{10... | collective-permute-start | bytes 196616 | tf_op jit(solution)/shard_map/ppermute | solution.py:110
  26.5 3.6 %collective-permute-start.15 = (f32[128,128]{1,0:T(8,128)S(1)}, f32[128,128]{1,0:T(8,128)S(1)}, u32[]{:S(2)}, u32[]{:S(2)}) collective-permute-start(f32[128,128]{1,0:T(8,128)S(1)} %get-tuple-element.45), channel_id=1, source_target_pairs={{0,1},{1,0},{2,3},{3,2},{4,5},{5,4},{6,7},{7,6},{8,9},{9,8},{10,11... | collective-permute-start | bytes 196616 | tf_op jit(solution)/shard_map/ppermute | solution.py:100
  26.5 1.3 %collective-permute-start.19 = (f32[32,128]{1,0:T(8,128)S(1)}, f32[32,128]{1,0:T(8,128)S(1)}, u32[]{:S(2)}, u32[]{:S(2)}) collective-permute-start(f32[32,128]{1,0:T(8,128)S(1)} %get-tuple-element.46.rows), channel_id=1, source_target_pairs={{0,1},{1,0},{2,3},{3,2},{4,5},{5,4},{6,7},{7,6},{8,9},{9,8},{10,11... | collective-permute-start | bytes 49160 | tf_op jit(solution)/shard_map/ppermute | solution.py:100
  30.2 1.3 %collective-permute-start.21 = (f32[128,128]{1,0:T(8,128)S(1)}, f32[128,128]{1,0:T(8,128)S(1)}, u32[]{:S(2)}, u32[]{:S(2)}) collective-permute-start(f32[128,128]{1,0:T(8,128)S(1)} %add_add_fusion.terms), channel_id=1, source_target_pairs={{0,1},{1,0},{2,3},{3,2},{4,5},{5,4},{6,7},{7,6},{8,9},{9,8},{10,11... | collective-permute-start | bytes 196616 | tf_op jit(solution)/shard_map/ppermute | solution.py:100

commit v22 on v19

--- a/solution.py
+++ b/solution.py
@@ -170,7 +170,7 @@
     chips, chip_rows = smp_count // 2, 2 * smp_rows
     chip_bits = bits_of(smp_count)[1:]
     vox_bits = [bit * smp_count for bit in bits_of(vox_count)]
-    pieces = 4 if flat_rows % 32 == 0 else 1
+    pieces = 1
     piece_rows = flat_rows // pieces
 
     def open_kernel(x_hbm, c_hbm, b_hbm, a_hbm, w_hbm, x, c, a, w, out, con, sems):
@@ -228,10 +228,10 @@
     got = swap(opened)
     terms = opened[:vox_rows] + got[:vox_rows]
     mate_con, mate_x = swap(con), swap(x)
-    packet = jnp.concatenate([terms, got[vox_rows:], opened[vox_rows:]], axis=0)
-    own = jnp.concatenate([terms, opened[vox_rows:], got[vox_rows:]], axis=0)
+    packet = jnp.concatenate([terms, opened[vox_rows:], got[vox_rows:]], axis=0)
+    own = jnp.concatenate([terms, got[vox_rows:], opened[vox_rows:]], axis=0)
     rows_b = own[vox_rows:]
-    holder = 1
+    holder = 0
     for group in groups_of(chip_bits):
         parts = [send(packet, holder, mask) for mask in masks_of(group)[:-1]] + [own]
         terms = tree([part[:vox_rows] for part in parts])

time: 31.6 us -> 32 us (1.013)
  starting transfers between devices: 12.7 us -> 16.3 us
  Pallas kernels: 5.63 us -> 4.01 us
  waiting for transfers between devices: 12.3 us -> 10.7 us
    ppermute x11, starting transfers between devices: 10 us -> 11.9 us  [send(): return lax.ppermute(values, ALL, pairs)]
    ppermute x11, starting transfers between devices: 2.7 us -> 4.43 us  [swap(): lax.ppermute(values, ALL, [(i, i ^ 1) for i in range(lax.axis_size(ALL))])]
    pallas_call x9, Pallas kernels: 5.63 us -> 4.01 us  [call(): pl.pallas_call(kernel, out_shape=outs, in_specs=specs, out_specs=[pl.Bloc...]
    ppermute x11, waiting for transfers between devices: 10.5 us -> 8.92 us  [send(): return lax.ppermute(values, ALL, pairs)]
  transfers between devices with their start and end apart: 22 -> 22, of which waited for: 12 -> 10; matrix products, arithmetic and copies ran while one was open for 0% -> 0% of each run, Pallas kernels for 7% -> 6%
where the time goes in v22:
time: 32 us; the launch traced here: 31.9 us
  starting transfers between devices  16.3 us (51%)
  waiting for transfers between devices  10.7 us (33%)
  Pallas kernels  4.01 us (13%)
  between operations  0.74 us (2%)
    ppermute x11, starting transfers between devices, send(): return lax.ppermute(values, ALL, pairs)  11.9 us
    ppermute x11, waiting for transfers between devices, send(): return lax.ppermute(values, ALL, pairs)  8.92 us
    ppermute x11, starting transfers between devices, swap(): lax.ppermute(values, ALL, [(i, i ^ 1) for i in range(lax.axis_size(ALL))])  4.43 us
    pallas_call x9, Pallas kernels, call(): pl.pallas_call(kernel, out_shape=outs, in_specs=specs, out_specs=[pl.Bloc...  4.01 us
    ppermute x11, waiting for transfers between devices, swap(): lax.ppermute(values, ALL, [(i, i ^ 1) for i in range(lax.axis_size(ALL))])  1.82 us
  transfers between devices with their start and end apart: 22, of which 10 were waited for; matrix products, arithmetic and copies ran while one was open for 0% of the time, Pallas kernels for 6%

profile of v22, /device:TPU:0, one launch (start us, length us, event | category | flops | bytes accessed | tf_op | source)
XLA Modules:
  0.0 31.9 jit_solution(3697648133381089466)
XLA Ops:
  0.6 1.5 %shard_map.84 = (f32[1024,128]{1,0:T(8,128)S(1)}, f32[128,128]{1,0:T(8,128)S(1)}, f32[128,128]{1,0:T(8,128)S(1)}, f32[1,128]{1,0:T(1,128)S(1)}, f32[136,128]{1,0:T(8,128)S(1)}, /*index=5*/f32[8,128,128]{2,1,0:T(8,128)S(1)}) custom-call(f32[1024,128]{1,0:T(8,128)} %bitcast.3, f32[128,128]{1,0:T(8,128)} %c_hbm.1, f32[8,128]{1,0:T(8,128)} %b_hbm.1, ...), custom_call_target="tpu_custom_call" | custom-call | flops 201326592 | bytes 65536 | tf_op jit(solution)/shard_map/pallas_call | solution.py:63
  2.1 0.5 %collective-permute-start = (f32[136,128]{1,0:T(8,128)S(1)}, f32[136,128]{1,0:T(8,128)S(1)}, u32[]{:S(2)}, u32[]{:S(2)}) collective-permute-start(f32[136,128]{1,0:T(8,128)S(1)} %get-tuple-element.34), channel_id=1, source_target_pairs={{0,1},{1,0},{2,3},{3,2},{4,5},{5,4},{6,7},{7,6},{8,9},{9,8},{10,11... | collective-permute-start | bytes 208904 | tf_op jit(solution)/shard_map/ppermute | solution.py:100
  2.6 0.1 collective-permute-start.2
  2.7 0.4 %collective-permute-start.3 = (f32[1024,128]{1,0:T(8,128)S(1)}, f32[1024,128]{1,0:T(8,128)S(1)}, u32[]{:S(2)}, u32[]{:S(2)}) collective-permute-start(f32[1024,128]{1,0:T(8,128)S(1)} %get-tuple-element.40.refs_0_), channel_id=1, source_target_pairs={{0,1},{1,0},{2,3},{3,2},{4,5},{5,4},{6,7},{7,6},{8,9},{9,8},{10,11... | collective-permute-start | bytes 1572872 | tf_op jit(solution)/shard_map/ppermute | solution.py:100
  3.1 0.4 %collective-permute-done = f32[136,128]{1,0:T(8,128)S(1)} collective-permute-done((f32[136,128]{1,0:T(8,128)S(1)}, f32[136,128]{1,0:T(8,128)S(1)}, u32[]{:S(2)}, u32[]{:S(2)}) %collective-permute-start) | collective-permute-done | bytes 69664 | tf_op jit(solution)/shard_map/ppermute | solution.py:100
  3.6 2.7 %collective-permute-start.1 = (f32[144,128]{1,0:T(8,128)S(1)}, f32[144,128]{1,0:T(8,128)S(1)}, u32[]{:S(2)}, u32[]{:S(2)}) collective-permute-start(f32[144,128]{1,0:T(8,128)S(1)} %pad_maximum_fusion), channel_id=1, source_target_pairs={{0,3},{1,0},{2,1},{3,2},{4,7},{5,4},{6,5},{7,6},{8,9},{9,10},{10,1... | collective-permute-start | bytes 221192 | tf_op jit(solution)/shard_map/ppermute | solution.py:110
  6.3 0.2 shard_map.85
  6.5 1.8 %collective-permute-done.1 = f32[144,128]{1,0:T(8,128)S(1)} collective-permute-done((f32[144,128]{1,0:T(8,128)S(1)}, f32[144,128]{1,0:T(8,128)S(1)}, u32[]{:S(2)}, u32[]{:S(2)}) %collective-permute-start.1) | collective-permute-done | bytes 73760 | tf_op jit(solution)/shard_map/ppermute | solution.py:110
  8.3 0.0 collective-permute-done.2.refs_6_
  8.3 0.0 collective-permute-done.3.refs_7_.refs_1_
  8.3 1.2 %collective-permute-start.7 = (f32[88,128]{1,0:T(8,128)S(1)}, f32[88,128]{1,0:T(8,128)S(1)}, u32[]{:S(2)}, u32[]{:S(2)}) collective-permute-start(f32[88,128]{1,0:T(8,128)S(1)} %get-tuple-element.41), channel_id=1, source_target_pairs={{0,1},{1,20},{2,3},{3,22},{4,5},{5,16},{6,7},{7,18},{8,29},{9,8},{... | collective-permute-start | bytes 135176 | tf_op jit(solution)/shard_map/ppermute | solution.py:110
  9.5 2.5 %collective-permute-start.6 = (f32[88,128]{1,0:T(8,128)S(1)}, f32[88,128]{1,0:T(8,128)S(1)}, u32[]{:S(2)}, u32[]{:S(2)}) collective-permute-start(f32[88,128]{1,0:T(8,128)S(1)} %get-tuple-element.41), channel_id=1, source_target_pairs={{0,1},{1,16},{2,3},{3,18},{4,5},{5,20},{6,7},{7,22},{8,25},{9,8},{... | collective-permute-start | bytes 135176 | tf_op jit(solution)/shard_map/ppermute | solution.py:110
  12.0 0.4 %collective-permute-start.5 = (f32[88,128]{1,0:T(8,128)S(1)}, f32[88,128]{1,0:T(8,128)S(1)}, u32[]{:S(2)}, u32[]{:S(2)}) collective-permute-start(f32[88,128]{1,0:T(8,128)S(1)} %get-tuple-element.41), channel_id=1, source_target_pairs={{0,1},{1,4},{2,3},{3,6},{4,5},{5,0},{6,7},{7,2},{8,13},{9,8},{10,1... | collective-permute-start | bytes 135176 | tf_op jit(solution)/shard_map/ppermute | solution.py:110
  12.4 0.2 collective-permute-start.4
  12.7 0.3 collective-permute-start.10
  13.0 1.6 %collective-permute-done.7 = f32[88,128]{1,0:T(8,128)S(1)} collective-permute-done((f32[88,128]{1,0:T(8,128)S(1)}, f32[88,128]{1,0:T(8,128)S(1)}, u32[]{:S(2)}, u32[]{:S(2)}) %collective-permute-start.7) | collective-permute-done | bytes 45088 | tf_op jit(solution)/shard_map/ppermute | solution.py:110
  14.6 0.0 collective-permute-done.6
  14.6 0.9 %collective-permute-done.5 = f32[88,128]{1,0:T(8,128)S(1)} collective-permute-done((f32[88,128]{1,0:T(8,128)S(1)}, f32[88,128]{1,0:T(8,128)S(1)}, u32[]{:S(2)}, u32[]{:S(2)}) %collective-permute-start.5) | collective-permute-done | bytes 45088 | tf_op jit(solution)/shard_map/ppermute | solution.py:110
  15.5 0.0 collective-permute-done.4
  15.5 0.4 %collective-permute-start.9 = (f32[88,128]{1,0:T(8,128)S(1)}, f32[88,128]{1,0:T(8,128)S(1)}, u32[]{:S(2)}, u32[]{:S(2)}) collective-permute-start(f32[88,128]{1,0:T(8,128)S(1)} %add_add_fusion.1), channel_id=1, source_target_pairs={{0,8},{1,0},{2,10},{3,2},{4,12},{5,4},{6,14},{7,6},{8,9},{9,1},{10... | collective-permute-start | bytes 135176 | tf_op jit(solution)/shard_map/ppermute | solution.py:110
  15.9 0.2 collective-permute-start.8
  16.1 0.0 collective-permute-done.10.refs_3_.mate_moved
  16.1 1.5 %collective-permute-done.9 = f32[88,128]{1,0:T(8,128)S(1)} collective-permute-done((f32[88,128]{1,0:T(8,128)S(1)}, f32[88,128]{1,0:T(8,128)S(1)}, u32[]{:S(2)}, u32[]{:S(2)}) %collective-permute-start.9) | collective-permute-done | bytes 45088 | tf_op jit(solution)/shard_map/ppermute | solution.py:110
  17.6 0.0 collective-permute-done.8
  17.6 1.2 %collective-permute-start.14 = (f32[144,128]{1,0:T(8,128)S(1)}, f32[144,128]{1,0:T(8,128)S(1)}, u32[]{:S(2)}, u32[]{:S(2)}) collective-permute-start(f32[144,128]{1,0:T(8,128)S(1)} %get-tuple-element.44), channel_id=1, source_target_pairs={{0,1},{1,11},{2,3},{3,9},{4,5},{5,15},{6,7},{7,13},{8,2},{9,8},{10... | collective-permute-start | bytes 221192 | tf_op jit(solution)/shard_map/ppermute | solution.py:110
  18.9 0.5 %collective-permute-start.13 = (f32[144,128]{1,0:T(8,128)S(1)}, f32[144,128]{1,0:T(8,128)S(1)}, u32[]{:S(2)}, u32[]{:S(2)}) collective-permute-start(f32[144,128]{1,0:T(8,128)S(1)} %get-tuple-element.44), channel_id=1, source_target_pairs={{0,1},{1,9},{2,3},{3,11},{4,5},{5,13},{6,7},{7,15},{8,0},{9,8},{10... | collective-permute-start | bytes 221192 | tf_op jit(solution)/shard_map/ppermute | solution.py:110
  19.4 1.2 %collective-permute-start.12 = (f32[144,128]{1,0:T(8,128)S(1)}, f32[144,128]{1,0:T(8,128)S(1)}, u32[]{:S(2)}, u32[]{:S(2)}) collective-permute-start(f32[144,128]{1,0:T(8,128)S(1)} %get-tuple-element.44), channel_id=1, source_target_pairs={{0,1},{1,2},{2,3},{3,0},{4,5},{5,6},{6,7},{7,4},{8,11},{9,8},{10,9... | collective-permute-start | bytes 221192 | tf_op jit(solution)/shard_map/ppermute | solution.py:110
  20.6 0.0 collective-permute-start.11
  20.6 0.5 %collective-permute-start.20 = (f32[128,128]{1,0:T(8,128)S(1)}, f32[128,128]{1,0:T(8,128)S(1)}, u32[]{:S(2)}, u32[]{:S(2)}) collective-permute-start(f32[128,128]{1,0:T(8,128)S(1)} %get-tuple-element.47.gram), channel_id=1, source_target_pairs={{0,1},{1,0},{2,3},{3,2},{4,5},{5,4},{6,7},{7,6},{8,9},{9,8},{10,11... | collective-permute-start | bytes 196616 | tf_op jit(solution)/shard_map/ppermute | solution.py:100
  21.1 2.4 %collective-permute-done.14.refs_3_ = f32[144,128]{1,0:T(8,128)S(1)} collective-permute-done((f32[144,128]{1,0:T(8,128)S(1)}, f32[144,128]{1,0:T(8,128)S(1)}, u32[]{:S(2)}, u32[]{:S(2)}) %collective-permute-start.14) | collective-permute-done | bytes 73760 | tf_op jit(solution)/shard_map/ppermute | solution.py:110
  23.5 0.1 collective-permute-done.13.refs_2_
  23.6 0.6 %collective-permute-done.12.refs_1_ = f32[144,128]{1,0:T(8,128)S(1)} collective-permute-done((f32[144,128]{1,0:T(8,128)S(1)}, f32[144,128]{1,0:T(8,128)S(1)}, u32[]{:S(2)}, u32[]{:S(2)}) %collective-permute-start.12) | collective-permute-done | bytes 73760 | tf_op jit(solution)/shard_map/ppermute | solution.py:110
  24.2 0.0 collective-permute-done.11.refs_0_
  24.3 0.2 collective-permute-start.18
  24.4 1.5 %collective-permute-start.17 = (f32[128,128]{1,0:T(8,128)S(1)}, f32[128,128]{1,0:T(8,128)S(1)}, u32[]{:S(2)}, u32[]{:S(2)}) collective-permute-start(f32[128,128]{1,0:T(8,128)S(1)} %get-tuple-element.45), channel_id=1, source_target_pairs={{0,17},{1,0},{2,19},{3,2},{4,21},{5,4},{6,23},{7,6},{8,9},{9,24},{... | collective-permute-start | bytes 196616 | tf_op jit(solution)/shard_map/ppermute | solution.py:110
  26.0 0.0 collective-permute-start.16
  26.0 0.5 %collective-permute-start.15 = (f32[128,128]{1,0:T(8,128)S(1)}, f32[128,128]{1,0:T(8,128)S(1)}, u32[]{:S(2)}, u32[]{:S(2)}) collective-permute-start(f32[128,128]{1,0:T(8,128)S(1)} %get-tuple-element.45), channel_id=1, source_target_pairs={{0,1},{1,0},{2,3},{3,2},{4,5},{5,4},{6,7},{7,6},{8,9},{9,8},{10,11... | collective-permute-start | bytes 196616 | tf_op jit(solution)/shard_map/ppermute | solution.py:100
  26.5 0.0 collective-permute-done.20.mate_gram
  26.5 0.0 collective-permute-start.19
  26.5 0.7 %shard_map.90 = (f32[128,128]{1,0:T(8,128)}, f32[1,128]{1,0:T(1,128)S(1)}, f32[128,128]{1,0:T(8,128)S(1)}) custom-call(f32[128,128]{1,0:T(8,128)S(1)} %get-tuple-element.47.gram, f32[128,128]{1,0:T(8,128)S(1)} %collective-permute-done.20.mate_gram, f32[128,128]{1,0:T(8,128)S(1)} %get-tuple-element.43.refs_2_.moved, ...), custom_call_target="tpu_custom_call" | custom-call | flops 131072 | bytes 65536 | tf_op jit(solution)/shard_map/pallas_call | solution.py:63
  27.2 0.5 %collective-permute-done.19.mate_rows = f32[32,128]{1,0:T(8,128)S(1)} collective-permute-done((f32[32,128]{1,0:T(8,128)S(1)}, f32[32,128]{1,0:T(8,128)S(1)}, u32[]{:S(2)}, u32[]{:S(2)}) %collective-permute-start.19) | collective-permute-done | bytes 16416 | tf_op jit(solution)/shard_map/ppermute | solution.py:100
  27.7 0.9 %shard_map.91 = (f32[8,128]{1,0:T(8,128)}, f32[128,128]{1,0:T(8,128)S(1)}, f32[1,128]{1,0:T(1,128)S(1)}, f32[1,128]{1,0:T(1,128)S(1)}) custom-call(f32[32,128]{1,0:T(8,128)S(1)} %get-tuple-element.46.rows, f32[32,128]{1,0:T(8,128)S(1)} %collective-permute-done.19.mate_rows, f32[128,128]{1,0:T(8,128)S(1)} %get-tuple-element.37.c, ...), custom_call_target="tpu_custom_call" | custom-call | flops 16777216 | bytes 65536 | tf_op jit(solution)/shard_map/pallas_call | solution.py:63
  28.5 0.0 collective-permute-done.18
  28.5 0.0 collective-permute-done.17
  28.6 0.0 collective-permute-done.16
  28.6 1.7 %collective-permute-start.21 = (f32[128,128]{1,0:T(8,128)S(1)}, f32[128,128]{1,0:T(8,128)S(1)}, u32[]{:S(2)}, u32[]{:S(2)}) collective-permute-start(f32[128,128]{1,0:T(8,128)S(1)} %add_add_fusion.terms), channel_id=1, source_target_pairs={{0,1},{1,0},{2,3},{3,2},{4,5},{5,4},{6,7},{7,6},{8,9},{9,8},{10,11... | collective-permute-start | bytes 196616 | tf_op jit(solution)/shard_map/ppermute | solution.py:100
  30.3 0.9 %collective-permute-done.21.mate_terms = f32[128,128]{1,0:T(8,128)S(1)} collective-permute-done((f32[128,128]{1,0:T(8,128)S(1)}, f32[128,128]{1,0:T(8,128)S(1)}, u32[]{:S(2)}, u32[]{:S(2)}) %collective-permute-start.21) | collective-permute-done | bytes 65568 | tf_op jit(solution)/shard_map/ppermute | solution.py:100
  31.2 0.7 %shard_map.92 = (f32[128,128]{1,0:T(8,128)}, f32[1,128]{1,0:T(1,128)}) custom-call(f32[128,128]{1,0:T(8,128)S(1)} %add_add_fusion.terms, f32[128,128]{1,0:T(8,128)S(1)} %collective-permute-done.21.mate_terms, f32[128,128]{1,0:T(8,128)S(1)} %get-tuple-element.59.base, f32[1,128]{1,0:T(1,128)S(1)} %get-tuple-element.60.gain, f32[1,128]{1,0:T(1,128)S(1)} %get-tuple-element.61.scale), custom_call_target="tpu_custom_call" | custom-call | flops 131072 | bytes 65536 | tf_op jit(solution)/shard_map/pallas_call | solution.py:63
  (15 shorter events, 0.2 us)
Async XLA Ops:
  2.1 1.4 %collective-permute-start = (f32[136,128]{1,0:T(8,128)S(1)}, f32[136,128]{1,0:T(8,128)S(1)}, u32[]{:S(2)}, u32[]{:S(2)}) collective-permute-start(f32[136,128]{1,0:T(8,128)S(1)} %get-tuple-element.34), channel_id=1, source_target_pairs={{0,1},{1,0},{2,3},{3,2},{4,5},{5,4},{6,7},{7,6},{8,9},{9,8},{10,11... | collective-permute-start | bytes 208904 | tf_op jit(solution)/shard_map/ppermute | solution.py:100
  2.6 5.6 %collective-permute-start.2 = (f32[8,128,128]{2,1,0:T(8,128)S(1)}, f32[8,128,128]{2,1,0:T(8,128)S(1)}, u32[]{:S(2)}, u32[]{:S(2)}) collective-permute-start(f32[8,128,128]{2,1,0:T(8,128)S(1)} %get-tuple-element.39.refs_5_), channel_id=1, source_target_pairs={{0,1},{1,0},{2,3},{3,2},{4,5},{5,4},{6,7},{7,6},{8,9},{9,8},{10,11... | collective-permute-start | bytes 1572872 | tf_op jit(solution)/shard_map/ppermute | solution.py:100
  2.7 5.6 %collective-permute-start.3 = (f32[1024,128]{1,0:T(8,128)S(1)}, f32[1024,128]{1,0:T(8,128)S(1)}, u32[]{:S(2)}, u32[]{:S(2)}) collective-permute-start(f32[1024,128]{1,0:T(8,128)S(1)} %get-tuple-element.40.refs_0_), channel_id=1, source_target_pairs={{0,1},{1,0},{2,3},{3,2},{4,5},{5,4},{6,7},{7,6},{8,9},{9,8},{10,11... | collective-permute-start | bytes 1572872 | tf_op jit(solution)/shard_map/ppermute | solution.py:100
  3.6 4.7 %collective-permute-start.1 = (f32[144,128]{1,0:T(8,128)S(1)}, f32[144,128]{1,0:T(8,128)S(1)}, u32[]{:S(2)}, u32[]{:S(2)}) collective-permute-start(f32[144,128]{1,0:T(8,128)S(1)} %pad_maximum_fusion), channel_id=1, source_target_pairs={{0,3},{1,0},{2,1},{3,2},{4,7},{5,4},{6,5},{7,6},{8,9},{9,10},{10,1... | collective-permute-start | bytes 221192 | tf_op jit(solution)/shard_map/ppermute | solution.py:110
  8.3 6.3 %collective-permute-start.7 = (f32[88,128]{1,0:T(8,128)S(1)}, f32[88,128]{1,0:T(8,128)S(1)}, u32[]{:S(2)}, u32[]{:S(2)}) collective-permute-start(f32[88,128]{1,0:T(8,128)S(1)} %get-tuple-element.41), channel_id=1, source_target_pairs={{0,1},{1,20},{2,3},{3,22},{4,5},{5,16},{6,7},{7,18},{8,29},{9,8},{... | collective-permute-start | bytes 135176 | tf_op jit(solution)/shard_map/ppermute | solution.py:110
  9.5 5.1 %collective-permute-start.6 = (f32[88,128]{1,0:T(8,128)S(1)}, f32[88,128]{1,0:T(8,128)S(1)}, u32[]{:S(2)}, u32[]{:S(2)}) collective-permute-start(f32[88,128]{1,0:T(8,128)S(1)} %get-tuple-element.41), channel_id=1, source_target_pairs={{0,1},{1,16},{2,3},{3,18},{4,5},{5,20},{6,7},{7,22},{8,25},{9,8},{... | collective-permute-start | bytes 135176 | tf_op jit(solution)/shard_map/ppermute | solution.py:110
  12.0 3.5 %collective-permute-start.5 = (f32[88,128]{1,0:T(8,128)S(1)}, f32[88,128]{1,0:T(8,128)S(1)}, u32[]{:S(2)}, u32[]{:S(2)}) collective-permute-start(f32[88,128]{1,0:T(8,128)S(1)} %get-tuple-element.41), channel_id=1, source_target_pairs={{0,1},{1,4},{2,3},{3,6},{4,5},{5,0},{6,7},{7,2},{8,13},{9,8},{10,1... | collective-permute-start | bytes 135176 | tf_op jit(solution)/shard_map/ppermute | solution.py:110
  12.4 3.0 %collective-permute-start.4 = (f32[88,128]{1,0:T(8,128)S(1)}, f32[88,128]{1,0:T(8,128)S(1)}, u32[]{:S(2)}, u32[]{:S(2)}) collective-permute-start(f32[88,128]{1,0:T(8,128)S(1)} %get-tuple-element.41), channel_id=1, source_target_pairs={{0,1},{1,0},{2,3},{3,2},{4,5},{5,4},{6,7},{7,6},{8,9},{9,8},{10,11... | collective-permute-start | bytes 135176 | tf_op jit(solution)/shard_map/ppermute | solution.py:100
  12.7 3.4 %collective-permute-start.10 = (f32[128,128]{1,0:T(8,128)S(1)}, f32[128,128]{1,0:T(8,128)S(1)}, u32[]{:S(2)}, u32[]{:S(2)}) collective-permute-start(f32[128,128]{1,0:T(8,128)S(1)} %get-tuple-element.43.refs_2_.moved), channel_id=1, source_target_pairs={{0,1},{1,0},{2,3},{3,2},{4,5},{5,4},{6,7},{7,6},{8,9},{9,8},{10,11... | collective-permute-start | bytes 196616 | tf_op jit(solution)/shard_map/ppermute | solution.py:100
  15.5 2.1 %collective-permute-start.9 = (f32[88,128]{1,0:T(8,128)S(1)}, f32[88,128]{1,0:T(8,128)S(1)}, u32[]{:S(2)}, u32[]{:S(2)}) collective-permute-start(f32[88,128]{1,0:T(8,128)S(1)} %add_add_fusion.1), channel_id=1, source_target_pairs={{0,8},{1,0},{2,10},{3,2},{4,12},{5,4},{6,14},{7,6},{8,9},{9,1},{10... | collective-permute-start | bytes 135176 | tf_op jit(solution)/shard_map/ppermute | solution.py:110
  15.9 1.7 %collective-permute-start.8 = (f32[88,128]{1,0:T(8,128)S(1)}, f32[88,128]{1,0:T(8,128)S(1)}, u32[]{:S(2)}, u32[]{:S(2)}) collective-permute-start(f32[88,128]{1,0:T(8,128)S(1)} %add_add_fusion.1), channel_id=1, source_target_pairs={{0,1},{1,0},{2,3},{3,2},{4,5},{5,4},{6,7},{7,6},{8,9},{9,8},{10,11... | collective-permute-start | bytes 135176 | tf_op jit(solution)/shard_map/ppermute | solution.py:100
  17.6 5.9 %collective-permute-start.14 = (f32[144,128]{1,0:T(8,128)S(1)}, f32[144,128]{1,0:T(8,128)S(1)}, u32[]{:S(2)}, u32[]{:S(2)}) collective-permute-start(f32[144,128]{1,0:T(8,128)S(1)} %get-tuple-element.44), channel_id=1, source_target_pairs={{0,1},{1,11},{2,3},{3,9},{4,5},{5,15},{6,7},{7,13},{8,2},{9,8},{10... | collective-permute-start | bytes 221192 | tf_op jit(solution)/shard_map/ppermute | solution.py:110
  18.9 4.7 %collective-permute-start.13 = (f32[144,128]{1,0:T(8,128)S(1)}, f32[144,128]{1,0:T(8,128)S(1)}, u32[]{:S(2)}, u32[]{:S(2)}) collective-permute-start(f32[144,128]{1,0:T(8,128)S(1)} %get-tuple-element.44), channel_id=1, source_target_pairs={{0,1},{1,9},{2,3},{3,11},{4,5},{5,13},{6,7},{7,15},{8,0},{9,8},{10... | collective-permute-start | bytes 221192 | tf_op jit(solution)/shard_map/ppermute | solution.py:110
  19.4 4.8 %collective-permute-start.12 = (f32[144,128]{1,0:T(8,128)S(1)}, f32[144,128]{1,0:T(8,128)S(1)}, u32[]{:S(2)}, u32[]{:S(2)}) collective-permute-start(f32[144,128]{1,0:T(8,128)S(1)} %get-tuple-element.44), channel_id=1, source_target_pairs={{0,1},{1,2},{2,3},{3,0},{4,5},{5,6},{6,7},{7,4},{8,11},{9,8},{10,9... | collective-permute-start | bytes 221192 | tf_op jit(solution)/shard_map/ppermute | solution.py:110
  20.6 3.6 %collective-permute-start.11 = (f32[144,128]{1,0:T(8,128)S(1)}, f32[144,128]{1,0:T(8,128)S(1)}, u32[]{:S(2)}, u32[]{:S(2)}) collective-permute-start(f32[144,128]{1,0:T(8,128)S(1)} %get-tuple-element.44), channel_id=1, source_target_pairs={{0,1},{1,0},{2,3},{3,2},{4,5},{5,4},{6,7},{7,6},{8,9},{9,8},{10,11... | collective-permute-start | bytes 221192 | tf_op jit(solution)/shard_map/ppermute | solution.py:100
  20.6 5.9 %collective-permute-start.20 = (f32[128,128]{1,0:T(8,128)S(1)}, f32[128,128]{1,0:T(8,128)S(1)}, u32[]{:S(2)}, u32[]{:S(2)}) collective-permute-start(f32[128,128]{1,0:T(8,128)S(1)} %get-tuple-element.47.gram), channel_id=1, source_target_pairs={{0,1},{1,0},{2,3},{3,2},{4,5},{5,4},{6,7},{7,6},{8,9},{9,8},{10,11... | collective-permute-start | bytes 196616 | tf_op jit(solution)/shard_map/ppermute | solution.py:100
  24.3 4.3 %collective-permute-start.18 = (f32[128,128]{1,0:T(8,128)S(1)}, f32[128,128]{1,0:T(8,128)S(1)}, u32[]{:S(2)}, u32[]{:S(2)}) collective-permute-start(f32[128,128]{1,0:T(8,128)S(1)} %get-tuple-element.45), channel_id=1, source_target_pairs={{0,21},{1,0},{2,23},{3,2},{4,17},{5,4},{6,19},{7,6},{8,9},{9,28},{... | collective-permute-start | bytes 196616 | tf_op jit(solution)/shard_map/ppermute | solution.py:110
  24.4 4.1 %collective-permute-start.17 = (f32[128,128]{1,0:T(8,128)S(1)}, f32[128,128]{1,0:T(8,128)S(1)}, u32[]{:S(2)}, u32[]{:S(2)}) collective-permute-start(f32[128,128]{1,0:T(8,128)S(1)} %get-tuple-element.45), channel_id=1, source_target_pairs={{0,17},{1,0},{2,19},{3,2},{4,21},{5,4},{6,23},{7,6},{8,9},{9,24},{... | collective-permute-start | bytes 196616 | tf_op jit(solution)/shard_map/ppermute | solution.py:110
  26.0 2.6 %collective-permute-start.16 = (f32[128,128]{1,0:T(8,128)S(1)}, f32[128,128]{1,0:T(8,128)S(1)}, u32[]{:S(2)}, u32[]{:S(2)}) collective-permute-start(f32[128,128]{1,0:T(8,128)S(1)} %get-tuple-element.45), channel_id=1, source_target_pairs={{0,5},{1,0},{2,7},{3,2},{4,1},{5,4},{6,3},{7,6},{8,9},{9,12},{10,1... | collective-permute-start | bytes 196616 | tf_op jit(solution)/shard_map/ppermute | solution.py:110
  26.0 2.6 %collective-permute-start.15 = (f32[128,128]{1,0:T(8,128)S(1)}, f32[128,128]{1,0:T(8,128)S(1)}, u32[]{:S(2)}, u32[]{:S(2)}) collective-permute-start(f32[128,128]{1,0:T(8,128)S(1)} %get-tuple-element.45), channel_id=1, source_target_pairs={{0,1},{1,0},{2,3},{3,2},{4,5},{5,4},{6,7},{7,6},{8,9},{9,8},{10,11... | collective-permute-start | bytes 196616 | tf_op jit(solution)/shard_map/ppermute | solution.py:100
  26.5 1.2 %collective-permute-start.19 = (f32[32,128]{1,0:T(8,128)S(1)}, f32[32,128]{1,0:T(8,128)S(1)}, u32[]{:S(2)}, u32[]{:S(2)}) collective-permute-start(f32[32,128]{1,0:T(8,128)S(1)} %get-tuple-element.46.rows), channel_id=1, source_target_pairs={{0,1},{1,0},{2,3},{3,2},{4,5},{5,4},{6,7},{7,6},{8,9},{9,8},{10,11... | collective-permute-start | bytes 49160 | tf_op jit(solution)/shard_map/ppermute | solution.py:100
  28.6 2.6 %collective-permute-start.21 = (f32[128,128]{1,0:T(8,128)S(1)}, f32[128,128]{1,0:T(8,128)S(1)}, u32[]{:S(2)}, u32[]{:S(2)}) collective-permute-start(f32[128,128]{1,0:T(8,128)S(1)} %add_add_fusion.terms), channel_id=1, source_target_pairs={{0,1},{1,0},{2,3},{3,2},{4,5},{5,4},{6,7},{7,6},{8,9},{9,8},{10,11... | collective-permute-start | bytes 196616 | tf_op jit(solution)/shard_map/ppermute | solution.py:100

commit v23 on v19

--- a/solution.py
+++ b/solution.py
@@ -170,7 +170,7 @@
     chips, chip_rows = smp_count // 2, 2 * smp_rows
     chip_bits = bits_of(smp_count)[1:]
     vox_bits = [bit * smp_count for bit in bits_of(vox_count)]
-    pieces = 4 if flat_rows % 32 == 0 else 1
+    pieces = 1
     piece_rows = flat_rows // pieces
 
     def open_kernel(x_hbm, c_hbm, b_hbm, a_hbm, w_hbm, x, c, a, w, out, con, sems):
@@ -268,7 +268,7 @@
 
     mate_moved_a = swap(moved_a)
 
-    for group in groups_of(vox_bits[:1] + vox_bits[:0:-1]):
+    for group in groups_of(vox_bits[1:] + vox_bits[:1]):
         sums = tree(fan(sums, holder, masks_of(group)))
         holder ^= 1
     sample_role = holder

time: 31.6 us -> 32.6 us (1.032)
  waiting for transfers between devices: 12.3 us -> 12.9 us
  starting transfers between devices: 12.7 us -> 13.2 us
    ppermute x11, starting transfers between devices: 2.7 us -> 3.14 us  [swap(): lax.ppermute(values, ALL, [(i, i ^ 1) for i in range(lax.axis_size(ALL))])]
    ppermute x11, waiting for transfers between devices: 1.81 us -> 2.15 us  [swap(): lax.ppermute(values, ALL, [(i, i ^ 1) for i in range(lax.axis_size(ALL))])]
  transfers between devices with their start and end apart: 22 -> 22, of which waited for: 12 -> 11; matrix products, arithmetic and copies ran while one was open for 0% -> 0% of each run, Pallas kernels for 7% -> 7%
where the time goes in v23:
time: 32.6 us; the launch traced here: 32.5 us
  starting transfers between devices  13.2 us (40%)
  waiting for transfers between devices  12.9 us (40%)
  Pallas kernels  5.56 us (17%)
  between operations  0.74 us (2%)
    ppermute x11, waiting for transfers between devices, send(): return lax.ppermute(values, ALL, pairs)  10.7 us
    ppermute x11, starting transfers between devices, send(): return lax.ppermute(values, ALL, pairs)  10.1 us
    pallas_call x9, Pallas kernels, call(): pl.pallas_call(kernel, out_shape=outs, in_specs=specs, out_specs=[pl.Bloc...  5.56 us
    ppermute x11, starting transfers between devices, swap(): lax.ppermute(values, ALL, [(i, i ^ 1) for i in range(lax.axis_size(ALL))])  3.14 us
    ppermute x11, waiting for transfers between devices, swap(): lax.ppermute(values, ALL, [(i, i ^ 1) for i in range(lax.axis_size(ALL))])  2.15 us
  transfers between devices with their start and end apart: 22, of which 11 were waited for; matrix products, arithmetic and copies ran while one was open for 0% of the time, Pallas kernels for 7%

profile of v23, /device:TPU:0, one launch (start us, length us, event | category | flops | bytes accessed | tf_op | source)
XLA Modules:
  0.0 32.5 jit_solution(14322621484026081718)
XLA Ops:
  0.6 1.5 %shard_map.84 = (f32[1024,128]{1,0:T(8,128)S(1)}, f32[128,128]{1,0:T(8,128)S(1)}, f32[128,128]{1,0:T(8,128)S(1)}, f32[1,128]{1,0:T(1,128)S(1)}, f32[136,128]{1,0:T(8,128)S(1)}, /*index=5*/f32[8,128,128]{2,1,0:T(8,128)S(1)}) custom-call(f32[1024,128]{1,0:T(8,128)} %bitcast.3, f32[128,128]{1,0:T(8,128)} %c_hbm.1, f32[8,128]{1,0:T(8,128)} %b_hbm.1, ...), custom_call_target="tpu_custom_call" | custom-call | flops 201326592 | bytes 65536 | tf_op jit(solution)/shard_map/pallas_call | solution.py:63
  2.1 0.5 %collective-permute-start = (f32[136,128]{1,0:T(8,128)S(1)}, f32[136,128]{1,0:T(8,128)S(1)}, u32[]{:S(2)}, u32[]{:S(2)}) collective-permute-start(f32[136,128]{1,0:T(8,128)S(1)} %get-tuple-element.34), channel_id=1, source_target_pairs={{0,1},{1,0},{2,3},{3,2},{4,5},{5,4},{6,7},{7,6},{8,9},{9,8},{10,11... | collective-permute-start | bytes 208904 | tf_op jit(solution)/shard_map/ppermute | solution.py:100
  2.6 0.1 collective-permute-start.2
  2.7 0.4 %collective-permute-start.3 = (f32[1024,128]{1,0:T(8,128)S(1)}, f32[1024,128]{1,0:T(8,128)S(1)}, u32[]{:S(2)}, u32[]{:S(2)}) collective-permute-start(f32[1024,128]{1,0:T(8,128)S(1)} %get-tuple-element.40.refs_0_), channel_id=1, source_target_pairs={{0,1},{1,0},{2,3},{3,2},{4,5},{5,4},{6,7},{7,6},{8,9},{9,8},{10,11... | collective-permute-start | bytes 1572872 | tf_op jit(solution)/shard_map/ppermute | solution.py:100
  3.1 0.4 %collective-permute-done = f32[136,128]{1,0:T(8,128)S(1)} collective-permute-done((f32[136,128]{1,0:T(8,128)S(1)}, f32[136,128]{1,0:T(8,128)S(1)}, u32[]{:S(2)}, u32[]{:S(2)}) %collective-permute-start) | collective-permute-done | bytes 69664 | tf_op jit(solution)/shard_map/ppermute | solution.py:100
  3.6 0.4 %collective-permute-start.1 = (f32[144,128]{1,0:T(8,128)S(1)}, f32[144,128]{1,0:T(8,128)S(1)}, u32[]{:S(2)}, u32[]{:S(2)}) collective-permute-start(f32[144,128]{1,0:T(8,128)S(1)} %pad_maximum_fusion), channel_id=1, source_target_pairs={{0,1},{1,2},{2,3},{3,0},{4,5},{5,6},{6,7},{7,4},{8,11},{9,8},{10,9... | collective-permute-start | bytes 221192 | tf_op jit(solution)/shard_map/ppermute | solution.py:110
  4.0 0.2 shard_map.85
  4.2 4.1 %collective-permute-done.1 = f32[144,128]{1,0:T(8,128)S(1)} collective-permute-done((f32[144,128]{1,0:T(8,128)S(1)}, f32[144,128]{1,0:T(8,128)S(1)}, u32[]{:S(2)}, u32[]{:S(2)}) %collective-permute-start.1) | collective-permute-done | bytes 73760 | tf_op jit(solution)/shard_map/ppermute | solution.py:110
  8.3 0.0 collective-permute-done.2.refs_6_
  8.3 0.0 collective-permute-done.3.refs_7_.refs_1_
  8.3 0.7 %shard_map.86 = (f32[128,128]{1,0:T(8,128)S(1)}, f32[16,128]{1,0:T(8,128)S(1)}, f32[88,128]{1,0:T(8,128)S(1)}) custom-call(f32[128,128]{1,0:T(8,128)S(1)} %slice_add_fusion.refs_0_, f32[32,128]{1,0:T(8,128)S(1)} %pad_maximum_fusion.1.refs_1_, f32[128,128]{1,0:T(8,128)S(1)} %get-tuple-element.35.refs_2_, f32[1,128]{1,0:T(1,128)S(1)} %get-tuple-element.36.w.refs_3_.refs_2_, ...), custom_call_target="tpu_custom_call" | custom-call | flops 50331648 | bytes 65536 | tf_op jit(solution)/shard_map/pallas_call | solution.py:63
  9.1 2.9 %collective-permute-start.7 = (f32[88,128]{1,0:T(8,128)S(1)}, f32[88,128]{1,0:T(8,128)S(1)}, u32[]{:S(2)}, u32[]{:S(2)}) collective-permute-start(f32[88,128]{1,0:T(8,128)S(1)} %get-tuple-element.41), channel_id=1, source_target_pairs={{0,24},{1,0},{2,26},{3,2},{4,28},{5,4},{6,30},{7,6},{8,9},{9,17},{... | collective-permute-start | bytes 135176 | tf_op jit(solution)/shard_map/ppermute | solution.py:110
  12.0 0.3 %collective-permute-start.6 = (f32[88,128]{1,0:T(8,128)S(1)}, f32[88,128]{1,0:T(8,128)S(1)}, u32[]{:S(2)}, u32[]{:S(2)}) collective-permute-start(f32[88,128]{1,0:T(8,128)S(1)} %get-tuple-element.41), channel_id=1, source_target_pairs={{0,17},{1,0},{2,19},{3,2},{4,21},{5,4},{6,23},{7,6},{8,9},{9,24},{... | collective-permute-start | bytes 135176 | tf_op jit(solution)/shard_map/ppermute | solution.py:110
  12.3 0.0 collective-permute-start.5
  12.3 0.5 %collective-permute-start.4 = (f32[88,128]{1,0:T(8,128)S(1)}, f32[88,128]{1,0:T(8,128)S(1)}, u32[]{:S(2)}, u32[]{:S(2)}) collective-permute-start(f32[88,128]{1,0:T(8,128)S(1)} %get-tuple-element.41), channel_id=1, source_target_pairs={{0,1},{1,0},{2,3},{3,2},{4,5},{5,4},{6,7},{7,6},{8,9},{9,8},{10,11... | collective-permute-start | bytes 135176 | tf_op jit(solution)/shard_map/ppermute | solution.py:100
  12.8 0.0 collective-permute-start.10
  12.8 0.9 %collective-permute-done.7 = f32[88,128]{1,0:T(8,128)S(1)} collective-permute-done((f32[88,128]{1,0:T(8,128)S(1)}, f32[88,128]{1,0:T(8,128)S(1)}, u32[]{:S(2)}, u32[]{:S(2)}) %collective-permute-start.7) | collective-permute-done | bytes 45088 | tf_op jit(solution)/shard_map/ppermute | solution.py:110
  13.7 0.4 %collective-permute-done.6 = f32[88,128]{1,0:T(8,128)S(1)} collective-permute-done((f32[88,128]{1,0:T(8,128)S(1)}, f32[88,128]{1,0:T(8,128)S(1)}, u32[]{:S(2)}, u32[]{:S(2)}) %collective-permute-start.6) | collective-permute-done | bytes 45088 | tf_op jit(solution)/shard_map/ppermute | solution.py:110
  14.1 0.4 %collective-permute-done.5 = f32[88,128]{1,0:T(8,128)S(1)} collective-permute-done((f32[88,128]{1,0:T(8,128)S(1)}, f32[88,128]{1,0:T(8,128)S(1)}, u32[]{:S(2)}, u32[]{:S(2)}) %collective-permute-start.5) | collective-permute-done | bytes 45088 | tf_op jit(solution)/shard_map/ppermute | solution.py:110
  14.5 0.0 collective-permute-done.4
  14.6 1.3 %collective-permute-start.9 = (f32[88,128]{1,0:T(8,128)S(1)}, f32[88,128]{1,0:T(8,128)S(1)}, u32[]{:S(2)}, u32[]{:S(2)}) collective-permute-start(f32[88,128]{1,0:T(8,128)S(1)} %add_add_fusion.1), channel_id=1, source_target_pairs={{0,1},{1,4},{2,3},{3,6},{4,5},{5,0},{6,7},{7,2},{8,13},{9,8},{10,1... | collective-permute-start | bytes 135176 | tf_op jit(solution)/shard_map/ppermute | solution.py:110
  15.8 0.4 %collective-permute-start.8 = (f32[88,128]{1,0:T(8,128)S(1)}, f32[88,128]{1,0:T(8,128)S(1)}, u32[]{:S(2)}, u32[]{:S(2)}) collective-permute-start(f32[88,128]{1,0:T(8,128)S(1)} %add_add_fusion.1), channel_id=1, source_target_pairs={{0,1},{1,0},{2,3},{3,2},{4,5},{5,4},{6,7},{7,6},{8,9},{9,8},{10,11... | collective-permute-start | bytes 135176 | tf_op jit(solution)/shard_map/ppermute | solution.py:100
  16.2 0.0 collective-permute-done.10.refs_3_.mate_moved
  16.2 0.5 %shard_map.87.refs_4_ = f32[16,128,128]{2,1,0:T(8,128)S(1)} custom-call(f32[1024,128]{1,0:T(8,128)S(1)} %get-tuple-element.40.refs_0_, f32[1024,128]{1,0:T(8,128)S(1)} %collective-permute-done.3.refs_7_.refs_1_, f32[128,128]{1,0:T(8,128)S(1)} %get-tuple-element.43.refs_2_.moved, f32[128,128]{1,0:T(8,128)S(1)} %collective-permute-done.10.refs_3_.mate_moved), custom_call_target="tpu_custom_call" | custom-call | flops 402653184 | bytes 65536 | tf_op jit(solution)/shard_map/pallas_call | solution.py:63
  16.7 1.9 %collective-permute-done.9 = f32[88,128]{1,0:T(8,128)S(1)} collective-permute-done((f32[88,128]{1,0:T(8,128)S(1)}, f32[88,128]{1,0:T(8,128)S(1)}, u32[]{:S(2)}, u32[]{:S(2)}) %collective-permute-start.9) | collective-permute-done | bytes 45088 | tf_op jit(solution)/shard_map/ppermute | solution.py:110
  18.7 0.0 collective-permute-done.8
  18.7 0.4 %shard_map.88 = (f32[128,128]{1,0:T(8,128)S(1)}, f32[144,128]{1,0:T(8,128)S(1)}) custom-call(f32[88,128]{1,0:T(8,128)S(1)} %add.32.refs_0_, f32[16,128]{1,0:T(8,128)S(1)} %get-tuple-element.42.refs_1_, f32[1,128]{1,0:T(1,128)S(1)} %get-tuple-element.36.w.refs_3_.refs_2_, f32[128,128]{1,0:T(8,128)S(1)} %get-tuple-element.38.refs_4_.refs_3_, ...), custom_call_target="tpu_custom_call" | custom-call | flops 3145728 | bytes 65536 | tf_op jit(solution)/shard_map/pallas_call | solution.py:63
  19.0 0.7 %collective-permute-start.14 = (f32[144,128]{1,0:T(8,128)S(1)}, f32[144,128]{1,0:T(8,128)S(1)}, u32[]{:S(2)}, u32[]{:S(2)}) collective-permute-start(f32[144,128]{1,0:T(8,128)S(1)} %get-tuple-element.44), channel_id=1, source_target_pairs={{0,10},{1,0},{2,8},{3,2},{4,14},{5,4},{6,12},{7,6},{8,9},{9,3},{10... | collective-permute-start | bytes 221192 | tf_op jit(solution)/shard_map/ppermute | solution.py:110
  19.7 1.1 %collective-permute-start.13 = (f32[144,128]{1,0:T(8,128)S(1)}, f32[144,128]{1,0:T(8,128)S(1)}, u32[]{:S(2)}, u32[]{:S(2)}) collective-permute-start(f32[144,128]{1,0:T(8,128)S(1)} %get-tuple-element.44), channel_id=1, source_target_pairs={{0,8},{1,0},{2,10},{3,2},{4,12},{5,4},{6,14},{7,6},{8,9},{9,1},{10... | collective-permute-start | bytes 221192 | tf_op jit(solution)/shard_map/ppermute | solution.py:110
  20.8 0.0 collective-permute-start.12
  20.8 0.5 %collective-permute-start.11 = (f32[144,128]{1,0:T(8,128)S(1)}, f32[144,128]{1,0:T(8,128)S(1)}, u32[]{:S(2)}, u32[]{:S(2)}) collective-permute-start(f32[144,128]{1,0:T(8,128)S(1)} %get-tuple-element.44), channel_id=1, source_target_pairs={{0,1},{1,0},{2,3},{3,2},{4,5},{5,4},{6,7},{7,6},{8,9},{9,8},{10,11... | collective-permute-start | bytes 221192 | tf_op jit(solution)/shard_map/ppermute | solution.py:100
  21.3 0.0 collective-permute-start.20
  21.3 0.3 %collective-permute-done.14.refs_3_ = f32[144,128]{1,0:T(8,128)S(1)} collective-permute-done((f32[144,128]{1,0:T(8,128)S(1)}, f32[144,128]{1,0:T(8,128)S(1)}, u32[]{:S(2)}, u32[]{:S(2)}) %collective-permute-start.14) | collective-permute-done | bytes 73760 | tf_op jit(solution)/shard_map/ppermute | solution.py:110
  21.7 1.1 %collective-permute-done.13.refs_2_ = f32[144,128]{1,0:T(8,128)S(1)} collective-permute-done((f32[144,128]{1,0:T(8,128)S(1)}, f32[144,128]{1,0:T(8,128)S(1)}, u32[]{:S(2)}, u32[]{:S(2)}) %collective-permute-start.13) | collective-permute-done | bytes 73760 | tf_op jit(solution)/shard_map/ppermute | solution.py:110
  22.8 1.6 %collective-permute-start.18 = (f32[128,128]{1,0:T(8,128)S(1)}, f32[128,128]{1,0:T(8,128)S(1)}, u32[]{:S(2)}, u32[]{:S(2)}) collective-permute-start(f32[128,128]{1,0:T(8,128)S(1)} %get-tuple-element.45), channel_id=1, source_target_pairs={{0,1},{1,20},{2,3},{3,22},{4,5},{5,16},{6,7},{7,18},{8,29},{9,8},{... | collective-permute-start | bytes 196616 | tf_op jit(solution)/shard_map/ppermute | solution.py:110
  24.4 1.4 %collective-permute-start.17 = (f32[128,128]{1,0:T(8,128)S(1)}, f32[128,128]{1,0:T(8,128)S(1)}, u32[]{:S(2)}, u32[]{:S(2)}) collective-permute-start(f32[128,128]{1,0:T(8,128)S(1)} %get-tuple-element.45), channel_id=1, source_target_pairs={{0,1},{1,16},{2,3},{3,18},{4,5},{5,20},{6,7},{7,22},{8,25},{9,8},{... | collective-permute-start | bytes 196616 | tf_op jit(solution)/shard_map/ppermute | solution.py:110
  25.9 0.4 %collective-permute-start.16 = (f32[128,128]{1,0:T(8,128)S(1)}, f32[128,128]{1,0:T(8,128)S(1)}, u32[]{:S(2)}, u32[]{:S(2)}) collective-permute-start(f32[128,128]{1,0:T(8,128)S(1)} %get-tuple-element.45), channel_id=1, source_target_pairs={{0,1},{1,4},{2,3},{3,6},{4,5},{5,0},{6,7},{7,2},{8,13},{9,8},{10,1... | collective-permute-start | bytes 196616 | tf_op jit(solution)/shard_map/ppermute | solution.py:110
  26.2 0.6 %collective-permute-start.15 = (f32[128,128]{1,0:T(8,128)S(1)}, f32[128,128]{1,0:T(8,128)S(1)}, u32[]{:S(2)}, u32[]{:S(2)}) collective-permute-start(f32[128,128]{1,0:T(8,128)S(1)} %get-tuple-element.45), channel_id=1, source_target_pairs={{0,1},{1,0},{2,3},{3,2},{4,5},{5,4},{6,7},{7,6},{8,9},{9,8},{10,11... | collective-permute-start | bytes 196616 | tf_op jit(solution)/shard_map/ppermute | solution.py:100
  26.9 0.0 collective-permute-done.20.mate_gram
  26.9 0.0 collective-permute-start.19
  26.9 0.7 %shard_map.90 = (f32[128,128]{1,0:T(8,128)}, f32[1,128]{1,0:T(1,128)S(1)}, f32[128,128]{1,0:T(8,128)S(1)}) custom-call(f32[128,128]{1,0:T(8,128)S(1)} %get-tuple-element.47.gram, f32[128,128]{1,0:T(8,128)S(1)} %collective-permute-done.20.mate_gram, f32[128,128]{1,0:T(8,128)S(1)} %get-tuple-element.43.refs_2_.moved, ...), custom_call_target="tpu_custom_call" | custom-call | flops 131072 | bytes 65536 | tf_op jit(solution)/shard_map/pallas_call | solution.py:63
  27.6 0.5 %collective-permute-done.19.mate_rows = f32[32,128]{1,0:T(8,128)S(1)} collective-permute-done((f32[32,128]{1,0:T(8,128)S(1)}, f32[32,128]{1,0:T(8,128)S(1)}, u32[]{:S(2)}, u32[]{:S(2)}) %collective-permute-start.19) | collective-permute-done | bytes 16416 | tf_op jit(solution)/shard_map/ppermute | solution.py:100
  28.1 0.9 %shard_map.91 = (f32[8,128]{1,0:T(8,128)}, f32[128,128]{1,0:T(8,128)S(1)}, f32[1,128]{1,0:T(1,128)S(1)}, f32[1,128]{1,0:T(1,128)S(1)}) custom-call(f32[32,128]{1,0:T(8,128)S(1)} %get-tuple-element.46.rows, f32[32,128]{1,0:T(8,128)S(1)} %collective-permute-done.19.mate_rows, f32[128,128]{1,0:T(8,128)S(1)} %get-tuple-element.37.c, ...), custom_call_target="tpu_custom_call" | custom-call | flops 16777216 | bytes 65536 | tf_op jit(solution)/shard_map/pallas_call | solution.py:63
  28.9 1.5 %collective-permute-done.17 = f32[128,128]{1,0:T(8,128)S(1)} collective-permute-done((f32[128,128]{1,0:T(8,128)S(1)}, f32[128,128]{1,0:T(8,128)S(1)}, u32[]{:S(2)}, u32[]{:S(2)}) %collective-permute-start.17) | collective-permute-done | bytes 65568 | tf_op jit(solution)/shard_map/ppermute | solution.py:110
  30.4 0.0 collective-permute-done.15
  30.5 0.1 collective-permute-start.21
  30.5 1.2 %collective-permute-done.21.mate_terms = f32[128,128]{1,0:T(8,128)S(1)} collective-permute-done((f32[128,128]{1,0:T(8,128)S(1)}, f32[128,128]{1,0:T(8,128)S(1)}, u32[]{:S(2)}, u32[]{:S(2)}) %collective-permute-start.21) | collective-permute-done | bytes 65568 | tf_op jit(solution)/shard_map/ppermute | solution.py:100
  31.8 0.7 %shard_map.92 = (f32[128,128]{1,0:T(8,128)}, f32[1,128]{1,0:T(1,128)}) custom-call(f32[128,128]{1,0:T(8,128)S(1)} %add_add_fusion.terms, f32[128,128]{1,0:T(8,128)S(1)} %collective-permute-done.21.mate_terms, f32[128,128]{1,0:T(8,128)S(1)} %get-tuple-element.59.base, f32[1,128]{1,0:T(1,128)S(1)} %get-tuple-element.60.gain, f32[1,128]{1,0:T(1,128)S(1)} %get-tuple-element.61.scale), custom_call_target="tpu_custom_call" | custom-call | flops 131072 | bytes 65536 | tf_op jit(solution)/shard_map/pallas_call | solution.py:63
  (15 shorter events, 0.1 us)
Async XLA Ops:
  2.1 1.4 %collective-permute-start = (f32[136,128]{1,0:T(8,128)S(1)}, f32[136,128]{1,0:T(8,128)S(1)}, u32[]{:S(2)}, u32[]{:S(2)}) collective-permute-start(f32[136,128]{1,0:T(8,128)S(1)} %get-tuple-element.34), channel_id=1, source_target_pairs={{0,1},{1,0},{2,3},{3,2},{4,5},{5,4},{6,7},{7,6},{8,9},{9,8},{10,11... | collective-permute-start | bytes 208904 | tf_op jit(solution)/shard_map/ppermute | solution.py:100
  2.6 5.7 %collective-permute-start.2 = (f32[8,128,128]{2,1,0:T(8,128)S(1)}, f32[8,128,128]{2,1,0:T(8,128)S(1)}, u32[]{:S(2)}, u32[]{:S(2)}) collective-permute-start(f32[8,128,128]{2,1,0:T(8,128)S(1)} %get-tuple-element.39.refs_5_), channel_id=1, source_target_pairs={{0,1},{1,0},{2,3},{3,2},{4,5},{5,4},{6,7},{7,6},{8,9},{9,8},{10,11... | collective-permute-start | bytes 1572872 | tf_op jit(solution)/shard_map/ppermute | solution.py:100
  2.7 5.6 %collective-permute-start.3 = (f32[1024,128]{1,0:T(8,128)S(1)}, f32[1024,128]{1,0:T(8,128)S(1)}, u32[]{:S(2)}, u32[]{:S(2)}) collective-permute-start(f32[1024,128]{1,0:T(8,128)S(1)} %get-tuple-element.40.refs_0_), channel_id=1, source_target_pairs={{0,1},{1,0},{2,3},{3,2},{4,5},{5,4},{6,7},{7,6},{8,9},{9,8},{10,11... | collective-permute-start | bytes 1572872 | tf_op jit(solution)/shard_map/ppermute | solution.py:100
  3.6 4.7 %collective-permute-start.1 = (f32[144,128]{1,0:T(8,128)S(1)}, f32[144,128]{1,0:T(8,128)S(1)}, u32[]{:S(2)}, u32[]{:S(2)}) collective-permute-start(f32[144,128]{1,0:T(8,128)S(1)} %pad_maximum_fusion), channel_id=1, source_target_pairs={{0,1},{1,2},{2,3},{3,0},{4,5},{5,6},{6,7},{7,4},{8,11},{9,8},{10,9... | collective-permute-start | bytes 221192 | tf_op jit(solution)/shard_map/ppermute | solution.py:110
  9.1 4.6 %collective-permute-start.7 = (f32[88,128]{1,0:T(8,128)S(1)}, f32[88,128]{1,0:T(8,128)S(1)}, u32[]{:S(2)}, u32[]{:S(2)}) collective-permute-start(f32[88,128]{1,0:T(8,128)S(1)} %get-tuple-element.41), channel_id=1, source_target_pairs={{0,24},{1,0},{2,26},{3,2},{4,28},{5,4},{6,30},{7,6},{8,9},{9,17},{... | collective-permute-start | bytes 135176 | tf_op jit(solution)/shard_map/ppermute | solution.py:110
  12.0 2.1 %collective-permute-start.6 = (f32[88,128]{1,0:T(8,128)S(1)}, f32[88,128]{1,0:T(8,128)S(1)}, u32[]{:S(2)}, u32[]{:S(2)}) collective-permute-start(f32[88,128]{1,0:T(8,128)S(1)} %get-tuple-element.41), channel_id=1, source_target_pairs={{0,17},{1,0},{2,19},{3,2},{4,21},{5,4},{6,23},{7,6},{8,9},{9,24},{... | collective-permute-start | bytes 135176 | tf_op jit(solution)/shard_map/ppermute | solution.py:110
  12.3 2.2 %collective-permute-start.5 = (f32[88,128]{1,0:T(8,128)S(1)}, f32[88,128]{1,0:T(8,128)S(1)}, u32[]{:S(2)}, u32[]{:S(2)}) collective-permute-start(f32[88,128]{1,0:T(8,128)S(1)} %get-tuple-element.41), channel_id=1, source_target_pairs={{0,8},{1,0},{2,10},{3,2},{4,12},{5,4},{6,14},{7,6},{8,9},{9,1},{10... | collective-permute-start | bytes 135176 | tf_op jit(solution)/shard_map/ppermute | solution.py:110
  12.3 2.2 %collective-permute-start.4 = (f32[88,128]{1,0:T(8,128)S(1)}, f32[88,128]{1,0:T(8,128)S(1)}, u32[]{:S(2)}, u32[]{:S(2)}) collective-permute-start(f32[88,128]{1,0:T(8,128)S(1)} %get-tuple-element.41), channel_id=1, source_target_pairs={{0,1},{1,0},{2,3},{3,2},{4,5},{5,4},{6,7},{7,6},{8,9},{9,8},{10,11... | collective-permute-start | bytes 135176 | tf_op jit(solution)/shard_map/ppermute | solution.py:100
  12.8 3.4 %collective-permute-start.10 = (f32[128,128]{1,0:T(8,128)S(1)}, f32[128,128]{1,0:T(8,128)S(1)}, u32[]{:S(2)}, u32[]{:S(2)}) collective-permute-start(f32[128,128]{1,0:T(8,128)S(1)} %get-tuple-element.43.refs_2_.moved), channel_id=1, source_target_pairs={{0,1},{1,0},{2,3},{3,2},{4,5},{5,4},{6,7},{7,6},{8,9},{9,8},{10,11... | collective-permute-start | bytes 196616 | tf_op jit(solution)/shard_map/ppermute | solution.py:100
  14.6 4.1 %collective-permute-start.9 = (f32[88,128]{1,0:T(8,128)S(1)}, f32[88,128]{1,0:T(8,128)S(1)}, u32[]{:S(2)}, u32[]{:S(2)}) collective-permute-start(f32[88,128]{1,0:T(8,128)S(1)} %add_add_fusion.1), channel_id=1, source_target_pairs={{0,1},{1,4},{2,3},{3,6},{4,5},{5,0},{6,7},{7,2},{8,13},{9,8},{10,1... | collective-permute-start | bytes 135176 | tf_op jit(solution)/shard_map/ppermute | solution.py:110
  15.8 2.8 %collective-permute-start.8 = (f32[88,128]{1,0:T(8,128)S(1)}, f32[88,128]{1,0:T(8,128)S(1)}, u32[]{:S(2)}, u32[]{:S(2)}) collective-permute-start(f32[88,128]{1,0:T(8,128)S(1)} %add_add_fusion.1), channel_id=1, source_target_pairs={{0,1},{1,0},{2,3},{3,2},{4,5},{5,4},{6,7},{7,6},{8,9},{9,8},{10,11... | collective-permute-start | bytes 135176 | tf_op jit(solution)/shard_map/ppermute | solution.py:100
  19.0 2.6 %collective-permute-start.14 = (f32[144,128]{1,0:T(8,128)S(1)}, f32[144,128]{1,0:T(8,128)S(1)}, u32[]{:S(2)}, u32[]{:S(2)}) collective-permute-start(f32[144,128]{1,0:T(8,128)S(1)} %get-tuple-element.44), channel_id=1, source_target_pairs={{0,10},{1,0},{2,8},{3,2},{4,14},{5,4},{6,12},{7,6},{8,9},{9,3},{10... | collective-permute-start | bytes 221192 | tf_op jit(solution)/shard_map/ppermute | solution.py:110
  19.7 3.1 %collective-permute-start.13 = (f32[144,128]{1,0:T(8,128)S(1)}, f32[144,128]{1,0:T(8,128)S(1)}, u32[]{:S(2)}, u32[]{:S(2)}) collective-permute-start(f32[144,128]{1,0:T(8,128)S(1)} %get-tuple-element.44), channel_id=1, source_target_pairs={{0,8},{1,0},{2,10},{3,2},{4,12},{5,4},{6,14},{7,6},{8,9},{9,1},{10... | collective-permute-start | bytes 221192 | tf_op jit(solution)/shard_map/ppermute | solution.py:110
  20.8 2.0 %collective-permute-start.12 = (f32[144,128]{1,0:T(8,128)S(1)}, f32[144,128]{1,0:T(8,128)S(1)}, u32[]{:S(2)}, u32[]{:S(2)}) collective-permute-start(f32[144,128]{1,0:T(8,128)S(1)} %get-tuple-element.44), channel_id=1, source_target_pairs={{0,3},{1,0},{2,1},{3,2},{4,7},{5,4},{6,5},{7,6},{8,9},{9,10},{10,1... | collective-permute-start | bytes 221192 | tf_op jit(solution)/shard_map/ppermute | solution.py:110
  20.8 2.0 %collective-permute-start.11 = (f32[144,128]{1,0:T(8,128)S(1)}, f32[144,128]{1,0:T(8,128)S(1)}, u32[]{:S(2)}, u32[]{:S(2)}) collective-permute-start(f32[144,128]{1,0:T(8,128)S(1)} %get-tuple-element.44), channel_id=1, source_target_pairs={{0,1},{1,0},{2,3},{3,2},{4,5},{5,4},{6,7},{7,6},{8,9},{9,8},{10,11... | collective-permute-start | bytes 221192 | tf_op jit(solution)/shard_map/ppermute | solution.py:100
  21.3 5.5 %collective-permute-start.20 = (f32[128,128]{1,0:T(8,128)S(1)}, f32[128,128]{1,0:T(8,128)S(1)}, u32[]{:S(2)}, u32[]{:S(2)}) collective-permute-start(f32[128,128]{1,0:T(8,128)S(1)} %get-tuple-element.47.gram), channel_id=1, source_target_pairs={{0,1},{1,0},{2,3},{3,2},{4,5},{5,4},{6,7},{7,6},{8,9},{9,8},{10,11... | collective-permute-start | bytes 196616 | tf_op jit(solution)/shard_map/ppermute | solution.py:100
  22.8 6.1 %collective-permute-start.18 = (f32[128,128]{1,0:T(8,128)S(1)}, f32[128,128]{1,0:T(8,128)S(1)}, u32[]{:S(2)}, u32[]{:S(2)}) collective-permute-start(f32[128,128]{1,0:T(8,128)S(1)} %get-tuple-element.45), channel_id=1, source_target_pairs={{0,1},{1,20},{2,3},{3,22},{4,5},{5,16},{6,7},{7,18},{8,29},{9,8},{... | collective-permute-start | bytes 196616 | tf_op jit(solution)/shard_map/ppermute | solution.py:110
  24.4 6.0 %collective-permute-start.17 = (f32[128,128]{1,0:T(8,128)S(1)}, f32[128,128]{1,0:T(8,128)S(1)}, u32[]{:S(2)}, u32[]{:S(2)}) collective-permute-start(f32[128,128]{1,0:T(8,128)S(1)} %get-tuple-element.45), channel_id=1, source_target_pairs={{0,1},{1,16},{2,3},{3,18},{4,5},{5,20},{6,7},{7,22},{8,25},{9,8},{... | collective-permute-start | bytes 196616 | tf_op jit(solution)/shard_map/ppermute | solution.py:110
  25.9 4.6 %collective-permute-start.16 = (f32[128,128]{1,0:T(8,128)S(1)}, f32[128,128]{1,0:T(8,128)S(1)}, u32[]{:S(2)}, u32[]{:S(2)}) collective-permute-start(f32[128,128]{1,0:T(8,128)S(1)} %get-tuple-element.45), channel_id=1, source_target_pairs={{0,1},{1,4},{2,3},{3,6},{4,5},{5,0},{6,7},{7,2},{8,13},{9,8},{10,1... | collective-permute-start | bytes 196616 | tf_op jit(solution)/shard_map/ppermute | solution.py:110
  26.2 4.2 %collective-permute-start.15 = (f32[128,128]{1,0:T(8,128)S(1)}, f32[128,128]{1,0:T(8,128)S(1)}, u32[]{:S(2)}, u32[]{:S(2)}) collective-permute-start(f32[128,128]{1,0:T(8,128)S(1)} %get-tuple-element.45), channel_id=1, source_target_pairs={{0,1},{1,0},{2,3},{3,2},{4,5},{5,4},{6,7},{7,6},{8,9},{9,8},{10,11... | collective-permute-start | bytes 196616 | tf_op jit(solution)/shard_map/ppermute | solution.py:100
  26.9 1.2 %collective-permute-start.19 = (f32[32,128]{1,0:T(8,128)S(1)}, f32[32,128]{1,0:T(8,128)S(1)}, u32[]{:S(2)}, u32[]{:S(2)}) collective-permute-start(f32[32,128]{1,0:T(8,128)S(1)} %get-tuple-element.46.rows), channel_id=1, source_target_pairs={{0,1},{1,0},{2,3},{3,2},{4,5},{5,4},{6,7},{7,6},{8,9},{9,8},{10,11... | collective-permute-start | bytes 49160 | tf_op jit(solution)/shard_map/ppermute | solution.py:100
  30.5 1.3 %collective-permute-start.21 = (f32[128,128]{1,0:T(8,128)S(1)}, f32[128,128]{1,0:T(8,128)S(1)}, u32[]{:S(2)}, u32[]{:S(2)}) collective-permute-start(f32[128,128]{1,0:T(8,128)S(1)} %add_add_fusion.terms), channel_id=1, source_target_pairs={{0,1},{1,0},{2,3},{3,2},{4,5},{5,4},{6,7},{7,6},{8,9},{9,8},{10,11... | collective-permute-start | bytes 196616 | tf_op jit(solution)/shard_map/ppermute | solution.py:100

commit v24 on v19

--- a/solution.py
+++ b/solution.py
@@ -170,25 +170,20 @@
     chips, chip_rows = smp_count // 2, 2 * smp_rows
     chip_bits = bits_of(smp_count)[1:]
     vox_bits = [bit * smp_count for bit in bits_of(vox_count)]
-    pieces = 4 if flat_rows % 32 == 0 else 1
-    piece_rows = flat_rows // pieces
 
     def open_kernel(x_hbm, c_hbm, b_hbm, a_hbm, w_hbm, x, c, a, w, out, con, sems):
         copies = [pltpu.make_async_copy(c_hbm, c, sems.at[0])]
         copies += [pltpu.make_async_copy(b_hbm, out.at[pl.ds(vox_rows, smp_rows), :], sems.at[1])]
-        for n in range(pieces):
-            piece = pl.ds(n * piece_rows, piece_rows)
-            copies.append(pltpu.make_async_copy(x_hbm.at[piece, :], x.at[piece, :], sems.at[2 + n]))
-        copies.append(pltpu.make_async_copy(a_hbm, a, sems.at[2 + pieces]))
-        copies.append(pltpu.make_async_copy(w_hbm, w, sems.at[3 + pieces]))
+        copies.append(pltpu.make_async_copy(x_hbm, x, sems.at[2]))
+        copies.append(pltpu.make_async_copy(a_hbm, a, sems.at[3]))
+        copies.append(pltpu.make_async_copy(w_hbm, w, sems.at[4]))
         for copy in copies:
             copy.start()
         copies[0].wait()
         copies[1].wait()
         factor = both(c[...])
         b = out[pl.ds(vox_rows, smp_rows), :]
-        for n in range(pieces):
-            copies[2 + n].wait()
+        copies[2].wait()
         blocks = [x[pl.ds(j, vox_rows, stride=smp_rows), :] for j in range(smp_rows)]
         blocks = jnp.concatenate([halves(block, 1) for block in blocks], axis=0)
         made = fold(jnp.dot(blocks, factor, preferred_element_type=F32)).reshape(smp_rows, vox_rows, rank)
@@ -197,8 +192,8 @@
         for j in range(1, smp_rows):
             total = total + made[j] * b[j : j + 1, :]
         out[:vox_rows, :] = total
-        copies[2 + pieces].wait()
-        copies[3 + pieces].wait()
+        copies[3].wait()
+        copies[4].wait()
 
     x, c_near, a_near, w_row, opened, con = call(
         open_kernel,
@@ -212,7 +207,7 @@
         ),
         (ensemble.reshape(flat_rows, times), time_factor, sample_factor, voxel_factor, weights.reshape(1, rank)),
         2 * flat_rows * times * rank * 6,
-        scratch=(pltpu.SemaphoreType.DMA((4 + pieces,)),),
+        scratch=(pltpu.SemaphoreType.DMA((5,)),),
         in_hbm=5,
     )
 
@@ -222,7 +217,7 @@
         outer_c[...] = squared * dot_rows(c[...], c[...])
 
     outer, outer_c = call(
-        weigh_kernel, (near(rank, rank), near(rank, rank)), (c_near, w_row), 2 * rank * rank * times * 6
+        weigh_kernel, (near(rank, rank), near(rank, rank)), (c_near, w_row), 2 * rank * rank * times * 4
     )
 
     got = swap(opened)

time: 31.6 us -> 31.6 us (level)
  no operation moved by 1% of the time
where the time goes in v24:
time: 31.6 us; the launch traced here: 31.4 us
  starting transfers between devices  12.7 us (40%)
  waiting for transfers between devices  12.3 us (39%)
  Pallas kernels  5.56 us (18%)
  between operations  0.74 us (2%)
    ppermute x11, waiting for transfers between devices, send(): return lax.ppermute(values, ALL, pairs)  10.5 us
    ppermute x11, starting transfers between devices, send(): return lax.ppermute(values, ALL, pairs)  10 us
    pallas_call x9, Pallas kernels, call(): pl.pallas_call(kernel, out_shape=outs, in_specs=specs, out_specs=[pl.Bloc...  5.56 us
    ppermute x11, starting transfers between devices, swap(): lax.ppermute(values, ALL, [(i, i ^ 1) for i in range(lax.axis_size(ALL))])  2.7 us
    ppermute x11, waiting for transfers between devices, swap(): lax.ppermute(values, ALL, [(i, i ^ 1) for i in range(lax.axis_size(ALL))])  1.81 us
  transfers between devices with their start and end apart: 22, of which 12 were waited for; matrix products, arithmetic and copies ran while one was open for 0% of the time, Pallas kernels for 7%

profile of v24, /device:TPU:0, one launch (start us, length us, event | category | flops | bytes accessed | tf_op | source)
XLA Modules:
  0.0 31.4 jit_solution(5590116533512823184)
XLA Ops:
  0.6 1.5 %shard_map.84 = (f32[1024,128]{1,0:T(8,128)S(1)}, f32[128,128]{1,0:T(8,128)S(1)}, f32[128,128]{1,0:T(8,128)S(1)}, f32[1,128]{1,0:T(1,128)S(1)}, f32[136,128]{1,0:T(8,128)S(1)}, /*index=5*/f32[8,128,128]{2,1,0:T(8,128)S(1)}) custom-call(f32[1024,128]{1,0:T(8,128)} %bitcast.3, f32[128,128]{1,0:T(8,128)} %c_hbm.1, f32[8,128]{1,0:T(8,128)} %b_hbm.1, ...), custom_call_target="tpu_custom_call" | custom-call | flops 201326592 | bytes 65536 | tf_op jit(solution)/shard_map/pallas_call | solution.py:63
  2.1 0.5 %collective-permute-start = (f32[136,128]{1,0:T(8,128)S(1)}, f32[136,128]{1,0:T(8,128)S(1)}, u32[]{:S(2)}, u32[]{:S(2)}) collective-permute-start(f32[136,128]{1,0:T(8,128)S(1)} %get-tuple-element.34), channel_id=1, source_target_pairs={{0,1},{1,0},{2,3},{3,2},{4,5},{5,4},{6,7},{7,6},{8,9},{9,8},{10,11... | collective-permute-start | bytes 208904 | tf_op jit(solution)/shard_map/ppermute | solution.py:100
  2.6 0.1 collective-permute-start.2
  2.7 0.4 %collective-permute-start.3 = (f32[1024,128]{1,0:T(8,128)S(1)}, f32[1024,128]{1,0:T(8,128)S(1)}, u32[]{:S(2)}, u32[]{:S(2)}) collective-permute-start(f32[1024,128]{1,0:T(8,128)S(1)} %get-tuple-element.40.refs_0_), channel_id=1, source_target_pairs={{0,1},{1,0},{2,3},{3,2},{4,5},{5,4},{6,7},{7,6},{8,9},{9,8},{10,11... | collective-permute-start | bytes 1572872 | tf_op jit(solution)/shard_map/ppermute | solution.py:100
  3.1 0.4 %collective-permute-done = f32[136,128]{1,0:T(8,128)S(1)} collective-permute-done((f32[136,128]{1,0:T(8,128)S(1)}, f32[136,128]{1,0:T(8,128)S(1)}, u32[]{:S(2)}, u32[]{:S(2)}) %collective-permute-start) | collective-permute-done | bytes 69664 | tf_op jit(solution)/shard_map/ppermute | solution.py:100
  3.6 0.4 %collective-permute-start.1 = (f32[144,128]{1,0:T(8,128)S(1)}, f32[144,128]{1,0:T(8,128)S(1)}, u32[]{:S(2)}, u32[]{:S(2)}) collective-permute-start(f32[144,128]{1,0:T(8,128)S(1)} %pad_maximum_fusion), channel_id=1, source_target_pairs={{0,1},{1,2},{2,3},{3,0},{4,5},{5,6},{6,7},{7,4},{8,11},{9,8},{10,9... | collective-permute-start | bytes 221192 | tf_op jit(solution)/shard_map/ppermute | solution.py:110
  4.0 0.2 shard_map.85
  4.2 4.1 %collective-permute-done.1 = f32[144,128]{1,0:T(8,128)S(1)} collective-permute-done((f32[144,128]{1,0:T(8,128)S(1)}, f32[144,128]{1,0:T(8,128)S(1)}, u32[]{:S(2)}, u32[]{:S(2)}) %collective-permute-start.1) | collective-permute-done | bytes 73760 | tf_op jit(solution)/shard_map/ppermute | solution.py:110
  8.3 0.0 collective-permute-done.2.refs_6_
  8.3 0.0 collective-permute-done.3.refs_7_.refs_1_
  8.3 0.7 %shard_map.86 = (f32[128,128]{1,0:T(8,128)S(1)}, f32[16,128]{1,0:T(8,128)S(1)}, f32[88,128]{1,0:T(8,128)S(1)}) custom-call(f32[128,128]{1,0:T(8,128)S(1)} %slice_add_fusion.refs_0_, f32[32,128]{1,0:T(8,128)S(1)} %pad_maximum_fusion.1.refs_1_, f32[128,128]{1,0:T(8,128)S(1)} %get-tuple-element.35.refs_2_, f32[1,128]{1,0:T(1,128)S(1)} %get-tuple-element.36.w.refs_3_.refs_2_, ...), custom_call_target="tpu_custom_call" | custom-call | flops 50331648 | bytes 65536 | tf_op jit(solution)/shard_map/pallas_call | solution.py:63
  9.1 2.2 %collective-permute-start.7 = (f32[88,128]{1,0:T(8,128)S(1)}, f32[88,128]{1,0:T(8,128)S(1)}, u32[]{:S(2)}, u32[]{:S(2)}) collective-permute-start(f32[88,128]{1,0:T(8,128)S(1)} %get-tuple-element.41), channel_id=1, source_target_pairs={{0,21},{1,0},{2,23},{3,2},{4,17},{5,4},{6,19},{7,6},{8,9},{9,28},{... | collective-permute-start | bytes 135176 | tf_op jit(solution)/shard_map/ppermute | solution.py:110
  11.3 1.0 %collective-permute-start.6 = (f32[88,128]{1,0:T(8,128)S(1)}, f32[88,128]{1,0:T(8,128)S(1)}, u32[]{:S(2)}, u32[]{:S(2)}) collective-permute-start(f32[88,128]{1,0:T(8,128)S(1)} %get-tuple-element.41), channel_id=1, source_target_pairs={{0,17},{1,0},{2,19},{3,2},{4,21},{5,4},{6,23},{7,6},{8,9},{9,24},{... | collective-permute-start | bytes 135176 | tf_op jit(solution)/shard_map/ppermute | solution.py:110
  12.3 0.0 collective-permute-start.5
  12.3 0.5 %collective-permute-start.4 = (f32[88,128]{1,0:T(8,128)S(1)}, f32[88,128]{1,0:T(8,128)S(1)}, u32[]{:S(2)}, u32[]{:S(2)}) collective-permute-start(f32[88,128]{1,0:T(8,128)S(1)} %get-tuple-element.41), channel_id=1, source_target_pairs={{0,1},{1,0},{2,3},{3,2},{4,5},{5,4},{6,7},{7,6},{8,9},{9,8},{10,11... | collective-permute-start | bytes 135176 | tf_op jit(solution)/shard_map/ppermute | solution.py:100
  12.8 0.0 collective-permute-start.10
  12.8 0.2 collective-permute-done.7
  13.0 1.0 %collective-permute-done.6 = f32[88,128]{1,0:T(8,128)S(1)} collective-permute-done((f32[88,128]{1,0:T(8,128)S(1)}, f32[88,128]{1,0:T(8,128)S(1)}, u32[]{:S(2)}, u32[]{:S(2)}) %collective-permute-start.6) | collective-permute-done | bytes 45088 | tf_op jit(solution)/shard_map/ppermute | solution.py:110
  14.0 0.0 collective-permute-done.5
  14.0 1.7 %collective-permute-start.9 = (f32[88,128]{1,0:T(8,128)S(1)}, f32[88,128]{1,0:T(8,128)S(1)}, u32[]{:S(2)}, u32[]{:S(2)}) collective-permute-start(f32[88,128]{1,0:T(8,128)S(1)} %add_add_fusion.1), channel_id=1, source_target_pairs={{0,1},{1,9},{2,3},{3,11},{4,5},{5,13},{6,7},{7,15},{8,0},{9,8},{10... | collective-permute-start | bytes 135176 | tf_op jit(solution)/shard_map/ppermute | solution.py:110
  15.7 0.1 collective-permute-start.8
  15.8 0.0 collective-permute-done.10.refs_3_.mate_moved
  15.8 0.5 %shard_map.87.refs_4_ = f32[16,128,128]{2,1,0:T(8,128)S(1)} custom-call(f32[1024,128]{1,0:T(8,128)S(1)} %get-tuple-element.40.refs_0_, f32[1024,128]{1,0:T(8,128)S(1)} %collective-permute-done.3.refs_7_.refs_1_, f32[128,128]{1,0:T(8,128)S(1)} %get-tuple-element.43.refs_2_.moved, f32[128,128]{1,0:T(8,128)S(1)} %collective-permute-done.10.refs_3_.mate_moved), custom_call_target="tpu_custom_call" | custom-call | flops 402653184 | bytes 65536 | tf_op jit(solution)/shard_map/pallas_call | solution.py:63
  16.3 2.8 %collective-permute-done.9 = f32[88,128]{1,0:T(8,128)S(1)} collective-permute-done((f32[88,128]{1,0:T(8,128)S(1)}, f32[88,128]{1,0:T(8,128)S(1)}, u32[]{:S(2)}, u32[]{:S(2)}) %collective-permute-start.9) | collective-permute-done | bytes 45088 | tf_op jit(solution)/shard_map/ppermute | solution.py:110
  19.2 0.0 collective-permute-done.8
  19.2 0.4 %shard_map.88 = (f32[128,128]{1,0:T(8,128)S(1)}, f32[144,128]{1,0:T(8,128)S(1)}) custom-call(f32[88,128]{1,0:T(8,128)S(1)} %add.32.refs_0_, f32[16,128]{1,0:T(8,128)S(1)} %get-tuple-element.42.refs_1_, f32[1,128]{1,0:T(1,128)S(1)} %get-tuple-element.36.w.refs_3_.refs_2_, f32[128,128]{1,0:T(8,128)S(1)} %get-tuple-element.38.refs_4_.refs_3_, ...), custom_call_target="tpu_custom_call" | custom-call | flops 3145728 | bytes 65536 | tf_op jit(solution)/shard_map/pallas_call | solution.py:63
  19.5 0.2 collective-permute-start.14
  19.7 1.4 %collective-permute-start.12 = (f32[144,128]{1,0:T(8,128)S(1)}, f32[144,128]{1,0:T(8,128)S(1)}, u32[]{:S(2)}, u32[]{:S(2)}) collective-permute-start(f32[144,128]{1,0:T(8,128)S(1)} %get-tuple-element.44), channel_id=1, source_target_pairs={{0,3},{1,0},{2,1},{3,2},{4,7},{5,4},{6,5},{7,6},{8,9},{9,10},{10,1... | collective-permute-start | bytes 221192 | tf_op jit(solution)/shard_map/ppermute | solution.py:110
  21.1 0.0 collective-permute-start.11
  21.1 0.5 %collective-permute-start.20 = (f32[128,128]{1,0:T(8,128)S(1)}, f32[128,128]{1,0:T(8,128)S(1)}, u32[]{:S(2)}, u32[]{:S(2)}) collective-permute-start(f32[128,128]{1,0:T(8,128)S(1)} %get-tuple-element.47.gram), channel_id=1, source_target_pairs={{0,1},{1,0},{2,3},{3,2},{4,5},{5,4},{6,7},{7,6},{8,9},{9,8},{10,11... | collective-permute-start | bytes 196616 | tf_op jit(solution)/shard_map/ppermute | solution.py:100
  21.6 0.1 collective-permute-done.14.refs_3_
  21.7 0.7 %collective-permute-done.13.refs_2_ = f32[144,128]{1,0:T(8,128)S(1)} collective-permute-done((f32[144,128]{1,0:T(8,128)S(1)}, f32[144,128]{1,0:T(8,128)S(1)}, u32[]{:S(2)}, u32[]{:S(2)}) %collective-permute-start.13) | collective-permute-done | bytes 73760 | tf_op jit(solution)/shard_map/ppermute | solution.py:110
  22.4 0.7 %collective-permute-done.12.refs_1_ = f32[144,128]{1,0:T(8,128)S(1)} collective-permute-done((f32[144,128]{1,0:T(8,128)S(1)}, f32[144,128]{1,0:T(8,128)S(1)}, u32[]{:S(2)}, u32[]{:S(2)}) %collective-permute-start.12) | collective-permute-done | bytes 73760 | tf_op jit(solution)/shard_map/ppermute | solution.py:110
  23.1 1.0 %collective-permute-start.18 = (f32[128,128]{1,0:T(8,128)S(1)}, f32[128,128]{1,0:T(8,128)S(1)}, u32[]{:S(2)}, u32[]{:S(2)}) collective-permute-start(f32[128,128]{1,0:T(8,128)S(1)} %get-tuple-element.45), channel_id=1, source_target_pairs={{0,1},{1,20},{2,3},{3,22},{4,5},{5,16},{6,7},{7,18},{8,29},{9,8},{... | collective-permute-start | bytes 196616 | tf_op jit(solution)/shard_map/ppermute | solution.py:110
  24.1 1.6 %collective-permute-start.17 = (f32[128,128]{1,0:T(8,128)S(1)}, f32[128,128]{1,0:T(8,128)S(1)}, u32[]{:S(2)}, u32[]{:S(2)}) collective-permute-start(f32[128,128]{1,0:T(8,128)S(1)} %get-tuple-element.45), channel_id=1, source_target_pairs={{0,1},{1,16},{2,3},{3,18},{4,5},{5,20},{6,7},{7,22},{8,25},{9,8},{... | collective-permute-start | bytes 196616 | tf_op jit(solution)/shard_map/ppermute | solution.py:110
  25.7 0.6 %collective-permute-start.16 = (f32[128,128]{1,0:T(8,128)S(1)}, f32[128,128]{1,0:T(8,128)S(1)}, u32[]{:S(2)}, u32[]{:S(2)}) collective-permute-start(f32[128,128]{1,0:T(8,128)S(1)} %get-tuple-element.45), channel_id=1, source_target_pairs={{0,1},{1,4},{2,3},{3,6},{4,5},{5,0},{6,7},{7,2},{8,13},{9,8},{10,1... | collective-permute-start | bytes 196616 | tf_op jit(solution)/shard_map/ppermute | solution.py:110
  26.2 0.1 collective-permute-start.15
  26.4 0.0 collective-permute-done.20.mate_gram
  26.4 0.4 %collective-permute-start.19 = (f32[32,128]{1,0:T(8,128)S(1)}, f32[32,128]{1,0:T(8,128)S(1)}, u32[]{:S(2)}, u32[]{:S(2)}) collective-permute-start(f32[32,128]{1,0:T(8,128)S(1)} %get-tuple-element.46.rows), channel_id=1, source_target_pairs={{0,1},{1,0},{2,3},{3,2},{4,5},{5,4},{6,7},{7,6},{8,9},{9,8},{10,11... | collective-permute-start | bytes 49160 | tf_op jit(solution)/shard_map/ppermute | solution.py:100
  26.8 0.7 %shard_map.90 = (f32[128,128]{1,0:T(8,128)}, f32[1,128]{1,0:T(1,128)S(1)}, f32[128,128]{1,0:T(8,128)S(1)}) custom-call(f32[128,128]{1,0:T(8,128)S(1)} %get-tuple-element.47.gram, f32[128,128]{1,0:T(8,128)S(1)} %collective-permute-done.20.mate_gram, f32[128,128]{1,0:T(8,128)S(1)} %get-tuple-element.43.refs_2_.moved, ...), custom_call_target="tpu_custom_call" | custom-call | flops 131072 | bytes 65536 | tf_op jit(solution)/shard_map/pallas_call | solution.py:63
  27.4 0.2 collective-permute-done.19.mate_rows
  27.6 0.9 %shard_map.91 = (f32[8,128]{1,0:T(8,128)}, f32[128,128]{1,0:T(8,128)S(1)}, f32[1,128]{1,0:T(1,128)S(1)}, f32[1,128]{1,0:T(1,128)S(1)}) custom-call(f32[32,128]{1,0:T(8,128)S(1)} %get-tuple-element.46.rows, f32[32,128]{1,0:T(8,128)S(1)} %collective-permute-done.19.mate_rows, f32[128,128]{1,0:T(8,128)S(1)} %get-tuple-element.37.c, ...), custom_call_target="tpu_custom_call" | custom-call | flops 16777216 | bytes 65536 | tf_op jit(solution)/shard_map/pallas_call | solution.py:63
  28.5 0.2 collective-permute-done.18
  28.7 0.7 %collective-permute-done.17 = f32[128,128]{1,0:T(8,128)S(1)} collective-permute-done((f32[128,128]{1,0:T(8,128)S(1)}, f32[128,128]{1,0:T(8,128)S(1)}, u32[]{:S(2)}, u32[]{:S(2)}) %collective-permute-start.17) | collective-permute-done | bytes 65568 | tf_op jit(solution)/shard_map/ppermute | solution.py:110
  29.4 0.0 collective-permute-done.15
  29.4 0.1 collective-permute-start.21
  29.5 1.2 %collective-permute-done.21.mate_terms = f32[128,128]{1,0:T(8,128)S(1)} collective-permute-done((f32[128,128]{1,0:T(8,128)S(1)}, f32[128,128]{1,0:T(8,128)S(1)}, u32[]{:S(2)}, u32[]{:S(2)}) %collective-permute-start.21) | collective-permute-done | bytes 65568 | tf_op jit(solution)/shard_map/ppermute | solution.py:100
  30.7 0.7 %shard_map.92 = (f32[128,128]{1,0:T(8,128)}, f32[1,128]{1,0:T(1,128)}) custom-call(f32[128,128]{1,0:T(8,128)S(1)} %add_add_fusion.terms, f32[128,128]{1,0:T(8,128)S(1)} %collective-permute-done.21.mate_terms, f32[128,128]{1,0:T(8,128)S(1)} %get-tuple-element.59.base, f32[1,128]{1,0:T(1,128)S(1)} %get-tuple-element.60.gain, f32[1,128]{1,0:T(1,128)S(1)} %get-tuple-element.61.scale), custom_call_target="tpu_custom_call" | custom-call | flops 131072 | bytes 65536 | tf_op jit(solution)/shard_map/pallas_call | solution.py:63
  (15 shorter events, 0.1 us)
Async XLA Ops:
  2.1 1.4 %collective-permute-start = (f32[136,128]{1,0:T(8,128)S(1)}, f32[136,128]{1,0:T(8,128)S(1)}, u32[]{:S(2)}, u32[]{:S(2)}) collective-permute-start(f32[136,128]{1,0:T(8,128)S(1)} %get-tuple-element.34), channel_id=1, source_target_pairs={{0,1},{1,0},{2,3},{3,2},{4,5},{5,4},{6,7},{7,6},{8,9},{9,8},{10,11... | collective-permute-start | bytes 208904 | tf_op jit(solution)/shard_map/ppermute | solution.py:100
  2.6 5.7 %collective-permute-start.2 = (f32[8,128,128]{2,1,0:T(8,128)S(1)}, f32[8,128,128]{2,1,0:T(8,128)S(1)}, u32[]{:S(2)}, u32[]{:S(2)}) collective-permute-start(f32[8,128,128]{2,1,0:T(8,128)S(1)} %get-tuple-element.39.refs_5_), channel_id=1, source_target_pairs={{0,1},{1,0},{2,3},{3,2},{4,5},{5,4},{6,7},{7,6},{8,9},{9,8},{10,11... | collective-permute-start | bytes 1572872 | tf_op jit(solution)/shard_map/ppermute | solution.py:100
  2.7 5.6 %collective-permute-start.3 = (f32[1024,128]{1,0:T(8,128)S(1)}, f32[1024,128]{1,0:T(8,128)S(1)}, u32[]{:S(2)}, u32[]{:S(2)}) collective-permute-start(f32[1024,128]{1,0:T(8,128)S(1)} %get-tuple-element.40.refs_0_), channel_id=1, source_target_pairs={{0,1},{1,0},{2,3},{3,2},{4,5},{5,4},{6,7},{7,6},{8,9},{9,8},{10,11... | collective-permute-start | bytes 1572872 | tf_op jit(solution)/shard_map/ppermute | solution.py:100
  3.6 4.7 %collective-permute-start.1 = (f32[144,128]{1,0:T(8,128)S(1)}, f32[144,128]{1,0:T(8,128)S(1)}, u32[]{:S(2)}, u32[]{:S(2)}) collective-permute-start(f32[144,128]{1,0:T(8,128)S(1)} %pad_maximum_fusion), channel_id=1, source_target_pairs={{0,1},{1,2},{2,3},{3,0},{4,5},{5,6},{6,7},{7,4},{8,11},{9,8},{10,9... | collective-permute-start | bytes 221192 | tf_op jit(solution)/shard_map/ppermute | solution.py:110
  9.1 3.9 %collective-permute-start.7 = (f32[88,128]{1,0:T(8,128)S(1)}, f32[88,128]{1,0:T(8,128)S(1)}, u32[]{:S(2)}, u32[]{:S(2)}) collective-permute-start(f32[88,128]{1,0:T(8,128)S(1)} %get-tuple-element.41), channel_id=1, source_target_pairs={{0,21},{1,0},{2,23},{3,2},{4,17},{5,4},{6,19},{7,6},{8,9},{9,28},{... | collective-permute-start | bytes 135176 | tf_op jit(solution)/shard_map/ppermute | solution.py:110
  11.3 2.7 %collective-permute-start.6 = (f32[88,128]{1,0:T(8,128)S(1)}, f32[88,128]{1,0:T(8,128)S(1)}, u32[]{:S(2)}, u32[]{:S(2)}) collective-permute-start(f32[88,128]{1,0:T(8,128)S(1)} %get-tuple-element.41), channel_id=1, source_target_pairs={{0,17},{1,0},{2,19},{3,2},{4,21},{5,4},{6,23},{7,6},{8,9},{9,24},{... | collective-permute-start | bytes 135176 | tf_op jit(solution)/shard_map/ppermute | solution.py:110
  12.3 1.7 %collective-permute-start.5 = (f32[88,128]{1,0:T(8,128)S(1)}, f32[88,128]{1,0:T(8,128)S(1)}, u32[]{:S(2)}, u32[]{:S(2)}) collective-permute-start(f32[88,128]{1,0:T(8,128)S(1)} %get-tuple-element.41), channel_id=1, source_target_pairs={{0,5},{1,0},{2,7},{3,2},{4,1},{5,4},{6,3},{7,6},{8,9},{9,12},{10,1... | collective-permute-start | bytes 135176 | tf_op jit(solution)/shard_map/ppermute | solution.py:110
  12.3 1.7 %collective-permute-start.4 = (f32[88,128]{1,0:T(8,128)S(1)}, f32[88,128]{1,0:T(8,128)S(1)}, u32[]{:S(2)}, u32[]{:S(2)}) collective-permute-start(f32[88,128]{1,0:T(8,128)S(1)} %get-tuple-element.41), channel_id=1, source_target_pairs={{0,1},{1,0},{2,3},{3,2},{4,5},{5,4},{6,7},{7,6},{8,9},{9,8},{10,11... | collective-permute-start | bytes 135176 | tf_op jit(solution)/shard_map/ppermute | solution.py:100
  12.8 3.0 %collective-permute-start.10 = (f32[128,128]{1,0:T(8,128)S(1)}, f32[128,128]{1,0:T(8,128)S(1)}, u32[]{:S(2)}, u32[]{:S(2)}) collective-permute-start(f32[128,128]{1,0:T(8,128)S(1)} %get-tuple-element.43.refs_2_.moved), channel_id=1, source_target_pairs={{0,1},{1,0},{2,3},{3,2},{4,5},{5,4},{6,7},{7,6},{8,9},{9,8},{10,11... | collective-permute-start | bytes 196616 | tf_op jit(solution)/shard_map/ppermute | solution.py:100
  14.0 5.1 %collective-permute-start.9 = (f32[88,128]{1,0:T(8,128)S(1)}, f32[88,128]{1,0:T(8,128)S(1)}, u32[]{:S(2)}, u32[]{:S(2)}) collective-permute-start(f32[88,128]{1,0:T(8,128)S(1)} %add_add_fusion.1), channel_id=1, source_target_pairs={{0,1},{1,9},{2,3},{3,11},{4,5},{5,13},{6,7},{7,15},{8,0},{9,8},{10... | collective-permute-start | bytes 135176 | tf_op jit(solution)/shard_map/ppermute | solution.py:110
  15.7 3.4 %collective-permute-start.8 = (f32[88,128]{1,0:T(8,128)S(1)}, f32[88,128]{1,0:T(8,128)S(1)}, u32[]{:S(2)}, u32[]{:S(2)}) collective-permute-start(f32[88,128]{1,0:T(8,128)S(1)} %add_add_fusion.1), channel_id=1, source_target_pairs={{0,1},{1,0},{2,3},{3,2},{4,5},{5,4},{6,7},{7,6},{8,9},{9,8},{10,11... | collective-permute-start | bytes 135176 | tf_op jit(solution)/shard_map/ppermute | solution.py:100
  19.5 2.2 %collective-permute-start.14 = (f32[144,128]{1,0:T(8,128)S(1)}, f32[144,128]{1,0:T(8,128)S(1)}, u32[]{:S(2)}, u32[]{:S(2)}) collective-permute-start(f32[144,128]{1,0:T(8,128)S(1)} %get-tuple-element.44), channel_id=1, source_target_pairs={{0,10},{1,0},{2,8},{3,2},{4,14},{5,4},{6,12},{7,6},{8,9},{9,3},{10... | collective-permute-start | bytes 221192 | tf_op jit(solution)/shard_map/ppermute | solution.py:110
  19.7 2.7 %collective-permute-start.13 = (f32[144,128]{1,0:T(8,128)S(1)}, f32[144,128]{1,0:T(8,128)S(1)}, u32[]{:S(2)}, u32[]{:S(2)}) collective-permute-start(f32[144,128]{1,0:T(8,128)S(1)} %get-tuple-element.44), channel_id=1, source_target_pairs={{0,8},{1,0},{2,10},{3,2},{4,12},{5,4},{6,14},{7,6},{8,9},{9,1},{10... | collective-permute-start | bytes 221192 | tf_op jit(solution)/shard_map/ppermute | solution.py:110
  19.7 3.4 %collective-permute-start.12 = (f32[144,128]{1,0:T(8,128)S(1)}, f32[144,128]{1,0:T(8,128)S(1)}, u32[]{:S(2)}, u32[]{:S(2)}) collective-permute-start(f32[144,128]{1,0:T(8,128)S(1)} %get-tuple-element.44), channel_id=1, source_target_pairs={{0,3},{1,0},{2,1},{3,2},{4,7},{5,4},{6,5},{7,6},{8,9},{9,10},{10,1... | collective-permute-start | bytes 221192 | tf_op jit(solution)/shard_map/ppermute | solution.py:110
  21.1 2.0 %collective-permute-start.11 = (f32[144,128]{1,0:T(8,128)S(1)}, f32[144,128]{1,0:T(8,128)S(1)}, u32[]{:S(2)}, u32[]{:S(2)}) collective-permute-start(f32[144,128]{1,0:T(8,128)S(1)} %get-tuple-element.44), channel_id=1, source_target_pairs={{0,1},{1,0},{2,3},{3,2},{4,5},{5,4},{6,7},{7,6},{8,9},{9,8},{10,11... | collective-permute-start | bytes 221192 | tf_op jit(solution)/shard_map/ppermute | solution.py:100
  21.1 5.3 %collective-permute-start.20 = (f32[128,128]{1,0:T(8,128)S(1)}, f32[128,128]{1,0:T(8,128)S(1)}, u32[]{:S(2)}, u32[]{:S(2)}) collective-permute-start(f32[128,128]{1,0:T(8,128)S(1)} %get-tuple-element.47.gram), channel_id=1, source_target_pairs={{0,1},{1,0},{2,3},{3,2},{4,5},{5,4},{6,7},{7,6},{8,9},{9,8},{10,11... | collective-permute-start | bytes 196616 | tf_op jit(solution)/shard_map/ppermute | solution.py:100
  23.1 5.5 %collective-permute-start.18 = (f32[128,128]{1,0:T(8,128)S(1)}, f32[128,128]{1,0:T(8,128)S(1)}, u32[]{:S(2)}, u32[]{:S(2)}) collective-permute-start(f32[128,128]{1,0:T(8,128)S(1)} %get-tuple-element.45), channel_id=1, source_target_pairs={{0,1},{1,20},{2,3},{3,22},{4,5},{5,16},{6,7},{7,18},{8,29},{9,8},{... | collective-permute-start | bytes 196616 | tf_op jit(solution)/shard_map/ppermute | solution.py:110
  24.1 5.3 %collective-permute-start.17 = (f32[128,128]{1,0:T(8,128)S(1)}, f32[128,128]{1,0:T(8,128)S(1)}, u32[]{:S(2)}, u32[]{:S(2)}) collective-permute-start(f32[128,128]{1,0:T(8,128)S(1)} %get-tuple-element.45), channel_id=1, source_target_pairs={{0,1},{1,16},{2,3},{3,18},{4,5},{5,20},{6,7},{7,22},{8,25},{9,8},{... | collective-permute-start | bytes 196616 | tf_op jit(solution)/shard_map/ppermute | solution.py:110
  25.7 3.7 %collective-permute-start.16 = (f32[128,128]{1,0:T(8,128)S(1)}, f32[128,128]{1,0:T(8,128)S(1)}, u32[]{:S(2)}, u32[]{:S(2)}) collective-permute-start(f32[128,128]{1,0:T(8,128)S(1)} %get-tuple-element.45), channel_id=1, source_target_pairs={{0,1},{1,4},{2,3},{3,6},{4,5},{5,0},{6,7},{7,2},{8,13},{9,8},{10,1... | collective-permute-start | bytes 196616 | tf_op jit(solution)/shard_map/ppermute | solution.py:110
  26.2 3.1 %collective-permute-start.15 = (f32[128,128]{1,0:T(8,128)S(1)}, f32[128,128]{1,0:T(8,128)S(1)}, u32[]{:S(2)}, u32[]{:S(2)}) collective-permute-start(f32[128,128]{1,0:T(8,128)S(1)} %get-tuple-element.45), channel_id=1, source_target_pairs={{0,1},{1,0},{2,3},{3,2},{4,5},{5,4},{6,7},{7,6},{8,9},{9,8},{10,11... | collective-permute-start | bytes 196616 | tf_op jit(solution)/shard_map/ppermute | solution.py:100
  26.4 1.2 %collective-permute-start.19 = (f32[32,128]{1,0:T(8,128)S(1)}, f32[32,128]{1,0:T(8,128)S(1)}, u32[]{:S(2)}, u32[]{:S(2)}) collective-permute-start(f32[32,128]{1,0:T(8,128)S(1)} %get-tuple-element.46.rows), channel_id=1, source_target_pairs={{0,1},{1,0},{2,3},{3,2},{4,5},{5,4},{6,7},{7,6},{8,9},{9,8},{10,11... | collective-permute-start | bytes 49160 | tf_op jit(solution)/shard_map/ppermute | solution.py:100
  29.4 1.3 %collective-permute-start.21 = (f32[128,128]{1,0:T(8,128)S(1)}, f32[128,128]{1,0:T(8,128)S(1)}, u32[]{:S(2)}, u32[]{:S(2)}) collective-permute-start(f32[128,128]{1,0:T(8,128)S(1)} %add_add_fusion.terms), channel_id=1, source_target_pairs={{0,1},{1,0},{2,3},{3,2},{4,5},{5,4},{6,7},{7,6},{8,9},{9,8},{10,11... | collective-permute-start | bytes 196616 | tf_op jit(solution)/shard_map/ppermute | solution.py:100

commit v25 on v24

--- a/solution.py
+++ b/solution.py
@@ -56,7 +56,7 @@
     return run
 
 
-def call(kernel, outs, operands, flops, scratch=(), in_hbm=0):
+def call(kernel, outs, operands, flops, scratch=(), in_hbm=0, aliases=None):
     spaces = [pltpu.HBM if i < in_hbm else pltpu.VMEM for i in range(len(operands))]
     placed = [pltpu.with_memory_space_constraint(x, space) for x, space in zip(operands, spaces)]
     specs = [pl.BlockSpec(memory_space=space) for space in spaces]
@@ -66,6 +66,7 @@
         in_specs=specs,
         out_specs=[pl.BlockSpec(memory_space=pltpu.VMEM)] * len(outs),
         scratch_shapes=list(scratch),
+        input_output_aliases=aliases or {},
         compiler_params=pltpu.CompilerParams(vmem_limit_bytes=VMEM_LIMIT),
         cost_estimate=pl.CostEstimate(flops=flops, bytes_accessed=1 << 16, transcendentals=0),
     )(*placed)
@@ -171,29 +172,35 @@
     chip_bits = bits_of(smp_count)[1:]
     vox_bits = [bit * smp_count for bit in bits_of(vox_count)]
 
-    def open_kernel(x_hbm, c_hbm, b_hbm, a_hbm, w_hbm, x, c, a, w, out, con, sems):
-        copies = [pltpu.make_async_copy(c_hbm, c, sems.at[0])]
-        copies += [pltpu.make_async_copy(b_hbm, out.at[pl.ds(vox_rows, smp_rows), :], sems.at[1])]
-        copies.append(pltpu.make_async_copy(x_hbm, x, sems.at[2]))
-        copies.append(pltpu.make_async_copy(a_hbm, a, sems.at[3]))
-        copies.append(pltpu.make_async_copy(w_hbm, w, sems.at[4]))
-        for copy in copies:
-            copy.start()
-        copies[0].wait()
-        copies[1].wait()
-        factor = both(c[...])
-        b = out[pl.ds(vox_rows, smp_rows), :]
-        copies[2].wait()
-        blocks = [x[pl.ds(j, vox_rows, stride=smp_rows), :] for j in range(smp_rows)]
+    cut = vox_rows // 2
+
+    def contract(x, c, b, con, out, first):
+        blocks = [x[pl.ds(first * smp_rows + j, cut, stride=smp_rows), :] for j in range(smp_rows)]
         blocks = jnp.concatenate([halves(block, 1) for block in blocks], axis=0)
-        made = fold(jnp.dot(blocks, factor, preferred_element_type=F32)).reshape(smp_rows, vox_rows, rank)
-        con[...] = made
+        made = fold(jnp.dot(blocks, both(c), preferred_element_type=F32)).reshape(smp_rows, cut, rank)
+        con[:, first : first + cut, :] = made
         total = made[0] * b[:1, :]
         for j in range(1, smp_rows):
             total = total + made[j] * b[j : j + 1, :]
-        out[:vox_rows, :] = total
-        copies[3].wait()
-        copies[4].wait()
+        out[:cut, :] = total
+
+    def open_kernel(x_hbm, c_hbm, b_hbm, a_hbm, w_hbm, x, c, a, w, out, con, sems):
+        near_half, far_half = pl.ds(0, cut * smp_rows), pl.ds(cut * smp_rows, cut * smp_rows)
+        copies = [
+            pltpu.make_async_copy(c_hbm, c, sems.at[0]),
+            pltpu.make_async_copy(x_hbm.at[near_half, :], x.at[near_half, :], sems.at[1]),
+            pltpu.make_async_copy(b_hbm, out.at[pl.ds(cut, smp_rows), :], sems.at[2]),
+            pltpu.make_async_copy(x_hbm.at[far_half, :], x.at[far_half, :], sems.at[3]),
+            pltpu.make_async_copy(a_hbm, a, sems.at[4]),
+            pltpu.make_async_copy(w_hbm, w, sems.at[5]),
+        ]
+        for copy in copies:
+            copy.start()
+        for copy in copies[:3]:
+            copy.wait()
+        contract(x, c[...], out[pl.ds(cut, smp_rows), :], con, out, 0)
+        for copy in copies[3:]:
+            copy.wait()
 
     x, c_near, a_near, w_row, opened, con = call(
         open_kernel,
@@ -202,13 +209,24 @@
             near(times, rank),
             near(vox_rows, rank),
             near(1, rank),
-            near(vox_rows + smp_rows, rank),
+            near(cut + smp_rows, rank),
             near(smp_rows, vox_rows, rank),
         ),
         (ensemble.reshape(flat_rows, times), time_factor, sample_factor, voxel_factor, weights.reshape(1, rank)),
-        2 * flat_rows * times * rank * 6,
-        scratch=(pltpu.SemaphoreType.DMA((5,)),),
+        flat_rows * times * rank * 4,
+        scratch=(pltpu.SemaphoreType.DMA((6,)),),
         in_hbm=5,
+    )
+
+    def late_kernel(x, c, opened, con_in, out, con):
+        contract(x, c[...], opened[cut:, :], con, out, cut)
+
+    late_opened, con = call(
+        late_kernel,
+        (near(cut, rank), near(smp_rows, vox_rows, rank)),
+        (x, c_near, opened, con),
+        flat_rows * times * rank * 4,
+        aliases={3: 1},
     )
 
     def weigh_kernel(c, w, outer, outer_c):
@@ -220,29 +238,33 @@
         weigh_kernel, (near(rank, rank), near(rank, rank)), (c_near, w_row), 2 * rank * rank * times * 4
     )
 
-    got = swap(opened)
-    terms = opened[:vox_rows] + got[:vox_rows]
-    mate_con, mate_x = swap(con), swap(x)
-    packet = jnp.concatenate([terms, got[vox_rows:], opened[vox_rows:]], axis=0)
-    own = jnp.concatenate([terms, opened[vox_rows:], got[vox_rows:]], axis=0)
-    rows_b = own[vox_rows:]
+    late_x, late_opened = lax.optimization_barrier((x, late_opened))
+    got, late_got = swap(opened), swap(late_opened)
+    terms, late_terms = opened[:cut] + got[:cut], late_opened + late_got
+    mate_con, mate_x = swap(con), swap(late_x)
+    packet = jnp.concatenate([terms, got[cut:], opened[cut:]], axis=0)
+    own = jnp.concatenate([terms, opened[cut:], got[cut:]], axis=0)
+    late_own = late_terms
     holder = 1
     for group in groups_of(chip_bits):
-        parts = [send(packet, holder, mask) for mask in masks_of(group)[:-1]] + [own]
-        terms = tree([part[:vox_rows] for part in parts])
-        rows_b = jnp.concatenate([part[vox_rows:] for part in parts], axis=0)
+        masks = masks_of(group)[:-1]
+        parts = [send(packet, holder, mask) for mask in masks] + [own]
+        late_terms = tree([send(late_terms, holder, mask) for mask in masks] + [late_own])
+        terms = tree([part[:cut] for part in parts])
+        rows_b = jnp.concatenate([part[cut:] for part in parts], axis=0)
         packet = jnp.concatenate([terms, rows_b], axis=0)
-        own = swap(packet)
+        own, late_own = swap(packet), swap(late_terms)
         holder ^= 1
     voxel_role = holder
 
     half, sums_rows = rank // 2, rank // 2 + chip_rows
 
-    def voxel_kernel(terms, rows, a, w, outer_c, con, mate_con, mate_x, moved_out, chip_b, out, all_b):
+    def voxel_kernel(terms, late_terms, rows, a, w, outer_c, con, mate_con, mate_x, moved_out, chip_b, out, all_b):
         b = in_order(rows, all_b, chips, lax.axis_index("vox") // 2 & 1)
         chip_b[...] = all_b[pl.ds(pl.multiple_of(smp_index() // 2 * chip_rows, chip_rows), chip_rows), :]
         coupled = outer_c[...] * dot_rows(b, b)
-        moved = a[...] - step_of(coupled) * (dot(a[...], coupled) - terms[...] * w[...])
+        terms = jnp.concatenate([terms[...], late_terms[...]], axis=0)
+        moved = a[...] - step_of(coupled) * (dot(a[...], coupled) - terms * w[...])
         moved_out[...] = moved
         packed, diagonal = pack(dot_rows(moved, moved))
         out[:half, :] = packed
@@ -256,7 +278,7 @@
     moved_a, chip_b, sums = call(
         only_on(voxel_role, voxel_kernel),
         (near(vox_rows, rank), near(chip_rows, rank), near(sums_rows + 8, rank)),
-        (terms, rows_b, a_near, w_row, outer_c, con, mate_con, mate_x),
+        (terms, late_terms, rows_b, a_near, w_row, outer_c, con, mate_con, mate_x),
         2 * rank * rank * vox_rows * 12,
         scratch=(near(smp_total, rank),),
     )

time: 31.6 us -> 31.5 us (level)
  waiting for transfers between devices: 12.3 us -> 9.47 us
  starting transfers between devices: 12.7 us -> 15.4 us
    ppermute x11 -> x12, waiting for transfers between devices: 10.5 us -> 7.95 us  [send(): return lax.ppermute(values, ALL, pairs)]
    ppermute x11 -> x12, starting transfers between devices: 10 us -> 12.6 us  [send(): return lax.ppermute(values, ALL, pairs)]
    ppermute x11 -> x12, waiting for transfers between devices: 1.81 us -> 1.52 us  [swap(): lax.ppermute(values, ALL, [(i, i ^ 1) for i in range(lax.axis_size(ALL))])]
    ppermute x11 -> x12, starting transfers between devices: 2.7 us -> 2.85 us  [swap(): lax.ppermute(values, ALL, [(i, i ^ 1) for i in range(lax.axis_size(ALL))])]
    pallas_call x9 -> x10, Pallas kernels: 5.56 us -> 5.61 us  [call(): pl.pallas_call(kernel, out_shape=outs, in_specs=specs, out_specs=[pl.Bloc...]
  transfers between devices with their start and end apart: 22 -> 24, of which waited for: 12 -> 12; matrix products, arithmetic and copies ran while one was open for 0% -> 0% of each run, Pallas kernels for 7% -> 8%
where the time goes in v25:
time: 31.5 us; the launch traced here: 31.4 us
  starting transfers between devices  15.4 us (49%)
  waiting for transfers between devices  9.47 us (30%)
  Pallas kernels  5.61 us (18%)
  between operations  0.78 us (2%)
    ppermute x12, starting transfers between devices, send(): return lax.ppermute(values, ALL, pairs)  12.6 us
    ppermute x12, waiting for transfers between devices, send(): return lax.ppermute(values, ALL, pairs)  7.95 us
    pallas_call x10, Pallas kernels, call(): pl.pallas_call(kernel, out_shape=outs, in_specs=specs, out_specs=[pl.Bloc...  5.61 us
    ppermute x12, starting transfers between devices, swap(): lax.ppermute(values, ALL, [(i, i ^ 1) for i in range(lax.axis_size(ALL))])  2.85 us
    ppermute x12, waiting for transfers between devices, swap(): lax.ppermute(values, ALL, [(i, i ^ 1) for i in range(lax.axis_size(ALL))])  1.52 us
  transfers between devices with their start and end apart: 24, of which 12 were waited for; matrix products, arithmetic and copies ran while one was open for 0% of the time, Pallas kernels for 8%

profile of v25, /device:TPU:0, one launch (start us, length us, event | category | flops | bytes accessed | tf_op | source)
XLA Modules:
  0.0 31.4 jit_solution(13056233137369977765)
XLA Ops:
  0.6 1.3 %shard_map.84 = (f32[1024,128]{1,0:T(8,128)S(1)}, f32[128,128]{1,0:T(8,128)S(1)}, f32[128,128]{1,0:T(8,128)S(1)}, f32[1,128]{1,0:T(1,128)S(1)}, f32[72,128]{1,0:T(8,128)S(1)}, /*index=5*/f32[8,128,128]{2,1,0:T(8,128)S(1)}) custom-call(f32[1024,128]{1,0:T(8,128)} %bitcast.3, f32[128,128]{1,0:T(8,128)} %c_hbm.1, f32[8,128]{1,0:T(8,128)} %b_hbm.1, ...), custom_call_target="tpu_custom_call" | custom-call | flops 67108864 | bytes 65536 | tf_op jit(solution)/shard_map/pallas_call | solution.py:63
  1.9 0.5 %collective-permute-start = (f32[72,128]{1,0:T(8,128)S(1)}, f32[72,128]{1,0:T(8,128)S(1)}, u32[]{:S(2)}, u32[]{:S(2)}) collective-permute-start(f32[72,128]{1,0:T(8,128)S(1)} %get-tuple-element.38.opened), channel_id=1, source_target_pairs={{0,1},{1,0},{2,3},{3,2},{4,5},{5,4},{6,7},{7,6},{8,9},{9,8},{10,11... | collective-permute-start | bytes 110600 | tf_op jit(solution)/shard_map/ppermute | solution.py:101
  2.5 0.2 shard_map.85
  2.7 0.1 collective-permute-start.2
  2.8 0.5 %collective-permute-start.5 = (f32[1024,128]{1,0:T(8,128)S(1)}, f32[1024,128]{1,0:T(8,128)S(1)}, u32[]{:S(2)}, u32[]{:S(2)}) collective-permute-start(f32[1024,128]{1,0:T(8,128)S(1)} %get-tuple-element.48.x.refs_0_), channel_id=1, source_target_pairs={{0,1},{1,0},{2,3},{3,2},{4,5},{5,4},{6,7},{7,6},{8,9},{9,8},{10,11... | collective-permute-start | bytes 1572872 | tf_op jit(solution)/shard_map/ppermute | solution.py:101
  3.3 0.1 collective-permute-start.4
  3.4 0.5 %collective-permute-start.1 = (f32[80,128]{1,0:T(8,128)S(1)}, f32[80,128]{1,0:T(8,128)S(1)}, u32[]{:S(2)}, u32[]{:S(2)}) collective-permute-start(f32[80,128]{1,0:T(8,128)S(1)} %pad_maximum_fusion), channel_id=1, source_target_pairs={{0,1},{1,2},{2,3},{3,0},{4,5},{5,6},{6,7},{7,4},{8,11},{9,8},{10,9... | collective-permute-start | bytes 122888 | tf_op jit(solution)/shard_map/ppermute | solution.py:111
  3.9 0.1 collective-permute-done.2
  4.0 2.6 %collective-permute-start.3 = (f32[64,128]{1,0:T(8,128)S(1)}, f32[64,128]{1,0:T(8,128)S(1)}, u32[]{:S(2)}, u32[]{:S(2)}) collective-permute-start(f32[64,128]{1,0:T(8,128)S(1)} %add.35), channel_id=1, source_target_pairs={{0,1},{1,2},{2,3},{3,0},{4,5},{5,6},{6,7},{7,4},{8,11},{9,8},{10,9... | collective-permute-start | bytes 98312 | tf_op jit(solution)/shard_map/ppermute | solution.py:111
  6.6 0.2 shard_map.86
  6.8 1.4 %collective-permute-done.3 = f32[64,128]{1,0:T(8,128)S(1)} collective-permute-done((f32[64,128]{1,0:T(8,128)S(1)}, f32[64,128]{1,0:T(8,128)S(1)}, u32[]{:S(2)}, u32[]{:S(2)}) %collective-permute-start.3) | collective-permute-done | bytes 32800 | tf_op jit(solution)/shard_map/ppermute | solution.py:111
  8.2 0.0 collective-permute-done.1
  8.3 0.0 collective-permute-done.5.refs_8_.refs_1_
  8.3 0.7 %shard_map.87 = (f32[128,128]{1,0:T(8,128)S(1)}, f32[16,128]{1,0:T(8,128)S(1)}, f32[88,128]{1,0:T(8,128)S(1)}) custom-call(f32[64,128]{1,0:T(8,128)S(1)} %slice_add_fusion.refs_0_, f32[64,128]{1,0:T(8,128)S(1)} %add.36.refs_1_, f32[32,128]{1,0:T(8,128)S(1)} %pad_maximum_fusion.1.refs_2_, f32[128,128]{1,0:T(8,128)S(1)} %get-tuple-element.44.refs_3_, ...), custom_call_target="tpu_custom_call" | custom-call | flops 50331648 | bytes 65536 | tf_op jit(solution)/shard_map/pallas_call | solution.py:63
  9.0 2.2 %collective-permute-start.9 = (f32[88,128]{1,0:T(8,128)S(1)}, f32[88,128]{1,0:T(8,128)S(1)}, u32[]{:S(2)}, u32[]{:S(2)}) collective-permute-start(f32[88,128]{1,0:T(8,128)S(1)} %get-tuple-element.49), channel_id=1, source_target_pairs={{0,21},{1,0},{2,23},{3,2},{4,17},{5,4},{6,19},{7,6},{8,9},{9,28},{... | collective-permute-start | bytes 135176 | tf_op jit(solution)/shard_map/ppermute | solution.py:111
  11.2 1.0 %collective-permute-start.8 = (f32[88,128]{1,0:T(8,128)S(1)}, f32[88,128]{1,0:T(8,128)S(1)}, u32[]{:S(2)}, u32[]{:S(2)}) collective-permute-start(f32[88,128]{1,0:T(8,128)S(1)} %get-tuple-element.49), channel_id=1, source_target_pairs={{0,17},{1,0},{2,19},{3,2},{4,21},{5,4},{6,23},{7,6},{8,9},{9,24},{... | collective-permute-start | bytes 135176 | tf_op jit(solution)/shard_map/ppermute | solution.py:111
  12.2 0.5 %collective-permute-start.6 = (f32[88,128]{1,0:T(8,128)S(1)}, f32[88,128]{1,0:T(8,128)S(1)}, u32[]{:S(2)}, u32[]{:S(2)}) collective-permute-start(f32[88,128]{1,0:T(8,128)S(1)} %get-tuple-element.49), channel_id=1, source_target_pairs={{0,1},{1,0},{2,3},{3,2},{4,5},{5,4},{6,7},{7,6},{8,9},{9,8},{10,11... | collective-permute-start | bytes 135176 | tf_op jit(solution)/shard_map/ppermute | solution.py:101
  12.7 0.0 collective-permute-start.12
  12.7 0.2 collective-permute-done.9
  12.9 1.0 %collective-permute-done.8 = f32[88,128]{1,0:T(8,128)S(1)} collective-permute-done((f32[88,128]{1,0:T(8,128)S(1)}, f32[88,128]{1,0:T(8,128)S(1)}, u32[]{:S(2)}, u32[]{:S(2)}) %collective-permute-start.8) | collective-permute-done | bytes 45088 | tf_op jit(solution)/shard_map/ppermute | solution.py:111
  13.9 0.0 collective-permute-done.7
  14.0 1.7 %collective-permute-start.11 = (f32[88,128]{1,0:T(8,128)S(1)}, f32[88,128]{1,0:T(8,128)S(1)}, u32[]{:S(2)}, u32[]{:S(2)}) collective-permute-start(f32[88,128]{1,0:T(8,128)S(1)} %add_add_fusion.1), channel_id=1, source_target_pairs={{0,1},{1,9},{2,3},{3,11},{4,5},{5,13},{6,7},{7,15},{8,0},{9,8},{10... | collective-permute-start | bytes 135176 | tf_op jit(solution)/shard_map/ppermute | solution.py:111
  15.6 0.1 collective-permute-start.10
  15.7 0.5 %shard_map.88.refs_4_ = f32[16,128,128]{2,1,0:T(8,128)S(1)} custom-call(f32[1024,128]{1,0:T(8,128)S(1)} %get-tuple-element.48.x.refs_0_, f32[1024,128]{1,0:T(8,128)S(1)} %collective-permute-done.5.refs_8_.refs_1_, f32[128,128]{1,0:T(8,128)S(1)} %get-tuple-element.51.refs_2_.moved, f32[128,128]{1,0:T(8,128)S(1)} %collective-permute-done.12.refs_3_.mate_moved), custom_call_target="tpu_custom_call" | custom-call | flops 402653184 | bytes 65536 | tf_op jit(solution)/shard_map/pallas_call | solution.py:63
  16.2 2.9 %collective-permute-done.11 = f32[88,128]{1,0:T(8,128)S(1)} collective-permute-done((f32[88,128]{1,0:T(8,128)S(1)}, f32[88,128]{1,0:T(8,128)S(1)}, u32[]{:S(2)}, u32[]{:S(2)}) %collective-permute-start.11) | collective-permute-done | bytes 45088 | tf_op jit(solution)/shard_map/ppermute | solution.py:111
  19.2 0.0 collective-permute-done.10
  19.2 0.4 %shard_map.89 = (f32[128,128]{1,0:T(8,128)S(1)}, f32[144,128]{1,0:T(8,128)S(1)}) custom-call(f32[88,128]{1,0:T(8,128)S(1)} %add.40.refs_0_, f32[16,128]{1,0:T(8,128)S(1)} %get-tuple-element.50.refs_1_, f32[1,128]{1,0:T(1,128)S(1)} %get-tuple-element.45.w.refs_4_.refs_2_, f32[128,128]{1,0:T(8,128)S(1)} %get-tuple-element.46.refs_5_.refs_3_, ...), custom_call_target="tpu_custom_call" | custom-call | flops 3145728 | bytes 65536 | tf_op jit(solution)/shard_map/pallas_call | solution.py:63
  19.5 0.1 collective-permute-start.16
  19.7 0.0 collective-permute-start.15
  19.7 1.4 %collective-permute-start.14 = (f32[144,128]{1,0:T(8,128)S(1)}, f32[144,128]{1,0:T(8,128)S(1)}, u32[]{:S(2)}, u32[]{:S(2)}) collective-permute-start(f32[144,128]{1,0:T(8,128)S(1)} %get-tuple-element.52), channel_id=1, source_target_pairs={{0,3},{1,0},{2,1},{3,2},{4,7},{5,4},{6,5},{7,6},{8,9},{9,10},{10,1... | collective-permute-start | bytes 221192 | tf_op jit(solution)/shard_map/ppermute | solution.py:111
  21.1 0.0 collective-permute-start.13
  21.1 0.5 %collective-permute-start.22 = (f32[128,128]{1,0:T(8,128)S(1)}, f32[128,128]{1,0:T(8,128)S(1)}, u32[]{:S(2)}, u32[]{:S(2)}) collective-permute-start(f32[128,128]{1,0:T(8,128)S(1)} %get-tuple-element.55.gram), channel_id=1, source_target_pairs={{0,1},{1,0},{2,3},{3,2},{4,5},{5,4},{6,7},{7,6},{8,9},{9,8},{10,11... | collective-permute-start | bytes 196616 | tf_op jit(solution)/shard_map/ppermute | solution.py:101
  21.6 0.1 collective-permute-done.16.refs_3_
  21.6 0.7 %collective-permute-done.15.refs_2_ = f32[144,128]{1,0:T(8,128)S(1)} collective-permute-done((f32[144,128]{1,0:T(8,128)S(1)}, f32[144,128]{1,0:T(8,128)S(1)}, u32[]{:S(2)}, u32[]{:S(2)}) %collective-permute-start.15) | collective-permute-done | bytes 73760 | tf_op jit(solution)/shard_map/ppermute | solution.py:111
  22.3 0.7 %collective-permute-done.14.refs_1_ = f32[144,128]{1,0:T(8,128)S(1)} collective-permute-done((f32[144,128]{1,0:T(8,128)S(1)}, f32[144,128]{1,0:T(8,128)S(1)}, u32[]{:S(2)}, u32[]{:S(2)}) %collective-permute-start.14) | collective-permute-done | bytes 73760 | tf_op jit(solution)/shard_map/ppermute | solution.py:111
  23.1 1.0 %collective-permute-start.20 = (f32[128,128]{1,0:T(8,128)S(1)}, f32[128,128]{1,0:T(8,128)S(1)}, u32[]{:S(2)}, u32[]{:S(2)}) collective-permute-start(f32[128,128]{1,0:T(8,128)S(1)} %get-tuple-element.53), channel_id=1, source_target_pairs={{0,1},{1,20},{2,3},{3,22},{4,5},{5,16},{6,7},{7,18},{8,29},{9,8},{... | collective-permute-start | bytes 196616 | tf_op jit(solution)/shard_map/ppermute | solution.py:111
  24.0 1.6 %collective-permute-start.19 = (f32[128,128]{1,0:T(8,128)S(1)}, f32[128,128]{1,0:T(8,128)S(1)}, u32[]{:S(2)}, u32[]{:S(2)}) collective-permute-start(f32[128,128]{1,0:T(8,128)S(1)} %get-tuple-element.53), channel_id=1, source_target_pairs={{0,1},{1,16},{2,3},{3,18},{4,5},{5,20},{6,7},{7,22},{8,25},{9,8},{... | collective-permute-start | bytes 196616 | tf_op jit(solution)/shard_map/ppermute | solution.py:111
  25.6 0.6 %collective-permute-start.18 = (f32[128,128]{1,0:T(8,128)S(1)}, f32[128,128]{1,0:T(8,128)S(1)}, u32[]{:S(2)}, u32[]{:S(2)}) collective-permute-start(f32[128,128]{1,0:T(8,128)S(1)} %get-tuple-element.53), channel_id=1, source_target_pairs={{0,1},{1,4},{2,3},{3,6},{4,5},{5,0},{6,7},{7,2},{8,13},{9,8},{10,1... | collective-permute-start | bytes 196616 | tf_op jit(solution)/shard_map/ppermute | solution.py:111
  26.2 0.1 collective-permute-start.17
  26.3 0.4 %collective-permute-start.21 = (f32[32,128]{1,0:T(8,128)S(1)}, f32[32,128]{1,0:T(8,128)S(1)}, u32[]{:S(2)}, u32[]{:S(2)}) collective-permute-start(f32[32,128]{1,0:T(8,128)S(1)} %get-tuple-element.54.rows), channel_id=1, source_target_pairs={{0,1},{1,0},{2,3},{3,2},{4,5},{5,4},{6,7},{7,6},{8,9},{9,8},{10,11... | collective-permute-start | bytes 49160 | tf_op jit(solution)/shard_map/ppermute | solution.py:101
  26.7 0.7 %shard_map.91 = (f32[128,128]{1,0:T(8,128)}, f32[1,128]{1,0:T(1,128)S(1)}, f32[128,128]{1,0:T(8,128)S(1)}) custom-call(f32[128,128]{1,0:T(8,128)S(1)} %get-tuple-element.55.gram, f32[128,128]{1,0:T(8,128)S(1)} %collective-permute-done.22.mate_gram, f32[128,128]{1,0:T(8,128)S(1)} %get-tuple-element.51.refs_2_.moved, ...), custom_call_target="tpu_custom_call" | custom-call | flops 131072 | bytes 65536 | tf_op jit(solution)/shard_map/pallas_call | solution.py:63
  27.4 0.2 collective-permute-done.21.mate_rows
  27.5 0.9 %shard_map.92 = (f32[8,128]{1,0:T(8,128)}, f32[128,128]{1,0:T(8,128)S(1)}, f32[1,128]{1,0:T(1,128)S(1)}, f32[1,128]{1,0:T(1,128)S(1)}) custom-call(f32[32,128]{1,0:T(8,128)S(1)} %get-tuple-element.54.rows, f32[32,128]{1,0:T(8,128)S(1)} %collective-permute-done.21.mate_rows, f32[128,128]{1,0:T(8,128)S(1)} %get-tuple-element.40.c, ...), custom_call_target="tpu_custom_call" | custom-call | flops 16777216 | bytes 65536 | tf_op jit(solution)/shard_map/pallas_call | solution.py:63
  28.4 0.2 collective-permute-done.20
  28.6 0.7 %collective-permute-done.19 = f32[128,128]{1,0:T(8,128)S(1)} collective-permute-done((f32[128,128]{1,0:T(8,128)S(1)}, f32[128,128]{1,0:T(8,128)S(1)}, u32[]{:S(2)}, u32[]{:S(2)}) %collective-permute-start.19) | collective-permute-done | bytes 65568 | tf_op jit(solution)/shard_map/ppermute | solution.py:111
  29.4 0.1 collective-permute-start.23
  29.4 1.2 %collective-permute-done.23.mate_terms = f32[128,128]{1,0:T(8,128)S(1)} collective-permute-done((f32[128,128]{1,0:T(8,128)S(1)}, f32[128,128]{1,0:T(8,128)S(1)}, u32[]{:S(2)}, u32[]{:S(2)}) %collective-permute-start.23) | collective-permute-done | bytes 65568 | tf_op jit(solution)/shard_map/ppermute | solution.py:101
  30.7 0.7 %shard_map.93 = (f32[128,128]{1,0:T(8,128)}, f32[1,128]{1,0:T(1,128)}) custom-call(f32[128,128]{1,0:T(8,128)S(1)} %add_add_fusion.terms, f32[128,128]{1,0:T(8,128)S(1)} %collective-permute-done.23.mate_terms, f32[128,128]{1,0:T(8,128)S(1)} %get-tuple-element.67.base, f32[1,128]{1,0:T(1,128)S(1)} %get-tuple-element.68.gain, f32[1,128]{1,0:T(1,128)S(1)} %get-tuple-element.69.scale), custom_call_target="tpu_custom_call" | custom-call | flops 131072 | bytes 65536 | tf_op jit(solution)/shard_map/pallas_call | solution.py:63
  (22 shorter events, 0.1 us)
Async XLA Ops:
  1.9 1.4 %collective-permute-start = (f32[72,128]{1,0:T(8,128)S(1)}, f32[72,128]{1,0:T(8,128)S(1)}, u32[]{:S(2)}, u32[]{:S(2)}) collective-permute-start(f32[72,128]{1,0:T(8,128)S(1)} %get-tuple-element.38.opened), channel_id=1, source_target_pairs={{0,1},{1,0},{2,3},{3,2},{4,5},{5,4},{6,7},{7,6},{8,9},{9,8},{10,11... | collective-permute-start | bytes 110600 | tf_op jit(solution)/shard_map/ppermute | solution.py:101
  2.7 1.3 %collective-permute-start.2 = (f32[64,128]{1,0:T(8,128)S(1)}, f32[64,128]{1,0:T(8,128)S(1)}, u32[]{:S(2)}, u32[]{:S(2)}) collective-permute-start(f32[64,128]{1,0:T(8,128)S(1)} %get-tuple-element.43), channel_id=1, source_target_pairs={{0,1},{1,0},{2,3},{3,2},{4,5},{5,4},{6,7},{7,6},{8,9},{9,8},{10,11... | collective-permute-start | bytes 98312 | tf_op jit(solution)/shard_map/ppermute | solution.py:101
  2.8 5.4 %collective-permute-start.5 = (f32[1024,128]{1,0:T(8,128)S(1)}, f32[1024,128]{1,0:T(8,128)S(1)}, u32[]{:S(2)}, u32[]{:S(2)}) collective-permute-start(f32[1024,128]{1,0:T(8,128)S(1)} %get-tuple-element.48.x.refs_0_), channel_id=1, source_target_pairs={{0,1},{1,0},{2,3},{3,2},{4,5},{5,4},{6,7},{7,6},{8,9},{9,8},{10,11... | collective-permute-start | bytes 1572872 | tf_op jit(solution)/shard_map/ppermute | solution.py:101
  3.3 5.0 %collective-permute-start.4 = (f32[8,128,128]{2,1,0:T(8,128)S(1)}, f32[8,128,128]{2,1,0:T(8,128)S(1)}, u32[]{:S(2)}, u32[]{:S(2)}) collective-permute-start(f32[8,128,128]{2,1,0:T(8,128)S(1)} %get-tuple-element.47.refs_6_), channel_id=1, source_target_pairs={{0,1},{1,0},{2,3},{3,2},{4,5},{5,4},{6,7},{7,6},{8,9},{9,8},{10,11... | collective-permute-start | bytes 1572872 | tf_op jit(solution)/shard_map/ppermute | solution.py:101
  3.4 4.8 %collective-permute-start.1 = (f32[80,128]{1,0:T(8,128)S(1)}, f32[80,128]{1,0:T(8,128)S(1)}, u32[]{:S(2)}, u32[]{:S(2)}) collective-permute-start(f32[80,128]{1,0:T(8,128)S(1)} %pad_maximum_fusion), channel_id=1, source_target_pairs={{0,1},{1,2},{2,3},{3,0},{4,5},{5,6},{6,7},{7,4},{8,11},{9,8},{10,9... | collective-permute-start | bytes 122888 | tf_op jit(solution)/shard_map/ppermute | solution.py:111
  4.0 4.2 %collective-permute-start.3 = (f32[64,128]{1,0:T(8,128)S(1)}, f32[64,128]{1,0:T(8,128)S(1)}, u32[]{:S(2)}, u32[]{:S(2)}) collective-permute-start(f32[64,128]{1,0:T(8,128)S(1)} %add.35), channel_id=1, source_target_pairs={{0,1},{1,2},{2,3},{3,0},{4,5},{5,6},{6,7},{7,4},{8,11},{9,8},{10,9... | collective-permute-start | bytes 98312 | tf_op jit(solution)/shard_map/ppermute | solution.py:111
  9.0 3.9 %collective-permute-start.9 = (f32[88,128]{1,0:T(8,128)S(1)}, f32[88,128]{1,0:T(8,128)S(1)}, u32[]{:S(2)}, u32[]{:S(2)}) collective-permute-start(f32[88,128]{1,0:T(8,128)S(1)} %get-tuple-element.49), channel_id=1, source_target_pairs={{0,21},{1,0},{2,23},{3,2},{4,17},{5,4},{6,19},{7,6},{8,9},{9,28},{... | collective-permute-start | bytes 135176 | tf_op jit(solution)/shard_map/ppermute | solution.py:111
  11.2 2.7 %collective-permute-start.8 = (f32[88,128]{1,0:T(8,128)S(1)}, f32[88,128]{1,0:T(8,128)S(1)}, u32[]{:S(2)}, u32[]{:S(2)}) collective-permute-start(f32[88,128]{1,0:T(8,128)S(1)} %get-tuple-element.49), channel_id=1, source_target_pairs={{0,17},{1,0},{2,19},{3,2},{4,21},{5,4},{6,23},{7,6},{8,9},{9,24},{... | collective-permute-start | bytes 135176 | tf_op jit(solution)/shard_map/ppermute | solution.py:111
  12.2 1.7 %collective-permute-start.7 = (f32[88,128]{1,0:T(8,128)S(1)}, f32[88,128]{1,0:T(8,128)S(1)}, u32[]{:S(2)}, u32[]{:S(2)}) collective-permute-start(f32[88,128]{1,0:T(8,128)S(1)} %get-tuple-element.49), channel_id=1, source_target_pairs={{0,5},{1,0},{2,7},{3,2},{4,1},{5,4},{6,3},{7,6},{8,9},{9,12},{10,1... | collective-permute-start | bytes 135176 | tf_op jit(solution)/shard_map/ppermute | solution.py:111
  12.2 1.7 %collective-permute-start.6 = (f32[88,128]{1,0:T(8,128)S(1)}, f32[88,128]{1,0:T(8,128)S(1)}, u32[]{:S(2)}, u32[]{:S(2)}) collective-permute-start(f32[88,128]{1,0:T(8,128)S(1)} %get-tuple-element.49), channel_id=1, source_target_pairs={{0,1},{1,0},{2,3},{3,2},{4,5},{5,4},{6,7},{7,6},{8,9},{9,8},{10,11... | collective-permute-start | bytes 135176 | tf_op jit(solution)/shard_map/ppermute | solution.py:101
  12.7 3.0 %collective-permute-start.12 = (f32[128,128]{1,0:T(8,128)S(1)}, f32[128,128]{1,0:T(8,128)S(1)}, u32[]{:S(2)}, u32[]{:S(2)}) collective-permute-start(f32[128,128]{1,0:T(8,128)S(1)} %get-tuple-element.51.refs_2_.moved), channel_id=1, source_target_pairs={{0,1},{1,0},{2,3},{3,2},{4,5},{5,4},{6,7},{7,6},{8,9},{9,8},{10,11... | collective-permute-start | bytes 196616 | tf_op jit(solution)/shard_map/ppermute | solution.py:101
  14.0 5.2 %collective-permute-start.11 = (f32[88,128]{1,0:T(8,128)S(1)}, f32[88,128]{1,0:T(8,128)S(1)}, u32[]{:S(2)}, u32[]{:S(2)}) collective-permute-start(f32[88,128]{1,0:T(8,128)S(1)} %add_add_fusion.1), channel_id=1, source_target_pairs={{0,1},{1,9},{2,3},{3,11},{4,5},{5,13},{6,7},{7,15},{8,0},{9,8},{10... | collective-permute-start | bytes 135176 | tf_op jit(solution)/shard_map/ppermute | solution.py:111
  15.6 3.5 %collective-permute-start.10 = (f32[88,128]{1,0:T(8,128)S(1)}, f32[88,128]{1,0:T(8,128)S(1)}, u32[]{:S(2)}, u32[]{:S(2)}) collective-permute-start(f32[88,128]{1,0:T(8,128)S(1)} %add_add_fusion.1), channel_id=1, source_target_pairs={{0,1},{1,0},{2,3},{3,2},{4,5},{5,4},{6,7},{7,6},{8,9},{9,8},{10,11... | collective-permute-start | bytes 135176 | tf_op jit(solution)/shard_map/ppermute | solution.py:101
  19.5 2.1 %collective-permute-start.16 = (f32[144,128]{1,0:T(8,128)S(1)}, f32[144,128]{1,0:T(8,128)S(1)}, u32[]{:S(2)}, u32[]{:S(2)}) collective-permute-start(f32[144,128]{1,0:T(8,128)S(1)} %get-tuple-element.52), channel_id=1, source_target_pairs={{0,10},{1,0},{2,8},{3,2},{4,14},{5,4},{6,12},{7,6},{8,9},{9,3},{10... | collective-permute-start | bytes 221192 | tf_op jit(solution)/shard_map/ppermute | solution.py:111
  19.7 2.7 %collective-permute-start.15 = (f32[144,128]{1,0:T(8,128)S(1)}, f32[144,128]{1,0:T(8,128)S(1)}, u32[]{:S(2)}, u32[]{:S(2)}) collective-permute-start(f32[144,128]{1,0:T(8,128)S(1)} %get-tuple-element.52), channel_id=1, source_target_pairs={{0,8},{1,0},{2,10},{3,2},{4,12},{5,4},{6,14},{7,6},{8,9},{9,1},{10... | collective-permute-start | bytes 221192 | tf_op jit(solution)/shard_map/ppermute | solution.py:111
  19.7 3.4 %collective-permute-start.14 = (f32[144,128]{1,0:T(8,128)S(1)}, f32[144,128]{1,0:T(8,128)S(1)}, u32[]{:S(2)}, u32[]{:S(2)}) collective-permute-start(f32[144,128]{1,0:T(8,128)S(1)} %get-tuple-element.52), channel_id=1, source_target_pairs={{0,3},{1,0},{2,1},{3,2},{4,7},{5,4},{6,5},{7,6},{8,9},{9,10},{10,1... | collective-permute-start | bytes 221192 | tf_op jit(solution)/shard_map/ppermute | solution.py:111
  21.1 2.0 %collective-permute-start.13 = (f32[144,128]{1,0:T(8,128)S(1)}, f32[144,128]{1,0:T(8,128)S(1)}, u32[]{:S(2)}, u32[]{:S(2)}) collective-permute-start(f32[144,128]{1,0:T(8,128)S(1)} %get-tuple-element.52), channel_id=1, source_target_pairs={{0,1},{1,0},{2,3},{3,2},{4,5},{5,4},{6,7},{7,6},{8,9},{9,8},{10,11... | collective-permute-start | bytes 221192 | tf_op jit(solution)/shard_map/ppermute | solution.py:101
  21.1 5.2 %collective-permute-start.22 = (f32[128,128]{1,0:T(8,128)S(1)}, f32[128,128]{1,0:T(8,128)S(1)}, u32[]{:S(2)}, u32[]{:S(2)}) collective-permute-start(f32[128,128]{1,0:T(8,128)S(1)} %get-tuple-element.55.gram), channel_id=1, source_target_pairs={{0,1},{1,0},{2,3},{3,2},{4,5},{5,4},{6,7},{7,6},{8,9},{9,8},{10,11... | collective-permute-start | bytes 196616 | tf_op jit(solution)/shard_map/ppermute | solution.py:101
  23.1 5.5 %collective-permute-start.20 = (f32[128,128]{1,0:T(8,128)S(1)}, f32[128,128]{1,0:T(8,128)S(1)}, u32[]{:S(2)}, u32[]{:S(2)}) collective-permute-start(f32[128,128]{1,0:T(8,128)S(1)} %get-tuple-element.53), channel_id=1, source_target_pairs={{0,1},{1,20},{2,3},{3,22},{4,5},{5,16},{6,7},{7,18},{8,29},{9,8},{... | collective-permute-start | bytes 196616 | tf_op jit(solution)/shard_map/ppermute | solution.py:111
  24.0 5.3 %collective-permute-start.19 = (f32[128,128]{1,0:T(8,128)S(1)}, f32[128,128]{1,0:T(8,128)S(1)}, u32[]{:S(2)}, u32[]{:S(2)}) collective-permute-start(f32[128,128]{1,0:T(8,128)S(1)} %get-tuple-element.53), channel_id=1, source_target_pairs={{0,1},{1,16},{2,3},{3,18},{4,5},{5,20},{6,7},{7,22},{8,25},{9,8},{... | collective-permute-start | bytes 196616 | tf_op jit(solution)/shard_map/ppermute | solution.py:111
  25.6 3.7 %collective-permute-start.18 = (f32[128,128]{1,0:T(8,128)S(1)}, f32[128,128]{1,0:T(8,128)S(1)}, u32[]{:S(2)}, u32[]{:S(2)}) collective-permute-start(f32[128,128]{1,0:T(8,128)S(1)} %get-tuple-element.53), channel_id=1, source_target_pairs={{0,1},{1,4},{2,3},{3,6},{4,5},{5,0},{6,7},{7,2},{8,13},{9,8},{10,1... | collective-permute-start | bytes 196616 | tf_op jit(solution)/shard_map/ppermute | solution.py:111
  26.2 3.2 %collective-permute-start.17 = (f32[128,128]{1,0:T(8,128)S(1)}, f32[128,128]{1,0:T(8,128)S(1)}, u32[]{:S(2)}, u32[]{:S(2)}) collective-permute-start(f32[128,128]{1,0:T(8,128)S(1)} %get-tuple-element.53), channel_id=1, source_target_pairs={{0,1},{1,0},{2,3},{3,2},{4,5},{5,4},{6,7},{7,6},{8,9},{9,8},{10,11... | collective-permute-start | bytes 196616 | tf_op jit(solution)/shard_map/ppermute | solution.py:101
  26.3 1.2 %collective-permute-start.21 = (f32[32,128]{1,0:T(8,128)S(1)}, f32[32,128]{1,0:T(8,128)S(1)}, u32[]{:S(2)}, u32[]{:S(2)}) collective-permute-start(f32[32,128]{1,0:T(8,128)S(1)} %get-tuple-element.54.rows), channel_id=1, source_target_pairs={{0,1},{1,0},{2,3},{3,2},{4,5},{5,4},{6,7},{7,6},{8,9},{9,8},{10,11... | collective-permute-start | bytes 49160 | tf_op jit(solution)/shard_map/ppermute | solution.py:101
  29.4 1.3 %collective-permute-start.23 = (f32[128,128]{1,0:T(8,128)S(1)}, f32[128,128]{1,0:T(8,128)S(1)}, u32[]{:S(2)}, u32[]{:S(2)}) collective-permute-start(f32[128,128]{1,0:T(8,128)S(1)} %add_add_fusion.terms), channel_id=1, source_target_pairs={{0,1},{1,0},{2,3},{3,2},{4,5},{5,4},{6,7},{7,6},{8,9},{9,8},{10,11... | collective-permute-start | bytes 196616 | tf_op jit(solution)/shard_map/ppermute | solution.py:101

commit v26 on v25

--- a/solution.py
+++ b/solution.py
@@ -56,7 +56,7 @@
     return run
 
 
-def call(kernel, outs, operands, flops, scratch=(), in_hbm=0, aliases=None):
+def call(kernel, outs, operands, flops, scratch=(), in_hbm=0, aliases=None, out_space=pltpu.VMEM):
     spaces = [pltpu.HBM if i < in_hbm else pltpu.VMEM for i in range(len(operands))]
     placed = [pltpu.with_memory_space_constraint(x, space) for x, space in zip(operands, spaces)]
     specs = [pl.BlockSpec(memory_space=space) for space in spaces]
@@ -64,7 +64,7 @@
         kernel,
         out_shape=outs,
         in_specs=specs,
-        out_specs=[pl.BlockSpec(memory_space=pltpu.VMEM)] * len(outs),
+        out_specs=[pl.BlockSpec(memory_space=out_space)] * len(outs),
         scratch_shapes=list(scratch),
         input_output_aliases=aliases or {},
         compiler_params=pltpu.CompilerParams(vmem_limit_bytes=VMEM_LIMIT),
@@ -392,17 +392,39 @@
     )
     mate_terms = swap(terms)
 
-    def last_kernel(terms, mate_terms, base, gain, scale, c_out, w_out):
-        moved = base[...] + on_role(last_role, terms[...], mate_terms[...]) * gain[...]
+    def finish(terms, base, gain, scale, c_out, w_out, c, w, sems):
+        moved = base[...] + terms[...] * gain[...]
         scales_c = jnp.sqrt(jnp.sum(moved * moved, axis=0, keepdims=True) / times + 1e-06)
-        c_out[...] = moved / scales_c
-        w_out[...] = scale[...] * scales_c
-
+        c[...] = moved / scales_c
+        w[...] = scale[...] * scales_c
+        copies = [pltpu.make_async_copy(c, c_out, sems.at[0]), pltpu.make_async_copy(w, w_out, sems.at[1])]
+        for copy in copies:
+            copy.start()
+        for copy in copies:
+            copy.wait()
+
+    def mate_kernel(c_in, w_in, *refs):
+        finish(*refs)
+
+    results = (far(times, rank), far(1, rank))
+    scratch = (near(times, rank), near(1, rank), pltpu.SemaphoreType.DMA((2,)))
+    held = call(
+        only_on(last_role, finish),
+        results,
+        (terms, base, gain, scale),
+        rank * times * 8,
+        scratch=scratch,
+        out_space=pltpu.HBM,
+    )
     time_result, scale_result = call(
-        last_kernel,
-        (far(times, rank), far(1, rank)),
-        (terms, mate_terms, base, gain, scale),
+        only_on(1 - last_role, mate_kernel),
+        results,
+        (*held, mate_terms, base, gain, scale),
         rank * times * 8,
+        scratch=scratch,
+        in_hbm=2,
+        aliases={0: 0, 1: 1},
+        out_space=pltpu.HBM,
     )
     return voxel_result, sample_result, time_result, scale_result.reshape(rank)
 

time: 31.5 us -> 31.2 us (level); the launches traced: 31.4 us -> 30.7 us
  waiting for transfers between devices: 9.47 us -> 8.74 us
    ppermute x12, waiting for transfers between devices: 1.52 us -> 0.79 us  [swap(): lax.ppermute(values, ALL, [(i, i ^ 1) for i in range(lax.axis_size(ALL))])]
    pallas_call x10 -> x11, Pallas kernels: 5.61 us -> 5.66 us  [call(): pl.pallas_call(kernel, out_shape=outs, in_specs=specs, out_specs=[pl.Bloc...]
  transfers between devices with their start and end apart: 24 -> 24, of which waited for: 12 -> 12; matrix products, arithmetic and copies ran while one was open for 0% -> 0% of each run, Pallas kernels for 8% -> 11%
where the time goes in v26:
time: 31.2 us; the launch traced here: 30.7 us
  starting transfers between devices  15.4 us (49%)
  waiting for transfers between devices  8.74 us (28%)
  Pallas kernels  5.66 us (18%)
  between operations  0.79 us (3%)
    ppermute x12, starting transfers between devices, send(): return lax.ppermute(values, ALL, pairs)  12.6 us
    ppermute x12, waiting for transfers between devices, send(): return lax.ppermute(values, ALL, pairs)  7.95 us
    pallas_call x11, Pallas kernels, call(): pl.pallas_call(kernel, out_shape=outs, in_specs=specs, out_specs=[pl.Bloc...  5.66 us
    ppermute x12, starting transfers between devices, swap(): lax.ppermute(values, ALL, [(i, i ^ 1) for i in range(lax.axis_size(ALL))])  2.85 us
    ppermute x12, waiting for transfers between devices, swap(): lax.ppermute(values, ALL, [(i, i ^ 1) for i in range(lax.axis_size(ALL))])  0.79 us
  transfers between devices with their start and end apart: 24, of which 12 were waited for; matrix products, arithmetic and copies ran while one was open for 0% of the time, Pallas kernels for 11%

profile of v26, /device:TPU:0, one launch (start us, length us, event | category | flops | bytes accessed | tf_op | source)
XLA Modules:
  0.0 30.7 jit_solution(17454202052321345455)
XLA Ops:
  0.6 1.3 %shard_map.84 = (f32[1024,128]{1,0:T(8,128)S(1)}, f32[128,128]{1,0:T(8,128)S(1)}, f32[128,128]{1,0:T(8,128)S(1)}, f32[1,128]{1,0:T(1,128)S(1)}, f32[72,128]{1,0:T(8,128)S(1)}, /*index=5*/f32[8,128,128]{2,1,0:T(8,128)S(1)}) custom-call(f32[1024,128]{1,0:T(8,128)} %bitcast.3, f32[128,128]{1,0:T(8,128)} %c_hbm.1, f32[8,128]{1,0:T(8,128)} %b_hbm.1, ...), custom_call_target="tpu_custom_call" | custom-call | flops 67108864 | bytes 65536 | tf_op jit(solution)/shard_map/pallas_call | solution.py:63
  1.9 0.5 %collective-permute-start = (f32[72,128]{1,0:T(8,128)S(1)}, f32[72,128]{1,0:T(8,128)S(1)}, u32[]{:S(2)}, u32[]{:S(2)}) collective-permute-start(f32[72,128]{1,0:T(8,128)S(1)} %get-tuple-element.40.opened), channel_id=1, source_target_pairs={{0,1},{1,0},{2,3},{3,2},{4,5},{5,4},{6,7},{7,6},{8,9},{9,8},{10,11... | collective-permute-start | bytes 110600 | tf_op jit(solution)/shard_map/ppermute | solution.py:101
  2.5 0.2 shard_map.85
  2.7 0.1 collective-permute-start.2
  2.8 0.5 %collective-permute-start.5 = (f32[1024,128]{1,0:T(8,128)S(1)}, f32[1024,128]{1,0:T(8,128)S(1)}, u32[]{:S(2)}, u32[]{:S(2)}) collective-permute-start(f32[1024,128]{1,0:T(8,128)S(1)} %get-tuple-element.50.x.refs_0_), channel_id=1, source_target_pairs={{0,1},{1,0},{2,3},{3,2},{4,5},{5,4},{6,7},{7,6},{8,9},{9,8},{10,11... | collective-permute-start | bytes 1572872 | tf_op jit(solution)/shard_map/ppermute | solution.py:101
  3.3 0.1 collective-permute-start.4
  3.4 0.0 collective-permute-done
  3.4 0.5 %collective-permute-start.1 = (f32[80,128]{1,0:T(8,128)S(1)}, f32[80,128]{1,0:T(8,128)S(1)}, u32[]{:S(2)}, u32[]{:S(2)}) collective-permute-start(f32[80,128]{1,0:T(8,128)S(1)} %pad_maximum_fusion), channel_id=1, source_target_pairs={{0,1},{1,2},{2,3},{3,0},{4,5},{5,6},{6,7},{7,4},{8,11},{9,8},{10,9... | collective-permute-start | bytes 122888 | tf_op jit(solution)/shard_map/ppermute | solution.py:111
  3.9 0.1 collective-permute-done.2
  4.0 2.6 %collective-permute-start.3 = (f32[64,128]{1,0:T(8,128)S(1)}, f32[64,128]{1,0:T(8,128)S(1)}, u32[]{:S(2)}, u32[]{:S(2)}) collective-permute-start(f32[64,128]{1,0:T(8,128)S(1)} %add.35), channel_id=1, source_target_pairs={{0,1},{1,2},{2,3},{3,0},{4,5},{5,6},{6,7},{7,4},{8,11},{9,8},{10,9... | collective-permute-start | bytes 98312 | tf_op jit(solution)/shard_map/ppermute | solution.py:111
  6.6 0.2 shard_map.86
  6.8 1.4 %collective-permute-done.3 = f32[64,128]{1,0:T(8,128)S(1)} collective-permute-done((f32[64,128]{1,0:T(8,128)S(1)}, f32[64,128]{1,0:T(8,128)S(1)}, u32[]{:S(2)}, u32[]{:S(2)}) %collective-permute-start.3) | collective-permute-done | bytes 32800 | tf_op jit(solution)/shard_map/ppermute | solution.py:111
  8.3 0.0 collective-permute-done.4.refs_7_
  8.3 0.7 %shard_map.87 = (f32[128,128]{1,0:T(8,128)S(1)}, f32[16,128]{1,0:T(8,128)S(1)}, f32[88,128]{1,0:T(8,128)S(1)}) custom-call(f32[64,128]{1,0:T(8,128)S(1)} %slice_add_fusion.refs_0_, f32[64,128]{1,0:T(8,128)S(1)} %add.36.refs_1_, f32[32,128]{1,0:T(8,128)S(1)} %pad_maximum_fusion.1.refs_2_, f32[128,128]{1,0:T(8,128)S(1)} %get-tuple-element.46.refs_3_, ...), custom_call_target="tpu_custom_call" | custom-call | flops 50331648 | bytes 65536 | tf_op jit(solution)/shard_map/pallas_call | solution.py:63
  9.0 2.2 %collective-permute-start.9 = (f32[88,128]{1,0:T(8,128)S(1)}, f32[88,128]{1,0:T(8,128)S(1)}, u32[]{:S(2)}, u32[]{:S(2)}) collective-permute-start(f32[88,128]{1,0:T(8,128)S(1)} %get-tuple-element.51), channel_id=1, source_target_pairs={{0,21},{1,0},{2,23},{3,2},{4,17},{5,4},{6,19},{7,6},{8,9},{9,28},{... | collective-permute-start | bytes 135176 | tf_op jit(solution)/shard_map/ppermute | solution.py:111
  11.2 1.0 %collective-permute-start.8 = (f32[88,128]{1,0:T(8,128)S(1)}, f32[88,128]{1,0:T(8,128)S(1)}, u32[]{:S(2)}, u32[]{:S(2)}) collective-permute-start(f32[88,128]{1,0:T(8,128)S(1)} %get-tuple-element.51), channel_id=1, source_target_pairs={{0,17},{1,0},{2,19},{3,2},{4,21},{5,4},{6,23},{7,6},{8,9},{9,24},{... | collective-permute-start | bytes 135176 | tf_op jit(solution)/shard_map/ppermute | solution.py:111
  12.2 0.0 collective-permute-start.7
  12.2 0.5 %collective-permute-start.6 = (f32[88,128]{1,0:T(8,128)S(1)}, f32[88,128]{1,0:T(8,128)S(1)}, u32[]{:S(2)}, u32[]{:S(2)}) collective-permute-start(f32[88,128]{1,0:T(8,128)S(1)} %get-tuple-element.51), channel_id=1, source_target_pairs={{0,1},{1,0},{2,3},{3,2},{4,5},{5,4},{6,7},{7,6},{8,9},{9,8},{10,11... | collective-permute-start | bytes 135176 | tf_op jit(solution)/shard_map/ppermute | solution.py:101
  12.7 0.0 collective-permute-start.12
  12.7 0.2 collective-permute-done.9
  12.9 1.0 %collective-permute-done.8 = f32[88,128]{1,0:T(8,128)S(1)} collective-permute-done((f32[88,128]{1,0:T(8,128)S(1)}, f32[88,128]{1,0:T(8,128)S(1)}, u32[]{:S(2)}, u32[]{:S(2)}) %collective-permute-start.8) | collective-permute-done | bytes 45088 | tf_op jit(solution)/shard_map/ppermute | solution.py:111
  14.0 1.7 %collective-permute-start.11 = (f32[88,128]{1,0:T(8,128)S(1)}, f32[88,128]{1,0:T(8,128)S(1)}, u32[]{:S(2)}, u32[]{:S(2)}) collective-permute-start(f32[88,128]{1,0:T(8,128)S(1)} %add_add_fusion.1), channel_id=1, source_target_pairs={{0,1},{1,9},{2,3},{3,11},{4,5},{5,13},{6,7},{7,15},{8,0},{9,8},{10... | collective-permute-start | bytes 135176 | tf_op jit(solution)/shard_map/ppermute | solution.py:111
  15.6 0.1 collective-permute-start.10
  15.7 0.0 collective-permute-done.12.refs_3_.mate_moved
  15.7 0.5 %shard_map.88.refs_4_ = f32[16,128,128]{2,1,0:T(8,128)S(1)} custom-call(f32[1024,128]{1,0:T(8,128)S(1)} %get-tuple-element.50.x.refs_0_, f32[1024,128]{1,0:T(8,128)S(1)} %collective-permute-done.5.refs_8_.refs_1_, f32[128,128]{1,0:T(8,128)S(1)} %get-tuple-element.53.refs_2_.moved, f32[128,128]{1,0:T(8,128)S(1)} %collective-permute-done.12.refs_3_.mate_moved), custom_call_target="tpu_custom_call" | custom-call | flops 402653184 | bytes 65536 | tf_op jit(solution)/shard_map/pallas_call | solution.py:63
  16.2 2.9 %collective-permute-done.11 = f32[88,128]{1,0:T(8,128)S(1)} collective-permute-done((f32[88,128]{1,0:T(8,128)S(1)}, f32[88,128]{1,0:T(8,128)S(1)}, u32[]{:S(2)}, u32[]{:S(2)}) %collective-permute-start.11) | collective-permute-done | bytes 45088 | tf_op jit(solution)/shard_map/ppermute | solution.py:111
  19.2 0.0 collective-permute-done.10
  19.2 0.4 %shard_map.89 = (f32[128,128]{1,0:T(8,128)S(1)}, f32[144,128]{1,0:T(8,128)S(1)}) custom-call(f32[88,128]{1,0:T(8,128)S(1)} %add.40.refs_0_, f32[16,128]{1,0:T(8,128)S(1)} %get-tuple-element.52.refs_1_, f32[1,128]{1,0:T(1,128)S(1)} %get-tuple-element.47.w.refs_4_.refs_2_, f32[128,128]{1,0:T(8,128)S(1)} %get-tuple-element.48.refs_5_.refs_3_, ...), custom_call_target="tpu_custom_call" | custom-call | flops 3145728 | bytes 65536 | tf_op jit(solution)/shard_map/pallas_call | solution.py:63
  19.5 0.1 collective-permute-start.16
  19.7 0.0 collective-permute-start.15
  19.7 1.4 %collective-permute-start.14 = (f32[144,128]{1,0:T(8,128)S(1)}, f32[144,128]{1,0:T(8,128)S(1)}, u32[]{:S(2)}, u32[]{:S(2)}) collective-permute-start(f32[144,128]{1,0:T(8,128)S(1)} %get-tuple-element.54), channel_id=1, source_target_pairs={{0,3},{1,0},{2,1},{3,2},{4,7},{5,4},{6,5},{7,6},{8,9},{9,10},{10,1... | collective-permute-start | bytes 221192 | tf_op jit(solution)/shard_map/ppermute | solution.py:111
  21.1 0.5 %collective-permute-start.22 = (f32[128,128]{1,0:T(8,128)S(1)}, f32[128,128]{1,0:T(8,128)S(1)}, u32[]{:S(2)}, u32[]{:S(2)}) collective-permute-start(f32[128,128]{1,0:T(8,128)S(1)} %get-tuple-element.57.gram), channel_id=1, source_target_pairs={{0,1},{1,0},{2,3},{3,2},{4,5},{5,4},{6,7},{7,6},{8,9},{9,8},{10,11... | collective-permute-start | bytes 196616 | tf_op jit(solution)/shard_map/ppermute | solution.py:101
  21.6 0.1 collective-permute-done.16.refs_3_
  21.6 0.7 %collective-permute-done.15.refs_2_ = f32[144,128]{1,0:T(8,128)S(1)} collective-permute-done((f32[144,128]{1,0:T(8,128)S(1)}, f32[144,128]{1,0:T(8,128)S(1)}, u32[]{:S(2)}, u32[]{:S(2)}) %collective-permute-start.15) | collective-permute-done | bytes 73760 | tf_op jit(solution)/shard_map/ppermute | solution.py:111
  22.3 0.7 %collective-permute-done.14.refs_1_ = f32[144,128]{1,0:T(8,128)S(1)} collective-permute-done((f32[144,128]{1,0:T(8,128)S(1)}, f32[144,128]{1,0:T(8,128)S(1)}, u32[]{:S(2)}, u32[]{:S(2)}) %collective-permute-start.14) | collective-permute-done | bytes 73760 | tf_op jit(solution)/shard_map/ppermute | solution.py:111
  23.1 1.0 %collective-permute-start.20 = (f32[128,128]{1,0:T(8,128)S(1)}, f32[128,128]{1,0:T(8,128)S(1)}, u32[]{:S(2)}, u32[]{:S(2)}) collective-permute-start(f32[128,128]{1,0:T(8,128)S(1)} %get-tuple-element.55), channel_id=1, source_target_pairs={{0,1},{1,20},{2,3},{3,22},{4,5},{5,16},{6,7},{7,18},{8,29},{9,8},{... | collective-permute-start | bytes 196616 | tf_op jit(solution)/shard_map/ppermute | solution.py:111
  24.0 1.6 %collective-permute-start.19 = (f32[128,128]{1,0:T(8,128)S(1)}, f32[128,128]{1,0:T(8,128)S(1)}, u32[]{:S(2)}, u32[]{:S(2)}) collective-permute-start(f32[128,128]{1,0:T(8,128)S(1)} %get-tuple-element.55), channel_id=1, source_target_pairs={{0,1},{1,16},{2,3},{3,18},{4,5},{5,20},{6,7},{7,22},{8,25},{9,8},{... | collective-permute-start | bytes 196616 | tf_op jit(solution)/shard_map/ppermute | solution.py:111
  25.6 0.6 %collective-permute-start.18 = (f32[128,128]{1,0:T(8,128)S(1)}, f32[128,128]{1,0:T(8,128)S(1)}, u32[]{:S(2)}, u32[]{:S(2)}) collective-permute-start(f32[128,128]{1,0:T(8,128)S(1)} %get-tuple-element.55), channel_id=1, source_target_pairs={{0,1},{1,4},{2,3},{3,6},{4,5},{5,0},{6,7},{7,2},{8,13},{9,8},{10,1... | collective-permute-start | bytes 196616 | tf_op jit(solution)/shard_map/ppermute | solution.py:111
  26.2 0.1 collective-permute-start.17
  26.3 0.4 %collective-permute-start.21 = (f32[32,128]{1,0:T(8,128)S(1)}, f32[32,128]{1,0:T(8,128)S(1)}, u32[]{:S(2)}, u32[]{:S(2)}) collective-permute-start(f32[32,128]{1,0:T(8,128)S(1)} %get-tuple-element.56.rows), channel_id=1, source_target_pairs={{0,1},{1,0},{2,3},{3,2},{4,5},{5,4},{6,7},{7,6},{8,9},{9,8},{10,11... | collective-permute-start | bytes 49160 | tf_op jit(solution)/shard_map/ppermute | solution.py:101
  26.7 0.7 %shard_map.91 = (f32[128,128]{1,0:T(8,128)}, f32[1,128]{1,0:T(1,128)S(1)}, f32[128,128]{1,0:T(8,128)S(1)}) custom-call(f32[128,128]{1,0:T(8,128)S(1)} %get-tuple-element.57.gram, f32[128,128]{1,0:T(8,128)S(1)} %collective-permute-done.22.mate_gram, f32[128,128]{1,0:T(8,128)S(1)} %get-tuple-element.53.refs_2_.moved, ...), custom_call_target="tpu_custom_call" | custom-call | flops 131072 | bytes 65536 | tf_op jit(solution)/shard_map/pallas_call | solution.py:63
  27.4 0.2 collective-permute-done.21.mate_rows
  27.5 0.9 %shard_map.92 = (f32[8,128]{1,0:T(8,128)}, f32[128,128]{1,0:T(8,128)S(1)}, f32[1,128]{1,0:T(1,128)S(1)}, f32[1,128]{1,0:T(1,128)S(1)}) custom-call(f32[32,128]{1,0:T(8,128)S(1)} %get-tuple-element.56.rows, f32[32,128]{1,0:T(8,128)S(1)} %collective-permute-done.21.mate_rows, f32[128,128]{1,0:T(8,128)S(1)} %get-tuple-element.42.c, ...), custom_call_target="tpu_custom_call" | custom-call | flops 16777216 | bytes 65536 | tf_op jit(solution)/shard_map/pallas_call | solution.py:63
  28.4 0.2 collective-permute-done.20
  28.6 0.7 %collective-permute-done.19 = f32[128,128]{1,0:T(8,128)S(1)} collective-permute-done((f32[128,128]{1,0:T(8,128)S(1)}, f32[128,128]{1,0:T(8,128)S(1)}, u32[]{:S(2)}, u32[]{:S(2)}) %collective-permute-start.19) | collective-permute-done | bytes 65568 | tf_op jit(solution)/shard_map/ppermute | solution.py:111
  29.4 0.1 collective-permute-start.23
  29.4 0.7 %shard_map.93 = (f32[128,128]{1,0:T(8,128)}, f32[1,128]{1,0:T(1,128)}) custom-call(f32[128,128]{1,0:T(8,128)S(1)} %add_add_fusion.refs_0_, f32[128,128]{1,0:T(8,128)S(1)} %get-tuple-element.69.refs_1_.refs_3_, f32[1,128]{1,0:T(1,128)S(1)} %get-tuple-element.70.refs_2_.refs_4_, f32[1,128]{1,0:T(1,128)S(1)} %get-tuple-element.71.refs_3_.refs_5_), custom_call_target="tpu_custom_call" | custom-call | flops 131072 | bytes 65536 | tf_op jit(solution)/shard_map/pallas_call | solution.py:63
  30.2 0.5 %collective-permute-done.23.refs_2_ = f32[128,128]{1,0:T(8,128)S(1)} collective-permute-done((f32[128,128]{1,0:T(8,128)S(1)}, f32[128,128]{1,0:T(8,128)S(1)}, u32[]{:S(2)}, u32[]{:S(2)}) %collective-permute-start.23) | collective-permute-done | bytes 65568 | tf_op jit(solution)/shard_map/ppermute | solution.py:101
  (23 shorter events, 0.1 us)
Async XLA Ops:
  1.9 1.4 %collective-permute-start = (f32[72,128]{1,0:T(8,128)S(1)}, f32[72,128]{1,0:T(8,128)S(1)}, u32[]{:S(2)}, u32[]{:S(2)}) collective-permute-start(f32[72,128]{1,0:T(8,128)S(1)} %get-tuple-element.40.opened), channel_id=1, source_target_pairs={{0,1},{1,0},{2,3},{3,2},{4,5},{5,4},{6,7},{7,6},{8,9},{9,8},{10,11... | collective-permute-start | bytes 110600 | tf_op jit(solution)/shard_map/ppermute | solution.py:101
  2.7 1.3 %collective-permute-start.2 = (f32[64,128]{1,0:T(8,128)S(1)}, f32[64,128]{1,0:T(8,128)S(1)}, u32[]{:S(2)}, u32[]{:S(2)}) collective-permute-start(f32[64,128]{1,0:T(8,128)S(1)} %get-tuple-element.45), channel_id=1, source_target_pairs={{0,1},{1,0},{2,3},{3,2},{4,5},{5,4},{6,7},{7,6},{8,9},{9,8},{10,11... | collective-permute-start | bytes 98312 | tf_op jit(solution)/shard_map/ppermute | solution.py:101
  2.8 5.4 %collective-permute-start.5 = (f32[1024,128]{1,0:T(8,128)S(1)}, f32[1024,128]{1,0:T(8,128)S(1)}, u32[]{:S(2)}, u32[]{:S(2)}) collective-permute-start(f32[1024,128]{1,0:T(8,128)S(1)} %get-tuple-element.50.x.refs_0_), channel_id=1, source_target_pairs={{0,1},{1,0},{2,3},{3,2},{4,5},{5,4},{6,7},{7,6},{8,9},{9,8},{10,11... | collective-permute-start | bytes 1572872 | tf_op jit(solution)/shard_map/ppermute | solution.py:101
  3.3 5.0 %collective-permute-start.4 = (f32[8,128,128]{2,1,0:T(8,128)S(1)}, f32[8,128,128]{2,1,0:T(8,128)S(1)}, u32[]{:S(2)}, u32[]{:S(2)}) collective-permute-start(f32[8,128,128]{2,1,0:T(8,128)S(1)} %get-tuple-element.49.refs_6_), channel_id=1, source_target_pairs={{0,1},{1,0},{2,3},{3,2},{4,5},{5,4},{6,7},{7,6},{8,9},{9,8},{10,11... | collective-permute-start | bytes 1572872 | tf_op jit(solution)/shard_map/ppermute | solution.py:101
  3.4 4.8 %collective-permute-start.1 = (f32[80,128]{1,0:T(8,128)S(1)}, f32[80,128]{1,0:T(8,128)S(1)}, u32[]{:S(2)}, u32[]{:S(2)}) collective-permute-start(f32[80,128]{1,0:T(8,128)S(1)} %pad_maximum_fusion), channel_id=1, source_target_pairs={{0,1},{1,2},{2,3},{3,0},{4,5},{5,6},{6,7},{7,4},{8,11},{9,8},{10,9... | collective-permute-start | bytes 122888 | tf_op jit(solution)/shard_map/ppermute | solution.py:111
  4.0 4.2 %collective-permute-start.3 = (f32[64,128]{1,0:T(8,128)S(1)}, f32[64,128]{1,0:T(8,128)S(1)}, u32[]{:S(2)}, u32[]{:S(2)}) collective-permute-start(f32[64,128]{1,0:T(8,128)S(1)} %add.35), channel_id=1, source_target_pairs={{0,1},{1,2},{2,3},{3,0},{4,5},{5,6},{6,7},{7,4},{8,11},{9,8},{10,9... | collective-permute-start | bytes 98312 | tf_op jit(solution)/shard_map/ppermute | solution.py:111
  9.0 3.9 %collective-permute-start.9 = (f32[88,128]{1,0:T(8,128)S(1)}, f32[88,128]{1,0:T(8,128)S(1)}, u32[]{:S(2)}, u32[]{:S(2)}) collective-permute-start(f32[88,128]{1,0:T(8,128)S(1)} %get-tuple-element.51), channel_id=1, source_target_pairs={{0,21},{1,0},{2,23},{3,2},{4,17},{5,4},{6,19},{7,6},{8,9},{9,28},{... | collective-permute-start | bytes 135176 | tf_op jit(solution)/shard_map/ppermute | solution.py:111
  11.2 2.7 %collective-permute-start.8 = (f32[88,128]{1,0:T(8,128)S(1)}, f32[88,128]{1,0:T(8,128)S(1)}, u32[]{:S(2)}, u32[]{:S(2)}) collective-permute-start(f32[88,128]{1,0:T(8,128)S(1)} %get-tuple-element.51), channel_id=1, source_target_pairs={{0,17},{1,0},{2,19},{3,2},{4,21},{5,4},{6,23},{7,6},{8,9},{9,24},{... | collective-permute-start | bytes 135176 | tf_op jit(solution)/shard_map/ppermute | solution.py:111
  12.2 1.7 %collective-permute-start.7 = (f32[88,128]{1,0:T(8,128)S(1)}, f32[88,128]{1,0:T(8,128)S(1)}, u32[]{:S(2)}, u32[]{:S(2)}) collective-permute-start(f32[88,128]{1,0:T(8,128)S(1)} %get-tuple-element.51), channel_id=1, source_target_pairs={{0,5},{1,0},{2,7},{3,2},{4,1},{5,4},{6,3},{7,6},{8,9},{9,12},{10,1... | collective-permute-start | bytes 135176 | tf_op jit(solution)/shard_map/ppermute | solution.py:111
  12.2 1.7 %collective-permute-start.6 = (f32[88,128]{1,0:T(8,128)S(1)}, f32[88,128]{1,0:T(8,128)S(1)}, u32[]{:S(2)}, u32[]{:S(2)}) collective-permute-start(f32[88,128]{1,0:T(8,128)S(1)} %get-tuple-element.51), channel_id=1, source_target_pairs={{0,1},{1,0},{2,3},{3,2},{4,5},{5,4},{6,7},{7,6},{8,9},{9,8},{10,11... | collective-permute-start | bytes 135176 | tf_op jit(solution)/shard_map/ppermute | solution.py:101
  12.7 3.0 %collective-permute-start.12 = (f32[128,128]{1,0:T(8,128)S(1)}, f32[128,128]{1,0:T(8,128)S(1)}, u32[]{:S(2)}, u32[]{:S(2)}) collective-permute-start(f32[128,128]{1,0:T(8,128)S(1)} %get-tuple-element.53.refs_2_.moved), channel_id=1, source_target_pairs={{0,1},{1,0},{2,3},{3,2},{4,5},{5,4},{6,7},{7,6},{8,9},{9,8},{10,11... | collective-permute-start | bytes 196616 | tf_op jit(solution)/shard_map/ppermute | solution.py:101
  14.0 5.2 %collective-permute-start.11 = (f32[88,128]{1,0:T(8,128)S(1)}, f32[88,128]{1,0:T(8,128)S(1)}, u32[]{:S(2)}, u32[]{:S(2)}) collective-permute-start(f32[88,128]{1,0:T(8,128)S(1)} %add_add_fusion.1), channel_id=1, source_target_pairs={{0,1},{1,9},{2,3},{3,11},{4,5},{5,13},{6,7},{7,15},{8,0},{9,8},{10... | collective-permute-start | bytes 135176 | tf_op jit(solution)/shard_map/ppermute | solution.py:111
  15.6 3.5 %collective-permute-start.10 = (f32[88,128]{1,0:T(8,128)S(1)}, f32[88,128]{1,0:T(8,128)S(1)}, u32[]{:S(2)}, u32[]{:S(2)}) collective-permute-start(f32[88,128]{1,0:T(8,128)S(1)} %add_add_fusion.1), channel_id=1, source_target_pairs={{0,1},{1,0},{2,3},{3,2},{4,5},{5,4},{6,7},{7,6},{8,9},{9,8},{10,11... | collective-permute-start | bytes 135176 | tf_op jit(solution)/shard_map/ppermute | solution.py:101
  19.5 2.1 %collective-permute-start.16 = (f32[144,128]{1,0:T(8,128)S(1)}, f32[144,128]{1,0:T(8,128)S(1)}, u32[]{:S(2)}, u32[]{:S(2)}) collective-permute-start(f32[144,128]{1,0:T(8,128)S(1)} %get-tuple-element.54), channel_id=1, source_target_pairs={{0,10},{1,0},{2,8},{3,2},{4,14},{5,4},{6,12},{7,6},{8,9},{9,3},{10... | collective-permute-start | bytes 221192 | tf_op jit(solution)/shard_map/ppermute | solution.py:111
  19.7 2.7 %collective-permute-start.15 = (f32[144,128]{1,0:T(8,128)S(1)}, f32[144,128]{1,0:T(8,128)S(1)}, u32[]{:S(2)}, u32[]{:S(2)}) collective-permute-start(f32[144,128]{1,0:T(8,128)S(1)} %get-tuple-element.54), channel_id=1, source_target_pairs={{0,8},{1,0},{2,10},{3,2},{4,12},{5,4},{6,14},{7,6},{8,9},{9,1},{10... | collective-permute-start | bytes 221192 | tf_op jit(solution)/shard_map/ppermute | solution.py:111
  19.7 3.4 %collective-permute-start.14 = (f32[144,128]{1,0:T(8,128)S(1)}, f32[144,128]{1,0:T(8,128)S(1)}, u32[]{:S(2)}, u32[]{:S(2)}) collective-permute-start(f32[144,128]{1,0:T(8,128)S(1)} %get-tuple-element.54), channel_id=1, source_target_pairs={{0,3},{1,0},{2,1},{3,2},{4,7},{5,4},{6,5},{7,6},{8,9},{9,10},{10,1... | collective-permute-start | bytes 221192 | tf_op jit(solution)/shard_map/ppermute | solution.py:111
  21.1 2.0 %collective-permute-start.13 = (f32[144,128]{1,0:T(8,128)S(1)}, f32[144,128]{1,0:T(8,128)S(1)}, u32[]{:S(2)}, u32[]{:S(2)}) collective-permute-start(f32[144,128]{1,0:T(8,128)S(1)} %get-tuple-element.54), channel_id=1, source_target_pairs={{0,1},{1,0},{2,3},{3,2},{4,5},{5,4},{6,7},{7,6},{8,9},{9,8},{10,11... | collective-permute-start | bytes 221192 | tf_op jit(solution)/shard_map/ppermute | solution.py:101
  21.1 5.2 %collective-permute-start.22 = (f32[128,128]{1,0:T(8,128)S(1)}, f32[128,128]{1,0:T(8,128)S(1)}, u32[]{:S(2)}, u32[]{:S(2)}) collective-permute-start(f32[128,128]{1,0:T(8,128)S(1)} %get-tuple-element.57.gram), channel_id=1, source_target_pairs={{0,1},{1,0},{2,3},{3,2},{4,5},{5,4},{6,7},{7,6},{8,9},{9,8},{10,11... | collective-permute-start | bytes 196616 | tf_op jit(solution)/shard_map/ppermute | solution.py:101
  23.1 5.5 %collective-permute-start.20 = (f32[128,128]{1,0:T(8,128)S(1)}, f32[128,128]{1,0:T(8,128)S(1)}, u32[]{:S(2)}, u32[]{:S(2)}) collective-permute-start(f32[128,128]{1,0:T(8,128)S(1)} %get-tuple-element.55), channel_id=1, source_target_pairs={{0,1},{1,20},{2,3},{3,22},{4,5},{5,16},{6,7},{7,18},{8,29},{9,8},{... | collective-permute-start | bytes 196616 | tf_op jit(solution)/shard_map/ppermute | solution.py:111
  24.0 5.3 %collective-permute-start.19 = (f32[128,128]{1,0:T(8,128)S(1)}, f32[128,128]{1,0:T(8,128)S(1)}, u32[]{:S(2)}, u32[]{:S(2)}) collective-permute-start(f32[128,128]{1,0:T(8,128)S(1)} %get-tuple-element.55), channel_id=1, source_target_pairs={{0,1},{1,16},{2,3},{3,18},{4,5},{5,20},{6,7},{7,22},{8,25},{9,8},{... | collective-permute-start | bytes 196616 | tf_op jit(solution)/shard_map/ppermute | solution.py:111
  25.6 3.7 %collective-permute-start.18 = (f32[128,128]{1,0:T(8,128)S(1)}, f32[128,128]{1,0:T(8,128)S(1)}, u32[]{:S(2)}, u32[]{:S(2)}) collective-permute-start(f32[128,128]{1,0:T(8,128)S(1)} %get-tuple-element.55), channel_id=1, source_target_pairs={{0,1},{1,4},{2,3},{3,6},{4,5},{5,0},{6,7},{7,2},{8,13},{9,8},{10,1... | collective-permute-start | bytes 196616 | tf_op jit(solution)/shard_map/ppermute | solution.py:111
  26.2 3.2 %collective-permute-start.17 = (f32[128,128]{1,0:T(8,128)S(1)}, f32[128,128]{1,0:T(8,128)S(1)}, u32[]{:S(2)}, u32[]{:S(2)}) collective-permute-start(f32[128,128]{1,0:T(8,128)S(1)} %get-tuple-element.55), channel_id=1, source_target_pairs={{0,1},{1,0},{2,3},{3,2},{4,5},{5,4},{6,7},{7,6},{8,9},{9,8},{10,11... | collective-permute-start | bytes 196616 | tf_op jit(solution)/shard_map/ppermute | solution.py:101
  26.3 1.2 %collective-permute-start.21 = (f32[32,128]{1,0:T(8,128)S(1)}, f32[32,128]{1,0:T(8,128)S(1)}, u32[]{:S(2)}, u32[]{:S(2)}) collective-permute-start(f32[32,128]{1,0:T(8,128)S(1)} %get-tuple-element.56.rows), channel_id=1, source_target_pairs={{0,1},{1,0},{2,3},{3,2},{4,5},{5,4},{6,7},{7,6},{8,9},{9,8},{10,11... | collective-permute-start | bytes 49160 | tf_op jit(solution)/shard_map/ppermute | solution.py:101
  29.4 1.3 %collective-permute-start.23 = (f32[128,128]{1,0:T(8,128)S(1)}, f32[128,128]{1,0:T(8,128)S(1)}, u32[]{:S(2)}, u32[]{:S(2)}) collective-permute-start(f32[128,128]{1,0:T(8,128)S(1)} %add_add_fusion.refs_0_), channel_id=1, source_target_pairs={{0,1},{1,0},{2,3},{3,2},{4,5},{5,4},{6,7},{7,6},{8,9},{9,8},{10,11... | collective-permute-start | bytes 196616 | tf_op jit(solution)/shard_map/ppermute | solution.py:101

commit v27 on v26

--- a/solution.py
+++ b/solution.py
@@ -307,7 +307,7 @@
         4 * flat_rows * times * rank * 6,
     )
 
-    def sample_kernel(sums, b, w, outer_c, each, gram_out, out):
+    def sample_kernel(sums, b, w, outer_c, each, gram_out, terms, out):
         gram = unpack(sums[:half, :], sums[sums_rows : sums_rows + 1, :])
         gram_out[...] = gram
         coupled = outer_c[...] * gram
@@ -317,11 +317,12 @@
         for j in range(chip_rows):
             made = each[j] * moved[j : j + 1, :]
             total = made if total is None else total + made
+        terms[...] = total
         out[:times, :] = total
 
-    gram_a, payload = call(
+    gram_a, terms, payload = call(
         only_on(sample_role, sample_kernel),
-        (near(rank, rank), near(times + chip_rows, rank)),
+        (near(rank, rank), near(times, rank), near(times + chip_rows, rank)),
         (sums, chip_b, w_row, outer_c, each),
         2 * rank * rank * chip_rows * 6,
     )
@@ -341,14 +342,17 @@
         vox_rows * rank * 8,
     )
 
-    terms, rows_b, rows_role = payload[:times], payload[times:], holder
+    rows_b, rows_role = payload[times:], holder
     smp_mask = sum(chip_bits)
     for group in groups_of(chip_bits + vox_bits[1:2] + vox_bits[:1] + vox_bits[2:]):
         masks = masks_of(group)
         if any(mask & smp_mask for mask in masks):
             packet = payload if rows_b.shape[0] == chip_rows else jnp.concatenate([terms, rows_b], axis=0)
-            parts = fan(packet, holder, masks)
-            gathered = [i for i, mask in enumerate(masks) if not mask & ~smp_mask]
+            gathered = [i for i, mask in enumerate(masks) if mask | smp_mask == masks[0] | smp_mask]
+            parts = [
+                send(packet if i in gathered else terms, holder, mask) if mask else swap(packet if i in gathered else terms)
+                for i, mask in enumerate(masks)
+            ]
             rows = rows_b.shape[0]
 
             def gather_kernel(*refs, gathered=gathered, rows=rows):

time: 31.2 us -> 31.2 us (level)
  transfers between devices with their start and end apart: 24 -> 24, of which waited for: 12 -> 10; matrix products, arithmetic and copies ran while one was open for 0% -> 0% of each run, Pallas kernels for 11% -> 11%
where the time goes in v27:
time: 31.2 us; the launch traced here: 30.6 us
  starting transfers between devices  15.4 us (49%)
  waiting for transfers between devices  8.67 us (28%)
  Pallas kernels  5.66 us (18%)
  between operations  0.79 us (3%)
    ppermute x12, starting transfers between devices, send(): return lax.ppermute(values, ALL, pairs)  12.6 us
    ppermute x12, waiting for transfers between devices, send(): return lax.ppermute(values, ALL, pairs)  7.88 us
    pallas_call x11, Pallas kernels, call(): pl.pallas_call(kernel, out_shape=outs, in_specs=specs, out_specs=[pl.Bloc...  5.66 us
    ppermute x12, starting transfers between devices, swap(): lax.ppermute(values, ALL, [(i, i ^ 1) for i in range(lax.axis_size(ALL))])  2.85 us
    ppermute x12, waiting for transfers between devices, swap(): lax.ppermute(values, ALL, [(i, i ^ 1) for i in range(lax.axis_size(ALL))])  0.79 us
  transfers between devices with their start and end apart: 24, of which 10 were waited for; matrix products, arithmetic and copies ran while one was open for 0% of the time, Pallas kernels for 11%

profile of v27, /device:TPU:0, one launch (start us, length us, event | category | flops | bytes accessed | tf_op | source)
XLA Modules:
  0.0 30.6 jit_solution(14050476075650789631)
XLA Ops:
  0.6 1.3 %shard_map.84 = (f32[1024,128]{1,0:T(8,128)S(1)}, f32[128,128]{1,0:T(8,128)S(1)}, f32[128,128]{1,0:T(8,128)S(1)}, f32[1,128]{1,0:T(1,128)S(1)}, f32[72,128]{1,0:T(8,128)S(1)}, /*index=5*/f32[8,128,128]{2,1,0:T(8,128)S(1)}) custom-call(f32[1024,128]{1,0:T(8,128)} %bitcast.3, f32[128,128]{1,0:T(8,128)} %c_hbm.1, f32[8,128]{1,0:T(8,128)} %b_hbm.1, ...), custom_call_target="tpu_custom_call" | custom-call | flops 67108864 | bytes 65536 | tf_op jit(solution)/shard_map/pallas_call | solution.py:63
  1.9 0.5 %collective-permute-start = (f32[72,128]{1,0:T(8,128)S(1)}, f32[72,128]{1,0:T(8,128)S(1)}, u32[]{:S(2)}, u32[]{:S(2)}) collective-permute-start(f32[72,128]{1,0:T(8,128)S(1)} %get-tuple-element.41.opened), channel_id=1, source_target_pairs={{0,1},{1,0},{2,3},{3,2},{4,5},{5,4},{6,7},{7,6},{8,9},{9,8},{10,11... | collective-permute-start | bytes 110600 | tf_op jit(solution)/shard_map/ppermute | solution.py:101
  2.5 0.2 shard_map.85
  2.7 0.1 collective-permute-start.2
  2.8 0.5 %collective-permute-start.5 = (f32[1024,128]{1,0:T(8,128)S(1)}, f32[1024,128]{1,0:T(8,128)S(1)}, u32[]{:S(2)}, u32[]{:S(2)}) collective-permute-start(f32[1024,128]{1,0:T(8,128)S(1)} %get-tuple-element.51.x.refs_0_), channel_id=1, source_target_pairs={{0,1},{1,0},{2,3},{3,2},{4,5},{5,4},{6,7},{7,6},{8,9},{9,8},{10,11... | collective-permute-start | bytes 1572872 | tf_op jit(solution)/shard_map/ppermute | solution.py:101
  3.3 0.1 collective-permute-start.4
  3.4 0.0 collective-permute-done
  3.4 0.5 %collective-permute-start.1 = (f32[80,128]{1,0:T(8,128)S(1)}, f32[80,128]{1,0:T(8,128)S(1)}, u32[]{:S(2)}, u32[]{:S(2)}) collective-permute-start(f32[80,128]{1,0:T(8,128)S(1)} %pad_maximum_fusion), channel_id=1, source_target_pairs={{0,1},{1,2},{2,3},{3,0},{4,5},{5,6},{6,7},{7,4},{8,11},{9,8},{10,9... | collective-permute-start | bytes 122888 | tf_op jit(solution)/shard_map/ppermute | solution.py:111
  3.9 0.1 collective-permute-done.2
  4.0 2.6 %collective-permute-start.3 = (f32[64,128]{1,0:T(8,128)S(1)}, f32[64,128]{1,0:T(8,128)S(1)}, u32[]{:S(2)}, u32[]{:S(2)}) collective-permute-start(f32[64,128]{1,0:T(8,128)S(1)} %add.35), channel_id=1, source_target_pairs={{0,1},{1,2},{2,3},{3,0},{4,5},{5,6},{6,7},{7,4},{8,11},{9,8},{10,9... | collective-permute-start | bytes 98312 | tf_op jit(solution)/shard_map/ppermute | solution.py:111
  6.6 0.2 shard_map.86
  6.8 1.4 %collective-permute-done.3 = f32[64,128]{1,0:T(8,128)S(1)} collective-permute-done((f32[64,128]{1,0:T(8,128)S(1)}, f32[64,128]{1,0:T(8,128)S(1)}, u32[]{:S(2)}, u32[]{:S(2)}) %collective-permute-start.3) | collective-permute-done | bytes 32800 | tf_op jit(solution)/shard_map/ppermute | solution.py:111
  8.2 0.0 collective-permute-done.1
  8.3 0.0 collective-permute-done.4.refs_7_
  8.3 0.7 %shard_map.87 = (f32[128,128]{1,0:T(8,128)S(1)}, f32[16,128]{1,0:T(8,128)S(1)}, f32[88,128]{1,0:T(8,128)S(1)}) custom-call(f32[64,128]{1,0:T(8,128)S(1)} %slice_add_fusion.refs_0_, f32[64,128]{1,0:T(8,128)S(1)} %add.36.refs_1_, f32[32,128]{1,0:T(8,128)S(1)} %pad_maximum_fusion.1.refs_2_, f32[128,128]{1,0:T(8,128)S(1)} %get-tuple-element.47.refs_3_, ...), custom_call_target="tpu_custom_call" | custom-call | flops 50331648 | bytes 65536 | tf_op jit(solution)/shard_map/pallas_call | solution.py:63
  9.0 2.2 %collective-permute-start.9 = (f32[88,128]{1,0:T(8,128)S(1)}, f32[88,128]{1,0:T(8,128)S(1)}, u32[]{:S(2)}, u32[]{:S(2)}) collective-permute-start(f32[88,128]{1,0:T(8,128)S(1)} %get-tuple-element.52), channel_id=1, source_target_pairs={{0,21},{1,0},{2,23},{3,2},{4,17},{5,4},{6,19},{7,6},{8,9},{9,28},{... | collective-permute-start | bytes 135176 | tf_op jit(solution)/shard_map/ppermute | solution.py:111
  11.2 1.0 %collective-permute-start.8 = (f32[88,128]{1,0:T(8,128)S(1)}, f32[88,128]{1,0:T(8,128)S(1)}, u32[]{:S(2)}, u32[]{:S(2)}) collective-permute-start(f32[88,128]{1,0:T(8,128)S(1)} %get-tuple-element.52), channel_id=1, source_target_pairs={{0,17},{1,0},{2,19},{3,2},{4,21},{5,4},{6,23},{7,6},{8,9},{9,24},{... | collective-permute-start | bytes 135176 | tf_op jit(solution)/shard_map/ppermute | solution.py:111
  12.2 0.0 collective-permute-start.7
  12.2 0.5 %collective-permute-start.6 = (f32[88,128]{1,0:T(8,128)S(1)}, f32[88,128]{1,0:T(8,128)S(1)}, u32[]{:S(2)}, u32[]{:S(2)}) collective-permute-start(f32[88,128]{1,0:T(8,128)S(1)} %get-tuple-element.52), channel_id=1, source_target_pairs={{0,1},{1,0},{2,3},{3,2},{4,5},{5,4},{6,7},{7,6},{8,9},{9,8},{10,11... | collective-permute-start | bytes 135176 | tf_op jit(solution)/shard_map/ppermute | solution.py:101
  12.7 0.2 collective-permute-done.9
  12.9 1.0 %collective-permute-done.8 = f32[88,128]{1,0:T(8,128)S(1)} collective-permute-done((f32[88,128]{1,0:T(8,128)S(1)}, f32[88,128]{1,0:T(8,128)S(1)}, u32[]{:S(2)}, u32[]{:S(2)}) %collective-permute-start.8) | collective-permute-done | bytes 45088 | tf_op jit(solution)/shard_map/ppermute | solution.py:111
  13.9 0.0 collective-permute-done.7
  13.9 0.0 collective-permute-done.6
  14.0 1.7 %collective-permute-start.11 = (f32[88,128]{1,0:T(8,128)S(1)}, f32[88,128]{1,0:T(8,128)S(1)}, u32[]{:S(2)}, u32[]{:S(2)}) collective-permute-start(f32[88,128]{1,0:T(8,128)S(1)} %add_add_fusion.1), channel_id=1, source_target_pairs={{0,1},{1,9},{2,3},{3,11},{4,5},{5,13},{6,7},{7,15},{8,0},{9,8},{10... | collective-permute-start | bytes 135176 | tf_op jit(solution)/shard_map/ppermute | solution.py:111
  15.6 0.1 collective-permute-start.10
  15.7 0.0 collective-permute-done.12.refs_3_.mate_moved
  15.7 0.5 %shard_map.88.refs_4_ = f32[16,128,128]{2,1,0:T(8,128)S(1)} custom-call(f32[1024,128]{1,0:T(8,128)S(1)} %get-tuple-element.51.x.refs_0_, f32[1024,128]{1,0:T(8,128)S(1)} %collective-permute-done.5.refs_8_.refs_1_, f32[128,128]{1,0:T(8,128)S(1)} %get-tuple-element.54.refs_2_.moved, f32[128,128]{1,0:T(8,128)S(1)} %collective-permute-done.12.refs_3_.mate_moved), custom_call_target="tpu_custom_call" | custom-call | flops 402653184 | bytes 65536 | tf_op jit(solution)/shard_map/pallas_call | solution.py:63
  16.2 2.9 %collective-permute-done.11 = f32[88,128]{1,0:T(8,128)S(1)} collective-permute-done((f32[88,128]{1,0:T(8,128)S(1)}, f32[88,128]{1,0:T(8,128)S(1)}, u32[]{:S(2)}, u32[]{:S(2)}) %collective-permute-start.11) | collective-permute-done | bytes 45088 | tf_op jit(solution)/shard_map/ppermute | solution.py:111
  19.2 0.4 %shard_map.89 = (f32[128,128]{1,0:T(8,128)S(1)}, f32[128,128]{1,0:T(8,128)S(1)}, f32[144,128]{1,0:T(8,128)S(1)}) custom-call(f32[88,128]{1,0:T(8,128)S(1)} %add.40.refs_0_, f32[16,128]{1,0:T(8,128)S(1)} %get-tuple-element.53.refs_1_, f32[1,128]{1,0:T(1,128)S(1)} %get-tuple-element.48.w.refs_4_.refs_2_, f32[128,128]{1,0:T(8,128)S(1)} %get-tuple-element.49.refs_5_.refs_3_, ...), custom_call_target="tpu_custom_call" | custom-call | flops 3145728 | bytes 65536 | tf_op jit(solution)/shard_map/pallas_call | solution.py:63
  19.5 0.1 collective-permute-start.16
  19.7 0.0 collective-permute-start.15
  19.7 1.4 %collective-permute-start.14 = (f32[128,128]{1,0:T(8,128)S(1)}, f32[128,128]{1,0:T(8,128)S(1)}, u32[]{:S(2)}, u32[]{:S(2)}) collective-permute-start(f32[128,128]{1,0:T(8,128)S(1)} %get-tuple-element.55), channel_id=1, source_target_pairs={{0,3},{1,0},{2,1},{3,2},{4,7},{5,4},{6,5},{7,6},{8,9},{9,10},{10,1... | collective-permute-start | bytes 196616 | tf_op jit(solution)/shard_map/ppermute | solution.py:111
  21.1 0.0 collective-permute-start.13
  21.1 0.5 %collective-permute-start.22 = (f32[128,128]{1,0:T(8,128)S(1)}, f32[128,128]{1,0:T(8,128)S(1)}, u32[]{:S(2)}, u32[]{:S(2)}) collective-permute-start(f32[128,128]{1,0:T(8,128)S(1)} %get-tuple-element.59.gram), channel_id=1, source_target_pairs={{0,1},{1,0},{2,3},{3,2},{4,5},{5,4},{6,7},{7,6},{8,9},{9,8},{10,11... | collective-permute-start | bytes 196616 | tf_op jit(solution)/shard_map/ppermute | solution.py:101
  21.6 1.4 %collective-permute-done.14.refs_1_ = f32[128,128]{1,0:T(8,128)S(1)} collective-permute-done((f32[128,128]{1,0:T(8,128)S(1)}, f32[128,128]{1,0:T(8,128)S(1)}, u32[]{:S(2)}, u32[]{:S(2)}) %collective-permute-start.14) | collective-permute-done | bytes 65568 | tf_op jit(solution)/shard_map/ppermute | solution.py:111
  23.0 1.0 %collective-permute-start.20 = (f32[128,128]{1,0:T(8,128)S(1)}, f32[128,128]{1,0:T(8,128)S(1)}, u32[]{:S(2)}, u32[]{:S(2)}) collective-permute-start(f32[128,128]{1,0:T(8,128)S(1)} %get-tuple-element.57), channel_id=1, source_target_pairs={{0,1},{1,20},{2,3},{3,22},{4,5},{5,16},{6,7},{7,18},{8,29},{9,8},{... | collective-permute-start | bytes 196616 | tf_op jit(solution)/shard_map/ppermute | solution.py:111
  24.0 1.6 %collective-permute-start.19 = (f32[128,128]{1,0:T(8,128)S(1)}, f32[128,128]{1,0:T(8,128)S(1)}, u32[]{:S(2)}, u32[]{:S(2)}) collective-permute-start(f32[128,128]{1,0:T(8,128)S(1)} %get-tuple-element.57), channel_id=1, source_target_pairs={{0,1},{1,16},{2,3},{3,18},{4,5},{5,20},{6,7},{7,22},{8,25},{9,8},{... | collective-permute-start | bytes 196616 | tf_op jit(solution)/shard_map/ppermute | solution.py:111
  25.5 0.5 %collective-permute-start.18 = (f32[128,128]{1,0:T(8,128)S(1)}, f32[128,128]{1,0:T(8,128)S(1)}, u32[]{:S(2)}, u32[]{:S(2)}) collective-permute-start(f32[128,128]{1,0:T(8,128)S(1)} %get-tuple-element.57), channel_id=1, source_target_pairs={{0,1},{1,4},{2,3},{3,6},{4,5},{5,0},{6,7},{7,2},{8,13},{9,8},{10,1... | collective-permute-start | bytes 196616 | tf_op jit(solution)/shard_map/ppermute | solution.py:111
  26.1 0.1 collective-permute-start.17
  26.2 0.4 %collective-permute-start.21 = (f32[32,128]{1,0:T(8,128)S(1)}, f32[32,128]{1,0:T(8,128)S(1)}, u32[]{:S(2)}, u32[]{:S(2)}) collective-permute-start(f32[32,128]{1,0:T(8,128)S(1)} %get-tuple-element.58.rows), channel_id=1, source_target_pairs={{0,1},{1,0},{2,3},{3,2},{4,5},{5,4},{6,7},{7,6},{8,9},{9,8},{10,11... | collective-permute-start | bytes 49160 | tf_op jit(solution)/shard_map/ppermute | solution.py:101
  26.6 0.7 %shard_map.91 = (f32[128,128]{1,0:T(8,128)}, f32[1,128]{1,0:T(1,128)S(1)}, f32[128,128]{1,0:T(8,128)S(1)}) custom-call(f32[128,128]{1,0:T(8,128)S(1)} %get-tuple-element.59.gram, f32[128,128]{1,0:T(8,128)S(1)} %collective-permute-done.22.mate_gram, f32[128,128]{1,0:T(8,128)S(1)} %get-tuple-element.54.refs_2_.moved, ...), custom_call_target="tpu_custom_call" | custom-call | flops 131072 | bytes 65536 | tf_op jit(solution)/shard_map/pallas_call | solution.py:63
  27.3 0.2 collective-permute-done.21.mate_rows
  27.4 0.9 %shard_map.92 = (f32[8,128]{1,0:T(8,128)}, f32[128,128]{1,0:T(8,128)S(1)}, f32[1,128]{1,0:T(1,128)S(1)}, f32[1,128]{1,0:T(1,128)S(1)}) custom-call(f32[32,128]{1,0:T(8,128)S(1)} %get-tuple-element.58.rows, f32[32,128]{1,0:T(8,128)S(1)} %collective-permute-done.21.mate_rows, f32[128,128]{1,0:T(8,128)S(1)} %get-tuple-element.43.c, ...), custom_call_target="tpu_custom_call" | custom-call | flops 16777216 | bytes 65536 | tf_op jit(solution)/shard_map/pallas_call | solution.py:63
  28.3 0.2 collective-permute-done.20
  28.5 0.7 %collective-permute-done.19 = f32[128,128]{1,0:T(8,128)S(1)} collective-permute-done((f32[128,128]{1,0:T(8,128)S(1)}, f32[128,128]{1,0:T(8,128)S(1)}, u32[]{:S(2)}, u32[]{:S(2)}) %collective-permute-start.19) | collective-permute-done | bytes 65568 | tf_op jit(solution)/shard_map/ppermute | solution.py:111
  29.3 0.1 collective-permute-start.23
  29.4 0.7 %shard_map.93 = (f32[128,128]{1,0:T(8,128)}, f32[1,128]{1,0:T(1,128)}) custom-call(f32[128,128]{1,0:T(8,128)S(1)} %add_add_fusion.refs_0_, f32[128,128]{1,0:T(8,128)S(1)} %get-tuple-element.71.refs_1_.refs_3_, f32[1,128]{1,0:T(1,128)S(1)} %get-tuple-element.72.refs_2_.refs_4_, f32[1,128]{1,0:T(1,128)S(1)} %get-tuple-element.73.refs_3_.refs_5_), custom_call_target="tpu_custom_call" | custom-call | flops 131072 | bytes 65536 | tf_op jit(solution)/shard_map/pallas_call | solution.py:63
  30.1 0.5 %collective-permute-done.23.refs_2_ = f32[128,128]{1,0:T(8,128)S(1)} collective-permute-done((f32[128,128]{1,0:T(8,128)S(1)}, f32[128,128]{1,0:T(8,128)S(1)}, u32[]{:S(2)}, u32[]{:S(2)}) %collective-permute-start.23) | collective-permute-done | bytes 65568 | tf_op jit(solution)/shard_map/ppermute | solution.py:101
  (23 shorter events, 0.1 us)
Async XLA Ops:
  1.9 1.4 %collective-permute-start = (f32[72,128]{1,0:T(8,128)S(1)}, f32[72,128]{1,0:T(8,128)S(1)}, u32[]{:S(2)}, u32[]{:S(2)}) collective-permute-start(f32[72,128]{1,0:T(8,128)S(1)} %get-tuple-element.41.opened), channel_id=1, source_target_pairs={{0,1},{1,0},{2,3},{3,2},{4,5},{5,4},{6,7},{7,6},{8,9},{9,8},{10,11... | collective-permute-start | bytes 110600 | tf_op jit(solution)/shard_map/ppermute | solution.py:101
  2.7 1.3 %collective-permute-start.2 = (f32[64,128]{1,0:T(8,128)S(1)}, f32[64,128]{1,0:T(8,128)S(1)}, u32[]{:S(2)}, u32[]{:S(2)}) collective-permute-start(f32[64,128]{1,0:T(8,128)S(1)} %get-tuple-element.46), channel_id=1, source_target_pairs={{0,1},{1,0},{2,3},{3,2},{4,5},{5,4},{6,7},{7,6},{8,9},{9,8},{10,11... | collective-permute-start | bytes 98312 | tf_op jit(solution)/shard_map/ppermute | solution.py:101
  2.8 5.4 %collective-permute-start.5 = (f32[1024,128]{1,0:T(8,128)S(1)}, f32[1024,128]{1,0:T(8,128)S(1)}, u32[]{:S(2)}, u32[]{:S(2)}) collective-permute-start(f32[1024,128]{1,0:T(8,128)S(1)} %get-tuple-element.51.x.refs_0_), channel_id=1, source_target_pairs={{0,1},{1,0},{2,3},{3,2},{4,5},{5,4},{6,7},{7,6},{8,9},{9,8},{10,11... | collective-permute-start | bytes 1572872 | tf_op jit(solution)/shard_map/ppermute | solution.py:101
  3.3 5.0 %collective-permute-start.4 = (f32[8,128,128]{2,1,0:T(8,128)S(1)}, f32[8,128,128]{2,1,0:T(8,128)S(1)}, u32[]{:S(2)}, u32[]{:S(2)}) collective-permute-start(f32[8,128,128]{2,1,0:T(8,128)S(1)} %get-tuple-element.50.refs_6_), channel_id=1, source_target_pairs={{0,1},{1,0},{2,3},{3,2},{4,5},{5,4},{6,7},{7,6},{8,9},{9,8},{10,11... | collective-permute-start | bytes 1572872 | tf_op jit(solution)/shard_map/ppermute | solution.py:101
  3.4 4.8 %collective-permute-start.1 = (f32[80,128]{1,0:T(8,128)S(1)}, f32[80,128]{1,0:T(8,128)S(1)}, u32[]{:S(2)}, u32[]{:S(2)}) collective-permute-start(f32[80,128]{1,0:T(8,128)S(1)} %pad_maximum_fusion), channel_id=1, source_target_pairs={{0,1},{1,2},{2,3},{3,0},{4,5},{5,6},{6,7},{7,4},{8,11},{9,8},{10,9... | collective-permute-start | bytes 122888 | tf_op jit(solution)/shard_map/ppermute | solution.py:111
  4.0 4.2 %collective-permute-start.3 = (f32[64,128]{1,0:T(8,128)S(1)}, f32[64,128]{1,0:T(8,128)S(1)}, u32[]{:S(2)}, u32[]{:S(2)}) collective-permute-start(f32[64,128]{1,0:T(8,128)S(1)} %add.35), channel_id=1, source_target_pairs={{0,1},{1,2},{2,3},{3,0},{4,5},{5,6},{6,7},{7,4},{8,11},{9,8},{10,9... | collective-permute-start | bytes 98312 | tf_op jit(solution)/shard_map/ppermute | solution.py:111
  9.0 3.9 %collective-permute-start.9 = (f32[88,128]{1,0:T(8,128)S(1)}, f32[88,128]{1,0:T(8,128)S(1)}, u32[]{:S(2)}, u32[]{:S(2)}) collective-permute-start(f32[88,128]{1,0:T(8,128)S(1)} %get-tuple-element.52), channel_id=1, source_target_pairs={{0,21},{1,0},{2,23},{3,2},{4,17},{5,4},{6,19},{7,6},{8,9},{9,28},{... | collective-permute-start | bytes 135176 | tf_op jit(solution)/shard_map/ppermute | solution.py:111
  11.2 2.7 %collective-permute-start.8 = (f32[88,128]{1,0:T(8,128)S(1)}, f32[88,128]{1,0:T(8,128)S(1)}, u32[]{:S(2)}, u32[]{:S(2)}) collective-permute-start(f32[88,128]{1,0:T(8,128)S(1)} %get-tuple-element.52), channel_id=1, source_target_pairs={{0,17},{1,0},{2,19},{3,2},{4,21},{5,4},{6,23},{7,6},{8,9},{9,24},{... | collective-permute-start | bytes 135176 | tf_op jit(solution)/shard_map/ppermute | solution.py:111
  12.2 1.7 %collective-permute-start.7 = (f32[88,128]{1,0:T(8,128)S(1)}, f32[88,128]{1,0:T(8,128)S(1)}, u32[]{:S(2)}, u32[]{:S(2)}) collective-permute-start(f32[88,128]{1,0:T(8,128)S(1)} %get-tuple-element.52), channel_id=1, source_target_pairs={{0,5},{1,0},{2,7},{3,2},{4,1},{5,4},{6,3},{7,6},{8,9},{9,12},{10,1... | collective-permute-start | bytes 135176 | tf_op jit(solution)/shard_map/ppermute | solution.py:111
  12.2 1.7 %collective-permute-start.6 = (f32[88,128]{1,0:T(8,128)S(1)}, f32[88,128]{1,0:T(8,128)S(1)}, u32[]{:S(2)}, u32[]{:S(2)}) collective-permute-start(f32[88,128]{1,0:T(8,128)S(1)} %get-tuple-element.52), channel_id=1, source_target_pairs={{0,1},{1,0},{2,3},{3,2},{4,5},{5,4},{6,7},{7,6},{8,9},{9,8},{10,11... | collective-permute-start | bytes 135176 | tf_op jit(solution)/shard_map/ppermute | solution.py:101
  12.7 3.0 %collective-permute-start.12 = (f32[128,128]{1,0:T(8,128)S(1)}, f32[128,128]{1,0:T(8,128)S(1)}, u32[]{:S(2)}, u32[]{:S(2)}) collective-permute-start(f32[128,128]{1,0:T(8,128)S(1)} %get-tuple-element.54.refs_2_.moved), channel_id=1, source_target_pairs={{0,1},{1,0},{2,3},{3,2},{4,5},{5,4},{6,7},{7,6},{8,9},{9,8},{10,11... | collective-permute-start | bytes 196616 | tf_op jit(solution)/shard_map/ppermute | solution.py:101
  14.0 5.2 %collective-permute-start.11 = (f32[88,128]{1,0:T(8,128)S(1)}, f32[88,128]{1,0:T(8,128)S(1)}, u32[]{:S(2)}, u32[]{:S(2)}) collective-permute-start(f32[88,128]{1,0:T(8,128)S(1)} %add_add_fusion.1), channel_id=1, source_target_pairs={{0,1},{1,9},{2,3},{3,11},{4,5},{5,13},{6,7},{7,15},{8,0},{9,8},{10... | collective-permute-start | bytes 135176 | tf_op jit(solution)/shard_map/ppermute | solution.py:111
  15.6 3.5 %collective-permute-start.10 = (f32[88,128]{1,0:T(8,128)S(1)}, f32[88,128]{1,0:T(8,128)S(1)}, u32[]{:S(2)}, u32[]{:S(2)}) collective-permute-start(f32[88,128]{1,0:T(8,128)S(1)} %add_add_fusion.1), channel_id=1, source_target_pairs={{0,1},{1,0},{2,3},{3,2},{4,5},{5,4},{6,7},{7,6},{8,9},{9,8},{10,11... | collective-permute-start | bytes 135176 | tf_op jit(solution)/shard_map/ppermute | solution.py:101
  19.5 3.4 %collective-permute-start.16 = (f32[144,128]{1,0:T(8,128)S(1)}, f32[144,128]{1,0:T(8,128)S(1)}, u32[]{:S(2)}, u32[]{:S(2)}) collective-permute-start(f32[144,128]{1,0:T(8,128)S(1)} %get-tuple-element.56), channel_id=1, source_target_pairs={{0,10},{1,0},{2,8},{3,2},{4,14},{5,4},{6,12},{7,6},{8,9},{9,3},{10... | collective-permute-start | bytes 221192 | tf_op jit(solution)/shard_map/ppermute | solution.py:111
  19.7 3.3 %collective-permute-start.15 = (f32[144,128]{1,0:T(8,128)S(1)}, f32[144,128]{1,0:T(8,128)S(1)}, u32[]{:S(2)}, u32[]{:S(2)}) collective-permute-start(f32[144,128]{1,0:T(8,128)S(1)} %get-tuple-element.56), channel_id=1, source_target_pairs={{0,8},{1,0},{2,10},{3,2},{4,12},{5,4},{6,14},{7,6},{8,9},{9,1},{10... | collective-permute-start | bytes 221192 | tf_op jit(solution)/shard_map/ppermute | solution.py:111
  19.7 3.3 %collective-permute-start.14 = (f32[128,128]{1,0:T(8,128)S(1)}, f32[128,128]{1,0:T(8,128)S(1)}, u32[]{:S(2)}, u32[]{:S(2)}) collective-permute-start(f32[128,128]{1,0:T(8,128)S(1)} %get-tuple-element.55), channel_id=1, source_target_pairs={{0,3},{1,0},{2,1},{3,2},{4,7},{5,4},{6,5},{7,6},{8,9},{9,10},{10,1... | collective-permute-start | bytes 196616 | tf_op jit(solution)/shard_map/ppermute | solution.py:111
  21.1 1.9 %collective-permute-start.13 = (f32[128,128]{1,0:T(8,128)S(1)}, f32[128,128]{1,0:T(8,128)S(1)}, u32[]{:S(2)}, u32[]{:S(2)}) collective-permute-start(f32[128,128]{1,0:T(8,128)S(1)} %get-tuple-element.55), channel_id=1, source_target_pairs={{0,1},{1,0},{2,3},{3,2},{4,5},{5,4},{6,7},{7,6},{8,9},{9,8},{10,11... | collective-permute-start | bytes 196616 | tf_op jit(solution)/shard_map/ppermute | solution.py:101
  21.1 5.2 %collective-permute-start.22 = (f32[128,128]{1,0:T(8,128)S(1)}, f32[128,128]{1,0:T(8,128)S(1)}, u32[]{:S(2)}, u32[]{:S(2)}) collective-permute-start(f32[128,128]{1,0:T(8,128)S(1)} %get-tuple-element.59.gram), channel_id=1, source_target_pairs={{0,1},{1,0},{2,3},{3,2},{4,5},{5,4},{6,7},{7,6},{8,9},{9,8},{10,11... | collective-permute-start | bytes 196616 | tf_op jit(solution)/shard_map/ppermute | solution.py:101
  23.0 5.5 %collective-permute-start.20 = (f32[128,128]{1,0:T(8,128)S(1)}, f32[128,128]{1,0:T(8,128)S(1)}, u32[]{:S(2)}, u32[]{:S(2)}) collective-permute-start(f32[128,128]{1,0:T(8,128)S(1)} %get-tuple-element.57), channel_id=1, source_target_pairs={{0,1},{1,20},{2,3},{3,22},{4,5},{5,16},{6,7},{7,18},{8,29},{9,8},{... | collective-permute-start | bytes 196616 | tf_op jit(solution)/shard_map/ppermute | solution.py:111
  24.0 5.3 %collective-permute-start.19 = (f32[128,128]{1,0:T(8,128)S(1)}, f32[128,128]{1,0:T(8,128)S(1)}, u32[]{:S(2)}, u32[]{:S(2)}) collective-permute-start(f32[128,128]{1,0:T(8,128)S(1)} %get-tuple-element.57), channel_id=1, source_target_pairs={{0,1},{1,16},{2,3},{3,18},{4,5},{5,20},{6,7},{7,22},{8,25},{9,8},{... | collective-permute-start | bytes 196616 | tf_op jit(solution)/shard_map/ppermute | solution.py:111
  25.5 3.7 %collective-permute-start.18 = (f32[128,128]{1,0:T(8,128)S(1)}, f32[128,128]{1,0:T(8,128)S(1)}, u32[]{:S(2)}, u32[]{:S(2)}) collective-permute-start(f32[128,128]{1,0:T(8,128)S(1)} %get-tuple-element.57), channel_id=1, source_target_pairs={{0,1},{1,4},{2,3},{3,6},{4,5},{5,0},{6,7},{7,2},{8,13},{9,8},{10,1... | collective-permute-start | bytes 196616 | tf_op jit(solution)/shard_map/ppermute | solution.py:111
  26.1 3.2 %collective-permute-start.17 = (f32[128,128]{1,0:T(8,128)S(1)}, f32[128,128]{1,0:T(8,128)S(1)}, u32[]{:S(2)}, u32[]{:S(2)}) collective-permute-start(f32[128,128]{1,0:T(8,128)S(1)} %get-tuple-element.57), channel_id=1, source_target_pairs={{0,1},{1,0},{2,3},{3,2},{4,5},{5,4},{6,7},{7,6},{8,9},{9,8},{10,11... | collective-permute-start | bytes 196616 | tf_op jit(solution)/shard_map/ppermute | solution.py:101
  26.2 1.2 %collective-permute-start.21 = (f32[32,128]{1,0:T(8,128)S(1)}, f32[32,128]{1,0:T(8,128)S(1)}, u32[]{:S(2)}, u32[]{:S(2)}) collective-permute-start(f32[32,128]{1,0:T(8,128)S(1)} %get-tuple-element.58.rows), channel_id=1, source_target_pairs={{0,1},{1,0},{2,3},{3,2},{4,5},{5,4},{6,7},{7,6},{8,9},{9,8},{10,11... | collective-permute-start | bytes 49160 | tf_op jit(solution)/shard_map/ppermute | solution.py:101
  29.3 1.3 %collective-permute-start.23 = (f32[128,128]{1,0:T(8,128)S(1)}, f32[128,128]{1,0:T(8,128)S(1)}, u32[]{:S(2)}, u32[]{:S(2)}) collective-permute-start(f32[128,128]{1,0:T(8,128)S(1)} %add_add_fusion.refs_0_), channel_id=1, source_target_pairs={{0,1},{1,0},{2,3},{3,2},{4,5},{5,4},{6,7},{7,6},{8,9},{9,8},{10,11... | collective-permute-start | bytes 196616 | tf_op jit(solution)/shard_map/ppermute | solution.py:101

commit v28 on v26

--- a/solution.py
+++ b/solution.py
@@ -184,15 +184,13 @@
             total = total + made[j] * b[j : j + 1, :]
         out[:cut, :] = total
 
-    def open_kernel(x_hbm, c_hbm, b_hbm, a_hbm, w_hbm, x, c, a, w, out, con, sems):
+    def open_kernel(x_hbm, c_hbm, b_hbm, x, c, out, con, sems):
         near_half, far_half = pl.ds(0, cut * smp_rows), pl.ds(cut * smp_rows, cut * smp_rows)
         copies = [
-            pltpu.make_async_copy(c_hbm, c, sems.at[0]),
-            pltpu.make_async_copy(x_hbm.at[near_half, :], x.at[near_half, :], sems.at[1]),
+            pltpu.make_async_copy(x_hbm.at[near_half, :], x.at[near_half, :], sems.at[0]),
+            pltpu.make_async_copy(c_hbm, c, sems.at[1]),
             pltpu.make_async_copy(b_hbm, out.at[pl.ds(cut, smp_rows), :], sems.at[2]),
             pltpu.make_async_copy(x_hbm.at[far_half, :], x.at[far_half, :], sems.at[3]),
-            pltpu.make_async_copy(a_hbm, a, sems.at[4]),
-            pltpu.make_async_copy(w_hbm, w, sems.at[5]),
         ]
         for copy in copies:
             copy.start()
@@ -202,20 +200,18 @@
         for copy in copies[3:]:
             copy.wait()
 
-    x, c_near, a_near, w_row, opened, con = call(
+    x, c_near, opened, con = call(
         open_kernel,
         (
             near(flat_rows, times),
             near(times, rank),
-            near(vox_rows, rank),
-            near(1, rank),
             near(cut + smp_rows, rank),
             near(smp_rows, vox_rows, rank),
         ),
-        (ensemble.reshape(flat_rows, times), time_factor, sample_factor, voxel_factor, weights.reshape(1, rank)),
+        (ensemble.reshape(flat_rows, times), time_factor, sample_factor),
         flat_rows * times * rank * 4,
-        scratch=(pltpu.SemaphoreType.DMA((6,)),),
-        in_hbm=5,
+        scratch=(pltpu.SemaphoreType.DMA((4,)),),
+        in_hbm=3,
     )
 
     def late_kernel(x, c, opened, con_in, out, con):
@@ -229,13 +225,24 @@
         aliases={3: 1},
     )
 
-    def weigh_kernel(c, w, outer, outer_c):
+    def weigh_kernel(a_hbm, w_hbm, c, a, w, outer, outer_c, sems):
+        copies = [pltpu.make_async_copy(w_hbm, w, sems.at[0]), pltpu.make_async_copy(a_hbm, a, sems.at[1])]
+        for copy in copies:
+            copy.start()
+        gram = dot_rows(c[...], c[...])
+        copies[0].wait()
         squared = dot_rows(w[...], w[...])
         outer[...] = squared
-        outer_c[...] = squared * dot_rows(c[...], c[...])
-
-    outer, outer_c = call(
-        weigh_kernel, (near(rank, rank), near(rank, rank)), (c_near, w_row), 2 * rank * rank * times * 4
+        outer_c[...] = squared * gram
+        copies[1].wait()
+
+    a_near, w_row, outer, outer_c = call(
+        weigh_kernel,
+        (near(vox_rows, rank), near(1, rank), near(rank, rank), near(rank, rank)),
+        (voxel_factor, weights.reshape(1, rank), c_near),
+        2 * rank * rank * times * 4,
+        scratch=(pltpu.SemaphoreType.DMA((2,)),),
+        in_hbm=2,
     )
 
     late_x, late_opened = lax.optimization_barrier((x, late_opened))

time: 31.2 us -> 31.2 us (level)
  waiting for transfers between devices: 8.74 us -> 8.08 us
  Pallas kernels: 5.66 us -> 6.26 us
    ppermute x12, waiting for transfers between devices: 7.95 us -> 7.29 us  [send(): return lax.ppermute(values, ALL, pairs)]
    pallas_call x11, Pallas kernels: 5.66 us -> 6.26 us  [call(): pl.pallas_call(kernel, out_shape=outs, in_specs=specs, out_specs=[pl.Bloc...]
  transfers between devices with their start and end apart: 24 -> 24, of which waited for: 12 -> 12; matrix products, arithmetic and copies ran while one was open for 0% -> 0% of each run, Pallas kernels for 11% -> 13%
where the time goes in v28:
time: 31.2 us; the launch traced here: 30.6 us
  starting transfers between devices  15.4 us (49%)
  waiting for transfers between devices  8.08 us (26%)
  Pallas kernels  6.26 us (20%)
  between operations  0.79 us (3%)
    ppermute x12, starting transfers between devices, send(): return lax.ppermute(values, ALL, pairs)  12.6 us
    ppermute x12, waiting for transfers between devices, send(): return lax.ppermute(values, ALL, pairs)  7.29 us
    pallas_call x11, Pallas kernels, call(): pl.pallas_call(kernel, out_shape=outs, in_specs=specs, out_specs=[pl.Bloc...  6.26 us
    ppermute x12, starting transfers between devices, swap(): lax.ppermute(values, ALL, [(i, i ^ 1) for i in range(lax.axis_size(ALL))])  2.85 us
    ppermute x12, waiting for transfers between devices, swap(): lax.ppermute(values, ALL, [(i, i ^ 1) for i in range(lax.axis_size(ALL))])  0.79 us
  transfers between devices with their start and end apart: 24, of which 12 were waited for; matrix products, arithmetic and copies ran while one was open for 0% of the time, Pallas kernels for 13%

profile of v28, /device:TPU:0, one launch (start us, length us, event | category | flops | bytes accessed | tf_op | source)
XLA Modules:
  0.0 30.6 jit_solution(2405797314558929985)
XLA Ops:
  0.6 1.2 %shard_map.84 = (f32[1024,128]{1,0:T(8,128)S(1)}, f32[128,128]{1,0:T(8,128)S(1)}, f32[72,128]{1,0:T(8,128)S(1)}, f32[8,128,128]{2,1,0:T(8,128)S(1)}) custom-call(f32[1024,128]{1,0:T(8,128)} %bitcast.3, f32[128,128]{1,0:T(8,128)} %c_hbm.1, f32[8,128]{1,0:T(8,128)} %b_hbm.1), custom_call_target="tpu_custom_call" | custom-call | flops 67108864 | bytes 65536 | tf_op jit(solution)/shard_map/pallas_call | solution.py:63
  1.9 0.5 %collective-permute-start = (f32[72,128]{1,0:T(8,128)S(1)}, f32[72,128]{1,0:T(8,128)S(1)}, u32[]{:S(2)}, u32[]{:S(2)}) collective-permute-start(f32[72,128]{1,0:T(8,128)S(1)} %get-tuple-element.40.opened), channel_id=1, source_target_pairs={{0,1},{1,0},{2,3},{3,2},{4,5},{5,4},{6,7},{7,6},{8,9},{9,8},{10,11... | collective-permute-start | bytes 110600 | tf_op jit(solution)/shard_map/ppermute | solution.py:101
  2.4 0.2 shard_map.85
  2.6 0.1 collective-permute-start.2
  2.8 0.5 %collective-permute-start.5 = (f32[1024,128]{1,0:T(8,128)S(1)}, f32[1024,128]{1,0:T(8,128)S(1)}, u32[]{:S(2)}, u32[]{:S(2)}) collective-permute-start(f32[1024,128]{1,0:T(8,128)S(1)} %get-tuple-element.50.x.refs_0_), channel_id=1, source_target_pairs={{0,1},{1,0},{2,3},{3,2},{4,5},{5,4},{6,7},{7,6},{8,9},{9,8},{10,11... | collective-permute-start | bytes 1572872 | tf_op jit(solution)/shard_map/ppermute | solution.py:101
  3.2 0.1 collective-permute-start.4
  3.3 0.0 collective-permute-done
  3.3 0.5 %collective-permute-start.1 = (f32[80,128]{1,0:T(8,128)S(1)}, f32[80,128]{1,0:T(8,128)S(1)}, u32[]{:S(2)}, u32[]{:S(2)}) collective-permute-start(f32[80,128]{1,0:T(8,128)S(1)} %pad_maximum_fusion), channel_id=1, source_target_pairs={{0,1},{1,2},{2,3},{3,0},{4,5},{5,6},{6,7},{7,4},{8,11},{9,8},{10,9... | collective-permute-start | bytes 122888 | tf_op jit(solution)/shard_map/ppermute | solution.py:111
  3.8 0.1 collective-permute-done.2
  3.9 2.6 %collective-permute-start.3 = (f32[64,128]{1,0:T(8,128)S(1)}, f32[64,128]{1,0:T(8,128)S(1)}, u32[]{:S(2)}, u32[]{:S(2)}) collective-permute-start(f32[64,128]{1,0:T(8,128)S(1)} %add.35), channel_id=1, source_target_pairs={{0,1},{1,2},{2,3},{3,0},{4,5},{5,6},{6,7},{7,4},{8,11},{9,8},{10,9... | collective-permute-start | bytes 98312 | tf_op jit(solution)/shard_map/ppermute | solution.py:111
  6.5 0.9 %shard_map.86 = (f32[128,128]{1,0:T(8,128)S(1)}, f32[1,128]{1,0:T(1,128)S(1)}, f32[128,128]{1,0:T(8,128)S(1)}, f32[128,128]{1,0:T(8,128)S(1)}) custom-call(f32[128,128]{1,0:T(8,128)} %a_hbm.1, f32[1,128]{1,0:T(1,128)} %bitcast.4, f32[128,128]{1,0:T(8,128)S(1)} %get-tuple-element.42.c), custom_call_target="tpu_custom_call" | custom-call | flops 16777216 | bytes 65536 | tf_op jit(solution)/shard_map/pallas_call | solution.py:63
  7.4 0.7 %collective-permute-done.3 = f32[64,128]{1,0:T(8,128)S(1)} collective-permute-done((f32[64,128]{1,0:T(8,128)S(1)}, f32[64,128]{1,0:T(8,128)S(1)}, u32[]{:S(2)}, u32[]{:S(2)}) %collective-permute-start.3) | collective-permute-done | bytes 32800 | tf_op jit(solution)/shard_map/ppermute | solution.py:111
  8.2 0.0 collective-permute-done.1
  8.2 0.0 collective-permute-done.4.refs_7_
  8.2 0.7 %shard_map.87 = (f32[128,128]{1,0:T(8,128)S(1)}, f32[16,128]{1,0:T(8,128)S(1)}, f32[88,128]{1,0:T(8,128)S(1)}) custom-call(f32[64,128]{1,0:T(8,128)S(1)} %slice_add_fusion.refs_0_, f32[64,128]{1,0:T(8,128)S(1)} %add.36.refs_1_, f32[32,128]{1,0:T(8,128)S(1)} %pad_maximum_fusion.1.refs_2_, f32[128,128]{1,0:T(8,128)S(1)} %get-tuple-element.46.refs_3_, ...), custom_call_target="tpu_custom_call" | custom-call | flops 50331648 | bytes 65536 | tf_op jit(solution)/shard_map/pallas_call | solution.py:63
  9.0 2.2 %collective-permute-start.9 = (f32[88,128]{1,0:T(8,128)S(1)}, f32[88,128]{1,0:T(8,128)S(1)}, u32[]{:S(2)}, u32[]{:S(2)}) collective-permute-start(f32[88,128]{1,0:T(8,128)S(1)} %get-tuple-element.51), channel_id=1, source_target_pairs={{0,21},{1,0},{2,23},{3,2},{4,17},{5,4},{6,19},{7,6},{8,9},{9,28},{... | collective-permute-start | bytes 135176 | tf_op jit(solution)/shard_map/ppermute | solution.py:111
  11.1 1.0 %collective-permute-start.8 = (f32[88,128]{1,0:T(8,128)S(1)}, f32[88,128]{1,0:T(8,128)S(1)}, u32[]{:S(2)}, u32[]{:S(2)}) collective-permute-start(f32[88,128]{1,0:T(8,128)S(1)} %get-tuple-element.51), channel_id=1, source_target_pairs={{0,17},{1,0},{2,19},{3,2},{4,21},{5,4},{6,23},{7,6},{8,9},{9,24},{... | collective-permute-start | bytes 135176 | tf_op jit(solution)/shard_map/ppermute | solution.py:111
  12.2 0.5 %collective-permute-start.6 = (f32[88,128]{1,0:T(8,128)S(1)}, f32[88,128]{1,0:T(8,128)S(1)}, u32[]{:S(2)}, u32[]{:S(2)}) collective-permute-start(f32[88,128]{1,0:T(8,128)S(1)} %get-tuple-element.51), channel_id=1, source_target_pairs={{0,1},{1,0},{2,3},{3,2},{4,5},{5,4},{6,7},{7,6},{8,9},{9,8},{10,11... | collective-permute-start | bytes 135176 | tf_op jit(solution)/shard_map/ppermute | solution.py:101
  12.7 0.0 collective-permute-start.12
  12.7 0.2 collective-permute-done.9
  12.8 1.0 %collective-permute-done.8 = f32[88,128]{1,0:T(8,128)S(1)} collective-permute-done((f32[88,128]{1,0:T(8,128)S(1)}, f32[88,128]{1,0:T(8,128)S(1)}, u32[]{:S(2)}, u32[]{:S(2)}) %collective-permute-start.8) | collective-permute-done | bytes 45088 | tf_op jit(solution)/shard_map/ppermute | solution.py:111
  13.9 0.0 collective-permute-done.7
  13.9 0.0 collective-permute-done.6
  13.9 1.7 %collective-permute-start.11 = (f32[88,128]{1,0:T(8,128)S(1)}, f32[88,128]{1,0:T(8,128)S(1)}, u32[]{:S(2)}, u32[]{:S(2)}) collective-permute-start(f32[88,128]{1,0:T(8,128)S(1)} %add_add_fusion.1), channel_id=1, source_target_pairs={{0,1},{1,9},{2,3},{3,11},{4,5},{5,13},{6,7},{7,15},{8,0},{9,8},{10... | collective-permute-start | bytes 135176 | tf_op jit(solution)/shard_map/ppermute | solution.py:111
  15.6 0.1 collective-permute-start.10
  15.7 0.5 %shard_map.88.refs_4_ = f32[16,128,128]{2,1,0:T(8,128)S(1)} custom-call(f32[1024,128]{1,0:T(8,128)S(1)} %get-tuple-element.50.x.refs_0_, f32[1024,128]{1,0:T(8,128)S(1)} %collective-permute-done.5.refs_8_.refs_1_, f32[128,128]{1,0:T(8,128)S(1)} %get-tuple-element.53.refs_2_.moved, f32[128,128]{1,0:T(8,128)S(1)} %collective-permute-done.12.refs_3_.mate_moved), custom_call_target="tpu_custom_call" | custom-call | flops 402653184 | bytes 65536 | tf_op jit(solution)/shard_map/pallas_call | solution.py:63
  16.2 2.9 %collective-permute-done.11 = f32[88,128]{1,0:T(8,128)S(1)} collective-permute-done((f32[88,128]{1,0:T(8,128)S(1)}, f32[88,128]{1,0:T(8,128)S(1)}, u32[]{:S(2)}, u32[]{:S(2)}) %collective-permute-start.11) | collective-permute-done | bytes 45088 | tf_op jit(solution)/shard_map/ppermute | solution.py:111
  19.1 0.4 %shard_map.89 = (f32[128,128]{1,0:T(8,128)S(1)}, f32[144,128]{1,0:T(8,128)S(1)}) custom-call(f32[88,128]{1,0:T(8,128)S(1)} %add.40.refs_0_, f32[16,128]{1,0:T(8,128)S(1)} %get-tuple-element.52.refs_1_, f32[1,128]{1,0:T(1,128)S(1)} %get-tuple-element.47.refs_4_.refs_2_.w, f32[128,128]{1,0:T(8,128)S(1)} %get-tuple-element.48.refs_5_.refs_3_, ...), custom_call_target="tpu_custom_call" | custom-call | flops 3145728 | bytes 65536 | tf_op jit(solution)/shard_map/pallas_call | solution.py:63
  19.5 0.1 collective-permute-start.16
  19.6 0.0 collective-permute-start.15
  19.6 1.4 %collective-permute-start.14 = (f32[144,128]{1,0:T(8,128)S(1)}, f32[144,128]{1,0:T(8,128)S(1)}, u32[]{:S(2)}, u32[]{:S(2)}) collective-permute-start(f32[144,128]{1,0:T(8,128)S(1)} %get-tuple-element.54), channel_id=1, source_target_pairs={{0,3},{1,0},{2,1},{3,2},{4,7},{5,4},{6,5},{7,6},{8,9},{9,10},{10,1... | collective-permute-start | bytes 221192 | tf_op jit(solution)/shard_map/ppermute | solution.py:111
  21.0 0.5 %collective-permute-start.22 = (f32[128,128]{1,0:T(8,128)S(1)}, f32[128,128]{1,0:T(8,128)S(1)}, u32[]{:S(2)}, u32[]{:S(2)}) collective-permute-start(f32[128,128]{1,0:T(8,128)S(1)} %get-tuple-element.57.gram), channel_id=1, source_target_pairs={{0,1},{1,0},{2,3},{3,2},{4,5},{5,4},{6,7},{7,6},{8,9},{9,8},{10,11... | collective-permute-start | bytes 196616 | tf_op jit(solution)/shard_map/ppermute | solution.py:101
  21.5 0.1 collective-permute-done.16.refs_3_
  21.6 0.7 %collective-permute-done.15.refs_2_ = f32[144,128]{1,0:T(8,128)S(1)} collective-permute-done((f32[144,128]{1,0:T(8,128)S(1)}, f32[144,128]{1,0:T(8,128)S(1)}, u32[]{:S(2)}, u32[]{:S(2)}) %collective-permute-start.15) | collective-permute-done | bytes 73760 | tf_op jit(solution)/shard_map/ppermute | solution.py:111
  22.3 0.7 %collective-permute-done.14.refs_1_ = f32[144,128]{1,0:T(8,128)S(1)} collective-permute-done((f32[144,128]{1,0:T(8,128)S(1)}, f32[144,128]{1,0:T(8,128)S(1)}, u32[]{:S(2)}, u32[]{:S(2)}) %collective-permute-start.14) | collective-permute-done | bytes 73760 | tf_op jit(solution)/shard_map/ppermute | solution.py:111
  23.0 1.0 %collective-permute-start.20 = (f32[128,128]{1,0:T(8,128)S(1)}, f32[128,128]{1,0:T(8,128)S(1)}, u32[]{:S(2)}, u32[]{:S(2)}) collective-permute-start(f32[128,128]{1,0:T(8,128)S(1)} %get-tuple-element.55), channel_id=1, source_target_pairs={{0,1},{1,20},{2,3},{3,22},{4,5},{5,16},{6,7},{7,18},{8,29},{9,8},{... | collective-permute-start | bytes 196616 | tf_op jit(solution)/shard_map/ppermute | solution.py:111
  24.0 1.6 %collective-permute-start.19 = (f32[128,128]{1,0:T(8,128)S(1)}, f32[128,128]{1,0:T(8,128)S(1)}, u32[]{:S(2)}, u32[]{:S(2)}) collective-permute-start(f32[128,128]{1,0:T(8,128)S(1)} %get-tuple-element.55), channel_id=1, source_target_pairs={{0,1},{1,16},{2,3},{3,18},{4,5},{5,20},{6,7},{7,22},{8,25},{9,8},{... | collective-permute-start | bytes 196616 | tf_op jit(solution)/shard_map/ppermute | solution.py:111
  25.5 0.6 %collective-permute-start.18 = (f32[128,128]{1,0:T(8,128)S(1)}, f32[128,128]{1,0:T(8,128)S(1)}, u32[]{:S(2)}, u32[]{:S(2)}) collective-permute-start(f32[128,128]{1,0:T(8,128)S(1)} %get-tuple-element.55), channel_id=1, source_target_pairs={{0,1},{1,4},{2,3},{3,6},{4,5},{5,0},{6,7},{7,2},{8,13},{9,8},{10,1... | collective-permute-start | bytes 196616 | tf_op jit(solution)/shard_map/ppermute | solution.py:111
  26.1 0.1 collective-permute-start.17
  26.2 0.4 %collective-permute-start.21 = (f32[32,128]{1,0:T(8,128)S(1)}, f32[32,128]{1,0:T(8,128)S(1)}, u32[]{:S(2)}, u32[]{:S(2)}) collective-permute-start(f32[32,128]{1,0:T(8,128)S(1)} %get-tuple-element.56.rows), channel_id=1, source_target_pairs={{0,1},{1,0},{2,3},{3,2},{4,5},{5,4},{6,7},{7,6},{8,9},{9,8},{10,11... | collective-permute-start | bytes 49160 | tf_op jit(solution)/shard_map/ppermute | solution.py:101
  26.6 0.7 %shard_map.91 = (f32[128,128]{1,0:T(8,128)}, f32[1,128]{1,0:T(1,128)S(1)}, f32[128,128]{1,0:T(8,128)S(1)}) custom-call(f32[128,128]{1,0:T(8,128)S(1)} %get-tuple-element.57.gram, f32[128,128]{1,0:T(8,128)S(1)} %collective-permute-done.22.mate_gram, f32[128,128]{1,0:T(8,128)S(1)} %get-tuple-element.53.refs_2_.moved, ...), custom_call_target="tpu_custom_call" | custom-call | flops 131072 | bytes 65536 | tf_op jit(solution)/shard_map/pallas_call | solution.py:63
  27.3 0.2 collective-permute-done.21.mate_rows
  27.5 0.9 %shard_map.92 = (f32[8,128]{1,0:T(8,128)}, f32[128,128]{1,0:T(8,128)S(1)}, f32[1,128]{1,0:T(1,128)S(1)}, f32[1,128]{1,0:T(1,128)S(1)}) custom-call(f32[32,128]{1,0:T(8,128)S(1)} %get-tuple-element.56.rows, f32[32,128]{1,0:T(8,128)S(1)} %collective-permute-done.21.mate_rows, f32[128,128]{1,0:T(8,128)S(1)} %get-tuple-element.42.c, ...), custom_call_target="tpu_custom_call" | custom-call | flops 16777216 | bytes 65536 | tf_op jit(solution)/shard_map/pallas_call | solution.py:63
  28.3 0.2 collective-permute-done.20
  28.5 0.7 %collective-permute-done.19 = f32[128,128]{1,0:T(8,128)S(1)} collective-permute-done((f32[128,128]{1,0:T(8,128)S(1)}, f32[128,128]{1,0:T(8,128)S(1)}, u32[]{:S(2)}, u32[]{:S(2)}) %collective-permute-start.19) | collective-permute-done | bytes 65568 | tf_op jit(solution)/shard_map/ppermute | solution.py:111
  29.3 0.1 collective-permute-start.23
  29.4 0.7 %shard_map.93 = (f32[128,128]{1,0:T(8,128)}, f32[1,128]{1,0:T(1,128)}) custom-call(f32[128,128]{1,0:T(8,128)S(1)} %add_add_fusion.refs_0_, f32[128,128]{1,0:T(8,128)S(1)} %get-tuple-element.69.refs_1_.refs_3_, f32[1,128]{1,0:T(1,128)S(1)} %get-tuple-element.70.refs_2_.refs_4_, f32[1,128]{1,0:T(1,128)S(1)} %get-tuple-element.71.refs_3_.refs_5_), custom_call_target="tpu_custom_call" | custom-call | flops 131072 | bytes 65536 | tf_op jit(solution)/shard_map/pallas_call | solution.py:63
  30.1 0.5 %collective-permute-done.23.refs_2_ = f32[128,128]{1,0:T(8,128)S(1)} collective-permute-done((f32[128,128]{1,0:T(8,128)S(1)}, f32[128,128]{1,0:T(8,128)S(1)}, u32[]{:S(2)}, u32[]{:S(2)}) %collective-permute-start.23) | collective-permute-done | bytes 65568 | tf_op jit(solution)/shard_map/ppermute | solution.py:101
  (23 shorter events, 0.1 us)
Async XLA Ops:
  1.9 1.4 %collective-permute-start = (f32[72,128]{1,0:T(8,128)S(1)}, f32[72,128]{1,0:T(8,128)S(1)}, u32[]{:S(2)}, u32[]{:S(2)}) collective-permute-start(f32[72,128]{1,0:T(8,128)S(1)} %get-tuple-element.40.opened), channel_id=1, source_target_pairs={{0,1},{1,0},{2,3},{3,2},{4,5},{5,4},{6,7},{7,6},{8,9},{9,8},{10,11... | collective-permute-start | bytes 110600 | tf_op jit(solution)/shard_map/ppermute | solution.py:101
  2.6 1.3 %collective-permute-start.2 = (f32[64,128]{1,0:T(8,128)S(1)}, f32[64,128]{1,0:T(8,128)S(1)}, u32[]{:S(2)}, u32[]{:S(2)}) collective-permute-start(f32[64,128]{1,0:T(8,128)S(1)} %get-tuple-element.45), channel_id=1, source_target_pairs={{0,1},{1,0},{2,3},{3,2},{4,5},{5,4},{6,7},{7,6},{8,9},{9,8},{10,11... | collective-permute-start | bytes 98312 | tf_op jit(solution)/shard_map/ppermute | solution.py:101
  2.8 5.4 %collective-permute-start.5 = (f32[1024,128]{1,0:T(8,128)S(1)}, f32[1024,128]{1,0:T(8,128)S(1)}, u32[]{:S(2)}, u32[]{:S(2)}) collective-permute-start(f32[1024,128]{1,0:T(8,128)S(1)} %get-tuple-element.50.x.refs_0_), channel_id=1, source_target_pairs={{0,1},{1,0},{2,3},{3,2},{4,5},{5,4},{6,7},{7,6},{8,9},{9,8},{10,11... | collective-permute-start | bytes 1572872 | tf_op jit(solution)/shard_map/ppermute | solution.py:101
  3.2 5.0 %collective-permute-start.4 = (f32[8,128,128]{2,1,0:T(8,128)S(1)}, f32[8,128,128]{2,1,0:T(8,128)S(1)}, u32[]{:S(2)}, u32[]{:S(2)}) collective-permute-start(f32[8,128,128]{2,1,0:T(8,128)S(1)} %get-tuple-element.49.refs_6_), channel_id=1, source_target_pairs={{0,1},{1,0},{2,3},{3,2},{4,5},{5,4},{6,7},{7,6},{8,9},{9,8},{10,11... | collective-permute-start | bytes 1572872 | tf_op jit(solution)/shard_map/ppermute | solution.py:101
  3.3 4.8 %collective-permute-start.1 = (f32[80,128]{1,0:T(8,128)S(1)}, f32[80,128]{1,0:T(8,128)S(1)}, u32[]{:S(2)}, u32[]{:S(2)}) collective-permute-start(f32[80,128]{1,0:T(8,128)S(1)} %pad_maximum_fusion), channel_id=1, source_target_pairs={{0,1},{1,2},{2,3},{3,0},{4,5},{5,6},{6,7},{7,4},{8,11},{9,8},{10,9... | collective-permute-start | bytes 122888 | tf_op jit(solution)/shard_map/ppermute | solution.py:111
  3.9 4.2 %collective-permute-start.3 = (f32[64,128]{1,0:T(8,128)S(1)}, f32[64,128]{1,0:T(8,128)S(1)}, u32[]{:S(2)}, u32[]{:S(2)}) collective-permute-start(f32[64,128]{1,0:T(8,128)S(1)} %add.35), channel_id=1, source_target_pairs={{0,1},{1,2},{2,3},{3,0},{4,5},{5,6},{6,7},{7,4},{8,11},{9,8},{10,9... | collective-permute-start | bytes 98312 | tf_op jit(solution)/shard_map/ppermute | solution.py:111
  9.0 3.9 %collective-permute-start.9 = (f32[88,128]{1,0:T(8,128)S(1)}, f32[88,128]{1,0:T(8,128)S(1)}, u32[]{:S(2)}, u32[]{:S(2)}) collective-permute-start(f32[88,128]{1,0:T(8,128)S(1)} %get-tuple-element.51), channel_id=1, source_target_pairs={{0,21},{1,0},{2,23},{3,2},{4,17},{5,4},{6,19},{7,6},{8,9},{9,28},{... | collective-permute-start | bytes 135176 | tf_op jit(solution)/shard_map/ppermute | solution.py:111
  11.1 2.7 %collective-permute-start.8 = (f32[88,128]{1,0:T(8,128)S(1)}, f32[88,128]{1,0:T(8,128)S(1)}, u32[]{:S(2)}, u32[]{:S(2)}) collective-permute-start(f32[88,128]{1,0:T(8,128)S(1)} %get-tuple-element.51), channel_id=1, source_target_pairs={{0,17},{1,0},{2,19},{3,2},{4,21},{5,4},{6,23},{7,6},{8,9},{9,24},{... | collective-permute-start | bytes 135176 | tf_op jit(solution)/shard_map/ppermute | solution.py:111
  12.2 1.7 %collective-permute-start.7 = (f32[88,128]{1,0:T(8,128)S(1)}, f32[88,128]{1,0:T(8,128)S(1)}, u32[]{:S(2)}, u32[]{:S(2)}) collective-permute-start(f32[88,128]{1,0:T(8,128)S(1)} %get-tuple-element.51), channel_id=1, source_target_pairs={{0,5},{1,0},{2,7},{3,2},{4,1},{5,4},{6,3},{7,6},{8,9},{9,12},{10,1... | collective-permute-start | bytes 135176 | tf_op jit(solution)/shard_map/ppermute | solution.py:111
  12.2 1.7 %collective-permute-start.6 = (f32[88,128]{1,0:T(8,128)S(1)}, f32[88,128]{1,0:T(8,128)S(1)}, u32[]{:S(2)}, u32[]{:S(2)}) collective-permute-start(f32[88,128]{1,0:T(8,128)S(1)} %get-tuple-element.51), channel_id=1, source_target_pairs={{0,1},{1,0},{2,3},{3,2},{4,5},{5,4},{6,7},{7,6},{8,9},{9,8},{10,11... | collective-permute-start | bytes 135176 | tf_op jit(solution)/shard_map/ppermute | solution.py:101
  12.7 3.0 %collective-permute-start.12 = (f32[128,128]{1,0:T(8,128)S(1)}, f32[128,128]{1,0:T(8,128)S(1)}, u32[]{:S(2)}, u32[]{:S(2)}) collective-permute-start(f32[128,128]{1,0:T(8,128)S(1)} %get-tuple-element.53.refs_2_.moved), channel_id=1, source_target_pairs={{0,1},{1,0},{2,3},{3,2},{4,5},{5,4},{6,7},{7,6},{8,9},{9,8},{10,11... | collective-permute-start | bytes 196616 | tf_op jit(solution)/shard_map/ppermute | solution.py:101
  13.9 5.2 %collective-permute-start.11 = (f32[88,128]{1,0:T(8,128)S(1)}, f32[88,128]{1,0:T(8,128)S(1)}, u32[]{:S(2)}, u32[]{:S(2)}) collective-permute-start(f32[88,128]{1,0:T(8,128)S(1)} %add_add_fusion.1), channel_id=1, source_target_pairs={{0,1},{1,9},{2,3},{3,11},{4,5},{5,13},{6,7},{7,15},{8,0},{9,8},{10... | collective-permute-start | bytes 135176 | tf_op jit(solution)/shard_map/ppermute | solution.py:111
  15.6 3.5 %collective-permute-start.10 = (f32[88,128]{1,0:T(8,128)S(1)}, f32[88,128]{1,0:T(8,128)S(1)}, u32[]{:S(2)}, u32[]{:S(2)}) collective-permute-start(f32[88,128]{1,0:T(8,128)S(1)} %add_add_fusion.1), channel_id=1, source_target_pairs={{0,1},{1,0},{2,3},{3,2},{4,5},{5,4},{6,7},{7,6},{8,9},{9,8},{10,11... | collective-permute-start | bytes 135176 | tf_op jit(solution)/shard_map/ppermute | solution.py:101
  19.5 2.1 %collective-permute-start.16 = (f32[144,128]{1,0:T(8,128)S(1)}, f32[144,128]{1,0:T(8,128)S(1)}, u32[]{:S(2)}, u32[]{:S(2)}) collective-permute-start(f32[144,128]{1,0:T(8,128)S(1)} %get-tuple-element.54), channel_id=1, source_target_pairs={{0,10},{1,0},{2,8},{3,2},{4,14},{5,4},{6,12},{7,6},{8,9},{9,3},{10... | collective-permute-start | bytes 221192 | tf_op jit(solution)/shard_map/ppermute | solution.py:111
  19.6 2.7 %collective-permute-start.15 = (f32[144,128]{1,0:T(8,128)S(1)}, f32[144,128]{1,0:T(8,128)S(1)}, u32[]{:S(2)}, u32[]{:S(2)}) collective-permute-start(f32[144,128]{1,0:T(8,128)S(1)} %get-tuple-element.54), channel_id=1, source_target_pairs={{0,8},{1,0},{2,10},{3,2},{4,12},{5,4},{6,14},{7,6},{8,9},{9,1},{10... | collective-permute-start | bytes 221192 | tf_op jit(solution)/shard_map/ppermute | solution.py:111
  19.6 3.4 %collective-permute-start.14 = (f32[144,128]{1,0:T(8,128)S(1)}, f32[144,128]{1,0:T(8,128)S(1)}, u32[]{:S(2)}, u32[]{:S(2)}) collective-permute-start(f32[144,128]{1,0:T(8,128)S(1)} %get-tuple-element.54), channel_id=1, source_target_pairs={{0,3},{1,0},{2,1},{3,2},{4,7},{5,4},{6,5},{7,6},{8,9},{9,10},{10,1... | collective-permute-start | bytes 221192 | tf_op jit(solution)/shard_map/ppermute | solution.py:111
  21.0 2.0 %collective-permute-start.13 = (f32[144,128]{1,0:T(8,128)S(1)}, f32[144,128]{1,0:T(8,128)S(1)}, u32[]{:S(2)}, u32[]{:S(2)}) collective-permute-start(f32[144,128]{1,0:T(8,128)S(1)} %get-tuple-element.54), channel_id=1, source_target_pairs={{0,1},{1,0},{2,3},{3,2},{4,5},{5,4},{6,7},{7,6},{8,9},{9,8},{10,11... | collective-permute-start | bytes 221192 | tf_op jit(solution)/shard_map/ppermute | solution.py:101
  21.0 5.2 %collective-permute-start.22 = (f32[128,128]{1,0:T(8,128)S(1)}, f32[128,128]{1,0:T(8,128)S(1)}, u32[]{:S(2)}, u32[]{:S(2)}) collective-permute-start(f32[128,128]{1,0:T(8,128)S(1)} %get-tuple-element.57.gram), channel_id=1, source_target_pairs={{0,1},{1,0},{2,3},{3,2},{4,5},{5,4},{6,7},{7,6},{8,9},{9,8},{10,11... | collective-permute-start | bytes 196616 | tf_op jit(solution)/shard_map/ppermute | solution.py:101
  23.0 5.5 %collective-permute-start.20 = (f32[128,128]{1,0:T(8,128)S(1)}, f32[128,128]{1,0:T(8,128)S(1)}, u32[]{:S(2)}, u32[]{:S(2)}) collective-permute-start(f32[128,128]{1,0:T(8,128)S(1)} %get-tuple-element.55), channel_id=1, source_target_pairs={{0,1},{1,20},{2,3},{3,22},{4,5},{5,16},{6,7},{7,18},{8,29},{9,8},{... | collective-permute-start | bytes 196616 | tf_op jit(solution)/shard_map/ppermute | solution.py:111
  24.0 5.3 %collective-permute-start.19 = (f32[128,128]{1,0:T(8,128)S(1)}, f32[128,128]{1,0:T(8,128)S(1)}, u32[]{:S(2)}, u32[]{:S(2)}) collective-permute-start(f32[128,128]{1,0:T(8,128)S(1)} %get-tuple-element.55), channel_id=1, source_target_pairs={{0,1},{1,16},{2,3},{3,18},{4,5},{5,20},{6,7},{7,22},{8,25},{9,8},{... | collective-permute-start | bytes 196616 | tf_op jit(solution)/shard_map/ppermute | solution.py:111
  25.5 3.7 %collective-permute-start.18 = (f32[128,128]{1,0:T(8,128)S(1)}, f32[128,128]{1,0:T(8,128)S(1)}, u32[]{:S(2)}, u32[]{:S(2)}) collective-permute-start(f32[128,128]{1,0:T(8,128)S(1)} %get-tuple-element.55), channel_id=1, source_target_pairs={{0,1},{1,4},{2,3},{3,6},{4,5},{5,0},{6,7},{7,2},{8,13},{9,8},{10,1... | collective-permute-start | bytes 196616 | tf_op jit(solution)/shard_map/ppermute | solution.py:111
  26.1 3.2 %collective-permute-start.17 = (f32[128,128]{1,0:T(8,128)S(1)}, f32[128,128]{1,0:T(8,128)S(1)}, u32[]{:S(2)}, u32[]{:S(2)}) collective-permute-start(f32[128,128]{1,0:T(8,128)S(1)} %get-tuple-element.55), channel_id=1, source_target_pairs={{0,1},{1,0},{2,3},{3,2},{4,5},{5,4},{6,7},{7,6},{8,9},{9,8},{10,11... | collective-permute-start | bytes 196616 | tf_op jit(solution)/shard_map/ppermute | solution.py:101
  26.2 1.2 %collective-permute-start.21 = (f32[32,128]{1,0:T(8,128)S(1)}, f32[32,128]{1,0:T(8,128)S(1)}, u32[]{:S(2)}, u32[]{:S(2)}) collective-permute-start(f32[32,128]{1,0:T(8,128)S(1)} %get-tuple-element.56.rows), channel_id=1, source_target_pairs={{0,1},{1,0},{2,3},{3,2},{4,5},{5,4},{6,7},{7,6},{8,9},{9,8},{10,11... | collective-permute-start | bytes 49160 | tf_op jit(solution)/shard_map/ppermute | solution.py:101
  29.3 1.3 %collective-permute-start.23 = (f32[128,128]{1,0:T(8,128)S(1)}, f32[128,128]{1,0:T(8,128)S(1)}, u32[]{:S(2)}, u32[]{:S(2)}) collective-permute-start(f32[128,128]{1,0:T(8,128)S(1)} %add_add_fusion.refs_0_), channel_id=1, source_target_pairs={{0,1},{1,0},{2,3},{3,2},{4,5},{5,4},{6,7},{7,6},{8,9},{9,8},{10,11... | collective-permute-start | bytes 196616 | tf_op jit(solution)/shard_map/ppermute | solution.py:101

commit v29 on v28

--- a/solution.py
+++ b/solution.py
@@ -26,8 +26,12 @@
     return product[:, :width] + product[:, width:]
 
 
+def dot_halves(parts, b):
+    return fold(jnp.dot(parts, both(b), preferred_element_type=F32))
+
+
 def dot(a, b):
-    return fold(jnp.dot(halves(a, 1), both(b), preferred_element_type=F32))
+    return dot_halves(halves(a, 1), b)
 
 
 def dot_rows(a, b):
@@ -225,7 +229,7 @@
         aliases={3: 1},
     )
 
-    def weigh_kernel(a_hbm, w_hbm, c, a, w, outer, outer_c, sems):
+    def weigh_kernel(a_hbm, w_hbm, c, a, w, outer, outer_c, a_parts, sems):
         copies = [pltpu.make_async_copy(w_hbm, w, sems.at[0]), pltpu.make_async_copy(a_hbm, a, sems.at[1])]
         for copy in copies:
             copy.start()
@@ -235,10 +239,17 @@
         outer[...] = squared
         outer_c[...] = squared * gram
         copies[1].wait()
-
-    a_near, w_row, outer, outer_c = call(
+        a_parts[...] = halves(a[...], 1)
+
+    a_near, w_row, outer, outer_c, a_parts = call(
         weigh_kernel,
-        (near(vox_rows, rank), near(1, rank), near(rank, rank), near(rank, rank)),
+        (
+            near(vox_rows, rank),
+            near(1, rank),
+            near(rank, rank),
+            near(rank, rank),
+            pltpu.VMEM((vox_rows, 2 * rank), BF16),
+        ),
         (voxel_factor, weights.reshape(1, rank), c_near),
         2 * rank * rank * times * 4,
         scratch=(pltpu.SemaphoreType.DMA((2,)),),
@@ -266,12 +277,12 @@
 
     half, sums_rows = rank // 2, rank // 2 + chip_rows
 
-    def voxel_kernel(terms, late_terms, rows, a, w, outer_c, con, mate_con, mate_x, moved_out, chip_b, out, all_b):
+    def voxel_kernel(terms, late_terms, rows, a, a_parts, w, outer_c, con, mate_con, mate_x, moved_out, chip_b, out, all_b):
         b = in_order(rows, all_b, chips, lax.axis_index("vox") // 2 & 1)
         chip_b[...] = all_b[pl.ds(pl.multiple_of(smp_index() // 2 * chip_rows, chip_rows), chip_rows), :]
         coupled = outer_c[...] * dot_rows(b, b)
         terms = jnp.concatenate([terms[...], late_terms[...]], axis=0)
-        moved = a[...] - step_of(coupled) * (dot(a[...], coupled) - terms * w[...])
+        moved = a[...] - step_of(coupled) * (dot_halves(a_parts[...], coupled) - terms * w[...])
         moved_out[...] = moved
         packed, diagonal = pack(dot_rows(moved, moved))
         out[:half, :] = packed
@@ -285,7 +296,7 @@
     moved_a, chip_b, sums = call(
         only_on(voxel_role, voxel_kernel),
         (near(vox_rows, rank), near(chip_rows, rank), near(sums_rows + 8, rank)),
-        (terms, late_terms, rows_b, a_near, w_row, outer_c, con, mate_con, mate_x),
+        (terms, late_terms, rows_b, a_near, a_parts, w_row, outer_c, con, mate_con, mate_x),
         2 * rank * rank * vox_rows * 12,
         scratch=(near(smp_total, rank),),
     )

time: 31.2 us -> 31.2 us (level)
  no operation moved by 1% of the time
where the time goes in v29:
time: 31.2 us; the launch traced here: 30.6 us
  starting transfers between devices  15.4 us (49%)
  waiting for transfers between devices  8.07 us (26%)
  Pallas kernels  6.26 us (20%)
  between operations  0.79 us (3%)
    ppermute x12, starting transfers between devices, send(): return lax.ppermute(values, ALL, pairs)  12.6 us
    ppermute x12, waiting for transfers between devices, send(): return lax.ppermute(values, ALL, pairs)  7.28 us
    pallas_call x11, Pallas kernels, call(): pl.pallas_call(kernel, out_shape=outs, in_specs=specs, out_specs=[pl.Bloc...  6.26 us
    ppermute x12, starting transfers between devices, swap(): lax.ppermute(values, ALL, [(i, i ^ 1) for i in range(lax.axis_size(ALL))])  2.85 us
    ppermute x12, waiting for transfers between devices, swap(): lax.ppermute(values, ALL, [(i, i ^ 1) for i in range(lax.axis_size(ALL))])  0.79 us
  transfers between devices with their start and end apart: 24, of which 12 were waited for; matrix products, arithmetic and copies ran while one was open for 0% of the time, Pallas kernels for 13%

profile of v29, /device:TPU:0, one launch (start us, length us, event | category | flops | bytes accessed | tf_op | source)
XLA Modules:
  0.0 30.6 jit_solution(11731269404492931819)
XLA Ops:
  0.6 1.2 %shard_map.84 = (f32[1024,128]{1,0:T(8,128)S(1)}, f32[128,128]{1,0:T(8,128)S(1)}, f32[72,128]{1,0:T(8,128)S(1)}, f32[8,128,128]{2,1,0:T(8,128)S(1)}) custom-call(f32[1024,128]{1,0:T(8,128)} %bitcast.3, f32[128,128]{1,0:T(8,128)} %c_hbm.1, f32[8,128]{1,0:T(8,128)} %b_hbm.1), custom_call_target="tpu_custom_call" | custom-call | flops 67108864 | bytes 65536 | tf_op jit(solution)/shard_map/pallas_call | solution.py:67
  1.9 0.5 %collective-permute-start = (f32[72,128]{1,0:T(8,128)S(1)}, f32[72,128]{1,0:T(8,128)S(1)}, u32[]{:S(2)}, u32[]{:S(2)}) collective-permute-start(f32[72,128]{1,0:T(8,128)S(1)} %get-tuple-element.41.opened), channel_id=1, source_target_pairs={{0,1},{1,0},{2,3},{3,2},{4,5},{5,4},{6,7},{7,6},{8,9},{9,8},{10,11... | collective-permute-start | bytes 110600 | tf_op jit(solution)/shard_map/ppermute | solution.py:105
  2.4 0.2 shard_map.85
  2.6 0.1 collective-permute-start.2
  2.8 0.5 %collective-permute-start.5 = (f32[1024,128]{1,0:T(8,128)S(1)}, f32[1024,128]{1,0:T(8,128)S(1)}, u32[]{:S(2)}, u32[]{:S(2)}) collective-permute-start(f32[1024,128]{1,0:T(8,128)S(1)} %get-tuple-element.52.x.refs_0_), channel_id=1, source_target_pairs={{0,1},{1,0},{2,3},{3,2},{4,5},{5,4},{6,7},{7,6},{8,9},{9,8},{10,11... | collective-permute-start | bytes 1572872 | tf_op jit(solution)/shard_map/ppermute | solution.py:105
  3.2 0.1 collective-permute-start.4
  3.3 0.0 collective-permute-done
  3.3 0.5 %collective-permute-start.1 = (f32[80,128]{1,0:T(8,128)S(1)}, f32[80,128]{1,0:T(8,128)S(1)}, u32[]{:S(2)}, u32[]{:S(2)}) collective-permute-start(f32[80,128]{1,0:T(8,128)S(1)} %pad_maximum_fusion), channel_id=1, source_target_pairs={{0,1},{1,2},{2,3},{3,0},{4,5},{5,6},{6,7},{7,4},{8,11},{9,8},{10,9... | collective-permute-start | bytes 122888 | tf_op jit(solution)/shard_map/ppermute | solution.py:115
  3.8 0.1 collective-permute-done.2
  3.9 2.6 %collective-permute-start.3 = (f32[64,128]{1,0:T(8,128)S(1)}, f32[64,128]{1,0:T(8,128)S(1)}, u32[]{:S(2)}, u32[]{:S(2)}) collective-permute-start(f32[64,128]{1,0:T(8,128)S(1)} %add.35), channel_id=1, source_target_pairs={{0,1},{1,2},{2,3},{3,0},{4,5},{5,6},{6,7},{7,4},{8,11},{9,8},{10,9... | collective-permute-start | bytes 98312 | tf_op jit(solution)/shard_map/ppermute | solution.py:115
  6.5 0.9 %shard_map.86 = (f32[128,128]{1,0:T(8,128)S(1)}, f32[1,128]{1,0:T(1,128)S(1)}, f32[128,128]{1,0:T(8,128)S(1)}, f32[128,128]{1,0:T(8,128)S(1)}, bf16[128,256]{1,0:T(8,128)(2,1)S(1)}) custom-call(f32[128,128]{1,0:T(8,128)} %a_hbm.1, f32[1,128]{1,0:T(1,128)} %bitcast.4, f32[128,128]{1,0:T(8,128)S(1)} %get-tuple-element.43.c), custom_call_target="tpu_custom_call" | custom-call | flops 16777216 | bytes 65536 | tf_op jit(solution)/shard_map/pallas_call | solution.py:67
  7.4 0.7 %collective-permute-done.3 = f32[64,128]{1,0:T(8,128)S(1)} collective-permute-done((f32[64,128]{1,0:T(8,128)S(1)}, f32[64,128]{1,0:T(8,128)S(1)}, u32[]{:S(2)}, u32[]{:S(2)}) %collective-permute-start.3) | collective-permute-done | bytes 32800 | tf_op jit(solution)/shard_map/ppermute | solution.py:115
  8.2 0.0 collective-permute-done.1
  8.2 0.0 collective-permute-done.5.refs_9_.refs_1_
  8.2 0.7 %shard_map.87 = (f32[128,128]{1,0:T(8,128)S(1)}, f32[16,128]{1,0:T(8,128)S(1)}, f32[88,128]{1,0:T(8,128)S(1)}) custom-call(f32[64,128]{1,0:T(8,128)S(1)} %slice_add_fusion.refs_0_, f32[64,128]{1,0:T(8,128)S(1)} %add.36.refs_1_, f32[32,128]{1,0:T(8,128)S(1)} %pad_maximum_fusion.1.refs_2_, f32[128,128]{1,0:T(8,128)S(1)} %get-tuple-element.47.refs_3_, ...), custom_call_target="tpu_custom_call" | custom-call | flops 50331648 | bytes 65536 | tf_op jit(solution)/shard_map/pallas_call | solution.py:67
  9.0 2.2 %collective-permute-start.9 = (f32[88,128]{1,0:T(8,128)S(1)}, f32[88,128]{1,0:T(8,128)S(1)}, u32[]{:S(2)}, u32[]{:S(2)}) collective-permute-start(f32[88,128]{1,0:T(8,128)S(1)} %get-tuple-element.53), channel_id=1, source_target_pairs={{0,21},{1,0},{2,23},{3,2},{4,17},{5,4},{6,19},{7,6},{8,9},{9,28},{... | collective-permute-start | bytes 135176 | tf_op jit(solution)/shard_map/ppermute | solution.py:115
  11.1 1.0 %collective-permute-start.8 = (f32[88,128]{1,0:T(8,128)S(1)}, f32[88,128]{1,0:T(8,128)S(1)}, u32[]{:S(2)}, u32[]{:S(2)}) collective-permute-start(f32[88,128]{1,0:T(8,128)S(1)} %get-tuple-element.53), channel_id=1, source_target_pairs={{0,17},{1,0},{2,19},{3,2},{4,21},{5,4},{6,23},{7,6},{8,9},{9,24},{... | collective-permute-start | bytes 135176 | tf_op jit(solution)/shard_map/ppermute | solution.py:115
  12.2 0.0 collective-permute-start.7
  12.2 0.5 %collective-permute-start.6 = (f32[88,128]{1,0:T(8,128)S(1)}, f32[88,128]{1,0:T(8,128)S(1)}, u32[]{:S(2)}, u32[]{:S(2)}) collective-permute-start(f32[88,128]{1,0:T(8,128)S(1)} %get-tuple-element.53), channel_id=1, source_target_pairs={{0,1},{1,0},{2,3},{3,2},{4,5},{5,4},{6,7},{7,6},{8,9},{9,8},{10,11... | collective-permute-start | bytes 135176 | tf_op jit(solution)/shard_map/ppermute | solution.py:105
  12.7 0.2 collective-permute-done.9
  12.8 1.0 %collective-permute-done.8 = f32[88,128]{1,0:T(8,128)S(1)} collective-permute-done((f32[88,128]{1,0:T(8,128)S(1)}, f32[88,128]{1,0:T(8,128)S(1)}, u32[]{:S(2)}, u32[]{:S(2)}) %collective-permute-start.8) | collective-permute-done | bytes 45088 | tf_op jit(solution)/shard_map/ppermute | solution.py:115
  13.9 0.0 collective-permute-done.7
  13.9 0.0 collective-permute-done.6
  13.9 1.7 %collective-permute-start.11 = (f32[88,128]{1,0:T(8,128)S(1)}, f32[88,128]{1,0:T(8,128)S(1)}, u32[]{:S(2)}, u32[]{:S(2)}) collective-permute-start(f32[88,128]{1,0:T(8,128)S(1)} %add_add_fusion.1), channel_id=1, source_target_pairs={{0,1},{1,9},{2,3},{3,11},{4,5},{5,13},{6,7},{7,15},{8,0},{9,8},{10... | collective-permute-start | bytes 135176 | tf_op jit(solution)/shard_map/ppermute | solution.py:115
  15.6 0.1 collective-permute-start.10
  15.7 0.5 %shard_map.88.refs_4_ = f32[16,128,128]{2,1,0:T(8,128)S(1)} custom-call(f32[1024,128]{1,0:T(8,128)S(1)} %get-tuple-element.52.x.refs_0_, f32[1024,128]{1,0:T(8,128)S(1)} %collective-permute-done.5.refs_9_.refs_1_, f32[128,128]{1,0:T(8,128)S(1)} %get-tuple-element.55.refs_2_.moved, f32[128,128]{1,0:T(8,128)S(1)} %collective-permute-done.12.refs_3_.mate_moved), custom_call_target="tpu_custom_call" | custom-call | flops 402653184 | bytes 65536 | tf_op jit(solution)/shard_map/pallas_call | solution.py:67
  16.2 2.9 %collective-permute-done.11 = f32[88,128]{1,0:T(8,128)S(1)} collective-permute-done((f32[88,128]{1,0:T(8,128)S(1)}, f32[88,128]{1,0:T(8,128)S(1)}, u32[]{:S(2)}, u32[]{:S(2)}) %collective-permute-start.11) | collective-permute-done | bytes 45088 | tf_op jit(solution)/shard_map/ppermute | solution.py:115
  19.1 0.4 %shard_map.89 = (f32[128,128]{1,0:T(8,128)S(1)}, f32[144,128]{1,0:T(8,128)S(1)}) custom-call(f32[88,128]{1,0:T(8,128)S(1)} %add.40.refs_0_, f32[16,128]{1,0:T(8,128)S(1)} %get-tuple-element.54.refs_1_, f32[1,128]{1,0:T(1,128)S(1)} %get-tuple-element.49.refs_5_.refs_2_.w, f32[128,128]{1,0:T(8,128)S(1)} %get-tuple-element.50.refs_6_.refs_3_, ...), custom_call_target="tpu_custom_call" | custom-call | flops 3145728 | bytes 65536 | tf_op jit(solution)/shard_map/pallas_call | solution.py:67
  19.5 0.1 collective-permute-start.16
  19.6 0.0 collective-permute-start.15
  19.6 1.4 %collective-permute-start.14 = (f32[144,128]{1,0:T(8,128)S(1)}, f32[144,128]{1,0:T(8,128)S(1)}, u32[]{:S(2)}, u32[]{:S(2)}) collective-permute-start(f32[144,128]{1,0:T(8,128)S(1)} %get-tuple-element.56), channel_id=1, source_target_pairs={{0,3},{1,0},{2,1},{3,2},{4,7},{5,4},{6,5},{7,6},{8,9},{9,10},{10,1... | collective-permute-start | bytes 221192 | tf_op jit(solution)/shard_map/ppermute | solution.py:115
  21.0 0.5 %collective-permute-start.22 = (f32[128,128]{1,0:T(8,128)S(1)}, f32[128,128]{1,0:T(8,128)S(1)}, u32[]{:S(2)}, u32[]{:S(2)}) collective-permute-start(f32[128,128]{1,0:T(8,128)S(1)} %get-tuple-element.59.gram), channel_id=1, source_target_pairs={{0,1},{1,0},{2,3},{3,2},{4,5},{5,4},{6,7},{7,6},{8,9},{9,8},{10,11... | collective-permute-start | bytes 196616 | tf_op jit(solution)/shard_map/ppermute | solution.py:105
  21.5 0.1 collective-permute-done.16.refs_3_
  21.6 0.7 %collective-permute-done.15.refs_2_ = f32[144,128]{1,0:T(8,128)S(1)} collective-permute-done((f32[144,128]{1,0:T(8,128)S(1)}, f32[144,128]{1,0:T(8,128)S(1)}, u32[]{:S(2)}, u32[]{:S(2)}) %collective-permute-start.15) | collective-permute-done | bytes 73760 | tf_op jit(solution)/shard_map/ppermute | solution.py:115
  22.3 0.7 %collective-permute-done.14.refs_1_ = f32[144,128]{1,0:T(8,128)S(1)} collective-permute-done((f32[144,128]{1,0:T(8,128)S(1)}, f32[144,128]{1,0:T(8,128)S(1)}, u32[]{:S(2)}, u32[]{:S(2)}) %collective-permute-start.14) | collective-permute-done | bytes 73760 | tf_op jit(solution)/shard_map/ppermute | solution.py:115
  23.0 1.0 %collective-permute-start.20 = (f32[128,128]{1,0:T(8,128)S(1)}, f32[128,128]{1,0:T(8,128)S(1)}, u32[]{:S(2)}, u32[]{:S(2)}) collective-permute-start(f32[128,128]{1,0:T(8,128)S(1)} %get-tuple-element.57), channel_id=1, source_target_pairs={{0,1},{1,20},{2,3},{3,22},{4,5},{5,16},{6,7},{7,18},{8,29},{9,8},{... | collective-permute-start | bytes 196616 | tf_op jit(solution)/shard_map/ppermute | solution.py:115
  24.0 1.6 %collective-permute-start.19 = (f32[128,128]{1,0:T(8,128)S(1)}, f32[128,128]{1,0:T(8,128)S(1)}, u32[]{:S(2)}, u32[]{:S(2)}) collective-permute-start(f32[128,128]{1,0:T(8,128)S(1)} %get-tuple-element.57), channel_id=1, source_target_pairs={{0,1},{1,16},{2,3},{3,18},{4,5},{5,20},{6,7},{7,22},{8,25},{9,8},{... | collective-permute-start | bytes 196616 | tf_op jit(solution)/shard_map/ppermute | solution.py:115
  25.5 0.6 %collective-permute-start.18 = (f32[128,128]{1,0:T(8,128)S(1)}, f32[128,128]{1,0:T(8,128)S(1)}, u32[]{:S(2)}, u32[]{:S(2)}) collective-permute-start(f32[128,128]{1,0:T(8,128)S(1)} %get-tuple-element.57), channel_id=1, source_target_pairs={{0,1},{1,4},{2,3},{3,6},{4,5},{5,0},{6,7},{7,2},{8,13},{9,8},{10,1... | collective-permute-start | bytes 196616 | tf_op jit(solution)/shard_map/ppermute | solution.py:115
  26.1 0.1 collective-permute-start.17
  26.2 0.4 %collective-permute-start.21 = (f32[32,128]{1,0:T(8,128)S(1)}, f32[32,128]{1,0:T(8,128)S(1)}, u32[]{:S(2)}, u32[]{:S(2)}) collective-permute-start(f32[32,128]{1,0:T(8,128)S(1)} %get-tuple-element.58.rows), channel_id=1, source_target_pairs={{0,1},{1,0},{2,3},{3,2},{4,5},{5,4},{6,7},{7,6},{8,9},{9,8},{10,11... | collective-permute-start | bytes 49160 | tf_op jit(solution)/shard_map/ppermute | solution.py:105
  26.6 0.7 %shard_map.91 = (f32[128,128]{1,0:T(8,128)}, f32[1,128]{1,0:T(1,128)S(1)}, f32[128,128]{1,0:T(8,128)S(1)}) custom-call(f32[128,128]{1,0:T(8,128)S(1)} %get-tuple-element.59.gram, f32[128,128]{1,0:T(8,128)S(1)} %collective-permute-done.22.mate_gram, f32[128,128]{1,0:T(8,128)S(1)} %get-tuple-element.55.refs_2_.moved, ...), custom_call_target="tpu_custom_call" | custom-call | flops 131072 | bytes 65536 | tf_op jit(solution)/shard_map/pallas_call | solution.py:67
  27.3 0.2 collective-permute-done.21.mate_rows
  27.5 0.9 %shard_map.92 = (f32[8,128]{1,0:T(8,128)}, f32[128,128]{1,0:T(8,128)S(1)}, f32[1,128]{1,0:T(1,128)S(1)}, f32[1,128]{1,0:T(1,128)S(1)}) custom-call(f32[32,128]{1,0:T(8,128)S(1)} %get-tuple-element.58.rows, f32[32,128]{1,0:T(8,128)S(1)} %collective-permute-done.21.mate_rows, f32[128,128]{1,0:T(8,128)S(1)} %get-tuple-element.43.c, ...), custom_call_target="tpu_custom_call" | custom-call | flops 16777216 | bytes 65536 | tf_op jit(solution)/shard_map/pallas_call | solution.py:67
  28.3 0.2 collective-permute-done.20
  28.5 0.7 %collective-permute-done.19 = f32[128,128]{1,0:T(8,128)S(1)} collective-permute-done((f32[128,128]{1,0:T(8,128)S(1)}, f32[128,128]{1,0:T(8,128)S(1)}, u32[]{:S(2)}, u32[]{:S(2)}) %collective-permute-start.19) | collective-permute-done | bytes 65568 | tf_op jit(solution)/shard_map/ppermute | solution.py:115
  29.3 0.1 collective-permute-start.23
  29.4 0.7 %shard_map.93 = (f32[128,128]{1,0:T(8,128)}, f32[1,128]{1,0:T(1,128)}) custom-call(f32[128,128]{1,0:T(8,128)S(1)} %add_add_fusion.refs_0_, f32[128,128]{1,0:T(8,128)S(1)} %get-tuple-element.71.refs_1_.refs_3_, f32[1,128]{1,0:T(1,128)S(1)} %get-tuple-element.72.refs_2_.refs_4_, f32[1,128]{1,0:T(1,128)S(1)} %get-tuple-element.73.refs_3_.refs_5_), custom_call_target="tpu_custom_call" | custom-call | flops 131072 | bytes 65536 | tf_op jit(solution)/shard_map/pallas_call | solution.py:67
  30.1 0.5 %collective-permute-done.23.refs_2_ = f32[128,128]{1,0:T(8,128)S(1)} collective-permute-done((f32[128,128]{1,0:T(8,128)S(1)}, f32[128,128]{1,0:T(8,128)S(1)}, u32[]{:S(2)}, u32[]{:S(2)}) %collective-permute-start.23) | collective-permute-done | bytes 65568 | tf_op jit(solution)/shard_map/ppermute | solution.py:105
  (23 shorter events, 0.1 us)
Async XLA Ops:
  1.9 1.4 %collective-permute-start = (f32[72,128]{1,0:T(8,128)S(1)}, f32[72,128]{1,0:T(8,128)S(1)}, u32[]{:S(2)}, u32[]{:S(2)}) collective-permute-start(f32[72,128]{1,0:T(8,128)S(1)} %get-tuple-element.41.opened), channel_id=1, source_target_pairs={{0,1},{1,0},{2,3},{3,2},{4,5},{5,4},{6,7},{7,6},{8,9},{9,8},{10,11... | collective-permute-start | bytes 110600 | tf_op jit(solution)/shard_map/ppermute | solution.py:105
  2.6 1.3 %collective-permute-start.2 = (f32[64,128]{1,0:T(8,128)S(1)}, f32[64,128]{1,0:T(8,128)S(1)}, u32[]{:S(2)}, u32[]{:S(2)}) collective-permute-start(f32[64,128]{1,0:T(8,128)S(1)} %get-tuple-element.46), channel_id=1, source_target_pairs={{0,1},{1,0},{2,3},{3,2},{4,5},{5,4},{6,7},{7,6},{8,9},{9,8},{10,11... | collective-permute-start | bytes 98312 | tf_op jit(solution)/shard_map/ppermute | solution.py:105
  2.8 5.4 %collective-permute-start.5 = (f32[1024,128]{1,0:T(8,128)S(1)}, f32[1024,128]{1,0:T(8,128)S(1)}, u32[]{:S(2)}, u32[]{:S(2)}) collective-permute-start(f32[1024,128]{1,0:T(8,128)S(1)} %get-tuple-element.52.x.refs_0_), channel_id=1, source_target_pairs={{0,1},{1,0},{2,3},{3,2},{4,5},{5,4},{6,7},{7,6},{8,9},{9,8},{10,11... | collective-permute-start | bytes 1572872 | tf_op jit(solution)/shard_map/ppermute | solution.py:105
  3.2 5.0 %collective-permute-start.4 = (f32[8,128,128]{2,1,0:T(8,128)S(1)}, f32[8,128,128]{2,1,0:T(8,128)S(1)}, u32[]{:S(2)}, u32[]{:S(2)}) collective-permute-start(f32[8,128,128]{2,1,0:T(8,128)S(1)} %get-tuple-element.51.refs_7_), channel_id=1, source_target_pairs={{0,1},{1,0},{2,3},{3,2},{4,5},{5,4},{6,7},{7,6},{8,9},{9,8},{10,11... | collective-permute-start | bytes 1572872 | tf_op jit(solution)/shard_map/ppermute | solution.py:105
  3.3 4.8 %collective-permute-start.1 = (f32[80,128]{1,0:T(8,128)S(1)}, f32[80,128]{1,0:T(8,128)S(1)}, u32[]{:S(2)}, u32[]{:S(2)}) collective-permute-start(f32[80,128]{1,0:T(8,128)S(1)} %pad_maximum_fusion), channel_id=1, source_target_pairs={{0,1},{1,2},{2,3},{3,0},{4,5},{5,6},{6,7},{7,4},{8,11},{9,8},{10,9... | collective-permute-start | bytes 122888 | tf_op jit(solution)/shard_map/ppermute | solution.py:115
  3.9 4.2 %collective-permute-start.3 = (f32[64,128]{1,0:T(8,128)S(1)}, f32[64,128]{1,0:T(8,128)S(1)}, u32[]{:S(2)}, u32[]{:S(2)}) collective-permute-start(f32[64,128]{1,0:T(8,128)S(1)} %add.35), channel_id=1, source_target_pairs={{0,1},{1,2},{2,3},{3,0},{4,5},{5,6},{6,7},{7,4},{8,11},{9,8},{10,9... | collective-permute-start | bytes 98312 | tf_op jit(solution)/shard_map/ppermute | solution.py:115
  9.0 3.9 %collective-permute-start.9 = (f32[88,128]{1,0:T(8,128)S(1)}, f32[88,128]{1,0:T(8,128)S(1)}, u32[]{:S(2)}, u32[]{:S(2)}) collective-permute-start(f32[88,128]{1,0:T(8,128)S(1)} %get-tuple-element.53), channel_id=1, source_target_pairs={{0,21},{1,0},{2,23},{3,2},{4,17},{5,4},{6,19},{7,6},{8,9},{9,28},{... | collective-permute-start | bytes 135176 | tf_op jit(solution)/shard_map/ppermute | solution.py:115
  11.1 2.7 %collective-permute-start.8 = (f32[88,128]{1,0:T(8,128)S(1)}, f32[88,128]{1,0:T(8,128)S(1)}, u32[]{:S(2)}, u32[]{:S(2)}) collective-permute-start(f32[88,128]{1,0:T(8,128)S(1)} %get-tuple-element.53), channel_id=1, source_target_pairs={{0,17},{1,0},{2,19},{3,2},{4,21},{5,4},{6,23},{7,6},{8,9},{9,24},{... | collective-permute-start | bytes 135176 | tf_op jit(solution)/shard_map/ppermute | solution.py:115
  12.2 1.7 %collective-permute-start.7 = (f32[88,128]{1,0:T(8,128)S(1)}, f32[88,128]{1,0:T(8,128)S(1)}, u32[]{:S(2)}, u32[]{:S(2)}) collective-permute-start(f32[88,128]{1,0:T(8,128)S(1)} %get-tuple-element.53), channel_id=1, source_target_pairs={{0,5},{1,0},{2,7},{3,2},{4,1},{5,4},{6,3},{7,6},{8,9},{9,12},{10,1... | collective-permute-start | bytes 135176 | tf_op jit(solution)/shard_map/ppermute | solution.py:115
  12.2 1.7 %collective-permute-start.6 = (f32[88,128]{1,0:T(8,128)S(1)}, f32[88,128]{1,0:T(8,128)S(1)}, u32[]{:S(2)}, u32[]{:S(2)}) collective-permute-start(f32[88,128]{1,0:T(8,128)S(1)} %get-tuple-element.53), channel_id=1, source_target_pairs={{0,1},{1,0},{2,3},{3,2},{4,5},{5,4},{6,7},{7,6},{8,9},{9,8},{10,11... | collective-permute-start | bytes 135176 | tf_op jit(solution)/shard_map/ppermute | solution.py:105
  12.7 3.0 %collective-permute-start.12 = (f32[128,128]{1,0:T(8,128)S(1)}, f32[128,128]{1,0:T(8,128)S(1)}, u32[]{:S(2)}, u32[]{:S(2)}) collective-permute-start(f32[128,128]{1,0:T(8,128)S(1)} %get-tuple-element.55.refs_2_.moved), channel_id=1, source_target_pairs={{0,1},{1,0},{2,3},{3,2},{4,5},{5,4},{6,7},{7,6},{8,9},{9,8},{10,11... | collective-permute-start | bytes 196616 | tf_op jit(solution)/shard_map/ppermute | solution.py:105
  13.9 5.2 %collective-permute-start.11 = (f32[88,128]{1,0:T(8,128)S(1)}, f32[88,128]{1,0:T(8,128)S(1)}, u32[]{:S(2)}, u32[]{:S(2)}) collective-permute-start(f32[88,128]{1,0:T(8,128)S(1)} %add_add_fusion.1), channel_id=1, source_target_pairs={{0,1},{1,9},{2,3},{3,11},{4,5},{5,13},{6,7},{7,15},{8,0},{9,8},{10... | collective-permute-start | bytes 135176 | tf_op jit(solution)/shard_map/ppermute | solution.py:115
  15.6 3.5 %collective-permute-start.10 = (f32[88,128]{1,0:T(8,128)S(1)}, f32[88,128]{1,0:T(8,128)S(1)}, u32[]{:S(2)}, u32[]{:S(2)}) collective-permute-start(f32[88,128]{1,0:T(8,128)S(1)} %add_add_fusion.1), channel_id=1, source_target_pairs={{0,1},{1,0},{2,3},{3,2},{4,5},{5,4},{6,7},{7,6},{8,9},{9,8},{10,11... | collective-permute-start | bytes 135176 | tf_op jit(solution)/shard_map/ppermute | solution.py:105
  19.5 2.1 %collective-permute-start.16 = (f32[144,128]{1,0:T(8,128)S(1)}, f32[144,128]{1,0:T(8,128)S(1)}, u32[]{:S(2)}, u32[]{:S(2)}) collective-permute-start(f32[144,128]{1,0:T(8,128)S(1)} %get-tuple-element.56), channel_id=1, source_target_pairs={{0,10},{1,0},{2,8},{3,2},{4,14},{5,4},{6,12},{7,6},{8,9},{9,3},{10... | collective-permute-start | bytes 221192 | tf_op jit(solution)/shard_map/ppermute | solution.py:115
  19.6 2.7 %collective-permute-start.15 = (f32[144,128]{1,0:T(8,128)S(1)}, f32[144,128]{1,0:T(8,128)S(1)}, u32[]{:S(2)}, u32[]{:S(2)}) collective-permute-start(f32[144,128]{1,0:T(8,128)S(1)} %get-tuple-element.56), channel_id=1, source_target_pairs={{0,8},{1,0},{2,10},{3,2},{4,12},{5,4},{6,14},{7,6},{8,9},{9,1},{10... | collective-permute-start | bytes 221192 | tf_op jit(solution)/shard_map/ppermute | solution.py:115
  19.6 3.4 %collective-permute-start.14 = (f32[144,128]{1,0:T(8,128)S(1)}, f32[144,128]{1,0:T(8,128)S(1)}, u32[]{:S(2)}, u32[]{:S(2)}) collective-permute-start(f32[144,128]{1,0:T(8,128)S(1)} %get-tuple-element.56), channel_id=1, source_target_pairs={{0,3},{1,0},{2,1},{3,2},{4,7},{5,4},{6,5},{7,6},{8,9},{9,10},{10,1... | collective-permute-start | bytes 221192 | tf_op jit(solution)/shard_map/ppermute | solution.py:115
  21.0 2.0 %collective-permute-start.13 = (f32[144,128]{1,0:T(8,128)S(1)}, f32[144,128]{1,0:T(8,128)S(1)}, u32[]{:S(2)}, u32[]{:S(2)}) collective-permute-start(f32[144,128]{1,0:T(8,128)S(1)} %get-tuple-element.56), channel_id=1, source_target_pairs={{0,1},{1,0},{2,3},{3,2},{4,5},{5,4},{6,7},{7,6},{8,9},{9,8},{10,11... | collective-permute-start | bytes 221192 | tf_op jit(solution)/shard_map/ppermute | solution.py:105
  21.0 5.2 %collective-permute-start.22 = (f32[128,128]{1,0:T(8,128)S(1)}, f32[128,128]{1,0:T(8,128)S(1)}, u32[]{:S(2)}, u32[]{:S(2)}) collective-permute-start(f32[128,128]{1,0:T(8,128)S(1)} %get-tuple-element.59.gram), channel_id=1, source_target_pairs={{0,1},{1,0},{2,3},{3,2},{4,5},{5,4},{6,7},{7,6},{8,9},{9,8},{10,11... | collective-permute-start | bytes 196616 | tf_op jit(solution)/shard_map/ppermute | solution.py:105
  23.0 5.5 %collective-permute-start.20 = (f32[128,128]{1,0:T(8,128)S(1)}, f32[128,128]{1,0:T(8,128)S(1)}, u32[]{:S(2)}, u32[]{:S(2)}) collective-permute-start(f32[128,128]{1,0:T(8,128)S(1)} %get-tuple-element.57), channel_id=1, source_target_pairs={{0,1},{1,20},{2,3},{3,22},{4,5},{5,16},{6,7},{7,18},{8,29},{9,8},{... | collective-permute-start | bytes 196616 | tf_op jit(solution)/shard_map/ppermute | solution.py:115
  24.0 5.3 %collective-permute-start.19 = (f32[128,128]{1,0:T(8,128)S(1)}, f32[128,128]{1,0:T(8,128)S(1)}, u32[]{:S(2)}, u32[]{:S(2)}) collective-permute-start(f32[128,128]{1,0:T(8,128)S(1)} %get-tuple-element.57), channel_id=1, source_target_pairs={{0,1},{1,16},{2,3},{3,18},{4,5},{5,20},{6,7},{7,22},{8,25},{9,8},{... | collective-permute-start | bytes 196616 | tf_op jit(solution)/shard_map/ppermute | solution.py:115
  25.5 3.7 %collective-permute-start.18 = (f32[128,128]{1,0:T(8,128)S(1)}, f32[128,128]{1,0:T(8,128)S(1)}, u32[]{:S(2)}, u32[]{:S(2)}) collective-permute-start(f32[128,128]{1,0:T(8,128)S(1)} %get-tuple-element.57), channel_id=1, source_target_pairs={{0,1},{1,4},{2,3},{3,6},{4,5},{5,0},{6,7},{7,2},{8,13},{9,8},{10,1... | collective-permute-start | bytes 196616 | tf_op jit(solution)/shard_map/ppermute | solution.py:115
  26.1 3.2 %collective-permute-start.17 = (f32[128,128]{1,0:T(8,128)S(1)}, f32[128,128]{1,0:T(8,128)S(1)}, u32[]{:S(2)}, u32[]{:S(2)}) collective-permute-start(f32[128,128]{1,0:T(8,128)S(1)} %get-tuple-element.57), channel_id=1, source_target_pairs={{0,1},{1,0},{2,3},{3,2},{4,5},{5,4},{6,7},{7,6},{8,9},{9,8},{10,11... | collective-permute-start | bytes 196616 | tf_op jit(solution)/shard_map/ppermute | solution.py:105
  26.2 1.2 %collective-permute-start.21 = (f32[32,128]{1,0:T(8,128)S(1)}, f32[32,128]{1,0:T(8,128)S(1)}, u32[]{:S(2)}, u32[]{:S(2)}) collective-permute-start(f32[32,128]{1,0:T(8,128)S(1)} %get-tuple-element.58.rows), channel_id=1, source_target_pairs={{0,1},{1,0},{2,3},{3,2},{4,5},{5,4},{6,7},{7,6},{8,9},{9,8},{10,11... | collective-permute-start | bytes 49160 | tf_op jit(solution)/shard_map/ppermute | solution.py:105
  29.3 1.3 %collective-permute-start.23 = (f32[128,128]{1,0:T(8,128)S(1)}, f32[128,128]{1,0:T(8,128)S(1)}, u32[]{:S(2)}, u32[]{:S(2)}) collective-permute-start(f32[128,128]{1,0:T(8,128)S(1)} %add_add_fusion.refs_0_), channel_id=1, source_target_pairs={{0,1},{1,0},{2,3},{3,2},{4,5},{5,4},{6,7},{7,6},{8,9},{9,8},{10,11... | collective-permute-start | bytes 196616 | tf_op jit(solution)/shard_map/ppermute | solution.py:105

commit v30 on v28

--- a/solution.py
+++ b/solution.py
@@ -402,11 +402,14 @@
     def finish(terms, base, gain, scale, c_out, w_out, c, w, sems):
         moved = base[...] + terms[...] * gain[...]
         scales_c = jnp.sqrt(jnp.sum(moved * moved, axis=0, keepdims=True) / times + 1e-06)
-        c[...] = moved / scales_c
         w[...] = scale[...] * scales_c
-        copies = [pltpu.make_async_copy(c, c_out, sems.at[0]), pltpu.make_async_copy(w, w_out, sems.at[1])]
-        for copy in copies:
-            copy.start()
+        copies = [pltpu.make_async_copy(w, w_out, sems.at[0])]
+        copies[0].start()
+        for n in range(2):
+            rows = pl.ds(n * (times // 2), times // 2)
+            c[rows, :] = moved[n * (times // 2) : (n + 1) * (times // 2), :] / scales_c
+            copies.append(pltpu.make_async_copy(c.at[rows, :], c_out.at[rows, :], sems.at[1 + n]))
+            copies[-1].start()
         for copy in copies:
             copy.wait()
 
@@ -414,7 +417,7 @@
         finish(*refs)
 
     results = (far(times, rank), far(1, rank))
-    scratch = (near(times, rank), near(1, rank), pltpu.SemaphoreType.DMA((2,)))
+    scratch = (near(times, rank), near(1, rank), pltpu.SemaphoreType.DMA((3,)))
     held = call(
         only_on(last_role, finish),
         results,

time: 31.2 us -> 31.2 us (level)
  no operation moved by 1% of the time
where the time goes in v30:
time: 31.2 us; the launch traced here: 30.6 us
  starting transfers between devices  15.4 us (49%)
  waiting for transfers between devices  8.08 us (26%)
  Pallas kernels  6.27 us (20%)
  between operations  0.79 us (3%)
    ppermute x12, starting transfers between devices, send(): return lax.ppermute(values, ALL, pairs)  12.6 us
    ppermute x12, waiting for transfers between devices, send(): return lax.ppermute(values, ALL, pairs)  7.29 us
    pallas_call x11, Pallas kernels, call(): pl.pallas_call(kernel, out_shape=outs, in_specs=specs, out_specs=[pl.Bloc...  6.27 us
    ppermute x12, starting transfers between devices, swap(): lax.ppermute(values, ALL, [(i, i ^ 1) for i in range(lax.axis_size(ALL))])  2.85 us
    ppermute x12, waiting for transfers between devices, swap(): lax.ppermute(values, ALL, [(i, i ^ 1) for i in range(lax.axis_size(ALL))])  0.79 us
  transfers between devices with their start and end apart: 24, of which 12 were waited for; matrix products, arithmetic and copies ran while one was open for 0% of the time, Pallas kernels for 13%

profile of v30, /device:TPU:0, one launch (start us, length us, event | category | flops | bytes accessed | tf_op | source)
XLA Modules:
  0.0 30.6 jit_solution(310819448323202770)
XLA Ops:
  0.6 1.2 %shard_map.84 = (f32[1024,128]{1,0:T(8,128)S(1)}, f32[128,128]{1,0:T(8,128)S(1)}, f32[72,128]{1,0:T(8,128)S(1)}, f32[8,128,128]{2,1,0:T(8,128)S(1)}) custom-call(f32[1024,128]{1,0:T(8,128)} %bitcast.3, f32[128,128]{1,0:T(8,128)} %c_hbm.1, f32[8,128]{1,0:T(8,128)} %b_hbm.1), custom_call_target="tpu_custom_call" | custom-call | flops 67108864 | bytes 65536 | tf_op jit(solution)/shard_map/pallas_call | solution.py:63
  1.9 0.5 %collective-permute-start = (f32[72,128]{1,0:T(8,128)S(1)}, f32[72,128]{1,0:T(8,128)S(1)}, u32[]{:S(2)}, u32[]{:S(2)}) collective-permute-start(f32[72,128]{1,0:T(8,128)S(1)} %get-tuple-element.40.opened), channel_id=1, source_target_pairs={{0,1},{1,0},{2,3},{3,2},{4,5},{5,4},{6,7},{7,6},{8,9},{9,8},{10,11... | collective-permute-start | bytes 110600 | tf_op jit(solution)/shard_map/ppermute | solution.py:101
  2.4 0.2 shard_map.85
  2.6 0.1 collective-permute-start.2
  2.8 0.5 %collective-permute-start.5 = (f32[1024,128]{1,0:T(8,128)S(1)}, f32[1024,128]{1,0:T(8,128)S(1)}, u32[]{:S(2)}, u32[]{:S(2)}) collective-permute-start(f32[1024,128]{1,0:T(8,128)S(1)} %get-tuple-element.50.x.refs_0_), channel_id=1, source_target_pairs={{0,1},{1,0},{2,3},{3,2},{4,5},{5,4},{6,7},{7,6},{8,9},{9,8},{10,11... | collective-permute-start | bytes 1572872 | tf_op jit(solution)/shard_map/ppermute | solution.py:101
  3.2 0.1 collective-permute-start.4
  3.3 0.5 %collective-permute-start.1 = (f32[80,128]{1,0:T(8,128)S(1)}, f32[80,128]{1,0:T(8,128)S(1)}, u32[]{:S(2)}, u32[]{:S(2)}) collective-permute-start(f32[80,128]{1,0:T(8,128)S(1)} %pad_maximum_fusion), channel_id=1, source_target_pairs={{0,1},{1,2},{2,3},{3,0},{4,5},{5,6},{6,7},{7,4},{8,11},{9,8},{10,9... | collective-permute-start | bytes 122888 | tf_op jit(solution)/shard_map/ppermute | solution.py:111
  3.8 0.1 collective-permute-done.2
  3.9 2.6 %collective-permute-start.3 = (f32[64,128]{1,0:T(8,128)S(1)}, f32[64,128]{1,0:T(8,128)S(1)}, u32[]{:S(2)}, u32[]{:S(2)}) collective-permute-start(f32[64,128]{1,0:T(8,128)S(1)} %add.35), channel_id=1, source_target_pairs={{0,1},{1,2},{2,3},{3,0},{4,5},{5,6},{6,7},{7,4},{8,11},{9,8},{10,9... | collective-permute-start | bytes 98312 | tf_op jit(solution)/shard_map/ppermute | solution.py:111
  6.5 0.9 %shard_map.86 = (f32[128,128]{1,0:T(8,128)S(1)}, f32[1,128]{1,0:T(1,128)S(1)}, f32[128,128]{1,0:T(8,128)S(1)}, f32[128,128]{1,0:T(8,128)S(1)}) custom-call(f32[128,128]{1,0:T(8,128)} %a_hbm.1, f32[1,128]{1,0:T(1,128)} %bitcast.4, f32[128,128]{1,0:T(8,128)S(1)} %get-tuple-element.42.c), custom_call_target="tpu_custom_call" | custom-call | flops 16777216 | bytes 65536 | tf_op jit(solution)/shard_map/pallas_call | solution.py:63
  7.4 0.7 %collective-permute-done.3 = f32[64,128]{1,0:T(8,128)S(1)} collective-permute-done((f32[64,128]{1,0:T(8,128)S(1)}, f32[64,128]{1,0:T(8,128)S(1)}, u32[]{:S(2)}, u32[]{:S(2)}) %collective-permute-start.3) | collective-permute-done | bytes 32800 | tf_op jit(solution)/shard_map/ppermute | solution.py:111
  8.2 0.0 collective-permute-done.4.refs_7_
  8.2 0.7 %shard_map.87 = (f32[128,128]{1,0:T(8,128)S(1)}, f32[16,128]{1,0:T(8,128)S(1)}, f32[88,128]{1,0:T(8,128)S(1)}) custom-call(f32[64,128]{1,0:T(8,128)S(1)} %slice_add_fusion.refs_0_, f32[64,128]{1,0:T(8,128)S(1)} %add.36.refs_1_, f32[32,128]{1,0:T(8,128)S(1)} %pad_maximum_fusion.1.refs_2_, f32[128,128]{1,0:T(8,128)S(1)} %get-tuple-element.46.refs_3_, ...), custom_call_target="tpu_custom_call" | custom-call | flops 50331648 | bytes 65536 | tf_op jit(solution)/shard_map/pallas_call | solution.py:63
  9.0 2.2 %collective-permute-start.9 = (f32[88,128]{1,0:T(8,128)S(1)}, f32[88,128]{1,0:T(8,128)S(1)}, u32[]{:S(2)}, u32[]{:S(2)}) collective-permute-start(f32[88,128]{1,0:T(8,128)S(1)} %get-tuple-element.51), channel_id=1, source_target_pairs={{0,21},{1,0},{2,23},{3,2},{4,17},{5,4},{6,19},{7,6},{8,9},{9,28},{... | collective-permute-start | bytes 135176 | tf_op jit(solution)/shard_map/ppermute | solution.py:111
  11.1 1.0 %collective-permute-start.8 = (f32[88,128]{1,0:T(8,128)S(1)}, f32[88,128]{1,0:T(8,128)S(1)}, u32[]{:S(2)}, u32[]{:S(2)}) collective-permute-start(f32[88,128]{1,0:T(8,128)S(1)} %get-tuple-element.51), channel_id=1, source_target_pairs={{0,17},{1,0},{2,19},{3,2},{4,21},{5,4},{6,23},{7,6},{8,9},{9,24},{... | collective-permute-start | bytes 135176 | tf_op jit(solution)/shard_map/ppermute | solution.py:111
  12.2 0.0 collective-permute-start.7
  12.2 0.5 %collective-permute-start.6 = (f32[88,128]{1,0:T(8,128)S(1)}, f32[88,128]{1,0:T(8,128)S(1)}, u32[]{:S(2)}, u32[]{:S(2)}) collective-permute-start(f32[88,128]{1,0:T(8,128)S(1)} %get-tuple-element.51), channel_id=1, source_target_pairs={{0,1},{1,0},{2,3},{3,2},{4,5},{5,4},{6,7},{7,6},{8,9},{9,8},{10,11... | collective-permute-start | bytes 135176 | tf_op jit(solution)/shard_map/ppermute | solution.py:101
  12.7 0.2 collective-permute-done.9
  12.8 1.0 %collective-permute-done.8 = f32[88,128]{1,0:T(8,128)S(1)} collective-permute-done((f32[88,128]{1,0:T(8,128)S(1)}, f32[88,128]{1,0:T(8,128)S(1)}, u32[]{:S(2)}, u32[]{:S(2)}) %collective-permute-start.8) | collective-permute-done | bytes 45088 | tf_op jit(solution)/shard_map/ppermute | solution.py:111
  13.9 0.0 collective-permute-done.7
  13.9 0.0 collective-permute-done.6
  13.9 1.7 %collective-permute-start.11 = (f32[88,128]{1,0:T(8,128)S(1)}, f32[88,128]{1,0:T(8,128)S(1)}, u32[]{:S(2)}, u32[]{:S(2)}) collective-permute-start(f32[88,128]{1,0:T(8,128)S(1)} %add_add_fusion.1), channel_id=1, source_target_pairs={{0,1},{1,9},{2,3},{3,11},{4,5},{5,13},{6,7},{7,15},{8,0},{9,8},{10... | collective-permute-start | bytes 135176 | tf_op jit(solution)/shard_map/ppermute | solution.py:111
  15.6 0.1 collective-permute-start.10
  15.7 0.0 collective-permute-done.12.refs_3_.mate_moved
  15.7 0.5 %shard_map.88.refs_4_ = f32[16,128,128]{2,1,0:T(8,128)S(1)} custom-call(f32[1024,128]{1,0:T(8,128)S(1)} %get-tuple-element.50.x.refs_0_, f32[1024,128]{1,0:T(8,128)S(1)} %collective-permute-done.5.refs_8_.refs_1_, f32[128,128]{1,0:T(8,128)S(1)} %get-tuple-element.53.refs_2_.moved, f32[128,128]{1,0:T(8,128)S(1)} %collective-permute-done.12.refs_3_.mate_moved), custom_call_target="tpu_custom_call" | custom-call | flops 402653184 | bytes 65536 | tf_op jit(solution)/shard_map/pallas_call | solution.py:63
  16.2 2.9 %collective-permute-done.11 = f32[88,128]{1,0:T(8,128)S(1)} collective-permute-done((f32[88,128]{1,0:T(8,128)S(1)}, f32[88,128]{1,0:T(8,128)S(1)}, u32[]{:S(2)}, u32[]{:S(2)}) %collective-permute-start.11) | collective-permute-done | bytes 45088 | tf_op jit(solution)/shard_map/ppermute | solution.py:111
  19.1 0.4 %shard_map.89 = (f32[128,128]{1,0:T(8,128)S(1)}, f32[144,128]{1,0:T(8,128)S(1)}) custom-call(f32[88,128]{1,0:T(8,128)S(1)} %add.40.refs_0_, f32[16,128]{1,0:T(8,128)S(1)} %get-tuple-element.52.refs_1_, f32[1,128]{1,0:T(1,128)S(1)} %get-tuple-element.47.refs_4_.refs_2_.w, f32[128,128]{1,0:T(8,128)S(1)} %get-tuple-element.48.refs_5_.refs_3_, ...), custom_call_target="tpu_custom_call" | custom-call | flops 3145728 | bytes 65536 | tf_op jit(solution)/shard_map/pallas_call | solution.py:63
  19.5 0.1 collective-permute-start.16
  19.6 0.0 collective-permute-start.15
  19.6 1.4 %collective-permute-start.14 = (f32[144,128]{1,0:T(8,128)S(1)}, f32[144,128]{1,0:T(8,128)S(1)}, u32[]{:S(2)}, u32[]{:S(2)}) collective-permute-start(f32[144,128]{1,0:T(8,128)S(1)} %get-tuple-element.54), channel_id=1, source_target_pairs={{0,3},{1,0},{2,1},{3,2},{4,7},{5,4},{6,5},{7,6},{8,9},{9,10},{10,1... | collective-permute-start | bytes 221192 | tf_op jit(solution)/shard_map/ppermute | solution.py:111
  21.0 0.5 %collective-permute-start.22 = (f32[128,128]{1,0:T(8,128)S(1)}, f32[128,128]{1,0:T(8,128)S(1)}, u32[]{:S(2)}, u32[]{:S(2)}) collective-permute-start(f32[128,128]{1,0:T(8,128)S(1)} %get-tuple-element.57.gram), channel_id=1, source_target_pairs={{0,1},{1,0},{2,3},{3,2},{4,5},{5,4},{6,7},{7,6},{8,9},{9,8},{10,11... | collective-permute-start | bytes 196616 | tf_op jit(solution)/shard_map/ppermute | solution.py:101
  21.5 0.1 collective-permute-done.16.refs_3_
  21.6 0.7 %collective-permute-done.15.refs_2_ = f32[144,128]{1,0:T(8,128)S(1)} collective-permute-done((f32[144,128]{1,0:T(8,128)S(1)}, f32[144,128]{1,0:T(8,128)S(1)}, u32[]{:S(2)}, u32[]{:S(2)}) %collective-permute-start.15) | collective-permute-done | bytes 73760 | tf_op jit(solution)/shard_map/ppermute | solution.py:111
  22.3 0.7 %collective-permute-done.14.refs_1_ = f32[144,128]{1,0:T(8,128)S(1)} collective-permute-done((f32[144,128]{1,0:T(8,128)S(1)}, f32[144,128]{1,0:T(8,128)S(1)}, u32[]{:S(2)}, u32[]{:S(2)}) %collective-permute-start.14) | collective-permute-done | bytes 73760 | tf_op jit(solution)/shard_map/ppermute | solution.py:111
  23.0 1.0 %collective-permute-start.20 = (f32[128,128]{1,0:T(8,128)S(1)}, f32[128,128]{1,0:T(8,128)S(1)}, u32[]{:S(2)}, u32[]{:S(2)}) collective-permute-start(f32[128,128]{1,0:T(8,128)S(1)} %get-tuple-element.55), channel_id=1, source_target_pairs={{0,1},{1,20},{2,3},{3,22},{4,5},{5,16},{6,7},{7,18},{8,29},{9,8},{... | collective-permute-start | bytes 196616 | tf_op jit(solution)/shard_map/ppermute | solution.py:111
  24.0 1.6 %collective-permute-start.19 = (f32[128,128]{1,0:T(8,128)S(1)}, f32[128,128]{1,0:T(8,128)S(1)}, u32[]{:S(2)}, u32[]{:S(2)}) collective-permute-start(f32[128,128]{1,0:T(8,128)S(1)} %get-tuple-element.55), channel_id=1, source_target_pairs={{0,1},{1,16},{2,3},{3,18},{4,5},{5,20},{6,7},{7,22},{8,25},{9,8},{... | collective-permute-start | bytes 196616 | tf_op jit(solution)/shard_map/ppermute | solution.py:111
  25.5 0.6 %collective-permute-start.18 = (f32[128,128]{1,0:T(8,128)S(1)}, f32[128,128]{1,0:T(8,128)S(1)}, u32[]{:S(2)}, u32[]{:S(2)}) collective-permute-start(f32[128,128]{1,0:T(8,128)S(1)} %get-tuple-element.55), channel_id=1, source_target_pairs={{0,1},{1,4},{2,3},{3,6},{4,5},{5,0},{6,7},{7,2},{8,13},{9,8},{10,1... | collective-permute-start | bytes 196616 | tf_op jit(solution)/shard_map/ppermute | solution.py:111
  26.1 0.1 collective-permute-start.17
  26.2 0.0 collective-permute-done.22.mate_gram
  26.2 0.4 %collective-permute-start.21 = (f32[32,128]{1,0:T(8,128)S(1)}, f32[32,128]{1,0:T(8,128)S(1)}, u32[]{:S(2)}, u32[]{:S(2)}) collective-permute-start(f32[32,128]{1,0:T(8,128)S(1)} %get-tuple-element.56.rows), channel_id=1, source_target_pairs={{0,1},{1,0},{2,3},{3,2},{4,5},{5,4},{6,7},{7,6},{8,9},{9,8},{10,11... | collective-permute-start | bytes 49160 | tf_op jit(solution)/shard_map/ppermute | solution.py:101
  26.6 0.7 %shard_map.91 = (f32[128,128]{1,0:T(8,128)}, f32[1,128]{1,0:T(1,128)S(1)}, f32[128,128]{1,0:T(8,128)S(1)}) custom-call(f32[128,128]{1,0:T(8,128)S(1)} %get-tuple-element.57.gram, f32[128,128]{1,0:T(8,128)S(1)} %collective-permute-done.22.mate_gram, f32[128,128]{1,0:T(8,128)S(1)} %get-tuple-element.53.refs_2_.moved, ...), custom_call_target="tpu_custom_call" | custom-call | flops 131072 | bytes 65536 | tf_op jit(solution)/shard_map/pallas_call | solution.py:63
  27.3 0.2 collective-permute-done.21.mate_rows
  27.5 0.9 %shard_map.92 = (f32[8,128]{1,0:T(8,128)}, f32[128,128]{1,0:T(8,128)S(1)}, f32[1,128]{1,0:T(1,128)S(1)}, f32[1,128]{1,0:T(1,128)S(1)}) custom-call(f32[32,128]{1,0:T(8,128)S(1)} %get-tuple-element.56.rows, f32[32,128]{1,0:T(8,128)S(1)} %collective-permute-done.21.mate_rows, f32[128,128]{1,0:T(8,128)S(1)} %get-tuple-element.42.c, ...), custom_call_target="tpu_custom_call" | custom-call | flops 16777216 | bytes 65536 | tf_op jit(solution)/shard_map/pallas_call | solution.py:63
  28.3 0.2 collective-permute-done.20
  28.5 0.7 %collective-permute-done.19 = f32[128,128]{1,0:T(8,128)S(1)} collective-permute-done((f32[128,128]{1,0:T(8,128)S(1)}, f32[128,128]{1,0:T(8,128)S(1)}, u32[]{:S(2)}, u32[]{:S(2)}) %collective-permute-start.19) | collective-permute-done | bytes 65568 | tf_op jit(solution)/shard_map/ppermute | solution.py:111
  29.3 0.1 collective-permute-start.23
  29.4 0.7 %shard_map.93 = (f32[128,128]{1,0:T(8,128)}, f32[1,128]{1,0:T(1,128)}) custom-call(f32[128,128]{1,0:T(8,128)S(1)} %add_add_fusion.refs_0_, f32[128,128]{1,0:T(8,128)S(1)} %get-tuple-element.69.refs_1_.refs_3_, f32[1,128]{1,0:T(1,128)S(1)} %get-tuple-element.70.refs_2_.refs_4_, f32[1,128]{1,0:T(1,128)S(1)} %get-tuple-element.71.refs_3_.refs_5_), custom_call_target="tpu_custom_call" | custom-call | flops 131072 | bytes 65536 | tf_op jit(solution)/shard_map/pallas_call | solution.py:63
  30.1 0.5 %collective-permute-done.23.refs_2_ = f32[128,128]{1,0:T(8,128)S(1)} collective-permute-done((f32[128,128]{1,0:T(8,128)S(1)}, f32[128,128]{1,0:T(8,128)S(1)}, u32[]{:S(2)}, u32[]{:S(2)}) %collective-permute-start.23) | collective-permute-done | bytes 65568 | tf_op jit(solution)/shard_map/ppermute | solution.py:101
  (23 shorter events, 0.2 us)
Async XLA Ops:
  1.9 1.4 %collective-permute-start = (f32[72,128]{1,0:T(8,128)S(1)}, f32[72,128]{1,0:T(8,128)S(1)}, u32[]{:S(2)}, u32[]{:S(2)}) collective-permute-start(f32[72,128]{1,0:T(8,128)S(1)} %get-tuple-element.40.opened), channel_id=1, source_target_pairs={{0,1},{1,0},{2,3},{3,2},{4,5},{5,4},{6,7},{7,6},{8,9},{9,8},{10,11... | collective-permute-start | bytes 110600 | tf_op jit(solution)/shard_map/ppermute | solution.py:101
  2.6 1.3 %collective-permute-start.2 = (f32[64,128]{1,0:T(8,128)S(1)}, f32[64,128]{1,0:T(8,128)S(1)}, u32[]{:S(2)}, u32[]{:S(2)}) collective-permute-start(f32[64,128]{1,0:T(8,128)S(1)} %get-tuple-element.45), channel_id=1, source_target_pairs={{0,1},{1,0},{2,3},{3,2},{4,5},{5,4},{6,7},{7,6},{8,9},{9,8},{10,11... | collective-permute-start | bytes 98312 | tf_op jit(solution)/shard_map/ppermute | solution.py:101
  2.8 5.4 %collective-permute-start.5 = (f32[1024,128]{1,0:T(8,128)S(1)}, f32[1024,128]{1,0:T(8,128)S(1)}, u32[]{:S(2)}, u32[]{:S(2)}) collective-permute-start(f32[1024,128]{1,0:T(8,128)S(1)} %get-tuple-element.50.x.refs_0_), channel_id=1, source_target_pairs={{0,1},{1,0},{2,3},{3,2},{4,5},{5,4},{6,7},{7,6},{8,9},{9,8},{10,11... | collective-permute-start | bytes 1572872 | tf_op jit(solution)/shard_map/ppermute | solution.py:101
  3.2 5.0 %collective-permute-start.4 = (f32[8,128,128]{2,1,0:T(8,128)S(1)}, f32[8,128,128]{2,1,0:T(8,128)S(1)}, u32[]{:S(2)}, u32[]{:S(2)}) collective-permute-start(f32[8,128,128]{2,1,0:T(8,128)S(1)} %get-tuple-element.49.refs_6_), channel_id=1, source_target_pairs={{0,1},{1,0},{2,3},{3,2},{4,5},{5,4},{6,7},{7,6},{8,9},{9,8},{10,11... | collective-permute-start | bytes 1572872 | tf_op jit(solution)/shard_map/ppermute | solution.py:101
  3.3 4.8 %collective-permute-start.1 = (f32[80,128]{1,0:T(8,128)S(1)}, f32[80,128]{1,0:T(8,128)S(1)}, u32[]{:S(2)}, u32[]{:S(2)}) collective-permute-start(f32[80,128]{1,0:T(8,128)S(1)} %pad_maximum_fusion), channel_id=1, source_target_pairs={{0,1},{1,2},{2,3},{3,0},{4,5},{5,6},{6,7},{7,4},{8,11},{9,8},{10,9... | collective-permute-start | bytes 122888 | tf_op jit(solution)/shard_map/ppermute | solution.py:111
  3.9 4.2 %collective-permute-start.3 = (f32[64,128]{1,0:T(8,128)S(1)}, f32[64,128]{1,0:T(8,128)S(1)}, u32[]{:S(2)}, u32[]{:S(2)}) collective-permute-start(f32[64,128]{1,0:T(8,128)S(1)} %add.35), channel_id=1, source_target_pairs={{0,1},{1,2},{2,3},{3,0},{4,5},{5,6},{6,7},{7,4},{8,11},{9,8},{10,9... | collective-permute-start | bytes 98312 | tf_op jit(solution)/shard_map/ppermute | solution.py:111
  9.0 3.9 %collective-permute-start.9 = (f32[88,128]{1,0:T(8,128)S(1)}, f32[88,128]{1,0:T(8,128)S(1)}, u32[]{:S(2)}, u32[]{:S(2)}) collective-permute-start(f32[88,128]{1,0:T(8,128)S(1)} %get-tuple-element.51), channel_id=1, source_target_pairs={{0,21},{1,0},{2,23},{3,2},{4,17},{5,4},{6,19},{7,6},{8,9},{9,28},{... | collective-permute-start | bytes 135176 | tf_op jit(solution)/shard_map/ppermute | solution.py:111
  11.1 2.7 %collective-permute-start.8 = (f32[88,128]{1,0:T(8,128)S(1)}, f32[88,128]{1,0:T(8,128)S(1)}, u32[]{:S(2)}, u32[]{:S(2)}) collective-permute-start(f32[88,128]{1,0:T(8,128)S(1)} %get-tuple-element.51), channel_id=1, source_target_pairs={{0,17},{1,0},{2,19},{3,2},{4,21},{5,4},{6,23},{7,6},{8,9},{9,24},{... | collective-permute-start | bytes 135176 | tf_op jit(solution)/shard_map/ppermute | solution.py:111
  12.2 1.7 %collective-permute-start.7 = (f32[88,128]{1,0:T(8,128)S(1)}, f32[88,128]{1,0:T(8,128)S(1)}, u32[]{:S(2)}, u32[]{:S(2)}) collective-permute-start(f32[88,128]{1,0:T(8,128)S(1)} %get-tuple-element.51), channel_id=1, source_target_pairs={{0,5},{1,0},{2,7},{3,2},{4,1},{5,4},{6,3},{7,6},{8,9},{9,12},{10,1... | collective-permute-start | bytes 135176 | tf_op jit(solution)/shard_map/ppermute | solution.py:111
  12.2 1.7 %collective-permute-start.6 = (f32[88,128]{1,0:T(8,128)S(1)}, f32[88,128]{1,0:T(8,128)S(1)}, u32[]{:S(2)}, u32[]{:S(2)}) collective-permute-start(f32[88,128]{1,0:T(8,128)S(1)} %get-tuple-element.51), channel_id=1, source_target_pairs={{0,1},{1,0},{2,3},{3,2},{4,5},{5,4},{6,7},{7,6},{8,9},{9,8},{10,11... | collective-permute-start | bytes 135176 | tf_op jit(solution)/shard_map/ppermute | solution.py:101
  12.7 3.0 %collective-permute-start.12 = (f32[128,128]{1,0:T(8,128)S(1)}, f32[128,128]{1,0:T(8,128)S(1)}, u32[]{:S(2)}, u32[]{:S(2)}) collective-permute-start(f32[128,128]{1,0:T(8,128)S(1)} %get-tuple-element.53.refs_2_.moved), channel_id=1, source_target_pairs={{0,1},{1,0},{2,3},{3,2},{4,5},{5,4},{6,7},{7,6},{8,9},{9,8},{10,11... | collective-permute-start | bytes 196616 | tf_op jit(solution)/shard_map/ppermute | solution.py:101
  13.9 5.2 %collective-permute-start.11 = (f32[88,128]{1,0:T(8,128)S(1)}, f32[88,128]{1,0:T(8,128)S(1)}, u32[]{:S(2)}, u32[]{:S(2)}) collective-permute-start(f32[88,128]{1,0:T(8,128)S(1)} %add_add_fusion.1), channel_id=1, source_target_pairs={{0,1},{1,9},{2,3},{3,11},{4,5},{5,13},{6,7},{7,15},{8,0},{9,8},{10... | collective-permute-start | bytes 135176 | tf_op jit(solution)/shard_map/ppermute | solution.py:111
  15.6 3.5 %collective-permute-start.10 = (f32[88,128]{1,0:T(8,128)S(1)}, f32[88,128]{1,0:T(8,128)S(1)}, u32[]{:S(2)}, u32[]{:S(2)}) collective-permute-start(f32[88,128]{1,0:T(8,128)S(1)} %add_add_fusion.1), channel_id=1, source_target_pairs={{0,1},{1,0},{2,3},{3,2},{4,5},{5,4},{6,7},{7,6},{8,9},{9,8},{10,11... | collective-permute-start | bytes 135176 | tf_op jit(solution)/shard_map/ppermute | solution.py:101
  19.5 2.1 %collective-permute-start.16 = (f32[144,128]{1,0:T(8,128)S(1)}, f32[144,128]{1,0:T(8,128)S(1)}, u32[]{:S(2)}, u32[]{:S(2)}) collective-permute-start(f32[144,128]{1,0:T(8,128)S(1)} %get-tuple-element.54), channel_id=1, source_target_pairs={{0,10},{1,0},{2,8},{3,2},{4,14},{5,4},{6,12},{7,6},{8,9},{9,3},{10... | collective-permute-start | bytes 221192 | tf_op jit(solution)/shard_map/ppermute | solution.py:111
  19.6 2.7 %collective-permute-start.15 = (f32[144,128]{1,0:T(8,128)S(1)}, f32[144,128]{1,0:T(8,128)S(1)}, u32[]{:S(2)}, u32[]{:S(2)}) collective-permute-start(f32[144,128]{1,0:T(8,128)S(1)} %get-tuple-element.54), channel_id=1, source_target_pairs={{0,8},{1,0},{2,10},{3,2},{4,12},{5,4},{6,14},{7,6},{8,9},{9,1},{10... | collective-permute-start | bytes 221192 | tf_op jit(solution)/shard_map/ppermute | solution.py:111
  19.6 3.4 %collective-permute-start.14 = (f32[144,128]{1,0:T(8,128)S(1)}, f32[144,128]{1,0:T(8,128)S(1)}, u32[]{:S(2)}, u32[]{:S(2)}) collective-permute-start(f32[144,128]{1,0:T(8,128)S(1)} %get-tuple-element.54), channel_id=1, source_target_pairs={{0,3},{1,0},{2,1},{3,2},{4,7},{5,4},{6,5},{7,6},{8,9},{9,10},{10,1... | collective-permute-start | bytes 221192 | tf_op jit(solution)/shard_map/ppermute | solution.py:111
  21.0 2.0 %collective-permute-start.13 = (f32[144,128]{1,0:T(8,128)S(1)}, f32[144,128]{1,0:T(8,128)S(1)}, u32[]{:S(2)}, u32[]{:S(2)}) collective-permute-start(f32[144,128]{1,0:T(8,128)S(1)} %get-tuple-element.54), channel_id=1, source_target_pairs={{0,1},{1,0},{2,3},{3,2},{4,5},{5,4},{6,7},{7,6},{8,9},{9,8},{10,11... | collective-permute-start | bytes 221192 | tf_op jit(solution)/shard_map/ppermute | solution.py:101
  21.0 5.2 %collective-permute-start.22 = (f32[128,128]{1,0:T(8,128)S(1)}, f32[128,128]{1,0:T(8,128)S(1)}, u32[]{:S(2)}, u32[]{:S(2)}) collective-permute-start(f32[128,128]{1,0:T(8,128)S(1)} %get-tuple-element.57.gram), channel_id=1, source_target_pairs={{0,1},{1,0},{2,3},{3,2},{4,5},{5,4},{6,7},{7,6},{8,9},{9,8},{10,11... | collective-permute-start | bytes 196616 | tf_op jit(solution)/shard_map/ppermute | solution.py:101
  23.0 5.5 %collective-permute-start.20 = (f32[128,128]{1,0:T(8,128)S(1)}, f32[128,128]{1,0:T(8,128)S(1)}, u32[]{:S(2)}, u32[]{:S(2)}) collective-permute-start(f32[128,128]{1,0:T(8,128)S(1)} %get-tuple-element.55), channel_id=1, source_target_pairs={{0,1},{1,20},{2,3},{3,22},{4,5},{5,16},{6,7},{7,18},{8,29},{9,8},{... | collective-permute-start | bytes 196616 | tf_op jit(solution)/shard_map/ppermute | solution.py:111
  24.0 5.3 %collective-permute-start.19 = (f32[128,128]{1,0:T(8,128)S(1)}, f32[128,128]{1,0:T(8,128)S(1)}, u32[]{:S(2)}, u32[]{:S(2)}) collective-permute-start(f32[128,128]{1,0:T(8,128)S(1)} %get-tuple-element.55), channel_id=1, source_target_pairs={{0,1},{1,16},{2,3},{3,18},{4,5},{5,20},{6,7},{7,22},{8,25},{9,8},{... | collective-permute-start | bytes 196616 | tf_op jit(solution)/shard_map/ppermute | solution.py:111
  25.5 3.7 %collective-permute-start.18 = (f32[128,128]{1,0:T(8,128)S(1)}, f32[128,128]{1,0:T(8,128)S(1)}, u32[]{:S(2)}, u32[]{:S(2)}) collective-permute-start(f32[128,128]{1,0:T(8,128)S(1)} %get-tuple-element.55), channel_id=1, source_target_pairs={{0,1},{1,4},{2,3},{3,6},{4,5},{5,0},{6,7},{7,2},{8,13},{9,8},{10,1... | collective-permute-start | bytes 196616 | tf_op jit(solution)/shard_map/ppermute | solution.py:111
  26.1 3.2 %collective-permute-start.17 = (f32[128,128]{1,0:T(8,128)S(1)}, f32[128,128]{1,0:T(8,128)S(1)}, u32[]{:S(2)}, u32[]{:S(2)}) collective-permute-start(f32[128,128]{1,0:T(8,128)S(1)} %get-tuple-element.55), channel_id=1, source_target_pairs={{0,1},{1,0},{2,3},{3,2},{4,5},{5,4},{6,7},{7,6},{8,9},{9,8},{10,11... | collective-permute-start | bytes 196616 | tf_op jit(solution)/shard_map/ppermute | solution.py:101
  26.2 1.2 %collective-permute-start.21 = (f32[32,128]{1,0:T(8,128)S(1)}, f32[32,128]{1,0:T(8,128)S(1)}, u32[]{:S(2)}, u32[]{:S(2)}) collective-permute-start(f32[32,128]{1,0:T(8,128)S(1)} %get-tuple-element.56.rows), channel_id=1, source_target_pairs={{0,1},{1,0},{2,3},{3,2},{4,5},{5,4},{6,7},{7,6},{8,9},{9,8},{10,11... | collective-permute-start | bytes 49160 | tf_op jit(solution)/shard_map/ppermute | solution.py:101
  29.3 1.3 %collective-permute-start.23 = (f32[128,128]{1,0:T(8,128)S(1)}, f32[128,128]{1,0:T(8,128)S(1)}, u32[]{:S(2)}, u32[]{:S(2)}) collective-permute-start(f32[128,128]{1,0:T(8,128)S(1)} %add_add_fusion.refs_0_), channel_id=1, source_target_pairs={{0,1},{1,0},{2,3},{3,2},{4,5},{5,4},{6,7},{7,6},{8,9},{9,8},{10,11... | collective-permute-start | bytes 196616 | tf_op jit(solution)/shard_map/ppermute | solution.py:101
